TPU v7x, 256 devices: a whole 4x4x8 slice. The times are simulated.
256 devices in a mesh: tm: 16 (over y_lo, x, core), row: 16 (over z, y_hi).
Axes of the slice: x: 4, y: 4 (y_hi: 2, y_lo: 2; y = y_hi * 2 + y_lo), z: 8, core: 2. Of those that a mesh axis runs over, the one named last changes fastest.
Arguments:
- fields: bfloat16 [2, 16, 2, 1024, 1024], P(None, 'tm', None, 'row'), may hold values from -2 to 2
- mom_table: int32 [2, 1, 4], replicated, may hold values from 0 to 1
Outputs:
- products: bfloat16 [2, 1, 16, 2, 1024, 1024], P(None, None, 'tm', None, 'row')
- correlator: float32 [2, 1, 16, 2], P(None, None, 'tm')
Inputs may be any that keep to these rules, and one draw needn't show every extreme that they name: `mom_table`: momentum indices of the fields.
All inputs are finite; a program needn't handle non-finite values.
Results may differ from a plain program's by a relative error of at most 0.0052.
Values may be sent and summed in bfloat16 or wider, within the bound.
No kernel may reach another device: no remote copies, remote signals or barrier semaphores. Data moves between devices by JAX's collectives and lax.ppermute only.
A program may use at most 128 MiB of HBM per device.

v0:
```python
import jax
import jax.numpy as jnp
from jax import lax
from jax.sharding import PartitionSpec as P


def shifted(block, axis, distance):
    devices = range(lax.axis_size(axis))
    route = [((i - distance) % len(devices), i) for i in devices]
    return lax.ppermute(block, axis, route)


def matmul_f32(left_side, right_side):
    return jnp.dot(left_side, right_side, preferred_element_type=jnp.float32)


def complex_product(left_side, right_side):
    real_part = matmul_f32(left_side[0], right_side[0]) - matmul_f32(left_side[1], right_side[1])
    imag_part = matmul_f32(left_side[0], right_side[1]) + matmul_f32(left_side[1], right_side[0])
    return jnp.stack([real_part, imag_part])


def select_field(stacked, mom_index):
    return lax.dynamic_index_in_dim(stacked, mom_index, 0, keepdims=False)


def shards(fields, mom_table):
    own_rows = fields[:, 0]
    rounds_total = mom_table.shape[0]
    modes_total = own_rows.shape[3]
    own_full = lax.all_gather(own_rows, "row", axis=2, tiled=True)
    product_rounds = []
    partial_rounds = []
    for round_number in range(rounds_total):
        step_size = round_number + 1
        partner_rows = shifted(own_rows, "tm", -step_size)
        partner_full = lax.all_gather(partner_rows, "row", axis=2, tiled=True)
        mom_a = mom_table[round_number, 0, 0]
        mom_b = mom_table[round_number, 0, 1]
        mom_c = mom_table[round_number, 0, 2]
        mom_d = mom_table[round_number, 0, 3]
        product = complex_product(select_field(own_rows, mom_a), select_field(partner_full, mom_b))
        product_list = [product.astype(jnp.bfloat16)]
        crossed = complex_product(select_field(partner_rows, mom_c), select_field(own_full, mom_d))
        crossed_list = [crossed.astype(jnp.bfloat16)]
        product_block = jnp.stack(product_list)
        crossed_block = jnp.stack(crossed_list)
        crossed_columns = lax.all_to_all(
            crossed_block, "row", split_axis=3, concat_axis=2, tiled=True
        )
        product_f = product_block.astype(jnp.float32)
        crossed_t = jnp.swapaxes(crossed_columns.astype(jnp.float32), 2, 3)
        real_part = jnp.sum(
            product_f[:, 0] * crossed_t[:, 0] - product_f[:, 1] * crossed_t[:, 1], axis=(1, 2)
        )
        imag_part = jnp.sum(
            product_f[:, 0] * crossed_t[:, 1] + product_f[:, 1] * crossed_t[:, 0], axis=(1, 2)
        )
        product_rounds.append(product_block)
        partial_rounds.append(jnp.stack([real_part, imag_part], axis=-1))
    partial_all = jnp.stack(partial_rounds)
    summed = lax.psum(partial_all, "row")
    correlator = (summed / jnp.float32(modes_total))[:, :, None, :]
    products = jnp.stack(product_rounds)[:, :, None]
    return (products, correlator)


def solution(mesh):
    return jax.shard_map(
        shards,
        mesh=mesh,
        in_specs=(P(None, "tm", None, "row", None), P()),
        out_specs=(P(None, None, "tm", None, "row", None), P(None, None, "tm", None)),
        check_vma=False,
    )
```

profile of v0, /device:TPU:1, one launch (start us, length us, event | category | flops | bytes accessed | tf_op | source)
XLA Modules:
  0.0 484.7 jit_solution(10256682482010733284)
XLA Ops:
  7.2 0.0 all-gather.9.cloned.1.call-start
  7.2 0.7 all-gather.9.cloned.1.call-update
  7.9 0.0 all-gather.7.cloned.1.call-start
  7.9 4.4 collective-permute-start.1
  12.3 10.9 %collective-permute-done.1 = bf16[2,2,64,1024]{3,2,1,0:T(8,128)(2,1)S(1)} collective-permute-done((bf16[2,2,64,1024]{3,2,1,0:T(8,128)(2,1)}, bf16[2,2,64,1024]{3,2,1,0:T(8,128)(2,1)S(1)}, u32[]{:S(2)}, u32[]{:S(2)}) %collective-permute-start.1) | collective-permute-done | bytes 524320 | tf_op jit(solution)/shard_map/ppermute | solution.py:10
  23.2 0.0 copy-start.4
  23.3 0.8 copy-done.4
  24.0 0.0 all-gather.7.cloned.1.call-update
  24.1 0.0 all-gather.5.cloned.1.call-start
  24.1 1.6 collective-permute-start
  25.7 7.7 %collective-permute-done = bf16[2,2,64,1024]{3,2,1,0:T(8,128)(2,1)S(1)} collective-permute-done((bf16[2,2,64,1024]{3,2,1,0:T(8,128)(2,1)}, bf16[2,2,64,1024]{3,2,1,0:T(8,128)(2,1)S(1)}, u32[]{:S(2)}, u32[]{:S(2)}) %collective-permute-start) | collective-permute-done | bytes 524320 | tf_op jit(solution)/shard_map/ppermute | solution.py:10
  33.4 0.0 copy-start.2
  33.4 0.8 copy-done.2
  34.2 0.0 all-gather.5.cloned.1.call-update
  34.3 1.5 fusion.52
  43.2 0.0 copy-start.5
  43.2 112.0 %all-gather.9.cloned.1.call-done = bf16[2,1,2,1024,1024]{4,3,2,1,0:T(8,128)(2,1)} async-done(((bf16[2,1,2,64,1024]{4,3,2,1,0:T(8,128)(2,1)}), bf16[2,1,2,1024,1024]{4,3,2,1,0:T(8,128)(2,1)}) %all-gather.9.cloned.1.call-update) | async-done | bytes 8388624 | tf_op jit(solution)/shard_map/all_gather | solution.py:31
  155.2 6.9 %dynamic-slice_bitcast_fusion.1 = (bf16[1,2,1024,1024]{3,2,1,0:T(8,128)(2,1)}, bf16[1,2,1024,1024]{3,2,1,0:T(8,128)(2,1)S(1)}) fusion(bf16[2,1,2,1024,1024]{4,3,2,1,0:T(8,128)(2,1)} %all-gather.9.cloned.1.call-done, s32[]{:T(128)S(6)} %select_n.31, s32[]{:T(128)S(6)} %select_n.33), kind=kLoop, calls=%fused_computation.1 | loop fusion | bytes 16777224 | tf_op jit(solution)/shard_map/jit(dynamic_index_in_dim)/dynamic_slice | solution.py:24
  162.1 0.0 copy-done.5
  162.1 0.5 fusion.7
  162.6 0.5 fusion.33
  163.1 0.0 copy-start.3
  163.1 0.5 fusion.4
  163.6 0.5 fusion.32
  164.1 0.4 copy.10
  164.5 1.1 reshape.481
  165.6 4.2 all-to-all-start.1
  169.8 0.0 copy-start
  169.8 0.0 copy-done.3
  169.8 2.2 fusion.3
  172.0 2.1 fusion
  174.1 0.0 copy-done
  174.1 0.5 fusion.35
  174.6 0.5 fusion.34
  175.1 0.4 copy.8
  175.5 1.1 reshape.483
  176.7 0.0 copy-start.1
  176.7 8.2 %all-to-all-done.1 = bf16[16,2,4096]{2,1,0:T(2,128)(2,1)S(1)} async-done(((bf16[16,2,4096]{2,1,0:T(2,128)(2,1)}), bf16[16,2,4096]{2,1,0:T(2,128)(2,1)S(1)}, u32[]{:S(2)}, u32[]{:S(2)}) %all-to-all-start.1) | async-done | bytes 262176 | tf_op jit(solution)/shard_map/all_to_all | solution.py:48
  184.9 3.7 all-to-all-start
  196.1 0.3 reshape.482
  196.4 0.3 copy.16
  196.8 0.3 reshape.475
  197.1 6.2 %all-to-all-done = bf16[16,2,4096]{2,1,0:T(2,128)(2,1)S(1)} async-done(((bf16[16,2,4096]{2,1,0:T(2,128)(2,1)}), bf16[16,2,4096]{2,1,0:T(2,128)(2,1)S(1)}, u32[]{:S(2)}, u32[]{:S(2)}) %all-to-all-start) | async-done | bytes 262176 | tf_op jit(solution)/shard_map/all_to_all | solution.py:48
  203.3 0.3 reshape.484
  203.6 0.3 copy.17
  204.0 0.3 reshape.474
  204.3 94.7 %all-gather.7.cloned.1.call-done = bf16[2,2,1024,1024]{3,2,1,0:T(8,128)(2,1)} async-done(((bf16[2,2,64,1024]{3,2,1,0:T(8,128)(2,1)}), bf16[2,2,1024,1024]{3,2,1,0:T(8,128)(2,1)}) %all-gather.7.cloned.1.call-update) | async-done | bytes 8388624 | tf_op jit(solution)/shard_map/all_gather | solution.py:37
  299.0 0.0 copy-done.1
  299.0 2.1 fusion.15
  301.0 2.1 fusion.10
  303.1 2.1 fusion.29
  305.2 2.1 fusion.31
  307.3 0.8 subtract_reduce_fusion
  308.2 126.1 %all-gather.5.cloned.1.call-done = bf16[2,2,1024,1024]{3,2,1,0:T(8,128)(2,1)} async-done(((bf16[2,2,64,1024]{3,2,1,0:T(8,128)(2,1)}), bf16[2,2,1024,1024]{3,2,1,0:T(8,128)(2,1)}) %all-gather.5.cloned.1.call-update) | async-done | bytes 8388624 | tf_op jit(solution)/shard_map/all_gather | solution.py:37
  434.2 2.1 fusion.8
  436.3 2.1 fusion.13
  438.4 2.1 fusion.30
  440.5 2.1 fusion.28
  442.6 0.7 subtract_reduce_fusion.1
  443.3 2.6 maximum_bitcast_fusion.1
  446.0 30.7 %psum.7 = f32[2,1,2]{2,1,0:T(1,128)S(1)} all-reduce(f32[2,1,2]{2,1,0:T(1,128)S(1)} %pad_maximum_fusion.2), channel_id=1, replica_groups=mesh['tm'=16,'row'=16] {'row'}, use_global_device_ids=true, to_apply=%region_4.5 | all-reduce | flops 4 | bytes 32 | tf_op jit(solution)/shard_map/psum | solution.py:62
  476.7 0.6 multiply_bitcast_fusion
  477.3 0.8 maximum_bitcast_fusion
  (5 shorter events, 0.1 us)
Async XLA Ops:
  7.2 148.0 %all-gather.9.cloned.1.call-start = ((), (), s32[]{:S(2)}) async-start(), calls=%async_computation.4 | async-start | bytes 8912896 | tf_op jit(solution)/shard_map/all_gather | solution.py:31
  7.9 291.1 %all-gather.7.cloned.1.call-start = ((), (), s32[]{:S(2)}) async-start(), calls=%async_computation.3 | async-start | bytes 8912896 | tf_op jit(solution)/shard_map/all_gather | solution.py:37
  7.9 15.3 %collective-permute-start.1 = (bf16[2,2,64,1024]{3,2,1,0:T(8,128)(2,1)}, bf16[2,2,64,1024]{3,2,1,0:T(8,128)(2,1)S(1)}, u32[]{:S(2)}, u32[]{:S(2)}) collective-permute-start(bf16[2,2,64,1024]{3,2,1,0:T(8,128)(2,1)} %bitcast.173), channel_id=1, source_target_pairs={{32,0},{48,16},{64,32},{80,48},{96,64},{112,80},{128,96},{144,112}... | collective-permute-start | bytes 1572872 | tf_op jit(solution)/shard_map/ppermute | solution.py:10
  23.2 0.8 copy-start.4
  24.1 410.2 %all-gather.5.cloned.1.call-start = ((), (), s32[]{:S(2)}) async-start(), calls=%async_computation.2 | async-start | bytes 8912896 | tf_op jit(solution)/shard_map/all_gather | solution.py:37
  24.1 9.3 %collective-permute-start = (bf16[2,2,64,1024]{3,2,1,0:T(8,128)(2,1)}, bf16[2,2,64,1024]{3,2,1,0:T(8,128)(2,1)S(1)}, u32[]{:S(2)}, u32[]{:S(2)}) collective-permute-start(bf16[2,2,64,1024]{3,2,1,0:T(8,128)(2,1)} %bitcast.174), channel_id=1, source_target_pairs={{16,0},{32,16},{48,32},{64,48},{80,64},{96,80},{112,96},{128,112},... | collective-permute-start | bytes 1572872 | tf_op jit(solution)/shard_map/ppermute | solution.py:10
  33.4 0.8 copy-start.2
  43.2 118.9 %copy-start.5 = (bf16[2,2,64,1024]{3,2,1,0:T(8,128)(2,1)S(1)}, bf16[2,2,64,1024]{3,2,1,0:T(8,128)(2,1)}, u32[]{:S(2)}) copy-start(bf16[2,2,64,1024]{3,2,1,0:T(8,128)(2,1)} %copy-done.4) | copy-start | bytes 1572868
  163.1 6.7 %copy-start.3 = (bf16[2,2,64,1024]{3,2,1,0:T(8,128)(2,1)S(1)}, bf16[2,2,64,1024]{3,2,1,0:T(8,128)(2,1)}, u32[]{:S(2)}) copy-start(bf16[2,2,64,1024]{3,2,1,0:T(8,128)(2,1)} %copy-done.2) | copy-start | bytes 1572868
  165.6 19.3 %all-to-all-start.1 = ((bf16[16,2,4096]{2,1,0:T(2,128)(2,1)}), bf16[16,2,4096]{2,1,0:T(2,128)(2,1)S(1)}, u32[]{:S(2)}, u32[]{:S(2)}) async-start(bf16[16,2,4096]{2,1,0:T(2,128)(2,1)} %reshape.481), calls=%async_computation.1 | async-start | bytes 524288 | tf_op jit(solution)/shard_map/all_to_all | solution.py:48
  169.8 4.3 copy-start
  176.7 122.3 %copy-start.1 = (bf16[2,1,2,64,1024]{4,3,2,1,0:T(8,128)(2,1)S(1)}, bf16[2,1,2,64,1024]{4,3,2,1,0:T(8,128)(2,1)}, u32[]{:S(2)}) copy-start(bf16[2,1,2,64,1024]{4,3,2,1,0:T(8,128)(2,1)} %param.2) | copy-start | bytes 1572868
  184.9 18.4 %all-to-all-start = ((bf16[16,2,4096]{2,1,0:T(2,128)(2,1)}), bf16[16,2,4096]{2,1,0:T(2,128)(2,1)S(1)}, u32[]{:S(2)}, u32[]{:S(2)}) async-start(bf16[16,2,4096]{2,1,0:T(2,128)(2,1)} %reshape.483), calls=%async_computation | async-start | bytes 524288 | tf_op jit(solution)/shard_map/all_to_all | solution.py:48
Sparse Core Ops, SparseCore 0:
  10.6 144.5 all-gather.8
  158.4 140.5 all-gather.6
  301.6 132.6 all-gather.4
where the time goes:
time: 492 us; the launch traced here: 485 us
  waiting for transfers between devices  366 us (74%)
  blocking collectives  30.7 us (6%)
  between operations  28.9 us (6%)
  matrix products  23.8 us (5%)
  local copies, waits for them, and re-layouts  15 us (3%)
  starting transfers between devices  14 us (3%)
  other arithmetic  5.73 us (1%)
    all_gather x2, waiting for transfers between devices, shards(): partner_full = lax.all_gather(partner_rows, 'row', axis=2, tiled=True)  221 us
    all_gather x1, waiting for transfers between devices, shards(): own_full = lax.all_gather(own_rows, 'row', axis=2, tiled=True)  112 us
    psum x1, blocking collectives, shards(): summed = lax.psum(partial_all, 'row')  30.7 us
    dot_general x16, matrix products, matmul_f32(): return jnp.dot(left_side, right_side, preferred_element_type=jnp.float32)  23.8 us
    ppermute x2, waiting for transfers between devices, shifted(): return lax.ppermute(block, axis, route)  18.6 us
    all_to_all x2, waiting for transfers between devices, shards(): lax.all_to_all(crossed_block, 'row', split_axis=3, concat_axis=2, tiled=T...  14.4 us
  transfers between devices with their start and end apart: 7, of which 7 were waited for; matrix products, arithmetic and copies ran while one was open for 6% of the time, Pallas kernels for 0%

commit v1 on v0

v1 whole, which is shorter than its diff:
```python
import functools

import jax
import jax.numpy as jnp
from jax import lax
from jax.experimental import pallas as pl
from jax.experimental.pallas import tpu as pltpu
from jax.sharding import PartitionSpec as P

BOTH = ("tm", "row")
BF16 = jnp.bfloat16
F32 = jnp.float32


def index_of(m, c, z, h, ring):
    return ((m % 8) * 2 + c) * (2 * ring) + (z % ring) * 2 + h


def moved(block, route, ring):
    pairs = []
    for m in range(8):
        for c in range(2):
            for z in range(ring):
                for h in range(2):
                    pairs.append((index_of(m, c, z, h, ring), index_of(*route(m, c, z, h), ring)))
    return lax.ppermute(block, BOTH, pairs)


def along(step):
    return lambda m, c, z, h: (m, c, z + step, h)


def other_core(m, c, z, h):
    return (m, 1 - c, z, h)


def to_hub(turn):
    return lambda m, c, z, h: (m, h ^ turn, z, c)


def hub_ahead(step):
    def route(m, c, z, h):
        s = (2 * m + h + 1 + c) % 16
        return (s // 2, c, z + step, s % 2)

    return route


def from_hub(turn):
    def route(m, c, z, h):
        t = (2 * m + h - 1 - c) % 16
        return (t // 2, t % 2, z, c ^ turn)

    return route


VMEM = pl.BlockSpec(memory_space=pltpu.VMEM)
SMEM = pl.BlockSpec(memory_space=pltpu.SMEM)


def left_side(a_ref, place):
    columns = pl.ds(pl.multiple_of(place * 128, 128), 128)
    real, imag = a_ref[0, :, columns], a_ref[1, :, columns]
    return jnp.concatenate(
        [jnp.concatenate([real, -imag], axis=1), jnp.concatenate([imag, real], axis=1)], axis=0
    )


def add_products(info, a_ref, own, other, acc_in, acc_out):
    total = acc_in[...] if acc_in is not None else None
    for number in range(len(own)):
        block = jnp.where(info[8] == 1, own[number][...], other[number][...]).reshape(256, 1024)
        term = jnp.dot(left_side(a_ref, info[number]), block, preferred_element_type=F32)
        total = term if total is None else total + term
    acc_out[...] = total


def first_kernel(info, a_ref, own, other, acc_out):
    add_products(info, a_ref, [own], [other], None, acc_out)


def step_kernel(info, a_ref, own_u, own_d, other_u, other_d, acc_in, acc_out):
    add_products(info, a_ref, [own_u, own_d], [other_u, other_d], acc_in, acc_out)


def params(flops):
    return dict(
        compiler_params=pltpu.CompilerParams(vmem_limit_bytes=32 * 1024 * 1024),
        cost_estimate=pl.CostEstimate(flops=flops, bytes_accessed=4 << 20, transcendentals=0),
    )


def first_step(info, a, own, other):
    return pl.pallas_call(
        first_kernel,
        out_shape=jax.ShapeDtypeStruct((256, 1024), F32),
        in_specs=[SMEM] + [VMEM] * 3,
        out_specs=VMEM,
        **params(2 * 256 * 256 * 1024),
    )(info, a, own, other)


def next_step(info, a, own_u, own_d, other_u, other_d, acc):
    return pl.pallas_call(
        step_kernel,
        out_shape=jax.ShapeDtypeStruct((256, 1024), F32),
        in_specs=[SMEM] + [VMEM] * 6,
        out_specs=VMEM,
        input_output_aliases={6: 0},
        **params(4 * 256 * 256 * 1024),
    )(info, a, own_u, own_d, other_u, other_d, acc)


def crossed_block(real, imag, drhs):
    block = jnp.dot(real, drhs[0:1024, :], preferred_element_type=F32)
    block += jnp.dot(imag, drhs[1024:2048, :], preferred_element_type=F32)
    turned = jnp.concatenate([block[:, :128].T, block[:, 128:].T], axis=0)
    return turned.astype(BF16)


def crossed_kernel(info, *refs):
    slices, own, other = refs[0:8], refs[8:15], refs[15:22]
    drhs, crossed = refs[22], refs[23]
    for number in range(8):
        top = pl.multiple_of(info[number] * 128, 128)
        real, imag = slices[number][0], slices[number][1]
        drhs[pl.ds(top, 128), 0:128] = real
        drhs[pl.ds(top, 128), 128:256] = imag
        drhs[pl.ds(1024 + top, 128), 0:128] = -imag
        drhs[pl.ds(1024 + top, 128), 128:256] = real
    for number in range(7):
        real = jnp.where(info[9] == 1, own[number][0], other[number][0])
        imag = jnp.where(info[9] == 1, own[number][1], other[number][1])
        columns = pl.ds(pl.multiple_of(info[number] * 128, 128), 128)
        crossed[:, columns] = crossed_block(real, imag, drhs)


def crossed_most(info, slices, own, other):
    return pl.pallas_call(
        crossed_kernel,
        out_shape=(jax.ShapeDtypeStruct((2048, 256), BF16), jax.ShapeDtypeStruct((256, 1024), BF16)),
        in_specs=[SMEM] + [VMEM] * 22,
        out_specs=(VMEM, VMEM),
        **params(14 * 128 * 2048 * 256),
    )(info, *slices, *own, *other)


def last_kernel(info, a_ref, own_re, own_im, other_re, other_im, acc, drhs, crossed, keep, send, trace, turned):
    place = info[7]
    real = jnp.where(info[8] == 1, own_re[...], other_re[...])
    imag = jnp.where(info[8] == 1, own_im[...], other_im[...])
    block = jnp.concatenate([real, imag], axis=0)
    product = acc[...] + jnp.dot(left_side(a_ref, place), block, preferred_element_type=F32)
    rounded = product.astype(BF16)
    for part in range(2):
        low, high = rounded[part * 128 : part * 128 + 64], rounded[part * 128 + 64 : part * 128 + 128]
        keep[part] = jnp.where(info[10] == 0, low, high)
        send[part] = jnp.where(info[10] == 0, high, low)
    real = jnp.where(info[9] == 1, own_re[...], other_re[...])
    imag = jnp.where(info[9] == 1, own_im[...], other_im[...])
    turned[...] = crossed[...]
    turned[:, pl.ds(pl.multiple_of(place * 128, 128), 128)] = crossed_block(real, imag, drhs)
    p_re, p_im = rounded[:128].astype(F32), rounded[128:].astype(F32)
    c_re, c_im = turned[:128, :].astype(F32), turned[128:, :].astype(F32)
    re = jnp.sum(p_re * c_re - p_im * c_im, axis=0, keepdims=True)
    im = jnp.sum(p_re * c_im + p_im * c_re, axis=0, keepdims=True)
    re = jnp.sum(re, axis=1, keepdims=True)
    im = jnp.sum(im, axis=1, keepdims=True)
    lane = lax.broadcasted_iota(jnp.int32, (1, 128), 1)
    trace[...] = jnp.where(lane == 0, re, im)


def last_step(info, a, own_re, own_im, other_re, other_im, acc, drhs, crossed):
    half = jax.ShapeDtypeStruct((2, 64, 1024), BF16)
    return pl.pallas_call(
        last_kernel,
        out_shape=(half, half, jax.ShapeDtypeStruct((1, 128), F32)),
        in_specs=[SMEM] + [VMEM] * 8,
        out_specs=(VMEM, VMEM, VMEM),
        scratch_shapes=[pltpu.VMEM((256, 1024), BF16)],
        **params(2 * 256 * 256 * 1024 + 2 * 128 * 2048 * 256),
    )(info, a, own_re, own_im, other_re, other_im, acc, drhs, crossed)


def shards(fields, mom_table):
    rows = fields[:, 0]
    tm, row = lax.axis_index("tm"), lax.axis_index("row")
    core, place, half = tm % 2, row // 2, row % 2
    ring = lax.axis_size("row") // 2
    mom_a, mom_b, mom_c, mom_d = [mom_table[core, 0, k] for k in range(4)]

    def go(block, route):
        return moved(block, route, ring)

    first = go(jnp.where(half == 0, rows[0], rows[1]), to_hub(0))
    second = go(jnp.where(half == 0, rows[1], rows[0]), to_hub(1))
    own = jnp.where(core == 0, jnp.concatenate([first, second], 1), jnp.concatenate([second, first], 1))

    offsets = [0, -1, 1, -2, 2, -3, 3, 4]
    own_blocks, up, down = [own], own, own
    for _ in range(3):
        up, down = go(up, along(1)), go(down, along(-1))
        own_blocks += [up, down]
    far_re, far_im = go(up[0], along(1)), go(down[1], along(-1))
    other_blocks = [go(block, other_core) for block in own_blocks]
    other_re, other_im = go(far_re, other_core), go(far_im, other_core)

    places = [lax.rem(place + offset + ring, ring) for offset in offsets]

    def info_of(order):
        flags = [mom_b == core, mom_c == core, core]
        return jnp.stack([places[k] for k in order] + [jnp.int32(f) for f in flags] + [jnp.int32(0)])

    whole_info = info_of(range(8))

    a = go(jnp.where(mom_a == core, own_blocks[0], other_blocks[0]), hub_ahead(0))

    def columns(k, at):
        def cut(block):
            return lax.dynamic_slice(block, (0, 0, at * 128), (2, 128, 128))

        return jnp.where(mom_d == core, cut(own_blocks[k]), cut(other_blocks[k]))

    slices = [None] * 8
    for group in ([0, 1, 2], [3, 4], [5, 6]):
        got = go(jnp.stack([columns(k, place) for k in group]), hub_ahead(0))
        for position, k in enumerate(group):
            slices[k] = got[position]
    slices[7] = go(columns(0, lax.rem(place + 4, ring)), hub_ahead(4))

    acc = first_step(whole_info, a, own_blocks[0], other_blocks[0])
    for k in (1, 3, 5):
        step_info = info_of([k, k + 1] + [0] * 6)
        acc = next_step(step_info, a, own_blocks[k], own_blocks[k + 1], other_blocks[k], other_blocks[k + 1], acc)
    drhs, crossed = crossed_most(whole_info, slices, own_blocks, other_blocks)
    keep, send, trace = last_step(whole_info, a, far_re, far_im, other_re, other_im, acc, drhs, crossed)

    for distance in (1, 2, 4):
        trace = trace + go(trace, lambda m, c, z, h: (m, c, z ^ distance, h))
    trace = trace[0, :2] / F32(1024)
    kept, sent = go(trace, from_hub(0)), go(trace, from_hub(1))
    correlator = jnp.where(half == 0, jnp.stack([kept, sent]), jnp.stack([sent, kept]))[:, None, None, :]

    kept, sent = go(keep, from_hub(0)), go(send, from_hub(1))
    products = jnp.where(half == 0, jnp.stack([kept, sent]), jnp.stack([sent, kept]))[:, None, None]
    return products, correlator


def solution(mesh):
    return jax.shard_map(
        shards,
        mesh=mesh,
        in_specs=(P(None, "tm", None, "row", None), P()),
        out_specs=(P(None, None, "tm", None, "row", None), P(None, None, "tm", None)),
        check_vma=False,
    )
```

time: 492 us -> 121 us (0.25); the launches traced: 485 us -> 121 us
  waiting for transfers between devices: 366 us -> 34.7 us
  starting transfers between devices: 14 us -> 62.9 us
  blocking collectives: 30.7 us -> 0 us
  between operations: 28.9 us -> 3.54 us
  matrix products: 23.8 us -> 0 us
  local copies, waits for them, and re-layouts: 15 us -> 1.76 us
  Pallas kernels: 0 us -> 10.2 us
    all_gather x3 -> x0, waiting for transfers between devices: 333 us -> none  [the longest x2 221 us: shards(): partner_full = lax.all_gather(partner_rows, 'row', axis=2, tiled=True)]
    ppermute x2 -> x31, starting transfers between devices: 6.02 us -> 62.9 us  [moved(): return lax.ppermute(block, BOTH, pairs)]
    psum x1 -> x0, blocking collectives: 30.7 us -> none  [shards(): summed = lax.psum(partial_all, 'row')]
    dot_general x16 -> x0, matrix products: 23.8 us -> none  [matmul_f32(): return jnp.dot(left_side, right_side, preferred_element_type=jnp.float32)]
    ppermute x2 -> x31, waiting for transfers between devices: 18.6 us -> 34.7 us  [moved(): return lax.ppermute(block, BOTH, pairs)]
    all_to_all x2 -> x0, waiting for transfers between devices: 14.4 us -> none  [shards(): lax.all_to_all(crossed_block, 'row', split_axis=3, concat_axis=2, tiled=T...]
    pallas_call x0 -> x6, Pallas kernels: none -> 10.2 us  [the longest x3 4.65 us: next_step(): pl.pallas_call(step_kernel, out_shape=jax.ShapeDtypeStruct((256, 1024), F...]
    all_to_all x2 -> x0, starting transfers between devices: 7.89 us -> none  [shards(): lax.all_to_all(crossed_block, 'row', split_axis=3, concat_axis=2, tiled=T...]
  transfers between devices with their start and end apart: 7 -> 31, of which waited for: 7 -> 11; matrix products, arithmetic and copies ran while one was open for 6% -> 6% of each run, Pallas kernels for 0% -> 7%
where the time goes in v1:
time: 121 us
  starting transfers between devices  62.9 us (52%)
  waiting for transfers between devices  34.7 us (29%)
  Pallas kernels  10.2 us (8%)
  other arithmetic  7.87 us (7%)
  between operations  3.54 us (3%)
  local copies, waits for them, and re-layouts  1.76 us (1%)
    ppermute x31, starting transfers between devices, moved(): return lax.ppermute(block, BOTH, pairs)  62.9 us
    ppermute x31, waiting for transfers between devices, moved(): return lax.ppermute(block, BOTH, pairs)  34.7 us
    pallas_call x3, Pallas kernels, next_step(): pl.pallas_call(step_kernel, out_shape=jax.ShapeDtypeStruct((256, 1024), F...  4.65 us
    another operation x9, other arithmetic, shards(): got = go(jnp.stack([columns(k, place) for k in group]), hub_ahead(0))  3.67 us
    pallas_call x1, Pallas kernels, crossed_most(): pl.pallas_call(crossed_kernel, out_shape=(jax.ShapeDtypeStruct((2048, 256...  3.21 us
  transfers between devices with their start and end apart: 31, of which 11 were waited for; matrix products, arithmetic and copies ran while one was open for 6% of the time, Pallas kernels for 7%

profile of v1, /device:TPU:1, one launch (start us, length us, event | category | flops | bytes accessed | tf_op | source)
XLA Modules:
  0.0 121.0 jit_solution(3074669178032397487)
XLA Ops:
  0.6 1.1 select_bitcast_fusion.1
  1.7 6.2 %collective-permute-start = (bf16[2,64,1024]{2,1,0:T(8,128)(2,1)S(1)}, bf16[2,64,1024]{2,1,0:T(8,128)(2,1)S(1)}, u32[]{:S(2)}, u32[]{:S(2)}) collective-permute-start(bf16[2,64,1024]{2,1,0:T(8,128)(2,1)S(1)} %get-tuple-element.14), channel_id=1, source_target_pairs={{0,0},{1,16},{2,2},{3,18},{4,4},{5,20},{6,6},{7,22},{8,8},{9,24},{... | collective-permute-start | bytes 786440 | tf_op jit(solution)/shard_map/ppermute | solution.py:26
  7.9 0.1 collective-permute-start.1
  8.1 3.9 %collective-permute-done = bf16[2,64,1024]{2,1,0:T(8,128)(2,1)S(1)} collective-permute-done((bf16[2,64,1024]{2,1,0:T(8,128)(2,1)S(1)}, bf16[2,64,1024]{2,1,0:T(8,128)(2,1)S(1)}, u32[]{:S(2)}, u32[]{:S(2)}) %collective-permute-start) | collective-permute-done | bytes 262176 | tf_op jit(solution)/shard_map/ppermute | solution.py:26
  12.0 2.1 %collective-permute-done.1 = bf16[2,64,1024]{2,1,0:T(8,128)(2,1)S(1)} collective-permute-done((bf16[2,64,1024]{2,1,0:T(8,128)(2,1)S(1)}, bf16[2,64,1024]{2,1,0:T(8,128)(2,1)S(1)}, u32[]{:S(2)}, u32[]{:S(2)}) %collective-permute-start.1) | collective-permute-done | bytes 262176 | tf_op jit(solution)/shard_map/ppermute | solution.py:26
  14.0 0.1 maximum_select_fusion.own.refs_8_
  14.2 5.7 %collective-permute-start.8 = (bf16[2,128,1024]{2,1,0:T(8,128)(2,1)S(1)}, bf16[2,128,1024]{2,1,0:T(8,128)(2,1)S(1)}, u32[]{:S(2)}, u32[]{:S(2)}) collective-permute-start(bf16[2,128,1024]{2,1,0:T(8,128)(2,1)S(1)} %maximum_select_fusion.own.refs_8_), channel_id=1, source_target_pairs={{0,14},{1,15},{2,0},{3,1},{4,2},{5,3},{6,4},{7,5},{8,6},{9,7},{10,... | collective-permute-start | bytes 1572872 | tf_op jit(solution)/shard_map/ppermute | solution.py:26
  19.8 1.7 %collective-permute-start.2 = (bf16[2,128,1024]{2,1,0:T(8,128)(2,1)S(1)}, bf16[2,128,1024]{2,1,0:T(8,128)(2,1)S(1)}, u32[]{:S(2)}, u32[]{:S(2)}) collective-permute-start(bf16[2,128,1024]{2,1,0:T(8,128)(2,1)S(1)} %maximum_select_fusion.own.refs_8_), channel_id=1, source_target_pairs={{0,16},{1,17},{2,18},{3,19},{4,20},{5,21},{6,22},{7,23},{8,24},{9,... | collective-permute-start | bytes 1572872 | tf_op jit(solution)/shard_map/ppermute | solution.py:26
  21.5 8.1 %collective-permute-done.8.own_d.refs_10_ = bf16[2,128,1024]{2,1,0:T(8,128)(2,1)S(1)} collective-permute-done((bf16[2,128,1024]{2,1,0:T(8,128)(2,1)S(1)}, bf16[2,128,1024]{2,1,0:T(8,128)(2,1)S(1)}, u32[]{:S(2)}, u32[]{:S(2)}) %collective-permute-start.8) | collective-permute-done | bytes 524320 | tf_op jit(solution)/shard_map/ppermute | solution.py:26
  29.6 3.4 %collective-permute-start.9 = (bf16[2,128,1024]{2,1,0:T(8,128)(2,1)S(1)}, bf16[2,128,1024]{2,1,0:T(8,128)(2,1)}, u32[]{:S(2)}, u32[]{:S(2)}) collective-permute-start(bf16[2,128,1024]{2,1,0:T(8,128)(2,1)S(1)} %collective-permute-done.8.own_d.refs_10_), channel_id=1, source_target_pairs={{0,14},{1,15},{2,0},{3,1},{4,2},{5,3},{6,4},{7,5},{8,6},{9,7},{10,... | collective-permute-start | bytes 1572872 | tf_op jit(solution)/shard_map/ppermute | solution.py:26
  33.0 2.6 %collective-permute-start.19 = (bf16[2,128,1024]{2,1,0:T(8,128)(2,1)S(1)}, bf16[2,128,1024]{2,1,0:T(8,128)(2,1)}, u32[]{:S(2)}, u32[]{:S(2)}) collective-permute-start(bf16[2,128,1024]{2,1,0:T(8,128)(2,1)S(1)} %collective-permute-done.8.own_d.refs_10_), channel_id=1, source_target_pairs={{0,16},{1,17},{2,18},{3,19},{4,20},{5,21},{6,22},{7,23},{8,24},{9,... | collective-permute-start | bytes 1572872 | tf_op jit(solution)/shard_map/ppermute | solution.py:26
  35.7 0.0 collective-permute-start.18
  35.7 0.7 copy-done
  36.3 0.6 constant_dynamic-slice_fusion
  38.3 0.1 collective-permute-start.5
  38.4 0.9 broadcast_select_fusion
  39.3 1.2 %collective-permute-start.3 = (bf16[2,128,1024]{2,1,0:T(8,128)(2,1)}, bf16[2,128,1024]{2,1,0:T(8,128)(2,1)S(1)}, u32[]{:S(2)}, u32[]{:S(2)}) collective-permute-start(bf16[2,128,1024]{2,1,0:T(8,128)(2,1)} %broadcast_select_fusion), channel_id=1, source_target_pairs={{0,1},{1,32},{2,3},{3,34},{4,5},{5,36},{6,7},{7,38},{8,9},{9,40},{... | collective-permute-start | bytes 1572872 | tf_op jit(solution)/shard_map/ppermute | solution.py:26
  40.5 0.7 dynamic-slice_select_fusion
  41.2 0.7 collective-permute-done.9.own_d.refs_12_
  41.9 3.5 %collective-permute-start.10 = (bf16[2,128,1024]{2,1,0:T(8,128)(2,1)}, bf16[2,128,1024]{2,1,0:T(8,128)(2,1)S(1)}, u32[]{:S(2)}, u32[]{:S(2)}) collective-permute-start(bf16[2,128,1024]{2,1,0:T(8,128)(2,1)} %collective-permute-done.9.own_d.refs_12_), channel_id=1, source_target_pairs={{0,14},{1,15},{2,0},{3,1},{4,2},{5,3},{6,4},{7,5},{8,6},{9,7},{10,... | collective-permute-start | bytes 1572872 | tf_op jit(solution)/shard_map/ppermute | solution.py:26
  45.4 3.6 %collective-permute-start.17 = (bf16[2,128,1024]{2,1,0:T(8,128)(2,1)}, bf16[2,128,1024]{2,1,0:T(8,128)(2,1)}, u32[]{:S(2)}, u32[]{:S(2)}) collective-permute-start(bf16[2,128,1024]{2,1,0:T(8,128)(2,1)} %collective-permute-done.9.own_d.refs_12_), channel_id=1, source_target_pairs={{0,16},{1,17},{2,18},{3,19},{4,20},{5,21},{6,22},{7,23},{8,24},{9,... | collective-permute-start | bytes 1572872 | tf_op jit(solution)/shard_map/ppermute | solution.py:26
  49.0 0.9 select_bitcast_fusion.6
  49.8 0.9 select_bitcast_fusion.7
  50.7 1.3 %collective-permute-start.20 = (bf16[3,2,128,128]{3,2,1,0:T(8,128)(2,1)S(1)}, bf16[3,2,128,128]{3,2,1,0:T(8,128)(2,1)S(1)}, u32[]{:S(2)}, u32[]{:S(2)}) collective-permute-start(bf16[3,2,128,128]{3,2,1,0:T(8,128)(2,1)S(1)} %pad_maximum_fusion), channel_id=1, source_target_pairs={{0,1},{1,32},{2,3},{3,34},{4,5},{5,36},{6,7},{7,38},{8,9},{9,40},{... | collective-permute-start | bytes 589832 | tf_op jit(solution)/shard_map/ppermute | solution.py:26
  52.0 0.6 collective-permute-done.5.own_u.refs_11_
  52.7 1.4 %collective-permute-start.16 = (bf16[2,128,1024]{2,1,0:T(8,128)(2,1)}, bf16[2,128,1024]{2,1,0:T(8,128)(2,1)}, u32[]{:S(2)}, u32[]{:S(2)}) collective-permute-start(bf16[2,128,1024]{2,1,0:T(8,128)(2,1)} %collective-permute-done.5.own_u.refs_11_), channel_id=1, source_target_pairs={{0,16},{1,17},{2,18},{3,19},{4,20},{5,21},{6,22},{7,23},{8,24},{9,... | collective-permute-start | bytes 1572872 | tf_op jit(solution)/shard_map/ppermute | solution.py:26
  55.3 0.1 stack.158.info
  55.4 0.1 stack.157.info
  55.5 0.1 stack.156.info
  55.5 0.1 stack.155.info
  55.6 2.3 %collective-permute-start.23 = (bf16[2,128,128]{2,1,0:T(8,128)(2,1)}, bf16[2,128,128]{2,1,0:T(8,128)(2,1)S(1)}, u32[]{:S(2)}, u32[]{:S(2)}) collective-permute-start(bf16[2,128,128]{2,1,0:T(8,128)(2,1)} %get-tuple-element.12), channel_id=1, source_target_pairs={{0,9},{1,40},{2,11},{3,42},{4,13},{5,44},{6,15},{7,46},{8,1},{9,32... | collective-permute-start | bytes 196616 | tf_op jit(solution)/shard_map/ppermute | solution.py:26
  58.0 0.8 shard_map.41.acc_in
  58.8 1.7 %shard_map.42.acc_in = f32[256,1024]{1,0:T(8,128)S(1)} custom-call(s32[12]{0:T(128)S(1)} %stack.158.info, bf16[2,128,1024]{2,1,0:T(8,128)(2,1)S(1)} %collective-permute-done.3.a_ref, bf16[2,128,1024]{2,1,0:T(8,128)(2,1)S(1)} %collective-permute-done.4.own_u.refs_9_, ...), custom_call_target="tpu_custom_call", output_to_operand_aliasing={{}: (6, {})} | custom-call | flops 268435456 | bytes 4194304 | tf_op jit(solution)/shard_map/pallas_call | solution.py:104
  60.5 0.1 collective-permute-start.6
  60.7 4.6 %collective-permute-start.15 = (bf16[2,128,1024]{2,1,0:T(8,128)(2,1)S(1)}, bf16[2,128,1024]{2,1,0:T(8,128)(2,1)S(1)}, u32[]{:S(2)}, u32[]{:S(2)}) collective-permute-start(bf16[2,128,1024]{2,1,0:T(8,128)(2,1)S(1)} %collective-permute-done.10.own_d.refs_14_), channel_id=1, source_target_pairs={{0,16},{1,17},{2,18},{3,19},{4,20},{5,21},{6,22},{7,23},{8,24},{9,... | collective-permute-start | bytes 1572872 | tf_op jit(solution)/shard_map/ppermute | solution.py:26
  65.2 0.9 select_bitcast_fusion.4
  66.1 0.9 select_bitcast_fusion.5
  67.1 0.1 collective-permute-start.21
  67.1 7.6 %collective-permute-done.6.own_u.refs_13_ = bf16[2,128,1024]{2,1,0:T(8,128)(2,1)S(1)} collective-permute-done((bf16[2,128,1024]{2,1,0:T(8,128)(2,1)}, bf16[2,128,1024]{2,1,0:T(8,128)(2,1)S(1)}, u32[]{:S(2)}, u32[]{:S(2)}) %collective-permute-start.6) | collective-permute-done | bytes 524320 | tf_op jit(solution)/shard_map/ppermute | solution.py:26
  74.8 2.6 %collective-permute-start.14 = (bf16[2,128,1024]{2,1,0:T(8,128)(2,1)S(1)}, bf16[2,128,1024]{2,1,0:T(8,128)(2,1)S(1)}, u32[]{:S(2)}, u32[]{:S(2)}) collective-permute-start(bf16[2,128,1024]{2,1,0:T(8,128)(2,1)S(1)} %collective-permute-done.6.own_u.refs_13_), channel_id=1, source_target_pairs={{0,16},{1,17},{2,18},{3,19},{4,20},{5,21},{6,22},{7,23},{8,24},{9,... | collective-permute-start | bytes 1572872 | tf_op jit(solution)/shard_map/ppermute | solution.py:26
  77.4 0.1 collective-permute-start.7
  77.4 2.0 %shard_map.43.acc_in = f32[256,1024]{1,0:T(8,128)S(1)} custom-call(s32[12]{0:T(128)S(1)} %stack.157.info, bf16[2,128,1024]{2,1,0:T(8,128)(2,1)S(1)} %collective-permute-done.3.a_ref, bf16[2,128,1024]{2,1,0:T(8,128)(2,1)} %collective-permute-done.5.own_u.refs_11_, ...), custom_call_target="tpu_custom_call", output_to_operand_aliasing={{}: (6, {})} | custom-call | flops 268435456 | bytes 4194304 | tf_op jit(solution)/shard_map/pallas_call | solution.py:104
  79.5 2.7 %collective-permute-start.11 = (bf16[128,1024]{1,0:T(8,128)(2,1)S(1)}, bf16[128,1024]{1,0:T(8,128)(2,1)S(1)}, u32[]{:S(2)}, u32[]{:S(2)}) collective-permute-start(bf16[128,1024]{1,0:T(8,128)(2,1)S(1)} %slice_bitcast_fusion), channel_id=1, source_target_pairs={{0,14},{1,15},{2,0},{3,1},{4,2},{5,3},{6,4},{7,5},{8,6},{9,7},{10,... | collective-permute-start | bytes 786440 | tf_op jit(solution)/shard_map/ppermute | solution.py:26
  82.3 1.2 collective-permute-start.22
  83.5 3.1 %collective-permute-done.7.own_re = bf16[128,1024]{1,0:T(8,128)(2,1)S(1)} collective-permute-done((bf16[128,1024]{1,0:T(8,128)(2,1)S(1)}, bf16[128,1024]{1,0:T(8,128)(2,1)S(1)}, u32[]{:S(2)}, u32[]{:S(2)}) %collective-permute-start.7) | collective-permute-done | bytes 262176 | tf_op jit(solution)/shard_map/ppermute | solution.py:26
  86.6 0.8 collective-permute-start.12
  87.4 0.3 collective-permute-done.11.own_im
  87.6 1.1 collective-permute-start.13
  88.7 1.0 shard_map.44.acc
  89.8 3.2 %shard_map.45 = (bf16[2048,256]{1,0:T(8,128)(2,1)S(1)}, bf16[256,1024]{1,0:T(8,128)(2,1)S(1)}) custom-call(s32[12]{0:T(128)S(1)} %stack.155.info, bf16[2,128,128]{2,1,0:T(8,128)(2,1)S(1)} %get-tuple-element.18.refs_0_, bf16[2,128,128]{2,1,0:T(8,128)(2,1)S(1)} %get-tuple-element.17.refs_1_, bf16[2,128,128]{2,1,0:T(8,128)(2,1)S(1)} %get-tuple-element.16.refs_2_, ...), custom_call_target="tpu_custom_call" | custom-call | flops 939524096 | bytes 4194304 | tf_op jit(solution)/shard_map/pallas_call | solution.py:139
  93.0 1.5 %shard_map.46 = (bf16[2,64,1024]{2,1,0:T(8,128)(2,1)S(1)}, bf16[2,64,1024]{2,1,0:T(8,128)(2,1)S(1)}, f32[1,128]{1,0:T(1,128)S(1)}) custom-call(s32[12]{0:T(128)S(1)} %stack.155.info, bf16[2,128,1024]{2,1,0:T(8,128)(2,1)S(1)} %collective-permute-done.3.a_ref, bf16[128,1024]{1,0:T(8,128)(2,1)S(1)} %collective-permute-done.7.own_re, ...), custom_call_target="tpu_custom_call" | custom-call | flops 268435456 | bytes 4194304 | tf_op jit(solution)/shard_map/pallas_call | solution.py:175
  94.5 0.0 collective-permute-start.26
  94.5 2.4 %collective-permute-done.26 = f32[1,128]{1,0:T(1,128)S(1)} collective-permute-done((f32[1,128]{1,0:T(1,128)S(1)}, f32[1,128]{1,0:T(1,128)S(1)}, u32[]{:S(2)}, u32[]{:S(2)}) %collective-permute-start.26) | collective-permute-done | bytes 544 | tf_op jit(solution)/shard_map/ppermute | solution.py:26
  96.9 3.1 %collective-permute-start.27 = (f32[1,128]{1,0:T(1,128)S(1)}, f32[1,128]{1,0:T(1,128)S(1)}, u32[]{:S(2)}, u32[]{:S(2)}) collective-permute-start(f32[1,128]{1,0:T(1,128)S(1)} %add.105), channel_id=1, source_target_pairs={{0,4},{1,5},{2,6},{3,7},{4,0},{5,1},{6,2},{7,3},{8,12},{9,13},{10,... | collective-permute-start | bytes 1544 | tf_op jit(solution)/shard_map/ppermute | solution.py:26
  100.0 0.9 collective-permute-done.27
  101.0 2.5 %collective-permute-start.28 = (f32[1,128]{1,0:T(1,128)S(1)}, f32[1,128]{1,0:T(1,128)S(1)}, u32[]{:S(2)}, u32[]{:S(2)}) collective-permute-start(f32[1,128]{1,0:T(1,128)S(1)} %add.106), channel_id=1, source_target_pairs={{0,8},{1,9},{2,10},{3,11},{4,12},{5,13},{6,14},{7,15},{8,0},{9,1},... | collective-permute-start | bytes 1544 | tf_op jit(solution)/shard_map/ppermute | solution.py:26
  103.5 5.0 %collective-permute-start.24 = (bf16[2,64,1024]{2,1,0:T(8,128)(2,1)S(1)}, bf16[2,64,1024]{2,1,0:T(8,128)(2,1)S(1)}, u32[]{:S(2)}, u32[]{:S(2)}) collective-permute-start(bf16[2,64,1024]{2,1,0:T(8,128)(2,1)S(1)} %get-tuple-element.9), channel_id=1, source_target_pairs={{0,240},{1,0},{2,242},{3,2},{4,244},{5,4},{6,246},{7,6},{8,248},{9... | collective-permute-start | bytes 786440 | tf_op jit(solution)/shard_map/ppermute | solution.py:26
  108.5 2.1 %collective-permute-start.25 = (bf16[2,64,1024]{2,1,0:T(8,128)(2,1)S(1)}, bf16[2,64,1024]{2,1,0:T(8,128)(2,1)S(1)}, u32[]{:S(2)}, u32[]{:S(2)}) collective-permute-start(bf16[2,64,1024]{2,1,0:T(8,128)(2,1)S(1)} %get-tuple-element.10), channel_id=1, source_target_pairs={{0,241},{1,1},{2,243},{3,3},{4,245},{5,5},{6,247},{7,7},{8,249},{9... | collective-permute-start | bytes 786440 | tf_op jit(solution)/shard_map/ppermute | solution.py:26
  110.7 1.9 %collective-permute-start.29 = (f32[2]{0:T(128)S(1)}, f32[2]{0:T(128)S(1)}, u32[]{:S(2)}, u32[]{:S(2)}) collective-permute-start(f32[2]{0:T(128)S(1)} %multiply_bitcast_fusion), channel_id=1, source_target_pairs={{0,240},{1,0},{2,242},{3,2},{4,244},{5,4},{6,246},{7,6},{8,248},{9... | collective-permute-start | bytes 32 | tf_op jit(solution)/shard_map/ppermute | solution.py:26
  112.6 1.9 %collective-permute-start.30 = (f32[2]{0:T(128)S(1)}, f32[2]{0:T(128)S(1)}, u32[]{:S(2)}, u32[]{:S(2)}) collective-permute-start(f32[2]{0:T(128)S(1)} %multiply_bitcast_fusion), channel_id=1, source_target_pairs={{0,241},{1,1},{2,243},{3,3},{4,245},{5,5},{6,247},{7,7},{8,249},{9... | collective-permute-start | bytes 32 | tf_op jit(solution)/shard_map/ppermute | solution.py:26
  114.5 5.0 %collective-permute-done.29 = f32[2]{0:T(128)S(1)} collective-permute-done((f32[2]{0:T(128)S(1)}, f32[2]{0:T(128)S(1)}, u32[]{:S(2)}, u32[]{:S(2)}) %collective-permute-start.29) | collective-permute-done | bytes 40 | tf_op jit(solution)/shard_map/ppermute | solution.py:26
  119.5 0.0 collective-permute-done.30
  119.5 0.6 broadcast_select_fusion.1
  120.1 0.9 maximum_select_fusion.1
  (35 shorter events, 0.3 us)
Async XLA Ops:
  1.7 10.3 %collective-permute-start = (bf16[2,64,1024]{2,1,0:T(8,128)(2,1)S(1)}, bf16[2,64,1024]{2,1,0:T(8,128)(2,1)S(1)}, u32[]{:S(2)}, u32[]{:S(2)}) collective-permute-start(bf16[2,64,1024]{2,1,0:T(8,128)(2,1)S(1)} %get-tuple-element.14), channel_id=1, source_target_pairs={{0,0},{1,16},{2,2},{3,18},{4,4},{5,20},{6,6},{7,22},{8,8},{9,24},{... | collective-permute-start | bytes 786440 | tf_op jit(solution)/shard_map/ppermute | solution.py:26
  7.9 6.1 %collective-permute-start.1 = (bf16[2,64,1024]{2,1,0:T(8,128)(2,1)S(1)}, bf16[2,64,1024]{2,1,0:T(8,128)(2,1)S(1)}, u32[]{:S(2)}, u32[]{:S(2)}) collective-permute-start(bf16[2,64,1024]{2,1,0:T(8,128)(2,1)S(1)} %get-tuple-element.15), channel_id=1, source_target_pairs={{0,16},{1,0},{2,18},{3,2},{4,20},{5,4},{6,22},{7,6},{8,24},{9,8},{... | collective-permute-start | bytes 786440 | tf_op jit(solution)/shard_map/ppermute | solution.py:26
  14.2 15.4 %collective-permute-start.8 = (bf16[2,128,1024]{2,1,0:T(8,128)(2,1)S(1)}, bf16[2,128,1024]{2,1,0:T(8,128)(2,1)S(1)}, u32[]{:S(2)}, u32[]{:S(2)}) collective-permute-start(bf16[2,128,1024]{2,1,0:T(8,128)(2,1)S(1)} %maximum_select_fusion.own.refs_8_), channel_id=1, source_target_pairs={{0,14},{1,15},{2,0},{3,1},{4,2},{5,3},{6,4},{7,5},{8,6},{9,7},{10,... | collective-permute-start | bytes 1572872 | tf_op jit(solution)/shard_map/ppermute | solution.py:26
  19.8 15.8 %collective-permute-start.4 = (bf16[2,128,1024]{2,1,0:T(8,128)(2,1)S(1)}, bf16[2,128,1024]{2,1,0:T(8,128)(2,1)S(1)}, u32[]{:S(2)}, u32[]{:S(2)}) collective-permute-start(bf16[2,128,1024]{2,1,0:T(8,128)(2,1)S(1)} %maximum_select_fusion.own.refs_8_), channel_id=1, source_target_pairs={{0,2},{1,3},{2,4},{3,5},{4,6},{5,7},{6,8},{7,9},{8,10},{9,11},{10,... | collective-permute-start | bytes 1572872 | tf_op jit(solution)/shard_map/ppermute | solution.py:26
  19.8 18.6 %collective-permute-start.2 = (bf16[2,128,1024]{2,1,0:T(8,128)(2,1)S(1)}, bf16[2,128,1024]{2,1,0:T(8,128)(2,1)S(1)}, u32[]{:S(2)}, u32[]{:S(2)}) collective-permute-start(bf16[2,128,1024]{2,1,0:T(8,128)(2,1)S(1)} %maximum_select_fusion.own.refs_8_), channel_id=1, source_target_pairs={{0,16},{1,17},{2,18},{3,19},{4,20},{5,21},{6,22},{7,23},{8,24},{9,... | collective-permute-start | bytes 1572872 | tf_op jit(solution)/shard_map/ppermute | solution.py:26
  29.6 12.3 %collective-permute-start.9 = (bf16[2,128,1024]{2,1,0:T(8,128)(2,1)S(1)}, bf16[2,128,1024]{2,1,0:T(8,128)(2,1)}, u32[]{:S(2)}, u32[]{:S(2)}) collective-permute-start(bf16[2,128,1024]{2,1,0:T(8,128)(2,1)S(1)} %collective-permute-done.8.own_d.refs_10_), channel_id=1, source_target_pairs={{0,14},{1,15},{2,0},{3,1},{4,2},{5,3},{6,4},{7,5},{8,6},{9,7},{10,... | collective-permute-start | bytes 1572872 | tf_op jit(solution)/shard_map/ppermute | solution.py:26
  33.0 12.4 %collective-permute-start.19 = (bf16[2,128,1024]{2,1,0:T(8,128)(2,1)S(1)}, bf16[2,128,1024]{2,1,0:T(8,128)(2,1)}, u32[]{:S(2)}, u32[]{:S(2)}) collective-permute-start(bf16[2,128,1024]{2,1,0:T(8,128)(2,1)S(1)} %collective-permute-done.8.own_d.refs_10_), channel_id=1, source_target_pairs={{0,16},{1,17},{2,18},{3,19},{4,20},{5,21},{6,22},{7,23},{8,24},{9,... | collective-permute-start | bytes 1572872 | tf_op jit(solution)/shard_map/ppermute | solution.py:26
  35.7 14.2 %collective-permute-start.18 = (bf16[2,128,1024]{2,1,0:T(8,128)(2,1)S(1)}, bf16[2,128,1024]{2,1,0:T(8,128)(2,1)}, u32[]{:S(2)}, u32[]{:S(2)}) collective-permute-start(bf16[2,128,1024]{2,1,0:T(8,128)(2,1)S(1)} %collective-permute-done.4.own_u.refs_9_), channel_id=1, source_target_pairs={{0,16},{1,17},{2,18},{3,19},{4,20},{5,21},{6,22},{7,23},{8,24},{9,... | collective-permute-start | bytes 1572872 | tf_op jit(solution)/shard_map/ppermute | solution.py:26
  35.7 0.7 copy-start
  38.3 14.4 %collective-permute-start.5 = (bf16[2,128,1024]{2,1,0:T(8,128)(2,1)S(1)}, bf16[2,128,1024]{2,1,0:T(8,128)(2,1)}, u32[]{:S(2)}, u32[]{:S(2)}) collective-permute-start(bf16[2,128,1024]{2,1,0:T(8,128)(2,1)S(1)} %collective-permute-done.4.own_u.refs_9_), channel_id=1, source_target_pairs={{0,2},{1,3},{2,4},{3,5},{4,6},{5,7},{6,8},{7,9},{8,10},{9,11},{10,... | collective-permute-start | bytes 1572872 | tf_op jit(solution)/shard_map/ppermute | solution.py:26
  39.3 16.4 %collective-permute-start.3 = (bf16[2,128,1024]{2,1,0:T(8,128)(2,1)}, bf16[2,128,1024]{2,1,0:T(8,128)(2,1)S(1)}, u32[]{:S(2)}, u32[]{:S(2)}) collective-permute-start(bf16[2,128,1024]{2,1,0:T(8,128)(2,1)} %broadcast_select_fusion), channel_id=1, source_target_pairs={{0,1},{1,32},{2,3},{3,34},{4,5},{5,36},{6,7},{7,38},{8,9},{9,40},{... | collective-permute-start | bytes 1572872 | tf_op jit(solution)/shard_map/ppermute | solution.py:26
  41.9 18.8 %collective-permute-start.10 = (bf16[2,128,1024]{2,1,0:T(8,128)(2,1)}, bf16[2,128,1024]{2,1,0:T(8,128)(2,1)S(1)}, u32[]{:S(2)}, u32[]{:S(2)}) collective-permute-start(bf16[2,128,1024]{2,1,0:T(8,128)(2,1)} %collective-permute-done.9.own_d.refs_12_), channel_id=1, source_target_pairs={{0,14},{1,15},{2,0},{3,1},{4,2},{5,3},{6,4},{7,5},{8,6},{9,7},{10,... | collective-permute-start | bytes 1572872 | tf_op jit(solution)/shard_map/ppermute | solution.py:26
  45.4 19.8 %collective-permute-start.17 = (bf16[2,128,1024]{2,1,0:T(8,128)(2,1)}, bf16[2,128,1024]{2,1,0:T(8,128)(2,1)}, u32[]{:S(2)}, u32[]{:S(2)}) collective-permute-start(bf16[2,128,1024]{2,1,0:T(8,128)(2,1)} %collective-permute-done.9.own_d.refs_12_), channel_id=1, source_target_pairs={{0,16},{1,17},{2,18},{3,19},{4,20},{5,21},{6,22},{7,23},{8,24},{9,... | collective-permute-start | bytes 1572872 | tf_op jit(solution)/shard_map/ppermute | solution.py:26
  50.7 9.8 %collective-permute-start.20 = (bf16[3,2,128,128]{3,2,1,0:T(8,128)(2,1)S(1)}, bf16[3,2,128,128]{3,2,1,0:T(8,128)(2,1)S(1)}, u32[]{:S(2)}, u32[]{:S(2)}) collective-permute-start(bf16[3,2,128,128]{3,2,1,0:T(8,128)(2,1)S(1)} %pad_maximum_fusion), channel_id=1, source_target_pairs={{0,1},{1,32},{2,3},{3,34},{4,5},{5,36},{6,7},{7,38},{8,9},{9,40},{... | collective-permute-start | bytes 589832 | tf_op jit(solution)/shard_map/ppermute | solution.py:26
  52.7 13.4 %collective-permute-start.16 = (bf16[2,128,1024]{2,1,0:T(8,128)(2,1)}, bf16[2,128,1024]{2,1,0:T(8,128)(2,1)}, u32[]{:S(2)}, u32[]{:S(2)}) collective-permute-start(bf16[2,128,1024]{2,1,0:T(8,128)(2,1)} %collective-permute-done.5.own_u.refs_11_), channel_id=1, source_target_pairs={{0,16},{1,17},{2,18},{3,19},{4,20},{5,21},{6,22},{7,23},{8,24},{9,... | collective-permute-start | bytes 1572872 | tf_op jit(solution)/shard_map/ppermute | solution.py:26
  55.6 34.1 %collective-permute-start.23 = (bf16[2,128,128]{2,1,0:T(8,128)(2,1)}, bf16[2,128,128]{2,1,0:T(8,128)(2,1)S(1)}, u32[]{:S(2)}, u32[]{:S(2)}) collective-permute-start(bf16[2,128,128]{2,1,0:T(8,128)(2,1)} %get-tuple-element.12), channel_id=1, source_target_pairs={{0,9},{1,40},{2,11},{3,42},{4,13},{5,44},{6,15},{7,46},{8,1},{9,32... | collective-permute-start | bytes 196616 | tf_op jit(solution)/shard_map/ppermute | solution.py:26
  60.5 14.2 %collective-permute-start.6 = (bf16[2,128,1024]{2,1,0:T(8,128)(2,1)}, bf16[2,128,1024]{2,1,0:T(8,128)(2,1)S(1)}, u32[]{:S(2)}, u32[]{:S(2)}) collective-permute-start(bf16[2,128,1024]{2,1,0:T(8,128)(2,1)} %collective-permute-done.5.own_u.refs_11_), channel_id=1, source_target_pairs={{0,2},{1,3},{2,4},{3,5},{4,6},{5,7},{6,8},{7,9},{8,10},{9,11},{10,... | collective-permute-start | bytes 1572872 | tf_op jit(solution)/shard_map/ppermute | solution.py:26
  60.7 18.8 %collective-permute-start.15 = (bf16[2,128,1024]{2,1,0:T(8,128)(2,1)S(1)}, bf16[2,128,1024]{2,1,0:T(8,128)(2,1)S(1)}, u32[]{:S(2)}, u32[]{:S(2)}) collective-permute-start(bf16[2,128,1024]{2,1,0:T(8,128)(2,1)S(1)} %collective-permute-done.10.own_d.refs_14_), channel_id=1, source_target_pairs={{0,16},{1,17},{2,18},{3,19},{4,20},{5,21},{6,22},{7,23},{8,24},{9,... | collective-permute-start | bytes 1572872 | tf_op jit(solution)/shard_map/ppermute | solution.py:26
  67.1 16.4 %collective-permute-start.21 = (bf16[2,2,128,128]{3,2,1,0:T(8,128)(2,1)S(1)}, bf16[2,2,128,128]{3,2,1,0:T(8,128)(2,1)S(1)}, u32[]{:S(2)}, u32[]{:S(2)}) collective-permute-start(bf16[2,2,128,128]{3,2,1,0:T(8,128)(2,1)S(1)} %pad_maximum_fusion.1), channel_id=1, source_target_pairs={{0,1},{1,32},{2,3},{3,34},{4,5},{5,36},{6,7},{7,38},{8,9},{9,40},{... | collective-permute-start | bytes 393224 | tf_op jit(solution)/shard_map/ppermute | solution.py:26
  74.8 7.5 %collective-permute-start.14 = (bf16[2,128,1024]{2,1,0:T(8,128)(2,1)S(1)}, bf16[2,128,1024]{2,1,0:T(8,128)(2,1)S(1)}, u32[]{:S(2)}, u32[]{:S(2)}) collective-permute-start(bf16[2,128,1024]{2,1,0:T(8,128)(2,1)S(1)} %collective-permute-done.6.own_u.refs_13_), channel_id=1, source_target_pairs={{0,16},{1,17},{2,18},{3,19},{4,20},{5,21},{6,22},{7,23},{8,24},{9,... | collective-permute-start | bytes 1572872 | tf_op jit(solution)/shard_map/ppermute | solution.py:26
  77.4 9.2 %collective-permute-start.7 = (bf16[128,1024]{1,0:T(8,128)(2,1)S(1)}, bf16[128,1024]{1,0:T(8,128)(2,1)S(1)}, u32[]{:S(2)}, u32[]{:S(2)}) collective-permute-start(bf16[128,1024]{1,0:T(8,128)(2,1)S(1)} %slice_bitcast_fusion.1), channel_id=1, source_target_pairs={{0,2},{1,3},{2,4},{3,5},{4,6},{5,7},{6,8},{7,9},{8,10},{9,11},{10,... | collective-permute-start | bytes 786440 | tf_op jit(solution)/shard_map/ppermute | solution.py:26
  79.5 8.1 %collective-permute-start.11 = (bf16[128,1024]{1,0:T(8,128)(2,1)S(1)}, bf16[128,1024]{1,0:T(8,128)(2,1)S(1)}, u32[]{:S(2)}, u32[]{:S(2)}) collective-permute-start(bf16[128,1024]{1,0:T(8,128)(2,1)S(1)} %slice_bitcast_fusion), channel_id=1, source_target_pairs={{0,14},{1,15},{2,0},{3,1},{4,2},{5,3},{6,4},{7,5},{8,6},{9,7},{10,... | collective-permute-start | bytes 786440 | tf_op jit(solution)/shard_map/ppermute | solution.py:26
  82.3 7.4 %collective-permute-start.22 = (bf16[2,2,128,128]{3,2,1,0:T(8,128)(2,1)S(1)}, bf16[2,2,128,128]{3,2,1,0:T(8,128)(2,1)S(1)}, u32[]{:S(2)}, u32[]{:S(2)}) collective-permute-start(bf16[2,2,128,128]{3,2,1,0:T(8,128)(2,1)S(1)} %pad_maximum_fusion.2), channel_id=1, source_target_pairs={{0,1},{1,32},{2,3},{3,34},{4,5},{5,36},{6,7},{7,38},{8,9},{9,40},{... | collective-permute-start | bytes 393224 | tf_op jit(solution)/shard_map/ppermute | solution.py:26
  86.6 6.4 %collective-permute-start.12 = (bf16[128,1024]{1,0:T(8,128)(2,1)S(1)}, bf16[128,1024]{1,0:T(8,128)(2,1)S(1)}, u32[]{:S(2)}, u32[]{:S(2)}) collective-permute-start(bf16[128,1024]{1,0:T(8,128)(2,1)S(1)} %collective-permute-done.7.own_re), channel_id=1, source_target_pairs={{0,16},{1,17},{2,18},{3,19},{4,20},{5,21},{6,22},{7,23},{8,24},{9,... | collective-permute-start | bytes 786440 | tf_op jit(solution)/shard_map/ppermute | solution.py:26
  87.6 5.4 %collective-permute-start.13 = (bf16[128,1024]{1,0:T(8,128)(2,1)S(1)}, bf16[128,1024]{1,0:T(8,128)(2,1)S(1)}, u32[]{:S(2)}, u32[]{:S(2)}) collective-permute-start(bf16[128,1024]{1,0:T(8,128)(2,1)S(1)} %collective-permute-done.11.own_im), channel_id=1, source_target_pairs={{0,16},{1,17},{2,18},{3,19},{4,20},{5,21},{6,22},{7,23},{8,24},{9,... | collective-permute-start | bytes 786440 | tf_op jit(solution)/shard_map/ppermute | solution.py:26
  94.5 2.4 %collective-permute-start.26 = (f32[1,128]{1,0:T(1,128)S(1)}, f32[1,128]{1,0:T(1,128)S(1)}, u32[]{:S(2)}, u32[]{:S(2)}) collective-permute-start(f32[1,128]{1,0:T(1,128)S(1)} %get-tuple-element.11), channel_id=1, source_target_pairs={{0,2},{1,3},{2,0},{3,1},{4,6},{5,7},{6,4},{7,5},{8,10},{9,11},{10,... | collective-permute-start | bytes 1544 | tf_op jit(solution)/shard_map/ppermute | solution.py:26
  96.9 4.0 %collective-permute-start.27 = (f32[1,128]{1,0:T(1,128)S(1)}, f32[1,128]{1,0:T(1,128)S(1)}, u32[]{:S(2)}, u32[]{:S(2)}) collective-permute-start(f32[1,128]{1,0:T(1,128)S(1)} %add.105), channel_id=1, source_target_pairs={{0,4},{1,5},{2,6},{3,7},{4,0},{5,1},{6,2},{7,3},{8,12},{9,13},{10,... | collective-permute-start | bytes 1544 | tf_op jit(solution)/shard_map/ppermute | solution.py:26
  101.0 9.7 %collective-permute-start.28 = (f32[1,128]{1,0:T(1,128)S(1)}, f32[1,128]{1,0:T(1,128)S(1)}, u32[]{:S(2)}, u32[]{:S(2)}) collective-permute-start(f32[1,128]{1,0:T(1,128)S(1)} %add.106), channel_id=1, source_target_pairs={{0,8},{1,9},{2,10},{3,11},{4,12},{5,13},{6,14},{7,15},{8,0},{9,1},... | collective-permute-start | bytes 1544 | tf_op jit(solution)/shard_map/ppermute | solution.py:26
  103.5 16.6 %collective-permute-start.24 = (bf16[2,64,1024]{2,1,0:T(8,128)(2,1)S(1)}, bf16[2,64,1024]{2,1,0:T(8,128)(2,1)S(1)}, u32[]{:S(2)}, u32[]{:S(2)}) collective-permute-start(bf16[2,64,1024]{2,1,0:T(8,128)(2,1)S(1)} %get-tuple-element.9), channel_id=1, source_target_pairs={{0,240},{1,0},{2,242},{3,2},{4,244},{5,4},{6,246},{7,6},{8,248},{9... | collective-permute-start | bytes 786440 | tf_op jit(solution)/shard_map/ppermute | solution.py:26
  108.5 11.6 %collective-permute-start.25 = (bf16[2,64,1024]{2,1,0:T(8,128)(2,1)S(1)}, bf16[2,64,1024]{2,1,0:T(8,128)(2,1)S(1)}, u32[]{:S(2)}, u32[]{:S(2)}) collective-permute-start(bf16[2,64,1024]{2,1,0:T(8,128)(2,1)S(1)} %get-tuple-element.10), channel_id=1, source_target_pairs={{0,241},{1,1},{2,243},{3,3},{4,245},{5,5},{6,247},{7,7},{8,249},{9... | collective-permute-start | bytes 786440 | tf_op jit(solution)/shard_map/ppermute | solution.py:26
  110.7 8.9 %collective-permute-start.29 = (f32[2]{0:T(128)S(1)}, f32[2]{0:T(128)S(1)}, u32[]{:S(2)}, u32[]{:S(2)}) collective-permute-start(f32[2]{0:T(128)S(1)} %multiply_bitcast_fusion), channel_id=1, source_target_pairs={{0,240},{1,0},{2,242},{3,2},{4,244},{5,4},{6,246},{7,6},{8,248},{9... | collective-permute-start | bytes 32 | tf_op jit(solution)/shard_map/ppermute | solution.py:26
  112.6 6.9 %collective-permute-start.30 = (f32[2]{0:T(128)S(1)}, f32[2]{0:T(128)S(1)}, u32[]{:S(2)}, u32[]{:S(2)}) collective-permute-start(f32[2]{0:T(128)S(1)} %multiply_bitcast_fusion), channel_id=1, source_target_pairs={{0,241},{1,1},{2,243},{3,3},{4,245},{5,5},{6,247},{7,7},{8,249},{9... | collective-permute-start | bytes 32 | tf_op jit(solution)/shard_map/ppermute | solution.py:26

commit v2 on v0

v2 whole, which is shorter than its diff:
```python
import jax
import jax.numpy as jnp
from jax import lax
from jax.experimental import pallas as pl
from jax.experimental.pallas import tpu as pltpu
from jax.sharding import PartitionSpec as P

BOTH = ("tm", "row")
BF16 = jnp.bfloat16
F32 = jnp.float32


def hub_of(s):
    m, odd = divmod(s % 16, 2)
    low, x = divmod(m, 4)
    return (1 - low) * 4 + x, odd ^ low


SERVED = {hub_of(s): s for s in range(16)}


def moved(block, route):
    def index_of(m, c, z, h):
        return ((m % 8) * 2 + c) * 16 + (z % 8) * 2 + h

    places = [(m, c, z, h) for m in range(8) for c in range(2) for z in range(8) for h in range(2)]
    return lax.ppermute(block, BOTH, [(index_of(*at), index_of(*route(*at))) for at in places])


def along(step):
    return lambda m, c, z, h: (m, c, z + step, h)


def other_core(m, c, z, h):
    return (m, 1 - c, z, h)


def to_hub(step):
    def route(m, c, z, h):
        column, half = hub_of(2 * m + c)
        return (column, h, z + step, half)

    return route


def hub_ahead(step):
    def route(m, c, z, h):
        column, half = hub_of(SERVED[m, h] + 1 + c)
        return (column, c, z + step, half)

    return route


def from_hub(turn):
    def route(m, c, z, h):
        t = (SERVED[m, h] - 1 - c) % 16
        return (t // 2, t % 2, z, c ^ turn)

    return route


VMEM = pl.BlockSpec(memory_space=pltpu.VMEM)
SMEM = pl.BlockSpec(memory_space=pltpu.SMEM)
SLICES = jax.ShapeDtypeStruct((2, 128, 128), BF16)


def call(kernel, info, arrays, out_shape, flops, scratch=()):
    outs = jax.tree.map(lambda _: VMEM, out_shape)
    return pl.pallas_call(
        kernel,
        out_shape=out_shape,
        in_specs=[SMEM] + [VMEM] * len(arrays),
        out_specs=outs,
        scratch_shapes=scratch,
        compiler_params=pltpu.CompilerParams(vmem_limit_bytes=24 * 1024 * 1024),
        cost_estimate=pl.CostEstimate(flops=flops, bytes_accessed=1 << 20, transcendentals=0),
    )(info, *arrays)


def place_of(info, offset):
    return lax.rem(info[0] + (offset + 8), 8)


def columns_of(info, offset):
    return pl.ds(pl.multiple_of(place_of(info, offset) * 128, 128), 128)


def halves(info, own, other):
    first = jnp.where(info[1] == 0, own, other)
    second = jnp.where(info[1] == 0, other, own)
    return first, second


def whole(info, own_ref, other_ref, momentum, part):
    return jnp.concatenate(halves(info, own_ref[momentum, part], other_ref[momentum, part]), axis=0)


def cut(info, own_ref, other_ref, offset, out):
    columns = columns_of(info, offset)
    for part in range(2):
        first, second = halves(info, own_ref[info[5], part, :, columns], other_ref[info[5], part, :, columns])
        out[part, 0:64] = first
        out[part, 64:128] = second


def first_cut_kernel(info, own, other, a, across):
    for part in range(2):
        a[part] = whole(info, own, other, info[2], part)
    cut(info, own, other, 4, across)


def cut_kernel(info, *refs):
    count = len(refs) // 2
    for k in range(count):
        cut(info, refs[k], refs[count + k], 0, refs[-1].at[k])


def left_side(info, a_ref, offset):
    columns = columns_of(info, offset)
    real, imag = a_ref[0, :, columns], a_ref[1, :, columns]
    return jnp.concatenate(
        [jnp.concatenate([real, -imag], axis=1), jnp.concatenate([imag, real], axis=1)], axis=0
    )


def products_kernel(offsets, info, a_ref, *refs):
    count = len(offsets)
    own, other, out = refs[:count], refs[count : 2 * count], refs[-1]
    total = refs[2 * count][...] if len(refs) > 2 * count + 1 else None
    for offset, one, two in zip(offsets, own, other):
        block = jnp.concatenate([whole(info, one, two, info[3], part) for part in range(2)], axis=0)
        term = jnp.dot(left_side(info, a_ref, offset), block, preferred_element_type=F32)
        total = term if total is None else total + term
    out[...] = total


def crossed_block(real, imag, drhs):
    block = jnp.dot(real, drhs[0:1024, :], preferred_element_type=F32)
    block += jnp.dot(imag, drhs[1024:2048, :], preferred_element_type=F32)
    turned = jnp.concatenate([block[:, :128].T, block[:, 128:].T], axis=0)
    return turned.astype(BF16)


OFFSETS = (0, -1, 1, -2, 2, -3, 3, 4)


def crossed_kernel(info, near, late, across, *refs):
    own, other, drhs, crossed = refs[0:7], refs[7:14], refs[14], refs[15]
    slices = [near.at[k] for k in range(3)] + [late.at[k] for k in range(4)] + [across]
    for offset, piece in zip(OFFSETS, slices):
        top = pl.multiple_of(place_of(info, offset) * 128, 128)
        real, imag = piece[0], piece[1]
        drhs[pl.ds(top, 128), 0:128] = real
        drhs[pl.ds(top, 128), 128:256] = imag
        drhs[pl.ds(1024 + top, 128), 0:128] = -imag
        drhs[pl.ds(1024 + top, 128), 128:256] = real
    for offset, one, two in zip(OFFSETS, own, other):
        real, imag = (whole(info, one, two, info[4], part) for part in range(2))
        crossed[:, columns_of(info, offset)] = crossed_block(real, imag, drhs)


def last_kernel(info, a_ref, own_0, own_1, other_0, other_1, acc, drhs, crossed, keep, send, trace, turned):
    def parts(momentum):
        own = jnp.where(momentum == 0, own_0[...], own_1[...])
        other = jnp.where(momentum == 0, other_0[...], other_1[...])
        return [jnp.concatenate(halves(info, own[part], other[part]), axis=0) for part in range(2)]

    block = jnp.concatenate(parts(info[3]), axis=0)
    product = acc[...] + jnp.dot(left_side(info, a_ref, 4), block, preferred_element_type=F32)
    rounded = product.astype(BF16)
    for part in range(2):
        low, high = rounded[part * 128 : part * 128 + 64], rounded[part * 128 + 64 : part * 128 + 128]
        keep[part], send[part] = halves(info, low, high)
    real, imag = parts(info[4])
    turned[...] = crossed[...]
    turned[:, columns_of(info, 4)] = crossed_block(real, imag, drhs)
    p_re, p_im = rounded[:128].astype(F32), rounded[128:].astype(F32)
    c_re, c_im = turned[:128, :].astype(F32), turned[128:, :].astype(F32)
    re = jnp.sum(p_re * c_re - p_im * c_im, axis=0, keepdims=True)
    im = jnp.sum(p_re * c_im + p_im * c_re, axis=0, keepdims=True)
    re = jnp.sum(re, axis=1, keepdims=True)
    im = jnp.sum(im, axis=1, keepdims=True)
    lane = lax.broadcasted_iota(jnp.int32, (1, 128), 1)
    trace[...] = jnp.where(lane == 2 * info[0], re, jnp.where(lane == 2 * info[0] + 1, im, 0.0))


def shards(fields, mom_table):
    rows = fields[:, 0]
    tm, row = lax.axis_index("tm"), lax.axis_index("row")
    core, place, half = tm % 2, row // 2, row % 2
    momenta = lax.dynamic_index_in_dim(mom_table, core, 0, keepdims=False)[0]
    info = jnp.concatenate([jnp.stack([place, core]), momenta])
    wall = lax.optimization_barrier
    block_of_products = jax.ShapeDtypeStruct((256, 1024), F32)

    own = moved(rows, to_hub(0))

    u1, d1, ownx = moved(own, along(1)), moved(own, along(-1)), moved(own, other_core)
    u1, d1, ownx = wall((u1, d1, ownx))

    u2, d2 = moved(u1, along(1)), moved(d1, along(-1))
    u1x, d1x = moved(u1, other_core), moved(d1, other_core)
    a, across = call(first_cut_kernel, info, [own, ownx], (jax.ShapeDtypeStruct((2, 128, 1024), BF16), SLICES), 1)
    a = moved(a, hub_ahead(0))
    u2, d2, u1x, d1x, a, across = wall((u2, d2, u1x, d1x, a, across))

    u3, d3 = moved(u2, along(1)), moved(d2, along(-1))
    u2x, d2x = moved(u2, other_core), moved(d2, other_core)
    near = call(cut_kernel, info, [own, u1, d1, ownx, u1x, d1x], jax.ShapeDtypeStruct((3, 2, 128, 128), BF16), 1)
    near, across = moved(near, hub_ahead(0)), moved(across, hub_ahead(4))
    acc = call(
        lambda *refs: products_kernel(OFFSETS[:3], *refs),
        info,
        [a, own, u1, d1, ownx, u1x, d1x],
        block_of_products,
        1,
    )
    u3, d3, u2x, d2x, near, across, acc = wall((u3, d3, u2x, d2x, near, across, acc))

    far_0, far_1 = moved(u3[0], along(1)), moved(d3[1], along(-1))
    u3x, d3x = moved(u3, other_core), moved(d3, other_core)
    late = call(
        cut_kernel, info, [u2, d2, u3, d3, u2x, d2x, u3x, d3x], jax.ShapeDtypeStruct((4, 2, 128, 128), BF16), 1
    )
    late = moved(late, hub_ahead(0))
    acc = call(
        lambda *refs: products_kernel(OFFSETS[3:7], *refs),
        info,
        [a, u2, d2, u3, d3, u2x, d2x, u3x, d3x, acc],
        block_of_products,
        1,
    )
    far_0, far_1, late, acc = wall((far_0, far_1, late, acc))

    far_0x, far_1x = moved(far_0, other_core), moved(far_1, other_core)
    drhs, crossed = call(
        crossed_kernel,
        info,
        [near, late, across, own, u1, d1, u2, d2, u3, d3, ownx, u1x, d1x, u2x, d2x, u3x, d3x],
        (jax.ShapeDtypeStruct((2048, 256), BF16), jax.ShapeDtypeStruct((256, 1024), BF16)),
        1,
    )
    half_block = jax.ShapeDtypeStruct((2, 64, 1024), BF16)
    keep, send, trace = call(
        last_kernel,
        info,
        [a, far_0, far_1, far_0x, far_1x, acc, drhs, crossed],
        (half_block, half_block, jax.ShapeDtypeStruct((1, 128), F32)),
        1,
        [pltpu.VMEM((256, 1024), BF16)],
    )

    below, above = moved(trace, along(1)), moved(trace, along(-1))
    kept, sent = moved(keep, from_hub(0)), moved(send, from_hub(1))
    two, three = wall((trace + above, below + trace + above))
    below, above = moved(two, along(3)), moved(three, along(-3))
    trace, kept, sent = wall((below + three + above, kept, sent))
    first, second = moved(trace, from_hub(0)), moved(trace, from_hub(1))
    products = jnp.where(half == 0, jnp.stack([kept, sent]), jnp.stack([sent, kept]))[:, None, None]
    both = jnp.where(half == 0, jnp.concatenate([first, second]), jnp.concatenate([second, first]))
    correlator = jnp.sum(both[:, :16].reshape(2, 8, 2), axis=1)[:, None, None, :] / F32(1024)
    return products, correlator


def solution(mesh):
    return jax.shard_map(
        shards,
        mesh=mesh,
        in_specs=(P(None, "tm", None, "row", None), P()),
        out_specs=(P(None, None, "tm", None, "row", None), P(None, None, "tm", None)),
        check_vma=False,
    )
```

time: 492 us -> 123 us (0.25); the launches traced: 485 us -> 123 us
  waiting for transfers between devices: 366 us -> 71.5 us
  blocking collectives: 30.7 us -> 0 us
  between operations: 28.9 us -> 0.79 us
  starting transfers between devices: 14 us -> 41.8 us
  matrix products: 23.8 us -> 0 us
  local copies, waits for them, and re-layouts: 15 us -> 0.13 us
  Pallas kernels: 0 us -> 7.7 us
    all_gather x3 -> x0, waiting for transfers between devices: 333 us -> none  [the longest x2 221 us: shards(): partner_full = lax.all_gather(partner_rows, 'row', axis=2, tiled=True)]
    ppermute x2 -> x30, waiting for transfers between devices: 18.6 us -> 71.5 us  [moved(): lax.ppermute(block, BOTH, [(index_of(*at), index_of(*route(*at))) for at...]
    ppermute x2 -> x30, starting transfers between devices: 6.02 us -> 41.8 us  [moved(): lax.ppermute(block, BOTH, [(index_of(*at), index_of(*route(*at))) for at...]
    psum x1 -> x0, blocking collectives: 30.7 us -> none  [shards(): summed = lax.psum(partial_all, 'row')]
    dot_general x16 -> x0, matrix products: 23.8 us -> none  [matmul_f32(): return jnp.dot(left_side, right_side, preferred_element_type=jnp.float32)]
    all_to_all x2 -> x0, waiting for transfers between devices: 14.4 us -> none  [shards(): lax.all_to_all(crossed_block, 'row', split_axis=3, concat_axis=2, tiled=T...]
    all_to_all x2 -> x0, starting transfers between devices: 7.89 us -> none  [shards(): lax.all_to_all(crossed_block, 'row', split_axis=3, concat_axis=2, tiled=T...]
    pallas_call x0 -> x7, Pallas kernels: none -> 7.7 us  [call(): pl.pallas_call(kernel, out_shape=out_shape, in_specs=[SMEM] + [VMEM] * le...]
  transfers between devices with their start and end apart: 7 -> 30, of which waited for: 7 -> 15; matrix products, arithmetic and copies ran while one was open for 6% -> 1% of each run, Pallas kernels for 0% -> 5%
where the time goes in v2:
time: 123 us
  waiting for transfers between devices  71.5 us (58%)
  starting transfers between devices  41.8 us (34%)
  Pallas kernels  7.7 us (6%)
  other arithmetic  1.56 us (1%)
    ppermute x30, waiting for transfers between devices, moved(): lax.ppermute(block, BOTH, [(index_of(*at), index_of(*route(*at))) for at...  71.5 us
    ppermute x30, starting transfers between devices, moved(): lax.ppermute(block, BOTH, [(index_of(*at), index_of(*route(*at))) for at...  41.8 us
    pallas_call x7, Pallas kernels, call(): pl.pallas_call(kernel, out_shape=out_shape, in_specs=[SMEM] + [VMEM] * le...  7.7 us
  transfers between devices with their start and end apart: 30, of which 15 were waited for; matrix products, arithmetic and copies ran while one was open for 1% of the time, Pallas kernels for 5%

profile of v2, /device:TPU:1, one launch (start us, length us, event | category | flops | bytes accessed | tf_op | source)
XLA Modules:
  0.0 123.4 jit_solution(1583388549284941869)
XLA Ops:
  0.6 0.0 copy-start
  0.6 4.2 %collective-permute-start = (bf16[2,2,64,1024]{3,2,1,0:T(8,128)(2,1)}, bf16[2,2,64,1024]{3,2,1,0:T(8,128)(2,1)S(1)}, u32[]{:S(2)}, u32[]{:S(2)}) collective-permute-start(bf16[2,2,64,1024]{3,2,1,0:T(8,128)(2,1)} %bitcast.19), channel_id=1, source_target_pairs={{0,128},{1,144},{2,130},{3,146},{4,132},{5,148},{6,134},{7,150},{8... | collective-permute-start | bytes 1572872 | tf_op jit(solution)/shard_map/ppermute | solution.py:27
  4.8 6.4 %collective-permute-done.own.refs_0_.refs_2_ = bf16[2,2,64,1024]{3,2,1,0:T(8,128)(2,1)S(1)} collective-permute-done((bf16[2,2,64,1024]{3,2,1,0:T(8,128)(2,1)}, bf16[2,2,64,1024]{3,2,1,0:T(8,128)(2,1)S(1)}, u32[]{:S(2)}, u32[]{:S(2)}) %collective-permute-start) | collective-permute-done | bytes 524320 | tf_op jit(solution)/shard_map/ppermute | solution.py:27
  11.3 1.5 %collective-permute-start.3 = (bf16[2,2,64,1024]{3,2,1,0:T(8,128)(2,1)S(1)}, bf16[2,2,64,1024]{3,2,1,0:T(8,128)(2,1)S(1)}, u32[]{:S(2)}, u32[]{:S(2)}) collective-permute-start(bf16[2,2,64,1024]{3,2,1,0:T(8,128)(2,1)S(1)} %collective-permute-done.own.refs_0_.refs_2_), channel_id=1, source_target_pairs={{0,16},{1,17},{2,18},{3,19},{4,20},{5,21},{6,22},{7,23},{8,24},{9,... | collective-permute-start | bytes 1572872 | tf_op jit(solution)/shard_map/ppermute | solution.py:27
  12.8 4.1 %collective-permute-start.2 = (bf16[2,2,64,1024]{3,2,1,0:T(8,128)(2,1)S(1)}, bf16[2,2,64,1024]{3,2,1,0:T(8,128)(2,1)S(1)}, u32[]{:S(2)}, u32[]{:S(2)}) collective-permute-start(bf16[2,2,64,1024]{3,2,1,0:T(8,128)(2,1)S(1)} %collective-permute-done.own.refs_0_.refs_2_), channel_id=1, source_target_pairs={{0,14},{1,15},{2,0},{3,1},{4,2},{5,3},{6,4},{7,5},{8,6},{9,7},{10,... | collective-permute-start | bytes 1572872 | tf_op jit(solution)/shard_map/ppermute | solution.py:27
  16.9 0.0 collective-permute-start.1
  16.9 0.1 pad_add_fusion.info.refs_0_
  17.0 0.0 collective-permute-done.3.other.refs_3_.refs_5_.refs_7_
  17.0 10.7 %collective-permute-done.2.refs_2_.refs_4_ = bf16[2,2,64,1024]{3,2,1,0:T(8,128)(2,1)S(1)} collective-permute-done((bf16[2,2,64,1024]{3,2,1,0:T(8,128)(2,1)S(1)}, bf16[2,2,64,1024]{3,2,1,0:T(8,128)(2,1)S(1)}, u32[]{:S(2)}, u32[]{:S(2)}) %collective-permute-start.2) | collective-permute-done | bytes 524320 | tf_op jit(solution)/shard_map/ppermute | solution.py:27
  27.6 3.1 %collective-permute-done.1.refs_1_.refs_3_ = bf16[2,2,64,1024]{3,2,1,0:T(8,128)(2,1)S(1)} collective-permute-done((bf16[2,2,64,1024]{3,2,1,0:T(8,128)(2,1)S(1)}, bf16[2,2,64,1024]{3,2,1,0:T(8,128)(2,1)S(1)}, u32[]{:S(2)}, u32[]{:S(2)}) %collective-permute-start.1) | collective-permute-done | bytes 524320 | tf_op jit(solution)/shard_map/ppermute | solution.py:27
  30.7 1.7 %collective-permute-start.6 = (bf16[2,2,64,1024]{3,2,1,0:T(8,128)(2,1)S(1)}, bf16[2,2,64,1024]{3,2,1,0:T(8,128)(2,1)S(1)}, u32[]{:S(2)}, u32[]{:S(2)}) collective-permute-start(bf16[2,2,64,1024]{3,2,1,0:T(8,128)(2,1)S(1)} %collective-permute-done.1.refs_1_.refs_3_), channel_id=1, source_target_pairs={{0,16},{1,17},{2,18},{3,19},{4,20},{5,21},{6,22},{7,23},{8,24},{9,... | collective-permute-start | bytes 1572872 | tf_op jit(solution)/shard_map/ppermute | solution.py:27
  32.4 0.0 collective-permute-start.7
  32.4 3.0 %collective-permute-start.5 = (bf16[2,2,64,1024]{3,2,1,0:T(8,128)(2,1)S(1)}, bf16[2,2,64,1024]{3,2,1,0:T(8,128)(2,1)S(1)}, u32[]{:S(2)}, u32[]{:S(2)}) collective-permute-start(bf16[2,2,64,1024]{3,2,1,0:T(8,128)(2,1)S(1)} %collective-permute-done.2.refs_2_.refs_4_), channel_id=1, source_target_pairs={{0,14},{1,15},{2,0},{3,1},{4,2},{5,3},{6,4},{7,5},{8,6},{9,7},{10,... | collective-permute-start | bytes 1572872 | tf_op jit(solution)/shard_map/ppermute | solution.py:27
  35.4 0.6 shard_map.41
  36.0 1.3 %collective-permute-start.8 = (bf16[2,128,1024]{2,1,0:T(8,128)(2,1)S(1)}, bf16[2,128,1024]{2,1,0:T(8,128)(2,1)S(1)}, u32[]{:S(2)}, u32[]{:S(2)}) collective-permute-start(bf16[2,128,1024]{2,1,0:T(8,128)(2,1)S(1)} %get-tuple-element.37), channel_id=1, source_target_pairs={{0,33},{1,0},{2,35},{3,2},{4,37},{5,4},{6,39},{7,6},{8,41},{9,8},{... | collective-permute-start | bytes 1572872 | tf_op jit(solution)/shard_map/ppermute | solution.py:27
  37.3 9.9 %collective-permute-done.4.refs_0_.refs_2_.refs_3_ = bf16[2,2,64,1024]{3,2,1,0:T(8,128)(2,1)S(1)} collective-permute-done((bf16[2,2,64,1024]{3,2,1,0:T(8,128)(2,1)S(1)}, bf16[2,2,64,1024]{3,2,1,0:T(8,128)(2,1)S(1)}, u32[]{:S(2)}, u32[]{:S(2)}) %collective-permute-start.4) | collective-permute-done | bytes 524320 | tf_op jit(solution)/shard_map/ppermute | solution.py:27
  47.2 0.0 collective-permute-done.7.refs_5_.refs_7_.refs_9_
  47.2 0.0 collective-permute-done.5.refs_1_.refs_3_.refs_4_
  47.2 6.3 %collective-permute-done.8.refs_1_.a_ref = bf16[2,128,1024]{2,1,0:T(8,128)(2,1)S(1)} collective-permute-done((bf16[2,128,1024]{2,1,0:T(8,128)(2,1)S(1)}, bf16[2,128,1024]{2,1,0:T(8,128)(2,1)S(1)}, u32[]{:S(2)}, u32[]{:S(2)}) %collective-permute-start.8) | collective-permute-done | bytes 524320 | tf_op jit(solution)/shard_map/ppermute | solution.py:27
  53.5 0.0 collective-permute-start.11
  53.5 0.0 collective-permute-start.9
  53.5 0.5 collective-permute-start.12
  54.0 3.0 %collective-permute-start.10 = (bf16[2,2,64,1024]{3,2,1,0:T(8,128)(2,1)S(1)}, bf16[2,2,64,1024]{3,2,1,0:T(8,128)(2,1)S(1)}, u32[]{:S(2)}, u32[]{:S(2)}) collective-permute-start(bf16[2,2,64,1024]{3,2,1,0:T(8,128)(2,1)S(1)} %collective-permute-done.5.refs_1_.refs_3_.refs_4_), channel_id=1, source_target_pairs={{0,14},{1,15},{2,0},{3,1},{4,2},{5,3},{6,4},{7,5},{8,6},{9,7},{10,... | collective-permute-start | bytes 1572872 | tf_op jit(solution)/shard_map/ppermute | solution.py:27
  56.9 0.0 collective-permute-start.14
  56.9 0.6 shard_map.42
  57.6 11.6 %collective-permute-done.14.across = bf16[2,128,128]{2,1,0:T(8,128)(2,1)S(1)} collective-permute-done((bf16[2,128,128]{2,1,0:T(8,128)(2,1)S(1)}, bf16[2,128,128]{2,1,0:T(8,128)(2,1)S(1)}, u32[]{:S(2)}, u32[]{:S(2)}) %collective-permute-start.14) | collective-permute-done | bytes 65568 | tf_op jit(solution)/shard_map/ppermute | solution.py:27
  69.1 0.3 collective-permute-start.13
  69.5 1.1 shard_map.43.refs_10_
  70.6 6.4 %collective-permute-done.13.near = bf16[3,2,128,128]{3,2,1,0:T(8,128)(2,1)S(1)} collective-permute-done((bf16[3,2,128,128]{3,2,1,0:T(8,128)(2,1)S(1)}, bf16[3,2,128,128]{3,2,1,0:T(8,128)(2,1)S(1)}, u32[]{:S(2)}, u32[]{:S(2)}) %collective-permute-start.13) | collective-permute-done | bytes 196640 | tf_op jit(solution)/shard_map/ppermute | solution.py:27
  77.0 0.0 collective-permute-done.11.refs_4_.refs_6_.refs_10_
  77.0 0.0 collective-permute-done.9.refs_2_.refs_4_.refs_5_
  77.0 3.1 %collective-permute-start.17 = (bf16[2,2,64,1024]{3,2,1,0:T(8,128)(2,1)S(1)}, bf16[2,2,64,1024]{3,2,1,0:T(8,128)(2,1)S(1)}, u32[]{:S(2)}, u32[]{:S(2)}) collective-permute-start(bf16[2,2,64,1024]{3,2,1,0:T(8,128)(2,1)S(1)} %collective-permute-done.9.refs_2_.refs_4_.refs_5_), channel_id=1, source_target_pairs={{0,16},{1,17},{2,18},{3,19},{4,20},{5,21},{6,22},{7,23},{8,24},{9,... | collective-permute-start | bytes 1572872 | tf_op jit(solution)/shard_map/ppermute | solution.py:27
  80.1 0.3 collective-permute-start.18
  80.4 4.5 %collective-permute-start.16 = (bf16[2,64,1024]{2,1,0:T(8,128)(2,1)S(1)}, bf16[2,64,1024]{2,1,0:T(8,128)(2,1)S(1)}, u32[]{:S(2)}, u32[]{:S(2)}) collective-permute-start(bf16[2,64,1024]{2,1,0:T(8,128)(2,1)S(1)} %slice_bitcast_fusion), channel_id=1, source_target_pairs={{0,14},{1,15},{2,0},{3,1},{4,2},{5,3},{6,4},{7,5},{8,6},{9,7},{10,... | collective-permute-start | bytes 786440 | tf_op jit(solution)/shard_map/ppermute | solution.py:27
  84.9 0.1 collective-permute-start.15
  85.0 0.0 collective-permute-done.18.refs_7_.refs_9_.refs_13_
  85.0 0.6 shard_map.44
  85.7 0.1 collective-permute-start.19
  85.8 1.3 %shard_map.45.acc = f32[256,1024]{1,0:T(8,128)S(1)} custom-call(s32[6]{0:T(128)S(1)} %pad_add_fusion.info.refs_0_, bf16[2,128,1024]{2,1,0:T(8,128)(2,1)S(1)} %collective-permute-done.8.refs_1_.a_ref, bf16[2,2,64,1024]{3,2,1,0:T(8,128)(2,1)S(1)} %collective-permute-done.4.refs_0_.refs_2_.refs_3_, ...), custom_call_target="tpu_custom_call" | custom-call | flops 1 | bytes 1048576 | tf_op jit(solution)/shard_map/pallas_call | solution.py:69
  87.1 3.3 %collective-permute-done.16.own_1 = bf16[2,64,1024]{2,1,0:T(8,128)(2,1)S(1)} collective-permute-done((bf16[2,64,1024]{2,1,0:T(8,128)(2,1)S(1)}, bf16[2,64,1024]{2,1,0:T(8,128)(2,1)S(1)}, u32[]{:S(2)}, u32[]{:S(2)}) %collective-permute-start.16) | collective-permute-done | bytes 262176 | tf_op jit(solution)/shard_map/ppermute | solution.py:27
  90.4 3.2 %collective-permute-done.15.own_0 = bf16[2,64,1024]{2,1,0:T(8,128)(2,1)S(1)} collective-permute-done((bf16[2,64,1024]{2,1,0:T(8,128)(2,1)S(1)}, bf16[2,64,1024]{2,1,0:T(8,128)(2,1)S(1)}, u32[]{:S(2)}, u32[]{:S(2)}) %collective-permute-start.15) | collective-permute-done | bytes 262176 | tf_op jit(solution)/shard_map/ppermute | solution.py:27
  93.6 3.5 %collective-permute-done.19.late = bf16[4,2,128,128]{3,2,1,0:T(8,128)(2,1)S(1)} collective-permute-done((bf16[4,2,128,128]{3,2,1,0:T(8,128)(2,1)S(1)}, bf16[4,2,128,128]{3,2,1,0:T(8,128)(2,1)S(1)}, u32[]{:S(2)}, u32[]{:S(2)}) %collective-permute-start.19) | collective-permute-done | bytes 262176 | tf_op jit(solution)/shard_map/ppermute | solution.py:27
  97.1 0.0 collective-permute-start.20
  97.1 0.5 collective-permute-start.21
  97.6 1.9 %shard_map.46 = (bf16[2048,256]{1,0:T(8,128)(2,1)S(1)}, bf16[256,1024]{1,0:T(8,128)(2,1)S(1)}) custom-call(s32[6]{0:T(128)S(1)} %pad_add_fusion.info.refs_0_, bf16[3,2,128,128]{3,2,1,0:T(8,128)(2,1)S(1)} %collective-permute-done.13.near, bf16[4,2,128,128]{3,2,1,0:T(8,128)(2,1)S(1)} %collective-permute-done.19.late, ...), custom_call_target="tpu_custom_call" | custom-call | flops 1 | bytes 1048576 | tf_op jit(solution)/shard_map/pallas_call | solution.py:69
  99.5 0.0 collective-permute-done.21.other_1
  99.5 1.6 %shard_map.47 = (bf16[2,64,1024]{2,1,0:T(8,128)(2,1)S(1)}, bf16[2,64,1024]{2,1,0:T(8,128)(2,1)S(1)}, f32[1,128]{1,0:T(1,128)S(1)}) custom-call(s32[6]{0:T(128)S(1)} %pad_add_fusion.info.refs_0_, bf16[2,128,1024]{2,1,0:T(8,128)(2,1)S(1)} %collective-permute-done.8.refs_1_.a_ref, bf16[2,64,1024]{2,1,0:T(8,128)(2,1)S(1)} %collective-permute-done.15.own_0, ...), custom_call_target="tpu_custom_call" | custom-call | flops 1 | bytes 1048576 | tf_op jit(solution)/shard_map/pallas_call | solution.py:69
  101.1 0.0 collective-permute-start.23
  101.1 2.7 %collective-permute-start.22 = (f32[1,128]{1,0:T(1,128)S(1)}, f32[1,128]{1,0:T(1,128)S(1)}, u32[]{:S(2)}, u32[]{:S(2)}) collective-permute-start(f32[1,128]{1,0:T(1,128)S(1)} %get-tuple-element.58), channel_id=1, source_target_pairs={{0,14},{1,15},{2,0},{3,1},{4,2},{5,3},{6,4},{7,5},{8,6},{9,7},{10,... | collective-permute-start | bytes 1544 | tf_op jit(solution)/shard_map/ppermute | solution.py:27
  103.8 0.0 collective-permute-start.26
  103.8 0.0 collective-permute-start.27
  103.8 0.9 collective-permute-done.23
  104.7 0.0 collective-permute-done.22
  104.7 4.2 %collective-permute-start.24 = (f32[1,128]{1,0:T(1,128)S(1)}, f32[1,128]{1,0:T(1,128)S(1)}, u32[]{:S(2)}, u32[]{:S(2)}) collective-permute-start(f32[1,128]{1,0:T(1,128)S(1)} %get-tuple-element.59), channel_id=1, source_target_pairs={{0,6},{1,7},{2,8},{3,9},{4,10},{5,11},{6,12},{7,13},{8,14},{9,15},... | collective-permute-start | bytes 1544 | tf_op jit(solution)/shard_map/ppermute | solution.py:27
  108.9 0.3 collective-permute-start.25
  109.3 0.9 collective-permute-done.24
  110.2 2.9 %collective-permute-done.25 = f32[1,128]{1,0:T(1,128)S(1)} collective-permute-done((f32[1,128]{1,0:T(1,128)S(1)}, f32[1,128]{1,0:T(1,128)S(1)}, u32[]{:S(2)}, u32[]{:S(2)}) %collective-permute-start.25) | collective-permute-done | bytes 544 | tf_op jit(solution)/shard_map/ppermute | solution.py:27
  113.2 0.4 collective-permute-done.26
  113.6 2.1 %collective-permute-start.29 = (f32[1,128]{1,0:T(1,128)S(1)}, f32[1,128]{1,0:T(1,128)S(1)}, u32[]{:S(2)}, u32[]{:S(2)}) collective-permute-start(f32[1,128]{1,0:T(1,128)S(1)} %add_add_fusion), channel_id=1, source_target_pairs={{0,129},{1,113},{2,131},{3,115},{4,133},{5,117},{6,135},{7,119},{8... | collective-permute-start | bytes 1544 | tf_op jit(solution)/shard_map/ppermute | solution.py:27
  115.7 4.4 %collective-permute-start.28 = (f32[1,128]{1,0:T(1,128)S(1)}, f32[1,128]{1,0:T(1,128)S(1)}, u32[]{:S(2)}, u32[]{:S(2)}) collective-permute-start(f32[1,128]{1,0:T(1,128)S(1)} %add_add_fusion), channel_id=1, source_target_pairs={{0,128},{1,112},{2,130},{3,114},{4,132},{5,116},{6,134},{7,118},{8... | collective-permute-start | bytes 1544 | tf_op jit(solution)/shard_map/ppermute | solution.py:27
  120.1 0.9 maximum_select_fusion
  120.9 1.8 %collective-permute-done.28 = f32[1,128]{1,0:T(1,128)S(1)} collective-permute-done((f32[1,128]{1,0:T(1,128)S(1)}, f32[1,128]{1,0:T(1,128)S(1)}, u32[]{:S(2)}, u32[]{:S(2)}) %collective-permute-start.28) | collective-permute-done | bytes 544 | tf_op jit(solution)/shard_map/ppermute | solution.py:27
  122.7 0.1 reshape.77
  122.8 0.6 broadcast_multiply_fusion
  (16 shorter events, 0.1 us)
Async XLA Ops:
  0.6 16.2 %copy-start = (s32[2,1,4]{2,1,0:T(1,128)S(1)}, s32[2,1,4]{2,1,0:T(1,128)}, u32[]{:S(2)}) copy-start(s32[2,1,4]{2,1,0:T(1,128)} %param.3) | copy-start | bytes 100
  0.6 10.6 %collective-permute-start = (bf16[2,2,64,1024]{3,2,1,0:T(8,128)(2,1)}, bf16[2,2,64,1024]{3,2,1,0:T(8,128)(2,1)S(1)}, u32[]{:S(2)}, u32[]{:S(2)}) collective-permute-start(bf16[2,2,64,1024]{3,2,1,0:T(8,128)(2,1)} %bitcast.19), channel_id=1, source_target_pairs={{0,128},{1,144},{2,130},{3,146},{4,132},{5,148},{6,134},{7,150},{8... | collective-permute-start | bytes 1572872 | tf_op jit(solution)/shard_map/ppermute | solution.py:27
  11.3 5.7 %collective-permute-start.3 = (bf16[2,2,64,1024]{3,2,1,0:T(8,128)(2,1)S(1)}, bf16[2,2,64,1024]{3,2,1,0:T(8,128)(2,1)S(1)}, u32[]{:S(2)}, u32[]{:S(2)}) collective-permute-start(bf16[2,2,64,1024]{3,2,1,0:T(8,128)(2,1)S(1)} %collective-permute-done.own.refs_0_.refs_2_), channel_id=1, source_target_pairs={{0,16},{1,17},{2,18},{3,19},{4,20},{5,21},{6,22},{7,23},{8,24},{9,... | collective-permute-start | bytes 1572872 | tf_op jit(solution)/shard_map/ppermute | solution.py:27
  12.8 14.9 %collective-permute-start.2 = (bf16[2,2,64,1024]{3,2,1,0:T(8,128)(2,1)S(1)}, bf16[2,2,64,1024]{3,2,1,0:T(8,128)(2,1)S(1)}, u32[]{:S(2)}, u32[]{:S(2)}) collective-permute-start(bf16[2,2,64,1024]{3,2,1,0:T(8,128)(2,1)S(1)} %collective-permute-done.own.refs_0_.refs_2_), channel_id=1, source_target_pairs={{0,14},{1,15},{2,0},{3,1},{4,2},{5,3},{6,4},{7,5},{8,6},{9,7},{10,... | collective-permute-start | bytes 1572872 | tf_op jit(solution)/shard_map/ppermute | solution.py:27
  16.9 13.9 %collective-permute-start.1 = (bf16[2,2,64,1024]{3,2,1,0:T(8,128)(2,1)S(1)}, bf16[2,2,64,1024]{3,2,1,0:T(8,128)(2,1)S(1)}, u32[]{:S(2)}, u32[]{:S(2)}) collective-permute-start(bf16[2,2,64,1024]{3,2,1,0:T(8,128)(2,1)S(1)} %collective-permute-done.own.refs_0_.refs_2_), channel_id=1, source_target_pairs={{0,2},{1,3},{2,4},{3,5},{4,6},{5,7},{6,8},{7,9},{8,10},{9,11},{10,... | collective-permute-start | bytes 1572872 | tf_op jit(solution)/shard_map/ppermute | solution.py:27
  30.7 6.5 %collective-permute-start.6 = (bf16[2,2,64,1024]{3,2,1,0:T(8,128)(2,1)S(1)}, bf16[2,2,64,1024]{3,2,1,0:T(8,128)(2,1)S(1)}, u32[]{:S(2)}, u32[]{:S(2)}) collective-permute-start(bf16[2,2,64,1024]{3,2,1,0:T(8,128)(2,1)S(1)} %collective-permute-done.1.refs_1_.refs_3_), channel_id=1, source_target_pairs={{0,16},{1,17},{2,18},{3,19},{4,20},{5,21},{6,22},{7,23},{8,24},{9,... | collective-permute-start | bytes 1572872 | tf_op jit(solution)/shard_map/ppermute | solution.py:27
  32.4 14.8 %collective-permute-start.4 = (bf16[2,2,64,1024]{3,2,1,0:T(8,128)(2,1)S(1)}, bf16[2,2,64,1024]{3,2,1,0:T(8,128)(2,1)S(1)}, u32[]{:S(2)}, u32[]{:S(2)}) collective-permute-start(bf16[2,2,64,1024]{3,2,1,0:T(8,128)(2,1)S(1)} %collective-permute-done.1.refs_1_.refs_3_), channel_id=1, source_target_pairs={{0,2},{1,3},{2,4},{3,5},{4,6},{5,7},{6,8},{7,9},{8,10},{9,11},{10,... | collective-permute-start | bytes 1572872 | tf_op jit(solution)/shard_map/ppermute | solution.py:27
  32.4 14.8 %collective-permute-start.7 = (bf16[2,2,64,1024]{3,2,1,0:T(8,128)(2,1)S(1)}, bf16[2,2,64,1024]{3,2,1,0:T(8,128)(2,1)S(1)}, u32[]{:S(2)}, u32[]{:S(2)}) collective-permute-start(bf16[2,2,64,1024]{3,2,1,0:T(8,128)(2,1)S(1)} %collective-permute-done.2.refs_2_.refs_4_), channel_id=1, source_target_pairs={{0,16},{1,17},{2,18},{3,19},{4,20},{5,21},{6,22},{7,23},{8,24},{9,... | collective-permute-start | bytes 1572872 | tf_op jit(solution)/shard_map/ppermute | solution.py:27
  32.4 14.8 %collective-permute-start.5 = (bf16[2,2,64,1024]{3,2,1,0:T(8,128)(2,1)S(1)}, bf16[2,2,64,1024]{3,2,1,0:T(8,128)(2,1)S(1)}, u32[]{:S(2)}, u32[]{:S(2)}) collective-permute-start(bf16[2,2,64,1024]{3,2,1,0:T(8,128)(2,1)S(1)} %collective-permute-done.2.refs_2_.refs_4_), channel_id=1, source_target_pairs={{0,14},{1,15},{2,0},{3,1},{4,2},{5,3},{6,4},{7,5},{8,6},{9,7},{10,... | collective-permute-start | bytes 1572872 | tf_op jit(solution)/shard_map/ppermute | solution.py:27
  36.0 17.5 %collective-permute-start.8 = (bf16[2,128,1024]{2,1,0:T(8,128)(2,1)S(1)}, bf16[2,128,1024]{2,1,0:T(8,128)(2,1)S(1)}, u32[]{:S(2)}, u32[]{:S(2)}) collective-permute-start(bf16[2,128,1024]{2,1,0:T(8,128)(2,1)S(1)} %get-tuple-element.37), channel_id=1, source_target_pairs={{0,33},{1,0},{2,35},{3,2},{4,37},{5,4},{6,39},{7,6},{8,41},{9,8},{... | collective-permute-start | bytes 1572872 | tf_op jit(solution)/shard_map/ppermute | solution.py:27
  53.5 23.5 %collective-permute-start.11 = (bf16[2,2,64,1024]{3,2,1,0:T(8,128)(2,1)S(1)}, bf16[2,2,64,1024]{3,2,1,0:T(8,128)(2,1)S(1)}, u32[]{:S(2)}, u32[]{:S(2)}) collective-permute-start(bf16[2,2,64,1024]{3,2,1,0:T(8,128)(2,1)S(1)} %collective-permute-done.4.refs_0_.refs_2_.refs_3_), channel_id=1, source_target_pairs={{0,16},{1,17},{2,18},{3,19},{4,20},{5,21},{6,22},{7,23},{8,24},{9,... | collective-permute-start | bytes 1572872 | tf_op jit(solution)/shard_map/ppermute | solution.py:27
  53.5 23.5 %collective-permute-start.9 = (bf16[2,2,64,1024]{3,2,1,0:T(8,128)(2,1)S(1)}, bf16[2,2,64,1024]{3,2,1,0:T(8,128)(2,1)S(1)}, u32[]{:S(2)}, u32[]{:S(2)}) collective-permute-start(bf16[2,2,64,1024]{3,2,1,0:T(8,128)(2,1)S(1)} %collective-permute-done.4.refs_0_.refs_2_.refs_3_), channel_id=1, source_target_pairs={{0,2},{1,3},{2,4},{3,5},{4,6},{5,7},{6,8},{7,9},{8,10},{9,11},{10,... | collective-permute-start | bytes 1572872 | tf_op jit(solution)/shard_map/ppermute | solution.py:27
  53.5 23.5 %collective-permute-start.12 = (bf16[2,2,64,1024]{3,2,1,0:T(8,128)(2,1)S(1)}, bf16[2,2,64,1024]{3,2,1,0:T(8,128)(2,1)S(1)}, u32[]{:S(2)}, u32[]{:S(2)}) collective-permute-start(bf16[2,2,64,1024]{3,2,1,0:T(8,128)(2,1)S(1)} %collective-permute-done.5.refs_1_.refs_3_.refs_4_), channel_id=1, source_target_pairs={{0,16},{1,17},{2,18},{3,19},{4,20},{5,21},{6,22},{7,23},{8,24},{9,... | collective-permute-start | bytes 1572872 | tf_op jit(solution)/shard_map/ppermute | solution.py:27
  54.0 23.0 %collective-permute-start.10 = (bf16[2,2,64,1024]{3,2,1,0:T(8,128)(2,1)S(1)}, bf16[2,2,64,1024]{3,2,1,0:T(8,128)(2,1)S(1)}, u32[]{:S(2)}, u32[]{:S(2)}) collective-permute-start(bf16[2,2,64,1024]{3,2,1,0:T(8,128)(2,1)S(1)} %collective-permute-done.5.refs_1_.refs_3_.refs_4_), channel_id=1, source_target_pairs={{0,14},{1,15},{2,0},{3,1},{4,2},{5,3},{6,4},{7,5},{8,6},{9,7},{10,... | collective-permute-start | bytes 1572872 | tf_op jit(solution)/shard_map/ppermute | solution.py:27
  56.9 12.2 %collective-permute-start.14 = (bf16[2,128,128]{2,1,0:T(8,128)(2,1)S(1)}, bf16[2,128,128]{2,1,0:T(8,128)(2,1)S(1)}, u32[]{:S(2)}, u32[]{:S(2)}) collective-permute-start(bf16[2,128,128]{2,1,0:T(8,128)(2,1)S(1)} %get-tuple-element.44), channel_id=1, source_target_pairs={{0,41},{1,8},{2,43},{3,10},{4,45},{5,12},{6,47},{7,14},{8,33},{9,0... | collective-permute-start | bytes 196616 | tf_op jit(solution)/shard_map/ppermute | solution.py:27
  69.1 7.8 %collective-permute-start.13 = (bf16[3,2,128,128]{3,2,1,0:T(8,128)(2,1)S(1)}, bf16[3,2,128,128]{3,2,1,0:T(8,128)(2,1)S(1)}, u32[]{:S(2)}, u32[]{:S(2)}) collective-permute-start(bf16[3,2,128,128]{3,2,1,0:T(8,128)(2,1)S(1)} %shard_map.42), channel_id=1, source_target_pairs={{0,33},{1,0},{2,35},{3,2},{4,37},{5,4},{6,39},{7,6},{8,41},{9,8},{... | collective-permute-start | bytes 589832 | tf_op jit(solution)/shard_map/ppermute | solution.py:27
  77.0 8.0 %collective-permute-start.17 = (bf16[2,2,64,1024]{3,2,1,0:T(8,128)(2,1)S(1)}, bf16[2,2,64,1024]{3,2,1,0:T(8,128)(2,1)S(1)}, u32[]{:S(2)}, u32[]{:S(2)}) collective-permute-start(bf16[2,2,64,1024]{3,2,1,0:T(8,128)(2,1)S(1)} %collective-permute-done.9.refs_2_.refs_4_.refs_5_), channel_id=1, source_target_pairs={{0,16},{1,17},{2,18},{3,19},{4,20},{5,21},{6,22},{7,23},{8,24},{9,... | collective-permute-start | bytes 1572872 | tf_op jit(solution)/shard_map/ppermute | solution.py:27
  80.1 4.9 %collective-permute-start.18 = (bf16[2,2,64,1024]{3,2,1,0:T(8,128)(2,1)S(1)}, bf16[2,2,64,1024]{3,2,1,0:T(8,128)(2,1)S(1)}, u32[]{:S(2)}, u32[]{:S(2)}) collective-permute-start(bf16[2,2,64,1024]{3,2,1,0:T(8,128)(2,1)S(1)} %collective-permute-done.10.refs_3_.refs_5_.refs_6_), channel_id=1, source_target_pairs={{0,16},{1,17},{2,18},{3,19},{4,20},{5,21},{6,22},{7,23},{8,24},{9,... | collective-permute-start | bytes 1572872 | tf_op jit(solution)/shard_map/ppermute | solution.py:27
  80.4 10.0 %collective-permute-start.16 = (bf16[2,64,1024]{2,1,0:T(8,128)(2,1)S(1)}, bf16[2,64,1024]{2,1,0:T(8,128)(2,1)S(1)}, u32[]{:S(2)}, u32[]{:S(2)}) collective-permute-start(bf16[2,64,1024]{2,1,0:T(8,128)(2,1)S(1)} %slice_bitcast_fusion), channel_id=1, source_target_pairs={{0,14},{1,15},{2,0},{3,1},{4,2},{5,3},{6,4},{7,5},{8,6},{9,7},{10,... | collective-permute-start | bytes 786440 | tf_op jit(solution)/shard_map/ppermute | solution.py:27
  84.9 8.6 %collective-permute-start.15 = (bf16[2,64,1024]{2,1,0:T(8,128)(2,1)S(1)}, bf16[2,64,1024]{2,1,0:T(8,128)(2,1)S(1)}, u32[]{:S(2)}, u32[]{:S(2)}) collective-permute-start(bf16[2,64,1024]{2,1,0:T(8,128)(2,1)S(1)} %slice_bitcast_fusion.1), channel_id=1, source_target_pairs={{0,2},{1,3},{2,4},{3,5},{4,6},{5,7},{6,8},{7,9},{8,10},{9,11},{10,... | collective-permute-start | bytes 786440 | tf_op jit(solution)/shard_map/ppermute | solution.py:27
  85.7 11.4 %collective-permute-start.19 = (bf16[4,2,128,128]{3,2,1,0:T(8,128)(2,1)S(1)}, bf16[4,2,128,128]{3,2,1,0:T(8,128)(2,1)S(1)}, u32[]{:S(2)}, u32[]{:S(2)}) collective-permute-start(bf16[4,2,128,128]{3,2,1,0:T(8,128)(2,1)S(1)} %shard_map.44), channel_id=1, source_target_pairs={{0,33},{1,0},{2,35},{3,2},{4,37},{5,4},{6,39},{7,6},{8,41},{9,8},{... | collective-permute-start | bytes 786440 | tf_op jit(solution)/shard_map/ppermute | solution.py:27
  97.1 2.4 %collective-permute-start.20 = (bf16[2,64,1024]{2,1,0:T(8,128)(2,1)S(1)}, bf16[2,64,1024]{2,1,0:T(8,128)(2,1)S(1)}, u32[]{:S(2)}, u32[]{:S(2)}) collective-permute-start(bf16[2,64,1024]{2,1,0:T(8,128)(2,1)S(1)} %collective-permute-done.15.own_0), channel_id=1, source_target_pairs={{0,16},{1,17},{2,18},{3,19},{4,20},{5,21},{6,22},{7,23},{8,24},{9,... | collective-permute-start | bytes 786440 | tf_op jit(solution)/shard_map/ppermute | solution.py:27
  97.1 2.4 %collective-permute-start.21 = (bf16[2,64,1024]{2,1,0:T(8,128)(2,1)S(1)}, bf16[2,64,1024]{2,1,0:T(8,128)(2,1)S(1)}, u32[]{:S(2)}, u32[]{:S(2)}) collective-permute-start(bf16[2,64,1024]{2,1,0:T(8,128)(2,1)S(1)} %collective-permute-done.16.own_1), channel_id=1, source_target_pairs={{0,16},{1,17},{2,18},{3,19},{4,20},{5,21},{6,22},{7,23},{8,24},{9,... | collective-permute-start | bytes 786440 | tf_op jit(solution)/shard_map/ppermute | solution.py:27
  101.1 3.6 %collective-permute-start.23 = (f32[1,128]{1,0:T(1,128)S(1)}, f32[1,128]{1,0:T(1,128)S(1)}, u32[]{:S(2)}, u32[]{:S(2)}) collective-permute-start(f32[1,128]{1,0:T(1,128)S(1)} %get-tuple-element.58), channel_id=1, source_target_pairs={{0,2},{1,3},{2,4},{3,5},{4,6},{5,7},{6,8},{7,9},{8,10},{9,11},{10,... | collective-permute-start | bytes 1544 | tf_op jit(solution)/shard_map/ppermute | solution.py:27
  101.1 3.6 %collective-permute-start.22 = (f32[1,128]{1,0:T(1,128)S(1)}, f32[1,128]{1,0:T(1,128)S(1)}, u32[]{:S(2)}, u32[]{:S(2)}) collective-permute-start(f32[1,128]{1,0:T(1,128)S(1)} %get-tuple-element.58), channel_id=1, source_target_pairs={{0,14},{1,15},{2,0},{3,1},{4,2},{5,3},{6,4},{7,5},{8,6},{9,7},{10,... | collective-permute-start | bytes 1544 | tf_op jit(solution)/shard_map/ppermute | solution.py:27
  103.8 9.8 %collective-permute-start.26 = (bf16[2,64,1024]{2,1,0:T(8,128)(2,1)S(1)}, bf16[2,64,1024]{2,1,0:T(8,128)(2,1)S(1)}, u32[]{:S(2)}, u32[]{:S(2)}) collective-permute-start(bf16[2,64,1024]{2,1,0:T(8,128)(2,1)S(1)} %get-tuple-element.61), channel_id=1, source_target_pairs={{0,128},{1,112},{2,130},{3,114},{4,132},{5,116},{6,134},{7,118},{8... | collective-permute-start | bytes 786440 | tf_op jit(solution)/shard_map/ppermute | solution.py:27
  103.8 9.8 %collective-permute-start.27 = (bf16[2,64,1024]{2,1,0:T(8,128)(2,1)S(1)}, bf16[2,64,1024]{2,1,0:T(8,128)(2,1)S(1)}, u32[]{:S(2)}, u32[]{:S(2)}) collective-permute-start(bf16[2,64,1024]{2,1,0:T(8,128)(2,1)S(1)} %get-tuple-element.62), channel_id=1, source_target_pairs={{0,129},{1,113},{2,131},{3,115},{4,133},{5,117},{6,135},{7,119},{8... | collective-permute-start | bytes 786440 | tf_op jit(solution)/shard_map/ppermute | solution.py:27
  104.7 5.5 %collective-permute-start.24 = (f32[1,128]{1,0:T(1,128)S(1)}, f32[1,128]{1,0:T(1,128)S(1)}, u32[]{:S(2)}, u32[]{:S(2)}) collective-permute-start(f32[1,128]{1,0:T(1,128)S(1)} %get-tuple-element.59), channel_id=1, source_target_pairs={{0,6},{1,7},{2,8},{3,9},{4,10},{5,11},{6,12},{7,13},{8,14},{9,15},... | collective-permute-start | bytes 1544 | tf_op jit(solution)/shard_map/ppermute | solution.py:27
  108.9 4.2 %collective-permute-start.25 = (f32[1,128]{1,0:T(1,128)S(1)}, f32[1,128]{1,0:T(1,128)S(1)}, u32[]{:S(2)}, u32[]{:S(2)}) collective-permute-start(f32[1,128]{1,0:T(1,128)S(1)} %get-tuple-element.60), channel_id=1, source_target_pairs={{0,10},{1,11},{2,12},{3,13},{4,14},{5,15},{6,0},{7,1},{8,2},{9,3},... | collective-permute-start | bytes 1544 | tf_op jit(solution)/shard_map/ppermute | solution.py:27
  113.6 7.3 %collective-permute-start.29 = (f32[1,128]{1,0:T(1,128)S(1)}, f32[1,128]{1,0:T(1,128)S(1)}, u32[]{:S(2)}, u32[]{:S(2)}) collective-permute-start(f32[1,128]{1,0:T(1,128)S(1)} %add_add_fusion), channel_id=1, source_target_pairs={{0,129},{1,113},{2,131},{3,115},{4,133},{5,117},{6,135},{7,119},{8... | collective-permute-start | bytes 1544 | tf_op jit(solution)/shard_map/ppermute | solution.py:27
  115.7 7.1 %collective-permute-start.28 = (f32[1,128]{1,0:T(1,128)S(1)}, f32[1,128]{1,0:T(1,128)S(1)}, u32[]{:S(2)}, u32[]{:S(2)}) collective-permute-start(f32[1,128]{1,0:T(1,128)S(1)} %add_add_fusion), channel_id=1, source_target_pairs={{0,128},{1,112},{2,130},{3,114},{4,132},{5,116},{6,134},{7,118},{8... | collective-permute-start | bytes 1544 | tf_op jit(solution)/shard_map/ppermute | solution.py:27

commit v3 on v2

--- a/solution.py
+++ b/solution.py
@@ -31,6 +31,10 @@
     return lambda m, c, z, h: (m, c, z + step, h)
 
 
+def onward(m, c, z, h):
+    return (m, c, z + (1 if c == 0 else -1), h)
+
+
 def other_core(m, c, z, h):
     return (m, 1 - c, z, h)
 
@@ -46,7 +50,7 @@
 def hub_ahead(step):
     def route(m, c, z, h):
         column, half = hub_of(SERVED[m, h] + 1 + c)
-        return (column, c, z + step, half)
+        return (column, c, z + (step if c == 0 else -step), half)
 
     return route
 
@@ -78,7 +82,7 @@
 
 
 def place_of(info, offset):
-    return lax.rem(info[0] + (offset + 8), 8)
+    return lax.rem(info[0] + jnp.where(info[1] == 0, 8 - offset, 8 + offset), 8)
 
 
 def columns_of(info, offset):
@@ -103,16 +107,19 @@
         out[part, 64:128] = second
 
 
-def first_cut_kernel(info, own, other, a, across):
+def first_cut_kernel(info, own, other, a):
     for part in range(2):
         a[part] = whole(info, own, other, info[2], part)
-    cut(info, own, other, 4, across)
 
 
 def cut_kernel(info, *refs):
     count = len(refs) // 2
     for k in range(count):
         cut(info, refs[k], refs[count + k], 0, refs[-1].at[k])
+
+
+def across_kernel(info, own, other, out):
+    cut(info, own, other, -2, out)
 
 
 def left_side(info, a_ref, offset):
@@ -141,7 +148,7 @@
     return turned.astype(BF16)
 
 
-OFFSETS = (0, -1, 1, -2, 2, -3, 3, 4)
+OFFSETS = (0, 1, -1, 2, -2, 3, -3, 4)
 
 
 def crossed_kernel(info, near, late, across, *refs):
@@ -159,11 +166,9 @@
         crossed[:, columns_of(info, offset)] = crossed_block(real, imag, drhs)
 
 
-def last_kernel(info, a_ref, own_0, own_1, other_0, other_1, acc, drhs, crossed, keep, send, trace, turned):
+def last_kernel(info, a_ref, own, other, acc, drhs, crossed, keep, send, trace, turned):
     def parts(momentum):
-        own = jnp.where(momentum == 0, own_0[...], own_1[...])
-        other = jnp.where(momentum == 0, other_0[...], other_1[...])
-        return [jnp.concatenate(halves(info, own[part], other[part]), axis=0) for part in range(2)]
+        return [whole(info, own, other, momentum, part) for part in range(2)]
 
     block = jnp.concatenate(parts(info[3]), axis=0)
     product = acc[...] + jnp.dot(left_side(info, a_ref, 4), block, preferred_element_type=F32)
@@ -194,49 +199,41 @@
     block_of_products = jax.ShapeDtypeStruct((256, 1024), F32)
 
     own = moved(rows, to_hub(0))
-
-    u1, d1, ownx = moved(own, along(1)), moved(own, along(-1)), moved(own, other_core)
-    u1, d1, ownx = wall((u1, d1, ownx))
-
-    u2, d2 = moved(u1, along(1)), moved(d1, along(-1))
-    u1x, d1x = moved(u1, other_core), moved(d1, other_core)
-    a, across = call(first_cut_kernel, info, [own, ownx], (jax.ShapeDtypeStruct((2, 128, 1024), BF16), SLICES), 1)
-    a = moved(a, hub_ahead(0))
-    u2, d2, u1x, d1x, a, across = wall((u2, d2, u1x, d1x, a, across))
-
-    u3, d3 = moved(u2, along(1)), moved(d2, along(-1))
-    u2x, d2x = moved(u2, other_core), moved(d2, other_core)
-    near = call(cut_kernel, info, [own, u1, d1, ownx, u1x, d1x], jax.ShapeDtypeStruct((3, 2, 128, 128), BF16), 1)
-    near, across = moved(near, hub_ahead(0)), moved(across, hub_ahead(4))
+    ownx = moved(own, other_core)
+
+    p1, q1 = moved(own, onward), moved(ownx, onward)
+    a = moved(call(first_cut_kernel, info, [own, ownx], jax.ShapeDtypeStruct((2, 128, 1024), BF16), 1), hub_ahead(0))
+
+    p2, p1x = moved(p1, onward), moved(p1, other_core)
+    q2, q1x = moved(q1, onward), moved(q1, other_core)
+    first_three = [own, p1, q1x, ownx, q1, p1x]
+    near = call(cut_kernel, info, first_three, jax.ShapeDtypeStruct((3, 2, 128, 128), BF16), 1)
+    near = moved(near, hub_ahead(0))
+    p2, a = wall((p2, a))
+
+    p3, p2x = moved(p2, onward), moved(p2, other_core)
+    q3, q2x = moved(q2, onward), moved(q2, other_core)
+    across = moved(call(across_kernel, info, [p2, q2], SLICES, 1), hub_ahead(2))
     acc = call(
-        lambda *refs: products_kernel(OFFSETS[:3], *refs),
-        info,
-        [a, own, u1, d1, ownx, u1x, d1x],
-        block_of_products,
-        1,
-    )
-    u3, d3, u2x, d2x, near, across, acc = wall((u3, d3, u2x, d2x, near, across, acc))
-
-    far_0, far_1 = moved(u3[0], along(1)), moved(d3[1], along(-1))
-    u3x, d3x = moved(u3, other_core), moved(d3, other_core)
-    late = call(
-        cut_kernel, info, [u2, d2, u3, d3, u2x, d2x, u3x, d3x], jax.ShapeDtypeStruct((4, 2, 128, 128), BF16), 1
-    )
+        lambda *refs: products_kernel(OFFSETS[:3], *refs), info, [a] + first_three, block_of_products, 1
+    )
+    p3, near = wall((p3, near))
+
+    p4, p3x = moved(p3, onward), moved(p3, other_core)
+    q3x = moved(q3, other_core)
+    next_four = [p2, q2x, p3, q3x, q2, p2x, q3, p3x]
+    late = call(cut_kernel, info, next_four, jax.ShapeDtypeStruct((4, 2, 128, 128), BF16), 1)
     late = moved(late, hub_ahead(0))
     acc = call(
-        lambda *refs: products_kernel(OFFSETS[3:7], *refs),
-        info,
-        [a, u2, d2, u3, d3, u2x, d2x, u3x, d3x, acc],
-        block_of_products,
-        1,
-    )
-    far_0, far_1, late, acc = wall((far_0, far_1, late, acc))
-
-    far_0x, far_1x = moved(far_0, other_core), moved(far_1, other_core)
+        lambda *refs: products_kernel(OFFSETS[3:7], *refs), info, [a] + next_four + [acc], block_of_products, 1
+    )
+    p4, across, acc, late = wall((p4, across, acc, late))
+
+    p4x = moved(p4, other_core)
     drhs, crossed = call(
         crossed_kernel,
         info,
-        [near, late, across, own, u1, d1, u2, d2, u3, d3, ownx, u1x, d1x, u2x, d2x, u3x, d3x],
+        [near, late, across] + first_three[:3] + next_four[:4] + first_three[3:] + next_four[4:],
         (jax.ShapeDtypeStruct((2048, 256), BF16), jax.ShapeDtypeStruct((256, 1024), BF16)),
         1,
     )
@@ -244,7 +241,7 @@
     keep, send, trace = call(
         last_kernel,
         info,
-        [a, far_0, far_1, far_0x, far_1x, acc, drhs, crossed],
+        [a, p4, p4x, acc, drhs, crossed],
         (half_block, half_block, jax.ShapeDtypeStruct((1, 128), F32)),
         1,
         [pltpu.VMEM((256, 1024), BF16)],

time: 123 us -> 97.5 us (0.79)
  the two profiles are of different devices: /device:TPU:1 before, /device:TPU:8 now
where the time goes in v3:
time: 97.5 us; the launch traced here: 97.4 us
  waiting for transfers between devices  50 us (51%)
  starting transfers between devices  36.8 us (38%)
  Pallas kernels  8.22 us (8%)
  other arithmetic  1.56 us (2%)
    ppermute x28, waiting for transfers between devices, moved(): lax.ppermute(block, BOTH, [(index_of(*at), index_of(*route(*at))) for at...  50 us
    ppermute x28, starting transfers between devices, moved(): lax.ppermute(block, BOTH, [(index_of(*at), index_of(*route(*at))) for at...  36.8 us
    pallas_call x8, Pallas kernels, call(): pl.pallas_call(kernel, out_shape=out_shape, in_specs=[SMEM] + [VMEM] * le...  8.22 us
  transfers between devices with their start and end apart: 28, of which 16 were waited for; matrix products, arithmetic and copies ran while one was open for 1% of the time, Pallas kernels for 7%

profile of v3, /device:TPU:8, one launch (start us, length us, event | category | flops | bytes accessed | tf_op | source)
XLA Modules:
  0.0 97.4 jit_solution(10671066076986799195)
XLA Ops:
  0.6 0.0 copy-start
  0.6 1.7 %collective-permute-start = (bf16[2,2,64,1024]{3,2,1,0:T(8,128)(2,1)}, bf16[2,2,64,1024]{3,2,1,0:T(8,128)(2,1)S(1)}, u32[]{:S(2)}, u32[]{:S(2)}) collective-permute-start(bf16[2,2,64,1024]{3,2,1,0:T(8,128)(2,1)} %bitcast.15), channel_id=1, source_target_pairs={{0,128},{1,144},{2,130},{3,146},{4,132},{5,148},{6,134},{7,150},{8... | collective-permute-start | bytes 1572872 | tf_op jit(solution)/shard_map/ppermute | solution.py:27
  2.3 8.0 %collective-permute-done.own.refs_0_.refs_2_ = bf16[2,2,64,1024]{3,2,1,0:T(8,128)(2,1)S(1)} collective-permute-done((bf16[2,2,64,1024]{3,2,1,0:T(8,128)(2,1)}, bf16[2,2,64,1024]{3,2,1,0:T(8,128)(2,1)S(1)}, u32[]{:S(2)}, u32[]{:S(2)}) %collective-permute-start) | collective-permute-done | bytes 524320 | tf_op jit(solution)/shard_map/ppermute | solution.py:27
  10.3 0.0 collective-permute-start.3
  10.3 1.8 %collective-permute-start.1 = (bf16[2,2,64,1024]{3,2,1,0:T(8,128)(2,1)S(1)}, bf16[2,2,64,1024]{3,2,1,0:T(8,128)(2,1)S(1)}, u32[]{:S(2)}, u32[]{:S(2)}) collective-permute-start(bf16[2,2,64,1024]{3,2,1,0:T(8,128)(2,1)S(1)} %collective-permute-done.own.refs_0_.refs_2_), channel_id=1, source_target_pairs={{0,2},{1,3},{2,4},{3,5},{4,6},{5,7},{6,8},{7,9},{8,10},{9,11},{10,... | collective-permute-start | bytes 1572872 | tf_op jit(solution)/shard_map/ppermute | solution.py:27
  12.0 0.2 collective-permute-done.3.other.refs_3_.refs_5_.refs_7_
  12.2 1.8 %collective-permute-start.6 = (bf16[2,2,64,1024]{3,2,1,0:T(8,128)(2,1)S(1)}, bf16[2,2,64,1024]{3,2,1,0:T(8,128)(2,1)S(1)}, u32[]{:S(2)}, u32[]{:S(2)}) collective-permute-start(bf16[2,2,64,1024]{3,2,1,0:T(8,128)(2,1)S(1)} %collective-permute-done.3.other.refs_3_.refs_5_.refs_7_), channel_id=1, source_target_pairs={{0,2},{1,3},{2,4},{3,5},{4,6},{5,7},{6,8},{7,9},{8,10},{9,11},{10,... | collective-permute-start | bytes 1572872 | tf_op jit(solution)/shard_map/ppermute | solution.py:27
  14.0 0.1 pad_add_fusion.info.refs_0_
  14.0 0.6 shard_map.41
  14.6 3.0 %collective-permute-start.4 = (bf16[2,128,1024]{2,1,0:T(8,128)(2,1)S(1)}, bf16[2,128,1024]{2,1,0:T(8,128)(2,1)S(1)}, u32[]{:S(2)}, u32[]{:S(2)}) collective-permute-start(bf16[2,128,1024]{2,1,0:T(8,128)(2,1)S(1)} %shard_map.41), channel_id=1, source_target_pairs={{0,33},{1,0},{2,35},{3,2},{4,37},{5,4},{6,39},{7,6},{8,41},{9,8},{... | collective-permute-start | bytes 1572872 | tf_op jit(solution)/shard_map/ppermute | solution.py:27
  17.6 5.5 %collective-permute-done.1.refs_1_.refs_3_ = bf16[2,2,64,1024]{3,2,1,0:T(8,128)(2,1)S(1)} collective-permute-done((bf16[2,2,64,1024]{3,2,1,0:T(8,128)(2,1)S(1)}, bf16[2,2,64,1024]{3,2,1,0:T(8,128)(2,1)S(1)}, u32[]{:S(2)}, u32[]{:S(2)}) %collective-permute-start.1) | collective-permute-done | bytes 524320 | tf_op jit(solution)/shard_map/ppermute | solution.py:27
  23.1 0.0 collective-permute-start.2
  23.1 5.6 %collective-permute-done.6.refs_4_.refs_6_.refs_8_ = bf16[2,2,64,1024]{3,2,1,0:T(8,128)(2,1)S(1)} collective-permute-done((bf16[2,2,64,1024]{3,2,1,0:T(8,128)(2,1)S(1)}, bf16[2,2,64,1024]{3,2,1,0:T(8,128)(2,1)S(1)}, u32[]{:S(2)}, u32[]{:S(2)}) %collective-permute-start.6) | collective-permute-done | bytes 524320 | tf_op jit(solution)/shard_map/ppermute | solution.py:27
  28.8 0.0 collective-permute-start.11
  28.8 2.6 %collective-permute-start.8 = (bf16[2,2,64,1024]{3,2,1,0:T(8,128)(2,1)S(1)}, bf16[2,2,64,1024]{3,2,1,0:T(8,128)(2,1)S(1)}, u32[]{:S(2)}, u32[]{:S(2)}) collective-permute-start(bf16[2,2,64,1024]{3,2,1,0:T(8,128)(2,1)S(1)} %collective-permute-done.1.refs_1_.refs_3_), channel_id=1, source_target_pairs={{0,16},{1,17},{2,18},{3,19},{4,20},{5,21},{6,22},{7,23},{8,24},{9,... | collective-permute-start | bytes 1572872 | tf_op jit(solution)/shard_map/ppermute | solution.py:27
  31.4 0.0 collective-permute-start.7
  31.4 3.0 %collective-permute-done.2.own.refs_2_.refs_0_.refs_3_ = bf16[2,2,64,1024]{3,2,1,0:T(8,128)(2,1)S(1)} collective-permute-done((bf16[2,2,64,1024]{3,2,1,0:T(8,128)(2,1)S(1)}, bf16[2,2,64,1024]{3,2,1,0:T(8,128)(2,1)S(1)}, u32[]{:S(2)}, u32[]{:S(2)}) %collective-permute-start.2) | collective-permute-done | bytes 524320 | tf_op jit(solution)/shard_map/ppermute | solution.py:27
  34.4 5.6 %collective-permute-done.11.other.refs_6_.refs_4_.refs_10_ = bf16[2,2,64,1024]{3,2,1,0:T(8,128)(2,1)S(1)} collective-permute-done((bf16[2,2,64,1024]{3,2,1,0:T(8,128)(2,1)S(1)}, bf16[2,2,64,1024]{3,2,1,0:T(8,128)(2,1)S(1)}, u32[]{:S(2)}, u32[]{:S(2)}) %collective-permute-start.11) | collective-permute-done | bytes 524320 | tf_op jit(solution)/shard_map/ppermute | solution.py:27
  40.0 0.0 collective-permute-start.14
  40.0 0.0 collective-permute-done.8.refs_5_.refs_7_.refs_9_
  40.0 0.0 collective-permute-done.7.refs_2_.refs_4_
  40.0 0.6 shard_map.42
  40.6 3.0 %collective-permute-start.9 = (bf16[3,2,128,128]{3,2,1,0:T(8,128)(2,1)S(1)}, bf16[3,2,128,128]{3,2,1,0:T(8,128)(2,1)S(1)}, u32[]{:S(2)}, u32[]{:S(2)}) collective-permute-start(bf16[3,2,128,128]{3,2,1,0:T(8,128)(2,1)S(1)} %shard_map.42), channel_id=1, source_target_pairs={{0,33},{1,0},{2,35},{3,2},{4,37},{5,4},{6,39},{7,6},{8,41},{9,8},{... | collective-permute-start | bytes 589832 | tf_op jit(solution)/shard_map/ppermute | solution.py:27
  43.6 0.6 collective-permute-start.16
  44.2 0.0 collective-permute-start.13
  44.2 1.4 %collective-permute-done.5.refs_4_.refs_2_.refs_5_ = bf16[2,2,64,1024]{3,2,1,0:T(8,128)(2,1)S(1)} collective-permute-done((bf16[2,2,64,1024]{3,2,1,0:T(8,128)(2,1)S(1)}, bf16[2,2,64,1024]{3,2,1,0:T(8,128)(2,1)S(1)}, u32[]{:S(2)}, u32[]{:S(2)}) %collective-permute-start.5) | collective-permute-done | bytes 524320 | tf_op jit(solution)/shard_map/ppermute | solution.py:27
  45.6 2.9 %collective-permute-done.9.near = bf16[3,2,128,128]{3,2,1,0:T(8,128)(2,1)S(1)} collective-permute-done((bf16[3,2,128,128]{3,2,1,0:T(8,128)(2,1)S(1)}, bf16[3,2,128,128]{3,2,1,0:T(8,128)(2,1)S(1)}, u32[]{:S(2)}, u32[]{:S(2)}) %collective-permute-start.9) | collective-permute-done | bytes 196640 | tf_op jit(solution)/shard_map/ppermute | solution.py:27
  48.5 1.2 %collective-permute-start.17 = (bf16[2,2,64,1024]{3,2,1,0:T(8,128)(2,1)S(1)}, bf16[2,2,64,1024]{3,2,1,0:T(8,128)(2,1)S(1)}, u32[]{:S(2)}, u32[]{:S(2)}) collective-permute-start(bf16[2,2,64,1024]{3,2,1,0:T(8,128)(2,1)S(1)} %collective-permute-done.5.refs_4_.refs_2_.refs_5_), channel_id=1, source_target_pairs={{0,16},{1,17},{2,18},{3,19},{4,20},{5,21},{6,22},{7,23},{8,24},{9,... | collective-permute-start | bytes 1572872 | tf_op jit(solution)/shard_map/ppermute | solution.py:27
  49.6 1.6 %collective-permute-done.14.refs_8_.refs_6_.refs_12_ = bf16[2,2,64,1024]{3,2,1,0:T(8,128)(2,1)S(1)} collective-permute-done((bf16[2,2,64,1024]{3,2,1,0:T(8,128)(2,1)S(1)}, bf16[2,2,64,1024]{3,2,1,0:T(8,128)(2,1)S(1)}, u32[]{:S(2)}, u32[]{:S(2)}) %collective-permute-start.14) | collective-permute-done | bytes 524320 | tf_op jit(solution)/shard_map/ppermute | solution.py:27
  51.2 0.0 collective-permute-start.15
  51.2 0.0 collective-permute-start.10
  51.2 0.0 collective-permute-done.16.refs_7_.refs_5_.refs_11_
  51.2 0.0 collective-permute-done.13.refs_3_.refs_1_.refs_4_
  51.2 0.0 collective-permute-done.17.refs_9_.refs_7_.refs_13_
  51.3 1.9 %collective-permute-done.15.refs_5_.refs_3_.refs_6_ = bf16[2,2,64,1024]{3,2,1,0:T(8,128)(2,1)S(1)} collective-permute-done((bf16[2,2,64,1024]{3,2,1,0:T(8,128)(2,1)S(1)}, bf16[2,2,64,1024]{3,2,1,0:T(8,128)(2,1)S(1)}, u32[]{:S(2)}, u32[]{:S(2)}) %collective-permute-start.15) | collective-permute-done | bytes 524320 | tf_op jit(solution)/shard_map/ppermute | solution.py:27
  53.1 0.6 shard_map.46
  53.8 3.2 %collective-permute-start.18 = (bf16[4,2,128,128]{3,2,1,0:T(8,128)(2,1)S(1)}, bf16[4,2,128,128]{3,2,1,0:T(8,128)(2,1)S(1)}, u32[]{:S(2)}, u32[]{:S(2)}) collective-permute-start(bf16[4,2,128,128]{3,2,1,0:T(8,128)(2,1)S(1)} %shard_map.46), channel_id=1, source_target_pairs={{0,33},{1,0},{2,35},{3,2},{4,37},{5,4},{6,39},{7,6},{8,41},{9,8},{... | collective-permute-start | bytes 786440 | tf_op jit(solution)/shard_map/ppermute | solution.py:27
  56.9 0.6 shard_map.43
  57.5 2.9 %collective-permute-start.12 = (bf16[2,128,128]{2,1,0:T(8,128)(2,1)S(1)}, bf16[2,128,128]{2,1,0:T(8,128)(2,1)S(1)}, u32[]{:S(2)}, u32[]{:S(2)}) collective-permute-start(bf16[2,128,128]{2,1,0:T(8,128)(2,1)S(1)} %shard_map.43), channel_id=1, source_target_pairs={{0,37},{1,4},{2,39},{3,6},{4,41},{5,8},{6,43},{7,10},{8,45},{9,12}... | collective-permute-start | bytes 196616 | tf_op jit(solution)/shard_map/ppermute | solution.py:27
  60.4 1.1 %shard_map.44.refs_10_ = f32[256,1024]{1,0:T(8,128)S(1)} custom-call(s32[6]{0:T(128)S(1)} %pad_add_fusion.info.refs_0_, bf16[2,128,1024]{2,1,0:T(8,128)(2,1)S(1)} %collective-permute-done.4.refs_1_.a_ref, bf16[2,2,64,1024]{3,2,1,0:T(8,128)(2,1)S(1)} %collective-permute-done.own.refs_0_.refs_2_, ...), custom_call_target="tpu_custom_call" | custom-call | flops 1 | bytes 1048576 | tf_op jit(solution)/shard_map/pallas_call | solution.py:73
  61.6 1.3 %shard_map.45.acc = f32[256,1024]{1,0:T(8,128)S(1)} custom-call(s32[6]{0:T(128)S(1)} %pad_add_fusion.info.refs_0_, bf16[2,128,1024]{2,1,0:T(8,128)(2,1)S(1)} %collective-permute-done.4.refs_1_.a_ref, bf16[2,2,64,1024]{3,2,1,0:T(8,128)(2,1)S(1)} %collective-permute-done.2.own.refs_2_.refs_0_.refs_3_, ...), custom_call_target="tpu_custom_call" | custom-call | flops 1 | bytes 1048576 | tf_op jit(solution)/shard_map/pallas_call | solution.py:73
  62.9 4.5 %collective-permute-done.12.across = bf16[2,128,128]{2,1,0:T(8,128)(2,1)S(1)} collective-permute-done((bf16[2,128,128]{2,1,0:T(8,128)(2,1)S(1)}, bf16[2,128,128]{2,1,0:T(8,128)(2,1)S(1)}, u32[]{:S(2)}, u32[]{:S(2)}) %collective-permute-start.12) | collective-permute-done | bytes 65568 | tf_op jit(solution)/shard_map/ppermute | solution.py:27
  67.3 0.0 collective-permute-done.10.own
  67.3 0.0 collective-permute-done.18.late
  67.3 0.0 collective-permute-start.19
  67.4 1.9 %shard_map.47 = (bf16[2048,256]{1,0:T(8,128)(2,1)S(1)}, bf16[256,1024]{1,0:T(8,128)(2,1)S(1)}) custom-call(s32[6]{0:T(128)S(1)} %pad_add_fusion.info.refs_0_, bf16[3,2,128,128]{3,2,1,0:T(8,128)(2,1)S(1)} %collective-permute-done.9.near, bf16[4,2,128,128]{3,2,1,0:T(8,128)(2,1)S(1)} %collective-permute-done.18.late, ...), custom_call_target="tpu_custom_call" | custom-call | flops 1 | bytes 1048576 | tf_op jit(solution)/shard_map/pallas_call | solution.py:73
  69.3 1.5 %shard_map.48 = (bf16[2,64,1024]{2,1,0:T(8,128)(2,1)S(1)}, bf16[2,64,1024]{2,1,0:T(8,128)(2,1)S(1)}, f32[1,128]{1,0:T(1,128)S(1)}) custom-call(s32[6]{0:T(128)S(1)} %pad_add_fusion.info.refs_0_, bf16[2,128,1024]{2,1,0:T(8,128)(2,1)S(1)} %collective-permute-done.4.refs_1_.a_ref, bf16[2,2,64,1024]{3,2,1,0:T(8,128)(2,1)S(1)} %collective-permute-done.10.own, ...), custom_call_target="tpu_custom_call" | custom-call | flops 1 | bytes 1048576 | tf_op jit(solution)/shard_map/pallas_call | solution.py:73
  70.8 0.0 collective-permute-start.21
  70.8 3.2 %collective-permute-start.20 = (f32[1,128]{1,0:T(1,128)S(1)}, f32[1,128]{1,0:T(1,128)S(1)}, u32[]{:S(2)}, u32[]{:S(2)}) collective-permute-start(f32[1,128]{1,0:T(1,128)S(1)} %get-tuple-element.30), channel_id=1, source_target_pairs={{0,14},{1,15},{2,0},{3,1},{4,2},{5,3},{6,4},{7,5},{8,6},{9,7},{10,... | collective-permute-start | bytes 1544 | tf_op jit(solution)/shard_map/ppermute | solution.py:27
  74.0 2.6 %collective-permute-start.24 = (bf16[2,64,1024]{2,1,0:T(8,128)(2,1)S(1)}, bf16[2,64,1024]{2,1,0:T(8,128)(2,1)S(1)}, u32[]{:S(2)}, u32[]{:S(2)}) collective-permute-start(bf16[2,64,1024]{2,1,0:T(8,128)(2,1)S(1)} %get-tuple-element.33), channel_id=1, source_target_pairs={{0,128},{1,112},{2,130},{3,114},{4,132},{5,116},{6,134},{7,118},{8... | collective-permute-start | bytes 786440 | tf_op jit(solution)/shard_map/ppermute | solution.py:27
  76.6 0.2 collective-permute-start.25
  76.9 0.0 collective-permute-done.21
  76.9 0.0 collective-permute-done.20
  76.9 3.8 %collective-permute-start.22 = (f32[1,128]{1,0:T(1,128)S(1)}, f32[1,128]{1,0:T(1,128)S(1)}, u32[]{:S(2)}, u32[]{:S(2)}) collective-permute-start(f32[1,128]{1,0:T(1,128)S(1)} %get-tuple-element.31), channel_id=1, source_target_pairs={{0,6},{1,7},{2,8},{3,9},{4,10},{5,11},{6,12},{7,13},{8,14},{9,15},... | collective-permute-start | bytes 1544 | tf_op jit(solution)/shard_map/ppermute | solution.py:27
  80.7 1.4 %collective-permute-start.23 = (f32[1,128]{1,0:T(1,128)S(1)}, f32[1,128]{1,0:T(1,128)S(1)}, u32[]{:S(2)}, u32[]{:S(2)}) collective-permute-start(f32[1,128]{1,0:T(1,128)S(1)} %get-tuple-element.32), channel_id=1, source_target_pairs={{0,10},{1,11},{2,12},{3,13},{4,14},{5,15},{6,0},{7,1},{8,2},{9,3},... | collective-permute-start | bytes 1544 | tf_op jit(solution)/shard_map/ppermute | solution.py:27
  82.0 1.5 %collective-permute-done.22 = f32[1,128]{1,0:T(1,128)S(1)} collective-permute-done((f32[1,128]{1,0:T(1,128)S(1)}, f32[1,128]{1,0:T(1,128)S(1)}, u32[]{:S(2)}, u32[]{:S(2)}) %collective-permute-start.22) | collective-permute-done | bytes 544 | tf_op jit(solution)/shard_map/ppermute | solution.py:27
  83.5 2.5 %collective-permute-done.23 = f32[1,128]{1,0:T(1,128)S(1)} collective-permute-done((f32[1,128]{1,0:T(1,128)S(1)}, f32[1,128]{1,0:T(1,128)S(1)}, u32[]{:S(2)}, u32[]{:S(2)}) %collective-permute-start.23) | collective-permute-done | bytes 544 | tf_op jit(solution)/shard_map/ppermute | solution.py:27
  86.0 3.3 %collective-permute-done.25 = bf16[2,64,1024]{2,1,0:T(8,128)(2,1)S(1)} collective-permute-done((bf16[2,64,1024]{2,1,0:T(8,128)(2,1)S(1)}, bf16[2,64,1024]{2,1,0:T(8,128)(2,1)S(1)}, u32[]{:S(2)}, u32[]{:S(2)}) %collective-permute-start.25) | collective-permute-done | bytes 262176 | tf_op jit(solution)/shard_map/ppermute | solution.py:27
  89.3 3.9 %collective-permute-start.27 = (f32[1,128]{1,0:T(1,128)S(1)}, f32[1,128]{1,0:T(1,128)S(1)}, u32[]{:S(2)}, u32[]{:S(2)}) collective-permute-start(f32[1,128]{1,0:T(1,128)S(1)} %add_add_fusion), channel_id=1, source_target_pairs={{0,129},{1,113},{2,131},{3,115},{4,133},{5,117},{6,135},{7,119},{8... | collective-permute-start | bytes 1544 | tf_op jit(solution)/shard_map/ppermute | solution.py:27
  93.2 0.9 maximum_select_fusion
  94.1 0.4 collective-permute-done.27
  94.5 2.2 %collective-permute-done.26 = f32[1,128]{1,0:T(1,128)S(1)} collective-permute-done((f32[1,128]{1,0:T(1,128)S(1)}, f32[1,128]{1,0:T(1,128)S(1)}, u32[]{:S(2)}, u32[]{:S(2)}) %collective-permute-start.26) | collective-permute-done | bytes 544 | tf_op jit(solution)/shard_map/ppermute | solution.py:27
  96.8 0.1 reshape.77
  96.9 0.6 broadcast_multiply_fusion
  (11 shorter events, 0.1 us)
Async XLA Ops:
  0.6 13.3 %copy-start = (s32[2,1,4]{2,1,0:T(1,128)S(1)}, s32[2,1,4]{2,1,0:T(1,128)}, u32[]{:S(2)}) copy-start(s32[2,1,4]{2,1,0:T(1,128)} %param.3) | copy-start | bytes 100
  0.6 9.6 %collective-permute-start = (bf16[2,2,64,1024]{3,2,1,0:T(8,128)(2,1)}, bf16[2,2,64,1024]{3,2,1,0:T(8,128)(2,1)S(1)}, u32[]{:S(2)}, u32[]{:S(2)}) collective-permute-start(bf16[2,2,64,1024]{3,2,1,0:T(8,128)(2,1)} %bitcast.15), channel_id=1, source_target_pairs={{0,128},{1,144},{2,130},{3,146},{4,132},{5,148},{6,134},{7,150},{8... | collective-permute-start | bytes 1572872 | tf_op jit(solution)/shard_map/ppermute | solution.py:27
  10.3 1.9 %collective-permute-start.3 = (bf16[2,2,64,1024]{3,2,1,0:T(8,128)(2,1)S(1)}, bf16[2,2,64,1024]{3,2,1,0:T(8,128)(2,1)S(1)}, u32[]{:S(2)}, u32[]{:S(2)}) collective-permute-start(bf16[2,2,64,1024]{3,2,1,0:T(8,128)(2,1)S(1)} %collective-permute-done.own.refs_0_.refs_2_), channel_id=1, source_target_pairs={{0,16},{1,17},{2,18},{3,19},{4,20},{5,21},{6,22},{7,23},{8,24},{9,... | collective-permute-start | bytes 1572872 | tf_op jit(solution)/shard_map/ppermute | solution.py:27
  10.3 12.8 %collective-permute-start.1 = (bf16[2,2,64,1024]{3,2,1,0:T(8,128)(2,1)S(1)}, bf16[2,2,64,1024]{3,2,1,0:T(8,128)(2,1)S(1)}, u32[]{:S(2)}, u32[]{:S(2)}) collective-permute-start(bf16[2,2,64,1024]{3,2,1,0:T(8,128)(2,1)S(1)} %collective-permute-done.own.refs_0_.refs_2_), channel_id=1, source_target_pairs={{0,2},{1,3},{2,4},{3,5},{4,6},{5,7},{6,8},{7,9},{8,10},{9,11},{10,... | collective-permute-start | bytes 1572872 | tf_op jit(solution)/shard_map/ppermute | solution.py:27
  12.2 16.6 %collective-permute-start.6 = (bf16[2,2,64,1024]{3,2,1,0:T(8,128)(2,1)S(1)}, bf16[2,2,64,1024]{3,2,1,0:T(8,128)(2,1)S(1)}, u32[]{:S(2)}, u32[]{:S(2)}) collective-permute-start(bf16[2,2,64,1024]{3,2,1,0:T(8,128)(2,1)S(1)} %collective-permute-done.3.other.refs_3_.refs_5_.refs_7_), channel_id=1, source_target_pairs={{0,2},{1,3},{2,4},{3,5},{4,6},{5,7},{6,8},{7,9},{8,10},{9,11},{10,... | collective-permute-start | bytes 1572872 | tf_op jit(solution)/shard_map/ppermute | solution.py:27
  14.6 16.7 %collective-permute-start.4 = (bf16[2,128,1024]{2,1,0:T(8,128)(2,1)S(1)}, bf16[2,128,1024]{2,1,0:T(8,128)(2,1)S(1)}, u32[]{:S(2)}, u32[]{:S(2)}) collective-permute-start(bf16[2,128,1024]{2,1,0:T(8,128)(2,1)S(1)} %shard_map.41), channel_id=1, source_target_pairs={{0,33},{1,0},{2,35},{3,2},{4,37},{5,4},{6,39},{7,6},{8,41},{9,8},{... | collective-permute-start | bytes 1572872 | tf_op jit(solution)/shard_map/ppermute | solution.py:27
  23.1 11.2 %collective-permute-start.2 = (bf16[2,2,64,1024]{3,2,1,0:T(8,128)(2,1)S(1)}, bf16[2,2,64,1024]{3,2,1,0:T(8,128)(2,1)S(1)}, u32[]{:S(2)}, u32[]{:S(2)}) collective-permute-start(bf16[2,2,64,1024]{3,2,1,0:T(8,128)(2,1)S(1)} %collective-permute-done.1.refs_1_.refs_3_), channel_id=1, source_target_pairs={{0,2},{1,3},{2,4},{3,5},{4,6},{5,7},{6,8},{7,9},{8,10},{9,11},{10,... | collective-permute-start | bytes 1572872 | tf_op jit(solution)/shard_map/ppermute | solution.py:27
  28.8 11.2 %collective-permute-start.11 = (bf16[2,2,64,1024]{3,2,1,0:T(8,128)(2,1)S(1)}, bf16[2,2,64,1024]{3,2,1,0:T(8,128)(2,1)S(1)}, u32[]{:S(2)}, u32[]{:S(2)}) collective-permute-start(bf16[2,2,64,1024]{3,2,1,0:T(8,128)(2,1)S(1)} %collective-permute-done.6.refs_4_.refs_6_.refs_8_), channel_id=1, source_target_pairs={{0,2},{1,3},{2,4},{3,5},{4,6},{5,7},{6,8},{7,9},{8,10},{9,11},{10,... | collective-permute-start | bytes 1572872 | tf_op jit(solution)/shard_map/ppermute | solution.py:27
  28.8 11.2 %collective-permute-start.8 = (bf16[2,2,64,1024]{3,2,1,0:T(8,128)(2,1)S(1)}, bf16[2,2,64,1024]{3,2,1,0:T(8,128)(2,1)S(1)}, u32[]{:S(2)}, u32[]{:S(2)}) collective-permute-start(bf16[2,2,64,1024]{3,2,1,0:T(8,128)(2,1)S(1)} %collective-permute-done.1.refs_1_.refs_3_), channel_id=1, source_target_pairs={{0,16},{1,17},{2,18},{3,19},{4,20},{5,21},{6,22},{7,23},{8,24},{9,... | collective-permute-start | bytes 1572872 | tf_op jit(solution)/shard_map/ppermute | solution.py:27
  31.4 8.6 %collective-permute-start.7 = (bf16[2,2,64,1024]{3,2,1,0:T(8,128)(2,1)S(1)}, bf16[2,2,64,1024]{3,2,1,0:T(8,128)(2,1)S(1)}, u32[]{:S(2)}, u32[]{:S(2)}) collective-permute-start(bf16[2,2,64,1024]{3,2,1,0:T(8,128)(2,1)S(1)} %collective-permute-done.6.refs_4_.refs_6_.refs_8_), channel_id=1, source_target_pairs={{0,16},{1,17},{2,18},{3,19},{4,20},{5,21},{6,22},{7,23},{8,24},{9,... | collective-permute-start | bytes 1572872 | tf_op jit(solution)/shard_map/ppermute | solution.py:27
  34.4 11.2 %collective-permute-start.5 = (bf16[2,2,64,1024]{3,2,1,0:T(8,128)(2,1)S(1)}, bf16[2,2,64,1024]{3,2,1,0:T(8,128)(2,1)S(1)}, u32[]{:S(2)}, u32[]{:S(2)}) collective-permute-start(bf16[2,2,64,1024]{3,2,1,0:T(8,128)(2,1)S(1)} %collective-permute-done.2.own.refs_2_.refs_0_.refs_3_), channel_id=1, source_target_pairs={{0,2},{1,3},{2,4},{3,5},{4,6},{5,7},{6,8},{7,9},{8,10},{9,11},{10,... | collective-permute-start | bytes 1572872 | tf_op jit(solution)/shard_map/ppermute | solution.py:27
  40.0 11.2 %collective-permute-start.14 = (bf16[2,2,64,1024]{3,2,1,0:T(8,128)(2,1)S(1)}, bf16[2,2,64,1024]{3,2,1,0:T(8,128)(2,1)S(1)}, u32[]{:S(2)}, u32[]{:S(2)}) collective-permute-start(bf16[2,2,64,1024]{3,2,1,0:T(8,128)(2,1)S(1)} %collective-permute-done.11.other.refs_6_.refs_4_.refs_10_), channel_id=1, source_target_pairs={{0,2},{1,3},{2,4},{3,5},{4,6},{5,7},{6,8},{7,9},{8,10},{9,11},{10,... | collective-permute-start | bytes 1572872 | tf_op jit(solution)/shard_map/ppermute | solution.py:27
  40.6 7.9 %collective-permute-start.9 = (bf16[3,2,128,128]{3,2,1,0:T(8,128)(2,1)S(1)}, bf16[3,2,128,128]{3,2,1,0:T(8,128)(2,1)S(1)}, u32[]{:S(2)}, u32[]{:S(2)}) collective-permute-start(bf16[3,2,128,128]{3,2,1,0:T(8,128)(2,1)S(1)} %shard_map.42), channel_id=1, source_target_pairs={{0,33},{1,0},{2,35},{3,2},{4,37},{5,4},{6,39},{7,6},{8,41},{9,8},{... | collective-permute-start | bytes 589832 | tf_op jit(solution)/shard_map/ppermute | solution.py:27
  43.6 7.6 %collective-permute-start.16 = (bf16[2,2,64,1024]{3,2,1,0:T(8,128)(2,1)S(1)}, bf16[2,2,64,1024]{3,2,1,0:T(8,128)(2,1)S(1)}, u32[]{:S(2)}, u32[]{:S(2)}) collective-permute-start(bf16[2,2,64,1024]{3,2,1,0:T(8,128)(2,1)S(1)} %collective-permute-done.2.own.refs_2_.refs_0_.refs_3_), channel_id=1, source_target_pairs={{0,16},{1,17},{2,18},{3,19},{4,20},{5,21},{6,22},{7,23},{8,24},{9,... | collective-permute-start | bytes 1572872 | tf_op jit(solution)/shard_map/ppermute | solution.py:27
  44.2 7.0 %collective-permute-start.13 = (bf16[2,2,64,1024]{3,2,1,0:T(8,128)(2,1)S(1)}, bf16[2,2,64,1024]{3,2,1,0:T(8,128)(2,1)S(1)}, u32[]{:S(2)}, u32[]{:S(2)}) collective-permute-start(bf16[2,2,64,1024]{3,2,1,0:T(8,128)(2,1)S(1)} %collective-permute-done.11.other.refs_6_.refs_4_.refs_10_), channel_id=1, source_target_pairs={{0,16},{1,17},{2,18},{3,19},{4,20},{5,21},{6,22},{7,23},{8,24},{9,... | collective-permute-start | bytes 1572872 | tf_op jit(solution)/shard_map/ppermute | solution.py:27
  48.5 2.8 %collective-permute-start.17 = (bf16[2,2,64,1024]{3,2,1,0:T(8,128)(2,1)S(1)}, bf16[2,2,64,1024]{3,2,1,0:T(8,128)(2,1)S(1)}, u32[]{:S(2)}, u32[]{:S(2)}) collective-permute-start(bf16[2,2,64,1024]{3,2,1,0:T(8,128)(2,1)S(1)} %collective-permute-done.5.refs_4_.refs_2_.refs_5_), channel_id=1, source_target_pairs={{0,16},{1,17},{2,18},{3,19},{4,20},{5,21},{6,22},{7,23},{8,24},{9,... | collective-permute-start | bytes 1572872 | tf_op jit(solution)/shard_map/ppermute | solution.py:27
  51.2 1.9 %collective-permute-start.15 = (bf16[2,2,64,1024]{3,2,1,0:T(8,128)(2,1)S(1)}, bf16[2,2,64,1024]{3,2,1,0:T(8,128)(2,1)S(1)}, u32[]{:S(2)}, u32[]{:S(2)}) collective-permute-start(bf16[2,2,64,1024]{3,2,1,0:T(8,128)(2,1)S(1)} %collective-permute-done.14.refs_8_.refs_6_.refs_12_), channel_id=1, source_target_pairs={{0,16},{1,17},{2,18},{3,19},{4,20},{5,21},{6,22},{7,23},{8,24},{9,... | collective-permute-start | bytes 1572872 | tf_op jit(solution)/shard_map/ppermute | solution.py:27
  51.2 16.1 %collective-permute-start.10 = (bf16[2,2,64,1024]{3,2,1,0:T(8,128)(2,1)S(1)}, bf16[2,2,64,1024]{3,2,1,0:T(8,128)(2,1)S(1)}, u32[]{:S(2)}, u32[]{:S(2)}) collective-permute-start(bf16[2,2,64,1024]{3,2,1,0:T(8,128)(2,1)S(1)} %collective-permute-done.5.refs_4_.refs_2_.refs_5_), channel_id=1, source_target_pairs={{0,2},{1,3},{2,4},{3,5},{4,6},{5,7},{6,8},{7,9},{8,10},{9,11},{10,... | collective-permute-start | bytes 1572872 | tf_op jit(solution)/shard_map/ppermute | solution.py:27
  53.8 13.6 %collective-permute-start.18 = (bf16[4,2,128,128]{3,2,1,0:T(8,128)(2,1)S(1)}, bf16[4,2,128,128]{3,2,1,0:T(8,128)(2,1)S(1)}, u32[]{:S(2)}, u32[]{:S(2)}) collective-permute-start(bf16[4,2,128,128]{3,2,1,0:T(8,128)(2,1)S(1)} %shard_map.46), channel_id=1, source_target_pairs={{0,33},{1,0},{2,35},{3,2},{4,37},{5,4},{6,39},{7,6},{8,41},{9,8},{... | collective-permute-start | bytes 786440 | tf_op jit(solution)/shard_map/ppermute | solution.py:27
  57.5 9.8 %collective-permute-start.12 = (bf16[2,128,128]{2,1,0:T(8,128)(2,1)S(1)}, bf16[2,128,128]{2,1,0:T(8,128)(2,1)S(1)}, u32[]{:S(2)}, u32[]{:S(2)}) collective-permute-start(bf16[2,128,128]{2,1,0:T(8,128)(2,1)S(1)} %shard_map.43), channel_id=1, source_target_pairs={{0,37},{1,4},{2,39},{3,6},{4,41},{5,8},{6,43},{7,10},{8,45},{9,12}... | collective-permute-start | bytes 196616 | tf_op jit(solution)/shard_map/ppermute | solution.py:27
  67.3 1.9 %collective-permute-start.19 = (bf16[2,2,64,1024]{3,2,1,0:T(8,128)(2,1)S(1)}, bf16[2,2,64,1024]{3,2,1,0:T(8,128)(2,1)S(1)}, u32[]{:S(2)}, u32[]{:S(2)}) collective-permute-start(bf16[2,2,64,1024]{3,2,1,0:T(8,128)(2,1)S(1)} %collective-permute-done.10.own), channel_id=1, source_target_pairs={{0,16},{1,17},{2,18},{3,19},{4,20},{5,21},{6,22},{7,23},{8,24},{9,... | collective-permute-start | bytes 1572872 | tf_op jit(solution)/shard_map/ppermute | solution.py:27
  70.8 6.1 %collective-permute-start.21 = (f32[1,128]{1,0:T(1,128)S(1)}, f32[1,128]{1,0:T(1,128)S(1)}, u32[]{:S(2)}, u32[]{:S(2)}) collective-permute-start(f32[1,128]{1,0:T(1,128)S(1)} %get-tuple-element.30), channel_id=1, source_target_pairs={{0,2},{1,3},{2,4},{3,5},{4,6},{5,7},{6,8},{7,9},{8,10},{9,11},{10,... | collective-permute-start | bytes 1544 | tf_op jit(solution)/shard_map/ppermute | solution.py:27
  70.8 6.1 %collective-permute-start.20 = (f32[1,128]{1,0:T(1,128)S(1)}, f32[1,128]{1,0:T(1,128)S(1)}, u32[]{:S(2)}, u32[]{:S(2)}) collective-permute-start(f32[1,128]{1,0:T(1,128)S(1)} %get-tuple-element.30), channel_id=1, source_target_pairs={{0,14},{1,15},{2,0},{3,1},{4,2},{5,3},{6,4},{7,5},{8,6},{9,7},{10,... | collective-permute-start | bytes 1544 | tf_op jit(solution)/shard_map/ppermute | solution.py:27
  74.0 11.9 %collective-permute-start.24 = (bf16[2,64,1024]{2,1,0:T(8,128)(2,1)S(1)}, bf16[2,64,1024]{2,1,0:T(8,128)(2,1)S(1)}, u32[]{:S(2)}, u32[]{:S(2)}) collective-permute-start(bf16[2,64,1024]{2,1,0:T(8,128)(2,1)S(1)} %get-tuple-element.33), channel_id=1, source_target_pairs={{0,128},{1,112},{2,130},{3,114},{4,132},{5,116},{6,134},{7,118},{8... | collective-permute-start | bytes 786440 | tf_op jit(solution)/shard_map/ppermute | solution.py:27
  76.6 12.6 %collective-permute-start.25 = (bf16[2,64,1024]{2,1,0:T(8,128)(2,1)S(1)}, bf16[2,64,1024]{2,1,0:T(8,128)(2,1)S(1)}, u32[]{:S(2)}, u32[]{:S(2)}) collective-permute-start(bf16[2,64,1024]{2,1,0:T(8,128)(2,1)S(1)} %get-tuple-element.34), channel_id=1, source_target_pairs={{0,129},{1,113},{2,131},{3,115},{4,133},{5,117},{6,135},{7,119},{8... | collective-permute-start | bytes 786440 | tf_op jit(solution)/shard_map/ppermute | solution.py:27
  76.9 6.6 %collective-permute-start.22 = (f32[1,128]{1,0:T(1,128)S(1)}, f32[1,128]{1,0:T(1,128)S(1)}, u32[]{:S(2)}, u32[]{:S(2)}) collective-permute-start(f32[1,128]{1,0:T(1,128)S(1)} %get-tuple-element.31), channel_id=1, source_target_pairs={{0,6},{1,7},{2,8},{3,9},{4,10},{5,11},{6,12},{7,13},{8,14},{9,15},... | collective-permute-start | bytes 1544 | tf_op jit(solution)/shard_map/ppermute | solution.py:27
  80.7 5.3 %collective-permute-start.23 = (f32[1,128]{1,0:T(1,128)S(1)}, f32[1,128]{1,0:T(1,128)S(1)}, u32[]{:S(2)}, u32[]{:S(2)}) collective-permute-start(f32[1,128]{1,0:T(1,128)S(1)} %get-tuple-element.32), channel_id=1, source_target_pairs={{0,10},{1,11},{2,12},{3,13},{4,14},{5,15},{6,0},{7,1},{8,2},{9,3},... | collective-permute-start | bytes 1544 | tf_op jit(solution)/shard_map/ppermute | solution.py:27
  89.3 5.2 %collective-permute-start.27 = (f32[1,128]{1,0:T(1,128)S(1)}, f32[1,128]{1,0:T(1,128)S(1)}, u32[]{:S(2)}, u32[]{:S(2)}) collective-permute-start(f32[1,128]{1,0:T(1,128)S(1)} %add_add_fusion), channel_id=1, source_target_pairs={{0,129},{1,113},{2,131},{3,115},{4,133},{5,117},{6,135},{7,119},{8... | collective-permute-start | bytes 1544 | tf_op jit(solution)/shard_map/ppermute | solution.py:27
  93.2 3.5 %collective-permute-start.26 = (f32[1,128]{1,0:T(1,128)S(1)}, f32[1,128]{1,0:T(1,128)S(1)}, u32[]{:S(2)}, u32[]{:S(2)}) collective-permute-start(f32[1,128]{1,0:T(1,128)S(1)} %add_add_fusion), channel_id=1, source_target_pairs={{0,128},{1,112},{2,130},{3,114},{4,132},{5,116},{6,134},{7,118},{8... | collective-permute-start | bytes 1544 | tf_op jit(solution)/shard_map/ppermute | solution.py:27

commit v4 on v3

--- a/solution.py
+++ b/solution.py
@@ -39,10 +39,11 @@
     return (m, 1 - c, z, h)
 
 
-def to_hub(step):
+def to_hub(turn, step):
     def route(m, c, z, h):
         column, half = hub_of(2 * m + c)
-        return (column, h, z + step, half)
+        core = h ^ turn
+        return (column, core, z + (step if core == 0 else -step), half)
 
     return route
 
@@ -112,14 +113,17 @@
         a[part] = whole(info, own, other, info[2], part)
 
 
-def cut_kernel(info, *refs):
-    count = len(refs) // 2
-    for k in range(count):
-        cut(info, refs[k], refs[count + k], 0, refs[-1].at[k])
-
-
-def across_kernel(info, own, other, out):
-    cut(info, own, other, -2, out)
+def near_kernel(info, *refs):
+    for k in range(3):
+        cut(info, refs[k], refs[3 + k], 0, refs[-1].at[k])
+
+
+def middle_kernel(info, own, own_x, other, other_x, middle, down, up, across):
+    cut(info, own, other, 0, middle.at[0])
+    cut(info, own_x, other_x, 0, middle.at[1])
+    cut(info, own, other, -1, down)
+    cut(info, own_x, other_x, 1, up)
+    cut(info, own, other, -2, across)
 
 
 def left_side(info, a_ref, offset):
@@ -151,9 +155,9 @@
 OFFSETS = (0, 1, -1, 2, -2, 3, -3, 4)
 
 
-def crossed_kernel(info, near, late, across, *refs):
+def crossed_kernel(info, near, middle, down, up, across, *refs):
     own, other, drhs, crossed = refs[0:7], refs[7:14], refs[14], refs[15]
-    slices = [near.at[k] for k in range(3)] + [late.at[k] for k in range(4)] + [across]
+    slices = [near.at[0], near.at[1], near.at[2], middle.at[0], middle.at[1], down, up, across]
     for offset, piece in zip(OFFSETS, slices):
         top = pl.multiple_of(place_of(info, offset) * 128, 128)
         real, imag = piece[0], piece[1]
@@ -198,42 +202,57 @@
     wall = lax.optimization_barrier
     block_of_products = jax.ShapeDtypeStruct((256, 1024), F32)
 
-    own = moved(rows, to_hub(0))
-    ownx = moved(own, other_core)
-
-    p1, q1 = moved(own, onward), moved(ownx, onward)
-    a = moved(call(first_cut_kernel, info, [own, ownx], jax.ShapeDtypeStruct((2, 128, 1024), BF16), 1), hub_ahead(0))
+    p1, q1, own = moved(rows, to_hub(0, 1)), moved(rows, to_hub(1, 1)), moved(rows, to_hub(0, 0))
 
     p2, p1x = moved(p1, onward), moved(p1, other_core)
     q2, q1x = moved(q1, onward), moved(q1, other_core)
+    ownx = moved(own, other_core)
     first_three = [own, p1, q1x, ownx, q1, p1x]
-    near = call(cut_kernel, info, first_three, jax.ShapeDtypeStruct((3, 2, 128, 128), BF16), 1)
-    near = moved(near, hub_ahead(0))
-    p2, a = wall((p2, a))
-
+    a = call(first_cut_kernel, info, [own, ownx], jax.ShapeDtypeStruct((2, 128, 1024), BF16), 1)
+    near = call(near_kernel, info, first_three, jax.ShapeDtypeStruct((3, 2, 128, 128), BF16), 1)
+    q2, near, a = wall((q2, near, a))
+
+    a, near = moved(a, hub_ahead(0)), moved(near, hub_ahead(0))
     p3, p2x = moved(p2, onward), moved(p2, other_core)
     q3, q2x = moved(q2, onward), moved(q2, other_core)
-    across = moved(call(across_kernel, info, [p2, q2], SLICES, 1), hub_ahead(2))
-    acc = call(
-        lambda *refs: products_kernel(OFFSETS[:3], *refs), info, [a] + first_three, block_of_products, 1
-    )
-    p3, near = wall((p3, near))
-
+    next_two = [p2, q2x, q2, p2x]
+    middle, down, up, across = call(
+        middle_kernel,
+        info,
+        next_two,
+        (jax.ShapeDtypeStruct((2, 2, 128, 128), BF16), SLICES, SLICES, SLICES),
+        1,
+    )
+    q3, near, a, middle, down, up, across = wall((q3, near, a, middle, down, up, across))
+
+    middle, down = moved(middle, hub_ahead(0)), moved(down, hub_ahead(1))
+    up, across = moved(up, hub_ahead(-1)), moved(across, hub_ahead(2))
     p4, p3x = moved(p3, onward), moved(p3, other_core)
     q3x = moved(q3, other_core)
-    next_four = [p2, q2x, p3, q3x, q2, p2x, q3, p3x]
-    late = call(cut_kernel, info, next_four, jax.ShapeDtypeStruct((4, 2, 128, 128), BF16), 1)
-    late = moved(late, hub_ahead(0))
     acc = call(
-        lambda *refs: products_kernel(OFFSETS[3:7], *refs), info, [a] + next_four + [acc], block_of_products, 1
-    )
-    p4, across, acc, late = wall((p4, across, acc, late))
+        lambda *refs: products_kernel(OFFSETS[:5], *refs),
+        info,
+        [a] + first_three[:3] + next_two[:2] + first_three[3:] + next_two[2:],
+        block_of_products,
+        1,
+    )
+    p4, acc, middle, down, up, across = wall((p4, acc, middle, down, up, across))
 
     p4x = moved(p4, other_core)
+    last_two = [p3, q3x, q3, p3x]
+    acc = call(
+        lambda *refs: products_kernel(OFFSETS[5:7], *refs), info, [a] + last_two + [acc], block_of_products, 1
+    )
     drhs, crossed = call(
         crossed_kernel,
         info,
-        [near, late, across] + first_three[:3] + next_four[:4] + first_three[3:] + next_four[4:],
+        [near, middle, down, up, across]
+        + first_three[:3]
+        + next_two[:2]
+        + last_two[:2]
+        + first_three[3:]
+        + next_two[2:]
+        + last_two[2:],
         (jax.ShapeDtypeStruct((2048, 256), BF16), jax.ShapeDtypeStruct((256, 1024), BF16)),
         1,
     )

time: 97.5 us -> 106 us (1.087)
  the two profiles are of different devices: /device:TPU:8 before, /device:TPU:1 now
where the time goes in v4:
time: 106 us
  starting transfers between devices  64.6 us (61%)
  waiting for transfers between devices  28.2 us (27%)
  Pallas kernels  10.3 us (10%)
  other arithmetic  1.56 us (1%)
    ppermute x30, starting transfers between devices, moved(): lax.ppermute(block, BOTH, [(index_of(*at), index_of(*route(*at))) for at...  64.6 us
    ppermute x30, waiting for transfers between devices, moved(): lax.ppermute(block, BOTH, [(index_of(*at), index_of(*route(*at))) for at...  28.2 us
    pallas_call x7, Pallas kernels, call(): pl.pallas_call(kernel, out_shape=out_shape, in_specs=[SMEM] + [VMEM] * le...  10.3 us
  transfers between devices with their start and end apart: 30, of which 10 were waited for; matrix products, arithmetic and copies ran while one was open for 1% of the time, Pallas kernels for 8%

profile of v4, /device:TPU:1, one launch (start us, length us, event | category | flops | bytes accessed | tf_op | source)
XLA Modules:
  0.0 105.7 jit_solution(16440553103455253599)
XLA Ops:
  0.6 0.0 copy-start
  0.6 5.6 %collective-permute-start.3 = (bf16[2,2,64,1024]{3,2,1,0:T(8,128)(2,1)}, bf16[2,2,64,1024]{3,2,1,0:T(8,128)(2,1)S(1)}, u32[]{:S(2)}, u32[]{:S(2)}) collective-permute-start(bf16[2,2,64,1024]{3,2,1,0:T(8,128)(2,1)} %bitcast.15), channel_id=1, source_target_pairs={{0,130},{1,158},{2,132},{3,144},{4,134},{5,146},{6,136},{7,148},{8... | collective-permute-start | bytes 1572872 | tf_op jit(solution)/shard_map/ppermute | solution.py:27
  6.2 4.1 %collective-permute-start.2 = (bf16[2,2,64,1024]{3,2,1,0:T(8,128)(2,1)}, bf16[2,2,64,1024]{3,2,1,0:T(8,128)(2,1)S(1)}, u32[]{:S(2)}, u32[]{:S(2)}) collective-permute-start(bf16[2,2,64,1024]{3,2,1,0:T(8,128)(2,1)} %bitcast.16), channel_id=1, source_target_pairs={{0,128},{1,144},{2,130},{3,146},{4,132},{5,148},{6,134},{7,150},{8... | collective-permute-start | bytes 1572872 | tf_op jit(solution)/shard_map/ppermute | solution.py:27
  10.3 0.0 collective-permute-start
  10.3 7.9 %collective-permute-done.3.refs_1_.refs_3_ = bf16[2,2,64,1024]{3,2,1,0:T(8,128)(2,1)S(1)} collective-permute-done((bf16[2,2,64,1024]{3,2,1,0:T(8,128)(2,1)}, bf16[2,2,64,1024]{3,2,1,0:T(8,128)(2,1)S(1)}, u32[]{:S(2)}, u32[]{:S(2)}) %collective-permute-start.3) | collective-permute-done | bytes 524320 | tf_op jit(solution)/shard_map/ppermute | solution.py:27
  18.2 5.0 %collective-permute-start.10 = (bf16[2,2,64,1024]{3,2,1,0:T(8,128)(2,1)S(1)}, bf16[2,2,64,1024]{3,2,1,0:T(8,128)(2,1)S(1)}, u32[]{:S(2)}, u32[]{:S(2)}) collective-permute-start(bf16[2,2,64,1024]{3,2,1,0:T(8,128)(2,1)S(1)} %collective-permute-done.3.refs_1_.refs_3_), channel_id=1, source_target_pairs={{0,2},{1,3},{2,4},{3,5},{4,6},{5,7},{6,8},{7,9},{8,10},{9,11},{10,... | collective-permute-start | bytes 1572872 | tf_op jit(solution)/shard_map/ppermute | solution.py:27
  23.3 2.7 %collective-permute-done.2.refs_0_.own.refs_2_ = bf16[2,2,64,1024]{3,2,1,0:T(8,128)(2,1)S(1)} collective-permute-done((bf16[2,2,64,1024]{3,2,1,0:T(8,128)(2,1)}, bf16[2,2,64,1024]{3,2,1,0:T(8,128)(2,1)S(1)}, u32[]{:S(2)}, u32[]{:S(2)}) %collective-permute-start.2) | collective-permute-done | bytes 524320 | tf_op jit(solution)/shard_map/ppermute | solution.py:27
  26.0 0.0 collective-permute-start.5
  26.0 0.5 collective-permute-start.6
  26.5 0.0 collective-permute-done.refs_4_.refs_8_
  26.5 0.0 collective-permute-start.4
  26.5 2.8 %collective-permute-start.1 = (bf16[2,2,64,1024]{3,2,1,0:T(8,128)(2,1)S(1)}, bf16[2,2,64,1024]{3,2,1,0:T(8,128)(2,1)S(1)}, u32[]{:S(2)}, u32[]{:S(2)}) collective-permute-start(bf16[2,2,64,1024]{3,2,1,0:T(8,128)(2,1)S(1)} %collective-permute-done.refs_4_.refs_8_), channel_id=1, source_target_pairs={{0,2},{1,3},{2,4},{3,5},{4,6},{5,7},{6,8},{7,9},{8,10},{9,11},{10,... | collective-permute-start | bytes 1572872 | tf_op jit(solution)/shard_map/ppermute | solution.py:27
  29.3 0.1 collective-permute-done.10.own.refs_5_.refs_3_
  29.4 3.1 %collective-permute-start.13 = (bf16[2,2,64,1024]{3,2,1,0:T(8,128)(2,1)S(1)}, bf16[2,2,64,1024]{3,2,1,0:T(8,128)(2,1)}, u32[]{:S(2)}, u32[]{:S(2)}) collective-permute-start(bf16[2,2,64,1024]{3,2,1,0:T(8,128)(2,1)S(1)} %collective-permute-done.10.own.refs_5_.refs_3_), channel_id=1, source_target_pairs={{0,2},{1,3},{2,4},{3,5},{4,6},{5,7},{6,8},{7,9},{8,10},{9,11},{10,... | collective-permute-start | bytes 1572872 | tf_op jit(solution)/shard_map/ppermute | solution.py:27
  32.5 0.0 collective-permute-done.5.refs_3_.other.refs_7_
  32.5 0.0 collective-permute-start.12
  32.5 0.1 pad_add_fusion.info.refs_0_
  32.6 0.6 shard_map.42
  33.2 0.0 collective-permute-done.6.refs_5_.refs_9_
  33.2 1.3 %shard_map.41 = bf16[3,2,128,128]{3,2,1,0:T(8,128)(2,1)S(1)} custom-call(s32[6]{0:T(128)S(1)} %pad_add_fusion.info.refs_0_, bf16[2,2,64,1024]{3,2,1,0:T(8,128)(2,1)S(1)} %collective-permute-done.2.refs_0_.own.refs_2_, bf16[2,2,64,1024]{3,2,1,0:T(8,128)(2,1)S(1)} %collective-permute-done.3.refs_1_.refs_3_, ...), custom_call_target="tpu_custom_call" | custom-call | flops 1 | bytes 1048576 | tf_op jit(solution)/shard_map/pallas_call | solution.py:74
  34.5 0.9 collective-permute-done.1.other.refs_10_
  35.4 2.0 %collective-permute-start.11 = (bf16[2,2,64,1024]{3,2,1,0:T(8,128)(2,1)S(1)}, bf16[2,2,64,1024]{3,2,1,0:T(8,128)(2,1)S(1)}, u32[]{:S(2)}, u32[]{:S(2)}) collective-permute-start(bf16[2,2,64,1024]{3,2,1,0:T(8,128)(2,1)S(1)} %collective-permute-done.1.other.refs_10_), channel_id=1, source_target_pairs={{0,16},{1,17},{2,18},{3,19},{4,20},{5,21},{6,22},{7,23},{8,24},{9,... | collective-permute-start | bytes 1572872 | tf_op jit(solution)/shard_map/ppermute | solution.py:27
  37.4 1.2 %collective-permute-start.9 = (bf16[2,128,1024]{2,1,0:T(8,128)(2,1)S(1)}, bf16[2,128,1024]{2,1,0:T(8,128)(2,1)S(1)}, u32[]{:S(2)}, u32[]{:S(2)}) collective-permute-start(bf16[2,128,1024]{2,1,0:T(8,128)(2,1)S(1)} %shard_map.42), channel_id=1, source_target_pairs={{0,33},{1,0},{2,35},{3,2},{4,37},{5,4},{6,39},{7,6},{8,41},{9,8},{... | collective-permute-start | bytes 1572872 | tf_op jit(solution)/shard_map/ppermute | solution.py:27
  38.6 1.6 %collective-permute-start.7 = (bf16[2,2,64,1024]{3,2,1,0:T(8,128)(2,1)S(1)}, bf16[2,2,64,1024]{3,2,1,0:T(8,128)(2,1)S(1)}, u32[]{:S(2)}, u32[]{:S(2)}) collective-permute-start(bf16[2,2,64,1024]{3,2,1,0:T(8,128)(2,1)S(1)} %collective-permute-done.1.other.refs_10_), channel_id=1, source_target_pairs={{0,2},{1,3},{2,4},{3,5},{4,6},{5,7},{6,8},{7,9},{8,10},{9,11},{10,... | collective-permute-start | bytes 1572872 | tf_op jit(solution)/shard_map/ppermute | solution.py:27
  40.2 0.8 collective-permute-done.13.refs_2_.refs_5_
  41.0 3.4 %collective-permute-start.14 = (bf16[2,2,64,1024]{3,2,1,0:T(8,128)(2,1)}, bf16[2,2,64,1024]{3,2,1,0:T(8,128)(2,1)S(1)}, u32[]{:S(2)}, u32[]{:S(2)}) collective-permute-start(bf16[2,2,64,1024]{3,2,1,0:T(8,128)(2,1)} %collective-permute-done.13.refs_2_.refs_5_), channel_id=1, source_target_pairs={{0,2},{1,3},{2,4},{3,5},{4,6},{5,7},{6,8},{7,9},{8,10},{9,11},{10,... | collective-permute-start | bytes 1572872 | tf_op jit(solution)/shard_map/ppermute | solution.py:27
  44.4 0.0 collective-permute-done.12.other_x.refs_11_
  44.4 1.2 %collective-permute-start.8 = (bf16[3,2,128,128]{3,2,1,0:T(8,128)(2,1)S(1)}, bf16[3,2,128,128]{3,2,1,0:T(8,128)(2,1)S(1)}, u32[]{:S(2)}, u32[]{:S(2)}) collective-permute-start(bf16[3,2,128,128]{3,2,1,0:T(8,128)(2,1)S(1)} %shard_map.41), channel_id=1, source_target_pairs={{0,33},{1,0},{2,35},{3,2},{4,37},{5,4},{6,39},{7,6},{8,41},{9,8},{... | collective-permute-start | bytes 589832 | tf_op jit(solution)/shard_map/ppermute | solution.py:27
  45.6 0.0 collective-permute-done.11.own_x.refs_6_.refs_4_
  45.6 0.6 shard_map.43
  46.3 11.7 %collective-permute-done.8.near = bf16[3,2,128,128]{3,2,1,0:T(8,128)(2,1)S(1)} collective-permute-done((bf16[3,2,128,128]{3,2,1,0:T(8,128)(2,1)S(1)}, bf16[3,2,128,128]{3,2,1,0:T(8,128)(2,1)S(1)}, u32[]{:S(2)}, u32[]{:S(2)}) %collective-permute-start.8) | collective-permute-done | bytes 196640 | tf_op jit(solution)/shard_map/ppermute | solution.py:27
  57.9 0.0 collective-permute-done.9.refs_1_.a_ref
  57.9 0.0 collective-permute-done.7.refs_4_.refs_12_
  57.9 0.0 collective-permute-start.15
  57.9 0.3 collective-permute-start.16
  58.2 1.1 %collective-permute-start.17 = (bf16[2,128,128]{2,1,0:T(8,128)(2,1)S(1)}, bf16[2,128,128]{2,1,0:T(8,128)(2,1)S(1)}, u32[]{:S(2)}, u32[]{:S(2)}) collective-permute-start(bf16[2,128,128]{2,1,0:T(8,128)(2,1)S(1)} %get-tuple-element.42), channel_id=1, source_target_pairs={{0,47},{1,14},{2,33},{3,0},{4,35},{5,2},{6,37},{7,4},{8,39},{9,6},... | collective-permute-start | bytes 196616 | tf_op jit(solution)/shard_map/ppermute | solution.py:27
  59.3 7.2 %collective-permute-start.18 = (bf16[2,128,128]{2,1,0:T(8,128)(2,1)S(1)}, bf16[2,128,128]{2,1,0:T(8,128)(2,1)S(1)}, u32[]{:S(2)}, u32[]{:S(2)}) collective-permute-start(bf16[2,128,128]{2,1,0:T(8,128)(2,1)S(1)} %get-tuple-element.43), channel_id=1, source_target_pairs={{0,37},{1,4},{2,39},{3,6},{4,41},{5,8},{6,43},{7,10},{8,45},{9,12}... | collective-permute-start | bytes 196616 | tf_op jit(solution)/shard_map/ppermute | solution.py:27
  66.4 0.0 collective-permute-done.16.down
  66.4 1.5 %collective-permute-start.21 = (bf16[2,2,64,1024]{3,2,1,0:T(8,128)(2,1)}, bf16[2,2,64,1024]{3,2,1,0:T(8,128)(2,1)S(1)}, u32[]{:S(2)}, u32[]{:S(2)}) collective-permute-start(bf16[2,2,64,1024]{3,2,1,0:T(8,128)(2,1)} %collective-permute-done.13.refs_2_.refs_5_), channel_id=1, source_target_pairs={{0,16},{1,17},{2,18},{3,19},{4,20},{5,21},{6,22},{7,23},{8,24},{9,... | collective-permute-start | bytes 1572872 | tf_op jit(solution)/shard_map/ppermute | solution.py:27
  67.9 1.7 %collective-permute-done.17.up = bf16[2,128,128]{2,1,0:T(8,128)(2,1)S(1)} collective-permute-done((bf16[2,128,128]{2,1,0:T(8,128)(2,1)S(1)}, bf16[2,128,128]{2,1,0:T(8,128)(2,1)S(1)}, u32[]{:S(2)}, u32[]{:S(2)}) %collective-permute-start.17) | collective-permute-done | bytes 65568 | tf_op jit(solution)/shard_map/ppermute | solution.py:27
  69.6 0.0 collective-permute-start.20
  69.6 2.1 %shard_map.44.refs_6_ = f32[256,1024]{1,0:T(8,128)S(1)} custom-call(s32[6]{0:T(128)S(1)} %pad_add_fusion.info.refs_0_, bf16[2,128,1024]{2,1,0:T(8,128)(2,1)S(1)} %collective-permute-done.9.refs_1_.a_ref, bf16[2,2,64,1024]{3,2,1,0:T(8,128)(2,1)S(1)} %collective-permute-done.2.refs_0_.own.refs_2_, ...), custom_call_target="tpu_custom_call" | custom-call | flops 1 | bytes 1048576 | tf_op jit(solution)/shard_map/pallas_call | solution.py:74
  71.7 0.0 collective-permute-done.15.middle
  71.7 0.0 collective-permute-done.14.own
  71.7 4.7 %collective-permute-start.19 = (bf16[2,2,64,1024]{3,2,1,0:T(8,128)(2,1)S(1)}, bf16[2,2,64,1024]{3,2,1,0:T(8,128)(2,1)S(1)}, u32[]{:S(2)}, u32[]{:S(2)}) collective-permute-start(bf16[2,2,64,1024]{3,2,1,0:T(8,128)(2,1)S(1)} %collective-permute-done.14.own), channel_id=1, source_target_pairs={{0,16},{1,17},{2,18},{3,19},{4,20},{5,21},{6,22},{7,23},{8,24},{9,... | collective-permute-start | bytes 1572872 | tf_op jit(solution)/shard_map/ppermute | solution.py:27
  76.4 1.5 %shard_map.45.acc = f32[256,1024]{1,0:T(8,128)S(1)} custom-call(s32[6]{0:T(128)S(1)} %pad_add_fusion.info.refs_0_, bf16[2,128,1024]{2,1,0:T(8,128)(2,1)S(1)} %collective-permute-done.9.refs_1_.a_ref, bf16[2,2,64,1024]{3,2,1,0:T(8,128)(2,1)} %collective-permute-done.13.refs_2_.refs_5_, bf16[2,2,64,1024]{3,2,1,0:T(8,128)(2,1)S(1)} %collective-permute-done.20.refs_3_.refs_6_, ...), custom_call_target="tpu_custom_call" | custom-call | flops 1 | bytes 1048576 | tf_op jit(solution)/shard_map/pallas_call | solution.py:74
  77.9 2.7 %shard_map.46 = (bf16[2048,256]{1,0:T(8,128)(2,1)S(1)}, bf16[256,1024]{1,0:T(8,128)(2,1)S(1)}) custom-call(s32[6]{0:T(128)S(1)} %pad_add_fusion.info.refs_0_, bf16[3,2,128,128]{3,2,1,0:T(8,128)(2,1)S(1)} %collective-permute-done.8.near, bf16[2,2,128,128]{3,2,1,0:T(8,128)(2,1)S(1)} %collective-permute-done.15.middle, ...), custom_call_target="tpu_custom_call" | custom-call | flops 1 | bytes 1048576 | tf_op jit(solution)/shard_map/pallas_call | solution.py:74
  80.7 0.0 collective-permute-done.19.other
  80.7 1.5 %shard_map.47 = (bf16[2,64,1024]{2,1,0:T(8,128)(2,1)S(1)}, bf16[2,64,1024]{2,1,0:T(8,128)(2,1)S(1)}, f32[1,128]{1,0:T(1,128)S(1)}) custom-call(s32[6]{0:T(128)S(1)} %pad_add_fusion.info.refs_0_, bf16[2,128,1024]{2,1,0:T(8,128)(2,1)S(1)} %collective-permute-done.9.refs_1_.a_ref, bf16[2,2,64,1024]{3,2,1,0:T(8,128)(2,1)S(1)} %collective-permute-done.14.own, ...), custom_call_target="tpu_custom_call" | custom-call | flops 1 | bytes 1048576 | tf_op jit(solution)/shard_map/pallas_call | solution.py:74
  82.2 0.0 collective-permute-start.23
  82.2 2.7 %collective-permute-start.22 = (f32[1,128]{1,0:T(1,128)S(1)}, f32[1,128]{1,0:T(1,128)S(1)}, u32[]{:S(2)}, u32[]{:S(2)}) collective-permute-start(f32[1,128]{1,0:T(1,128)S(1)} %get-tuple-element.54), channel_id=1, source_target_pairs={{0,14},{1,15},{2,0},{3,1},{4,2},{5,3},{6,4},{7,5},{8,6},{9,7},{10,... | collective-permute-start | bytes 1544 | tf_op jit(solution)/shard_map/ppermute | solution.py:27
  84.9 1.2 %collective-permute-start.26 = (bf16[2,64,1024]{2,1,0:T(8,128)(2,1)S(1)}, bf16[2,64,1024]{2,1,0:T(8,128)(2,1)S(1)}, u32[]{:S(2)}, u32[]{:S(2)}) collective-permute-start(bf16[2,64,1024]{2,1,0:T(8,128)(2,1)S(1)} %get-tuple-element.57), channel_id=1, source_target_pairs={{0,128},{1,112},{2,130},{3,114},{4,132},{5,116},{6,134},{7,118},{8... | collective-permute-start | bytes 786440 | tf_op jit(solution)/shard_map/ppermute | solution.py:27
  86.1 1.7 %collective-permute-start.27 = (bf16[2,64,1024]{2,1,0:T(8,128)(2,1)S(1)}, bf16[2,64,1024]{2,1,0:T(8,128)(2,1)S(1)}, u32[]{:S(2)}, u32[]{:S(2)}) collective-permute-start(bf16[2,64,1024]{2,1,0:T(8,128)(2,1)S(1)} %get-tuple-element.58), channel_id=1, source_target_pairs={{0,129},{1,113},{2,131},{3,115},{4,133},{5,117},{6,135},{7,119},{8... | collective-permute-start | bytes 786440 | tf_op jit(solution)/shard_map/ppermute | solution.py:27
  87.9 2.5 %collective-permute-start.24 = (f32[1,128]{1,0:T(1,128)S(1)}, f32[1,128]{1,0:T(1,128)S(1)}, u32[]{:S(2)}, u32[]{:S(2)}) collective-permute-start(f32[1,128]{1,0:T(1,128)S(1)} %get-tuple-element.55), channel_id=1, source_target_pairs={{0,6},{1,7},{2,8},{3,9},{4,10},{5,11},{6,12},{7,13},{8,14},{9,15},... | collective-permute-start | bytes 1544 | tf_op jit(solution)/shard_map/ppermute | solution.py:27
  90.4 2.0 %collective-permute-start.25 = (f32[1,128]{1,0:T(1,128)S(1)}, f32[1,128]{1,0:T(1,128)S(1)}, u32[]{:S(2)}, u32[]{:S(2)}) collective-permute-start(f32[1,128]{1,0:T(1,128)S(1)} %get-tuple-element.56), channel_id=1, source_target_pairs={{0,10},{1,11},{2,12},{3,13},{4,14},{5,15},{6,0},{7,1},{8,2},{9,3},... | collective-permute-start | bytes 1544 | tf_op jit(solution)/shard_map/ppermute | solution.py:27
  92.4 0.9 collective-permute-done.24
  93.3 1.3 %collective-permute-done.25 = f32[1,128]{1,0:T(1,128)S(1)} collective-permute-done((f32[1,128]{1,0:T(1,128)S(1)}, f32[1,128]{1,0:T(1,128)S(1)}, u32[]{:S(2)}, u32[]{:S(2)}) %collective-permute-start.25) | collective-permute-done | bytes 544 | tf_op jit(solution)/shard_map/ppermute | solution.py:27
  94.6 0.2 collective-permute-done.26
  94.8 4.0 %collective-permute-start.29 = (f32[1,128]{1,0:T(1,128)S(1)}, f32[1,128]{1,0:T(1,128)S(1)}, u32[]{:S(2)}, u32[]{:S(2)}) collective-permute-start(f32[1,128]{1,0:T(1,128)S(1)} %add_add_fusion), channel_id=1, source_target_pairs={{0,129},{1,113},{2,131},{3,115},{4,133},{5,117},{6,135},{7,119},{8... | collective-permute-start | bytes 1544 | tf_op jit(solution)/shard_map/ppermute | solution.py:27
  98.8 5.3 %collective-permute-start.28 = (f32[1,128]{1,0:T(1,128)S(1)}, f32[1,128]{1,0:T(1,128)S(1)}, u32[]{:S(2)}, u32[]{:S(2)}) collective-permute-start(f32[1,128]{1,0:T(1,128)S(1)} %add_add_fusion), channel_id=1, source_target_pairs={{0,128},{1,112},{2,130},{3,114},{4,132},{5,116},{6,134},{7,118},{8... | collective-permute-start | bytes 1544 | tf_op jit(solution)/shard_map/ppermute | solution.py:27
  104.1 0.9 maximum_select_fusion
  105.0 0.0 collective-permute-done.29
  105.0 0.1 reshape.77
  105.1 0.6 broadcast_multiply_fusion
  (14 shorter events, 0.1 us)
Async XLA Ops:
  0.6 31.9 %copy-start = (s32[2,1,4]{2,1,0:T(1,128)S(1)}, s32[2,1,4]{2,1,0:T(1,128)}, u32[]{:S(2)}) copy-start(s32[2,1,4]{2,1,0:T(1,128)} %param.3) | copy-start | bytes 100
  0.6 17.6 %collective-permute-start.3 = (bf16[2,2,64,1024]{3,2,1,0:T(8,128)(2,1)}, bf16[2,2,64,1024]{3,2,1,0:T(8,128)(2,1)S(1)}, u32[]{:S(2)}, u32[]{:S(2)}) collective-permute-start(bf16[2,2,64,1024]{3,2,1,0:T(8,128)(2,1)} %bitcast.15), channel_id=1, source_target_pairs={{0,130},{1,158},{2,132},{3,144},{4,134},{5,146},{6,136},{7,148},{8... | collective-permute-start | bytes 1572872 | tf_op jit(solution)/shard_map/ppermute | solution.py:27
  6.2 19.8 %collective-permute-start.2 = (bf16[2,2,64,1024]{3,2,1,0:T(8,128)(2,1)}, bf16[2,2,64,1024]{3,2,1,0:T(8,128)(2,1)S(1)}, u32[]{:S(2)}, u32[]{:S(2)}) collective-permute-start(bf16[2,2,64,1024]{3,2,1,0:T(8,128)(2,1)} %bitcast.16), channel_id=1, source_target_pairs={{0,128},{1,144},{2,130},{3,146},{4,132},{5,148},{6,134},{7,150},{8... | collective-permute-start | bytes 1572872 | tf_op jit(solution)/shard_map/ppermute | solution.py:27
  10.3 16.2 %collective-permute-start = (bf16[2,2,64,1024]{3,2,1,0:T(8,128)(2,1)}, bf16[2,2,64,1024]{3,2,1,0:T(8,128)(2,1)S(1)}, u32[]{:S(2)}, u32[]{:S(2)}) collective-permute-start(bf16[2,2,64,1024]{3,2,1,0:T(8,128)(2,1)} %bitcast.17), channel_id=1, source_target_pairs={{0,158},{1,130},{2,144},{3,132},{4,146},{5,134},{6,148},{7,136},{8... | collective-permute-start | bytes 1572872 | tf_op jit(solution)/shard_map/ppermute | solution.py:27
  18.2 11.1 %collective-permute-start.10 = (bf16[2,2,64,1024]{3,2,1,0:T(8,128)(2,1)S(1)}, bf16[2,2,64,1024]{3,2,1,0:T(8,128)(2,1)S(1)}, u32[]{:S(2)}, u32[]{:S(2)}) collective-permute-start(bf16[2,2,64,1024]{3,2,1,0:T(8,128)(2,1)S(1)} %collective-permute-done.3.refs_1_.refs_3_), channel_id=1, source_target_pairs={{0,2},{1,3},{2,4},{3,5},{4,6},{5,7},{6,8},{7,9},{8,10},{9,11},{10,... | collective-permute-start | bytes 1572872 | tf_op jit(solution)/shard_map/ppermute | solution.py:27
  26.0 6.5 %collective-permute-start.5 = (bf16[2,2,64,1024]{3,2,1,0:T(8,128)(2,1)S(1)}, bf16[2,2,64,1024]{3,2,1,0:T(8,128)(2,1)S(1)}, u32[]{:S(2)}, u32[]{:S(2)}) collective-permute-start(bf16[2,2,64,1024]{3,2,1,0:T(8,128)(2,1)S(1)} %collective-permute-done.2.refs_0_.own.refs_2_), channel_id=1, source_target_pairs={{0,16},{1,17},{2,18},{3,19},{4,20},{5,21},{6,22},{7,23},{8,24},{9,... | collective-permute-start | bytes 1572872 | tf_op jit(solution)/shard_map/ppermute | solution.py:27
  26.0 7.2 %collective-permute-start.6 = (bf16[2,2,64,1024]{3,2,1,0:T(8,128)(2,1)S(1)}, bf16[2,2,64,1024]{3,2,1,0:T(8,128)(2,1)}, u32[]{:S(2)}, u32[]{:S(2)}) collective-permute-start(bf16[2,2,64,1024]{3,2,1,0:T(8,128)(2,1)S(1)} %collective-permute-done.3.refs_1_.refs_3_), channel_id=1, source_target_pairs={{0,16},{1,17},{2,18},{3,19},{4,20},{5,21},{6,22},{7,23},{8,24},{9,... | collective-permute-start | bytes 1572872 | tf_op jit(solution)/shard_map/ppermute | solution.py:27
  26.5 6.7 %collective-permute-start.4 = (bf16[2,2,64,1024]{3,2,1,0:T(8,128)(2,1)S(1)}, bf16[2,2,64,1024]{3,2,1,0:T(8,128)(2,1)}, u32[]{:S(2)}, u32[]{:S(2)}) collective-permute-start(bf16[2,2,64,1024]{3,2,1,0:T(8,128)(2,1)S(1)} %collective-permute-done.refs_4_.refs_8_), channel_id=1, source_target_pairs={{0,16},{1,17},{2,18},{3,19},{4,20},{5,21},{6,22},{7,23},{8,24},{9,... | collective-permute-start | bytes 1572872 | tf_op jit(solution)/shard_map/ppermute | solution.py:27
  26.5 8.9 %collective-permute-start.1 = (bf16[2,2,64,1024]{3,2,1,0:T(8,128)(2,1)S(1)}, bf16[2,2,64,1024]{3,2,1,0:T(8,128)(2,1)S(1)}, u32[]{:S(2)}, u32[]{:S(2)}) collective-permute-start(bf16[2,2,64,1024]{3,2,1,0:T(8,128)(2,1)S(1)} %collective-permute-done.refs_4_.refs_8_), channel_id=1, source_target_pairs={{0,2},{1,3},{2,4},{3,5},{4,6},{5,7},{6,8},{7,9},{8,10},{9,11},{10,... | collective-permute-start | bytes 1572872 | tf_op jit(solution)/shard_map/ppermute | solution.py:27
  29.4 11.6 %collective-permute-start.13 = (bf16[2,2,64,1024]{3,2,1,0:T(8,128)(2,1)S(1)}, bf16[2,2,64,1024]{3,2,1,0:T(8,128)(2,1)}, u32[]{:S(2)}, u32[]{:S(2)}) collective-permute-start(bf16[2,2,64,1024]{3,2,1,0:T(8,128)(2,1)S(1)} %collective-permute-done.10.own.refs_5_.refs_3_), channel_id=1, source_target_pairs={{0,2},{1,3},{2,4},{3,5},{4,6},{5,7},{6,8},{7,9},{8,10},{9,11},{10,... | collective-permute-start | bytes 1572872 | tf_op jit(solution)/shard_map/ppermute | solution.py:27
  32.5 11.9 %collective-permute-start.12 = (bf16[2,2,64,1024]{3,2,1,0:T(8,128)(2,1)S(1)}, bf16[2,2,64,1024]{3,2,1,0:T(8,128)(2,1)S(1)}, u32[]{:S(2)}, u32[]{:S(2)}) collective-permute-start(bf16[2,2,64,1024]{3,2,1,0:T(8,128)(2,1)S(1)} %collective-permute-done.10.own.refs_5_.refs_3_), channel_id=1, source_target_pairs={{0,16},{1,17},{2,18},{3,19},{4,20},{5,21},{6,22},{7,23},{8,24},{9,... | collective-permute-start | bytes 1572872 | tf_op jit(solution)/shard_map/ppermute | solution.py:27
  35.4 10.2 %collective-permute-start.11 = (bf16[2,2,64,1024]{3,2,1,0:T(8,128)(2,1)S(1)}, bf16[2,2,64,1024]{3,2,1,0:T(8,128)(2,1)S(1)}, u32[]{:S(2)}, u32[]{:S(2)}) collective-permute-start(bf16[2,2,64,1024]{3,2,1,0:T(8,128)(2,1)S(1)} %collective-permute-done.1.other.refs_10_), channel_id=1, source_target_pairs={{0,16},{1,17},{2,18},{3,19},{4,20},{5,21},{6,22},{7,23},{8,24},{9,... | collective-permute-start | bytes 1572872 | tf_op jit(solution)/shard_map/ppermute | solution.py:27
  37.4 20.6 %collective-permute-start.9 = (bf16[2,128,1024]{2,1,0:T(8,128)(2,1)S(1)}, bf16[2,128,1024]{2,1,0:T(8,128)(2,1)S(1)}, u32[]{:S(2)}, u32[]{:S(2)}) collective-permute-start(bf16[2,128,1024]{2,1,0:T(8,128)(2,1)S(1)} %shard_map.42), channel_id=1, source_target_pairs={{0,33},{1,0},{2,35},{3,2},{4,37},{5,4},{6,39},{7,6},{8,41},{9,8},{... | collective-permute-start | bytes 1572872 | tf_op jit(solution)/shard_map/ppermute | solution.py:27
  38.6 19.3 %collective-permute-start.7 = (bf16[2,2,64,1024]{3,2,1,0:T(8,128)(2,1)S(1)}, bf16[2,2,64,1024]{3,2,1,0:T(8,128)(2,1)S(1)}, u32[]{:S(2)}, u32[]{:S(2)}) collective-permute-start(bf16[2,2,64,1024]{3,2,1,0:T(8,128)(2,1)S(1)} %collective-permute-done.1.other.refs_10_), channel_id=1, source_target_pairs={{0,2},{1,3},{2,4},{3,5},{4,6},{5,7},{6,8},{7,9},{8,10},{9,11},{10,... | collective-permute-start | bytes 1572872 | tf_op jit(solution)/shard_map/ppermute | solution.py:27
  41.0 30.7 %collective-permute-start.14 = (bf16[2,2,64,1024]{3,2,1,0:T(8,128)(2,1)}, bf16[2,2,64,1024]{3,2,1,0:T(8,128)(2,1)S(1)}, u32[]{:S(2)}, u32[]{:S(2)}) collective-permute-start(bf16[2,2,64,1024]{3,2,1,0:T(8,128)(2,1)} %collective-permute-done.13.refs_2_.refs_5_), channel_id=1, source_target_pairs={{0,2},{1,3},{2,4},{3,5},{4,6},{5,7},{6,8},{7,9},{8,10},{9,11},{10,... | collective-permute-start | bytes 1572872 | tf_op jit(solution)/shard_map/ppermute | solution.py:27
  44.4 13.5 %collective-permute-start.8 = (bf16[3,2,128,128]{3,2,1,0:T(8,128)(2,1)S(1)}, bf16[3,2,128,128]{3,2,1,0:T(8,128)(2,1)S(1)}, u32[]{:S(2)}, u32[]{:S(2)}) collective-permute-start(bf16[3,2,128,128]{3,2,1,0:T(8,128)(2,1)S(1)} %shard_map.41), channel_id=1, source_target_pairs={{0,33},{1,0},{2,35},{3,2},{4,37},{5,4},{6,39},{7,6},{8,41},{9,8},{... | collective-permute-start | bytes 589832 | tf_op jit(solution)/shard_map/ppermute | solution.py:27
  57.9 13.8 %collective-permute-start.15 = (bf16[2,2,128,128]{3,2,1,0:T(8,128)(2,1)S(1)}, bf16[2,2,128,128]{3,2,1,0:T(8,128)(2,1)S(1)}, u32[]{:S(2)}, u32[]{:S(2)}) collective-permute-start(bf16[2,2,128,128]{3,2,1,0:T(8,128)(2,1)S(1)} %get-tuple-element.40), channel_id=1, source_target_pairs={{0,33},{1,0},{2,35},{3,2},{4,37},{5,4},{6,39},{7,6},{8,41},{9,8},{... | collective-permute-start | bytes 393224 | tf_op jit(solution)/shard_map/ppermute | solution.py:27
  57.9 8.5 %collective-permute-start.16 = (bf16[2,128,128]{2,1,0:T(8,128)(2,1)S(1)}, bf16[2,128,128]{2,1,0:T(8,128)(2,1)S(1)}, u32[]{:S(2)}, u32[]{:S(2)}) collective-permute-start(bf16[2,128,128]{2,1,0:T(8,128)(2,1)S(1)} %get-tuple-element.41), channel_id=1, source_target_pairs={{0,35},{1,2},{2,37},{3,4},{4,39},{5,6},{6,41},{7,8},{8,43},{9,10},... | collective-permute-start | bytes 196616 | tf_op jit(solution)/shard_map/ppermute | solution.py:27
  58.2 11.4 %collective-permute-start.17 = (bf16[2,128,128]{2,1,0:T(8,128)(2,1)S(1)}, bf16[2,128,128]{2,1,0:T(8,128)(2,1)S(1)}, u32[]{:S(2)}, u32[]{:S(2)}) collective-permute-start(bf16[2,128,128]{2,1,0:T(8,128)(2,1)S(1)} %get-tuple-element.42), channel_id=1, source_target_pairs={{0,47},{1,14},{2,33},{3,0},{4,35},{5,2},{6,37},{7,4},{8,39},{9,6},... | collective-permute-start | bytes 196616 | tf_op jit(solution)/shard_map/ppermute | solution.py:27
  59.3 12.4 %collective-permute-start.18 = (bf16[2,128,128]{2,1,0:T(8,128)(2,1)S(1)}, bf16[2,128,128]{2,1,0:T(8,128)(2,1)S(1)}, u32[]{:S(2)}, u32[]{:S(2)}) collective-permute-start(bf16[2,128,128]{2,1,0:T(8,128)(2,1)S(1)} %get-tuple-element.43), channel_id=1, source_target_pairs={{0,37},{1,4},{2,39},{3,6},{4,41},{5,8},{6,43},{7,10},{8,45},{9,12}... | collective-permute-start | bytes 196616 | tf_op jit(solution)/shard_map/ppermute | solution.py:27
  66.4 10.0 %collective-permute-start.21 = (bf16[2,2,64,1024]{3,2,1,0:T(8,128)(2,1)}, bf16[2,2,64,1024]{3,2,1,0:T(8,128)(2,1)S(1)}, u32[]{:S(2)}, u32[]{:S(2)}) collective-permute-start(bf16[2,2,64,1024]{3,2,1,0:T(8,128)(2,1)} %collective-permute-done.13.refs_2_.refs_5_), channel_id=1, source_target_pairs={{0,16},{1,17},{2,18},{3,19},{4,20},{5,21},{6,22},{7,23},{8,24},{9,... | collective-permute-start | bytes 1572872 | tf_op jit(solution)/shard_map/ppermute | solution.py:27
  69.6 6.8 %collective-permute-start.20 = (bf16[2,2,64,1024]{3,2,1,0:T(8,128)(2,1)S(1)}, bf16[2,2,64,1024]{3,2,1,0:T(8,128)(2,1)S(1)}, u32[]{:S(2)}, u32[]{:S(2)}) collective-permute-start(bf16[2,2,64,1024]{3,2,1,0:T(8,128)(2,1)S(1)} %collective-permute-done.7.refs_4_.refs_12_), channel_id=1, source_target_pairs={{0,16},{1,17},{2,18},{3,19},{4,20},{5,21},{6,22},{7,23},{8,24},{9,... | collective-permute-start | bytes 1572872 | tf_op jit(solution)/shard_map/ppermute | solution.py:27
  71.7 9.0 %collective-permute-start.19 = (bf16[2,2,64,1024]{3,2,1,0:T(8,128)(2,1)S(1)}, bf16[2,2,64,1024]{3,2,1,0:T(8,128)(2,1)S(1)}, u32[]{:S(2)}, u32[]{:S(2)}) collective-permute-start(bf16[2,2,64,1024]{3,2,1,0:T(8,128)(2,1)S(1)} %collective-permute-done.14.own), channel_id=1, source_target_pairs={{0,16},{1,17},{2,18},{3,19},{4,20},{5,21},{6,22},{7,23},{8,24},{9,... | collective-permute-start | bytes 1572872 | tf_op jit(solution)/shard_map/ppermute | solution.py:27
  82.2 5.6 %collective-permute-start.23 = (f32[1,128]{1,0:T(1,128)S(1)}, f32[1,128]{1,0:T(1,128)S(1)}, u32[]{:S(2)}, u32[]{:S(2)}) collective-permute-start(f32[1,128]{1,0:T(1,128)S(1)} %get-tuple-element.54), channel_id=1, source_target_pairs={{0,2},{1,3},{2,4},{3,5},{4,6},{5,7},{6,8},{7,9},{8,10},{9,11},{10,... | collective-permute-start | bytes 1544 | tf_op jit(solution)/shard_map/ppermute | solution.py:27
  82.2 5.6 %collective-permute-start.22 = (f32[1,128]{1,0:T(1,128)S(1)}, f32[1,128]{1,0:T(1,128)S(1)}, u32[]{:S(2)}, u32[]{:S(2)}) collective-permute-start(f32[1,128]{1,0:T(1,128)S(1)} %get-tuple-element.54), channel_id=1, source_target_pairs={{0,14},{1,15},{2,0},{3,1},{4,2},{5,3},{6,4},{7,5},{8,6},{9,7},{10,... | collective-permute-start | bytes 1544 | tf_op jit(solution)/shard_map/ppermute | solution.py:27
  84.9 9.9 %collective-permute-start.26 = (bf16[2,64,1024]{2,1,0:T(8,128)(2,1)S(1)}, bf16[2,64,1024]{2,1,0:T(8,128)(2,1)S(1)}, u32[]{:S(2)}, u32[]{:S(2)}) collective-permute-start(bf16[2,64,1024]{2,1,0:T(8,128)(2,1)S(1)} %get-tuple-element.57), channel_id=1, source_target_pairs={{0,128},{1,112},{2,130},{3,114},{4,132},{5,116},{6,134},{7,118},{8... | collective-permute-start | bytes 786440 | tf_op jit(solution)/shard_map/ppermute | solution.py:27
  86.1 8.7 %collective-permute-start.27 = (bf16[2,64,1024]{2,1,0:T(8,128)(2,1)S(1)}, bf16[2,64,1024]{2,1,0:T(8,128)(2,1)S(1)}, u32[]{:S(2)}, u32[]{:S(2)}) collective-permute-start(bf16[2,64,1024]{2,1,0:T(8,128)(2,1)S(1)} %get-tuple-element.58), channel_id=1, source_target_pairs={{0,129},{1,113},{2,131},{3,115},{4,133},{5,117},{6,135},{7,119},{8... | collective-permute-start | bytes 786440 | tf_op jit(solution)/shard_map/ppermute | solution.py:27
  87.9 5.5 %collective-permute-start.24 = (f32[1,128]{1,0:T(1,128)S(1)}, f32[1,128]{1,0:T(1,128)S(1)}, u32[]{:S(2)}, u32[]{:S(2)}) collective-permute-start(f32[1,128]{1,0:T(1,128)S(1)} %get-tuple-element.55), channel_id=1, source_target_pairs={{0,6},{1,7},{2,8},{3,9},{4,10},{5,11},{6,12},{7,13},{8,14},{9,15},... | collective-permute-start | bytes 1544 | tf_op jit(solution)/shard_map/ppermute | solution.py:27
  90.4 4.2 %collective-permute-start.25 = (f32[1,128]{1,0:T(1,128)S(1)}, f32[1,128]{1,0:T(1,128)S(1)}, u32[]{:S(2)}, u32[]{:S(2)}) collective-permute-start(f32[1,128]{1,0:T(1,128)S(1)} %get-tuple-element.56), channel_id=1, source_target_pairs={{0,10},{1,11},{2,12},{3,13},{4,14},{5,15},{6,0},{7,1},{8,2},{9,3},... | collective-permute-start | bytes 1544 | tf_op jit(solution)/shard_map/ppermute | solution.py:27
  94.8 10.2 %collective-permute-start.29 = (f32[1,128]{1,0:T(1,128)S(1)}, f32[1,128]{1,0:T(1,128)S(1)}, u32[]{:S(2)}, u32[]{:S(2)}) collective-permute-start(f32[1,128]{1,0:T(1,128)S(1)} %add_add_fusion), channel_id=1, source_target_pairs={{0,129},{1,113},{2,131},{3,115},{4,133},{5,117},{6,135},{7,119},{8... | collective-permute-start | bytes 1544 | tf_op jit(solution)/shard_map/ppermute | solution.py:27
  98.8 6.2 %collective-permute-start.28 = (f32[1,128]{1,0:T(1,128)S(1)}, f32[1,128]{1,0:T(1,128)S(1)}, u32[]{:S(2)}, u32[]{:S(2)}) collective-permute-start(f32[1,128]{1,0:T(1,128)S(1)} %add_add_fusion), channel_id=1, source_target_pairs={{0,128},{1,112},{2,130},{3,114},{4,132},{5,116},{6,134},{7,118},{8... | collective-permute-start | bytes 1544 | tf_op jit(solution)/shard_map/ppermute | solution.py:27

commit v5 on v3

v5 whole, which is shorter than its diff:
```python
import jax
import jax.numpy as jnp
from jax import lax
from jax.experimental import pallas as pl
from jax.experimental.pallas import tpu as pltpu
from jax.sharding import PartitionSpec as P

BOTH = ("tm", "row")
BF16 = jnp.bfloat16
F32 = jnp.float32


def hub_of(s):
    m, odd = divmod(s % 16, 2)
    low, x = divmod(m, 4)
    return (1 - low) * 4 + x, odd ^ low


SERVED = {hub_of(s): s for s in range(16)}


def moved(block, route):
    def index_of(m, c, z, h):
        return ((m % 8) * 2 + c) * 16 + (z % 8) * 2 + h

    places = [(m, c, z, h) for m in range(8) for c in range(2) for z in range(8) for h in range(2)]
    return lax.ppermute(block, BOTH, [(index_of(*at), index_of(*route(*at))) for at in places])


def along(step):
    return lambda m, c, z, h: (m, c, z + step, h)


def onward(m, c, z, h):
    return (m, c, z + (1 if c == 0 else -1), h)


def other_core(m, c, z, h):
    return (m, 1 - c, z, h)


def to_hub(m, c, z, h):
    column, half = hub_of(2 * m + c)
    return (column, h, z, half)


def hub_ahead(turn, step):
    def route(m, c, z, h):
        r = c ^ turn
        column, half = hub_of(SERVED[m, h] + 1 + r)
        return (column, r, z + (step if r == 0 else -step), half)

    return route


def from_hub(turn):
    def route(m, c, z, h):
        t = (SERVED[m, h] - 1 - c) % 16
        return (t // 2, t % 2, z, c ^ turn)

    return route


VMEM = pl.BlockSpec(memory_space=pltpu.VMEM)
SMEM = pl.BlockSpec(memory_space=pltpu.SMEM)
SLICES = jax.ShapeDtypeStruct((2, 128, 128), BF16)


def call(kernel, info, arrays, out_shape, flops, scratch=()):
    outs = jax.tree.map(lambda _: VMEM, out_shape)
    return pl.pallas_call(
        kernel,
        out_shape=out_shape,
        in_specs=[SMEM] + [VMEM] * len(arrays),
        out_specs=outs,
        scratch_shapes=scratch,
        compiler_params=pltpu.CompilerParams(vmem_limit_bytes=24 * 1024 * 1024),
        cost_estimate=pl.CostEstimate(flops=flops, bytes_accessed=1 << 20, transcendentals=0),
    )(info, *arrays)


def place_of(info, offset):
    return lax.rem(info[0] + jnp.where(info[1] == 0, 8 - offset, 8 + offset), 8)


def columns_of(info, offset):
    return pl.ds(pl.multiple_of(place_of(info, offset) * 128, 128), 128)


def halves(info, own, other):
    first = jnp.where(info[1] == 0, own, other)
    second = jnp.where(info[1] == 0, other, own)
    return first, second


def whole(info, own_ref, other_ref, momentum, part):
    return jnp.concatenate(halves(info, own_ref[momentum, part], other_ref[momentum, part]), axis=0)


def cut(info, own_ref, other_ref, offset, out, momentum=5):
    columns = columns_of(info, offset)
    for part in range(2):
        first, second = halves(
            info, own_ref[info[momentum], part, :, columns], other_ref[info[momentum], part, :, columns]
        )
        out[part, 0:64] = first
        out[part, 64:128] = second


def first_cut_kernel(info, own, other, a):
    for part in range(2):
        a[part] = whole(info, own, other, info[2], part)


def near_kernel(info, *refs):
    for k in range(3):
        cut(info, refs[k], refs[3 + k], 0, refs[-1].at[k])


def across_kernel(info, own, other, out):
    cut(info, own, other, -2, out)


def late_kernel(info, own_2, own_3, other_2, other_3, here, there):
    for k, (own, other) in enumerate([(own_2, other_2), (own_3, other_3)]):
        cut(info, own, other, 0, here.at[k])
        cut(info, own, other, 0, there.at[k], momentum=6)


def left_side(info, a_ref, offset):
    columns = columns_of(info, offset)
    real, imag = a_ref[0, :, columns], a_ref[1, :, columns]
    return jnp.concatenate(
        [jnp.concatenate([real, -imag], axis=1), jnp.concatenate([imag, real], axis=1)], axis=0
    )


def products_kernel(offsets, info, a_ref, *refs):
    count = len(offsets)
    own, other, out = refs[:count], refs[count : 2 * count], refs[-1]
    total = refs[2 * count][...] if len(refs) > 2 * count + 1 else None
    for offset, one, two in zip(offsets, own, other):
        block = jnp.concatenate([whole(info, one, two, info[3], part) for part in range(2)], axis=0)
        term = jnp.dot(left_side(info, a_ref, offset), block, preferred_element_type=F32)
        total = term if total is None else total + term
    out[...] = total


OFFSETS = (0, 1, -1, 2, -2, 3, -3, 4)


def crossed_sum(info, own, other, slices):
    total = None
    for offset, piece in slices:
        columns = columns_of(info, offset)
        left = []
        for one, two in zip(own, other):
            parts = [halves(info, one[info[4], part, :, columns], two[info[4], part, :, columns]) for part in range(2)]
            left += [jnp.concatenate([parts[0][k], parts[1][k]], axis=1) for k in range(2)]
        real, imag = piece[0], piece[1]
        right = jnp.concatenate(
            [jnp.concatenate([real, imag], axis=1), jnp.concatenate([-imag, real], axis=1)], axis=0
        )
        term = jnp.dot(jnp.concatenate(left, axis=0), right, preferred_element_type=F32)
        total = term if total is None else total + term
    return total


def crossed_kernel(info, near, across, here, there, *refs):
    slices = [(0, near.at[0]), (1, near.at[1]), (-1, near.at[2]), (4, across)]
    slices += [(2, here.at[0]), (-2, there.at[0]), (3, here.at[1]), (-3, there.at[1])]
    total = crossed_sum(info, refs[0:7], refs[7:14], slices)
    for k, offset in enumerate(OFFSETS[:7]):
        refs[14][columns_of(info, offset), :] = total[128 * k : 128 * k + 128].astype(BF16)
    refs[14][columns_of(info, 4), :] = jnp.zeros((128, 256), BF16)


def last_kernel(info, a_ref, acc, near, across, here, there, early, own, other, keep, send, trace, crossed):
    block = jnp.concatenate([whole(info, own, other, info[3], part) for part in range(2)], axis=0)
    product = acc[...] + jnp.dot(left_side(info, a_ref, 4), block, preferred_element_type=F32)
    rounded = product.astype(BF16)
    for part in range(2):
        low, high = rounded[part * 128 : part * 128 + 64], rounded[part * 128 + 64 : part * 128 + 128]
        keep[part], send[part] = halves(info, low, high)
    slices = [(0, near.at[0]), (1, near.at[1]), (-1, near.at[2]), (4, across)]
    slices += [(2, here.at[0]), (-2, there.at[0]), (3, here.at[1]), (-3, there.at[1])]
    crossed[...] = early[...]
    crossed[columns_of(info, 4), :] = crossed_sum(info, [own], [other], slices).astype(BF16)
    square = jnp.dot(rounded, crossed[...], preferred_element_type=F32)
    row = lax.broadcasted_iota(jnp.int32, (128, 128), 0)
    column = lax.broadcasted_iota(jnp.int32, (128, 128), 1)
    re = jnp.where(row == column, square[:128, :128] - square[128:, 128:], 0.0)
    im = jnp.where(row == column, square[:128, 128:] + square[128:, :128], 0.0)
    re = jnp.sum(jnp.sum(re, axis=0, keepdims=True), axis=1, keepdims=True)
    im = jnp.sum(jnp.sum(im, axis=0, keepdims=True), axis=1, keepdims=True)
    lane = lax.broadcasted_iota(jnp.int32, (1, 128), 1)
    trace[...] = jnp.where(lane == 2 * info[0], re, jnp.where(lane == 2 * info[0] + 1, im, 0.0))


def shards(fields, mom_table):
    rows = fields[:, 0]
    tm, row = lax.axis_index("tm"), lax.axis_index("row")
    core, place, half = tm % 2, row // 2, row % 2
    momenta = lax.dynamic_index_in_dim(mom_table, core, 0, keepdims=False)[0]
    others = lax.dynamic_index_in_dim(mom_table, 1 - core, 0, keepdims=False)[0]
    info = jnp.concatenate([jnp.stack([place, core]), momenta, others[3:]])
    wall = lax.optimization_barrier
    block_of_products = jax.ShapeDtypeStruct((256, 1024), F32)

    own = moved(rows, to_hub)

    ownx, p1 = moved(own, other_core), moved(own, onward)
    q1 = moved(ownx, onward)
    a = call(first_cut_kernel, info, [own, ownx], jax.ShapeDtypeStruct((2, 128, 1024), BF16), 1)
    a = moved(a, hub_ahead(0, 0))

    p2, p1x = moved(p1, onward), moved(p1, other_core)
    q2, q1x = moved(q1, onward), moved(q1, other_core)
    three, three_x = [own, p1, q1x], [ownx, q1, p1x]
    near = call(near_kernel, info, three + three_x, jax.ShapeDtypeStruct((3, 2, 128, 128), BF16), 1)
    p2, a = wall((p2, a))
    q2, near = wall((q2, near))

    p3, p2x = moved(p2, onward), moved(p2, other_core)
    q3, q2x = moved(q2, onward), moved(q2, other_core)
    across = call(across_kernel, info, [p2, q2], SLICES, 1)
    five, five_x = three + [p2, q2x], three_x + [q2, p2x]
    acc = call(lambda *refs: products_kernel(OFFSETS[:5], *refs), info, [a] + five + five_x, block_of_products, 1)
    p3, near = wall((p3, near))

    near = moved(near, hub_ahead(0, 0))
    p4, p3x = moved(p3, onward), moved(p3, other_core)
    q3, across, acc = wall((q3, across, acc))

    pair = jax.ShapeDtypeStruct((2, 2, 128, 128), BF16)
    here, there = call(late_kernel, info, [p2, p3, q2, q3], (pair, pair), 1)
    here, there, across = moved(here, hub_ahead(0, 0)), moved(there, hub_ahead(1, 0)), moved(across, hub_ahead(0, 2))
    p4, near, across, here, there = wall((p4, near, across, here, there))

    p4x, q3x = moved(p4, other_core), moved(q3, other_core)
    two, two_x = [p3, q3x], [q3, p3x]
    acc = call(
        lambda *refs: products_kernel(OFFSETS[5:7], *refs), info, [a] + two + two_x + [acc], block_of_products, 1
    )
    slices = [near, across, here, there]
    early = call(
        crossed_kernel, info, slices + five + two + five_x + two_x, jax.ShapeDtypeStruct((1024, 256), BF16), 1
    )
    half_block = jax.ShapeDtypeStruct((2, 64, 1024), BF16)
    keep, send, trace = call(
        last_kernel,
        info,
        [a, acc] + slices + [early, p4, p4x],
        (half_block, half_block, jax.ShapeDtypeStruct((1, 128), F32)),
        1,
        [pltpu.VMEM((1024, 256), BF16)],
    )

    below, above = moved(trace, along(1)), moved(trace, along(-1))
    kept, sent = moved(keep, from_hub(0)), moved(send, from_hub(1))
    two, three = wall((trace + above, below + trace + above))
    below, above = moved(two, along(3)), moved(three, along(-3))
    trace, kept, sent = wall((below + three + above, kept, sent))
    first, second = moved(trace, from_hub(0)), moved(trace, from_hub(1))
    products = jnp.where(half == 0, jnp.stack([kept, sent]), jnp.stack([sent, kept]))[:, None, None]
    both = jnp.where(half == 0, jnp.concatenate([first, second]), jnp.concatenate([second, first]))
    correlator = jnp.sum(both[:, :16].reshape(2, 8, 2), axis=1)[:, None, None, :] / F32(1024)
    return products, correlator


def solution(mesh):
    return jax.shard_map(
        shards,
        mesh=mesh,
        in_specs=(P(None, "tm", None, "row", None), P()),
        out_specs=(P(None, None, "tm", None, "row", None), P(None, None, "tm", None)),
        check_vma=False,
    )
```

time: 97.5 us -> 98.6 us (1.011)
  the two profiles are of different devices: /device:TPU:8 before, /device:TPU:1 now
where the time goes in v5:
time: 98.6 us; the launch traced here: 98.5 us
  starting transfers between devices  46.1 us (47%)
  waiting for transfers between devices  40.3 us (41%)
  Pallas kernels  8.36 us (8%)
  other arithmetic  2.2 us (2%)
    ppermute x29, starting transfers between devices, moved(): lax.ppermute(block, BOTH, [(index_of(*at), index_of(*route(*at))) for at...  46.1 us
    ppermute x29, waiting for transfers between devices, moved(): lax.ppermute(block, BOTH, [(index_of(*at), index_of(*route(*at))) for at...  40.3 us
    pallas_call x8, Pallas kernels, call(): pl.pallas_call(kernel, out_shape=out_shape, in_specs=[SMEM] + [VMEM] * le...  8.36 us
  transfers between devices with their start and end apart: 29, of which 12 were waited for; matrix products, arithmetic and copies ran while one was open for 2% of the time, Pallas kernels for 7%

profile of v5, /device:TPU:1, one launch (start us, length us, event | category | flops | bytes accessed | tf_op | source)
XLA Modules:
  0.0 98.5 jit_solution(6764028361009738191)
XLA Ops:
  0.6 4.2 %collective-permute-start = (bf16[2,2,64,1024]{3,2,1,0:T(8,128)(2,1)}, bf16[2,2,64,1024]{3,2,1,0:T(8,128)(2,1)S(1)}, u32[]{:S(2)}, u32[]{:S(2)}) collective-permute-start(bf16[2,2,64,1024]{3,2,1,0:T(8,128)(2,1)} %bitcast.16), channel_id=1, source_target_pairs={{0,128},{1,144},{2,130},{3,146},{4,132},{5,148},{6,134},{7,150},{8... | collective-permute-start | bytes 1572872 | tf_op jit(solution)/shard_map/ppermute | solution.py:27
  4.8 6.4 %collective-permute-done.own.refs_0_.refs_2_ = bf16[2,2,64,1024]{3,2,1,0:T(8,128)(2,1)S(1)} collective-permute-done((bf16[2,2,64,1024]{3,2,1,0:T(8,128)(2,1)}, bf16[2,2,64,1024]{3,2,1,0:T(8,128)(2,1)S(1)}, u32[]{:S(2)}, u32[]{:S(2)}) %collective-permute-start) | collective-permute-done | bytes 524320 | tf_op jit(solution)/shard_map/ppermute | solution.py:27
  11.3 1.5 %collective-permute-start.3 = (bf16[2,2,64,1024]{3,2,1,0:T(8,128)(2,1)S(1)}, bf16[2,2,64,1024]{3,2,1,0:T(8,128)(2,1)S(1)}, u32[]{:S(2)}, u32[]{:S(2)}) collective-permute-start(bf16[2,2,64,1024]{3,2,1,0:T(8,128)(2,1)S(1)} %collective-permute-done.own.refs_0_.refs_2_), channel_id=1, source_target_pairs={{0,16},{1,17},{2,18},{3,19},{4,20},{5,21},{6,22},{7,23},{8,24},{9,... | collective-permute-start | bytes 1572872 | tf_op jit(solution)/shard_map/ppermute | solution.py:27
  12.8 4.1 %collective-permute-start.1 = (bf16[2,2,64,1024]{3,2,1,0:T(8,128)(2,1)S(1)}, bf16[2,2,64,1024]{3,2,1,0:T(8,128)(2,1)S(1)}, u32[]{:S(2)}, u32[]{:S(2)}) collective-permute-start(bf16[2,2,64,1024]{3,2,1,0:T(8,128)(2,1)S(1)} %collective-permute-done.own.refs_0_.refs_2_), channel_id=1, source_target_pairs={{0,2},{1,3},{2,4},{3,5},{4,6},{5,7},{6,8},{7,9},{8,10},{9,11},{10,... | collective-permute-start | bytes 1572872 | tf_op jit(solution)/shard_map/ppermute | solution.py:27
  16.9 0.0 collective-permute-done.3.other.refs_3_.refs_7_
  16.9 1.9 %collective-permute-start.6 = (bf16[2,2,64,1024]{3,2,1,0:T(8,128)(2,1)S(1)}, bf16[2,2,64,1024]{3,2,1,0:T(8,128)(2,1)S(1)}, u32[]{:S(2)}, u32[]{:S(2)}) collective-permute-start(bf16[2,2,64,1024]{3,2,1,0:T(8,128)(2,1)S(1)} %collective-permute-done.3.other.refs_3_.refs_7_), channel_id=1, source_target_pairs={{0,2},{1,3},{2,4},{3,5},{4,6},{5,7},{6,8},{7,9},{8,10},{9,11},{10,... | collective-permute-start | bytes 1572872 | tf_op jit(solution)/shard_map/ppermute | solution.py:27
  18.8 0.6 slice.9
  19.4 0.7 pad_add_fusion.info.refs_0_
  20.1 2.9 %collective-permute-done.1.refs_1_.refs_3_ = bf16[2,2,64,1024]{3,2,1,0:T(8,128)(2,1)S(1)} collective-permute-done((bf16[2,2,64,1024]{3,2,1,0:T(8,128)(2,1)S(1)}, bf16[2,2,64,1024]{3,2,1,0:T(8,128)(2,1)S(1)}, u32[]{:S(2)}, u32[]{:S(2)}) %collective-permute-start.1) | collective-permute-done | bytes 524320 | tf_op jit(solution)/shard_map/ppermute | solution.py:27
  23.0 3.1 %collective-permute-start.2 = (bf16[2,2,64,1024]{3,2,1,0:T(8,128)(2,1)S(1)}, bf16[2,2,64,1024]{3,2,1,0:T(8,128)(2,1)S(1)}, u32[]{:S(2)}, u32[]{:S(2)}) collective-permute-start(bf16[2,2,64,1024]{3,2,1,0:T(8,128)(2,1)S(1)} %collective-permute-done.1.refs_1_.refs_3_), channel_id=1, source_target_pairs={{0,2},{1,3},{2,4},{3,5},{4,6},{5,7},{6,8},{7,9},{8,10},{9,11},{10,... | collective-permute-start | bytes 1572872 | tf_op jit(solution)/shard_map/ppermute | solution.py:27
  26.1 0.6 shard_map.41
  26.7 1.3 %collective-permute-start.4 = (bf16[2,128,1024]{2,1,0:T(8,128)(2,1)S(1)}, bf16[2,128,1024]{2,1,0:T(8,128)(2,1)S(1)}, u32[]{:S(2)}, u32[]{:S(2)}) collective-permute-start(bf16[2,128,1024]{2,1,0:T(8,128)(2,1)S(1)} %shard_map.41), channel_id=1, source_target_pairs={{0,33},{1,0},{2,35},{3,2},{4,37},{5,4},{6,39},{7,6},{8,41},{9,8},{... | collective-permute-start | bytes 1572872 | tf_op jit(solution)/shard_map/ppermute | solution.py:27
  28.0 1.4 %collective-permute-start.9 = (bf16[2,2,64,1024]{3,2,1,0:T(8,128)(2,1)S(1)}, bf16[2,2,64,1024]{3,2,1,0:T(8,128)(2,1)S(1)}, u32[]{:S(2)}, u32[]{:S(2)}) collective-permute-start(bf16[2,2,64,1024]{3,2,1,0:T(8,128)(2,1)S(1)} %collective-permute-done.1.refs_1_.refs_3_), channel_id=1, source_target_pairs={{0,16},{1,17},{2,18},{3,19},{4,20},{5,21},{6,22},{7,23},{8,24},{9,... | collective-permute-start | bytes 1572872 | tf_op jit(solution)/shard_map/ppermute | solution.py:27
  29.4 0.0 collective-permute-done.6.refs_4_.refs_8_
  29.4 1.0 %collective-permute-start.8 = (bf16[2,2,64,1024]{3,2,1,0:T(8,128)(2,1)S(1)}, bf16[2,2,64,1024]{3,2,1,0:T(8,128)(2,1)S(1)}, u32[]{:S(2)}, u32[]{:S(2)}) collective-permute-start(bf16[2,2,64,1024]{3,2,1,0:T(8,128)(2,1)S(1)} %collective-permute-done.6.refs_4_.refs_8_), channel_id=1, source_target_pairs={{0,16},{1,17},{2,18},{3,19},{4,20},{5,21},{6,22},{7,23},{8,24},{9,... | collective-permute-start | bytes 1572872 | tf_op jit(solution)/shard_map/ppermute | solution.py:27
  30.4 2.0 %collective-permute-start.7 = (bf16[2,2,64,1024]{3,2,1,0:T(8,128)(2,1)S(1)}, bf16[2,2,64,1024]{3,2,1,0:T(8,128)(2,1)S(1)}, u32[]{:S(2)}, u32[]{:S(2)}) collective-permute-start(bf16[2,2,64,1024]{3,2,1,0:T(8,128)(2,1)S(1)} %collective-permute-done.6.refs_4_.refs_8_), channel_id=1, source_target_pairs={{0,2},{1,3},{2,4},{3,5},{4,6},{5,7},{6,8},{7,9},{8,10},{9,11},{10,... | collective-permute-start | bytes 1572872 | tf_op jit(solution)/shard_map/ppermute | solution.py:27
  32.4 1.8 %collective-permute-done.2.own.refs_5_.own_2.refs_3_ = bf16[2,2,64,1024]{3,2,1,0:T(8,128)(2,1)S(1)} collective-permute-done((bf16[2,2,64,1024]{3,2,1,0:T(8,128)(2,1)S(1)}, bf16[2,2,64,1024]{3,2,1,0:T(8,128)(2,1)S(1)}, u32[]{:S(2)}, u32[]{:S(2)}) %collective-permute-start.2) | collective-permute-done | bytes 524320 | tf_op jit(solution)/shard_map/ppermute | solution.py:27
  34.2 9.0 %collective-permute-done.4.refs_1_.a_ref = bf16[2,128,1024]{2,1,0:T(8,128)(2,1)S(1)} collective-permute-done((bf16[2,128,1024]{2,1,0:T(8,128)(2,1)S(1)}, bf16[2,128,1024]{2,1,0:T(8,128)(2,1)S(1)}, u32[]{:S(2)}, u32[]{:S(2)}) %collective-permute-start.4) | collective-permute-done | bytes 524320 | tf_op jit(solution)/shard_map/ppermute | solution.py:27
  43.2 0.8 collective-permute-start.5
  44.0 0.0 collective-permute-start.12
  44.0 0.0 collective-permute-done.9.refs_5_.refs_9_
  44.0 0.0 collective-permute-done.8.refs_2_.refs_4_
  44.0 0.6 shard_map.42
  44.7 0.0 collective-permute-done.7.other.refs_10_.other_2
  44.7 0.6 collective-permute-start.11
  45.3 0.5 collective-permute-start.10
  45.8 5.8 %collective-permute-done.5.refs_2_.own_3.refs_5_ = bf16[2,2,64,1024]{3,2,1,0:T(8,128)(2,1)S(1)} collective-permute-done((bf16[2,2,64,1024]{3,2,1,0:T(8,128)(2,1)S(1)}, bf16[2,2,64,1024]{3,2,1,0:T(8,128)(2,1)S(1)}, u32[]{:S(2)}, u32[]{:S(2)}) %collective-permute-start.5) | collective-permute-done | bytes 524320 | tf_op jit(solution)/shard_map/ppermute | solution.py:27
  51.6 1.7 %collective-permute-start.15 = (bf16[2,2,64,1024]{3,2,1,0:T(8,128)(2,1)S(1)}, bf16[2,2,64,1024]{3,2,1,0:T(8,128)(2,1)S(1)}, u32[]{:S(2)}, u32[]{:S(2)}) collective-permute-start(bf16[2,2,64,1024]{3,2,1,0:T(8,128)(2,1)S(1)} %collective-permute-done.5.refs_2_.own_3.refs_5_), channel_id=1, source_target_pairs={{0,2},{1,3},{2,4},{3,5},{4,6},{5,7},{6,8},{7,9},{8,10},{9,11},{10,... | collective-permute-start | bytes 1572872 | tf_op jit(solution)/shard_map/ppermute | solution.py:27
  53.3 0.0 collective-permute-start.16
  53.3 0.6 shard_map.43
  53.9 0.0 collective-permute-done.12.refs_11_
  53.9 0.0 collective-permute-done.11.refs_6_.refs_4_
  53.9 1.4 %shard_map.44.refs_6_ = f32[256,1024]{1,0:T(8,128)S(1)} custom-call(s32[7]{0:T(128)S(1)} %pad_add_fusion.info.refs_0_, bf16[2,128,1024]{2,1,0:T(8,128)(2,1)S(1)} %collective-permute-done.4.refs_1_.a_ref, bf16[2,2,64,1024]{3,2,1,0:T(8,128)(2,1)S(1)} %collective-permute-done.own.refs_0_.refs_2_, ...), custom_call_target="tpu_custom_call" | custom-call | flops 1 | bytes 1048576 | tf_op jit(solution)/shard_map/pallas_call | solution.py:71
  55.3 1.9 %collective-permute-done.10.refs_4_.other_3.refs_12_ = bf16[2,2,64,1024]{3,2,1,0:T(8,128)(2,1)S(1)} collective-permute-done((bf16[2,2,64,1024]{3,2,1,0:T(8,128)(2,1)S(1)}, bf16[2,2,64,1024]{3,2,1,0:T(8,128)(2,1)S(1)}, u32[]{:S(2)}, u32[]{:S(2)}) %collective-permute-start.10) | collective-permute-done | bytes 524320 | tf_op jit(solution)/shard_map/ppermute | solution.py:27
  57.2 0.6 shard_map.46
  57.8 0.3 collective-permute-start.18
  58.1 4.3 %collective-permute-start.19 = (bf16[2,2,128,128]{3,2,1,0:T(8,128)(2,1)S(1)}, bf16[2,2,128,128]{3,2,1,0:T(8,128)(2,1)S(1)}, u32[]{:S(2)}, u32[]{:S(2)}) collective-permute-start(bf16[2,2,128,128]{3,2,1,0:T(8,128)(2,1)S(1)} %get-tuple-element.36), channel_id=1, source_target_pairs={{0,48},{1,49},{2,50},{3,51},{4,52},{5,53},{6,54},{7,55},{8,56},{9,... | collective-permute-start | bytes 393224 | tf_op jit(solution)/shard_map/ppermute | solution.py:27
  62.4 1.4 %collective-permute-start.17 = (bf16[2,128,128]{2,1,0:T(8,128)(2,1)S(1)}, bf16[2,128,128]{2,1,0:T(8,128)(2,1)S(1)}, u32[]{:S(2)}, u32[]{:S(2)}) collective-permute-start(bf16[2,128,128]{2,1,0:T(8,128)(2,1)S(1)} %shard_map.43), channel_id=1, source_target_pairs={{0,37},{1,4},{2,39},{3,6},{4,41},{5,8},{6,43},{7,10},{8,45},{9,12}... | collective-permute-start | bytes 196616 | tf_op jit(solution)/shard_map/ppermute | solution.py:27
  63.7 0.0 collective-permute-done.16.near
  63.7 0.0 collective-permute-start.14
  63.7 0.0 collective-permute-done.15.own
  63.7 0.5 collective-permute-start.13
  64.3 6.9 %collective-permute-done.17.across = bf16[2,128,128]{2,1,0:T(8,128)(2,1)S(1)} collective-permute-done((bf16[2,128,128]{2,1,0:T(8,128)(2,1)S(1)}, bf16[2,128,128]{2,1,0:T(8,128)(2,1)S(1)}, u32[]{:S(2)}, u32[]{:S(2)}) %collective-permute-start.17) | collective-permute-done | bytes 65568 | tf_op jit(solution)/shard_map/ppermute | solution.py:27
  71.2 0.0 collective-permute-done.18.here
  71.2 0.2 collective-permute-done.19.there
  71.4 1.0 %shard_map.45.acc = f32[256,1024]{1,0:T(8,128)S(1)} custom-call(s32[7]{0:T(128)S(1)} %pad_add_fusion.info.refs_0_, bf16[2,128,1024]{2,1,0:T(8,128)(2,1)S(1)} %collective-permute-done.4.refs_1_.a_ref, bf16[2,2,64,1024]{3,2,1,0:T(8,128)(2,1)S(1)} %collective-permute-done.5.refs_2_.own_3.refs_5_, ...), custom_call_target="tpu_custom_call" | custom-call | flops 1 | bytes 1048576 | tf_op jit(solution)/shard_map/pallas_call | solution.py:71
  72.4 1.9 %shard_map.47.early = bf16[1024,256]{1,0:T(8,128)(2,1)S(1)} custom-call(s32[7]{0:T(128)S(1)} %pad_add_fusion.info.refs_0_, bf16[3,2,128,128]{3,2,1,0:T(8,128)(2,1)S(1)} %collective-permute-done.16.near, bf16[2,128,128]{2,1,0:T(8,128)(2,1)S(1)} %collective-permute-done.17.across, bf16[2,2,128,128]{3,2,1,0:T(8,128)(2,1)S(1)} %collective-permute-done.18.here, ...), custom_call_target="tpu_custom_call" | custom-call | flops 1 | bytes 1048576 | tf_op jit(solution)/shard_map/pallas_call | solution.py:71
  74.3 1.7 %shard_map.48 = (bf16[2,64,1024]{2,1,0:T(8,128)(2,1)S(1)}, bf16[2,64,1024]{2,1,0:T(8,128)(2,1)S(1)}, f32[1,128]{1,0:T(1,128)S(1)}) custom-call(s32[7]{0:T(128)S(1)} %pad_add_fusion.info.refs_0_, bf16[2,128,1024]{2,1,0:T(8,128)(2,1)S(1)} %collective-permute-done.4.refs_1_.a_ref, f32[256,1024]{1,0:T(8,128)S(1)} %shard_map.45.acc, ...), custom_call_target="tpu_custom_call" | custom-call | flops 1 | bytes 1048576 | tf_op jit(solution)/shard_map/pallas_call | solution.py:71
  76.0 3.4 %collective-permute-start.21 = (f32[1,128]{1,0:T(1,128)S(1)}, f32[1,128]{1,0:T(1,128)S(1)}, u32[]{:S(2)}, u32[]{:S(2)}) collective-permute-start(f32[1,128]{1,0:T(1,128)S(1)} %get-tuple-element.42), channel_id=1, source_target_pairs={{0,14},{1,15},{2,0},{3,1},{4,2},{5,3},{6,4},{7,5},{8,6},{9,7},{10,... | collective-permute-start | bytes 1544 | tf_op jit(solution)/shard_map/ppermute | solution.py:27
  79.4 0.0 collective-permute-start.25
  79.4 1.2 %collective-permute-start.26 = (bf16[2,64,1024]{2,1,0:T(8,128)(2,1)S(1)}, bf16[2,64,1024]{2,1,0:T(8,128)(2,1)S(1)}, u32[]{:S(2)}, u32[]{:S(2)}) collective-permute-start(bf16[2,64,1024]{2,1,0:T(8,128)(2,1)S(1)} %get-tuple-element.46), channel_id=1, source_target_pairs={{0,129},{1,113},{2,131},{3,115},{4,133},{5,117},{6,135},{7,119},{8... | collective-permute-start | bytes 786440 | tf_op jit(solution)/shard_map/ppermute | solution.py:27
  80.6 0.0 collective-permute-done.21
  80.6 2.4 %collective-permute-done.22 = f32[1,128]{1,0:T(1,128)S(1)} collective-permute-done((f32[1,128]{1,0:T(1,128)S(1)}, f32[1,128]{1,0:T(1,128)S(1)}, u32[]{:S(2)}, u32[]{:S(2)}) %collective-permute-start.22) | collective-permute-done | bytes 544 | tf_op jit(solution)/shard_map/ppermute | solution.py:27
  83.0 0.1 collective-permute-start.24
  83.1 3.1 %collective-permute-start.23 = (f32[1,128]{1,0:T(1,128)S(1)}, f32[1,128]{1,0:T(1,128)S(1)}, u32[]{:S(2)}, u32[]{:S(2)}) collective-permute-start(f32[1,128]{1,0:T(1,128)S(1)} %get-tuple-element.43), channel_id=1, source_target_pairs={{0,6},{1,7},{2,8},{3,9},{4,10},{5,11},{6,12},{7,13},{8,14},{9,15},... | collective-permute-start | bytes 1544 | tf_op jit(solution)/shard_map/ppermute | solution.py:27
  86.3 1.0 collective-permute-done.24
  87.2 1.3 %collective-permute-done.23 = f32[1,128]{1,0:T(1,128)S(1)} collective-permute-done((f32[1,128]{1,0:T(1,128)S(1)}, f32[1,128]{1,0:T(1,128)S(1)}, u32[]{:S(2)}, u32[]{:S(2)}) %collective-permute-start.23) | collective-permute-done | bytes 544 | tf_op jit(solution)/shard_map/ppermute | solution.py:27
  88.5 0.6 collective-permute-done.25
  89.1 0.0 collective-permute-done.26
  89.1 1.8 %collective-permute-start.28 = (f32[1,128]{1,0:T(1,128)S(1)}, f32[1,128]{1,0:T(1,128)S(1)}, u32[]{:S(2)}, u32[]{:S(2)}) collective-permute-start(f32[1,128]{1,0:T(1,128)S(1)} %add_add_fusion), channel_id=1, source_target_pairs={{0,129},{1,113},{2,131},{3,115},{4,133},{5,117},{6,135},{7,119},{8... | collective-permute-start | bytes 1544 | tf_op jit(solution)/shard_map/ppermute | solution.py:27
  90.9 6.0 %collective-permute-start.27 = (f32[1,128]{1,0:T(1,128)S(1)}, f32[1,128]{1,0:T(1,128)S(1)}, u32[]{:S(2)}, u32[]{:S(2)}) collective-permute-start(f32[1,128]{1,0:T(1,128)S(1)} %add_add_fusion), channel_id=1, source_target_pairs={{0,128},{1,112},{2,130},{3,114},{4,132},{5,116},{6,134},{7,118},{8... | collective-permute-start | bytes 1544 | tf_op jit(solution)/shard_map/ppermute | solution.py:27
  96.9 0.9 maximum_select_fusion
  97.8 0.1 reshape.79
  97.9 0.6 broadcast_multiply_fusion
  (14 shorter events, 0.1 us)
Async XLA Ops:
  0.6 10.6 %collective-permute-start = (bf16[2,2,64,1024]{3,2,1,0:T(8,128)(2,1)}, bf16[2,2,64,1024]{3,2,1,0:T(8,128)(2,1)S(1)}, u32[]{:S(2)}, u32[]{:S(2)}) collective-permute-start(bf16[2,2,64,1024]{3,2,1,0:T(8,128)(2,1)} %bitcast.16), channel_id=1, source_target_pairs={{0,128},{1,144},{2,130},{3,146},{4,132},{5,148},{6,134},{7,150},{8... | collective-permute-start | bytes 1572872 | tf_op jit(solution)/shard_map/ppermute | solution.py:27
  11.3 5.6 %collective-permute-start.3 = (bf16[2,2,64,1024]{3,2,1,0:T(8,128)(2,1)S(1)}, bf16[2,2,64,1024]{3,2,1,0:T(8,128)(2,1)S(1)}, u32[]{:S(2)}, u32[]{:S(2)}) collective-permute-start(bf16[2,2,64,1024]{3,2,1,0:T(8,128)(2,1)S(1)} %collective-permute-done.own.refs_0_.refs_2_), channel_id=1, source_target_pairs={{0,16},{1,17},{2,18},{3,19},{4,20},{5,21},{6,22},{7,23},{8,24},{9,... | collective-permute-start | bytes 1572872 | tf_op jit(solution)/shard_map/ppermute | solution.py:27
  12.8 10.2 %collective-permute-start.1 = (bf16[2,2,64,1024]{3,2,1,0:T(8,128)(2,1)S(1)}, bf16[2,2,64,1024]{3,2,1,0:T(8,128)(2,1)S(1)}, u32[]{:S(2)}, u32[]{:S(2)}) collective-permute-start(bf16[2,2,64,1024]{3,2,1,0:T(8,128)(2,1)S(1)} %collective-permute-done.own.refs_0_.refs_2_), channel_id=1, source_target_pairs={{0,2},{1,3},{2,4},{3,5},{4,6},{5,7},{6,8},{7,9},{8,10},{9,11},{10,... | collective-permute-start | bytes 1572872 | tf_op jit(solution)/shard_map/ppermute | solution.py:27
  16.9 1.9 %copy-start = (s32[2,1,4]{2,1,0:T(1,128)S(1)}, s32[2,1,4]{2,1,0:T(1,128)}, u32[]{:S(2)}) copy-start(s32[2,1,4]{2,1,0:T(1,128)} %param.3) | copy-start | bytes 100
  16.9 12.6 %collective-permute-start.6 = (bf16[2,2,64,1024]{3,2,1,0:T(8,128)(2,1)S(1)}, bf16[2,2,64,1024]{3,2,1,0:T(8,128)(2,1)S(1)}, u32[]{:S(2)}, u32[]{:S(2)}) collective-permute-start(bf16[2,2,64,1024]{3,2,1,0:T(8,128)(2,1)S(1)} %collective-permute-done.3.other.refs_3_.refs_7_), channel_id=1, source_target_pairs={{0,2},{1,3},{2,4},{3,5},{4,6},{5,7},{6,8},{7,9},{8,10},{9,11},{10,... | collective-permute-start | bytes 1572872 | tf_op jit(solution)/shard_map/ppermute | solution.py:27
  23.0 11.2 %collective-permute-start.2 = (bf16[2,2,64,1024]{3,2,1,0:T(8,128)(2,1)S(1)}, bf16[2,2,64,1024]{3,2,1,0:T(8,128)(2,1)S(1)}, u32[]{:S(2)}, u32[]{:S(2)}) collective-permute-start(bf16[2,2,64,1024]{3,2,1,0:T(8,128)(2,1)S(1)} %collective-permute-done.1.refs_1_.refs_3_), channel_id=1, source_target_pairs={{0,2},{1,3},{2,4},{3,5},{4,6},{5,7},{6,8},{7,9},{8,10},{9,11},{10,... | collective-permute-start | bytes 1572872 | tf_op jit(solution)/shard_map/ppermute | solution.py:27
  26.7 16.6 %collective-permute-start.4 = (bf16[2,128,1024]{2,1,0:T(8,128)(2,1)S(1)}, bf16[2,128,1024]{2,1,0:T(8,128)(2,1)S(1)}, u32[]{:S(2)}, u32[]{:S(2)}) collective-permute-start(bf16[2,128,1024]{2,1,0:T(8,128)(2,1)S(1)} %shard_map.41), channel_id=1, source_target_pairs={{0,33},{1,0},{2,35},{3,2},{4,37},{5,4},{6,39},{7,6},{8,41},{9,8},{... | collective-permute-start | bytes 1572872 | tf_op jit(solution)/shard_map/ppermute | solution.py:27
  28.0 16.1 %collective-permute-start.9 = (bf16[2,2,64,1024]{3,2,1,0:T(8,128)(2,1)S(1)}, bf16[2,2,64,1024]{3,2,1,0:T(8,128)(2,1)S(1)}, u32[]{:S(2)}, u32[]{:S(2)}) collective-permute-start(bf16[2,2,64,1024]{3,2,1,0:T(8,128)(2,1)S(1)} %collective-permute-done.1.refs_1_.refs_3_), channel_id=1, source_target_pairs={{0,16},{1,17},{2,18},{3,19},{4,20},{5,21},{6,22},{7,23},{8,24},{9,... | collective-permute-start | bytes 1572872 | tf_op jit(solution)/shard_map/ppermute | solution.py:27
  29.4 14.6 %collective-permute-start.8 = (bf16[2,2,64,1024]{3,2,1,0:T(8,128)(2,1)S(1)}, bf16[2,2,64,1024]{3,2,1,0:T(8,128)(2,1)S(1)}, u32[]{:S(2)}, u32[]{:S(2)}) collective-permute-start(bf16[2,2,64,1024]{3,2,1,0:T(8,128)(2,1)S(1)} %collective-permute-done.6.refs_4_.refs_8_), channel_id=1, source_target_pairs={{0,16},{1,17},{2,18},{3,19},{4,20},{5,21},{6,22},{7,23},{8,24},{9,... | collective-permute-start | bytes 1572872 | tf_op jit(solution)/shard_map/ppermute | solution.py:27
  30.4 14.2 %collective-permute-start.7 = (bf16[2,2,64,1024]{3,2,1,0:T(8,128)(2,1)S(1)}, bf16[2,2,64,1024]{3,2,1,0:T(8,128)(2,1)S(1)}, u32[]{:S(2)}, u32[]{:S(2)}) collective-permute-start(bf16[2,2,64,1024]{3,2,1,0:T(8,128)(2,1)S(1)} %collective-permute-done.6.refs_4_.refs_8_), channel_id=1, source_target_pairs={{0,2},{1,3},{2,4},{3,5},{4,6},{5,7},{6,8},{7,9},{8,10},{9,11},{10,... | collective-permute-start | bytes 1572872 | tf_op jit(solution)/shard_map/ppermute | solution.py:27
  43.2 8.3 %collective-permute-start.5 = (bf16[2,2,64,1024]{3,2,1,0:T(8,128)(2,1)S(1)}, bf16[2,2,64,1024]{3,2,1,0:T(8,128)(2,1)S(1)}, u32[]{:S(2)}, u32[]{:S(2)}) collective-permute-start(bf16[2,2,64,1024]{3,2,1,0:T(8,128)(2,1)S(1)} %collective-permute-done.2.own.refs_5_.own_2.refs_3_), channel_id=1, source_target_pairs={{0,2},{1,3},{2,4},{3,5},{4,6},{5,7},{6,8},{7,9},{8,10},{9,11},{10,... | collective-permute-start | bytes 1572872 | tf_op jit(solution)/shard_map/ppermute | solution.py:27
  44.0 9.8 %collective-permute-start.12 = (bf16[2,2,64,1024]{3,2,1,0:T(8,128)(2,1)S(1)}, bf16[2,2,64,1024]{3,2,1,0:T(8,128)(2,1)S(1)}, u32[]{:S(2)}, u32[]{:S(2)}) collective-permute-start(bf16[2,2,64,1024]{3,2,1,0:T(8,128)(2,1)S(1)} %collective-permute-done.2.own.refs_5_.own_2.refs_3_), channel_id=1, source_target_pairs={{0,16},{1,17},{2,18},{3,19},{4,20},{5,21},{6,22},{7,23},{8,24},{9,... | collective-permute-start | bytes 1572872 | tf_op jit(solution)/shard_map/ppermute | solution.py:27
  44.7 9.2 %collective-permute-start.11 = (bf16[2,2,64,1024]{3,2,1,0:T(8,128)(2,1)S(1)}, bf16[2,2,64,1024]{3,2,1,0:T(8,128)(2,1)S(1)}, u32[]{:S(2)}, u32[]{:S(2)}) collective-permute-start(bf16[2,2,64,1024]{3,2,1,0:T(8,128)(2,1)S(1)} %collective-permute-done.7.other.refs_10_.other_2), channel_id=1, source_target_pairs={{0,16},{1,17},{2,18},{3,19},{4,20},{5,21},{6,22},{7,23},{8,24},{9,... | collective-permute-start | bytes 1572872 | tf_op jit(solution)/shard_map/ppermute | solution.py:27
  45.3 11.9 %collective-permute-start.10 = (bf16[2,2,64,1024]{3,2,1,0:T(8,128)(2,1)S(1)}, bf16[2,2,64,1024]{3,2,1,0:T(8,128)(2,1)S(1)}, u32[]{:S(2)}, u32[]{:S(2)}) collective-permute-start(bf16[2,2,64,1024]{3,2,1,0:T(8,128)(2,1)S(1)} %collective-permute-done.7.other.refs_10_.other_2), channel_id=1, source_target_pairs={{0,2},{1,3},{2,4},{3,5},{4,6},{5,7},{6,8},{7,9},{8,10},{9,11},{10,... | collective-permute-start | bytes 1572872 | tf_op jit(solution)/shard_map/ppermute | solution.py:27
  51.6 12.2 %collective-permute-start.15 = (bf16[2,2,64,1024]{3,2,1,0:T(8,128)(2,1)S(1)}, bf16[2,2,64,1024]{3,2,1,0:T(8,128)(2,1)S(1)}, u32[]{:S(2)}, u32[]{:S(2)}) collective-permute-start(bf16[2,2,64,1024]{3,2,1,0:T(8,128)(2,1)S(1)} %collective-permute-done.5.refs_2_.own_3.refs_5_), channel_id=1, source_target_pairs={{0,2},{1,3},{2,4},{3,5},{4,6},{5,7},{6,8},{7,9},{8,10},{9,11},{10,... | collective-permute-start | bytes 1572872 | tf_op jit(solution)/shard_map/ppermute | solution.py:27
  53.3 10.5 %collective-permute-start.16 = (bf16[3,2,128,128]{3,2,1,0:T(8,128)(2,1)S(1)}, bf16[3,2,128,128]{3,2,1,0:T(8,128)(2,1)S(1)}, u32[]{:S(2)}, u32[]{:S(2)}) collective-permute-start(bf16[3,2,128,128]{3,2,1,0:T(8,128)(2,1)S(1)} %shard_map.42), channel_id=1, source_target_pairs={{0,33},{1,0},{2,35},{3,2},{4,37},{5,4},{6,39},{7,6},{8,41},{9,8},{... | collective-permute-start | bytes 589832 | tf_op jit(solution)/shard_map/ppermute | solution.py:27
  57.8 13.4 %collective-permute-start.18 = (bf16[2,2,128,128]{3,2,1,0:T(8,128)(2,1)S(1)}, bf16[2,2,128,128]{3,2,1,0:T(8,128)(2,1)S(1)}, u32[]{:S(2)}, u32[]{:S(2)}) collective-permute-start(bf16[2,2,128,128]{3,2,1,0:T(8,128)(2,1)S(1)} %get-tuple-element.35), channel_id=1, source_target_pairs={{0,33},{1,0},{2,35},{3,2},{4,37},{5,4},{6,39},{7,6},{8,41},{9,8},{... | collective-permute-start | bytes 393224 | tf_op jit(solution)/shard_map/ppermute | solution.py:27
  58.1 13.3 %collective-permute-start.19 = (bf16[2,2,128,128]{3,2,1,0:T(8,128)(2,1)S(1)}, bf16[2,2,128,128]{3,2,1,0:T(8,128)(2,1)S(1)}, u32[]{:S(2)}, u32[]{:S(2)}) collective-permute-start(bf16[2,2,128,128]{3,2,1,0:T(8,128)(2,1)S(1)} %get-tuple-element.36), channel_id=1, source_target_pairs={{0,48},{1,49},{2,50},{3,51},{4,52},{5,53},{6,54},{7,55},{8,56},{9,... | collective-permute-start | bytes 393224 | tf_op jit(solution)/shard_map/ppermute | solution.py:27
  62.4 8.8 %collective-permute-start.17 = (bf16[2,128,128]{2,1,0:T(8,128)(2,1)S(1)}, bf16[2,128,128]{2,1,0:T(8,128)(2,1)S(1)}, u32[]{:S(2)}, u32[]{:S(2)}) collective-permute-start(bf16[2,128,128]{2,1,0:T(8,128)(2,1)S(1)} %shard_map.43), channel_id=1, source_target_pairs={{0,37},{1,4},{2,39},{3,6},{4,41},{5,8},{6,43},{7,10},{8,45},{9,12}... | collective-permute-start | bytes 196616 | tf_op jit(solution)/shard_map/ppermute | solution.py:27
  63.7 7.7 %collective-permute-start.14 = (bf16[2,2,64,1024]{3,2,1,0:T(8,128)(2,1)S(1)}, bf16[2,2,64,1024]{3,2,1,0:T(8,128)(2,1)S(1)}, u32[]{:S(2)}, u32[]{:S(2)}) collective-permute-start(bf16[2,2,64,1024]{3,2,1,0:T(8,128)(2,1)S(1)} %collective-permute-done.5.refs_2_.own_3.refs_5_), channel_id=1, source_target_pairs={{0,16},{1,17},{2,18},{3,19},{4,20},{5,21},{6,22},{7,23},{8,24},{9,... | collective-permute-start | bytes 1572872 | tf_op jit(solution)/shard_map/ppermute | solution.py:27
  63.7 7.7 %collective-permute-start.13 = (bf16[2,2,64,1024]{3,2,1,0:T(8,128)(2,1)S(1)}, bf16[2,2,64,1024]{3,2,1,0:T(8,128)(2,1)S(1)}, u32[]{:S(2)}, u32[]{:S(2)}) collective-permute-start(bf16[2,2,64,1024]{3,2,1,0:T(8,128)(2,1)S(1)} %collective-permute-done.10.refs_4_.other_3.refs_12_), channel_id=1, source_target_pairs={{0,16},{1,17},{2,18},{3,19},{4,20},{5,21},{6,22},{7,23},{8,24},{9,... | collective-permute-start | bytes 1572872 | tf_op jit(solution)/shard_map/ppermute | solution.py:27
  71.4 2.9 %collective-permute-start.20 = (bf16[2,2,64,1024]{3,2,1,0:T(8,128)(2,1)S(1)}, bf16[2,2,64,1024]{3,2,1,0:T(8,128)(2,1)S(1)}, u32[]{:S(2)}, u32[]{:S(2)}) collective-permute-start(bf16[2,2,64,1024]{3,2,1,0:T(8,128)(2,1)S(1)} %collective-permute-done.15.own), channel_id=1, source_target_pairs={{0,16},{1,17},{2,18},{3,19},{4,20},{5,21},{6,22},{7,23},{8,24},{9,... | collective-permute-start | bytes 1572872 | tf_op jit(solution)/shard_map/ppermute | solution.py:27
  76.0 4.6 %collective-permute-start.21 = (f32[1,128]{1,0:T(1,128)S(1)}, f32[1,128]{1,0:T(1,128)S(1)}, u32[]{:S(2)}, u32[]{:S(2)}) collective-permute-start(f32[1,128]{1,0:T(1,128)S(1)} %get-tuple-element.42), channel_id=1, source_target_pairs={{0,14},{1,15},{2,0},{3,1},{4,2},{5,3},{6,4},{7,5},{8,6},{9,7},{10,... | collective-permute-start | bytes 1544 | tf_op jit(solution)/shard_map/ppermute | solution.py:27
  79.4 3.6 %collective-permute-start.22 = (f32[1,128]{1,0:T(1,128)S(1)}, f32[1,128]{1,0:T(1,128)S(1)}, u32[]{:S(2)}, u32[]{:S(2)}) collective-permute-start(f32[1,128]{1,0:T(1,128)S(1)} %get-tuple-element.42), channel_id=1, source_target_pairs={{0,2},{1,3},{2,4},{3,5},{4,6},{5,7},{6,8},{7,9},{8,10},{9,11},{10,... | collective-permute-start | bytes 1544 | tf_op jit(solution)/shard_map/ppermute | solution.py:27
  79.4 9.7 %collective-permute-start.25 = (bf16[2,64,1024]{2,1,0:T(8,128)(2,1)S(1)}, bf16[2,64,1024]{2,1,0:T(8,128)(2,1)S(1)}, u32[]{:S(2)}, u32[]{:S(2)}) collective-permute-start(bf16[2,64,1024]{2,1,0:T(8,128)(2,1)S(1)} %get-tuple-element.45), channel_id=1, source_target_pairs={{0,128},{1,112},{2,130},{3,114},{4,132},{5,116},{6,134},{7,118},{8... | collective-permute-start | bytes 786440 | tf_op jit(solution)/shard_map/ppermute | solution.py:27
  79.4 9.7 %collective-permute-start.26 = (bf16[2,64,1024]{2,1,0:T(8,128)(2,1)S(1)}, bf16[2,64,1024]{2,1,0:T(8,128)(2,1)S(1)}, u32[]{:S(2)}, u32[]{:S(2)}) collective-permute-start(bf16[2,64,1024]{2,1,0:T(8,128)(2,1)S(1)} %get-tuple-element.46), channel_id=1, source_target_pairs={{0,129},{1,113},{2,131},{3,115},{4,133},{5,117},{6,135},{7,119},{8... | collective-permute-start | bytes 786440 | tf_op jit(solution)/shard_map/ppermute | solution.py:27
  83.0 4.2 %collective-permute-start.24 = (f32[1,128]{1,0:T(1,128)S(1)}, f32[1,128]{1,0:T(1,128)S(1)}, u32[]{:S(2)}, u32[]{:S(2)}) collective-permute-start(f32[1,128]{1,0:T(1,128)S(1)} %get-tuple-element.44), channel_id=1, source_target_pairs={{0,10},{1,11},{2,12},{3,13},{4,14},{5,15},{6,0},{7,1},{8,2},{9,3},... | collective-permute-start | bytes 1544 | tf_op jit(solution)/shard_map/ppermute | solution.py:27
  83.1 5.4 %collective-permute-start.23 = (f32[1,128]{1,0:T(1,128)S(1)}, f32[1,128]{1,0:T(1,128)S(1)}, u32[]{:S(2)}, u32[]{:S(2)}) collective-permute-start(f32[1,128]{1,0:T(1,128)S(1)} %get-tuple-element.43), channel_id=1, source_target_pairs={{0,6},{1,7},{2,8},{3,9},{4,10},{5,11},{6,12},{7,13},{8,14},{9,15},... | collective-permute-start | bytes 1544 | tf_op jit(solution)/shard_map/ppermute | solution.py:27
  89.1 8.7 %collective-permute-start.28 = (f32[1,128]{1,0:T(1,128)S(1)}, f32[1,128]{1,0:T(1,128)S(1)}, u32[]{:S(2)}, u32[]{:S(2)}) collective-permute-start(f32[1,128]{1,0:T(1,128)S(1)} %add_add_fusion), channel_id=1, source_target_pairs={{0,129},{1,113},{2,131},{3,115},{4,133},{5,117},{6,135},{7,119},{8... | collective-permute-start | bytes 1544 | tf_op jit(solution)/shard_map/ppermute | solution.py:27
  90.9 6.9 %collective-permute-start.27 = (f32[1,128]{1,0:T(1,128)S(1)}, f32[1,128]{1,0:T(1,128)S(1)}, u32[]{:S(2)}, u32[]{:S(2)}) collective-permute-start(f32[1,128]{1,0:T(1,128)S(1)} %add_add_fusion), channel_id=1, source_target_pairs={{0,128},{1,112},{2,130},{3,114},{4,132},{5,116},{6,134},{7,118},{8... | collective-permute-start | bytes 1544 | tf_op jit(solution)/shard_map/ppermute | solution.py:27

commit v6 on v5

--- a/solution.py
+++ b/solution.py
@@ -60,6 +60,9 @@
 
     return route
 
+
+WEIGHT = 3_000_000_000
+SMALL = 1_000_000_000
 
 VMEM = pl.BlockSpec(memory_space=pltpu.VMEM)
 SMEM = pl.BlockSpec(memory_space=pltpu.SMEM)
@@ -166,13 +169,25 @@
     return total
 
 
-def crossed_kernel(info, near, across, here, there, *refs):
-    slices = [(0, near.at[0]), (1, near.at[1]), (-1, near.at[2]), (4, across)]
-    slices += [(2, here.at[0]), (-2, there.at[0]), (3, here.at[1]), (-3, there.at[1])]
-    total = crossed_sum(info, refs[0:7], refs[7:14], slices)
+def first_slices(near, across):
+    return [(0, near.at[0]), (1, near.at[1]), (-1, near.at[2]), (4, across)]
+
+
+def last_slices(here, there):
+    return [(2, here.at[0]), (-2, there.at[0]), (3, here.at[1]), (-3, there.at[1])]
+
+
+def early_kernel(info, near, across, *refs):
+    refs[10][...] = crossed_sum(info, refs[0:5], refs[5:10], first_slices(near, across))
+
+
+def crossed_kernel(info, near, across, here, there, early, *refs):
+    own, other, out = refs[0:7], refs[7:14], refs[14]
+    later = crossed_sum(info, own[5:], other[5:], first_slices(near, across))
+    total = jnp.concatenate([early[...], later], axis=0) + crossed_sum(info, own, other, last_slices(here, there))
     for k, offset in enumerate(OFFSETS[:7]):
-        refs[14][columns_of(info, offset), :] = total[128 * k : 128 * k + 128].astype(BF16)
-    refs[14][columns_of(info, 4), :] = jnp.zeros((128, 256), BF16)
+        out[columns_of(info, offset), :] = total[128 * k : 128 * k + 128].astype(BF16)
+    out[columns_of(info, 4), :] = jnp.zeros((128, 256), BF16)
 
 
 def last_kernel(info, a_ref, acc, near, across, here, there, early, own, other, keep, send, trace, crossed):
@@ -182,8 +197,7 @@
     for part in range(2):
         low, high = rounded[part * 128 : part * 128 + 64], rounded[part * 128 + 64 : part * 128 + 128]
         keep[part], send[part] = halves(info, low, high)
-    slices = [(0, near.at[0]), (1, near.at[1]), (-1, near.at[2]), (4, across)]
-    slices += [(2, here.at[0]), (-2, there.at[0]), (3, here.at[1]), (-3, there.at[1])]
+    slices = first_slices(near, across) + last_slices(here, there)
     crossed[...] = early[...]
     crossed[columns_of(info, 4), :] = crossed_sum(info, [own], [other], slices).astype(BF16)
     square = jnp.dot(rounded, crossed[...], preferred_element_type=F32)
@@ -218,24 +232,28 @@
     q2, q1x = moved(q1, onward), moved(q1, other_core)
     three, three_x = [own, p1, q1x], [ownx, q1, p1x]
     near = call(near_kernel, info, three + three_x, jax.ShapeDtypeStruct((3, 2, 128, 128), BF16), 1)
-    p2, a = wall((p2, a))
+    acc = call(lambda *refs: products_kernel(OFFSETS[:1], *refs), info, [a, own, ownx], block_of_products, WEIGHT)
+    p2, a, acc = wall((p2, a, acc))
     q2, near = wall((q2, near))
 
     p3, p2x = moved(p2, onward), moved(p2, other_core)
     q3, q2x = moved(q2, onward), moved(q2, other_core)
     across = call(across_kernel, info, [p2, q2], SLICES, 1)
     five, five_x = three + [p2, q2x], three_x + [q2, p2x]
-    acc = call(lambda *refs: products_kernel(OFFSETS[:5], *refs), info, [a] + five + five_x, block_of_products, 1)
+    acc = call(
+        lambda *refs: products_kernel(OFFSETS[1:5], *refs), info, [a] + five[1:] + five_x[1:] + [acc], block_of_products, 1
+    )
     p3, near = wall((p3, near))
 
     near = moved(near, hub_ahead(0, 0))
     p4, p3x = moved(p3, onward), moved(p3, other_core)
-    q3, across, acc = wall((q3, across, acc))
+    q3, acc = wall((q3, acc))
 
     pair = jax.ShapeDtypeStruct((2, 2, 128, 128), BF16)
     here, there = call(late_kernel, info, [p2, p3, q2, q3], (pair, pair), 1)
     here, there, across = moved(here, hub_ahead(0, 0)), moved(there, hub_ahead(1, 0)), moved(across, hub_ahead(0, 2))
-    p4, near, across, here, there = wall((p4, near, across, here, there))
+    early = call(early_kernel, info, [near, across] + five + five_x, jax.ShapeDtypeStruct((640, 256), F32), SMALL)
+    p4, near, across, here, there, early = wall((p4, near, across, here, there, early))
 
     p4x, q3x = moved(p4, other_core), moved(q3, other_core)
     two, two_x = [p3, q3x], [q3, p3x]
@@ -244,7 +262,7 @@
     )
     slices = [near, across, here, there]
     early = call(
-        crossed_kernel, info, slices + five + two + five_x + two_x, jax.ShapeDtypeStruct((1024, 256), BF16), 1
+        crossed_kernel, info, slices + [early] + five + two + five_x + two_x, jax.ShapeDtypeStruct((1024, 256), BF16), 1
     )
     half_block = jax.ShapeDtypeStruct((2, 64, 1024), BF16)
     keep, send, trace = call(

time: 98.6 us -> 96.3 us (0.977)
  the two profiles are of different devices: /device:TPU:1 before, /device:TPU:8 now
where the time goes in v6:
time: 96.3 us; the launch traced here: 96.2 us
  waiting for transfers between devices  45.6 us (47%)
  starting transfers between devices  36.5 us (38%)
  Pallas kernels  9.84 us (10%)
  other arithmetic  2.2 us (2%)
  local copies, waits for them, and re-layouts  1.34 us (1%)
    ppermute x29, waiting for transfers between devices, moved(): lax.ppermute(block, BOTH, [(index_of(*at), index_of(*route(*at))) for at...  45.6 us
    ppermute x29, starting transfers between devices, moved(): lax.ppermute(block, BOTH, [(index_of(*at), index_of(*route(*at))) for at...  36.5 us
    pallas_call x10, Pallas kernels, call(): pl.pallas_call(kernel, out_shape=out_shape, in_specs=[SMEM] + [VMEM] * le...  9.84 us
  transfers between devices with their start and end apart: 29, of which 15 were waited for; matrix products, arithmetic and copies ran while one was open for 2% of the time, Pallas kernels for 9%

profile of v6, /device:TPU:8, one launch (start us, length us, event | category | flops | bytes accessed | tf_op | source)
XLA Modules:
  0.0 96.2 jit_solution(2356995013591628299)
XLA Ops:
  0.6 1.7 %collective-permute-start = (bf16[2,2,64,1024]{3,2,1,0:T(8,128)(2,1)}, bf16[2,2,64,1024]{3,2,1,0:T(8,128)(2,1)S(1)}, u32[]{:S(2)}, u32[]{:S(2)}) collective-permute-start(bf16[2,2,64,1024]{3,2,1,0:T(8,128)(2,1)} %bitcast.16), channel_id=1, source_target_pairs={{0,128},{1,144},{2,130},{3,146},{4,132},{5,148},{6,134},{7,150},{8... | collective-permute-start | bytes 1572872 | tf_op jit(solution)/shard_map/ppermute | solution.py:27
  2.3 8.0 %collective-permute-done.own.refs_2_.refs_0_ = bf16[2,2,64,1024]{3,2,1,0:T(8,128)(2,1)S(1)} collective-permute-done((bf16[2,2,64,1024]{3,2,1,0:T(8,128)(2,1)}, bf16[2,2,64,1024]{3,2,1,0:T(8,128)(2,1)S(1)}, u32[]{:S(2)}, u32[]{:S(2)}) %collective-permute-start) | collective-permute-done | bytes 524320 | tf_op jit(solution)/shard_map/ppermute | solution.py:27
  10.3 0.0 collective-permute-start.3
  10.3 1.8 %collective-permute-start.1 = (bf16[2,2,64,1024]{3,2,1,0:T(8,128)(2,1)S(1)}, bf16[2,2,64,1024]{3,2,1,0:T(8,128)(2,1)S(1)}, u32[]{:S(2)}, u32[]{:S(2)}) collective-permute-start(bf16[2,2,64,1024]{3,2,1,0:T(8,128)(2,1)S(1)} %collective-permute-done.own.refs_2_.refs_0_), channel_id=1, source_target_pairs={{0,2},{1,3},{2,4},{3,5},{4,6},{5,7},{6,8},{7,9},{8,10},{9,11},{10,... | collective-permute-start | bytes 1572872 | tf_op jit(solution)/shard_map/ppermute | solution.py:27
  12.0 0.7 copy-done
  12.7 0.6 slice.9
  13.3 0.0 collective-permute-done.3.other.refs_3_.refs_5_.refs_7_
  13.3 1.9 %collective-permute-start.6 = (bf16[2,2,64,1024]{3,2,1,0:T(8,128)(2,1)S(1)}, bf16[2,2,64,1024]{3,2,1,0:T(8,128)(2,1)S(1)}, u32[]{:S(2)}, u32[]{:S(2)}) collective-permute-start(bf16[2,2,64,1024]{3,2,1,0:T(8,128)(2,1)S(1)} %collective-permute-done.3.other.refs_3_.refs_5_.refs_7_), channel_id=1, source_target_pairs={{0,2},{1,3},{2,4},{3,5},{4,6},{5,7},{6,8},{7,9},{8,10},{9,11},{10,... | collective-permute-start | bytes 1572872 | tf_op jit(solution)/shard_map/ppermute | solution.py:27
  15.2 0.7 pad_add_fusion.info.refs_0_
  15.9 0.6 shard_map.41
  16.5 3.0 %collective-permute-start.4 = (bf16[2,128,1024]{2,1,0:T(8,128)(2,1)S(1)}, bf16[2,128,1024]{2,1,0:T(8,128)(2,1)S(1)}, u32[]{:S(2)}, u32[]{:S(2)}) collective-permute-start(bf16[2,128,1024]{2,1,0:T(8,128)(2,1)S(1)} %shard_map.41), channel_id=1, source_target_pairs={{0,33},{1,0},{2,35},{3,2},{4,37},{5,4},{6,39},{7,6},{8,41},{9,8},{... | collective-permute-start | bytes 1572872 | tf_op jit(solution)/shard_map/ppermute | solution.py:27
  19.5 3.6 %collective-permute-done.1.refs_1_.refs_2_ = bf16[2,2,64,1024]{3,2,1,0:T(8,128)(2,1)S(1)} collective-permute-done((bf16[2,2,64,1024]{3,2,1,0:T(8,128)(2,1)S(1)}, bf16[2,2,64,1024]{3,2,1,0:T(8,128)(2,1)S(1)}, u32[]{:S(2)}, u32[]{:S(2)}) %collective-permute-start.1) | collective-permute-done | bytes 524320 | tf_op jit(solution)/shard_map/ppermute | solution.py:27
  23.1 0.0 collective-permute-start.2
  23.1 2.6 %collective-permute-start.9 = (bf16[2,2,64,1024]{3,2,1,0:T(8,128)(2,1)S(1)}, bf16[2,2,64,1024]{3,2,1,0:T(8,128)(2,1)S(1)}, u32[]{:S(2)}, u32[]{:S(2)}) collective-permute-start(bf16[2,2,64,1024]{3,2,1,0:T(8,128)(2,1)S(1)} %collective-permute-done.1.refs_1_.refs_2_), channel_id=1, source_target_pairs={{0,16},{1,17},{2,18},{3,19},{4,20},{5,21},{6,22},{7,23},{8,24},{9,... | collective-permute-start | bytes 1572872 | tf_op jit(solution)/shard_map/ppermute | solution.py:27
  25.7 3.0 %collective-permute-done.6.refs_4_.refs_6_.refs_8_ = bf16[2,2,64,1024]{3,2,1,0:T(8,128)(2,1)S(1)} collective-permute-done((bf16[2,2,64,1024]{3,2,1,0:T(8,128)(2,1)S(1)}, bf16[2,2,64,1024]{3,2,1,0:T(8,128)(2,1)S(1)}, u32[]{:S(2)}, u32[]{:S(2)}) %collective-permute-start.6) | collective-permute-done | bytes 524320 | tf_op jit(solution)/shard_map/ppermute | solution.py:27
  28.7 0.0 collective-permute-start.8
  28.7 0.6 collective-permute-done.4.refs_1_.a_ref
  29.4 0.9 shard_map.42.refs_10_
  30.2 4.1 %collective-permute-done.2.refs_4_.own.own_2.refs_3_ = bf16[2,2,64,1024]{3,2,1,0:T(8,128)(2,1)S(1)} collective-permute-done((bf16[2,2,64,1024]{3,2,1,0:T(8,128)(2,1)S(1)}, bf16[2,2,64,1024]{3,2,1,0:T(8,128)(2,1)S(1)}, u32[]{:S(2)}, u32[]{:S(2)}) %collective-permute-start.2) | collective-permute-done | bytes 524320 | tf_op jit(solution)/shard_map/ppermute | solution.py:27
  34.4 0.0 collective-permute-start.5
  34.4 2.3 %collective-permute-start.12 = (bf16[2,2,64,1024]{3,2,1,0:T(8,128)(2,1)S(1)}, bf16[2,2,64,1024]{3,2,1,0:T(8,128)(2,1)S(1)}, u32[]{:S(2)}, u32[]{:S(2)}) collective-permute-start(bf16[2,2,64,1024]{3,2,1,0:T(8,128)(2,1)S(1)} %collective-permute-done.2.refs_4_.own.own_2.refs_3_), channel_id=1, source_target_pairs={{0,16},{1,17},{2,18},{3,19},{4,20},{5,21},{6,22},{7,23},{8,24},{9,... | collective-permute-start | bytes 1572872 | tf_op jit(solution)/shard_map/ppermute | solution.py:27
  36.7 0.0 collective-permute-done.9.refs_5_.refs_7_.refs_9_
  36.7 0.0 collective-permute-done.8.refs_2_.refs_3_
  36.7 0.6 shard_map.43
  37.3 2.7 %collective-permute-done.7.refs_8_.other.other_2.refs_10_ = bf16[2,2,64,1024]{3,2,1,0:T(8,128)(2,1)S(1)} collective-permute-done((bf16[2,2,64,1024]{3,2,1,0:T(8,128)(2,1)S(1)}, bf16[2,2,64,1024]{3,2,1,0:T(8,128)(2,1)S(1)}, u32[]{:S(2)}, u32[]{:S(2)}) %collective-permute-start.7) | collective-permute-done | bytes 524320 | tf_op jit(solution)/shard_map/ppermute | solution.py:27
  40.0 0.0 collective-permute-start.11
  40.0 0.0 collective-permute-start.10
  40.0 5.6 %collective-permute-done.5.refs_2_.own_3.refs_5_ = bf16[2,2,64,1024]{3,2,1,0:T(8,128)(2,1)S(1)} collective-permute-done((bf16[2,2,64,1024]{3,2,1,0:T(8,128)(2,1)S(1)}, bf16[2,2,64,1024]{3,2,1,0:T(8,128)(2,1)S(1)}, u32[]{:S(2)}, u32[]{:S(2)}) %collective-permute-start.5) | collective-permute-done | bytes 524320 | tf_op jit(solution)/shard_map/ppermute | solution.py:27
  45.6 2.9 %collective-permute-start.16 = (bf16[3,2,128,128]{3,2,1,0:T(8,128)(2,1)S(1)}, bf16[3,2,128,128]{3,2,1,0:T(8,128)(2,1)S(1)}, u32[]{:S(2)}, u32[]{:S(2)}) collective-permute-start(bf16[3,2,128,128]{3,2,1,0:T(8,128)(2,1)S(1)} %shard_map.43), channel_id=1, source_target_pairs={{0,33},{1,0},{2,35},{3,2},{4,37},{5,4},{6,39},{7,6},{8,41},{9,8},{... | collective-permute-start | bytes 589832 | tf_op jit(solution)/shard_map/ppermute | solution.py:27
  48.5 0.6 shard_map.46
  49.1 3.2 %collective-permute-start.17 = (bf16[2,128,128]{2,1,0:T(8,128)(2,1)S(1)}, bf16[2,128,128]{2,1,0:T(8,128)(2,1)S(1)}, u32[]{:S(2)}, u32[]{:S(2)}) collective-permute-start(bf16[2,128,128]{2,1,0:T(8,128)(2,1)S(1)} %shard_map.46), channel_id=1, source_target_pairs={{0,37},{1,4},{2,39},{3,6},{4,41},{5,8},{6,43},{7,10},{8,45},{9,12}... | collective-permute-start | bytes 196616 | tf_op jit(solution)/shard_map/ppermute | solution.py:27
  52.3 0.0 collective-permute-done.11.refs_5_.refs_4_
  52.3 1.3 %shard_map.44.refs_6_ = f32[256,1024]{1,0:T(8,128)S(1)} custom-call(s32[7]{0:T(128)S(1)} %pad_add_fusion.info.refs_0_, bf16[2,128,1024]{2,1,0:T(8,128)(2,1)S(1)} %collective-permute-done.4.refs_1_.a_ref, bf16[2,2,64,1024]{3,2,1,0:T(8,128)(2,1)S(1)} %collective-permute-done.1.refs_1_.refs_2_, ...), custom_call_target="tpu_custom_call" | custom-call | flops 1 | bytes 1048576 | tf_op jit(solution)/shard_map/pallas_call | solution.py:74
  53.6 0.0 collective-permute-done.10.refs_4_.other_3.refs_12_
  53.6 0.6 shard_map.47
  54.3 3.0 %collective-permute-start.18 = (bf16[2,2,128,128]{3,2,1,0:T(8,128)(2,1)S(1)}, bf16[2,2,128,128]{3,2,1,0:T(8,128)(2,1)S(1)}, u32[]{:S(2)}, u32[]{:S(2)}) collective-permute-start(bf16[2,2,128,128]{3,2,1,0:T(8,128)(2,1)S(1)} %get-tuple-element.36), channel_id=1, source_target_pairs={{0,33},{1,0},{2,35},{3,2},{4,37},{5,4},{6,39},{7,6},{8,41},{9,8},{... | collective-permute-start | bytes 393224 | tf_op jit(solution)/shard_map/ppermute | solution.py:27
  57.3 4.5 %collective-permute-done.17.across = bf16[2,128,128]{2,1,0:T(8,128)(2,1)S(1)} collective-permute-done((bf16[2,128,128]{2,1,0:T(8,128)(2,1)S(1)}, bf16[2,128,128]{2,1,0:T(8,128)(2,1)S(1)}, u32[]{:S(2)}, u32[]{:S(2)}) %collective-permute-start.17) | collective-permute-done | bytes 65568 | tf_op jit(solution)/shard_map/ppermute | solution.py:27
  61.8 0.0 collective-permute-start.14
  61.8 0.0 collective-permute-done.16.near
  61.8 0.5 collective-permute-start.13
  62.3 1.1 %shard_map.48.early = f32[640,256]{1,0:T(8,128)S(1)} custom-call(s32[7]{0:T(128)S(1)} %pad_add_fusion.info.refs_0_, bf16[3,2,128,128]{3,2,1,0:T(8,128)(2,1)S(1)} %collective-permute-done.16.near, bf16[2,128,128]{2,1,0:T(8,128)(2,1)S(1)} %collective-permute-done.17.across, bf16[2,2,64,1024]{3,2,1,0:T(8,128)(2,1)S(1)} %collective-permute-done.own.refs_2_.refs_0_, ...), custom_call_target="tpu_custom_call" | custom-call | flops 1000000000 | bytes 1048576 | tf_op jit(solution)/shard_map/pallas_call | solution.py:74
  63.4 0.1 collective-permute-done.18.here
  63.5 2.6 %collective-permute-done.19.there = bf16[2,2,128,128]{3,2,1,0:T(8,128)(2,1)S(1)} collective-permute-done((bf16[2,2,128,128]{3,2,1,0:T(8,128)(2,1)S(1)}, bf16[2,2,128,128]{3,2,1,0:T(8,128)(2,1)S(1)}, u32[]{:S(2)}, u32[]{:S(2)}) %collective-permute-start.19) | collective-permute-done | bytes 131104 | tf_op jit(solution)/shard_map/ppermute | solution.py:27
  66.2 1.0 %shard_map.45.acc = f32[256,1024]{1,0:T(8,128)S(1)} custom-call(s32[7]{0:T(128)S(1)} %pad_add_fusion.info.refs_0_, bf16[2,128,1024]{2,1,0:T(8,128)(2,1)S(1)} %collective-permute-done.4.refs_1_.a_ref, bf16[2,2,64,1024]{3,2,1,0:T(8,128)(2,1)S(1)} %collective-permute-done.5.refs_2_.own_3.refs_5_, ...), custom_call_target="tpu_custom_call" | custom-call | flops 1 | bytes 1048576 | tf_op jit(solution)/shard_map/pallas_call | solution.py:74
  67.2 1.6 %shard_map.49.early = bf16[1024,256]{1,0:T(8,128)(2,1)S(1)} custom-call(s32[7]{0:T(128)S(1)} %pad_add_fusion.info.refs_0_, bf16[3,2,128,128]{3,2,1,0:T(8,128)(2,1)S(1)} %collective-permute-done.16.near, bf16[2,128,128]{2,1,0:T(8,128)(2,1)S(1)} %collective-permute-done.17.across, bf16[2,2,128,128]{3,2,1,0:T(8,128)(2,1)S(1)} %collective-permute-done.18.here, ...), custom_call_target="tpu_custom_call" | custom-call | flops 1 | bytes 1048576 | tf_op jit(solution)/shard_map/pallas_call | solution.py:74
  68.7 0.0 collective-permute-done.20.other
  68.7 1.7 %shard_map.50 = (bf16[2,64,1024]{2,1,0:T(8,128)(2,1)S(1)}, bf16[2,64,1024]{2,1,0:T(8,128)(2,1)S(1)}, f32[1,128]{1,0:T(1,128)S(1)}) custom-call(s32[7]{0:T(128)S(1)} %pad_add_fusion.info.refs_0_, bf16[2,128,1024]{2,1,0:T(8,128)(2,1)S(1)} %collective-permute-done.4.refs_1_.a_ref, f32[256,1024]{1,0:T(8,128)S(1)} %shard_map.45.acc, ...), custom_call_target="tpu_custom_call" | custom-call | flops 1 | bytes 1048576 | tf_op jit(solution)/shard_map/pallas_call | solution.py:74
  70.4 1.8 %collective-permute-start.22 = (f32[1,128]{1,0:T(1,128)S(1)}, f32[1,128]{1,0:T(1,128)S(1)}, u32[]{:S(2)}, u32[]{:S(2)}) collective-permute-start(f32[1,128]{1,0:T(1,128)S(1)} %get-tuple-element.44), channel_id=1, source_target_pairs={{0,2},{1,3},{2,4},{3,5},{4,6},{5,7},{6,8},{7,9},{8,10},{9,11},{10,... | collective-permute-start | bytes 1544 | tf_op jit(solution)/shard_map/ppermute | solution.py:27
  72.2 1.5 %collective-permute-start.21 = (f32[1,128]{1,0:T(1,128)S(1)}, f32[1,128]{1,0:T(1,128)S(1)}, u32[]{:S(2)}, u32[]{:S(2)}) collective-permute-start(f32[1,128]{1,0:T(1,128)S(1)} %get-tuple-element.44), channel_id=1, source_target_pairs={{0,14},{1,15},{2,0},{3,1},{4,2},{5,3},{6,4},{7,5},{8,6},{9,7},{10,... | collective-permute-start | bytes 1544 | tf_op jit(solution)/shard_map/ppermute | solution.py:27
  73.7 0.6 collective-permute-start.25
  74.3 1.5 %collective-permute-start.26 = (bf16[2,64,1024]{2,1,0:T(8,128)(2,1)S(1)}, bf16[2,64,1024]{2,1,0:T(8,128)(2,1)S(1)}, u32[]{:S(2)}, u32[]{:S(2)}) collective-permute-start(bf16[2,64,1024]{2,1,0:T(8,128)(2,1)S(1)} %get-tuple-element.48), channel_id=1, source_target_pairs={{0,129},{1,113},{2,131},{3,115},{4,133},{5,117},{6,135},{7,119},{8... | collective-permute-start | bytes 786440 | tf_op jit(solution)/shard_map/ppermute | solution.py:27
  75.8 0.0 collective-permute-done.22
  75.8 2.5 %collective-permute-start.23 = (f32[1,128]{1,0:T(1,128)S(1)}, f32[1,128]{1,0:T(1,128)S(1)}, u32[]{:S(2)}, u32[]{:S(2)}) collective-permute-start(f32[1,128]{1,0:T(1,128)S(1)} %get-tuple-element.45), channel_id=1, source_target_pairs={{0,6},{1,7},{2,8},{3,9},{4,10},{5,11},{6,12},{7,13},{8,14},{9,15},... | collective-permute-start | bytes 1544 | tf_op jit(solution)/shard_map/ppermute | solution.py:27
  78.3 2.6 %collective-permute-start.24 = (f32[1,128]{1,0:T(1,128)S(1)}, f32[1,128]{1,0:T(1,128)S(1)}, u32[]{:S(2)}, u32[]{:S(2)}) collective-permute-start(f32[1,128]{1,0:T(1,128)S(1)} %get-tuple-element.46), channel_id=1, source_target_pairs={{0,10},{1,11},{2,12},{3,13},{4,14},{5,15},{6,0},{7,1},{8,2},{9,3},... | collective-permute-start | bytes 1544 | tf_op jit(solution)/shard_map/ppermute | solution.py:27
  80.9 1.5 %collective-permute-done.23 = f32[1,128]{1,0:T(1,128)S(1)} collective-permute-done((f32[1,128]{1,0:T(1,128)S(1)}, f32[1,128]{1,0:T(1,128)S(1)}, u32[]{:S(2)}, u32[]{:S(2)}) %collective-permute-start.23) | collective-permute-done | bytes 544 | tf_op jit(solution)/shard_map/ppermute | solution.py:27
  82.4 1.2 %collective-permute-done.24 = f32[1,128]{1,0:T(1,128)S(1)} collective-permute-done((f32[1,128]{1,0:T(1,128)S(1)}, f32[1,128]{1,0:T(1,128)S(1)}, u32[]{:S(2)}, u32[]{:S(2)}) %collective-permute-start.24) | collective-permute-done | bytes 544 | tf_op jit(solution)/shard_map/ppermute | solution.py:27
  83.6 5.3 %collective-permute-done.26 = bf16[2,64,1024]{2,1,0:T(8,128)(2,1)S(1)} collective-permute-done((bf16[2,64,1024]{2,1,0:T(8,128)(2,1)S(1)}, bf16[2,64,1024]{2,1,0:T(8,128)(2,1)S(1)}, u32[]{:S(2)}, u32[]{:S(2)}) %collective-permute-start.26) | collective-permute-done | bytes 262176 | tf_op jit(solution)/shard_map/ppermute | solution.py:27
  88.9 3.1 %collective-permute-start.28 = (f32[1,128]{1,0:T(1,128)S(1)}, f32[1,128]{1,0:T(1,128)S(1)}, u32[]{:S(2)}, u32[]{:S(2)}) collective-permute-start(f32[1,128]{1,0:T(1,128)S(1)} %add_add_fusion), channel_id=1, source_target_pairs={{0,129},{1,113},{2,131},{3,115},{4,133},{5,117},{6,135},{7,119},{8... | collective-permute-start | bytes 1544 | tf_op jit(solution)/shard_map/ppermute | solution.py:27
  92.0 0.0 collective-permute-start.27
  92.0 0.9 maximum_select_fusion
  92.8 0.4 collective-permute-done.28
  93.3 2.2 %collective-permute-done.27 = f32[1,128]{1,0:T(1,128)S(1)} collective-permute-done((f32[1,128]{1,0:T(1,128)S(1)}, f32[1,128]{1,0:T(1,128)S(1)}, u32[]{:S(2)}, u32[]{:S(2)}) %collective-permute-start.27) | collective-permute-done | bytes 544 | tf_op jit(solution)/shard_map/ppermute | solution.py:27
  95.5 0.1 reshape.79
  95.6 0.6 broadcast_multiply_fusion
  (16 shorter events, 0.1 us)
Async XLA Ops:
  0.6 9.6 %collective-permute-start = (bf16[2,2,64,1024]{3,2,1,0:T(8,128)(2,1)}, bf16[2,2,64,1024]{3,2,1,0:T(8,128)(2,1)S(1)}, u32[]{:S(2)}, u32[]{:S(2)}) collective-permute-start(bf16[2,2,64,1024]{3,2,1,0:T(8,128)(2,1)} %bitcast.16), channel_id=1, source_target_pairs={{0,128},{1,144},{2,130},{3,146},{4,132},{5,148},{6,134},{7,150},{8... | collective-permute-start | bytes 1572872 | tf_op jit(solution)/shard_map/ppermute | solution.py:27
  10.3 3.0 %collective-permute-start.3 = (bf16[2,2,64,1024]{3,2,1,0:T(8,128)(2,1)S(1)}, bf16[2,2,64,1024]{3,2,1,0:T(8,128)(2,1)S(1)}, u32[]{:S(2)}, u32[]{:S(2)}) collective-permute-start(bf16[2,2,64,1024]{3,2,1,0:T(8,128)(2,1)S(1)} %collective-permute-done.own.refs_2_.refs_0_), channel_id=1, source_target_pairs={{0,16},{1,17},{2,18},{3,19},{4,20},{5,21},{6,22},{7,23},{8,24},{9,... | collective-permute-start | bytes 1572872 | tf_op jit(solution)/shard_map/ppermute | solution.py:27
  10.3 12.8 %collective-permute-start.1 = (bf16[2,2,64,1024]{3,2,1,0:T(8,128)(2,1)S(1)}, bf16[2,2,64,1024]{3,2,1,0:T(8,128)(2,1)S(1)}, u32[]{:S(2)}, u32[]{:S(2)}) collective-permute-start(bf16[2,2,64,1024]{3,2,1,0:T(8,128)(2,1)S(1)} %collective-permute-done.own.refs_2_.refs_0_), channel_id=1, source_target_pairs={{0,2},{1,3},{2,4},{3,5},{4,6},{5,7},{6,8},{7,9},{8,10},{9,11},{10,... | collective-permute-start | bytes 1572872 | tf_op jit(solution)/shard_map/ppermute | solution.py:27
  12.0 0.7 copy-start
  13.3 15.4 %collective-permute-start.6 = (bf16[2,2,64,1024]{3,2,1,0:T(8,128)(2,1)S(1)}, bf16[2,2,64,1024]{3,2,1,0:T(8,128)(2,1)S(1)}, u32[]{:S(2)}, u32[]{:S(2)}) collective-permute-start(bf16[2,2,64,1024]{3,2,1,0:T(8,128)(2,1)S(1)} %collective-permute-done.3.other.refs_3_.refs_5_.refs_7_), channel_id=1, source_target_pairs={{0,2},{1,3},{2,4},{3,5},{4,6},{5,7},{6,8},{7,9},{8,10},{9,11},{10,... | collective-permute-start | bytes 1572872 | tf_op jit(solution)/shard_map/ppermute | solution.py:27
  16.5 12.8 %collective-permute-start.4 = (bf16[2,128,1024]{2,1,0:T(8,128)(2,1)S(1)}, bf16[2,128,1024]{2,1,0:T(8,128)(2,1)S(1)}, u32[]{:S(2)}, u32[]{:S(2)}) collective-permute-start(bf16[2,128,1024]{2,1,0:T(8,128)(2,1)S(1)} %shard_map.41), channel_id=1, source_target_pairs={{0,33},{1,0},{2,35},{3,2},{4,37},{5,4},{6,39},{7,6},{8,41},{9,8},{... | collective-permute-start | bytes 1572872 | tf_op jit(solution)/shard_map/ppermute | solution.py:27
  23.1 11.2 %collective-permute-start.2 = (bf16[2,2,64,1024]{3,2,1,0:T(8,128)(2,1)S(1)}, bf16[2,2,64,1024]{3,2,1,0:T(8,128)(2,1)S(1)}, u32[]{:S(2)}, u32[]{:S(2)}) collective-permute-start(bf16[2,2,64,1024]{3,2,1,0:T(8,128)(2,1)S(1)} %collective-permute-done.1.refs_1_.refs_2_), channel_id=1, source_target_pairs={{0,2},{1,3},{2,4},{3,5},{4,6},{5,7},{6,8},{7,9},{8,10},{9,11},{10,... | collective-permute-start | bytes 1572872 | tf_op jit(solution)/shard_map/ppermute | solution.py:27
  23.1 13.5 %collective-permute-start.9 = (bf16[2,2,64,1024]{3,2,1,0:T(8,128)(2,1)S(1)}, bf16[2,2,64,1024]{3,2,1,0:T(8,128)(2,1)S(1)}, u32[]{:S(2)}, u32[]{:S(2)}) collective-permute-start(bf16[2,2,64,1024]{3,2,1,0:T(8,128)(2,1)S(1)} %collective-permute-done.1.refs_1_.refs_2_), channel_id=1, source_target_pairs={{0,16},{1,17},{2,18},{3,19},{4,20},{5,21},{6,22},{7,23},{8,24},{9,... | collective-permute-start | bytes 1572872 | tf_op jit(solution)/shard_map/ppermute | solution.py:27
  28.7 7.9 %collective-permute-start.8 = (bf16[2,2,64,1024]{3,2,1,0:T(8,128)(2,1)S(1)}, bf16[2,2,64,1024]{3,2,1,0:T(8,128)(2,1)S(1)}, u32[]{:S(2)}, u32[]{:S(2)}) collective-permute-start(bf16[2,2,64,1024]{3,2,1,0:T(8,128)(2,1)S(1)} %collective-permute-done.6.refs_4_.refs_6_.refs_8_), channel_id=1, source_target_pairs={{0,16},{1,17},{2,18},{3,19},{4,20},{5,21},{6,22},{7,23},{8,24},{9,... | collective-permute-start | bytes 1572872 | tf_op jit(solution)/shard_map/ppermute | solution.py:27
  28.7 11.2 %collective-permute-start.7 = (bf16[2,2,64,1024]{3,2,1,0:T(8,128)(2,1)S(1)}, bf16[2,2,64,1024]{3,2,1,0:T(8,128)(2,1)S(1)}, u32[]{:S(2)}, u32[]{:S(2)}) collective-permute-start(bf16[2,2,64,1024]{3,2,1,0:T(8,128)(2,1)S(1)} %collective-permute-done.6.refs_4_.refs_6_.refs_8_), channel_id=1, source_target_pairs={{0,2},{1,3},{2,4},{3,5},{4,6},{5,7},{6,8},{7,9},{8,10},{9,11},{10,... | collective-permute-start | bytes 1572872 | tf_op jit(solution)/shard_map/ppermute | solution.py:27
  34.4 11.2 %collective-permute-start.5 = (bf16[2,2,64,1024]{3,2,1,0:T(8,128)(2,1)S(1)}, bf16[2,2,64,1024]{3,2,1,0:T(8,128)(2,1)S(1)}, u32[]{:S(2)}, u32[]{:S(2)}) collective-permute-start(bf16[2,2,64,1024]{3,2,1,0:T(8,128)(2,1)S(1)} %collective-permute-done.2.refs_4_.own.own_2.refs_3_), channel_id=1, source_target_pairs={{0,2},{1,3},{2,4},{3,5},{4,6},{5,7},{6,8},{7,9},{8,10},{9,11},{10,... | collective-permute-start | bytes 1572872 | tf_op jit(solution)/shard_map/ppermute | solution.py:27
  34.4 14.7 %collective-permute-start.12 = (bf16[2,2,64,1024]{3,2,1,0:T(8,128)(2,1)S(1)}, bf16[2,2,64,1024]{3,2,1,0:T(8,128)(2,1)S(1)}, u32[]{:S(2)}, u32[]{:S(2)}) collective-permute-start(bf16[2,2,64,1024]{3,2,1,0:T(8,128)(2,1)S(1)} %collective-permute-done.2.refs_4_.own.own_2.refs_3_), channel_id=1, source_target_pairs={{0,16},{1,17},{2,18},{3,19},{4,20},{5,21},{6,22},{7,23},{8,24},{9,... | collective-permute-start | bytes 1572872 | tf_op jit(solution)/shard_map/ppermute | solution.py:27
  40.0 12.4 %collective-permute-start.11 = (bf16[2,2,64,1024]{3,2,1,0:T(8,128)(2,1)S(1)}, bf16[2,2,64,1024]{3,2,1,0:T(8,128)(2,1)S(1)}, u32[]{:S(2)}, u32[]{:S(2)}) collective-permute-start(bf16[2,2,64,1024]{3,2,1,0:T(8,128)(2,1)S(1)} %collective-permute-done.7.refs_8_.other.other_2.refs_10_), channel_id=1, source_target_pairs={{0,16},{1,17},{2,18},{3,19},{4,20},{5,21},{6,22},{7,23},{8,24},{9,... | collective-permute-start | bytes 1572872 | tf_op jit(solution)/shard_map/ppermute | solution.py:27
  40.0 13.7 %collective-permute-start.10 = (bf16[2,2,64,1024]{3,2,1,0:T(8,128)(2,1)S(1)}, bf16[2,2,64,1024]{3,2,1,0:T(8,128)(2,1)S(1)}, u32[]{:S(2)}, u32[]{:S(2)}) collective-permute-start(bf16[2,2,64,1024]{3,2,1,0:T(8,128)(2,1)S(1)} %collective-permute-done.7.refs_8_.other.other_2.refs_10_), channel_id=1, source_target_pairs={{0,2},{1,3},{2,4},{3,5},{4,6},{5,7},{6,8},{7,9},{8,10},{9,11},{10,... | collective-permute-start | bytes 1572872 | tf_op jit(solution)/shard_map/ppermute | solution.py:27
  45.6 17.8 %collective-permute-start.15 = (bf16[2,2,64,1024]{3,2,1,0:T(8,128)(2,1)S(1)}, bf16[2,2,64,1024]{3,2,1,0:T(8,128)(2,1)S(1)}, u32[]{:S(2)}, u32[]{:S(2)}) collective-permute-start(bf16[2,2,64,1024]{3,2,1,0:T(8,128)(2,1)S(1)} %collective-permute-done.5.refs_2_.own_3.refs_5_), channel_id=1, source_target_pairs={{0,2},{1,3},{2,4},{3,5},{4,6},{5,7},{6,8},{7,9},{8,10},{9,11},{10,... | collective-permute-start | bytes 1572872 | tf_op jit(solution)/shard_map/ppermute | solution.py:27
  45.6 16.2 %collective-permute-start.16 = (bf16[3,2,128,128]{3,2,1,0:T(8,128)(2,1)S(1)}, bf16[3,2,128,128]{3,2,1,0:T(8,128)(2,1)S(1)}, u32[]{:S(2)}, u32[]{:S(2)}) collective-permute-start(bf16[3,2,128,128]{3,2,1,0:T(8,128)(2,1)S(1)} %shard_map.43), channel_id=1, source_target_pairs={{0,33},{1,0},{2,35},{3,2},{4,37},{5,4},{6,39},{7,6},{8,41},{9,8},{... | collective-permute-start | bytes 589832 | tf_op jit(solution)/shard_map/ppermute | solution.py:27
  49.1 12.7 %collective-permute-start.17 = (bf16[2,128,128]{2,1,0:T(8,128)(2,1)S(1)}, bf16[2,128,128]{2,1,0:T(8,128)(2,1)S(1)}, u32[]{:S(2)}, u32[]{:S(2)}) collective-permute-start(bf16[2,128,128]{2,1,0:T(8,128)(2,1)S(1)} %shard_map.46), channel_id=1, source_target_pairs={{0,37},{1,4},{2,39},{3,6},{4,41},{5,8},{6,43},{7,10},{8,45},{9,12}... | collective-permute-start | bytes 196616 | tf_op jit(solution)/shard_map/ppermute | solution.py:27
  54.3 9.3 %collective-permute-start.18 = (bf16[2,2,128,128]{3,2,1,0:T(8,128)(2,1)S(1)}, bf16[2,2,128,128]{3,2,1,0:T(8,128)(2,1)S(1)}, u32[]{:S(2)}, u32[]{:S(2)}) collective-permute-start(bf16[2,2,128,128]{3,2,1,0:T(8,128)(2,1)S(1)} %get-tuple-element.36), channel_id=1, source_target_pairs={{0,33},{1,0},{2,35},{3,2},{4,37},{5,4},{6,39},{7,6},{8,41},{9,8},{... | collective-permute-start | bytes 393224 | tf_op jit(solution)/shard_map/ppermute | solution.py:27
  57.3 8.9 %collective-permute-start.19 = (bf16[2,2,128,128]{3,2,1,0:T(8,128)(2,1)S(1)}, bf16[2,2,128,128]{3,2,1,0:T(8,128)(2,1)S(1)}, u32[]{:S(2)}, u32[]{:S(2)}) collective-permute-start(bf16[2,2,128,128]{3,2,1,0:T(8,128)(2,1)S(1)} %get-tuple-element.37), channel_id=1, source_target_pairs={{0,48},{1,49},{2,50},{3,51},{4,52},{5,53},{6,54},{7,55},{8,56},{9,... | collective-permute-start | bytes 393224 | tf_op jit(solution)/shard_map/ppermute | solution.py:27
  61.8 4.4 %collective-permute-start.14 = (bf16[2,2,64,1024]{3,2,1,0:T(8,128)(2,1)S(1)}, bf16[2,2,64,1024]{3,2,1,0:T(8,128)(2,1)S(1)}, u32[]{:S(2)}, u32[]{:S(2)}) collective-permute-start(bf16[2,2,64,1024]{3,2,1,0:T(8,128)(2,1)S(1)} %collective-permute-done.5.refs_2_.own_3.refs_5_), channel_id=1, source_target_pairs={{0,16},{1,17},{2,18},{3,19},{4,20},{5,21},{6,22},{7,23},{8,24},{9,... | collective-permute-start | bytes 1572872 | tf_op jit(solution)/shard_map/ppermute | solution.py:27
  61.8 4.4 %collective-permute-start.13 = (bf16[2,2,64,1024]{3,2,1,0:T(8,128)(2,1)S(1)}, bf16[2,2,64,1024]{3,2,1,0:T(8,128)(2,1)S(1)}, u32[]{:S(2)}, u32[]{:S(2)}) collective-permute-start(bf16[2,2,64,1024]{3,2,1,0:T(8,128)(2,1)S(1)} %collective-permute-done.10.refs_4_.other_3.refs_12_), channel_id=1, source_target_pairs={{0,16},{1,17},{2,18},{3,19},{4,20},{5,21},{6,22},{7,23},{8,24},{9,... | collective-permute-start | bytes 1572872 | tf_op jit(solution)/shard_map/ppermute | solution.py:27
  66.1 2.6 %collective-permute-start.20 = (bf16[2,2,64,1024]{3,2,1,0:T(8,128)(2,1)S(1)}, bf16[2,2,64,1024]{3,2,1,0:T(8,128)(2,1)S(1)}, u32[]{:S(2)}, u32[]{:S(2)}) collective-permute-start(bf16[2,2,64,1024]{3,2,1,0:T(8,128)(2,1)S(1)} %collective-permute-done.15.own), channel_id=1, source_target_pairs={{0,16},{1,17},{2,18},{3,19},{4,20},{5,21},{6,22},{7,23},{8,24},{9,... | collective-permute-start | bytes 1572872 | tf_op jit(solution)/shard_map/ppermute | solution.py:27
  70.4 5.4 %collective-permute-start.22 = (f32[1,128]{1,0:T(1,128)S(1)}, f32[1,128]{1,0:T(1,128)S(1)}, u32[]{:S(2)}, u32[]{:S(2)}) collective-permute-start(f32[1,128]{1,0:T(1,128)S(1)} %get-tuple-element.44), channel_id=1, source_target_pairs={{0,2},{1,3},{2,4},{3,5},{4,6},{5,7},{6,8},{7,9},{8,10},{9,11},{10,... | collective-permute-start | bytes 1544 | tf_op jit(solution)/shard_map/ppermute | solution.py:27
  72.2 3.6 %collective-permute-start.21 = (f32[1,128]{1,0:T(1,128)S(1)}, f32[1,128]{1,0:T(1,128)S(1)}, u32[]{:S(2)}, u32[]{:S(2)}) collective-permute-start(f32[1,128]{1,0:T(1,128)S(1)} %get-tuple-element.44), channel_id=1, source_target_pairs={{0,14},{1,15},{2,0},{3,1},{4,2},{5,3},{6,4},{7,5},{8,6},{9,7},{10,... | collective-permute-start | bytes 1544 | tf_op jit(solution)/shard_map/ppermute | solution.py:27
  73.7 10.0 %collective-permute-start.25 = (bf16[2,64,1024]{2,1,0:T(8,128)(2,1)S(1)}, bf16[2,64,1024]{2,1,0:T(8,128)(2,1)S(1)}, u32[]{:S(2)}, u32[]{:S(2)}) collective-permute-start(bf16[2,64,1024]{2,1,0:T(8,128)(2,1)S(1)} %get-tuple-element.47), channel_id=1, source_target_pairs={{0,128},{1,112},{2,130},{3,114},{4,132},{5,116},{6,134},{7,118},{8... | collective-permute-start | bytes 786440 | tf_op jit(solution)/shard_map/ppermute | solution.py:27
  74.3 14.6 %collective-permute-start.26 = (bf16[2,64,1024]{2,1,0:T(8,128)(2,1)S(1)}, bf16[2,64,1024]{2,1,0:T(8,128)(2,1)S(1)}, u32[]{:S(2)}, u32[]{:S(2)}) collective-permute-start(bf16[2,64,1024]{2,1,0:T(8,128)(2,1)S(1)} %get-tuple-element.48), channel_id=1, source_target_pairs={{0,129},{1,113},{2,131},{3,115},{4,133},{5,117},{6,135},{7,119},{8... | collective-permute-start | bytes 786440 | tf_op jit(solution)/shard_map/ppermute | solution.py:27
  75.8 6.6 %collective-permute-start.23 = (f32[1,128]{1,0:T(1,128)S(1)}, f32[1,128]{1,0:T(1,128)S(1)}, u32[]{:S(2)}, u32[]{:S(2)}) collective-permute-start(f32[1,128]{1,0:T(1,128)S(1)} %get-tuple-element.45), channel_id=1, source_target_pairs={{0,6},{1,7},{2,8},{3,9},{4,10},{5,11},{6,12},{7,13},{8,14},{9,15},... | collective-permute-start | bytes 1544 | tf_op jit(solution)/shard_map/ppermute | solution.py:27
  78.3 5.3 %collective-permute-start.24 = (f32[1,128]{1,0:T(1,128)S(1)}, f32[1,128]{1,0:T(1,128)S(1)}, u32[]{:S(2)}, u32[]{:S(2)}) collective-permute-start(f32[1,128]{1,0:T(1,128)S(1)} %get-tuple-element.46), channel_id=1, source_target_pairs={{0,10},{1,11},{2,12},{3,13},{4,14},{5,15},{6,0},{7,1},{8,2},{9,3},... | collective-permute-start | bytes 1544 | tf_op jit(solution)/shard_map/ppermute | solution.py:27
  88.9 4.4 %collective-permute-start.28 = (f32[1,128]{1,0:T(1,128)S(1)}, f32[1,128]{1,0:T(1,128)S(1)}, u32[]{:S(2)}, u32[]{:S(2)}) collective-permute-start(f32[1,128]{1,0:T(1,128)S(1)} %add_add_fusion), channel_id=1, source_target_pairs={{0,129},{1,113},{2,131},{3,115},{4,133},{5,117},{6,135},{7,119},{8... | collective-permute-start | bytes 1544 | tf_op jit(solution)/shard_map/ppermute | solution.py:27
  92.0 3.5 %collective-permute-start.27 = (f32[1,128]{1,0:T(1,128)S(1)}, f32[1,128]{1,0:T(1,128)S(1)}, u32[]{:S(2)}, u32[]{:S(2)}) collective-permute-start(f32[1,128]{1,0:T(1,128)S(1)} %add_add_fusion), channel_id=1, source_target_pairs={{0,128},{1,112},{2,130},{3,114},{4,132},{5,116},{6,134},{7,118},{8... | collective-permute-start | bytes 1544 | tf_op jit(solution)/shard_map/ppermute | solution.py:27

commit v7 on v3

--- a/solution.py
+++ b/solution.py
@@ -39,12 +39,9 @@
     return (m, 1 - c, z, h)
 
 
-def to_hub(step):
-    def route(m, c, z, h):
-        column, half = hub_of(2 * m + c)
-        return (column, h, z + step, half)
-
-    return route
+def to_hub(m, c, z, h):
+    column, half = hub_of(2 * m + c)
+    return (column, h, z, half)
 
 
 def hub_ahead(step):
@@ -62,6 +59,8 @@
 
     return route
 
+
+WEIGHT = 3_000_000_000
 
 VMEM = pl.BlockSpec(memory_space=pltpu.VMEM)
 SMEM = pl.BlockSpec(memory_space=pltpu.SMEM)
@@ -103,8 +102,7 @@
     columns = columns_of(info, offset)
     for part in range(2):
         first, second = halves(info, own_ref[info[5], part, :, columns], other_ref[info[5], part, :, columns])
-        out[part, 0:64] = first
-        out[part, 64:128] = second
+        out[part] = jnp.concatenate([first, second], axis=0).T
 
 
 def first_cut_kernel(info, own, other, a):
@@ -141,50 +139,39 @@
     out[...] = total
 
 
-def crossed_block(real, imag, drhs):
-    block = jnp.dot(real, drhs[0:1024, :], preferred_element_type=F32)
-    block += jnp.dot(imag, drhs[1024:2048, :], preferred_element_type=F32)
-    turned = jnp.concatenate([block[:, :128].T, block[:, 128:].T], axis=0)
-    return turned.astype(BF16)
-
-
 OFFSETS = (0, 1, -1, 2, -2, 3, -3, 4)
 
 
-def crossed_kernel(info, near, late, across, *refs):
-    own, other, drhs, crossed = refs[0:7], refs[7:14], refs[14], refs[15]
-    slices = [near.at[k] for k in range(3)] + [late.at[k] for k in range(4)] + [across]
-    for offset, piece in zip(OFFSETS, slices):
-        top = pl.multiple_of(place_of(info, offset) * 128, 128)
-        real, imag = piece[0], piece[1]
-        drhs[pl.ds(top, 128), 0:128] = real
-        drhs[pl.ds(top, 128), 128:256] = imag
-        drhs[pl.ds(1024 + top, 128), 0:128] = -imag
-        drhs[pl.ds(1024 + top, 128), 128:256] = real
-    for offset, one, two in zip(OFFSETS, own, other):
-        real, imag = (whole(info, one, two, info[4], part) for part in range(2))
-        crossed[:, columns_of(info, offset)] = crossed_block(real, imag, drhs)
-
-
-def last_kernel(info, a_ref, own, other, acc, drhs, crossed, keep, send, trace, turned):
-    def parts(momentum):
-        return [whole(info, own, other, momentum, part) for part in range(2)]
-
-    block = jnp.concatenate(parts(info[3]), axis=0)
+def last_kernel(info, a_ref, acc, *refs):
+    own, other = refs[0:8], refs[8:16]
+    keep, send, out, rounded_ref = refs[16:20]
+    block = jnp.concatenate([whole(info, own[7], other[7], info[3], part) for part in range(2)], axis=0)
     product = acc[...] + jnp.dot(left_side(info, a_ref, 4), block, preferred_element_type=F32)
     rounded = product.astype(BF16)
     for part in range(2):
+        rounded_ref[part] = rounded[part * 128 : part * 128 + 128]
         low, high = rounded[part * 128 : part * 128 + 64], rounded[part * 128 + 64 : part * 128 + 128]
         keep[part], send[part] = halves(info, low, high)
-    real, imag = parts(info[4])
-    turned[...] = crossed[...]
-    turned[:, columns_of(info, 4)] = crossed_block(real, imag, drhs)
-    p_re, p_im = rounded[:128].astype(F32), rounded[128:].astype(F32)
-    c_re, c_im = turned[:128, :].astype(F32), turned[128:, :].astype(F32)
-    re = jnp.sum(p_re * c_re - p_im * c_im, axis=0, keepdims=True)
-    im = jnp.sum(p_re * c_im + p_im * c_re, axis=0, keepdims=True)
-    re = jnp.sum(re, axis=1, keepdims=True)
-    im = jnp.sum(im, axis=1, keepdims=True)
+    total = None
+    for offset, one, two in zip(OFFSETS, own, other):
+        block = jnp.concatenate([whole(info, one, two, info[4], part) for part in range(2)], axis=0)
+        term = jnp.dot(left_side(info, rounded_ref, offset), block, preferred_element_type=F32)
+        total = term if total is None else total + term
+    out[...] = total
+
+
+def trace_kernel(info, product, near, late, across, trace):
+    slices = [near.at[0], near.at[1], near.at[2], late.at[0], late.at[1], late.at[2], late.at[3], across]
+    re = im = None
+    for offset, piece in zip(OFFSETS, slices):
+        columns = columns_of(info, offset)
+        q_re, q_im = product[0:128, columns], product[128:256, columns]
+        d_re, d_im = piece[0].astype(F32), piece[1].astype(F32)
+        more_re, more_im = q_re * d_re - q_im * d_im, q_re * d_im + q_im * d_re
+        re = more_re if re is None else re + more_re
+        im = more_im if im is None else im + more_im
+    re = jnp.sum(jnp.sum(re, axis=0, keepdims=True), axis=1, keepdims=True)
+    im = jnp.sum(jnp.sum(im, axis=0, keepdims=True), axis=1, keepdims=True)
     lane = lax.broadcasted_iota(jnp.int32, (1, 128), 1)
     trace[...] = jnp.where(lane == 2 * info[0], re, jnp.where(lane == 2 * info[0] + 1, im, 0.0))
 
@@ -198,54 +185,56 @@
     wall = lax.optimization_barrier
     block_of_products = jax.ShapeDtypeStruct((256, 1024), F32)
 
-    own = moved(rows, to_hub(0))
-    ownx = moved(own, other_core)
-
-    p1, q1 = moved(own, onward), moved(ownx, onward)
-    a = moved(call(first_cut_kernel, info, [own, ownx], jax.ShapeDtypeStruct((2, 128, 1024), BF16), 1), hub_ahead(0))
+    own = moved(rows, to_hub)
+
+    ownx, p1 = moved(own, other_core), moved(own, onward)
+    q1 = moved(ownx, onward)
+    a = call(first_cut_kernel, info, [own, ownx], jax.ShapeDtypeStruct((2, 128, 1024), BF16), 1)
+    a = moved(a, hub_ahead(0))
 
     p2, p1x = moved(p1, onward), moved(p1, other_core)
     q2, q1x = moved(q1, onward), moved(q1, other_core)
-    first_three = [own, p1, q1x, ownx, q1, p1x]
-    near = call(cut_kernel, info, first_three, jax.ShapeDtypeStruct((3, 2, 128, 128), BF16), 1)
-    near = moved(near, hub_ahead(0))
-    p2, a = wall((p2, a))
+    three, three_x = [own, p1, q1x], [ownx, q1, p1x]
+    near = call(cut_kernel, info, three + three_x, jax.ShapeDtypeStruct((3, 2, 128, 128), BF16), 1)
+    acc = call(lambda *refs: products_kernel(OFFSETS[:1], *refs), info, [a, own, ownx], block_of_products, WEIGHT)
+    p2, a, acc = wall((p2, a, acc))
+    q2, near = wall((q2, near))
 
     p3, p2x = moved(p2, onward), moved(p2, other_core)
     q3, q2x = moved(q2, onward), moved(q2, other_core)
-    across = moved(call(across_kernel, info, [p2, q2], SLICES, 1), hub_ahead(2))
+    across = call(across_kernel, info, [p2, q2], SLICES, 1)
+    five, five_x = three + [p2, q2x], three_x + [q2, p2x]
     acc = call(
-        lambda *refs: products_kernel(OFFSETS[:3], *refs), info, [a] + first_three, block_of_products, 1
+        lambda *refs: products_kernel(OFFSETS[1:5], *refs), info, [a] + five[1:] + five_x[1:] + [acc], block_of_products, 1
     )
     p3, near = wall((p3, near))
 
+    near = moved(near, hub_ahead(0))
     p4, p3x = moved(p3, onward), moved(p3, other_core)
+    q3, acc = wall((q3, acc))
+
     q3x = moved(q3, other_core)
-    next_four = [p2, q2x, p3, q3x, q2, p2x, q3, p3x]
-    late = call(cut_kernel, info, next_four, jax.ShapeDtypeStruct((4, 2, 128, 128), BF16), 1)
+    p4, near, across = wall((p4, near, across))
+
+    p4x = moved(p4, other_core)
+    across = moved(across, hub_ahead(2))
+    two, two_x = [p3, q3x], [q3, p3x]
+    four, four_x = five[3:] + two, five_x[3:] + two_x
+    late = call(cut_kernel, info, four + four_x, jax.ShapeDtypeStruct((4, 2, 128, 128), BF16), 1)
     late = moved(late, hub_ahead(0))
     acc = call(
-        lambda *refs: products_kernel(OFFSETS[3:7], *refs), info, [a] + next_four + [acc], block_of_products, 1
-    )
-    p4, across, acc, late = wall((p4, across, acc, late))
-
-    p4x = moved(p4, other_core)
-    drhs, crossed = call(
-        crossed_kernel,
-        info,
-        [near, late, across] + first_three[:3] + next_four[:4] + first_three[3:] + next_four[4:],
-        (jax.ShapeDtypeStruct((2048, 256), BF16), jax.ShapeDtypeStruct((256, 1024), BF16)),
-        1,
+        lambda *refs: products_kernel(OFFSETS[5:7], *refs), info, [a] + two + two_x + [acc], block_of_products, 1
     )
     half_block = jax.ShapeDtypeStruct((2, 64, 1024), BF16)
-    keep, send, trace = call(
+    keep, send, product = call(
         last_kernel,
         info,
-        [a, p4, p4x, acc, drhs, crossed],
-        (half_block, half_block, jax.ShapeDtypeStruct((1, 128), F32)),
-        1,
-        [pltpu.VMEM((256, 1024), BF16)],
-    )
+        [a, acc] + five + two + [p4] + five_x + two_x + [p4x],
+        (half_block, half_block, block_of_products),
+        WEIGHT,
+        [pltpu.VMEM((2, 128, 1024), BF16)],
+    )
+    trace = call(trace_kernel, info, [product, near, late, across], jax.ShapeDtypeStruct((1, 128), F32), 1)
 
     below, above = moved(trace, along(1)), moved(trace, along(-1))
     kept, sent = moved(keep, from_hub(0)), moved(send, from_hub(1))

time: 97.5 us -> 98.2 us (level)
  the two profiles are of different devices: /device:TPU:8 before, /device:TPU:1 now
where the time goes in v7:
time: 98.2 us; the launch traced here: 96.6 us
  starting transfers between devices  57 us (58%)
  waiting for transfers between devices  28.3 us (29%)
  Pallas kernels  8.85 us (9%)
  other arithmetic  1.55 us (2%)
    ppermute x28, starting transfers between devices, moved(): lax.ppermute(block, BOTH, [(index_of(*at), index_of(*route(*at))) for at...  57 us
    ppermute x28, waiting for transfers between devices, moved(): lax.ppermute(block, BOTH, [(index_of(*at), index_of(*route(*at))) for at...  28.3 us
    pallas_call x9, Pallas kernels, call(): pl.pallas_call(kernel, out_shape=out_shape, in_specs=[SMEM] + [VMEM] * le...  8.85 us
  transfers between devices with their start and end apart: 28, of which 12 were waited for; matrix products, arithmetic and copies ran while one was open for 1% of the time, Pallas kernels for 8%

profile of v7, /device:TPU:1, one launch (start us, length us, event | category | flops | bytes accessed | tf_op | source)
XLA Modules:
  0.0 96.6 jit_solution(3562598670005843353)
XLA Ops:
  0.6 0.0 copy-start
  0.6 4.2 %collective-permute-start = (bf16[2,2,64,1024]{3,2,1,0:T(8,128)(2,1)}, bf16[2,2,64,1024]{3,2,1,0:T(8,128)(2,1)S(1)}, u32[]{:S(2)}, u32[]{:S(2)}) collective-permute-start(bf16[2,2,64,1024]{3,2,1,0:T(8,128)(2,1)} %bitcast.15), channel_id=1, source_target_pairs={{0,128},{1,144},{2,130},{3,146},{4,132},{5,148},{6,134},{7,150},{8... | collective-permute-start | bytes 1572872 | tf_op jit(solution)/shard_map/ppermute | solution.py:27
  4.8 6.4 %collective-permute-done.own.refs_2_.refs_0_ = bf16[2,2,64,1024]{3,2,1,0:T(8,128)(2,1)S(1)} collective-permute-done((bf16[2,2,64,1024]{3,2,1,0:T(8,128)(2,1)}, bf16[2,2,64,1024]{3,2,1,0:T(8,128)(2,1)S(1)}, u32[]{:S(2)}, u32[]{:S(2)}) %collective-permute-start) | collective-permute-done | bytes 524320 | tf_op jit(solution)/shard_map/ppermute | solution.py:27
  11.3 1.5 %collective-permute-start.3 = (bf16[2,2,64,1024]{3,2,1,0:T(8,128)(2,1)S(1)}, bf16[2,2,64,1024]{3,2,1,0:T(8,128)(2,1)S(1)}, u32[]{:S(2)}, u32[]{:S(2)}) collective-permute-start(bf16[2,2,64,1024]{3,2,1,0:T(8,128)(2,1)S(1)} %collective-permute-done.own.refs_2_.refs_0_), channel_id=1, source_target_pairs={{0,16},{1,17},{2,18},{3,19},{4,20},{5,21},{6,22},{7,23},{8,24},{9,... | collective-permute-start | bytes 1572872 | tf_op jit(solution)/shard_map/ppermute | solution.py:27
  12.8 4.1 %collective-permute-start.1 = (bf16[2,2,64,1024]{3,2,1,0:T(8,128)(2,1)S(1)}, bf16[2,2,64,1024]{3,2,1,0:T(8,128)(2,1)S(1)}, u32[]{:S(2)}, u32[]{:S(2)}) collective-permute-start(bf16[2,2,64,1024]{3,2,1,0:T(8,128)(2,1)S(1)} %collective-permute-done.own.refs_2_.refs_0_), channel_id=1, source_target_pairs={{0,2},{1,3},{2,4},{3,5},{4,6},{5,7},{6,8},{7,9},{8,10},{9,11},{10,... | collective-permute-start | bytes 1572872 | tf_op jit(solution)/shard_map/ppermute | solution.py:27
  16.9 0.0 collective-permute-done.3.other.refs_3_.refs_8_
  16.9 1.9 %collective-permute-start.6 = (bf16[2,2,64,1024]{3,2,1,0:T(8,128)(2,1)S(1)}, bf16[2,2,64,1024]{3,2,1,0:T(8,128)(2,1)S(1)}, u32[]{:S(2)}, u32[]{:S(2)}) collective-permute-start(bf16[2,2,64,1024]{3,2,1,0:T(8,128)(2,1)S(1)} %collective-permute-done.3.other.refs_3_.refs_8_), channel_id=1, source_target_pairs={{0,2},{1,3},{2,4},{3,5},{4,6},{5,7},{6,8},{7,9},{8,10},{9,11},{10,... | collective-permute-start | bytes 1572872 | tf_op jit(solution)/shard_map/ppermute | solution.py:27
  18.8 0.1 pad_add_fusion.info.refs_0_
  18.9 0.6 shard_map.41
  19.4 1.3 %collective-permute-start.4 = (bf16[2,128,1024]{2,1,0:T(8,128)(2,1)S(1)}, bf16[2,128,1024]{2,1,0:T(8,128)(2,1)S(1)}, u32[]{:S(2)}, u32[]{:S(2)}) collective-permute-start(bf16[2,128,1024]{2,1,0:T(8,128)(2,1)S(1)} %shard_map.41), channel_id=1, source_target_pairs={{0,33},{1,0},{2,35},{3,2},{4,37},{5,4},{6,39},{7,6},{8,41},{9,8},{... | collective-permute-start | bytes 1572872 | tf_op jit(solution)/shard_map/ppermute | solution.py:27
  20.7 2.3 %collective-permute-done.1.refs_1_.refs_2_ = bf16[2,2,64,1024]{3,2,1,0:T(8,128)(2,1)S(1)} collective-permute-done((bf16[2,2,64,1024]{3,2,1,0:T(8,128)(2,1)S(1)}, bf16[2,2,64,1024]{3,2,1,0:T(8,128)(2,1)S(1)}, u32[]{:S(2)}, u32[]{:S(2)}) %collective-permute-start.1) | collective-permute-done | bytes 524320 | tf_op jit(solution)/shard_map/ppermute | solution.py:27
  23.0 3.4 %collective-permute-start.2 = (bf16[2,2,64,1024]{3,2,1,0:T(8,128)(2,1)S(1)}, bf16[2,2,64,1024]{3,2,1,0:T(8,128)(2,1)S(1)}, u32[]{:S(2)}, u32[]{:S(2)}) collective-permute-start(bf16[2,2,64,1024]{3,2,1,0:T(8,128)(2,1)S(1)} %collective-permute-done.1.refs_1_.refs_2_), channel_id=1, source_target_pairs={{0,2},{1,3},{2,4},{3,5},{4,6},{5,7},{6,8},{7,9},{8,10},{9,11},{10,... | collective-permute-start | bytes 1572872 | tf_op jit(solution)/shard_map/ppermute | solution.py:27
  26.4 0.0 collective-permute-start.9
  26.4 2.2 %collective-permute-done.6.refs_4_.refs_6_.refs_9_ = bf16[2,2,64,1024]{3,2,1,0:T(8,128)(2,1)S(1)} collective-permute-done((bf16[2,2,64,1024]{3,2,1,0:T(8,128)(2,1)S(1)}, bf16[2,2,64,1024]{3,2,1,0:T(8,128)(2,1)S(1)}, u32[]{:S(2)}, u32[]{:S(2)}) %collective-permute-start.6) | collective-permute-done | bytes 524320 | tf_op jit(solution)/shard_map/ppermute | solution.py:27
  28.6 1.8 %collective-permute-start.8 = (bf16[2,2,64,1024]{3,2,1,0:T(8,128)(2,1)S(1)}, bf16[2,2,64,1024]{3,2,1,0:T(8,128)(2,1)S(1)}, u32[]{:S(2)}, u32[]{:S(2)}) collective-permute-start(bf16[2,2,64,1024]{3,2,1,0:T(8,128)(2,1)S(1)} %collective-permute-done.6.refs_4_.refs_6_.refs_9_), channel_id=1, source_target_pairs={{0,16},{1,17},{2,18},{3,19},{4,20},{5,21},{6,22},{7,23},{8,24},{9,... | collective-permute-start | bytes 1572872 | tf_op jit(solution)/shard_map/ppermute | solution.py:27
  30.4 1.7 %collective-permute-start.7 = (bf16[2,2,64,1024]{3,2,1,0:T(8,128)(2,1)S(1)}, bf16[2,2,64,1024]{3,2,1,0:T(8,128)(2,1)S(1)}, u32[]{:S(2)}, u32[]{:S(2)}) collective-permute-start(bf16[2,2,64,1024]{3,2,1,0:T(8,128)(2,1)S(1)} %collective-permute-done.6.refs_4_.refs_6_.refs_9_), channel_id=1, source_target_pairs={{0,2},{1,3},{2,4},{3,5},{4,6},{5,7},{6,8},{7,9},{8,10},{9,11},{10,... | collective-permute-start | bytes 1572872 | tf_op jit(solution)/shard_map/ppermute | solution.py:27
  32.2 2.1 %collective-permute-done.4.refs_1_.a_ref = bf16[2,128,1024]{2,1,0:T(8,128)(2,1)S(1)} collective-permute-done((bf16[2,128,1024]{2,1,0:T(8,128)(2,1)S(1)}, bf16[2,128,1024]{2,1,0:T(8,128)(2,1)S(1)}, u32[]{:S(2)}, u32[]{:S(2)}) %collective-permute-start.4) | collective-permute-done | bytes 524320 | tf_op jit(solution)/shard_map/ppermute | solution.py:27
  34.2 0.9 shard_map.42.refs_10_
  35.1 0.0 collective-permute-done.2.refs_4_.own.refs_3_.refs_0_
  35.1 3.6 %collective-permute-start.5 = (bf16[2,2,64,1024]{3,2,1,0:T(8,128)(2,1)S(1)}, bf16[2,2,64,1024]{3,2,1,0:T(8,128)(2,1)S(1)}, u32[]{:S(2)}, u32[]{:S(2)}) collective-permute-start(bf16[2,2,64,1024]{3,2,1,0:T(8,128)(2,1)S(1)} %collective-permute-done.2.refs_4_.own.refs_3_.refs_0_), channel_id=1, source_target_pairs={{0,2},{1,3},{2,4},{3,5},{4,6},{5,7},{6,8},{7,9},{8,10},{9,11},{10,... | collective-permute-start | bytes 1572872 | tf_op jit(solution)/shard_map/ppermute | solution.py:27
  38.7 0.0 collective-permute-start.12
  38.8 0.0 collective-permute-done.9.refs_5_.refs_7_.refs_10_
  38.8 0.0 collective-permute-done.8.refs_2_.refs_3_
  38.8 0.7 shard_map.43
  39.4 0.4 collective-permute-done.7.refs_8_.other.refs_11_.refs_4_
  39.8 1.8 %collective-permute-start.11 = (bf16[2,2,64,1024]{3,2,1,0:T(8,128)(2,1)S(1)}, bf16[2,2,64,1024]{3,2,1,0:T(8,128)(2,1)S(1)}, u32[]{:S(2)}, u32[]{:S(2)}) collective-permute-start(bf16[2,2,64,1024]{3,2,1,0:T(8,128)(2,1)S(1)} %collective-permute-done.7.refs_8_.other.refs_11_.refs_4_), channel_id=1, source_target_pairs={{0,16},{1,17},{2,18},{3,19},{4,20},{5,21},{6,22},{7,23},{8,24},{9,... | collective-permute-start | bytes 1572872 | tf_op jit(solution)/shard_map/ppermute | solution.py:27
  41.7 1.7 %collective-permute-start.10 = (bf16[2,2,64,1024]{3,2,1,0:T(8,128)(2,1)S(1)}, bf16[2,2,64,1024]{3,2,1,0:T(8,128)(2,1)S(1)}, u32[]{:S(2)}, u32[]{:S(2)}) collective-permute-start(bf16[2,2,64,1024]{3,2,1,0:T(8,128)(2,1)S(1)} %collective-permute-done.7.refs_8_.other.refs_11_.refs_4_), channel_id=1, source_target_pairs={{0,2},{1,3},{2,4},{3,5},{4,6},{5,7},{6,8},{7,9},{8,10},{9,11},{10,... | collective-permute-start | bytes 1572872 | tf_op jit(solution)/shard_map/ppermute | solution.py:27
  43.4 2.1 %collective-permute-done.5.refs_2_.refs_5_ = bf16[2,2,64,1024]{3,2,1,0:T(8,128)(2,1)S(1)} collective-permute-done((bf16[2,2,64,1024]{3,2,1,0:T(8,128)(2,1)S(1)}, bf16[2,2,64,1024]{3,2,1,0:T(8,128)(2,1)S(1)}, u32[]{:S(2)}, u32[]{:S(2)}) %collective-permute-start.5) | collective-permute-done | bytes 524320 | tf_op jit(solution)/shard_map/ppermute | solution.py:27
  45.5 3.1 %collective-permute-start.15 = (bf16[2,2,64,1024]{3,2,1,0:T(8,128)(2,1)S(1)}, bf16[2,2,64,1024]{3,2,1,0:T(8,128)(2,1)S(1)}, u32[]{:S(2)}, u32[]{:S(2)}) collective-permute-start(bf16[2,2,64,1024]{3,2,1,0:T(8,128)(2,1)S(1)} %collective-permute-done.5.refs_2_.refs_5_), channel_id=1, source_target_pairs={{0,2},{1,3},{2,4},{3,5},{4,6},{5,7},{6,8},{7,9},{8,10},{9,11},{10,... | collective-permute-start | bytes 1572872 | tf_op jit(solution)/shard_map/ppermute | solution.py:27
  48.6 1.2 %collective-permute-start.16 = (bf16[3,2,128,128]{3,2,1,0:T(8,128)(2,1)S(1)}, bf16[3,2,128,128]{3,2,1,0:T(8,128)(2,1)S(1)}, u32[]{:S(2)}, u32[]{:S(2)}) collective-permute-start(bf16[3,2,128,128]{3,2,1,0:T(8,128)(2,1)S(1)} %shard_map.43), channel_id=1, source_target_pairs={{0,33},{1,0},{2,35},{3,2},{4,37},{5,4},{6,39},{7,6},{8,41},{9,8},{... | collective-permute-start | bytes 589832 | tf_op jit(solution)/shard_map/ppermute | solution.py:27
  49.8 0.6 shard_map.46
  50.4 0.0 collective-permute-done.12.refs_9_.refs_12_.refs_5_
  50.4 1.5 %collective-permute-start.14 = (bf16[2,2,64,1024]{3,2,1,0:T(8,128)(2,1)S(1)}, bf16[2,2,64,1024]{3,2,1,0:T(8,128)(2,1)S(1)}, u32[]{:S(2)}, u32[]{:S(2)}) collective-permute-start(bf16[2,2,64,1024]{3,2,1,0:T(8,128)(2,1)S(1)} %collective-permute-done.5.refs_2_.refs_5_), channel_id=1, source_target_pairs={{0,16},{1,17},{2,18},{3,19},{4,20},{5,21},{6,22},{7,23},{8,24},{9,... | collective-permute-start | bytes 1572872 | tf_op jit(solution)/shard_map/ppermute | solution.py:27
  52.0 0.0 collective-permute-done.11.refs_5_.refs_4_.refs_1_
  52.0 1.3 %shard_map.44.refs_6_ = f32[256,1024]{1,0:T(8,128)S(1)} custom-call(s32[6]{0:T(128)S(1)} %pad_add_fusion.info.refs_0_, bf16[2,128,1024]{2,1,0:T(8,128)(2,1)S(1)} %collective-permute-done.4.refs_1_.a_ref, bf16[2,2,64,1024]{3,2,1,0:T(8,128)(2,1)S(1)} %collective-permute-done.1.refs_1_.refs_2_, ...), custom_call_target="tpu_custom_call" | custom-call | flops 1 | bytes 1048576 | tf_op jit(solution)/shard_map/pallas_call | solution.py:72
  53.2 0.0 collective-permute-done.10.refs_4_.refs_13_.refs_6_
  53.3 0.3 collective-permute-start.13
  53.6 4.5 %collective-permute-done.16.near = bf16[3,2,128,128]{3,2,1,0:T(8,128)(2,1)S(1)} collective-permute-done((bf16[3,2,128,128]{3,2,1,0:T(8,128)(2,1)S(1)}, bf16[3,2,128,128]{3,2,1,0:T(8,128)(2,1)S(1)}, u32[]{:S(2)}, u32[]{:S(2)}) %collective-permute-start.16) | collective-permute-done | bytes 196640 | tf_op jit(solution)/shard_map/ppermute | solution.py:27
  58.0 0.0 collective-permute-done.15.refs_7_
  58.0 0.5 collective-permute-start.17
  58.5 3.1 %collective-permute-start.19 = (bf16[2,128,128]{2,1,0:T(8,128)(2,1)S(1)}, bf16[2,128,128]{2,1,0:T(8,128)(2,1)S(1)}, u32[]{:S(2)}, u32[]{:S(2)}) collective-permute-start(bf16[2,128,128]{2,1,0:T(8,128)(2,1)S(1)} %shard_map.46), channel_id=1, source_target_pairs={{0,37},{1,4},{2,39},{3,6},{4,41},{5,8},{6,43},{7,10},{8,45},{9,12}... | collective-permute-start | bytes 196616 | tf_op jit(solution)/shard_map/ppermute | solution.py:27
  61.6 0.7 shard_map.48
  62.4 1.3 %collective-permute-start.18 = (bf16[4,2,128,128]{3,2,1,0:T(8,128)(2,1)S(1)}, bf16[4,2,128,128]{3,2,1,0:T(8,128)(2,1)S(1)}, u32[]{:S(2)}, u32[]{:S(2)}) collective-permute-start(bf16[4,2,128,128]{3,2,1,0:T(8,128)(2,1)S(1)} %shard_map.48), channel_id=1, source_target_pairs={{0,33},{1,0},{2,35},{3,2},{4,37},{5,4},{6,39},{7,6},{8,41},{9,8},{... | collective-permute-start | bytes 786440 | tf_op jit(solution)/shard_map/ppermute | solution.py:27
  63.7 1.0 %shard_map.45.acc = f32[256,1024]{1,0:T(8,128)S(1)} custom-call(s32[6]{0:T(128)S(1)} %pad_add_fusion.info.refs_0_, bf16[2,128,1024]{2,1,0:T(8,128)(2,1)S(1)} %collective-permute-done.4.refs_1_.a_ref, bf16[2,2,64,1024]{3,2,1,0:T(8,128)(2,1)S(1)} %collective-permute-done.5.refs_2_.refs_5_, ...), custom_call_target="tpu_custom_call" | custom-call | flops 1 | bytes 1048576 | tf_op jit(solution)/shard_map/pallas_call | solution.py:72
  64.7 2.2 %shard_map.47 = (bf16[2,64,1024]{2,1,0:T(8,128)(2,1)S(1)}, bf16[2,64,1024]{2,1,0:T(8,128)(2,1)S(1)}, f32[256,1024]{1,0:T(8,128)S(1)}) custom-call(s32[6]{0:T(128)S(1)} %pad_add_fusion.info.refs_0_, bf16[2,128,1024]{2,1,0:T(8,128)(2,1)S(1)} %collective-permute-done.4.refs_1_.a_ref, f32[256,1024]{1,0:T(8,128)S(1)} %shard_map.45.acc, ...), custom_call_target="tpu_custom_call" | custom-call | flops 3000000000 | bytes 1048576 | tf_op jit(solution)/shard_map/pallas_call | solution.py:72
  66.8 1.1 %collective-permute-done.19.across = bf16[2,128,128]{2,1,0:T(8,128)(2,1)S(1)} collective-permute-done((bf16[2,128,128]{2,1,0:T(8,128)(2,1)S(1)}, bf16[2,128,128]{2,1,0:T(8,128)(2,1)S(1)}, u32[]{:S(2)}, u32[]{:S(2)}) %collective-permute-start.19) | collective-permute-done | bytes 65568 | tf_op jit(solution)/shard_map/ppermute | solution.py:27
  67.9 5.2 %collective-permute-done.18.late = bf16[4,2,128,128]{3,2,1,0:T(8,128)(2,1)S(1)} collective-permute-done((bf16[4,2,128,128]{3,2,1,0:T(8,128)(2,1)S(1)}, bf16[4,2,128,128]{3,2,1,0:T(8,128)(2,1)S(1)}, u32[]{:S(2)}, u32[]{:S(2)}) %collective-permute-start.18) | collective-permute-done | bytes 262176 | tf_op jit(solution)/shard_map/ppermute | solution.py:27
  73.1 1.0 %shard_map.49 = f32[1,128]{1,0:T(1,128)S(1)} custom-call(s32[6]{0:T(128)S(1)} %pad_add_fusion.info.refs_0_, f32[256,1024]{1,0:T(8,128)S(1)} %get-tuple-element.32.product, bf16[3,2,128,128]{3,2,1,0:T(8,128)(2,1)S(1)} %collective-permute-done.16.near, bf16[4,2,128,128]{3,2,1,0:T(8,128)(2,1)S(1)} %collective-permute-done.18.late, ...), custom_call_target="tpu_custom_call" | custom-call | flops 1 | bytes 1048576 | tf_op jit(solution)/shard_map/pallas_call | solution.py:72
  74.1 1.7 %collective-permute-start.21 = (f32[1,128]{1,0:T(1,128)S(1)}, f32[1,128]{1,0:T(1,128)S(1)}, u32[]{:S(2)}, u32[]{:S(2)}) collective-permute-start(f32[1,128]{1,0:T(1,128)S(1)} %shard_map.49), channel_id=1, source_target_pairs={{0,2},{1,3},{2,4},{3,5},{4,6},{5,7},{6,8},{7,9},{8,10},{9,11},{10,... | collective-permute-start | bytes 1544 | tf_op jit(solution)/shard_map/ppermute | solution.py:27
  75.8 1.0 collective-permute-start.20
  76.8 0.0 collective-permute-start.24
  76.8 3.2 %collective-permute-start.25 = (bf16[2,64,1024]{2,1,0:T(8,128)(2,1)S(1)}, bf16[2,64,1024]{2,1,0:T(8,128)(2,1)S(1)}, u32[]{:S(2)}, u32[]{:S(2)}) collective-permute-start(bf16[2,64,1024]{2,1,0:T(8,128)(2,1)S(1)} %get-tuple-element.38), channel_id=1, source_target_pairs={{0,129},{1,113},{2,131},{3,115},{4,133},{5,117},{6,135},{7,119},{8... | collective-permute-start | bytes 786440 | tf_op jit(solution)/shard_map/ppermute | solution.py:27
  80.0 0.0 collective-permute-done.21
  80.0 0.0 collective-permute-done.20
  80.0 1.9 %collective-permute-start.22 = (f32[1,128]{1,0:T(1,128)S(1)}, f32[1,128]{1,0:T(1,128)S(1)}, u32[]{:S(2)}, u32[]{:S(2)}) collective-permute-start(f32[1,128]{1,0:T(1,128)S(1)} %get-tuple-element.35), channel_id=1, source_target_pairs={{0,6},{1,7},{2,8},{3,9},{4,10},{5,11},{6,12},{7,13},{8,14},{9,15},... | collective-permute-start | bytes 1544 | tf_op jit(solution)/shard_map/ppermute | solution.py:27
  81.9 2.7 %collective-permute-start.23 = (f32[1,128]{1,0:T(1,128)S(1)}, f32[1,128]{1,0:T(1,128)S(1)}, u32[]{:S(2)}, u32[]{:S(2)}) collective-permute-start(f32[1,128]{1,0:T(1,128)S(1)} %get-tuple-element.36), channel_id=1, source_target_pairs={{0,10},{1,11},{2,12},{3,13},{4,14},{5,15},{6,0},{7,1},{8,2},{9,3},... | collective-permute-start | bytes 1544 | tf_op jit(solution)/shard_map/ppermute | solution.py:27
  84.5 0.9 collective-permute-done.22
  85.4 0.6 collective-permute-done.23
  86.1 0.6 collective-permute-done.24
  86.6 2.9 %collective-permute-start.27 = (f32[1,128]{1,0:T(1,128)S(1)}, f32[1,128]{1,0:T(1,128)S(1)}, u32[]{:S(2)}, u32[]{:S(2)}) collective-permute-start(f32[1,128]{1,0:T(1,128)S(1)} %add_add_fusion), channel_id=1, source_target_pairs={{0,129},{1,113},{2,131},{3,115},{4,133},{5,117},{6,135},{7,119},{8... | collective-permute-start | bytes 1544 | tf_op jit(solution)/shard_map/ppermute | solution.py:27
  89.6 5.5 %collective-permute-start.26 = (f32[1,128]{1,0:T(1,128)S(1)}, f32[1,128]{1,0:T(1,128)S(1)}, u32[]{:S(2)}, u32[]{:S(2)}) collective-permute-start(f32[1,128]{1,0:T(1,128)S(1)} %add_add_fusion), channel_id=1, source_target_pairs={{0,128},{1,112},{2,130},{3,114},{4,132},{5,116},{6,134},{7,118},{8... | collective-permute-start | bytes 1544 | tf_op jit(solution)/shard_map/ppermute | solution.py:27
  95.1 0.9 maximum_select_fusion
  96.0 0.1 reshape.77
  96.1 0.6 broadcast_multiply_fusion
  (12 shorter events, 0.1 us)
Async XLA Ops:
  0.6 16.2 %copy-start = (s32[2,1,4]{2,1,0:T(1,128)S(1)}, s32[2,1,4]{2,1,0:T(1,128)}, u32[]{:S(2)}) copy-start(s32[2,1,4]{2,1,0:T(1,128)} %param.3) | copy-start | bytes 100
  0.6 10.6 %collective-permute-start = (bf16[2,2,64,1024]{3,2,1,0:T(8,128)(2,1)}, bf16[2,2,64,1024]{3,2,1,0:T(8,128)(2,1)S(1)}, u32[]{:S(2)}, u32[]{:S(2)}) collective-permute-start(bf16[2,2,64,1024]{3,2,1,0:T(8,128)(2,1)} %bitcast.15), channel_id=1, source_target_pairs={{0,128},{1,144},{2,130},{3,146},{4,132},{5,148},{6,134},{7,150},{8... | collective-permute-start | bytes 1572872 | tf_op jit(solution)/shard_map/ppermute | solution.py:27
  11.3 5.6 %collective-permute-start.3 = (bf16[2,2,64,1024]{3,2,1,0:T(8,128)(2,1)S(1)}, bf16[2,2,64,1024]{3,2,1,0:T(8,128)(2,1)S(1)}, u32[]{:S(2)}, u32[]{:S(2)}) collective-permute-start(bf16[2,2,64,1024]{3,2,1,0:T(8,128)(2,1)S(1)} %collective-permute-done.own.refs_2_.refs_0_), channel_id=1, source_target_pairs={{0,16},{1,17},{2,18},{3,19},{4,20},{5,21},{6,22},{7,23},{8,24},{9,... | collective-permute-start | bytes 1572872 | tf_op jit(solution)/shard_map/ppermute | solution.py:27
  12.8 10.2 %collective-permute-start.1 = (bf16[2,2,64,1024]{3,2,1,0:T(8,128)(2,1)S(1)}, bf16[2,2,64,1024]{3,2,1,0:T(8,128)(2,1)S(1)}, u32[]{:S(2)}, u32[]{:S(2)}) collective-permute-start(bf16[2,2,64,1024]{3,2,1,0:T(8,128)(2,1)S(1)} %collective-permute-done.own.refs_2_.refs_0_), channel_id=1, source_target_pairs={{0,2},{1,3},{2,4},{3,5},{4,6},{5,7},{6,8},{7,9},{8,10},{9,11},{10,... | collective-permute-start | bytes 1572872 | tf_op jit(solution)/shard_map/ppermute | solution.py:27
  16.9 11.7 %collective-permute-start.6 = (bf16[2,2,64,1024]{3,2,1,0:T(8,128)(2,1)S(1)}, bf16[2,2,64,1024]{3,2,1,0:T(8,128)(2,1)S(1)}, u32[]{:S(2)}, u32[]{:S(2)}) collective-permute-start(bf16[2,2,64,1024]{3,2,1,0:T(8,128)(2,1)S(1)} %collective-permute-done.3.other.refs_3_.refs_8_), channel_id=1, source_target_pairs={{0,2},{1,3},{2,4},{3,5},{4,6},{5,7},{6,8},{7,9},{8,10},{9,11},{10,... | collective-permute-start | bytes 1572872 | tf_op jit(solution)/shard_map/ppermute | solution.py:27
  19.4 14.8 %collective-permute-start.4 = (bf16[2,128,1024]{2,1,0:T(8,128)(2,1)S(1)}, bf16[2,128,1024]{2,1,0:T(8,128)(2,1)S(1)}, u32[]{:S(2)}, u32[]{:S(2)}) collective-permute-start(bf16[2,128,1024]{2,1,0:T(8,128)(2,1)S(1)} %shard_map.41), channel_id=1, source_target_pairs={{0,33},{1,0},{2,35},{3,2},{4,37},{5,4},{6,39},{7,6},{8,41},{9,8},{... | collective-permute-start | bytes 1572872 | tf_op jit(solution)/shard_map/ppermute | solution.py:27
  23.0 12.1 %collective-permute-start.2 = (bf16[2,2,64,1024]{3,2,1,0:T(8,128)(2,1)S(1)}, bf16[2,2,64,1024]{3,2,1,0:T(8,128)(2,1)S(1)}, u32[]{:S(2)}, u32[]{:S(2)}) collective-permute-start(bf16[2,2,64,1024]{3,2,1,0:T(8,128)(2,1)S(1)} %collective-permute-done.1.refs_1_.refs_2_), channel_id=1, source_target_pairs={{0,2},{1,3},{2,4},{3,5},{4,6},{5,7},{6,8},{7,9},{8,10},{9,11},{10,... | collective-permute-start | bytes 1572872 | tf_op jit(solution)/shard_map/ppermute | solution.py:27
  26.4 12.3 %collective-permute-start.9 = (bf16[2,2,64,1024]{3,2,1,0:T(8,128)(2,1)S(1)}, bf16[2,2,64,1024]{3,2,1,0:T(8,128)(2,1)S(1)}, u32[]{:S(2)}, u32[]{:S(2)}) collective-permute-start(bf16[2,2,64,1024]{3,2,1,0:T(8,128)(2,1)S(1)} %collective-permute-done.1.refs_1_.refs_2_), channel_id=1, source_target_pairs={{0,16},{1,17},{2,18},{3,19},{4,20},{5,21},{6,22},{7,23},{8,24},{9,... | collective-permute-start | bytes 1572872 | tf_op jit(solution)/shard_map/ppermute | solution.py:27
  28.6 10.1 %collective-permute-start.8 = (bf16[2,2,64,1024]{3,2,1,0:T(8,128)(2,1)S(1)}, bf16[2,2,64,1024]{3,2,1,0:T(8,128)(2,1)S(1)}, u32[]{:S(2)}, u32[]{:S(2)}) collective-permute-start(bf16[2,2,64,1024]{3,2,1,0:T(8,128)(2,1)S(1)} %collective-permute-done.6.refs_4_.refs_6_.refs_9_), channel_id=1, source_target_pairs={{0,16},{1,17},{2,18},{3,19},{4,20},{5,21},{6,22},{7,23},{8,24},{9,... | collective-permute-start | bytes 1572872 | tf_op jit(solution)/shard_map/ppermute | solution.py:27
  30.4 9.4 %collective-permute-start.7 = (bf16[2,2,64,1024]{3,2,1,0:T(8,128)(2,1)S(1)}, bf16[2,2,64,1024]{3,2,1,0:T(8,128)(2,1)S(1)}, u32[]{:S(2)}, u32[]{:S(2)}) collective-permute-start(bf16[2,2,64,1024]{3,2,1,0:T(8,128)(2,1)S(1)} %collective-permute-done.6.refs_4_.refs_6_.refs_9_), channel_id=1, source_target_pairs={{0,2},{1,3},{2,4},{3,5},{4,6},{5,7},{6,8},{7,9},{8,10},{9,11},{10,... | collective-permute-start | bytes 1572872 | tf_op jit(solution)/shard_map/ppermute | solution.py:27
  35.1 10.4 %collective-permute-start.5 = (bf16[2,2,64,1024]{3,2,1,0:T(8,128)(2,1)S(1)}, bf16[2,2,64,1024]{3,2,1,0:T(8,128)(2,1)S(1)}, u32[]{:S(2)}, u32[]{:S(2)}) collective-permute-start(bf16[2,2,64,1024]{3,2,1,0:T(8,128)(2,1)S(1)} %collective-permute-done.2.refs_4_.own.refs_3_.refs_0_), channel_id=1, source_target_pairs={{0,2},{1,3},{2,4},{3,5},{4,6},{5,7},{6,8},{7,9},{8,10},{9,11},{10,... | collective-permute-start | bytes 1572872 | tf_op jit(solution)/shard_map/ppermute | solution.py:27
  38.7 11.7 %collective-permute-start.12 = (bf16[2,2,64,1024]{3,2,1,0:T(8,128)(2,1)S(1)}, bf16[2,2,64,1024]{3,2,1,0:T(8,128)(2,1)S(1)}, u32[]{:S(2)}, u32[]{:S(2)}) collective-permute-start(bf16[2,2,64,1024]{3,2,1,0:T(8,128)(2,1)S(1)} %collective-permute-done.2.refs_4_.own.refs_3_.refs_0_), channel_id=1, source_target_pairs={{0,16},{1,17},{2,18},{3,19},{4,20},{5,21},{6,22},{7,23},{8,24},{9,... | collective-permute-start | bytes 1572872 | tf_op jit(solution)/shard_map/ppermute | solution.py:27
  39.8 12.1 %collective-permute-start.11 = (bf16[2,2,64,1024]{3,2,1,0:T(8,128)(2,1)S(1)}, bf16[2,2,64,1024]{3,2,1,0:T(8,128)(2,1)S(1)}, u32[]{:S(2)}, u32[]{:S(2)}) collective-permute-start(bf16[2,2,64,1024]{3,2,1,0:T(8,128)(2,1)S(1)} %collective-permute-done.7.refs_8_.other.refs_11_.refs_4_), channel_id=1, source_target_pairs={{0,16},{1,17},{2,18},{3,19},{4,20},{5,21},{6,22},{7,23},{8,24},{9,... | collective-permute-start | bytes 1572872 | tf_op jit(solution)/shard_map/ppermute | solution.py:27
  41.7 11.6 %collective-permute-start.10 = (bf16[2,2,64,1024]{3,2,1,0:T(8,128)(2,1)S(1)}, bf16[2,2,64,1024]{3,2,1,0:T(8,128)(2,1)S(1)}, u32[]{:S(2)}, u32[]{:S(2)}) collective-permute-start(bf16[2,2,64,1024]{3,2,1,0:T(8,128)(2,1)S(1)} %collective-permute-done.7.refs_8_.other.refs_11_.refs_4_), channel_id=1, source_target_pairs={{0,2},{1,3},{2,4},{3,5},{4,6},{5,7},{6,8},{7,9},{8,10},{9,11},{10,... | collective-permute-start | bytes 1572872 | tf_op jit(solution)/shard_map/ppermute | solution.py:27
  45.5 12.6 %collective-permute-start.15 = (bf16[2,2,64,1024]{3,2,1,0:T(8,128)(2,1)S(1)}, bf16[2,2,64,1024]{3,2,1,0:T(8,128)(2,1)S(1)}, u32[]{:S(2)}, u32[]{:S(2)}) collective-permute-start(bf16[2,2,64,1024]{3,2,1,0:T(8,128)(2,1)S(1)} %collective-permute-done.5.refs_2_.refs_5_), channel_id=1, source_target_pairs={{0,2},{1,3},{2,4},{3,5},{4,6},{5,7},{6,8},{7,9},{8,10},{9,11},{10,... | collective-permute-start | bytes 1572872 | tf_op jit(solution)/shard_map/ppermute | solution.py:27
  48.6 9.5 %collective-permute-start.16 = (bf16[3,2,128,128]{3,2,1,0:T(8,128)(2,1)S(1)}, bf16[3,2,128,128]{3,2,1,0:T(8,128)(2,1)S(1)}, u32[]{:S(2)}, u32[]{:S(2)}) collective-permute-start(bf16[3,2,128,128]{3,2,1,0:T(8,128)(2,1)S(1)} %shard_map.43), channel_id=1, source_target_pairs={{0,33},{1,0},{2,35},{3,2},{4,37},{5,4},{6,39},{7,6},{8,41},{9,8},{... | collective-permute-start | bytes 589832 | tf_op jit(solution)/shard_map/ppermute | solution.py:27
  50.4 11.2 %collective-permute-start.14 = (bf16[2,2,64,1024]{3,2,1,0:T(8,128)(2,1)S(1)}, bf16[2,2,64,1024]{3,2,1,0:T(8,128)(2,1)S(1)}, u32[]{:S(2)}, u32[]{:S(2)}) collective-permute-start(bf16[2,2,64,1024]{3,2,1,0:T(8,128)(2,1)S(1)} %collective-permute-done.5.refs_2_.refs_5_), channel_id=1, source_target_pairs={{0,16},{1,17},{2,18},{3,19},{4,20},{5,21},{6,22},{7,23},{8,24},{9,... | collective-permute-start | bytes 1572872 | tf_op jit(solution)/shard_map/ppermute | solution.py:27
  53.3 8.4 %collective-permute-start.13 = (bf16[2,2,64,1024]{3,2,1,0:T(8,128)(2,1)S(1)}, bf16[2,2,64,1024]{3,2,1,0:T(8,128)(2,1)S(1)}, u32[]{:S(2)}, u32[]{:S(2)}) collective-permute-start(bf16[2,2,64,1024]{3,2,1,0:T(8,128)(2,1)S(1)} %collective-permute-done.10.refs_4_.refs_13_.refs_6_), channel_id=1, source_target_pairs={{0,16},{1,17},{2,18},{3,19},{4,20},{5,21},{6,22},{7,23},{8,24},{9,... | collective-permute-start | bytes 1572872 | tf_op jit(solution)/shard_map/ppermute | solution.py:27
  58.0 6.6 %collective-permute-start.17 = (bf16[2,2,64,1024]{3,2,1,0:T(8,128)(2,1)S(1)}, bf16[2,2,64,1024]{3,2,1,0:T(8,128)(2,1)S(1)}, u32[]{:S(2)}, u32[]{:S(2)}) collective-permute-start(bf16[2,2,64,1024]{3,2,1,0:T(8,128)(2,1)S(1)} %collective-permute-done.15.refs_7_), channel_id=1, source_target_pairs={{0,16},{1,17},{2,18},{3,19},{4,20},{5,21},{6,22},{7,23},{8,24},{9,... | collective-permute-start | bytes 1572872 | tf_op jit(solution)/shard_map/ppermute | solution.py:27
  58.5 9.4 %collective-permute-start.19 = (bf16[2,128,128]{2,1,0:T(8,128)(2,1)S(1)}, bf16[2,128,128]{2,1,0:T(8,128)(2,1)S(1)}, u32[]{:S(2)}, u32[]{:S(2)}) collective-permute-start(bf16[2,128,128]{2,1,0:T(8,128)(2,1)S(1)} %shard_map.46), channel_id=1, source_target_pairs={{0,37},{1,4},{2,39},{3,6},{4,41},{5,8},{6,43},{7,10},{8,45},{9,12}... | collective-permute-start | bytes 196616 | tf_op jit(solution)/shard_map/ppermute | solution.py:27
  62.4 10.8 %collective-permute-start.18 = (bf16[4,2,128,128]{3,2,1,0:T(8,128)(2,1)S(1)}, bf16[4,2,128,128]{3,2,1,0:T(8,128)(2,1)S(1)}, u32[]{:S(2)}, u32[]{:S(2)}) collective-permute-start(bf16[4,2,128,128]{3,2,1,0:T(8,128)(2,1)S(1)} %shard_map.48), channel_id=1, source_target_pairs={{0,33},{1,0},{2,35},{3,2},{4,37},{5,4},{6,39},{7,6},{8,41},{9,8},{... | collective-permute-start | bytes 786440 | tf_op jit(solution)/shard_map/ppermute | solution.py:27
  74.1 5.9 %collective-permute-start.21 = (f32[1,128]{1,0:T(1,128)S(1)}, f32[1,128]{1,0:T(1,128)S(1)}, u32[]{:S(2)}, u32[]{:S(2)}) collective-permute-start(f32[1,128]{1,0:T(1,128)S(1)} %shard_map.49), channel_id=1, source_target_pairs={{0,2},{1,3},{2,4},{3,5},{4,6},{5,7},{6,8},{7,9},{8,10},{9,11},{10,... | collective-permute-start | bytes 1544 | tf_op jit(solution)/shard_map/ppermute | solution.py:27
  75.8 4.1 %collective-permute-start.20 = (f32[1,128]{1,0:T(1,128)S(1)}, f32[1,128]{1,0:T(1,128)S(1)}, u32[]{:S(2)}, u32[]{:S(2)}) collective-permute-start(f32[1,128]{1,0:T(1,128)S(1)} %shard_map.49), channel_id=1, source_target_pairs={{0,14},{1,15},{2,0},{3,1},{4,2},{5,3},{6,4},{7,5},{8,6},{9,7},{10,... | collective-permute-start | bytes 1544 | tf_op jit(solution)/shard_map/ppermute | solution.py:27
  76.8 9.9 %collective-permute-start.24 = (bf16[2,64,1024]{2,1,0:T(8,128)(2,1)S(1)}, bf16[2,64,1024]{2,1,0:T(8,128)(2,1)S(1)}, u32[]{:S(2)}, u32[]{:S(2)}) collective-permute-start(bf16[2,64,1024]{2,1,0:T(8,128)(2,1)S(1)} %get-tuple-element.37), channel_id=1, source_target_pairs={{0,128},{1,112},{2,130},{3,114},{4,132},{5,116},{6,134},{7,118},{8... | collective-permute-start | bytes 786440 | tf_op jit(solution)/shard_map/ppermute | solution.py:27
  76.8 9.9 %collective-permute-start.25 = (bf16[2,64,1024]{2,1,0:T(8,128)(2,1)S(1)}, bf16[2,64,1024]{2,1,0:T(8,128)(2,1)S(1)}, u32[]{:S(2)}, u32[]{:S(2)}) collective-permute-start(bf16[2,64,1024]{2,1,0:T(8,128)(2,1)S(1)} %get-tuple-element.38), channel_id=1, source_target_pairs={{0,129},{1,113},{2,131},{3,115},{4,133},{5,117},{6,135},{7,119},{8... | collective-permute-start | bytes 786440 | tf_op jit(solution)/shard_map/ppermute | solution.py:27
  80.0 5.5 %collective-permute-start.22 = (f32[1,128]{1,0:T(1,128)S(1)}, f32[1,128]{1,0:T(1,128)S(1)}, u32[]{:S(2)}, u32[]{:S(2)}) collective-permute-start(f32[1,128]{1,0:T(1,128)S(1)} %get-tuple-element.35), channel_id=1, source_target_pairs={{0,6},{1,7},{2,8},{3,9},{4,10},{5,11},{6,12},{7,13},{8,14},{9,15},... | collective-permute-start | bytes 1544 | tf_op jit(solution)/shard_map/ppermute | solution.py:27
  81.9 4.2 %collective-permute-start.23 = (f32[1,128]{1,0:T(1,128)S(1)}, f32[1,128]{1,0:T(1,128)S(1)}, u32[]{:S(2)}, u32[]{:S(2)}) collective-permute-start(f32[1,128]{1,0:T(1,128)S(1)} %get-tuple-element.36), channel_id=1, source_target_pairs={{0,10},{1,11},{2,12},{3,13},{4,14},{5,15},{6,0},{7,1},{8,2},{9,3},... | collective-permute-start | bytes 1544 | tf_op jit(solution)/shard_map/ppermute | solution.py:27
  86.6 9.3 %collective-permute-start.27 = (f32[1,128]{1,0:T(1,128)S(1)}, f32[1,128]{1,0:T(1,128)S(1)}, u32[]{:S(2)}, u32[]{:S(2)}) collective-permute-start(f32[1,128]{1,0:T(1,128)S(1)} %add_add_fusion), channel_id=1, source_target_pairs={{0,129},{1,113},{2,131},{3,115},{4,133},{5,117},{6,135},{7,119},{8... | collective-permute-start | bytes 1544 | tf_op jit(solution)/shard_map/ppermute | solution.py:27
  89.6 6.4 %collective-permute-start.26 = (f32[1,128]{1,0:T(1,128)S(1)}, f32[1,128]{1,0:T(1,128)S(1)}, u32[]{:S(2)}, u32[]{:S(2)}) collective-permute-start(f32[1,128]{1,0:T(1,128)S(1)} %add_add_fusion), channel_id=1, source_target_pairs={{0,128},{1,112},{2,130},{3,114},{4,132},{5,116},{6,134},{7,118},{8... | collective-permute-start | bytes 1544 | tf_op jit(solution)/shard_map/ppermute | solution.py:27

commit v8 on v7

--- a/solution.py
+++ b/solution.py
@@ -64,7 +64,10 @@
 
 VMEM = pl.BlockSpec(memory_space=pltpu.VMEM)
 SMEM = pl.BlockSpec(memory_space=pltpu.SMEM)
-SLICES = jax.ShapeDtypeStruct((2, 128, 128), BF16)
+
+
+def slices_of(count):
+    return jax.ShapeDtypeStruct((count, 2, 128, 128), BF16)
 
 
 def call(kernel, info, arrays, out_shape, flops, scratch=()):
@@ -114,10 +117,6 @@
     count = len(refs) // 2
     for k in range(count):
         cut(info, refs[k], refs[count + k], 0, refs[-1].at[k])
-
-
-def across_kernel(info, own, other, out):
-    cut(info, own, other, -2, out)
 
 
 def left_side(info, a_ref, offset):
@@ -160,8 +159,8 @@
     out[...] = total
 
 
-def trace_kernel(info, product, near, late, across, trace):
-    slices = [near.at[0], near.at[1], near.at[2], late.at[0], late.at[1], late.at[2], late.at[3], across]
+def trace_kernel(info, product, near, middle, late, trace):
+    slices = [near.at[0], near.at[1], near.at[2], middle.at[0], middle.at[1], late.at[0], late.at[1], late.at[2]]
     re = im = None
     for offset, piece in zip(OFFSETS, slices):
         columns = columns_of(info, offset)
@@ -176,6 +175,11 @@
     trace[...] = jnp.where(lane == 2 * info[0], re, jnp.where(lane == 2 * info[0] + 1, im, 0.0))
 
 
+def add_kernel(info, below, own, above, two, three):
+    two[...] = own[...] + above[...]
+    three[...] = below[...] + own[...] + above[...]
+
+
 def shards(fields, mom_table):
     rows = fields[:, 0]
     tm, row = lax.axis_index("tm"), lax.axis_index("row")
@@ -195,36 +199,32 @@
     p2, p1x = moved(p1, onward), moved(p1, other_core)
     q2, q1x = moved(q1, onward), moved(q1, other_core)
     three, three_x = [own, p1, q1x], [ownx, q1, p1x]
-    near = call(cut_kernel, info, three + three_x, jax.ShapeDtypeStruct((3, 2, 128, 128), BF16), 1)
+    near = call(cut_kernel, info, three + three_x, slices_of(3), 1)
     acc = call(lambda *refs: products_kernel(OFFSETS[:1], *refs), info, [a, own, ownx], block_of_products, WEIGHT)
     p2, a, acc = wall((p2, a, acc))
-    q2, near = wall((q2, near))
-
+
+    near = moved(near, hub_ahead(0))
     p3, p2x = moved(p2, onward), moved(p2, other_core)
     q3, q2x = moved(q2, onward), moved(q2, other_core)
-    across = call(across_kernel, info, [p2, q2], SLICES, 1)
+    p3, near = wall((p3, near))
+
+    p4, p3x = moved(p3, onward), moved(p3, other_core)
     five, five_x = three + [p2, q2x], three_x + [q2, p2x]
+    middle = moved(call(cut_kernel, info, five[3:] + five_x[3:], slices_of(2), 1), hub_ahead(0))
     acc = call(
         lambda *refs: products_kernel(OFFSETS[1:5], *refs), info, [a] + five[1:] + five_x[1:] + [acc], block_of_products, 1
     )
-    p3, near = wall((p3, near))
-
-    near = moved(near, hub_ahead(0))
-    p4, p3x = moved(p3, onward), moved(p3, other_core)
     q3, acc = wall((q3, acc))
 
     q3x = moved(q3, other_core)
-    p4, near, across = wall((p4, near, across))
+    p4, middle = wall((p4, middle))
 
     p4x = moved(p4, other_core)
-    across = moved(across, hub_ahead(2))
     two, two_x = [p3, q3x], [q3, p3x]
-    four, four_x = five[3:] + two, five_x[3:] + two_x
-    late = call(cut_kernel, info, four + four_x, jax.ShapeDtypeStruct((4, 2, 128, 128), BF16), 1)
-    late = moved(late, hub_ahead(0))
     acc = call(
         lambda *refs: products_kernel(OFFSETS[5:7], *refs), info, [a] + two + two_x + [acc], block_of_products, 1
     )
+    late = moved(call(cut_kernel, info, two + [p4] + two_x + [p4x], slices_of(3), 1), hub_ahead(0))
     half_block = jax.ShapeDtypeStruct((2, 64, 1024), BF16)
     keep, send, product = call(
         last_kernel,
@@ -234,11 +234,12 @@
         WEIGHT,
         [pltpu.VMEM((2, 128, 1024), BF16)],
     )
-    trace = call(trace_kernel, info, [product, near, late, across], jax.ShapeDtypeStruct((1, 128), F32), 1)
+    share = jax.ShapeDtypeStruct((1, 128), F32)
+    trace = call(trace_kernel, info, [product, near, middle, late], share, 1)
 
     below, above = moved(trace, along(1)), moved(trace, along(-1))
     kept, sent = moved(keep, from_hub(0)), moved(send, from_hub(1))
-    two, three = wall((trace + above, below + trace + above))
+    two, three = call(add_kernel, info, [below, trace, above], (share, share), WEIGHT)
     below, above = moved(two, along(3)), moved(three, along(-3))
     trace, kept, sent = wall((below + three + above, kept, sent))
     first, second = moved(trace, from_hub(0)), moved(trace, from_hub(1))

time: 98.2 us -> 95.5 us (0.973)
  starting transfers between devices: 57 us -> 51 us
  waiting for transfers between devices: 28.3 us -> 31.5 us
    ppermute x28, starting transfers between devices: 57 us -> 51 us  [moved(): lax.ppermute(block, BOTH, [(index_of(*at), index_of(*route(*at))) for at...]
    ppermute x28, waiting for transfers between devices: 28.3 us -> 31.5 us  [moved(): lax.ppermute(block, BOTH, [(index_of(*at), index_of(*route(*at))) for at...]
    pallas_call x9 -> x10, Pallas kernels: 8.85 us -> 9.37 us  [call(): pl.pallas_call(kernel, out_shape=out_shape, in_specs=[SMEM] + [VMEM] * le...]
  transfers between devices with their start and end apart: 28 -> 28, of which waited for: 12 -> 11; matrix products, arithmetic and copies ran while one was open for 1% -> 1% of each run, Pallas kernels for 8% -> 8%
where the time goes in v8:
time: 95.5 us; the launch traced here: 94.3 us
  starting transfers between devices  51 us (53%)
  waiting for transfers between devices  31.5 us (33%)
  Pallas kernels  9.37 us (10%)
  other arithmetic  1.55 us (2%)
    ppermute x28, starting transfers between devices, moved(): lax.ppermute(block, BOTH, [(index_of(*at), index_of(*route(*at))) for at...  51 us
    ppermute x28, waiting for transfers between devices, moved(): lax.ppermute(block, BOTH, [(index_of(*at), index_of(*route(*at))) for at...  31.5 us
    pallas_call x10, Pallas kernels, call(): pl.pallas_call(kernel, out_shape=out_shape, in_specs=[SMEM] + [VMEM] * le...  9.37 us
  transfers between devices with their start and end apart: 28, of which 11 were waited for; matrix products, arithmetic and copies ran while one was open for 1% of the time, Pallas kernels for 8%

profile of v8, /device:TPU:1, one launch (start us, length us, event | category | flops | bytes accessed | tf_op | source)
XLA Modules:
  0.0 94.3 jit_solution(9959581971523720973)
XLA Ops:
  0.6 0.0 copy-start
  0.6 4.2 %collective-permute-start = (bf16[2,2,64,1024]{3,2,1,0:T(8,128)(2,1)}, bf16[2,2,64,1024]{3,2,1,0:T(8,128)(2,1)S(1)}, u32[]{:S(2)}, u32[]{:S(2)}) collective-permute-start(bf16[2,2,64,1024]{3,2,1,0:T(8,128)(2,1)} %bitcast.15), channel_id=1, source_target_pairs={{0,128},{1,144},{2,130},{3,146},{4,132},{5,148},{6,134},{7,150},{8... | collective-permute-start | bytes 1572872 | tf_op jit(solution)/shard_map/ppermute | solution.py:27
  4.8 6.4 %collective-permute-done.own.refs_2_.refs_0_ = bf16[2,2,64,1024]{3,2,1,0:T(8,128)(2,1)S(1)} collective-permute-done((bf16[2,2,64,1024]{3,2,1,0:T(8,128)(2,1)}, bf16[2,2,64,1024]{3,2,1,0:T(8,128)(2,1)S(1)}, u32[]{:S(2)}, u32[]{:S(2)}) %collective-permute-start) | collective-permute-done | bytes 524320 | tf_op jit(solution)/shard_map/ppermute | solution.py:27
  11.3 1.5 %collective-permute-start.3 = (bf16[2,2,64,1024]{3,2,1,0:T(8,128)(2,1)S(1)}, bf16[2,2,64,1024]{3,2,1,0:T(8,128)(2,1)S(1)}, u32[]{:S(2)}, u32[]{:S(2)}) collective-permute-start(bf16[2,2,64,1024]{3,2,1,0:T(8,128)(2,1)S(1)} %collective-permute-done.own.refs_2_.refs_0_), channel_id=1, source_target_pairs={{0,16},{1,17},{2,18},{3,19},{4,20},{5,21},{6,22},{7,23},{8,24},{9,... | collective-permute-start | bytes 1572872 | tf_op jit(solution)/shard_map/ppermute | solution.py:27
  12.8 4.1 %collective-permute-start.1 = (bf16[2,2,64,1024]{3,2,1,0:T(8,128)(2,1)S(1)}, bf16[2,2,64,1024]{3,2,1,0:T(8,128)(2,1)S(1)}, u32[]{:S(2)}, u32[]{:S(2)}) collective-permute-start(bf16[2,2,64,1024]{3,2,1,0:T(8,128)(2,1)S(1)} %collective-permute-done.own.refs_2_.refs_0_), channel_id=1, source_target_pairs={{0,2},{1,3},{2,4},{3,5},{4,6},{5,7},{6,8},{7,9},{8,10},{9,11},{10,... | collective-permute-start | bytes 1572872 | tf_op jit(solution)/shard_map/ppermute | solution.py:27
  16.9 0.0 collective-permute-done.3.other.refs_3_.refs_8_
  16.9 1.9 %collective-permute-start.6 = (bf16[2,2,64,1024]{3,2,1,0:T(8,128)(2,1)S(1)}, bf16[2,2,64,1024]{3,2,1,0:T(8,128)(2,1)S(1)}, u32[]{:S(2)}, u32[]{:S(2)}) collective-permute-start(bf16[2,2,64,1024]{3,2,1,0:T(8,128)(2,1)S(1)} %collective-permute-done.3.other.refs_3_.refs_8_), channel_id=1, source_target_pairs={{0,2},{1,3},{2,4},{3,5},{4,6},{5,7},{6,8},{7,9},{8,10},{9,11},{10,... | collective-permute-start | bytes 1572872 | tf_op jit(solution)/shard_map/ppermute | solution.py:27
  18.8 0.1 pad_add_fusion.info.refs_0_
  18.9 0.6 shard_map.41
  19.4 1.3 %collective-permute-start.4 = (bf16[2,128,1024]{2,1,0:T(8,128)(2,1)S(1)}, bf16[2,128,1024]{2,1,0:T(8,128)(2,1)S(1)}, u32[]{:S(2)}, u32[]{:S(2)}) collective-permute-start(bf16[2,128,1024]{2,1,0:T(8,128)(2,1)S(1)} %shard_map.41), channel_id=1, source_target_pairs={{0,33},{1,0},{2,35},{3,2},{4,37},{5,4},{6,39},{7,6},{8,41},{9,8},{... | collective-permute-start | bytes 1572872 | tf_op jit(solution)/shard_map/ppermute | solution.py:27
  20.7 2.3 %collective-permute-done.1.refs_1_.refs_2_ = bf16[2,2,64,1024]{3,2,1,0:T(8,128)(2,1)S(1)} collective-permute-done((bf16[2,2,64,1024]{3,2,1,0:T(8,128)(2,1)S(1)}, bf16[2,2,64,1024]{3,2,1,0:T(8,128)(2,1)S(1)}, u32[]{:S(2)}, u32[]{:S(2)}) %collective-permute-start.1) | collective-permute-done | bytes 524320 | tf_op jit(solution)/shard_map/ppermute | solution.py:27
  23.0 3.4 %collective-permute-start.2 = (bf16[2,2,64,1024]{3,2,1,0:T(8,128)(2,1)S(1)}, bf16[2,2,64,1024]{3,2,1,0:T(8,128)(2,1)S(1)}, u32[]{:S(2)}, u32[]{:S(2)}) collective-permute-start(bf16[2,2,64,1024]{3,2,1,0:T(8,128)(2,1)S(1)} %collective-permute-done.1.refs_1_.refs_2_), channel_id=1, source_target_pairs={{0,2},{1,3},{2,4},{3,5},{4,6},{5,7},{6,8},{7,9},{8,10},{9,11},{10,... | collective-permute-start | bytes 1572872 | tf_op jit(solution)/shard_map/ppermute | solution.py:27
  26.4 2.2 %collective-permute-done.6.refs_4_.refs_6_.refs_9_ = bf16[2,2,64,1024]{3,2,1,0:T(8,128)(2,1)S(1)} collective-permute-done((bf16[2,2,64,1024]{3,2,1,0:T(8,128)(2,1)S(1)}, bf16[2,2,64,1024]{3,2,1,0:T(8,128)(2,1)S(1)}, u32[]{:S(2)}, u32[]{:S(2)}) %collective-permute-start.6) | collective-permute-done | bytes 524320 | tf_op jit(solution)/shard_map/ppermute | solution.py:27
  28.6 3.1 %collective-permute-start.10 = (bf16[2,2,64,1024]{3,2,1,0:T(8,128)(2,1)S(1)}, bf16[2,2,64,1024]{3,2,1,0:T(8,128)(2,1)S(1)}, u32[]{:S(2)}, u32[]{:S(2)}) collective-permute-start(bf16[2,2,64,1024]{3,2,1,0:T(8,128)(2,1)S(1)} %collective-permute-done.6.refs_4_.refs_6_.refs_9_), channel_id=1, source_target_pairs={{0,2},{1,3},{2,4},{3,5},{4,6},{5,7},{6,8},{7,9},{8,10},{9,11},{10,... | collective-permute-start | bytes 1572872 | tf_op jit(solution)/shard_map/ppermute | solution.py:27
  31.7 2.5 %collective-permute-done.4.refs_1_.a_ref = bf16[2,128,1024]{2,1,0:T(8,128)(2,1)S(1)} collective-permute-done((bf16[2,128,1024]{2,1,0:T(8,128)(2,1)S(1)}, bf16[2,128,1024]{2,1,0:T(8,128)(2,1)S(1)}, u32[]{:S(2)}, u32[]{:S(2)}) %collective-permute-start.4) | collective-permute-done | bytes 524320 | tf_op jit(solution)/shard_map/ppermute | solution.py:27
  34.2 0.9 shard_map.42.refs_10_
  35.1 0.0 collective-permute-done.2.refs_4_.refs_0_.refs_3_
  35.1 3.6 %collective-permute-start.5 = (bf16[2,2,64,1024]{3,2,1,0:T(8,128)(2,1)S(1)}, bf16[2,2,64,1024]{3,2,1,0:T(8,128)(2,1)S(1)}, u32[]{:S(2)}, u32[]{:S(2)}) collective-permute-start(bf16[2,2,64,1024]{3,2,1,0:T(8,128)(2,1)S(1)} %collective-permute-done.2.refs_4_.refs_0_.refs_3_), channel_id=1, source_target_pairs={{0,2},{1,3},{2,4},{3,5},{4,6},{5,7},{6,8},{7,9},{8,10},{9,11},{10,... | collective-permute-start | bytes 1572872 | tf_op jit(solution)/shard_map/ppermute | solution.py:27
  38.7 0.0 collective-permute-done.8.refs_5_.refs_7_.refs_10_
  38.8 0.0 collective-permute-done.7.refs_2_.refs_3_
  38.8 0.7 shard_map.43
  39.4 0.1 collective-permute-start.9
  39.5 1.2 %collective-permute-start.13 = (bf16[2,2,64,1024]{3,2,1,0:T(8,128)(2,1)S(1)}, bf16[2,2,64,1024]{3,2,1,0:T(8,128)(2,1)S(1)}, u32[]{:S(2)}, u32[]{:S(2)}) collective-permute-start(bf16[2,2,64,1024]{3,2,1,0:T(8,128)(2,1)S(1)} %collective-permute-done.2.refs_4_.refs_0_.refs_3_), channel_id=1, source_target_pairs={{0,16},{1,17},{2,18},{3,19},{4,20},{5,21},{6,22},{7,23},{8,24},{9,... | collective-permute-start | bytes 1572872 | tf_op jit(solution)/shard_map/ppermute | solution.py:27
  40.8 0.0 collective-permute-done.10.refs_8_.refs_2_.refs_11_
  40.8 0.9 collective-permute-start.12
  41.7 2.1 %collective-permute-start.11 = (bf16[2,2,64,1024]{3,2,1,0:T(8,128)(2,1)S(1)}, bf16[2,2,64,1024]{3,2,1,0:T(8,128)(2,1)S(1)}, u32[]{:S(2)}, u32[]{:S(2)}) collective-permute-start(bf16[2,2,64,1024]{3,2,1,0:T(8,128)(2,1)S(1)} %collective-permute-done.10.refs_8_.refs_2_.refs_11_), channel_id=1, source_target_pairs={{0,2},{1,3},{2,4},{3,5},{4,6},{5,7},{6,8},{7,9},{8,10},{9,11},{10,... | collective-permute-start | bytes 1572872 | tf_op jit(solution)/shard_map/ppermute | solution.py:27
  43.7 1.7 %collective-permute-done.5.refs_2_.refs_5_.refs_0_ = bf16[2,2,64,1024]{3,2,1,0:T(8,128)(2,1)S(1)} collective-permute-done((bf16[2,2,64,1024]{3,2,1,0:T(8,128)(2,1)S(1)}, bf16[2,2,64,1024]{3,2,1,0:T(8,128)(2,1)S(1)}, u32[]{:S(2)}, u32[]{:S(2)}) %collective-permute-start.5) | collective-permute-done | bytes 524320 | tf_op jit(solution)/shard_map/ppermute | solution.py:27
  45.5 2.1 %collective-permute-done.9.near = bf16[3,2,128,128]{3,2,1,0:T(8,128)(2,1)S(1)} collective-permute-done((bf16[3,2,128,128]{3,2,1,0:T(8,128)(2,1)S(1)}, bf16[3,2,128,128]{3,2,1,0:T(8,128)(2,1)S(1)}, u32[]{:S(2)}, u32[]{:S(2)}) %collective-permute-start.9) | collective-permute-done | bytes 196640 | tf_op jit(solution)/shard_map/ppermute | solution.py:27
  47.6 1.0 %collective-permute-start.16 = (bf16[2,2,64,1024]{3,2,1,0:T(8,128)(2,1)S(1)}, bf16[2,2,64,1024]{3,2,1,0:T(8,128)(2,1)S(1)}, u32[]{:S(2)}, u32[]{:S(2)}) collective-permute-start(bf16[2,2,64,1024]{3,2,1,0:T(8,128)(2,1)S(1)} %collective-permute-done.5.refs_2_.refs_5_.refs_0_), channel_id=1, source_target_pairs={{0,2},{1,3},{2,4},{3,5},{4,6},{5,7},{6,8},{7,9},{8,10},{9,11},{10,... | collective-permute-start | bytes 1572872 | tf_op jit(solution)/shard_map/ppermute | solution.py:27
  48.6 0.0 collective-permute-done.13.refs_9_.refs_3_.refs_12_
  48.6 0.0 collective-permute-done.12.refs_5_.refs_1_.refs_4_
  48.6 0.6 shard_map.46
  49.2 1.3 %collective-permute-start.17 = (bf16[2,2,128,128]{3,2,1,0:T(8,128)(2,1)S(1)}, bf16[2,2,128,128]{3,2,1,0:T(8,128)(2,1)S(1)}, u32[]{:S(2)}, u32[]{:S(2)}) collective-permute-start(bf16[2,2,128,128]{3,2,1,0:T(8,128)(2,1)S(1)} %shard_map.46), channel_id=1, source_target_pairs={{0,33},{1,0},{2,35},{3,2},{4,37},{5,4},{6,39},{7,6},{8,41},{9,8},{... | collective-permute-start | bytes 393224 | tf_op jit(solution)/shard_map/ppermute | solution.py:27
  50.5 1.4 %collective-permute-start.15 = (bf16[2,2,64,1024]{3,2,1,0:T(8,128)(2,1)S(1)}, bf16[2,2,64,1024]{3,2,1,0:T(8,128)(2,1)S(1)}, u32[]{:S(2)}, u32[]{:S(2)}) collective-permute-start(bf16[2,2,64,1024]{3,2,1,0:T(8,128)(2,1)S(1)} %collective-permute-done.5.refs_2_.refs_5_.refs_0_), channel_id=1, source_target_pairs={{0,16},{1,17},{2,18},{3,19},{4,20},{5,21},{6,22},{7,23},{8,24},{9,... | collective-permute-start | bytes 1572872 | tf_op jit(solution)/shard_map/ppermute | solution.py:27
  52.0 1.3 %shard_map.44.refs_6_ = f32[256,1024]{1,0:T(8,128)S(1)} custom-call(s32[6]{0:T(128)S(1)} %pad_add_fusion.info.refs_0_, bf16[2,128,1024]{2,1,0:T(8,128)(2,1)S(1)} %collective-permute-done.4.refs_1_.a_ref, bf16[2,2,64,1024]{3,2,1,0:T(8,128)(2,1)S(1)} %collective-permute-done.1.refs_1_.refs_2_, ...), custom_call_target="tpu_custom_call" | custom-call | flops 1 | bytes 1048576 | tf_op jit(solution)/shard_map/pallas_call | solution.py:75
  53.3 0.0 collective-permute-done.11.refs_4_.refs_13_.refs_3_
  53.3 0.1 collective-permute-start.14
  53.4 4.2 %collective-permute-done.17.middle = bf16[2,2,128,128]{3,2,1,0:T(8,128)(2,1)S(1)} collective-permute-done((bf16[2,2,128,128]{3,2,1,0:T(8,128)(2,1)S(1)}, bf16[2,2,128,128]{3,2,1,0:T(8,128)(2,1)S(1)}, u32[]{:S(2)}, u32[]{:S(2)}) %collective-permute-start.17) | collective-permute-done | bytes 131104 | tf_op jit(solution)/shard_map/ppermute | solution.py:27
  57.6 0.0 collective-permute-done.16.refs_7_.refs_2_
  57.6 0.9 %collective-permute-start.18 = (bf16[2,2,64,1024]{3,2,1,0:T(8,128)(2,1)S(1)}, bf16[2,2,64,1024]{3,2,1,0:T(8,128)(2,1)S(1)}, u32[]{:S(2)}, u32[]{:S(2)}) collective-permute-start(bf16[2,2,64,1024]{3,2,1,0:T(8,128)(2,1)S(1)} %collective-permute-done.16.refs_7_.refs_2_), channel_id=1, source_target_pairs={{0,16},{1,17},{2,18},{3,19},{4,20},{5,21},{6,22},{7,23},{8,24},{9,... | collective-permute-start | bytes 1572872 | tf_op jit(solution)/shard_map/ppermute | solution.py:27
  58.5 1.0 %shard_map.45.acc = f32[256,1024]{1,0:T(8,128)S(1)} custom-call(s32[6]{0:T(128)S(1)} %pad_add_fusion.info.refs_0_, bf16[2,128,1024]{2,1,0:T(8,128)(2,1)S(1)} %collective-permute-done.4.refs_1_.a_ref, bf16[2,2,64,1024]{3,2,1,0:T(8,128)(2,1)S(1)} %collective-permute-done.5.refs_2_.refs_5_.refs_0_, ...), custom_call_target="tpu_custom_call" | custom-call | flops 1 | bytes 1048576 | tf_op jit(solution)/shard_map/pallas_call | solution.py:75
  59.5 0.5 collective-permute-done.18.refs_15_.refs_5_
  60.1 0.7 shard_map.48
  60.7 1.3 %collective-permute-start.19 = (bf16[3,2,128,128]{3,2,1,0:T(8,128)(2,1)S(1)}, bf16[3,2,128,128]{3,2,1,0:T(8,128)(2,1)S(1)}, u32[]{:S(2)}, u32[]{:S(2)}) collective-permute-start(bf16[3,2,128,128]{3,2,1,0:T(8,128)(2,1)S(1)} %shard_map.48), channel_id=1, source_target_pairs={{0,33},{1,0},{2,35},{3,2},{4,37},{5,4},{6,39},{7,6},{8,41},{9,8},{... | collective-permute-start | bytes 589832 | tf_op jit(solution)/shard_map/ppermute | solution.py:27
  62.0 2.1 %shard_map.47 = (bf16[2,64,1024]{2,1,0:T(8,128)(2,1)S(1)}, bf16[2,64,1024]{2,1,0:T(8,128)(2,1)S(1)}, f32[256,1024]{1,0:T(8,128)S(1)}) custom-call(s32[6]{0:T(128)S(1)} %pad_add_fusion.info.refs_0_, bf16[2,128,1024]{2,1,0:T(8,128)(2,1)S(1)} %collective-permute-done.4.refs_1_.a_ref, f32[256,1024]{1,0:T(8,128)S(1)} %shard_map.45.acc, ...), custom_call_target="tpu_custom_call" | custom-call | flops 3000000000 | bytes 1048576 | tf_op jit(solution)/shard_map/pallas_call | solution.py:75
  64.2 6.7 %collective-permute-done.19.late = bf16[3,2,128,128]{3,2,1,0:T(8,128)(2,1)S(1)} collective-permute-done((bf16[3,2,128,128]{3,2,1,0:T(8,128)(2,1)S(1)}, bf16[3,2,128,128]{3,2,1,0:T(8,128)(2,1)S(1)}, u32[]{:S(2)}, u32[]{:S(2)}) %collective-permute-start.19) | collective-permute-done | bytes 196640 | tf_op jit(solution)/shard_map/ppermute | solution.py:27
  70.9 1.0 %shard_map.49.own = f32[1,128]{1,0:T(1,128)S(1)} custom-call(s32[6]{0:T(128)S(1)} %pad_add_fusion.info.refs_0_, f32[256,1024]{1,0:T(8,128)S(1)} %get-tuple-element.26.product, bf16[3,2,128,128]{3,2,1,0:T(8,128)(2,1)S(1)} %collective-permute-done.9.near, bf16[2,2,128,128]{3,2,1,0:T(8,128)(2,1)S(1)} %collective-permute-done.17.middle, ...), custom_call_target="tpu_custom_call" | custom-call | flops 1 | bytes 1048576 | tf_op jit(solution)/shard_map/pallas_call | solution.py:75
  71.8 2.3 %collective-permute-start.21 = (f32[1,128]{1,0:T(1,128)S(1)}, f32[1,128]{1,0:T(1,128)S(1)}, u32[]{:S(2)}, u32[]{:S(2)}) collective-permute-start(f32[1,128]{1,0:T(1,128)S(1)} %shard_map.49.own), channel_id=1, source_target_pairs={{0,14},{1,15},{2,0},{3,1},{4,2},{5,3},{6,4},{7,5},{8,6},{9,7},{10,... | collective-permute-start | bytes 1544 | tf_op jit(solution)/shard_map/ppermute | solution.py:27
  74.2 2.1 %collective-permute-start.25 = (bf16[2,64,1024]{2,1,0:T(8,128)(2,1)S(1)}, bf16[2,64,1024]{2,1,0:T(8,128)(2,1)S(1)}, u32[]{:S(2)}, u32[]{:S(2)}) collective-permute-start(bf16[2,64,1024]{2,1,0:T(8,128)(2,1)S(1)} %get-tuple-element.32), channel_id=1, source_target_pairs={{0,129},{1,113},{2,131},{3,115},{4,133},{5,117},{6,135},{7,119},{8... | collective-permute-start | bytes 786440 | tf_op jit(solution)/shard_map/ppermute | solution.py:27
  76.2 0.0 collective-permute-done.21.above
  76.2 1.8 %collective-permute-done.20.below = f32[1,128]{1,0:T(1,128)S(1)} collective-permute-done((f32[1,128]{1,0:T(1,128)S(1)}, f32[1,128]{1,0:T(1,128)S(1)}, u32[]{:S(2)}, u32[]{:S(2)}) %collective-permute-start.20) | collective-permute-done | bytes 544 | tf_op jit(solution)/shard_map/ppermute | solution.py:27
  78.1 0.5 shard_map.50
  78.6 0.5 collective-permute-start.22
  79.1 4.1 %collective-permute-start.23 = (f32[1,128]{1,0:T(1,128)S(1)}, f32[1,128]{1,0:T(1,128)S(1)}, u32[]{:S(2)}, u32[]{:S(2)}) collective-permute-start(f32[1,128]{1,0:T(1,128)S(1)} %get-tuple-element.30), channel_id=1, source_target_pairs={{0,10},{1,11},{2,12},{3,13},{4,14},{5,15},{6,0},{7,1},{8,2},{9,3},... | collective-permute-start | bytes 1544 | tf_op jit(solution)/shard_map/ppermute | solution.py:27
  83.2 0.9 collective-permute-done.22
  84.1 0.0 collective-permute-done.23
  84.1 0.0 collective-permute-done.24
  84.1 0.0 collective-permute-done.25
  84.1 1.0 %collective-permute-start.27 = (f32[1,128]{1,0:T(1,128)S(1)}, f32[1,128]{1,0:T(1,128)S(1)}, u32[]{:S(2)}, u32[]{:S(2)}) collective-permute-start(f32[1,128]{1,0:T(1,128)S(1)} %add_add_fusion), channel_id=1, source_target_pairs={{0,129},{1,113},{2,131},{3,115},{4,133},{5,117},{6,135},{7,119},{8... | collective-permute-start | bytes 1544 | tf_op jit(solution)/shard_map/ppermute | solution.py:27
  85.2 7.5 %collective-permute-start.26 = (f32[1,128]{1,0:T(1,128)S(1)}, f32[1,128]{1,0:T(1,128)S(1)}, u32[]{:S(2)}, u32[]{:S(2)}) collective-permute-start(f32[1,128]{1,0:T(1,128)S(1)} %add_add_fusion), channel_id=1, source_target_pairs={{0,128},{1,112},{2,130},{3,114},{4,132},{5,116},{6,134},{7,118},{8... | collective-permute-start | bytes 1544 | tf_op jit(solution)/shard_map/ppermute | solution.py:27
  92.7 0.9 maximum_select_fusion
  93.6 0.0 collective-permute-done.27
  93.6 0.1 reshape.77
  93.7 0.6 broadcast_multiply_fusion
  (12 shorter events, 0.1 us)
Async XLA Ops:
  0.6 16.2 %copy-start = (s32[2,1,4]{2,1,0:T(1,128)S(1)}, s32[2,1,4]{2,1,0:T(1,128)}, u32[]{:S(2)}) copy-start(s32[2,1,4]{2,1,0:T(1,128)} %param.3) | copy-start | bytes 100
  0.6 10.6 %collective-permute-start = (bf16[2,2,64,1024]{3,2,1,0:T(8,128)(2,1)}, bf16[2,2,64,1024]{3,2,1,0:T(8,128)(2,1)S(1)}, u32[]{:S(2)}, u32[]{:S(2)}) collective-permute-start(bf16[2,2,64,1024]{3,2,1,0:T(8,128)(2,1)} %bitcast.15), channel_id=1, source_target_pairs={{0,128},{1,144},{2,130},{3,146},{4,132},{5,148},{6,134},{7,150},{8... | collective-permute-start | bytes 1572872 | tf_op jit(solution)/shard_map/ppermute | solution.py:27
  11.3 5.6 %collective-permute-start.3 = (bf16[2,2,64,1024]{3,2,1,0:T(8,128)(2,1)S(1)}, bf16[2,2,64,1024]{3,2,1,0:T(8,128)(2,1)S(1)}, u32[]{:S(2)}, u32[]{:S(2)}) collective-permute-start(bf16[2,2,64,1024]{3,2,1,0:T(8,128)(2,1)S(1)} %collective-permute-done.own.refs_2_.refs_0_), channel_id=1, source_target_pairs={{0,16},{1,17},{2,18},{3,19},{4,20},{5,21},{6,22},{7,23},{8,24},{9,... | collective-permute-start | bytes 1572872 | tf_op jit(solution)/shard_map/ppermute | solution.py:27
  12.8 10.2 %collective-permute-start.1 = (bf16[2,2,64,1024]{3,2,1,0:T(8,128)(2,1)S(1)}, bf16[2,2,64,1024]{3,2,1,0:T(8,128)(2,1)S(1)}, u32[]{:S(2)}, u32[]{:S(2)}) collective-permute-start(bf16[2,2,64,1024]{3,2,1,0:T(8,128)(2,1)S(1)} %collective-permute-done.own.refs_2_.refs_0_), channel_id=1, source_target_pairs={{0,2},{1,3},{2,4},{3,5},{4,6},{5,7},{6,8},{7,9},{8,10},{9,11},{10,... | collective-permute-start | bytes 1572872 | tf_op jit(solution)/shard_map/ppermute | solution.py:27
  16.9 11.7 %collective-permute-start.6 = (bf16[2,2,64,1024]{3,2,1,0:T(8,128)(2,1)S(1)}, bf16[2,2,64,1024]{3,2,1,0:T(8,128)(2,1)S(1)}, u32[]{:S(2)}, u32[]{:S(2)}) collective-permute-start(bf16[2,2,64,1024]{3,2,1,0:T(8,128)(2,1)S(1)} %collective-permute-done.3.other.refs_3_.refs_8_), channel_id=1, source_target_pairs={{0,2},{1,3},{2,4},{3,5},{4,6},{5,7},{6,8},{7,9},{8,10},{9,11},{10,... | collective-permute-start | bytes 1572872 | tf_op jit(solution)/shard_map/ppermute | solution.py:27
  19.4 14.8 %collective-permute-start.4 = (bf16[2,128,1024]{2,1,0:T(8,128)(2,1)S(1)}, bf16[2,128,1024]{2,1,0:T(8,128)(2,1)S(1)}, u32[]{:S(2)}, u32[]{:S(2)}) collective-permute-start(bf16[2,128,1024]{2,1,0:T(8,128)(2,1)S(1)} %shard_map.41), channel_id=1, source_target_pairs={{0,33},{1,0},{2,35},{3,2},{4,37},{5,4},{6,39},{7,6},{8,41},{9,8},{... | collective-permute-start | bytes 1572872 | tf_op jit(solution)/shard_map/ppermute | solution.py:27
  23.0 12.1 %collective-permute-start.2 = (bf16[2,2,64,1024]{3,2,1,0:T(8,128)(2,1)S(1)}, bf16[2,2,64,1024]{3,2,1,0:T(8,128)(2,1)S(1)}, u32[]{:S(2)}, u32[]{:S(2)}) collective-permute-start(bf16[2,2,64,1024]{3,2,1,0:T(8,128)(2,1)S(1)} %collective-permute-done.1.refs_1_.refs_2_), channel_id=1, source_target_pairs={{0,2},{1,3},{2,4},{3,5},{4,6},{5,7},{6,8},{7,9},{8,10},{9,11},{10,... | collective-permute-start | bytes 1572872 | tf_op jit(solution)/shard_map/ppermute | solution.py:27
  26.4 12.3 %collective-permute-start.8 = (bf16[2,2,64,1024]{3,2,1,0:T(8,128)(2,1)S(1)}, bf16[2,2,64,1024]{3,2,1,0:T(8,128)(2,1)S(1)}, u32[]{:S(2)}, u32[]{:S(2)}) collective-permute-start(bf16[2,2,64,1024]{3,2,1,0:T(8,128)(2,1)S(1)} %collective-permute-done.1.refs_1_.refs_2_), channel_id=1, source_target_pairs={{0,16},{1,17},{2,18},{3,19},{4,20},{5,21},{6,22},{7,23},{8,24},{9,... | collective-permute-start | bytes 1572872 | tf_op jit(solution)/shard_map/ppermute | solution.py:27
  28.6 12.2 %collective-permute-start.10 = (bf16[2,2,64,1024]{3,2,1,0:T(8,128)(2,1)S(1)}, bf16[2,2,64,1024]{3,2,1,0:T(8,128)(2,1)S(1)}, u32[]{:S(2)}, u32[]{:S(2)}) collective-permute-start(bf16[2,2,64,1024]{3,2,1,0:T(8,128)(2,1)S(1)} %collective-permute-done.6.refs_4_.refs_6_.refs_9_), channel_id=1, source_target_pairs={{0,2},{1,3},{2,4},{3,5},{4,6},{5,7},{6,8},{7,9},{8,10},{9,11},{10,... | collective-permute-start | bytes 1572872 | tf_op jit(solution)/shard_map/ppermute | solution.py:27
  31.7 7.0 %collective-permute-start.7 = (bf16[2,2,64,1024]{3,2,1,0:T(8,128)(2,1)S(1)}, bf16[2,2,64,1024]{3,2,1,0:T(8,128)(2,1)S(1)}, u32[]{:S(2)}, u32[]{:S(2)}) collective-permute-start(bf16[2,2,64,1024]{3,2,1,0:T(8,128)(2,1)S(1)} %collective-permute-done.6.refs_4_.refs_6_.refs_9_), channel_id=1, source_target_pairs={{0,16},{1,17},{2,18},{3,19},{4,20},{5,21},{6,22},{7,23},{8,24},{9,... | collective-permute-start | bytes 1572872 | tf_op jit(solution)/shard_map/ppermute | solution.py:27
  35.1 10.4 %collective-permute-start.5 = (bf16[2,2,64,1024]{3,2,1,0:T(8,128)(2,1)S(1)}, bf16[2,2,64,1024]{3,2,1,0:T(8,128)(2,1)S(1)}, u32[]{:S(2)}, u32[]{:S(2)}) collective-permute-start(bf16[2,2,64,1024]{3,2,1,0:T(8,128)(2,1)S(1)} %collective-permute-done.2.refs_4_.refs_0_.refs_3_), channel_id=1, source_target_pairs={{0,2},{1,3},{2,4},{3,5},{4,6},{5,7},{6,8},{7,9},{8,10},{9,11},{10,... | collective-permute-start | bytes 1572872 | tf_op jit(solution)/shard_map/ppermute | solution.py:27
  39.4 8.1 %collective-permute-start.9 = (bf16[3,2,128,128]{3,2,1,0:T(8,128)(2,1)S(1)}, bf16[3,2,128,128]{3,2,1,0:T(8,128)(2,1)S(1)}, u32[]{:S(2)}, u32[]{:S(2)}) collective-permute-start(bf16[3,2,128,128]{3,2,1,0:T(8,128)(2,1)S(1)} %shard_map.43), channel_id=1, source_target_pairs={{0,33},{1,0},{2,35},{3,2},{4,37},{5,4},{6,39},{7,6},{8,41},{9,8},{... | collective-permute-start | bytes 589832 | tf_op jit(solution)/shard_map/ppermute | solution.py:27
  39.5 9.1 %collective-permute-start.13 = (bf16[2,2,64,1024]{3,2,1,0:T(8,128)(2,1)S(1)}, bf16[2,2,64,1024]{3,2,1,0:T(8,128)(2,1)S(1)}, u32[]{:S(2)}, u32[]{:S(2)}) collective-permute-start(bf16[2,2,64,1024]{3,2,1,0:T(8,128)(2,1)S(1)} %collective-permute-done.2.refs_4_.refs_0_.refs_3_), channel_id=1, source_target_pairs={{0,16},{1,17},{2,18},{3,19},{4,20},{5,21},{6,22},{7,23},{8,24},{9,... | collective-permute-start | bytes 1572872 | tf_op jit(solution)/shard_map/ppermute | solution.py:27
  40.8 7.8 %collective-permute-start.12 = (bf16[2,2,64,1024]{3,2,1,0:T(8,128)(2,1)S(1)}, bf16[2,2,64,1024]{3,2,1,0:T(8,128)(2,1)S(1)}, u32[]{:S(2)}, u32[]{:S(2)}) collective-permute-start(bf16[2,2,64,1024]{3,2,1,0:T(8,128)(2,1)S(1)} %collective-permute-done.10.refs_8_.refs_2_.refs_11_), channel_id=1, source_target_pairs={{0,16},{1,17},{2,18},{3,19},{4,20},{5,21},{6,22},{7,23},{8,24},{9,... | collective-permute-start | bytes 1572872 | tf_op jit(solution)/shard_map/ppermute | solution.py:27
  41.7 11.6 %collective-permute-start.11 = (bf16[2,2,64,1024]{3,2,1,0:T(8,128)(2,1)S(1)}, bf16[2,2,64,1024]{3,2,1,0:T(8,128)(2,1)S(1)}, u32[]{:S(2)}, u32[]{:S(2)}) collective-permute-start(bf16[2,2,64,1024]{3,2,1,0:T(8,128)(2,1)S(1)} %collective-permute-done.10.refs_8_.refs_2_.refs_11_), channel_id=1, source_target_pairs={{0,2},{1,3},{2,4},{3,5},{4,6},{5,7},{6,8},{7,9},{8,10},{9,11},{10,... | collective-permute-start | bytes 1572872 | tf_op jit(solution)/shard_map/ppermute | solution.py:27
  47.6 10.0 %collective-permute-start.16 = (bf16[2,2,64,1024]{3,2,1,0:T(8,128)(2,1)S(1)}, bf16[2,2,64,1024]{3,2,1,0:T(8,128)(2,1)S(1)}, u32[]{:S(2)}, u32[]{:S(2)}) collective-permute-start(bf16[2,2,64,1024]{3,2,1,0:T(8,128)(2,1)S(1)} %collective-permute-done.5.refs_2_.refs_5_.refs_0_), channel_id=1, source_target_pairs={{0,2},{1,3},{2,4},{3,5},{4,6},{5,7},{6,8},{7,9},{8,10},{9,11},{10,... | collective-permute-start | bytes 1572872 | tf_op jit(solution)/shard_map/ppermute | solution.py:27
  49.2 8.3 %collective-permute-start.17 = (bf16[2,2,128,128]{3,2,1,0:T(8,128)(2,1)S(1)}, bf16[2,2,128,128]{3,2,1,0:T(8,128)(2,1)S(1)}, u32[]{:S(2)}, u32[]{:S(2)}) collective-permute-start(bf16[2,2,128,128]{3,2,1,0:T(8,128)(2,1)S(1)} %shard_map.46), channel_id=1, source_target_pairs={{0,33},{1,0},{2,35},{3,2},{4,37},{5,4},{6,39},{7,6},{8,41},{9,8},{... | collective-permute-start | bytes 393224 | tf_op jit(solution)/shard_map/ppermute | solution.py:27
  50.5 8.0 %collective-permute-start.15 = (bf16[2,2,64,1024]{3,2,1,0:T(8,128)(2,1)S(1)}, bf16[2,2,64,1024]{3,2,1,0:T(8,128)(2,1)S(1)}, u32[]{:S(2)}, u32[]{:S(2)}) collective-permute-start(bf16[2,2,64,1024]{3,2,1,0:T(8,128)(2,1)S(1)} %collective-permute-done.5.refs_2_.refs_5_.refs_0_), channel_id=1, source_target_pairs={{0,16},{1,17},{2,18},{3,19},{4,20},{5,21},{6,22},{7,23},{8,24},{9,... | collective-permute-start | bytes 1572872 | tf_op jit(solution)/shard_map/ppermute | solution.py:27
  53.3 5.3 %collective-permute-start.14 = (bf16[2,2,64,1024]{3,2,1,0:T(8,128)(2,1)S(1)}, bf16[2,2,64,1024]{3,2,1,0:T(8,128)(2,1)S(1)}, u32[]{:S(2)}, u32[]{:S(2)}) collective-permute-start(bf16[2,2,64,1024]{3,2,1,0:T(8,128)(2,1)S(1)} %collective-permute-done.11.refs_4_.refs_13_.refs_3_), channel_id=1, source_target_pairs={{0,16},{1,17},{2,18},{3,19},{4,20},{5,21},{6,22},{7,23},{8,24},{9,... | collective-permute-start | bytes 1572872 | tf_op jit(solution)/shard_map/ppermute | solution.py:27
  57.6 2.5 %collective-permute-start.18 = (bf16[2,2,64,1024]{3,2,1,0:T(8,128)(2,1)S(1)}, bf16[2,2,64,1024]{3,2,1,0:T(8,128)(2,1)S(1)}, u32[]{:S(2)}, u32[]{:S(2)}) collective-permute-start(bf16[2,2,64,1024]{3,2,1,0:T(8,128)(2,1)S(1)} %collective-permute-done.16.refs_7_.refs_2_), channel_id=1, source_target_pairs={{0,16},{1,17},{2,18},{3,19},{4,20},{5,21},{6,22},{7,23},{8,24},{9,... | collective-permute-start | bytes 1572872 | tf_op jit(solution)/shard_map/ppermute | solution.py:27
  60.7 10.1 %collective-permute-start.19 = (bf16[3,2,128,128]{3,2,1,0:T(8,128)(2,1)S(1)}, bf16[3,2,128,128]{3,2,1,0:T(8,128)(2,1)S(1)}, u32[]{:S(2)}, u32[]{:S(2)}) collective-permute-start(bf16[3,2,128,128]{3,2,1,0:T(8,128)(2,1)S(1)} %shard_map.48), channel_id=1, source_target_pairs={{0,33},{1,0},{2,35},{3,2},{4,37},{5,4},{6,39},{7,6},{8,41},{9,8},{... | collective-permute-start | bytes 589832 | tf_op jit(solution)/shard_map/ppermute | solution.py:27
  71.8 4.4 %collective-permute-start.21 = (f32[1,128]{1,0:T(1,128)S(1)}, f32[1,128]{1,0:T(1,128)S(1)}, u32[]{:S(2)}, u32[]{:S(2)}) collective-permute-start(f32[1,128]{1,0:T(1,128)S(1)} %shard_map.49.own), channel_id=1, source_target_pairs={{0,14},{1,15},{2,0},{3,1},{4,2},{5,3},{6,4},{7,5},{8,6},{9,7},{10,... | collective-permute-start | bytes 1544 | tf_op jit(solution)/shard_map/ppermute | solution.py:27
  74.2 3.9 %collective-permute-start.20 = (f32[1,128]{1,0:T(1,128)S(1)}, f32[1,128]{1,0:T(1,128)S(1)}, u32[]{:S(2)}, u32[]{:S(2)}) collective-permute-start(f32[1,128]{1,0:T(1,128)S(1)} %shard_map.49.own), channel_id=1, source_target_pairs={{0,2},{1,3},{2,4},{3,5},{4,6},{5,7},{6,8},{7,9},{8,10},{9,11},{10,... | collective-permute-start | bytes 1544 | tf_op jit(solution)/shard_map/ppermute | solution.py:27
  74.2 9.9 %collective-permute-start.24 = (bf16[2,64,1024]{2,1,0:T(8,128)(2,1)S(1)}, bf16[2,64,1024]{2,1,0:T(8,128)(2,1)S(1)}, u32[]{:S(2)}, u32[]{:S(2)}) collective-permute-start(bf16[2,64,1024]{2,1,0:T(8,128)(2,1)S(1)} %get-tuple-element.31), channel_id=1, source_target_pairs={{0,128},{1,112},{2,130},{3,114},{4,132},{5,116},{6,134},{7,118},{8... | collective-permute-start | bytes 786440 | tf_op jit(solution)/shard_map/ppermute | solution.py:27
  74.2 9.9 %collective-permute-start.25 = (bf16[2,64,1024]{2,1,0:T(8,128)(2,1)S(1)}, bf16[2,64,1024]{2,1,0:T(8,128)(2,1)S(1)}, u32[]{:S(2)}, u32[]{:S(2)}) collective-permute-start(bf16[2,64,1024]{2,1,0:T(8,128)(2,1)S(1)} %get-tuple-element.32), channel_id=1, source_target_pairs={{0,129},{1,113},{2,131},{3,115},{4,133},{5,117},{6,135},{7,119},{8... | collective-permute-start | bytes 786440 | tf_op jit(solution)/shard_map/ppermute | solution.py:27
  78.6 5.5 %collective-permute-start.22 = (f32[1,128]{1,0:T(1,128)S(1)}, f32[1,128]{1,0:T(1,128)S(1)}, u32[]{:S(2)}, u32[]{:S(2)}) collective-permute-start(f32[1,128]{1,0:T(1,128)S(1)} %get-tuple-element.29), channel_id=1, source_target_pairs={{0,6},{1,7},{2,8},{3,9},{4,10},{5,11},{6,12},{7,13},{8,14},{9,15},... | collective-permute-start | bytes 1544 | tf_op jit(solution)/shard_map/ppermute | solution.py:27
  79.1 5.0 %collective-permute-start.23 = (f32[1,128]{1,0:T(1,128)S(1)}, f32[1,128]{1,0:T(1,128)S(1)}, u32[]{:S(2)}, u32[]{:S(2)}) collective-permute-start(f32[1,128]{1,0:T(1,128)S(1)} %get-tuple-element.30), channel_id=1, source_target_pairs={{0,10},{1,11},{2,12},{3,13},{4,14},{5,15},{6,0},{7,1},{8,2},{9,3},... | collective-permute-start | bytes 1544 | tf_op jit(solution)/shard_map/ppermute | solution.py:27
  84.1 9.4 %collective-permute-start.27 = (f32[1,128]{1,0:T(1,128)S(1)}, f32[1,128]{1,0:T(1,128)S(1)}, u32[]{:S(2)}, u32[]{:S(2)}) collective-permute-start(f32[1,128]{1,0:T(1,128)S(1)} %add_add_fusion), channel_id=1, source_target_pairs={{0,129},{1,113},{2,131},{3,115},{4,133},{5,117},{6,135},{7,119},{8... | collective-permute-start | bytes 1544 | tf_op jit(solution)/shard_map/ppermute | solution.py:27
  85.2 8.4 %collective-permute-start.26 = (f32[1,128]{1,0:T(1,128)S(1)}, f32[1,128]{1,0:T(1,128)S(1)}, u32[]{:S(2)}, u32[]{:S(2)}) collective-permute-start(f32[1,128]{1,0:T(1,128)S(1)} %add_add_fusion), channel_id=1, source_target_pairs={{0,128},{1,112},{2,130},{3,114},{4,132},{5,116},{6,134},{7,118},{8... | collective-permute-start | bytes 1544 | tf_op jit(solution)/shard_map/ppermute | solution.py:27

commit v9 on v8

--- a/solution.py
+++ b/solution.py
@@ -175,11 +175,6 @@
     trace[...] = jnp.where(lane == 2 * info[0], re, jnp.where(lane == 2 * info[0] + 1, im, 0.0))
 
 
-def add_kernel(info, below, own, above, two, three):
-    two[...] = own[...] + above[...]
-    three[...] = below[...] + own[...] + above[...]
-
-
 def shards(fields, mom_table):
     rows = fields[:, 0]
     tm, row = lax.axis_index("tm"), lax.axis_index("row")
@@ -239,7 +234,7 @@
 
     below, above = moved(trace, along(1)), moved(trace, along(-1))
     kept, sent = moved(keep, from_hub(0)), moved(send, from_hub(1))
-    two, three = call(add_kernel, info, [below, trace, above], (share, share), WEIGHT)
+    two, three, kept = wall((trace + above, below + trace + above, kept))
     below, above = moved(two, along(3)), moved(three, along(-3))
     trace, kept, sent = wall((below + three + above, kept, sent))
     first, second = moved(trace, from_hub(0)), moved(trace, from_hub(1))

time: 95.5 us -> 95 us (level); the launches traced: 94.3 us -> 94.9 us
  starting transfers between devices: 51 us -> 53.8 us
  waiting for transfers between devices: 31.5 us -> 29.9 us
    ppermute x28, starting transfers between devices: 51 us -> 53.8 us  [moved(): lax.ppermute(block, BOTH, [(index_of(*at), index_of(*route(*at))) for at...]
    ppermute x28, waiting for transfers between devices: 31.5 us -> 29.9 us  [moved(): lax.ppermute(block, BOTH, [(index_of(*at), index_of(*route(*at))) for at...]
    pallas_call x10 -> x9, Pallas kernels: 9.37 us -> 8.83 us  [call(): pl.pallas_call(kernel, out_shape=out_shape, in_specs=[SMEM] + [VMEM] * le...]
  transfers between devices with their start and end apart: 28 -> 28, of which waited for: 11 -> 12; matrix products, arithmetic and copies ran while one was open for 1% -> 1% of each run, Pallas kernels for 8% -> 9%
where the time goes in v9:
time: 95 us; the launch traced here: 94.9 us
  starting transfers between devices  53.8 us (57%)
  waiting for transfers between devices  29.9 us (31%)
  Pallas kernels  8.83 us (9%)
  other arithmetic  1.55 us (2%)
    ppermute x28, starting transfers between devices, moved(): lax.ppermute(block, BOTH, [(index_of(*at), index_of(*route(*at))) for at...  53.8 us
    ppermute x28, waiting for transfers between devices, moved(): lax.ppermute(block, BOTH, [(index_of(*at), index_of(*route(*at))) for at...  29.9 us
    pallas_call x9, Pallas kernels, call(): pl.pallas_call(kernel, out_shape=out_shape, in_specs=[SMEM] + [VMEM] * le...  8.83 us
  transfers between devices with their start and end apart: 28, of which 12 were waited for; matrix products, arithmetic and copies ran while one was open for 1% of the time, Pallas kernels for 9%

profile of v9, /device:TPU:1, one launch (start us, length us, event | category | flops | bytes accessed | tf_op | source)
XLA Modules:
  0.0 94.9 jit_solution(14564703760998687125)
XLA Ops:
  0.6 0.0 copy-start
  0.6 4.2 %collective-permute-start = (bf16[2,2,64,1024]{3,2,1,0:T(8,128)(2,1)}, bf16[2,2,64,1024]{3,2,1,0:T(8,128)(2,1)S(1)}, u32[]{:S(2)}, u32[]{:S(2)}) collective-permute-start(bf16[2,2,64,1024]{3,2,1,0:T(8,128)(2,1)} %bitcast.15), channel_id=1, source_target_pairs={{0,128},{1,144},{2,130},{3,146},{4,132},{5,148},{6,134},{7,150},{8... | collective-permute-start | bytes 1572872 | tf_op jit(solution)/shard_map/ppermute | solution.py:27
  4.8 6.4 %collective-permute-done.own.refs_2_.refs_0_ = bf16[2,2,64,1024]{3,2,1,0:T(8,128)(2,1)S(1)} collective-permute-done((bf16[2,2,64,1024]{3,2,1,0:T(8,128)(2,1)}, bf16[2,2,64,1024]{3,2,1,0:T(8,128)(2,1)S(1)}, u32[]{:S(2)}, u32[]{:S(2)}) %collective-permute-start) | collective-permute-done | bytes 524320 | tf_op jit(solution)/shard_map/ppermute | solution.py:27
  11.3 1.5 %collective-permute-start.3 = (bf16[2,2,64,1024]{3,2,1,0:T(8,128)(2,1)S(1)}, bf16[2,2,64,1024]{3,2,1,0:T(8,128)(2,1)S(1)}, u32[]{:S(2)}, u32[]{:S(2)}) collective-permute-start(bf16[2,2,64,1024]{3,2,1,0:T(8,128)(2,1)S(1)} %collective-permute-done.own.refs_2_.refs_0_), channel_id=1, source_target_pairs={{0,16},{1,17},{2,18},{3,19},{4,20},{5,21},{6,22},{7,23},{8,24},{9,... | collective-permute-start | bytes 1572872 | tf_op jit(solution)/shard_map/ppermute | solution.py:27
  12.8 4.1 %collective-permute-start.1 = (bf16[2,2,64,1024]{3,2,1,0:T(8,128)(2,1)S(1)}, bf16[2,2,64,1024]{3,2,1,0:T(8,128)(2,1)S(1)}, u32[]{:S(2)}, u32[]{:S(2)}) collective-permute-start(bf16[2,2,64,1024]{3,2,1,0:T(8,128)(2,1)S(1)} %collective-permute-done.own.refs_2_.refs_0_), channel_id=1, source_target_pairs={{0,2},{1,3},{2,4},{3,5},{4,6},{5,7},{6,8},{7,9},{8,10},{9,11},{10,... | collective-permute-start | bytes 1572872 | tf_op jit(solution)/shard_map/ppermute | solution.py:27
  16.9 0.0 collective-permute-done.3.other.refs_3_.refs_8_
  16.9 1.9 %collective-permute-start.6 = (bf16[2,2,64,1024]{3,2,1,0:T(8,128)(2,1)S(1)}, bf16[2,2,64,1024]{3,2,1,0:T(8,128)(2,1)S(1)}, u32[]{:S(2)}, u32[]{:S(2)}) collective-permute-start(bf16[2,2,64,1024]{3,2,1,0:T(8,128)(2,1)S(1)} %collective-permute-done.3.other.refs_3_.refs_8_), channel_id=1, source_target_pairs={{0,2},{1,3},{2,4},{3,5},{4,6},{5,7},{6,8},{7,9},{8,10},{9,11},{10,... | collective-permute-start | bytes 1572872 | tf_op jit(solution)/shard_map/ppermute | solution.py:27
  18.8 0.1 pad_add_fusion.info.refs_0_
  18.9 0.6 shard_map.41
  19.4 1.3 %collective-permute-start.4 = (bf16[2,128,1024]{2,1,0:T(8,128)(2,1)S(1)}, bf16[2,128,1024]{2,1,0:T(8,128)(2,1)S(1)}, u32[]{:S(2)}, u32[]{:S(2)}) collective-permute-start(bf16[2,128,1024]{2,1,0:T(8,128)(2,1)S(1)} %shard_map.41), channel_id=1, source_target_pairs={{0,33},{1,0},{2,35},{3,2},{4,37},{5,4},{6,39},{7,6},{8,41},{9,8},{... | collective-permute-start | bytes 1572872 | tf_op jit(solution)/shard_map/ppermute | solution.py:27
  20.7 2.3 %collective-permute-done.1.refs_1_.refs_2_ = bf16[2,2,64,1024]{3,2,1,0:T(8,128)(2,1)S(1)} collective-permute-done((bf16[2,2,64,1024]{3,2,1,0:T(8,128)(2,1)S(1)}, bf16[2,2,64,1024]{3,2,1,0:T(8,128)(2,1)S(1)}, u32[]{:S(2)}, u32[]{:S(2)}) %collective-permute-start.1) | collective-permute-done | bytes 524320 | tf_op jit(solution)/shard_map/ppermute | solution.py:27
  23.0 3.4 %collective-permute-start.2 = (bf16[2,2,64,1024]{3,2,1,0:T(8,128)(2,1)S(1)}, bf16[2,2,64,1024]{3,2,1,0:T(8,128)(2,1)S(1)}, u32[]{:S(2)}, u32[]{:S(2)}) collective-permute-start(bf16[2,2,64,1024]{3,2,1,0:T(8,128)(2,1)S(1)} %collective-permute-done.1.refs_1_.refs_2_), channel_id=1, source_target_pairs={{0,2},{1,3},{2,4},{3,5},{4,6},{5,7},{6,8},{7,9},{8,10},{9,11},{10,... | collective-permute-start | bytes 1572872 | tf_op jit(solution)/shard_map/ppermute | solution.py:27
  26.4 0.0 collective-permute-start.8
  26.4 2.2 %collective-permute-done.6.refs_4_.refs_6_.refs_9_ = bf16[2,2,64,1024]{3,2,1,0:T(8,128)(2,1)S(1)} collective-permute-done((bf16[2,2,64,1024]{3,2,1,0:T(8,128)(2,1)S(1)}, bf16[2,2,64,1024]{3,2,1,0:T(8,128)(2,1)S(1)}, u32[]{:S(2)}, u32[]{:S(2)}) %collective-permute-start.6) | collective-permute-done | bytes 524320 | tf_op jit(solution)/shard_map/ppermute | solution.py:27
  28.6 3.1 %collective-permute-start.10 = (bf16[2,2,64,1024]{3,2,1,0:T(8,128)(2,1)S(1)}, bf16[2,2,64,1024]{3,2,1,0:T(8,128)(2,1)S(1)}, u32[]{:S(2)}, u32[]{:S(2)}) collective-permute-start(bf16[2,2,64,1024]{3,2,1,0:T(8,128)(2,1)S(1)} %collective-permute-done.6.refs_4_.refs_6_.refs_9_), channel_id=1, source_target_pairs={{0,2},{1,3},{2,4},{3,5},{4,6},{5,7},{6,8},{7,9},{8,10},{9,11},{10,... | collective-permute-start | bytes 1572872 | tf_op jit(solution)/shard_map/ppermute | solution.py:27
  31.7 0.0 collective-permute-start.7
  31.7 2.5 %collective-permute-done.4.refs_1_.a_ref = bf16[2,128,1024]{2,1,0:T(8,128)(2,1)S(1)} collective-permute-done((bf16[2,128,1024]{2,1,0:T(8,128)(2,1)S(1)}, bf16[2,128,1024]{2,1,0:T(8,128)(2,1)S(1)}, u32[]{:S(2)}, u32[]{:S(2)}) %collective-permute-start.4) | collective-permute-done | bytes 524320 | tf_op jit(solution)/shard_map/ppermute | solution.py:27
  34.2 0.9 shard_map.42.refs_10_
  35.1 0.0 collective-permute-done.2.refs_4_.refs_0_.refs_3_
  35.1 3.6 %collective-permute-start.5 = (bf16[2,2,64,1024]{3,2,1,0:T(8,128)(2,1)S(1)}, bf16[2,2,64,1024]{3,2,1,0:T(8,128)(2,1)S(1)}, u32[]{:S(2)}, u32[]{:S(2)}) collective-permute-start(bf16[2,2,64,1024]{3,2,1,0:T(8,128)(2,1)S(1)} %collective-permute-done.2.refs_4_.refs_0_.refs_3_), channel_id=1, source_target_pairs={{0,2},{1,3},{2,4},{3,5},{4,6},{5,7},{6,8},{7,9},{8,10},{9,11},{10,... | collective-permute-start | bytes 1572872 | tf_op jit(solution)/shard_map/ppermute | solution.py:27
  38.7 0.0 collective-permute-done.8.refs_5_.refs_7_.refs_10_
  38.8 0.0 collective-permute-done.7.refs_2_.refs_3_
  38.8 0.7 shard_map.43
  39.4 0.1 collective-permute-start.9
  39.5 1.2 %collective-permute-start.13 = (bf16[2,2,64,1024]{3,2,1,0:T(8,128)(2,1)S(1)}, bf16[2,2,64,1024]{3,2,1,0:T(8,128)(2,1)S(1)}, u32[]{:S(2)}, u32[]{:S(2)}) collective-permute-start(bf16[2,2,64,1024]{3,2,1,0:T(8,128)(2,1)S(1)} %collective-permute-done.2.refs_4_.refs_0_.refs_3_), channel_id=1, source_target_pairs={{0,16},{1,17},{2,18},{3,19},{4,20},{5,21},{6,22},{7,23},{8,24},{9,... | collective-permute-start | bytes 1572872 | tf_op jit(solution)/shard_map/ppermute | solution.py:27
  40.8 0.9 collective-permute-start.12
  41.7 2.1 %collective-permute-start.11 = (bf16[2,2,64,1024]{3,2,1,0:T(8,128)(2,1)S(1)}, bf16[2,2,64,1024]{3,2,1,0:T(8,128)(2,1)S(1)}, u32[]{:S(2)}, u32[]{:S(2)}) collective-permute-start(bf16[2,2,64,1024]{3,2,1,0:T(8,128)(2,1)S(1)} %collective-permute-done.10.refs_8_.refs_2_.refs_11_), channel_id=1, source_target_pairs={{0,2},{1,3},{2,4},{3,5},{4,6},{5,7},{6,8},{7,9},{8,10},{9,11},{10,... | collective-permute-start | bytes 1572872 | tf_op jit(solution)/shard_map/ppermute | solution.py:27
  43.7 1.7 %collective-permute-done.5.refs_2_.refs_5_.refs_0_ = bf16[2,2,64,1024]{3,2,1,0:T(8,128)(2,1)S(1)} collective-permute-done((bf16[2,2,64,1024]{3,2,1,0:T(8,128)(2,1)S(1)}, bf16[2,2,64,1024]{3,2,1,0:T(8,128)(2,1)S(1)}, u32[]{:S(2)}, u32[]{:S(2)}) %collective-permute-start.5) | collective-permute-done | bytes 524320 | tf_op jit(solution)/shard_map/ppermute | solution.py:27
  45.5 2.1 %collective-permute-done.9.near = bf16[3,2,128,128]{3,2,1,0:T(8,128)(2,1)S(1)} collective-permute-done((bf16[3,2,128,128]{3,2,1,0:T(8,128)(2,1)S(1)}, bf16[3,2,128,128]{3,2,1,0:T(8,128)(2,1)S(1)}, u32[]{:S(2)}, u32[]{:S(2)}) %collective-permute-start.9) | collective-permute-done | bytes 196640 | tf_op jit(solution)/shard_map/ppermute | solution.py:27
  47.6 1.0 %collective-permute-start.16 = (bf16[2,2,64,1024]{3,2,1,0:T(8,128)(2,1)S(1)}, bf16[2,2,64,1024]{3,2,1,0:T(8,128)(2,1)S(1)}, u32[]{:S(2)}, u32[]{:S(2)}) collective-permute-start(bf16[2,2,64,1024]{3,2,1,0:T(8,128)(2,1)S(1)} %collective-permute-done.5.refs_2_.refs_5_.refs_0_), channel_id=1, source_target_pairs={{0,2},{1,3},{2,4},{3,5},{4,6},{5,7},{6,8},{7,9},{8,10},{9,11},{10,... | collective-permute-start | bytes 1572872 | tf_op jit(solution)/shard_map/ppermute | solution.py:27
  48.6 0.6 shard_map.46
  49.2 1.3 %collective-permute-start.17 = (bf16[2,2,128,128]{3,2,1,0:T(8,128)(2,1)S(1)}, bf16[2,2,128,128]{3,2,1,0:T(8,128)(2,1)S(1)}, u32[]{:S(2)}, u32[]{:S(2)}) collective-permute-start(bf16[2,2,128,128]{3,2,1,0:T(8,128)(2,1)S(1)} %shard_map.46), channel_id=1, source_target_pairs={{0,33},{1,0},{2,35},{3,2},{4,37},{5,4},{6,39},{7,6},{8,41},{9,8},{... | collective-permute-start | bytes 393224 | tf_op jit(solution)/shard_map/ppermute | solution.py:27
  50.5 1.4 %collective-permute-start.15 = (bf16[2,2,64,1024]{3,2,1,0:T(8,128)(2,1)S(1)}, bf16[2,2,64,1024]{3,2,1,0:T(8,128)(2,1)S(1)}, u32[]{:S(2)}, u32[]{:S(2)}) collective-permute-start(bf16[2,2,64,1024]{3,2,1,0:T(8,128)(2,1)S(1)} %collective-permute-done.5.refs_2_.refs_5_.refs_0_), channel_id=1, source_target_pairs={{0,16},{1,17},{2,18},{3,19},{4,20},{5,21},{6,22},{7,23},{8,24},{9,... | collective-permute-start | bytes 1572872 | tf_op jit(solution)/shard_map/ppermute | solution.py:27
  52.0 1.3 %shard_map.44.refs_6_ = f32[256,1024]{1,0:T(8,128)S(1)} custom-call(s32[6]{0:T(128)S(1)} %pad_add_fusion.info.refs_0_, bf16[2,128,1024]{2,1,0:T(8,128)(2,1)S(1)} %collective-permute-done.4.refs_1_.a_ref, bf16[2,2,64,1024]{3,2,1,0:T(8,128)(2,1)S(1)} %collective-permute-done.1.refs_1_.refs_2_, ...), custom_call_target="tpu_custom_call" | custom-call | flops 1 | bytes 1048576 | tf_op jit(solution)/shard_map/pallas_call | solution.py:75
  53.3 0.0 collective-permute-done.11.refs_4_.refs_13_.refs_3_
  53.3 0.1 collective-permute-start.14
  53.4 4.2 %collective-permute-done.17.middle = bf16[2,2,128,128]{3,2,1,0:T(8,128)(2,1)S(1)} collective-permute-done((bf16[2,2,128,128]{3,2,1,0:T(8,128)(2,1)S(1)}, bf16[2,2,128,128]{3,2,1,0:T(8,128)(2,1)S(1)}, u32[]{:S(2)}, u32[]{:S(2)}) %collective-permute-start.17) | collective-permute-done | bytes 131104 | tf_op jit(solution)/shard_map/ppermute | solution.py:27
  57.6 0.0 collective-permute-done.16.refs_7_.refs_2_
  57.6 0.9 collective-permute-start.18
  58.5 0.0 collective-permute-done.15.refs_5_.refs_14_.refs_4_
  58.5 0.0 collective-permute-done.14.refs_3_.refs_6_.refs_1_
  58.5 1.0 %shard_map.45.acc = f32[256,1024]{1,0:T(8,128)S(1)} custom-call(s32[6]{0:T(128)S(1)} %pad_add_fusion.info.refs_0_, bf16[2,128,1024]{2,1,0:T(8,128)(2,1)S(1)} %collective-permute-done.4.refs_1_.a_ref, bf16[2,2,64,1024]{3,2,1,0:T(8,128)(2,1)S(1)} %collective-permute-done.5.refs_2_.refs_5_.refs_0_, ...), custom_call_target="tpu_custom_call" | custom-call | flops 1 | bytes 1048576 | tf_op jit(solution)/shard_map/pallas_call | solution.py:75
  59.5 0.5 collective-permute-done.18.refs_15_.refs_5_
  60.1 0.7 shard_map.48
  60.7 1.3 %collective-permute-start.19 = (bf16[3,2,128,128]{3,2,1,0:T(8,128)(2,1)S(1)}, bf16[3,2,128,128]{3,2,1,0:T(8,128)(2,1)S(1)}, u32[]{:S(2)}, u32[]{:S(2)}) collective-permute-start(bf16[3,2,128,128]{3,2,1,0:T(8,128)(2,1)S(1)} %shard_map.48), channel_id=1, source_target_pairs={{0,33},{1,0},{2,35},{3,2},{4,37},{5,4},{6,39},{7,6},{8,41},{9,8},{... | collective-permute-start | bytes 589832 | tf_op jit(solution)/shard_map/ppermute | solution.py:27
  62.0 2.1 %shard_map.47 = (bf16[2,64,1024]{2,1,0:T(8,128)(2,1)S(1)}, bf16[2,64,1024]{2,1,0:T(8,128)(2,1)S(1)}, f32[256,1024]{1,0:T(8,128)S(1)}) custom-call(s32[6]{0:T(128)S(1)} %pad_add_fusion.info.refs_0_, bf16[2,128,1024]{2,1,0:T(8,128)(2,1)S(1)} %collective-permute-done.4.refs_1_.a_ref, f32[256,1024]{1,0:T(8,128)S(1)} %shard_map.45.acc, ...), custom_call_target="tpu_custom_call" | custom-call | flops 3000000000 | bytes 1048576 | tf_op jit(solution)/shard_map/pallas_call | solution.py:75
  64.2 3.9 %collective-permute-start.22 = (bf16[2,64,1024]{2,1,0:T(8,128)(2,1)S(1)}, bf16[2,64,1024]{2,1,0:T(8,128)(2,1)S(1)}, u32[]{:S(2)}, u32[]{:S(2)}) collective-permute-start(bf16[2,64,1024]{2,1,0:T(8,128)(2,1)S(1)} %get-tuple-element.30), channel_id=1, source_target_pairs={{0,128},{1,112},{2,130},{3,114},{4,132},{5,116},{6,134},{7,118},{8... | collective-permute-start | bytes 786440 | tf_op jit(solution)/shard_map/ppermute | solution.py:27
  68.1 2.8 %collective-permute-done.19.late = bf16[3,2,128,128]{3,2,1,0:T(8,128)(2,1)S(1)} collective-permute-done((bf16[3,2,128,128]{3,2,1,0:T(8,128)(2,1)S(1)}, bf16[3,2,128,128]{3,2,1,0:T(8,128)(2,1)S(1)}, u32[]{:S(2)}, u32[]{:S(2)}) %collective-permute-start.19) | collective-permute-done | bytes 196640 | tf_op jit(solution)/shard_map/ppermute | solution.py:27
  70.9 1.0 %shard_map.49 = f32[1,128]{1,0:T(1,128)S(1)} custom-call(s32[6]{0:T(128)S(1)} %pad_add_fusion.info.refs_0_, f32[256,1024]{1,0:T(8,128)S(1)} %get-tuple-element.27.product, bf16[3,2,128,128]{3,2,1,0:T(8,128)(2,1)S(1)} %collective-permute-done.9.near, bf16[2,2,128,128]{3,2,1,0:T(8,128)(2,1)S(1)} %collective-permute-done.17.middle, ...), custom_call_target="tpu_custom_call" | custom-call | flops 1 | bytes 1048576 | tf_op jit(solution)/shard_map/pallas_call | solution.py:75
  71.8 0.0 collective-permute-start.21
  71.9 2.7 %collective-permute-start.20 = (f32[1,128]{1,0:T(1,128)S(1)}, f32[1,128]{1,0:T(1,128)S(1)}, u32[]{:S(2)}, u32[]{:S(2)}) collective-permute-start(f32[1,128]{1,0:T(1,128)S(1)} %shard_map.49), channel_id=1, source_target_pairs={{0,14},{1,15},{2,0},{3,1},{4,2},{5,3},{6,4},{7,5},{8,6},{9,7},{10,... | collective-permute-start | bytes 1544 | tf_op jit(solution)/shard_map/ppermute | solution.py:27
  74.5 0.9 collective-permute-done.21
  75.4 0.0 collective-permute-done.20
  75.5 4.8 %collective-permute-start.23 = (f32[1,128]{1,0:T(1,128)S(1)}, f32[1,128]{1,0:T(1,128)S(1)}, u32[]{:S(2)}, u32[]{:S(2)}) collective-permute-start(f32[1,128]{1,0:T(1,128)S(1)} %get-tuple-element.31), channel_id=1, source_target_pairs={{0,6},{1,7},{2,8},{3,9},{4,10},{5,11},{6,12},{7,13},{8,14},{9,15},... | collective-permute-start | bytes 1544 | tf_op jit(solution)/shard_map/ppermute | solution.py:27
  80.3 0.7 collective-permute-done.23
  81.0 3.5 %collective-permute-done.24 = f32[1,128]{1,0:T(1,128)S(1)} collective-permute-done((f32[1,128]{1,0:T(1,128)S(1)}, f32[1,128]{1,0:T(1,128)S(1)}, u32[]{:S(2)}, u32[]{:S(2)}) %collective-permute-start.24) | collective-permute-done | bytes 544 | tf_op jit(solution)/shard_map/ppermute | solution.py:27
  84.5 0.0 collective-permute-done.25
  84.5 0.0 collective-permute-start.27
  84.5 8.9 %collective-permute-start.26 = (f32[1,128]{1,0:T(1,128)S(1)}, f32[1,128]{1,0:T(1,128)S(1)}, u32[]{:S(2)}, u32[]{:S(2)}) collective-permute-start(f32[1,128]{1,0:T(1,128)S(1)} %add_add_fusion), channel_id=1, source_target_pairs={{0,128},{1,112},{2,130},{3,114},{4,132},{5,116},{6,134},{7,118},{8... | collective-permute-start | bytes 1544 | tf_op jit(solution)/shard_map/ppermute | solution.py:27
  93.4 0.9 maximum_select_fusion
  94.2 0.0 collective-permute-done.27
  94.2 0.0 collective-permute-done.26
  94.3 0.1 reshape.77
  94.4 0.6 broadcast_multiply_fusion
  (12 shorter events, 0.1 us)
Async XLA Ops:
  0.6 16.2 %copy-start = (s32[2,1,4]{2,1,0:T(1,128)S(1)}, s32[2,1,4]{2,1,0:T(1,128)}, u32[]{:S(2)}) copy-start(s32[2,1,4]{2,1,0:T(1,128)} %param.3) | copy-start | bytes 100
  0.6 10.6 %collective-permute-start = (bf16[2,2,64,1024]{3,2,1,0:T(8,128)(2,1)}, bf16[2,2,64,1024]{3,2,1,0:T(8,128)(2,1)S(1)}, u32[]{:S(2)}, u32[]{:S(2)}) collective-permute-start(bf16[2,2,64,1024]{3,2,1,0:T(8,128)(2,1)} %bitcast.15), channel_id=1, source_target_pairs={{0,128},{1,144},{2,130},{3,146},{4,132},{5,148},{6,134},{7,150},{8... | collective-permute-start | bytes 1572872 | tf_op jit(solution)/shard_map/ppermute | solution.py:27
  11.3 5.6 %collective-permute-start.3 = (bf16[2,2,64,1024]{3,2,1,0:T(8,128)(2,1)S(1)}, bf16[2,2,64,1024]{3,2,1,0:T(8,128)(2,1)S(1)}, u32[]{:S(2)}, u32[]{:S(2)}) collective-permute-start(bf16[2,2,64,1024]{3,2,1,0:T(8,128)(2,1)S(1)} %collective-permute-done.own.refs_2_.refs_0_), channel_id=1, source_target_pairs={{0,16},{1,17},{2,18},{3,19},{4,20},{5,21},{6,22},{7,23},{8,24},{9,... | collective-permute-start | bytes 1572872 | tf_op jit(solution)/shard_map/ppermute | solution.py:27
  12.8 10.2 %collective-permute-start.1 = (bf16[2,2,64,1024]{3,2,1,0:T(8,128)(2,1)S(1)}, bf16[2,2,64,1024]{3,2,1,0:T(8,128)(2,1)S(1)}, u32[]{:S(2)}, u32[]{:S(2)}) collective-permute-start(bf16[2,2,64,1024]{3,2,1,0:T(8,128)(2,1)S(1)} %collective-permute-done.own.refs_2_.refs_0_), channel_id=1, source_target_pairs={{0,2},{1,3},{2,4},{3,5},{4,6},{5,7},{6,8},{7,9},{8,10},{9,11},{10,... | collective-permute-start | bytes 1572872 | tf_op jit(solution)/shard_map/ppermute | solution.py:27
  16.9 11.7 %collective-permute-start.6 = (bf16[2,2,64,1024]{3,2,1,0:T(8,128)(2,1)S(1)}, bf16[2,2,64,1024]{3,2,1,0:T(8,128)(2,1)S(1)}, u32[]{:S(2)}, u32[]{:S(2)}) collective-permute-start(bf16[2,2,64,1024]{3,2,1,0:T(8,128)(2,1)S(1)} %collective-permute-done.3.other.refs_3_.refs_8_), channel_id=1, source_target_pairs={{0,2},{1,3},{2,4},{3,5},{4,6},{5,7},{6,8},{7,9},{8,10},{9,11},{10,... | collective-permute-start | bytes 1572872 | tf_op jit(solution)/shard_map/ppermute | solution.py:27
  19.4 14.8 %collective-permute-start.4 = (bf16[2,128,1024]{2,1,0:T(8,128)(2,1)S(1)}, bf16[2,128,1024]{2,1,0:T(8,128)(2,1)S(1)}, u32[]{:S(2)}, u32[]{:S(2)}) collective-permute-start(bf16[2,128,1024]{2,1,0:T(8,128)(2,1)S(1)} %shard_map.41), channel_id=1, source_target_pairs={{0,33},{1,0},{2,35},{3,2},{4,37},{5,4},{6,39},{7,6},{8,41},{9,8},{... | collective-permute-start | bytes 1572872 | tf_op jit(solution)/shard_map/ppermute | solution.py:27
  23.0 12.1 %collective-permute-start.2 = (bf16[2,2,64,1024]{3,2,1,0:T(8,128)(2,1)S(1)}, bf16[2,2,64,1024]{3,2,1,0:T(8,128)(2,1)S(1)}, u32[]{:S(2)}, u32[]{:S(2)}) collective-permute-start(bf16[2,2,64,1024]{3,2,1,0:T(8,128)(2,1)S(1)} %collective-permute-done.1.refs_1_.refs_2_), channel_id=1, source_target_pairs={{0,2},{1,3},{2,4},{3,5},{4,6},{5,7},{6,8},{7,9},{8,10},{9,11},{10,... | collective-permute-start | bytes 1572872 | tf_op jit(solution)/shard_map/ppermute | solution.py:27
  26.4 12.3 %collective-permute-start.8 = (bf16[2,2,64,1024]{3,2,1,0:T(8,128)(2,1)S(1)}, bf16[2,2,64,1024]{3,2,1,0:T(8,128)(2,1)S(1)}, u32[]{:S(2)}, u32[]{:S(2)}) collective-permute-start(bf16[2,2,64,1024]{3,2,1,0:T(8,128)(2,1)S(1)} %collective-permute-done.1.refs_1_.refs_2_), channel_id=1, source_target_pairs={{0,16},{1,17},{2,18},{3,19},{4,20},{5,21},{6,22},{7,23},{8,24},{9,... | collective-permute-start | bytes 1572872 | tf_op jit(solution)/shard_map/ppermute | solution.py:27
  28.6 12.2 %collective-permute-start.10 = (bf16[2,2,64,1024]{3,2,1,0:T(8,128)(2,1)S(1)}, bf16[2,2,64,1024]{3,2,1,0:T(8,128)(2,1)S(1)}, u32[]{:S(2)}, u32[]{:S(2)}) collective-permute-start(bf16[2,2,64,1024]{3,2,1,0:T(8,128)(2,1)S(1)} %collective-permute-done.6.refs_4_.refs_6_.refs_9_), channel_id=1, source_target_pairs={{0,2},{1,3},{2,4},{3,5},{4,6},{5,7},{6,8},{7,9},{8,10},{9,11},{10,... | collective-permute-start | bytes 1572872 | tf_op jit(solution)/shard_map/ppermute | solution.py:27
  31.7 7.0 %collective-permute-start.7 = (bf16[2,2,64,1024]{3,2,1,0:T(8,128)(2,1)S(1)}, bf16[2,2,64,1024]{3,2,1,0:T(8,128)(2,1)S(1)}, u32[]{:S(2)}, u32[]{:S(2)}) collective-permute-start(bf16[2,2,64,1024]{3,2,1,0:T(8,128)(2,1)S(1)} %collective-permute-done.6.refs_4_.refs_6_.refs_9_), channel_id=1, source_target_pairs={{0,16},{1,17},{2,18},{3,19},{4,20},{5,21},{6,22},{7,23},{8,24},{9,... | collective-permute-start | bytes 1572872 | tf_op jit(solution)/shard_map/ppermute | solution.py:27
  35.1 10.4 %collective-permute-start.5 = (bf16[2,2,64,1024]{3,2,1,0:T(8,128)(2,1)S(1)}, bf16[2,2,64,1024]{3,2,1,0:T(8,128)(2,1)S(1)}, u32[]{:S(2)}, u32[]{:S(2)}) collective-permute-start(bf16[2,2,64,1024]{3,2,1,0:T(8,128)(2,1)S(1)} %collective-permute-done.2.refs_4_.refs_0_.refs_3_), channel_id=1, source_target_pairs={{0,2},{1,3},{2,4},{3,5},{4,6},{5,7},{6,8},{7,9},{8,10},{9,11},{10,... | collective-permute-start | bytes 1572872 | tf_op jit(solution)/shard_map/ppermute | solution.py:27
  39.4 8.1 %collective-permute-start.9 = (bf16[3,2,128,128]{3,2,1,0:T(8,128)(2,1)S(1)}, bf16[3,2,128,128]{3,2,1,0:T(8,128)(2,1)S(1)}, u32[]{:S(2)}, u32[]{:S(2)}) collective-permute-start(bf16[3,2,128,128]{3,2,1,0:T(8,128)(2,1)S(1)} %shard_map.43), channel_id=1, source_target_pairs={{0,33},{1,0},{2,35},{3,2},{4,37},{5,4},{6,39},{7,6},{8,41},{9,8},{... | collective-permute-start | bytes 589832 | tf_op jit(solution)/shard_map/ppermute | solution.py:27
  39.5 9.1 %collective-permute-start.13 = (bf16[2,2,64,1024]{3,2,1,0:T(8,128)(2,1)S(1)}, bf16[2,2,64,1024]{3,2,1,0:T(8,128)(2,1)S(1)}, u32[]{:S(2)}, u32[]{:S(2)}) collective-permute-start(bf16[2,2,64,1024]{3,2,1,0:T(8,128)(2,1)S(1)} %collective-permute-done.2.refs_4_.refs_0_.refs_3_), channel_id=1, source_target_pairs={{0,16},{1,17},{2,18},{3,19},{4,20},{5,21},{6,22},{7,23},{8,24},{9,... | collective-permute-start | bytes 1572872 | tf_op jit(solution)/shard_map/ppermute | solution.py:27
  40.8 7.8 %collective-permute-start.12 = (bf16[2,2,64,1024]{3,2,1,0:T(8,128)(2,1)S(1)}, bf16[2,2,64,1024]{3,2,1,0:T(8,128)(2,1)S(1)}, u32[]{:S(2)}, u32[]{:S(2)}) collective-permute-start(bf16[2,2,64,1024]{3,2,1,0:T(8,128)(2,1)S(1)} %collective-permute-done.10.refs_8_.refs_2_.refs_11_), channel_id=1, source_target_pairs={{0,16},{1,17},{2,18},{3,19},{4,20},{5,21},{6,22},{7,23},{8,24},{9,... | collective-permute-start | bytes 1572872 | tf_op jit(solution)/shard_map/ppermute | solution.py:27
  41.7 11.6 %collective-permute-start.11 = (bf16[2,2,64,1024]{3,2,1,0:T(8,128)(2,1)S(1)}, bf16[2,2,64,1024]{3,2,1,0:T(8,128)(2,1)S(1)}, u32[]{:S(2)}, u32[]{:S(2)}) collective-permute-start(bf16[2,2,64,1024]{3,2,1,0:T(8,128)(2,1)S(1)} %collective-permute-done.10.refs_8_.refs_2_.refs_11_), channel_id=1, source_target_pairs={{0,2},{1,3},{2,4},{3,5},{4,6},{5,7},{6,8},{7,9},{8,10},{9,11},{10,... | collective-permute-start | bytes 1572872 | tf_op jit(solution)/shard_map/ppermute | solution.py:27
  47.6 10.0 %collective-permute-start.16 = (bf16[2,2,64,1024]{3,2,1,0:T(8,128)(2,1)S(1)}, bf16[2,2,64,1024]{3,2,1,0:T(8,128)(2,1)S(1)}, u32[]{:S(2)}, u32[]{:S(2)}) collective-permute-start(bf16[2,2,64,1024]{3,2,1,0:T(8,128)(2,1)S(1)} %collective-permute-done.5.refs_2_.refs_5_.refs_0_), channel_id=1, source_target_pairs={{0,2},{1,3},{2,4},{3,5},{4,6},{5,7},{6,8},{7,9},{8,10},{9,11},{10,... | collective-permute-start | bytes 1572872 | tf_op jit(solution)/shard_map/ppermute | solution.py:27
  49.2 8.3 %collective-permute-start.17 = (bf16[2,2,128,128]{3,2,1,0:T(8,128)(2,1)S(1)}, bf16[2,2,128,128]{3,2,1,0:T(8,128)(2,1)S(1)}, u32[]{:S(2)}, u32[]{:S(2)}) collective-permute-start(bf16[2,2,128,128]{3,2,1,0:T(8,128)(2,1)S(1)} %shard_map.46), channel_id=1, source_target_pairs={{0,33},{1,0},{2,35},{3,2},{4,37},{5,4},{6,39},{7,6},{8,41},{9,8},{... | collective-permute-start | bytes 393224 | tf_op jit(solution)/shard_map/ppermute | solution.py:27
  50.5 8.0 %collective-permute-start.15 = (bf16[2,2,64,1024]{3,2,1,0:T(8,128)(2,1)S(1)}, bf16[2,2,64,1024]{3,2,1,0:T(8,128)(2,1)S(1)}, u32[]{:S(2)}, u32[]{:S(2)}) collective-permute-start(bf16[2,2,64,1024]{3,2,1,0:T(8,128)(2,1)S(1)} %collective-permute-done.5.refs_2_.refs_5_.refs_0_), channel_id=1, source_target_pairs={{0,16},{1,17},{2,18},{3,19},{4,20},{5,21},{6,22},{7,23},{8,24},{9,... | collective-permute-start | bytes 1572872 | tf_op jit(solution)/shard_map/ppermute | solution.py:27
  53.3 5.3 %collective-permute-start.14 = (bf16[2,2,64,1024]{3,2,1,0:T(8,128)(2,1)S(1)}, bf16[2,2,64,1024]{3,2,1,0:T(8,128)(2,1)S(1)}, u32[]{:S(2)}, u32[]{:S(2)}) collective-permute-start(bf16[2,2,64,1024]{3,2,1,0:T(8,128)(2,1)S(1)} %collective-permute-done.11.refs_4_.refs_13_.refs_3_), channel_id=1, source_target_pairs={{0,16},{1,17},{2,18},{3,19},{4,20},{5,21},{6,22},{7,23},{8,24},{9,... | collective-permute-start | bytes 1572872 | tf_op jit(solution)/shard_map/ppermute | solution.py:27
  57.6 2.5 %collective-permute-start.18 = (bf16[2,2,64,1024]{3,2,1,0:T(8,128)(2,1)S(1)}, bf16[2,2,64,1024]{3,2,1,0:T(8,128)(2,1)S(1)}, u32[]{:S(2)}, u32[]{:S(2)}) collective-permute-start(bf16[2,2,64,1024]{3,2,1,0:T(8,128)(2,1)S(1)} %collective-permute-done.16.refs_7_.refs_2_), channel_id=1, source_target_pairs={{0,16},{1,17},{2,18},{3,19},{4,20},{5,21},{6,22},{7,23},{8,24},{9,... | collective-permute-start | bytes 1572872 | tf_op jit(solution)/shard_map/ppermute | solution.py:27
  60.7 10.1 %collective-permute-start.19 = (bf16[3,2,128,128]{3,2,1,0:T(8,128)(2,1)S(1)}, bf16[3,2,128,128]{3,2,1,0:T(8,128)(2,1)S(1)}, u32[]{:S(2)}, u32[]{:S(2)}) collective-permute-start(bf16[3,2,128,128]{3,2,1,0:T(8,128)(2,1)S(1)} %shard_map.48), channel_id=1, source_target_pairs={{0,33},{1,0},{2,35},{3,2},{4,37},{5,4},{6,39},{7,6},{8,41},{9,8},{... | collective-permute-start | bytes 589832 | tf_op jit(solution)/shard_map/ppermute | solution.py:27
  64.2 11.3 %collective-permute-start.22 = (bf16[2,64,1024]{2,1,0:T(8,128)(2,1)S(1)}, bf16[2,64,1024]{2,1,0:T(8,128)(2,1)S(1)}, u32[]{:S(2)}, u32[]{:S(2)}) collective-permute-start(bf16[2,64,1024]{2,1,0:T(8,128)(2,1)S(1)} %get-tuple-element.30), channel_id=1, source_target_pairs={{0,128},{1,112},{2,130},{3,114},{4,132},{5,116},{6,134},{7,118},{8... | collective-permute-start | bytes 786440 | tf_op jit(solution)/shard_map/ppermute | solution.py:27
  71.8 3.6 %collective-permute-start.21 = (f32[1,128]{1,0:T(1,128)S(1)}, f32[1,128]{1,0:T(1,128)S(1)}, u32[]{:S(2)}, u32[]{:S(2)}) collective-permute-start(f32[1,128]{1,0:T(1,128)S(1)} %shard_map.49), channel_id=1, source_target_pairs={{0,2},{1,3},{2,4},{3,5},{4,6},{5,7},{6,8},{7,9},{8,10},{9,11},{10,... | collective-permute-start | bytes 1544 | tf_op jit(solution)/shard_map/ppermute | solution.py:27
  71.9 3.6 %collective-permute-start.20 = (f32[1,128]{1,0:T(1,128)S(1)}, f32[1,128]{1,0:T(1,128)S(1)}, u32[]{:S(2)}, u32[]{:S(2)}) collective-permute-start(f32[1,128]{1,0:T(1,128)S(1)} %shard_map.49), channel_id=1, source_target_pairs={{0,14},{1,15},{2,0},{3,1},{4,2},{5,3},{6,4},{7,5},{8,6},{9,7},{10,... | collective-permute-start | bytes 1544 | tf_op jit(solution)/shard_map/ppermute | solution.py:27
  74.5 9.9 %collective-permute-start.25 = (bf16[2,64,1024]{2,1,0:T(8,128)(2,1)S(1)}, bf16[2,64,1024]{2,1,0:T(8,128)(2,1)S(1)}, u32[]{:S(2)}, u32[]{:S(2)}) collective-permute-start(bf16[2,64,1024]{2,1,0:T(8,128)(2,1)S(1)} %get-tuple-element.34), channel_id=1, source_target_pairs={{0,129},{1,113},{2,131},{3,115},{4,133},{5,117},{6,135},{7,119},{8... | collective-permute-start | bytes 786440 | tf_op jit(solution)/shard_map/ppermute | solution.py:27
  75.5 5.5 %collective-permute-start.23 = (f32[1,128]{1,0:T(1,128)S(1)}, f32[1,128]{1,0:T(1,128)S(1)}, u32[]{:S(2)}, u32[]{:S(2)}) collective-permute-start(f32[1,128]{1,0:T(1,128)S(1)} %get-tuple-element.31), channel_id=1, source_target_pairs={{0,6},{1,7},{2,8},{3,9},{4,10},{5,11},{6,12},{7,13},{8,14},{9,15},... | collective-permute-start | bytes 1544 | tf_op jit(solution)/shard_map/ppermute | solution.py:27
  80.3 4.2 %collective-permute-start.24 = (f32[1,128]{1,0:T(1,128)S(1)}, f32[1,128]{1,0:T(1,128)S(1)}, u32[]{:S(2)}, u32[]{:S(2)}) collective-permute-start(f32[1,128]{1,0:T(1,128)S(1)} %get-tuple-element.32), channel_id=1, source_target_pairs={{0,10},{1,11},{2,12},{3,13},{4,14},{5,15},{6,0},{7,1},{8,2},{9,3},... | collective-permute-start | bytes 1544 | tf_op jit(solution)/shard_map/ppermute | solution.py:27
  84.5 9.8 %collective-permute-start.27 = (f32[1,128]{1,0:T(1,128)S(1)}, f32[1,128]{1,0:T(1,128)S(1)}, u32[]{:S(2)}, u32[]{:S(2)}) collective-permute-start(f32[1,128]{1,0:T(1,128)S(1)} %add_add_fusion), channel_id=1, source_target_pairs={{0,129},{1,113},{2,131},{3,115},{4,133},{5,117},{6,135},{7,119},{8... | collective-permute-start | bytes 1544 | tf_op jit(solution)/shard_map/ppermute | solution.py:27
  84.5 9.8 %collective-permute-start.26 = (f32[1,128]{1,0:T(1,128)S(1)}, f32[1,128]{1,0:T(1,128)S(1)}, u32[]{:S(2)}, u32[]{:S(2)}) collective-permute-start(f32[1,128]{1,0:T(1,128)S(1)} %add_add_fusion), channel_id=1, source_target_pairs={{0,128},{1,112},{2,130},{3,114},{4,132},{5,116},{6,134},{7,118},{8... | collective-permute-start | bytes 1544 | tf_op jit(solution)/shard_map/ppermute | solution.py:27

commit v10 on v9

--- a/solution.py
+++ b/solution.py
@@ -119,6 +119,12 @@
         cut(info, refs[k], refs[count + k], 0, refs[-1].at[k])
 
 
+def late_kernel(info, own_u, own_d, other_u, other_d, out, across):
+    cut(info, own_u, other_u, 0, out.at[0])
+    cut(info, own_d, other_d, 0, out.at[1])
+    cut(info, own_u, other_u, -1, across)
+
+
 def left_side(info, a_ref, offset):
     columns = columns_of(info, offset)
     real, imag = a_ref[0, :, columns], a_ref[1, :, columns]
@@ -141,9 +147,9 @@
 OFFSETS = (0, 1, -1, 2, -2, 3, -3, 4)
 
 
-def last_kernel(info, a_ref, acc, *refs):
+def last_kernel(info, a_ref, acc, near, middle, *refs):
     own, other = refs[0:8], refs[8:16]
-    keep, send, out, rounded_ref = refs[16:20]
+    keep, send, out, early, rounded_ref = refs[16:21]
     block = jnp.concatenate([whole(info, own[7], other[7], info[3], part) for part in range(2)], axis=0)
     product = acc[...] + jnp.dot(left_side(info, a_ref, 4), block, preferred_element_type=F32)
     rounded = product.astype(BF16)
@@ -157,20 +163,26 @@
         term = jnp.dot(left_side(info, rounded_ref, offset), block, preferred_element_type=F32)
         total = term if total is None else total + term
     out[...] = total
-
-
-def trace_kernel(info, product, near, middle, late, trace):
-    slices = [near.at[0], near.at[1], near.at[2], middle.at[0], middle.at[1], late.at[0], late.at[1], late.at[2]]
+    slices = [near.at[0], near.at[1], near.at[2], middle.at[0], middle.at[1]]
+    early[0:1, :], early[1:2, :] = trace_sum(info, out, list(zip(OFFSETS, slices)))
+
+
+def trace_sum(info, product, slices):
     re = im = None
-    for offset, piece in zip(OFFSETS, slices):
+    for offset, piece in slices:
         columns = columns_of(info, offset)
         q_re, q_im = product[0:128, columns], product[128:256, columns]
         d_re, d_im = piece[0].astype(F32), piece[1].astype(F32)
         more_re, more_im = q_re * d_re - q_im * d_im, q_re * d_im + q_im * d_re
         re = more_re if re is None else re + more_re
         im = more_im if im is None else im + more_im
-    re = jnp.sum(jnp.sum(re, axis=0, keepdims=True), axis=1, keepdims=True)
-    im = jnp.sum(jnp.sum(im, axis=0, keepdims=True), axis=1, keepdims=True)
+    return [jnp.sum(part, axis=0, keepdims=True) for part in (re, im)]
+
+
+def trace_kernel(info, product, early, late, across, trace):
+    re, im = trace_sum(info, product, [(3, late.at[0]), (-3, late.at[1]), (4, across)])
+    re = jnp.sum(re + early[0:1, :], axis=1, keepdims=True)
+    im = jnp.sum(im + early[1:2, :], axis=1, keepdims=True)
     lane = lax.broadcasted_iota(jnp.int32, (1, 128), 1)
     trace[...] = jnp.where(lane == 2 * info[0], re, jnp.where(lane == 2 * info[0] + 1, im, 0.0))
 
@@ -212,25 +224,25 @@
     q3, acc = wall((q3, acc))
 
     q3x = moved(q3, other_core)
+    two, two_x = [p3, q3x], [q3, p3x]
+    late, across = call(late_kernel, info, two + two_x, (slices_of(2), jax.ShapeDtypeStruct((2, 128, 128), BF16)), 1)
     p4, middle = wall((p4, middle))
 
     p4x = moved(p4, other_core)
-    two, two_x = [p3, q3x], [q3, p3x]
+    late, across = moved(late, hub_ahead(0)), moved(across, hub_ahead(1))
     acc = call(
         lambda *refs: products_kernel(OFFSETS[5:7], *refs), info, [a] + two + two_x + [acc], block_of_products, 1
     )
-    late = moved(call(cut_kernel, info, two + [p4] + two_x + [p4x], slices_of(3), 1), hub_ahead(0))
     half_block = jax.ShapeDtypeStruct((2, 64, 1024), BF16)
-    keep, send, product = call(
+    keep, send, product, early = call(
         last_kernel,
         info,
-        [a, acc] + five + two + [p4] + five_x + two_x + [p4x],
-        (half_block, half_block, block_of_products),
-        WEIGHT,
+        [a, acc, near, middle] + five + two + [p4] + five_x + two_x + [p4x],
+        (half_block, half_block, block_of_products, jax.ShapeDtypeStruct((8, 128), F32)),
+        1,
         [pltpu.VMEM((2, 128, 1024), BF16)],
     )
-    share = jax.ShapeDtypeStruct((1, 128), F32)
-    trace = call(trace_kernel, info, [product, near, middle, late], share, 1)
+    trace = call(trace_kernel, info, [product, early, late, across], jax.ShapeDtypeStruct((1, 128), F32), 1)
 
     below, above = moved(trace, along(1)), moved(trace, along(-1))
     kept, sent = moved(keep, from_hub(0)), moved(send, from_hub(1))

time: 95 us -> 95 us (level)
  starting transfers between devices: 53.8 us -> 57.8 us
  waiting for transfers between devices: 29.9 us -> 25.9 us
    ppermute x28 -> x29, starting transfers between devices: 53.8 us -> 57.8 us  [moved(): lax.ppermute(block, BOTH, [(index_of(*at), index_of(*route(*at))) for at...]
    ppermute x28 -> x29, waiting for transfers between devices: 29.9 us -> 25.9 us  [moved(): lax.ppermute(block, BOTH, [(index_of(*at), index_of(*route(*at))) for at...]
  transfers between devices with their start and end apart: 28 -> 29, of which waited for: 12 -> 11; matrix products, arithmetic and copies ran while one was open for 1% -> 1% of each run, Pallas kernels for 9% -> 9%
where the time goes in v10:
time: 95 us; the launch traced here: 94.9 us
  starting transfers between devices  57.8 us (61%)
  waiting for transfers between devices  25.9 us (27%)
  Pallas kernels  8.85 us (9%)
  other arithmetic  1.55 us (2%)
    ppermute x29, starting transfers between devices, moved(): lax.ppermute(block, BOTH, [(index_of(*at), index_of(*route(*at))) for at...  57.8 us
    ppermute x29, waiting for transfers between devices, moved(): lax.ppermute(block, BOTH, [(index_of(*at), index_of(*route(*at))) for at...  25.9 us
    pallas_call x9, Pallas kernels, call(): pl.pallas_call(kernel, out_shape=out_shape, in_specs=[SMEM] + [VMEM] * le...  8.85 us
  transfers between devices with their start and end apart: 29, of which 11 were waited for; matrix products, arithmetic and copies ran while one was open for 1% of the time, Pallas kernels for 9%

profile of v10, /device:TPU:1, one launch (start us, length us, event | category | flops | bytes accessed | tf_op | source)
XLA Modules:
  0.0 94.9 jit_solution(10204432124331600221)
XLA Ops:
  0.6 0.0 copy-start
  0.6 4.2 %collective-permute-start = (bf16[2,2,64,1024]{3,2,1,0:T(8,128)(2,1)}, bf16[2,2,64,1024]{3,2,1,0:T(8,128)(2,1)S(1)}, u32[]{:S(2)}, u32[]{:S(2)}) collective-permute-start(bf16[2,2,64,1024]{3,2,1,0:T(8,128)(2,1)} %bitcast.15), channel_id=1, source_target_pairs={{0,128},{1,144},{2,130},{3,146},{4,132},{5,148},{6,134},{7,150},{8... | collective-permute-start | bytes 1572872 | tf_op jit(solution)/shard_map/ppermute | solution.py:27
  4.8 6.4 %collective-permute-done.own.refs_2_.refs_0_ = bf16[2,2,64,1024]{3,2,1,0:T(8,128)(2,1)S(1)} collective-permute-done((bf16[2,2,64,1024]{3,2,1,0:T(8,128)(2,1)}, bf16[2,2,64,1024]{3,2,1,0:T(8,128)(2,1)S(1)}, u32[]{:S(2)}, u32[]{:S(2)}) %collective-permute-start) | collective-permute-done | bytes 524320 | tf_op jit(solution)/shard_map/ppermute | solution.py:27
  11.3 1.5 %collective-permute-start.3 = (bf16[2,2,64,1024]{3,2,1,0:T(8,128)(2,1)S(1)}, bf16[2,2,64,1024]{3,2,1,0:T(8,128)(2,1)S(1)}, u32[]{:S(2)}, u32[]{:S(2)}) collective-permute-start(bf16[2,2,64,1024]{3,2,1,0:T(8,128)(2,1)S(1)} %collective-permute-done.own.refs_2_.refs_0_), channel_id=1, source_target_pairs={{0,16},{1,17},{2,18},{3,19},{4,20},{5,21},{6,22},{7,23},{8,24},{9,... | collective-permute-start | bytes 1572872 | tf_op jit(solution)/shard_map/ppermute | solution.py:27
  12.8 4.1 %collective-permute-start.1 = (bf16[2,2,64,1024]{3,2,1,0:T(8,128)(2,1)S(1)}, bf16[2,2,64,1024]{3,2,1,0:T(8,128)(2,1)S(1)}, u32[]{:S(2)}, u32[]{:S(2)}) collective-permute-start(bf16[2,2,64,1024]{3,2,1,0:T(8,128)(2,1)S(1)} %collective-permute-done.own.refs_2_.refs_0_), channel_id=1, source_target_pairs={{0,2},{1,3},{2,4},{3,5},{4,6},{5,7},{6,8},{7,9},{8,10},{9,11},{10,... | collective-permute-start | bytes 1572872 | tf_op jit(solution)/shard_map/ppermute | solution.py:27
  16.9 0.0 collective-permute-done.3.other.refs_3_.refs_8_
  16.9 1.9 %collective-permute-start.6 = (bf16[2,2,64,1024]{3,2,1,0:T(8,128)(2,1)S(1)}, bf16[2,2,64,1024]{3,2,1,0:T(8,128)(2,1)S(1)}, u32[]{:S(2)}, u32[]{:S(2)}) collective-permute-start(bf16[2,2,64,1024]{3,2,1,0:T(8,128)(2,1)S(1)} %collective-permute-done.3.other.refs_3_.refs_8_), channel_id=1, source_target_pairs={{0,2},{1,3},{2,4},{3,5},{4,6},{5,7},{6,8},{7,9},{8,10},{9,11},{10,... | collective-permute-start | bytes 1572872 | tf_op jit(solution)/shard_map/ppermute | solution.py:27
  18.8 0.1 pad_add_fusion.info.refs_0_
  18.9 0.6 shard_map.41
  19.4 1.3 %collective-permute-start.4 = (bf16[2,128,1024]{2,1,0:T(8,128)(2,1)S(1)}, bf16[2,128,1024]{2,1,0:T(8,128)(2,1)S(1)}, u32[]{:S(2)}, u32[]{:S(2)}) collective-permute-start(bf16[2,128,1024]{2,1,0:T(8,128)(2,1)S(1)} %shard_map.41), channel_id=1, source_target_pairs={{0,33},{1,0},{2,35},{3,2},{4,37},{5,4},{6,39},{7,6},{8,41},{9,8},{... | collective-permute-start | bytes 1572872 | tf_op jit(solution)/shard_map/ppermute | solution.py:27
  20.7 2.3 %collective-permute-done.1.refs_1_.refs_2_ = bf16[2,2,64,1024]{3,2,1,0:T(8,128)(2,1)S(1)} collective-permute-done((bf16[2,2,64,1024]{3,2,1,0:T(8,128)(2,1)S(1)}, bf16[2,2,64,1024]{3,2,1,0:T(8,128)(2,1)S(1)}, u32[]{:S(2)}, u32[]{:S(2)}) %collective-permute-start.1) | collective-permute-done | bytes 524320 | tf_op jit(solution)/shard_map/ppermute | solution.py:27
  23.0 3.4 %collective-permute-start.2 = (bf16[2,2,64,1024]{3,2,1,0:T(8,128)(2,1)S(1)}, bf16[2,2,64,1024]{3,2,1,0:T(8,128)(2,1)S(1)}, u32[]{:S(2)}, u32[]{:S(2)}) collective-permute-start(bf16[2,2,64,1024]{3,2,1,0:T(8,128)(2,1)S(1)} %collective-permute-done.1.refs_1_.refs_2_), channel_id=1, source_target_pairs={{0,2},{1,3},{2,4},{3,5},{4,6},{5,7},{6,8},{7,9},{8,10},{9,11},{10,... | collective-permute-start | bytes 1572872 | tf_op jit(solution)/shard_map/ppermute | solution.py:27
  26.4 2.2 %collective-permute-done.6.refs_4_.refs_6_.refs_9_ = bf16[2,2,64,1024]{3,2,1,0:T(8,128)(2,1)S(1)} collective-permute-done((bf16[2,2,64,1024]{3,2,1,0:T(8,128)(2,1)S(1)}, bf16[2,2,64,1024]{3,2,1,0:T(8,128)(2,1)S(1)}, u32[]{:S(2)}, u32[]{:S(2)}) %collective-permute-start.6) | collective-permute-done | bytes 524320 | tf_op jit(solution)/shard_map/ppermute | solution.py:27
  28.6 3.1 %collective-permute-start.10 = (bf16[2,2,64,1024]{3,2,1,0:T(8,128)(2,1)S(1)}, bf16[2,2,64,1024]{3,2,1,0:T(8,128)(2,1)S(1)}, u32[]{:S(2)}, u32[]{:S(2)}) collective-permute-start(bf16[2,2,64,1024]{3,2,1,0:T(8,128)(2,1)S(1)} %collective-permute-done.6.refs_4_.refs_6_.refs_9_), channel_id=1, source_target_pairs={{0,2},{1,3},{2,4},{3,5},{4,6},{5,7},{6,8},{7,9},{8,10},{9,11},{10,... | collective-permute-start | bytes 1572872 | tf_op jit(solution)/shard_map/ppermute | solution.py:27
  31.7 2.5 %collective-permute-done.4.refs_1_.a_ref = bf16[2,128,1024]{2,1,0:T(8,128)(2,1)S(1)} collective-permute-done((bf16[2,128,1024]{2,1,0:T(8,128)(2,1)S(1)}, bf16[2,128,1024]{2,1,0:T(8,128)(2,1)S(1)}, u32[]{:S(2)}, u32[]{:S(2)}) %collective-permute-start.4) | collective-permute-done | bytes 524320 | tf_op jit(solution)/shard_map/ppermute | solution.py:27
  34.2 0.9 shard_map.42.refs_10_
  35.1 3.6 %collective-permute-start.5 = (bf16[2,2,64,1024]{3,2,1,0:T(8,128)(2,1)S(1)}, bf16[2,2,64,1024]{3,2,1,0:T(8,128)(2,1)S(1)}, u32[]{:S(2)}, u32[]{:S(2)}) collective-permute-start(bf16[2,2,64,1024]{3,2,1,0:T(8,128)(2,1)S(1)} %collective-permute-done.2.refs_4_.refs_0_.refs_3_), channel_id=1, source_target_pairs={{0,2},{1,3},{2,4},{3,5},{4,6},{5,7},{6,8},{7,9},{8,10},{9,11},{10,... | collective-permute-start | bytes 1572872 | tf_op jit(solution)/shard_map/ppermute | solution.py:27
  38.7 0.0 collective-permute-done.8.refs_5_.refs_7_.refs_10_
  38.8 0.0 collective-permute-done.7.refs_2_.refs_3_
  38.8 0.7 shard_map.43
  39.4 0.1 collective-permute-start.9
  39.5 1.2 %collective-permute-start.13 = (bf16[2,2,64,1024]{3,2,1,0:T(8,128)(2,1)S(1)}, bf16[2,2,64,1024]{3,2,1,0:T(8,128)(2,1)S(1)}, u32[]{:S(2)}, u32[]{:S(2)}) collective-permute-start(bf16[2,2,64,1024]{3,2,1,0:T(8,128)(2,1)S(1)} %collective-permute-done.2.refs_4_.refs_0_.refs_3_), channel_id=1, source_target_pairs={{0,16},{1,17},{2,18},{3,19},{4,20},{5,21},{6,22},{7,23},{8,24},{9,... | collective-permute-start | bytes 1572872 | tf_op jit(solution)/shard_map/ppermute | solution.py:27
  40.8 0.0 collective-permute-done.10.refs_8_.refs_2_.refs_11_
  40.8 0.9 collective-permute-start.12
  41.7 2.1 %collective-permute-start.11 = (bf16[2,2,64,1024]{3,2,1,0:T(8,128)(2,1)S(1)}, bf16[2,2,64,1024]{3,2,1,0:T(8,128)(2,1)S(1)}, u32[]{:S(2)}, u32[]{:S(2)}) collective-permute-start(bf16[2,2,64,1024]{3,2,1,0:T(8,128)(2,1)S(1)} %collective-permute-done.10.refs_8_.refs_2_.refs_11_), channel_id=1, source_target_pairs={{0,2},{1,3},{2,4},{3,5},{4,6},{5,7},{6,8},{7,9},{8,10},{9,11},{10,... | collective-permute-start | bytes 1572872 | tf_op jit(solution)/shard_map/ppermute | solution.py:27
  43.7 1.7 %collective-permute-done.5.refs_2_.refs_5_.own_u = bf16[2,2,64,1024]{3,2,1,0:T(8,128)(2,1)S(1)} collective-permute-done((bf16[2,2,64,1024]{3,2,1,0:T(8,128)(2,1)S(1)}, bf16[2,2,64,1024]{3,2,1,0:T(8,128)(2,1)S(1)}, u32[]{:S(2)}, u32[]{:S(2)}) %collective-permute-start.5) | collective-permute-done | bytes 524320 | tf_op jit(solution)/shard_map/ppermute | solution.py:27
  45.5 2.1 %collective-permute-done.9.near = bf16[3,2,128,128]{3,2,1,0:T(8,128)(2,1)S(1)} collective-permute-done((bf16[3,2,128,128]{3,2,1,0:T(8,128)(2,1)S(1)}, bf16[3,2,128,128]{3,2,1,0:T(8,128)(2,1)S(1)}, u32[]{:S(2)}, u32[]{:S(2)}) %collective-permute-start.9) | collective-permute-done | bytes 196640 | tf_op jit(solution)/shard_map/ppermute | solution.py:27
  47.6 1.0 %collective-permute-start.16 = (bf16[2,2,64,1024]{3,2,1,0:T(8,128)(2,1)S(1)}, bf16[2,2,64,1024]{3,2,1,0:T(8,128)(2,1)S(1)}, u32[]{:S(2)}, u32[]{:S(2)}) collective-permute-start(bf16[2,2,64,1024]{3,2,1,0:T(8,128)(2,1)S(1)} %collective-permute-done.5.refs_2_.refs_5_.own_u), channel_id=1, source_target_pairs={{0,2},{1,3},{2,4},{3,5},{4,6},{5,7},{6,8},{7,9},{8,10},{9,11},{10,... | collective-permute-start | bytes 1572872 | tf_op jit(solution)/shard_map/ppermute | solution.py:27
  48.6 0.0 collective-permute-done.13.refs_9_.refs_3_.refs_12_
  48.6 0.6 shard_map.46
  49.2 1.3 %collective-permute-start.17 = (bf16[2,2,128,128]{3,2,1,0:T(8,128)(2,1)S(1)}, bf16[2,2,128,128]{3,2,1,0:T(8,128)(2,1)S(1)}, u32[]{:S(2)}, u32[]{:S(2)}) collective-permute-start(bf16[2,2,128,128]{3,2,1,0:T(8,128)(2,1)S(1)} %shard_map.46), channel_id=1, source_target_pairs={{0,33},{1,0},{2,35},{3,2},{4,37},{5,4},{6,39},{7,6},{8,41},{9,8},{... | collective-permute-start | bytes 393224 | tf_op jit(solution)/shard_map/ppermute | solution.py:27
  50.5 1.4 %collective-permute-start.15 = (bf16[2,2,64,1024]{3,2,1,0:T(8,128)(2,1)S(1)}, bf16[2,2,64,1024]{3,2,1,0:T(8,128)(2,1)S(1)}, u32[]{:S(2)}, u32[]{:S(2)}) collective-permute-start(bf16[2,2,64,1024]{3,2,1,0:T(8,128)(2,1)S(1)} %collective-permute-done.5.refs_2_.refs_5_.own_u), channel_id=1, source_target_pairs={{0,16},{1,17},{2,18},{3,19},{4,20},{5,21},{6,22},{7,23},{8,24},{9,... | collective-permute-start | bytes 1572872 | tf_op jit(solution)/shard_map/ppermute | solution.py:27
  52.0 1.3 %shard_map.44.refs_6_ = f32[256,1024]{1,0:T(8,128)S(1)} custom-call(s32[6]{0:T(128)S(1)} %pad_add_fusion.info.refs_0_, bf16[2,128,1024]{2,1,0:T(8,128)(2,1)S(1)} %collective-permute-done.4.refs_1_.a_ref, bf16[2,2,64,1024]{3,2,1,0:T(8,128)(2,1)S(1)} %collective-permute-done.1.refs_1_.refs_2_, ...), custom_call_target="tpu_custom_call" | custom-call | flops 1 | bytes 1048576 | tf_op jit(solution)/shard_map/pallas_call | solution.py:75
  53.3 0.0 collective-permute-done.11.refs_4_.refs_13_.other_u
  53.3 0.1 collective-permute-start.14
  53.4 4.2 %collective-permute-done.17.middle = bf16[2,2,128,128]{3,2,1,0:T(8,128)(2,1)S(1)} collective-permute-done((bf16[2,2,128,128]{3,2,1,0:T(8,128)(2,1)S(1)}, bf16[2,2,128,128]{3,2,1,0:T(8,128)(2,1)S(1)}, u32[]{:S(2)}, u32[]{:S(2)}) %collective-permute-start.17) | collective-permute-done | bytes 131104 | tf_op jit(solution)/shard_map/ppermute | solution.py:27
  57.6 0.9 collective-permute-start.18
  58.5 0.0 collective-permute-done.15.refs_5_.refs_14_.other_d
  58.5 0.0 collective-permute-done.14.refs_3_.refs_6_.own_d
  58.5 0.7 shard_map.48
  59.2 1.3 %collective-permute-start.19 = (bf16[2,2,128,128]{3,2,1,0:T(8,128)(2,1)S(1)}, bf16[2,2,128,128]{3,2,1,0:T(8,128)(2,1)S(1)}, u32[]{:S(2)}, u32[]{:S(2)}) collective-permute-start(bf16[2,2,128,128]{3,2,1,0:T(8,128)(2,1)S(1)} %get-tuple-element.34), channel_id=1, source_target_pairs={{0,33},{1,0},{2,35},{3,2},{4,37},{5,4},{6,39},{7,6},{8,41},{9,8},{... | collective-permute-start | bytes 393224 | tf_op jit(solution)/shard_map/ppermute | solution.py:27
  60.5 2.7 %collective-permute-start.20 = (bf16[2,128,128]{2,1,0:T(8,128)(2,1)S(1)}, bf16[2,128,128]{2,1,0:T(8,128)(2,1)S(1)}, u32[]{:S(2)}, u32[]{:S(2)}) collective-permute-start(bf16[2,128,128]{2,1,0:T(8,128)(2,1)S(1)} %get-tuple-element.35), channel_id=1, source_target_pairs={{0,35},{1,2},{2,37},{3,4},{4,39},{5,6},{6,41},{7,8},{8,43},{9,10},... | collective-permute-start | bytes 196616 | tf_op jit(solution)/shard_map/ppermute | solution.py:27
  63.2 1.0 %shard_map.45.acc = f32[256,1024]{1,0:T(8,128)S(1)} custom-call(s32[6]{0:T(128)S(1)} %pad_add_fusion.info.refs_0_, bf16[2,128,1024]{2,1,0:T(8,128)(2,1)S(1)} %collective-permute-done.4.refs_1_.a_ref, bf16[2,2,64,1024]{3,2,1,0:T(8,128)(2,1)S(1)} %collective-permute-done.5.refs_2_.refs_5_.own_u, ...), custom_call_target="tpu_custom_call" | custom-call | flops 1 | bytes 1048576 | tf_op jit(solution)/shard_map/pallas_call | solution.py:75
  64.2 0.0 collective-permute-done.18.refs_15_
  64.2 2.4 %shard_map.47 = (bf16[2,64,1024]{2,1,0:T(8,128)(2,1)S(1)}, bf16[2,64,1024]{2,1,0:T(8,128)(2,1)S(1)}, f32[256,1024]{1,0:T(8,128)S(1)}, f32[8,128]{1,0:T(8,128)S(1)}) custom-call(s32[6]{0:T(128)S(1)} %pad_add_fusion.info.refs_0_, bf16[2,128,1024]{2,1,0:T(8,128)(2,1)S(1)} %collective-permute-done.4.refs_1_.a_ref, f32[256,1024]{1,0:T(8,128)S(1)} %shard_map.45.acc, ...), custom_call_target="tpu_custom_call" | custom-call | flops 1 | bytes 1048576 | tf_op jit(solution)/shard_map/pallas_call | solution.py:75
  66.6 4.0 %collective-permute-start.23 = (bf16[2,64,1024]{2,1,0:T(8,128)(2,1)S(1)}, bf16[2,64,1024]{2,1,0:T(8,128)(2,1)S(1)}, u32[]{:S(2)}, u32[]{:S(2)}) collective-permute-start(bf16[2,64,1024]{2,1,0:T(8,128)(2,1)S(1)} %get-tuple-element.36), channel_id=1, source_target_pairs={{0,128},{1,112},{2,130},{3,114},{4,132},{5,116},{6,134},{7,118},{8... | collective-permute-start | bytes 786440 | tf_op jit(solution)/shard_map/ppermute | solution.py:27
  70.5 0.7 shard_map.49
  71.3 0.0 collective-permute-start.22
  71.3 2.7 %collective-permute-start.21 = (f32[1,128]{1,0:T(1,128)S(1)}, f32[1,128]{1,0:T(1,128)S(1)}, u32[]{:S(2)}, u32[]{:S(2)}) collective-permute-start(f32[1,128]{1,0:T(1,128)S(1)} %shard_map.49), channel_id=1, source_target_pairs={{0,14},{1,15},{2,0},{3,1},{4,2},{5,3},{6,4},{7,5},{8,6},{9,7},{10,... | collective-permute-start | bytes 1544 | tf_op jit(solution)/shard_map/ppermute | solution.py:27
  74.0 0.7 collective-permute-start.26
  74.7 0.2 collective-permute-done.22
  74.9 0.0 collective-permute-done.21
  74.9 0.2 collective-permute-done.23
  75.1 4.3 %collective-permute-start.24 = (f32[1,128]{1,0:T(1,128)S(1)}, f32[1,128]{1,0:T(1,128)S(1)}, u32[]{:S(2)}, u32[]{:S(2)}) collective-permute-start(f32[1,128]{1,0:T(1,128)S(1)} %get-tuple-element.37), channel_id=1, source_target_pairs={{0,6},{1,7},{2,8},{3,9},{4,10},{5,11},{6,12},{7,13},{8,14},{9,15},... | collective-permute-start | bytes 1544 | tf_op jit(solution)/shard_map/ppermute | solution.py:27
  79.3 0.2 collective-permute-start.25
  79.5 0.9 collective-permute-done.24
  80.5 3.1 %collective-permute-done.25 = f32[1,128]{1,0:T(1,128)S(1)} collective-permute-done((f32[1,128]{1,0:T(1,128)S(1)}, f32[1,128]{1,0:T(1,128)S(1)}, u32[]{:S(2)}, u32[]{:S(2)}) %collective-permute-start.25) | collective-permute-done | bytes 544 | tf_op jit(solution)/shard_map/ppermute | solution.py:27
  83.5 0.0 collective-permute-done.26
  83.5 4.1 %collective-permute-start.28 = (f32[1,128]{1,0:T(1,128)S(1)}, f32[1,128]{1,0:T(1,128)S(1)}, u32[]{:S(2)}, u32[]{:S(2)}) collective-permute-start(f32[1,128]{1,0:T(1,128)S(1)} %add_add_fusion), channel_id=1, source_target_pairs={{0,129},{1,113},{2,131},{3,115},{4,133},{5,117},{6,135},{7,119},{8... | collective-permute-start | bytes 1544 | tf_op jit(solution)/shard_map/ppermute | solution.py:27
  87.7 5.7 %collective-permute-start.27 = (f32[1,128]{1,0:T(1,128)S(1)}, f32[1,128]{1,0:T(1,128)S(1)}, u32[]{:S(2)}, u32[]{:S(2)}) collective-permute-start(f32[1,128]{1,0:T(1,128)S(1)} %add_add_fusion), channel_id=1, source_target_pairs={{0,128},{1,112},{2,130},{3,114},{4,132},{5,116},{6,134},{7,118},{8... | collective-permute-start | bytes 1544 | tf_op jit(solution)/shard_map/ppermute | solution.py:27
  93.4 0.9 maximum_select_fusion
  94.3 0.0 collective-permute-done.28
  94.3 0.1 reshape.77
  94.4 0.6 broadcast_multiply_fusion
  (14 shorter events, 0.1 us)
Async XLA Ops:
  0.6 16.2 %copy-start = (s32[2,1,4]{2,1,0:T(1,128)S(1)}, s32[2,1,4]{2,1,0:T(1,128)}, u32[]{:S(2)}) copy-start(s32[2,1,4]{2,1,0:T(1,128)} %param.3) | copy-start | bytes 100
  0.6 10.6 %collective-permute-start = (bf16[2,2,64,1024]{3,2,1,0:T(8,128)(2,1)}, bf16[2,2,64,1024]{3,2,1,0:T(8,128)(2,1)S(1)}, u32[]{:S(2)}, u32[]{:S(2)}) collective-permute-start(bf16[2,2,64,1024]{3,2,1,0:T(8,128)(2,1)} %bitcast.15), channel_id=1, source_target_pairs={{0,128},{1,144},{2,130},{3,146},{4,132},{5,148},{6,134},{7,150},{8... | collective-permute-start | bytes 1572872 | tf_op jit(solution)/shard_map/ppermute | solution.py:27
  11.3 5.6 %collective-permute-start.3 = (bf16[2,2,64,1024]{3,2,1,0:T(8,128)(2,1)S(1)}, bf16[2,2,64,1024]{3,2,1,0:T(8,128)(2,1)S(1)}, u32[]{:S(2)}, u32[]{:S(2)}) collective-permute-start(bf16[2,2,64,1024]{3,2,1,0:T(8,128)(2,1)S(1)} %collective-permute-done.own.refs_2_.refs_0_), channel_id=1, source_target_pairs={{0,16},{1,17},{2,18},{3,19},{4,20},{5,21},{6,22},{7,23},{8,24},{9,... | collective-permute-start | bytes 1572872 | tf_op jit(solution)/shard_map/ppermute | solution.py:27
  12.8 10.2 %collective-permute-start.1 = (bf16[2,2,64,1024]{3,2,1,0:T(8,128)(2,1)S(1)}, bf16[2,2,64,1024]{3,2,1,0:T(8,128)(2,1)S(1)}, u32[]{:S(2)}, u32[]{:S(2)}) collective-permute-start(bf16[2,2,64,1024]{3,2,1,0:T(8,128)(2,1)S(1)} %collective-permute-done.own.refs_2_.refs_0_), channel_id=1, source_target_pairs={{0,2},{1,3},{2,4},{3,5},{4,6},{5,7},{6,8},{7,9},{8,10},{9,11},{10,... | collective-permute-start | bytes 1572872 | tf_op jit(solution)/shard_map/ppermute | solution.py:27
  16.9 11.7 %collective-permute-start.6 = (bf16[2,2,64,1024]{3,2,1,0:T(8,128)(2,1)S(1)}, bf16[2,2,64,1024]{3,2,1,0:T(8,128)(2,1)S(1)}, u32[]{:S(2)}, u32[]{:S(2)}) collective-permute-start(bf16[2,2,64,1024]{3,2,1,0:T(8,128)(2,1)S(1)} %collective-permute-done.3.other.refs_3_.refs_8_), channel_id=1, source_target_pairs={{0,2},{1,3},{2,4},{3,5},{4,6},{5,7},{6,8},{7,9},{8,10},{9,11},{10,... | collective-permute-start | bytes 1572872 | tf_op jit(solution)/shard_map/ppermute | solution.py:27
  19.4 14.8 %collective-permute-start.4 = (bf16[2,128,1024]{2,1,0:T(8,128)(2,1)S(1)}, bf16[2,128,1024]{2,1,0:T(8,128)(2,1)S(1)}, u32[]{:S(2)}, u32[]{:S(2)}) collective-permute-start(bf16[2,128,1024]{2,1,0:T(8,128)(2,1)S(1)} %shard_map.41), channel_id=1, source_target_pairs={{0,33},{1,0},{2,35},{3,2},{4,37},{5,4},{6,39},{7,6},{8,41},{9,8},{... | collective-permute-start | bytes 1572872 | tf_op jit(solution)/shard_map/ppermute | solution.py:27
  23.0 12.1 %collective-permute-start.2 = (bf16[2,2,64,1024]{3,2,1,0:T(8,128)(2,1)S(1)}, bf16[2,2,64,1024]{3,2,1,0:T(8,128)(2,1)S(1)}, u32[]{:S(2)}, u32[]{:S(2)}) collective-permute-start(bf16[2,2,64,1024]{3,2,1,0:T(8,128)(2,1)S(1)} %collective-permute-done.1.refs_1_.refs_2_), channel_id=1, source_target_pairs={{0,2},{1,3},{2,4},{3,5},{4,6},{5,7},{6,8},{7,9},{8,10},{9,11},{10,... | collective-permute-start | bytes 1572872 | tf_op jit(solution)/shard_map/ppermute | solution.py:27
  26.4 12.3 %collective-permute-start.8 = (bf16[2,2,64,1024]{3,2,1,0:T(8,128)(2,1)S(1)}, bf16[2,2,64,1024]{3,2,1,0:T(8,128)(2,1)S(1)}, u32[]{:S(2)}, u32[]{:S(2)}) collective-permute-start(bf16[2,2,64,1024]{3,2,1,0:T(8,128)(2,1)S(1)} %collective-permute-done.1.refs_1_.refs_2_), channel_id=1, source_target_pairs={{0,16},{1,17},{2,18},{3,19},{4,20},{5,21},{6,22},{7,23},{8,24},{9,... | collective-permute-start | bytes 1572872 | tf_op jit(solution)/shard_map/ppermute | solution.py:27
  28.6 12.2 %collective-permute-start.10 = (bf16[2,2,64,1024]{3,2,1,0:T(8,128)(2,1)S(1)}, bf16[2,2,64,1024]{3,2,1,0:T(8,128)(2,1)S(1)}, u32[]{:S(2)}, u32[]{:S(2)}) collective-permute-start(bf16[2,2,64,1024]{3,2,1,0:T(8,128)(2,1)S(1)} %collective-permute-done.6.refs_4_.refs_6_.refs_9_), channel_id=1, source_target_pairs={{0,2},{1,3},{2,4},{3,5},{4,6},{5,7},{6,8},{7,9},{8,10},{9,11},{10,... | collective-permute-start | bytes 1572872 | tf_op jit(solution)/shard_map/ppermute | solution.py:27
  31.7 7.0 %collective-permute-start.7 = (bf16[2,2,64,1024]{3,2,1,0:T(8,128)(2,1)S(1)}, bf16[2,2,64,1024]{3,2,1,0:T(8,128)(2,1)S(1)}, u32[]{:S(2)}, u32[]{:S(2)}) collective-permute-start(bf16[2,2,64,1024]{3,2,1,0:T(8,128)(2,1)S(1)} %collective-permute-done.6.refs_4_.refs_6_.refs_9_), channel_id=1, source_target_pairs={{0,16},{1,17},{2,18},{3,19},{4,20},{5,21},{6,22},{7,23},{8,24},{9,... | collective-permute-start | bytes 1572872 | tf_op jit(solution)/shard_map/ppermute | solution.py:27
  35.1 10.4 %collective-permute-start.5 = (bf16[2,2,64,1024]{3,2,1,0:T(8,128)(2,1)S(1)}, bf16[2,2,64,1024]{3,2,1,0:T(8,128)(2,1)S(1)}, u32[]{:S(2)}, u32[]{:S(2)}) collective-permute-start(bf16[2,2,64,1024]{3,2,1,0:T(8,128)(2,1)S(1)} %collective-permute-done.2.refs_4_.refs_0_.refs_3_), channel_id=1, source_target_pairs={{0,2},{1,3},{2,4},{3,5},{4,6},{5,7},{6,8},{7,9},{8,10},{9,11},{10,... | collective-permute-start | bytes 1572872 | tf_op jit(solution)/shard_map/ppermute | solution.py:27
  39.4 8.1 %collective-permute-start.9 = (bf16[3,2,128,128]{3,2,1,0:T(8,128)(2,1)S(1)}, bf16[3,2,128,128]{3,2,1,0:T(8,128)(2,1)S(1)}, u32[]{:S(2)}, u32[]{:S(2)}) collective-permute-start(bf16[3,2,128,128]{3,2,1,0:T(8,128)(2,1)S(1)} %shard_map.43), channel_id=1, source_target_pairs={{0,33},{1,0},{2,35},{3,2},{4,37},{5,4},{6,39},{7,6},{8,41},{9,8},{... | collective-permute-start | bytes 589832 | tf_op jit(solution)/shard_map/ppermute | solution.py:27
  39.5 9.1 %collective-permute-start.13 = (bf16[2,2,64,1024]{3,2,1,0:T(8,128)(2,1)S(1)}, bf16[2,2,64,1024]{3,2,1,0:T(8,128)(2,1)S(1)}, u32[]{:S(2)}, u32[]{:S(2)}) collective-permute-start(bf16[2,2,64,1024]{3,2,1,0:T(8,128)(2,1)S(1)} %collective-permute-done.2.refs_4_.refs_0_.refs_3_), channel_id=1, source_target_pairs={{0,16},{1,17},{2,18},{3,19},{4,20},{5,21},{6,22},{7,23},{8,24},{9,... | collective-permute-start | bytes 1572872 | tf_op jit(solution)/shard_map/ppermute | solution.py:27
  40.8 7.8 %collective-permute-start.12 = (bf16[2,2,64,1024]{3,2,1,0:T(8,128)(2,1)S(1)}, bf16[2,2,64,1024]{3,2,1,0:T(8,128)(2,1)S(1)}, u32[]{:S(2)}, u32[]{:S(2)}) collective-permute-start(bf16[2,2,64,1024]{3,2,1,0:T(8,128)(2,1)S(1)} %collective-permute-done.10.refs_8_.refs_2_.refs_11_), channel_id=1, source_target_pairs={{0,16},{1,17},{2,18},{3,19},{4,20},{5,21},{6,22},{7,23},{8,24},{9,... | collective-permute-start | bytes 1572872 | tf_op jit(solution)/shard_map/ppermute | solution.py:27
  41.7 11.6 %collective-permute-start.11 = (bf16[2,2,64,1024]{3,2,1,0:T(8,128)(2,1)S(1)}, bf16[2,2,64,1024]{3,2,1,0:T(8,128)(2,1)S(1)}, u32[]{:S(2)}, u32[]{:S(2)}) collective-permute-start(bf16[2,2,64,1024]{3,2,1,0:T(8,128)(2,1)S(1)} %collective-permute-done.10.refs_8_.refs_2_.refs_11_), channel_id=1, source_target_pairs={{0,2},{1,3},{2,4},{3,5},{4,6},{5,7},{6,8},{7,9},{8,10},{9,11},{10,... | collective-permute-start | bytes 1572872 | tf_op jit(solution)/shard_map/ppermute | solution.py:27
  47.6 10.0 %collective-permute-start.16 = (bf16[2,2,64,1024]{3,2,1,0:T(8,128)(2,1)S(1)}, bf16[2,2,64,1024]{3,2,1,0:T(8,128)(2,1)S(1)}, u32[]{:S(2)}, u32[]{:S(2)}) collective-permute-start(bf16[2,2,64,1024]{3,2,1,0:T(8,128)(2,1)S(1)} %collective-permute-done.5.refs_2_.refs_5_.own_u), channel_id=1, source_target_pairs={{0,2},{1,3},{2,4},{3,5},{4,6},{5,7},{6,8},{7,9},{8,10},{9,11},{10,... | collective-permute-start | bytes 1572872 | tf_op jit(solution)/shard_map/ppermute | solution.py:27
  49.2 8.3 %collective-permute-start.17 = (bf16[2,2,128,128]{3,2,1,0:T(8,128)(2,1)S(1)}, bf16[2,2,128,128]{3,2,1,0:T(8,128)(2,1)S(1)}, u32[]{:S(2)}, u32[]{:S(2)}) collective-permute-start(bf16[2,2,128,128]{3,2,1,0:T(8,128)(2,1)S(1)} %shard_map.46), channel_id=1, source_target_pairs={{0,33},{1,0},{2,35},{3,2},{4,37},{5,4},{6,39},{7,6},{8,41},{9,8},{... | collective-permute-start | bytes 393224 | tf_op jit(solution)/shard_map/ppermute | solution.py:27
  50.5 8.0 %collective-permute-start.15 = (bf16[2,2,64,1024]{3,2,1,0:T(8,128)(2,1)S(1)}, bf16[2,2,64,1024]{3,2,1,0:T(8,128)(2,1)S(1)}, u32[]{:S(2)}, u32[]{:S(2)}) collective-permute-start(bf16[2,2,64,1024]{3,2,1,0:T(8,128)(2,1)S(1)} %collective-permute-done.5.refs_2_.refs_5_.own_u), channel_id=1, source_target_pairs={{0,16},{1,17},{2,18},{3,19},{4,20},{5,21},{6,22},{7,23},{8,24},{9,... | collective-permute-start | bytes 1572872 | tf_op jit(solution)/shard_map/ppermute | solution.py:27
  53.3 5.2 %collective-permute-start.14 = (bf16[2,2,64,1024]{3,2,1,0:T(8,128)(2,1)S(1)}, bf16[2,2,64,1024]{3,2,1,0:T(8,128)(2,1)S(1)}, u32[]{:S(2)}, u32[]{:S(2)}) collective-permute-start(bf16[2,2,64,1024]{3,2,1,0:T(8,128)(2,1)S(1)} %collective-permute-done.11.refs_4_.refs_13_.other_u), channel_id=1, source_target_pairs={{0,16},{1,17},{2,18},{3,19},{4,20},{5,21},{6,22},{7,23},{8,24},{9,... | collective-permute-start | bytes 1572872 | tf_op jit(solution)/shard_map/ppermute | solution.py:27
  57.6 6.6 %collective-permute-start.18 = (bf16[2,2,64,1024]{3,2,1,0:T(8,128)(2,1)S(1)}, bf16[2,2,64,1024]{3,2,1,0:T(8,128)(2,1)S(1)}, u32[]{:S(2)}, u32[]{:S(2)}) collective-permute-start(bf16[2,2,64,1024]{3,2,1,0:T(8,128)(2,1)S(1)} %collective-permute-done.16.refs_7_), channel_id=1, source_target_pairs={{0,16},{1,17},{2,18},{3,19},{4,20},{5,21},{6,22},{7,23},{8,24},{9,... | collective-permute-start | bytes 1572872 | tf_op jit(solution)/shard_map/ppermute | solution.py:27
  59.2 11.3 %collective-permute-start.19 = (bf16[2,2,128,128]{3,2,1,0:T(8,128)(2,1)S(1)}, bf16[2,2,128,128]{3,2,1,0:T(8,128)(2,1)S(1)}, u32[]{:S(2)}, u32[]{:S(2)}) collective-permute-start(bf16[2,2,128,128]{3,2,1,0:T(8,128)(2,1)S(1)} %get-tuple-element.34), channel_id=1, source_target_pairs={{0,33},{1,0},{2,35},{3,2},{4,37},{5,4},{6,39},{7,6},{8,41},{9,8},{... | collective-permute-start | bytes 393224 | tf_op jit(solution)/shard_map/ppermute | solution.py:27
  60.5 10.0 %collective-permute-start.20 = (bf16[2,128,128]{2,1,0:T(8,128)(2,1)S(1)}, bf16[2,128,128]{2,1,0:T(8,128)(2,1)S(1)}, u32[]{:S(2)}, u32[]{:S(2)}) collective-permute-start(bf16[2,128,128]{2,1,0:T(8,128)(2,1)S(1)} %get-tuple-element.35), channel_id=1, source_target_pairs={{0,35},{1,2},{2,37},{3,4},{4,39},{5,6},{6,41},{7,8},{8,43},{9,10},... | collective-permute-start | bytes 196616 | tf_op jit(solution)/shard_map/ppermute | solution.py:27
  66.6 8.5 %collective-permute-start.23 = (bf16[2,64,1024]{2,1,0:T(8,128)(2,1)S(1)}, bf16[2,64,1024]{2,1,0:T(8,128)(2,1)S(1)}, u32[]{:S(2)}, u32[]{:S(2)}) collective-permute-start(bf16[2,64,1024]{2,1,0:T(8,128)(2,1)S(1)} %get-tuple-element.36), channel_id=1, source_target_pairs={{0,128},{1,112},{2,130},{3,114},{4,132},{5,116},{6,134},{7,118},{8... | collective-permute-start | bytes 786440 | tf_op jit(solution)/shard_map/ppermute | solution.py:27
  71.3 3.6 %collective-permute-start.22 = (f32[1,128]{1,0:T(1,128)S(1)}, f32[1,128]{1,0:T(1,128)S(1)}, u32[]{:S(2)}, u32[]{:S(2)}) collective-permute-start(f32[1,128]{1,0:T(1,128)S(1)} %shard_map.49), channel_id=1, source_target_pairs={{0,2},{1,3},{2,4},{3,5},{4,6},{5,7},{6,8},{7,9},{8,10},{9,11},{10,... | collective-permute-start | bytes 1544 | tf_op jit(solution)/shard_map/ppermute | solution.py:27
  71.3 3.6 %collective-permute-start.21 = (f32[1,128]{1,0:T(1,128)S(1)}, f32[1,128]{1,0:T(1,128)S(1)}, u32[]{:S(2)}, u32[]{:S(2)}) collective-permute-start(f32[1,128]{1,0:T(1,128)S(1)} %shard_map.49), channel_id=1, source_target_pairs={{0,14},{1,15},{2,0},{3,1},{4,2},{5,3},{6,4},{7,5},{8,6},{9,7},{10,... | collective-permute-start | bytes 1544 | tf_op jit(solution)/shard_map/ppermute | solution.py:27
  74.0 9.6 %collective-permute-start.26 = (bf16[2,64,1024]{2,1,0:T(8,128)(2,1)S(1)}, bf16[2,64,1024]{2,1,0:T(8,128)(2,1)S(1)}, u32[]{:S(2)}, u32[]{:S(2)}) collective-permute-start(bf16[2,64,1024]{2,1,0:T(8,128)(2,1)S(1)} %get-tuple-element.40), channel_id=1, source_target_pairs={{0,129},{1,113},{2,131},{3,115},{4,133},{5,117},{6,135},{7,119},{8... | collective-permute-start | bytes 786440 | tf_op jit(solution)/shard_map/ppermute | solution.py:27
  75.1 5.4 %collective-permute-start.24 = (f32[1,128]{1,0:T(1,128)S(1)}, f32[1,128]{1,0:T(1,128)S(1)}, u32[]{:S(2)}, u32[]{:S(2)}) collective-permute-start(f32[1,128]{1,0:T(1,128)S(1)} %get-tuple-element.37), channel_id=1, source_target_pairs={{0,6},{1,7},{2,8},{3,9},{4,10},{5,11},{6,12},{7,13},{8,14},{9,15},... | collective-permute-start | bytes 1544 | tf_op jit(solution)/shard_map/ppermute | solution.py:27
  79.3 4.2 %collective-permute-start.25 = (f32[1,128]{1,0:T(1,128)S(1)}, f32[1,128]{1,0:T(1,128)S(1)}, u32[]{:S(2)}, u32[]{:S(2)}) collective-permute-start(f32[1,128]{1,0:T(1,128)S(1)} %get-tuple-element.38), channel_id=1, source_target_pairs={{0,10},{1,11},{2,12},{3,13},{4,14},{5,15},{6,0},{7,1},{8,2},{9,3},... | collective-permute-start | bytes 1544 | tf_op jit(solution)/shard_map/ppermute | solution.py:27
  83.5 10.7 %collective-permute-start.28 = (f32[1,128]{1,0:T(1,128)S(1)}, f32[1,128]{1,0:T(1,128)S(1)}, u32[]{:S(2)}, u32[]{:S(2)}) collective-permute-start(f32[1,128]{1,0:T(1,128)S(1)} %add_add_fusion), channel_id=1, source_target_pairs={{0,129},{1,113},{2,131},{3,115},{4,133},{5,117},{6,135},{7,119},{8... | collective-permute-start | bytes 1544 | tf_op jit(solution)/shard_map/ppermute | solution.py:27
  87.7 6.6 %collective-permute-start.27 = (f32[1,128]{1,0:T(1,128)S(1)}, f32[1,128]{1,0:T(1,128)S(1)}, u32[]{:S(2)}, u32[]{:S(2)}) collective-permute-start(f32[1,128]{1,0:T(1,128)S(1)} %add_add_fusion), channel_id=1, source_target_pairs={{0,128},{1,112},{2,130},{3,114},{4,132},{5,116},{6,134},{7,118},{8... | collective-permute-start | bytes 1544 | tf_op jit(solution)/shard_map/ppermute | solution.py:27

commit v11 on v10

--- a/solution.py
+++ b/solution.py
@@ -44,10 +44,11 @@
     return (column, h, z, half)
 
 
-def hub_ahead(step):
+def hub_ahead(step, turn=0):
     def route(m, c, z, h):
-        column, half = hub_of(SERVED[m, h] + 1 + c)
-        return (column, c, z + (step if c == 0 else -step), half)
+        r = c ^ turn
+        column, half = hub_of(SERVED[m, h] + 1 + r)
+        return (column, r, z + (step if r == 0 else -step), half)
 
     return route
 
@@ -61,6 +62,7 @@
 
 
 WEIGHT = 3_000_000_000
+ROOM = 5_000_000_000
 
 VMEM = pl.BlockSpec(memory_space=pltpu.VMEM)
 SMEM = pl.BlockSpec(memory_space=pltpu.SMEM)
@@ -101,10 +103,12 @@
     return jnp.concatenate(halves(info, own_ref[momentum, part], other_ref[momentum, part]), axis=0)
 
 
-def cut(info, own_ref, other_ref, offset, out):
+def cut(info, own_ref, other_ref, offset, out, momentum=5):
     columns = columns_of(info, offset)
     for part in range(2):
-        first, second = halves(info, own_ref[info[5], part, :, columns], other_ref[info[5], part, :, columns])
+        first, second = halves(
+            info, own_ref[info[momentum], part, :, columns], other_ref[info[momentum], part, :, columns]
+        )
         out[part] = jnp.concatenate([first, second], axis=0).T
 
 
@@ -119,10 +123,10 @@
         cut(info, refs[k], refs[count + k], 0, refs[-1].at[k])
 
 
-def late_kernel(info, own_u, own_d, other_u, other_d, out, across):
-    cut(info, own_u, other_u, 0, out.at[0])
-    cut(info, own_d, other_d, 0, out.at[1])
-    cut(info, own_u, other_u, -1, across)
+def late_kernel(info, own, other, here, there, across):
+    cut(info, own, other, 0, here)
+    cut(info, own, other, 0, there, momentum=6)
+    cut(info, own, other, -1, across)
 
 
 def left_side(info, a_ref, offset):
@@ -179,8 +183,12 @@
     return [jnp.sum(part, axis=0, keepdims=True) for part in (re, im)]
 
 
-def trace_kernel(info, product, early, late, across, trace):
-    re, im = trace_sum(info, product, [(3, late.at[0]), (-3, late.at[1]), (4, across)])
+def collect_kernel(info, here, there, across, out):
+    out[0], out[1], out[2] = here[...], there[...], across[...]
+
+
+def trace_kernel(info, product, early, late, trace):
+    re, im = trace_sum(info, product, [(3, late.at[0]), (-3, late.at[1]), (4, late.at[2])])
     re = jnp.sum(re + early[0:1, :], axis=1, keepdims=True)
     im = jnp.sum(im + early[1:2, :], axis=1, keepdims=True)
     lane = lax.broadcasted_iota(jnp.int32, (1, 128), 1)
@@ -192,7 +200,8 @@
     tm, row = lax.axis_index("tm"), lax.axis_index("row")
     core, place, half = tm % 2, row // 2, row % 2
     momenta = lax.dynamic_index_in_dim(mom_table, core, 0, keepdims=False)[0]
-    info = jnp.concatenate([jnp.stack([place, core]), momenta])
+    others = lax.dynamic_index_in_dim(mom_table, 1 - core, 0, keepdims=False)[0]
+    info = jnp.concatenate([jnp.stack([place, core]), momenta, others[3:]])
     wall = lax.optimization_barrier
     block_of_products = jax.ShapeDtypeStruct((256, 1024), F32)
 
@@ -223,16 +232,18 @@
     )
     q3, acc = wall((q3, acc))
 
-    q3x = moved(q3, other_core)
+    piece = jax.ShapeDtypeStruct((2, 128, 128), BF16)
+    here, there, across = call(late_kernel, info, [p3, q3], (piece, piece, piece), 1)
+    here, there, across = moved(here, hub_ahead(0)), moved(there, hub_ahead(0, 1)), moved(across, hub_ahead(1))
+    late = call(collect_kernel, info, [here, there, across], slices_of(3), ROOM)
+    p4, middle = wall((p4, middle))
+
+    p4x, q3x = moved(p4, other_core), moved(q3, other_core)
     two, two_x = [p3, q3x], [q3, p3x]
-    late, across = call(late_kernel, info, two + two_x, (slices_of(2), jax.ShapeDtypeStruct((2, 128, 128), BF16)), 1)
-    p4, middle = wall((p4, middle))
-
-    p4x = moved(p4, other_core)
-    late, across = moved(late, hub_ahead(0)), moved(across, hub_ahead(1))
     acc = call(
         lambda *refs: products_kernel(OFFSETS[5:7], *refs), info, [a] + two + two_x + [acc], block_of_products, 1
     )
+    p4x, late = wall((p4x, late))
     half_block = jax.ShapeDtypeStruct((2, 64, 1024), BF16)
     keep, send, product, early = call(
         last_kernel,
@@ -242,7 +253,7 @@
         1,
         [pltpu.VMEM((2, 128, 1024), BF16)],
     )
-    trace = call(trace_kernel, info, [product, early, late, across], jax.ShapeDtypeStruct((1, 128), F32), 1)
+    trace = call(trace_kernel, info, [product, early, late], jax.ShapeDtypeStruct((1, 128), F32), 1)
 
     below, above = moved(trace, along(1)), moved(trace, along(-1))
     kept, sent = moved(keep, from_hub(0)), moved(send, from_hub(1))

time: 95 us -> 94.5 us (level)
  starting transfers between devices: 57.8 us -> 48.1 us
  waiting for transfers between devices: 25.9 us -> 32.5 us
  local copies, waits for them, and re-layouts: 0.09 us -> 1.34 us
    ppermute x29 -> x30, starting transfers between devices: 57.8 us -> 48.1 us  [moved(): lax.ppermute(block, BOTH, [(index_of(*at), index_of(*route(*at))) for at...]
    ppermute x29 -> x30, waiting for transfers between devices: 25.9 us -> 32.5 us  [moved(): lax.ppermute(block, BOTH, [(index_of(*at), index_of(*route(*at))) for at...]
    pallas_call x9 -> x10, Pallas kernels: 8.85 us -> 9.41 us  [call(): pl.pallas_call(kernel, out_shape=out_shape, in_specs=[SMEM] + [VMEM] * le...]
  transfers between devices with their start and end apart: 29 -> 30, of which waited for: 11 -> 13; matrix products, arithmetic and copies ran while one was open for 1% -> 2% of each run, Pallas kernels for 9% -> 7%
where the time goes in v11:
time: 94.5 us; the launch traced here: 94.4 us
  starting transfers between devices  48.1 us (51%)
  waiting for transfers between devices  32.5 us (34%)
  Pallas kernels  9.41 us (10%)
  other arithmetic  2.2 us (2%)
  local copies, waits for them, and re-layouts  1.34 us (1%)
    ppermute x30, starting transfers between devices, moved(): lax.ppermute(block, BOTH, [(index_of(*at), index_of(*route(*at))) for at...  48.1 us
    ppermute x30, waiting for transfers between devices, moved(): lax.ppermute(block, BOTH, [(index_of(*at), index_of(*route(*at))) for at...  32.5 us
    pallas_call x10, Pallas kernels, call(): pl.pallas_call(kernel, out_shape=out_shape, in_specs=[SMEM] + [VMEM] * le...  9.41 us
  transfers between devices with their start and end apart: 30, of which 13 were waited for; matrix products, arithmetic and copies ran while one was open for 2% of the time, Pallas kernels for 7%

profile of v11, /device:TPU:1, one launch (start us, length us, event | category | flops | bytes accessed | tf_op | source)
XLA Modules:
  0.0 94.4 jit_solution(3117890094500290741)
XLA Ops:
  0.6 4.2 %collective-permute-start = (bf16[2,2,64,1024]{3,2,1,0:T(8,128)(2,1)}, bf16[2,2,64,1024]{3,2,1,0:T(8,128)(2,1)S(1)}, u32[]{:S(2)}, u32[]{:S(2)}) collective-permute-start(bf16[2,2,64,1024]{3,2,1,0:T(8,128)(2,1)} %bitcast.16), channel_id=1, source_target_pairs={{0,128},{1,144},{2,130},{3,146},{4,132},{5,148},{6,134},{7,150},{8... | collective-permute-start | bytes 1572872 | tf_op jit(solution)/shard_map/ppermute | solution.py:27
  4.8 6.4 %collective-permute-done.own.refs_2_.refs_0_ = bf16[2,2,64,1024]{3,2,1,0:T(8,128)(2,1)S(1)} collective-permute-done((bf16[2,2,64,1024]{3,2,1,0:T(8,128)(2,1)}, bf16[2,2,64,1024]{3,2,1,0:T(8,128)(2,1)S(1)}, u32[]{:S(2)}, u32[]{:S(2)}) %collective-permute-start) | collective-permute-done | bytes 524320 | tf_op jit(solution)/shard_map/ppermute | solution.py:27
  11.3 1.5 %collective-permute-start.3 = (bf16[2,2,64,1024]{3,2,1,0:T(8,128)(2,1)S(1)}, bf16[2,2,64,1024]{3,2,1,0:T(8,128)(2,1)S(1)}, u32[]{:S(2)}, u32[]{:S(2)}) collective-permute-start(bf16[2,2,64,1024]{3,2,1,0:T(8,128)(2,1)S(1)} %collective-permute-done.own.refs_2_.refs_0_), channel_id=1, source_target_pairs={{0,16},{1,17},{2,18},{3,19},{4,20},{5,21},{6,22},{7,23},{8,24},{9,... | collective-permute-start | bytes 1572872 | tf_op jit(solution)/shard_map/ppermute | solution.py:27
  12.8 4.1 %collective-permute-start.1 = (bf16[2,2,64,1024]{3,2,1,0:T(8,128)(2,1)S(1)}, bf16[2,2,64,1024]{3,2,1,0:T(8,128)(2,1)S(1)}, u32[]{:S(2)}, u32[]{:S(2)}) collective-permute-start(bf16[2,2,64,1024]{3,2,1,0:T(8,128)(2,1)S(1)} %collective-permute-done.own.refs_2_.refs_0_), channel_id=1, source_target_pairs={{0,2},{1,3},{2,4},{3,5},{4,6},{5,7},{6,8},{7,9},{8,10},{9,11},{10,... | collective-permute-start | bytes 1572872 | tf_op jit(solution)/shard_map/ppermute | solution.py:27
  16.9 0.7 copy-done
  17.5 0.6 slice.9
  18.1 0.0 collective-permute-done.3.other.refs_3_.refs_8_
  18.1 0.7 collective-permute-start.6
  18.9 0.7 pad_add_fusion.info.refs_0_
  19.6 0.6 shard_map.41
  20.2 1.3 %collective-permute-start.4 = (bf16[2,128,1024]{2,1,0:T(8,128)(2,1)S(1)}, bf16[2,128,1024]{2,1,0:T(8,128)(2,1)S(1)}, u32[]{:S(2)}, u32[]{:S(2)}) collective-permute-start(bf16[2,128,1024]{2,1,0:T(8,128)(2,1)S(1)} %shard_map.41), channel_id=1, source_target_pairs={{0,33},{1,0},{2,35},{3,2},{4,37},{5,4},{6,39},{7,6},{8,41},{9,8},{... | collective-permute-start | bytes 1572872 | tf_op jit(solution)/shard_map/ppermute | solution.py:27
  21.5 1.5 %collective-permute-done.1.refs_1_.refs_2_ = bf16[2,2,64,1024]{3,2,1,0:T(8,128)(2,1)S(1)} collective-permute-done((bf16[2,2,64,1024]{3,2,1,0:T(8,128)(2,1)S(1)}, bf16[2,2,64,1024]{3,2,1,0:T(8,128)(2,1)S(1)}, u32[]{:S(2)}, u32[]{:S(2)}) %collective-permute-start.1) | collective-permute-done | bytes 524320 | tf_op jit(solution)/shard_map/ppermute | solution.py:27
  23.0 3.4 %collective-permute-start.2 = (bf16[2,2,64,1024]{3,2,1,0:T(8,128)(2,1)S(1)}, bf16[2,2,64,1024]{3,2,1,0:T(8,128)(2,1)S(1)}, u32[]{:S(2)}, u32[]{:S(2)}) collective-permute-start(bf16[2,2,64,1024]{3,2,1,0:T(8,128)(2,1)S(1)} %collective-permute-done.1.refs_1_.refs_2_), channel_id=1, source_target_pairs={{0,2},{1,3},{2,4},{3,5},{4,6},{5,7},{6,8},{7,9},{8,10},{9,11},{10,... | collective-permute-start | bytes 1572872 | tf_op jit(solution)/shard_map/ppermute | solution.py:27
  26.4 0.0 collective-permute-start.8
  26.4 2.2 %collective-permute-done.6.refs_4_.refs_6_.refs_9_ = bf16[2,2,64,1024]{3,2,1,0:T(8,128)(2,1)S(1)} collective-permute-done((bf16[2,2,64,1024]{3,2,1,0:T(8,128)(2,1)S(1)}, bf16[2,2,64,1024]{3,2,1,0:T(8,128)(2,1)S(1)}, u32[]{:S(2)}, u32[]{:S(2)}) %collective-permute-start.6) | collective-permute-done | bytes 524320 | tf_op jit(solution)/shard_map/ppermute | solution.py:27
  28.6 3.1 %collective-permute-start.10 = (bf16[2,2,64,1024]{3,2,1,0:T(8,128)(2,1)S(1)}, bf16[2,2,64,1024]{3,2,1,0:T(8,128)(2,1)S(1)}, u32[]{:S(2)}, u32[]{:S(2)}) collective-permute-start(bf16[2,2,64,1024]{3,2,1,0:T(8,128)(2,1)S(1)} %collective-permute-done.6.refs_4_.refs_6_.refs_9_), channel_id=1, source_target_pairs={{0,2},{1,3},{2,4},{3,5},{4,6},{5,7},{6,8},{7,9},{8,10},{9,11},{10,... | collective-permute-start | bytes 1572872 | tf_op jit(solution)/shard_map/ppermute | solution.py:27
  31.7 0.0 collective-permute-start.7
  31.7 4.3 %collective-permute-done.4.refs_1_.a_ref = bf16[2,128,1024]{2,1,0:T(8,128)(2,1)S(1)} collective-permute-done((bf16[2,128,1024]{2,1,0:T(8,128)(2,1)S(1)}, bf16[2,128,1024]{2,1,0:T(8,128)(2,1)S(1)}, u32[]{:S(2)}, u32[]{:S(2)}) %collective-permute-start.4) | collective-permute-done | bytes 524320 | tf_op jit(solution)/shard_map/ppermute | solution.py:27
  36.1 0.9 shard_map.42.refs_10_
  36.9 0.0 collective-permute-done.2.refs_4_.refs_0_.refs_3_
  36.9 2.4 %collective-permute-start.5 = (bf16[2,2,64,1024]{3,2,1,0:T(8,128)(2,1)S(1)}, bf16[2,2,64,1024]{3,2,1,0:T(8,128)(2,1)S(1)}, u32[]{:S(2)}, u32[]{:S(2)}) collective-permute-start(bf16[2,2,64,1024]{3,2,1,0:T(8,128)(2,1)S(1)} %collective-permute-done.2.refs_4_.refs_0_.refs_3_), channel_id=1, source_target_pairs={{0,2},{1,3},{2,4},{3,5},{4,6},{5,7},{6,8},{7,9},{8,10},{9,11},{10,... | collective-permute-start | bytes 1572872 | tf_op jit(solution)/shard_map/ppermute | solution.py:27
  39.4 0.0 collective-permute-done.8.refs_5_.refs_7_.refs_10_
  39.4 0.7 shard_map.43
  40.1 0.1 collective-permute-start.9
  40.2 1.1 %collective-permute-start.13 = (bf16[2,2,64,1024]{3,2,1,0:T(8,128)(2,1)S(1)}, bf16[2,2,64,1024]{3,2,1,0:T(8,128)(2,1)S(1)}, u32[]{:S(2)}, u32[]{:S(2)}) collective-permute-start(bf16[2,2,64,1024]{3,2,1,0:T(8,128)(2,1)S(1)} %collective-permute-done.2.refs_4_.refs_0_.refs_3_), channel_id=1, source_target_pairs={{0,16},{1,17},{2,18},{3,19},{4,20},{5,21},{6,22},{7,23},{8,24},{9,... | collective-permute-start | bytes 1572872 | tf_op jit(solution)/shard_map/ppermute | solution.py:27
  41.2 0.0 collective-permute-done.10.refs_8_.refs_2_.refs_11_
  41.2 0.4 collective-permute-start.12
  41.7 2.1 %collective-permute-start.11 = (bf16[2,2,64,1024]{3,2,1,0:T(8,128)(2,1)S(1)}, bf16[2,2,64,1024]{3,2,1,0:T(8,128)(2,1)S(1)}, u32[]{:S(2)}, u32[]{:S(2)}) collective-permute-start(bf16[2,2,64,1024]{3,2,1,0:T(8,128)(2,1)S(1)} %collective-permute-done.10.refs_8_.refs_2_.refs_11_), channel_id=1, source_target_pairs={{0,2},{1,3},{2,4},{3,5},{4,6},{5,7},{6,8},{7,9},{8,10},{9,11},{10,... | collective-permute-start | bytes 1572872 | tf_op jit(solution)/shard_map/ppermute | solution.py:27
  43.7 1.8 %collective-permute-done.5.refs_2_.own.refs_5_ = bf16[2,2,64,1024]{3,2,1,0:T(8,128)(2,1)S(1)} collective-permute-done((bf16[2,2,64,1024]{3,2,1,0:T(8,128)(2,1)S(1)}, bf16[2,2,64,1024]{3,2,1,0:T(8,128)(2,1)S(1)}, u32[]{:S(2)}, u32[]{:S(2)}) %collective-permute-start.5) | collective-permute-done | bytes 524320 | tf_op jit(solution)/shard_map/ppermute | solution.py:27
  45.5 2.7 %collective-permute-done.9.near = bf16[3,2,128,128]{3,2,1,0:T(8,128)(2,1)S(1)} collective-permute-done((bf16[3,2,128,128]{3,2,1,0:T(8,128)(2,1)S(1)}, bf16[3,2,128,128]{3,2,1,0:T(8,128)(2,1)S(1)}, u32[]{:S(2)}, u32[]{:S(2)}) %collective-permute-start.9) | collective-permute-done | bytes 196640 | tf_op jit(solution)/shard_map/ppermute | solution.py:27
  48.2 2.4 %collective-permute-start.16 = (bf16[2,2,64,1024]{3,2,1,0:T(8,128)(2,1)S(1)}, bf16[2,2,64,1024]{3,2,1,0:T(8,128)(2,1)S(1)}, u32[]{:S(2)}, u32[]{:S(2)}) collective-permute-start(bf16[2,2,64,1024]{3,2,1,0:T(8,128)(2,1)S(1)} %collective-permute-done.5.refs_2_.own.refs_5_), channel_id=1, source_target_pairs={{0,2},{1,3},{2,4},{3,5},{4,6},{5,7},{6,8},{7,9},{8,10},{9,11},{10,... | collective-permute-start | bytes 1572872 | tf_op jit(solution)/shard_map/ppermute | solution.py:27
  50.5 0.0 collective-permute-done.13.refs_9_.refs_3_.refs_12_
  50.5 0.0 collective-permute-done.12.refs_5_.refs_1_.refs_4_
  50.5 0.6 shard_map.46
  51.2 0.3 collective-permute-start.17
  51.4 1.3 %shard_map.44.refs_6_ = f32[256,1024]{1,0:T(8,128)S(1)} custom-call(s32[7]{0:T(128)S(1)} %pad_add_fusion.info.refs_0_, bf16[2,128,1024]{2,1,0:T(8,128)(2,1)S(1)} %collective-permute-done.4.refs_1_.a_ref, bf16[2,2,64,1024]{3,2,1,0:T(8,128)(2,1)S(1)} %collective-permute-done.1.refs_1_.refs_2_, ...), custom_call_target="tpu_custom_call" | custom-call | flops 1 | bytes 1048576 | tf_op jit(solution)/shard_map/pallas_call | solution.py:77
  52.7 0.0 collective-permute-done.11.refs_4_.other.refs_13_
  52.7 0.7 shard_map.47
  53.4 0.5 collective-permute-start.19
  54.0 4.3 %collective-permute-start.20 = (bf16[2,128,128]{2,1,0:T(8,128)(2,1)S(1)}, bf16[2,128,128]{2,1,0:T(8,128)(2,1)S(1)}, u32[]{:S(2)}, u32[]{:S(2)}) collective-permute-start(bf16[2,128,128]{2,1,0:T(8,128)(2,1)S(1)} %get-tuple-element.36), channel_id=1, source_target_pairs={{0,48},{1,49},{2,50},{3,51},{4,52},{5,53},{6,54},{7,55},{8,56},{9,... | collective-permute-start | bytes 196616 | tf_op jit(solution)/shard_map/ppermute | solution.py:27
  58.3 3.6 %collective-permute-start.21 = (bf16[2,128,128]{2,1,0:T(8,128)(2,1)S(1)}, bf16[2,128,128]{2,1,0:T(8,128)(2,1)S(1)}, u32[]{:S(2)}, u32[]{:S(2)}) collective-permute-start(bf16[2,128,128]{2,1,0:T(8,128)(2,1)S(1)} %get-tuple-element.37), channel_id=1, source_target_pairs={{0,35},{1,2},{2,37},{3,4},{4,39},{5,6},{6,41},{7,8},{8,43},{9,10},... | collective-permute-start | bytes 196616 | tf_op jit(solution)/shard_map/ppermute | solution.py:27
  61.9 0.0 collective-permute-done.17.middle
  61.9 0.5 collective-permute-start.14
  62.4 0.1 collective-permute-start.18
  62.5 0.2 collective-permute-done.20.there
  62.7 3.2 %collective-permute-done.21.across = bf16[2,128,128]{2,1,0:T(8,128)(2,1)S(1)} collective-permute-done((bf16[2,128,128]{2,1,0:T(8,128)(2,1)S(1)}, bf16[2,128,128]{2,1,0:T(8,128)(2,1)S(1)}, u32[]{:S(2)}, u32[]{:S(2)}) %collective-permute-start.21) | collective-permute-done | bytes 65568 | tf_op jit(solution)/shard_map/ppermute | solution.py:27
  65.8 0.6 shard_map.48.late
  66.4 1.0 %shard_map.45.acc = f32[256,1024]{1,0:T(8,128)S(1)} custom-call(s32[7]{0:T(128)S(1)} %pad_add_fusion.info.refs_0_, bf16[2,128,1024]{2,1,0:T(8,128)(2,1)S(1)} %collective-permute-done.4.refs_1_.a_ref, bf16[2,2,64,1024]{3,2,1,0:T(8,128)(2,1)S(1)} %collective-permute-done.5.refs_2_.own.refs_5_, ...), custom_call_target="tpu_custom_call" | custom-call | flops 1 | bytes 1048576 | tf_op jit(solution)/shard_map/pallas_call | solution.py:77
  67.4 2.4 %shard_map.49 = (bf16[2,64,1024]{2,1,0:T(8,128)(2,1)S(1)}, bf16[2,64,1024]{2,1,0:T(8,128)(2,1)S(1)}, f32[256,1024]{1,0:T(8,128)S(1)}, f32[8,128]{1,0:T(8,128)S(1)}) custom-call(s32[7]{0:T(128)S(1)} %pad_add_fusion.info.refs_0_, bf16[2,128,1024]{2,1,0:T(8,128)(2,1)S(1)} %collective-permute-done.4.refs_1_.a_ref, f32[256,1024]{1,0:T(8,128)S(1)} %shard_map.45.acc, ...), custom_call_target="tpu_custom_call" | custom-call | flops 1 | bytes 1048576 | tf_op jit(solution)/shard_map/pallas_call | solution.py:77
  69.8 1.3 %collective-permute-start.24 = (bf16[2,64,1024]{2,1,0:T(8,128)(2,1)S(1)}, bf16[2,64,1024]{2,1,0:T(8,128)(2,1)S(1)}, u32[]{:S(2)}, u32[]{:S(2)}) collective-permute-start(bf16[2,64,1024]{2,1,0:T(8,128)(2,1)S(1)} %get-tuple-element.42), channel_id=1, source_target_pairs={{0,128},{1,112},{2,130},{3,114},{4,132},{5,116},{6,134},{7,118},{8... | collective-permute-start | bytes 786440 | tf_op jit(solution)/shard_map/ppermute | solution.py:27
  71.1 0.7 shard_map.50
  71.8 0.0 collective-permute-start.23
  71.9 2.8 %collective-permute-start.22 = (f32[1,128]{1,0:T(1,128)S(1)}, f32[1,128]{1,0:T(1,128)S(1)}, u32[]{:S(2)}, u32[]{:S(2)}) collective-permute-start(f32[1,128]{1,0:T(1,128)S(1)} %shard_map.50), channel_id=1, source_target_pairs={{0,14},{1,15},{2,0},{3,1},{4,2},{5,3},{6,4},{7,5},{8,6},{9,7},{10,... | collective-permute-start | bytes 1544 | tf_op jit(solution)/shard_map/ppermute | solution.py:27
  74.7 0.5 collective-permute-start.27
  75.2 0.6 collective-permute-done.23
  75.8 3.3 %collective-permute-done.24 = bf16[2,64,1024]{2,1,0:T(8,128)(2,1)S(1)} collective-permute-done((bf16[2,64,1024]{2,1,0:T(8,128)(2,1)S(1)}, bf16[2,64,1024]{2,1,0:T(8,128)(2,1)S(1)}, u32[]{:S(2)}, u32[]{:S(2)}) %collective-permute-start.24) | collective-permute-done | bytes 262176 | tf_op jit(solution)/shard_map/ppermute | solution.py:27
  79.1 5.8 %collective-permute-start.25 = (f32[1,128]{1,0:T(1,128)S(1)}, f32[1,128]{1,0:T(1,128)S(1)}, u32[]{:S(2)}, u32[]{:S(2)}) collective-permute-start(f32[1,128]{1,0:T(1,128)S(1)} %get-tuple-element.43), channel_id=1, source_target_pairs={{0,6},{1,7},{2,8},{3,9},{4,10},{5,11},{6,12},{7,13},{8,14},{9,15},... | collective-permute-start | bytes 1544 | tf_op jit(solution)/shard_map/ppermute | solution.py:27
  85.0 0.7 collective-permute-done.25
  85.7 3.5 %collective-permute-done.26 = f32[1,128]{1,0:T(1,128)S(1)} collective-permute-done((f32[1,128]{1,0:T(1,128)S(1)}, f32[1,128]{1,0:T(1,128)S(1)}, u32[]{:S(2)}, u32[]{:S(2)}) %collective-permute-start.26) | collective-permute-done | bytes 544 | tf_op jit(solution)/shard_map/ppermute | solution.py:27
  89.2 1.6 %collective-permute-start.28 = (f32[1,128]{1,0:T(1,128)S(1)}, f32[1,128]{1,0:T(1,128)S(1)}, u32[]{:S(2)}, u32[]{:S(2)}) collective-permute-start(f32[1,128]{1,0:T(1,128)S(1)} %add_add_fusion), channel_id=1, source_target_pairs={{0,128},{1,112},{2,130},{3,114},{4,132},{5,116},{6,134},{7,118},{8... | collective-permute-start | bytes 1544 | tf_op jit(solution)/shard_map/ppermute | solution.py:27
  90.8 0.9 maximum_select_fusion
  91.6 2.0 %collective-permute-done.29 = f32[1,128]{1,0:T(1,128)S(1)} collective-permute-done((f32[1,128]{1,0:T(1,128)S(1)}, f32[1,128]{1,0:T(1,128)S(1)}, u32[]{:S(2)}, u32[]{:S(2)}) %collective-permute-start.29) | collective-permute-done | bytes 544 | tf_op jit(solution)/shard_map/ppermute | solution.py:27
  93.7 0.1 reshape.79
  93.8 0.6 broadcast_multiply_fusion
  (18 shorter events, 0.1 us)
Async XLA Ops:
  0.6 10.6 %collective-permute-start = (bf16[2,2,64,1024]{3,2,1,0:T(8,128)(2,1)}, bf16[2,2,64,1024]{3,2,1,0:T(8,128)(2,1)S(1)}, u32[]{:S(2)}, u32[]{:S(2)}) collective-permute-start(bf16[2,2,64,1024]{3,2,1,0:T(8,128)(2,1)} %bitcast.16), channel_id=1, source_target_pairs={{0,128},{1,144},{2,130},{3,146},{4,132},{5,148},{6,134},{7,150},{8... | collective-permute-start | bytes 1572872 | tf_op jit(solution)/shard_map/ppermute | solution.py:27
  11.3 6.8 %collective-permute-start.3 = (bf16[2,2,64,1024]{3,2,1,0:T(8,128)(2,1)S(1)}, bf16[2,2,64,1024]{3,2,1,0:T(8,128)(2,1)S(1)}, u32[]{:S(2)}, u32[]{:S(2)}) collective-permute-start(bf16[2,2,64,1024]{3,2,1,0:T(8,128)(2,1)S(1)} %collective-permute-done.own.refs_2_.refs_0_), channel_id=1, source_target_pairs={{0,16},{1,17},{2,18},{3,19},{4,20},{5,21},{6,22},{7,23},{8,24},{9,... | collective-permute-start | bytes 1572872 | tf_op jit(solution)/shard_map/ppermute | solution.py:27
  12.8 10.2 %collective-permute-start.1 = (bf16[2,2,64,1024]{3,2,1,0:T(8,128)(2,1)S(1)}, bf16[2,2,64,1024]{3,2,1,0:T(8,128)(2,1)S(1)}, u32[]{:S(2)}, u32[]{:S(2)}) collective-permute-start(bf16[2,2,64,1024]{3,2,1,0:T(8,128)(2,1)S(1)} %collective-permute-done.own.refs_2_.refs_0_), channel_id=1, source_target_pairs={{0,2},{1,3},{2,4},{3,5},{4,6},{5,7},{6,8},{7,9},{8,10},{9,11},{10,... | collective-permute-start | bytes 1572872 | tf_op jit(solution)/shard_map/ppermute | solution.py:27
  16.9 0.7 copy-start
  18.1 10.5 %collective-permute-start.6 = (bf16[2,2,64,1024]{3,2,1,0:T(8,128)(2,1)S(1)}, bf16[2,2,64,1024]{3,2,1,0:T(8,128)(2,1)S(1)}, u32[]{:S(2)}, u32[]{:S(2)}) collective-permute-start(bf16[2,2,64,1024]{3,2,1,0:T(8,128)(2,1)S(1)} %collective-permute-done.3.other.refs_3_.refs_8_), channel_id=1, source_target_pairs={{0,2},{1,3},{2,4},{3,5},{4,6},{5,7},{6,8},{7,9},{8,10},{9,11},{10,... | collective-permute-start | bytes 1572872 | tf_op jit(solution)/shard_map/ppermute | solution.py:27
  20.2 15.9 %collective-permute-start.4 = (bf16[2,128,1024]{2,1,0:T(8,128)(2,1)S(1)}, bf16[2,128,1024]{2,1,0:T(8,128)(2,1)S(1)}, u32[]{:S(2)}, u32[]{:S(2)}) collective-permute-start(bf16[2,128,1024]{2,1,0:T(8,128)(2,1)S(1)} %shard_map.41), channel_id=1, source_target_pairs={{0,33},{1,0},{2,35},{3,2},{4,37},{5,4},{6,39},{7,6},{8,41},{9,8},{... | collective-permute-start | bytes 1572872 | tf_op jit(solution)/shard_map/ppermute | solution.py:27
  23.0 13.9 %collective-permute-start.2 = (bf16[2,2,64,1024]{3,2,1,0:T(8,128)(2,1)S(1)}, bf16[2,2,64,1024]{3,2,1,0:T(8,128)(2,1)S(1)}, u32[]{:S(2)}, u32[]{:S(2)}) collective-permute-start(bf16[2,2,64,1024]{3,2,1,0:T(8,128)(2,1)S(1)} %collective-permute-done.1.refs_1_.refs_2_), channel_id=1, source_target_pairs={{0,2},{1,3},{2,4},{3,5},{4,6},{5,7},{6,8},{7,9},{8,10},{9,11},{10,... | collective-permute-start | bytes 1572872 | tf_op jit(solution)/shard_map/ppermute | solution.py:27
  26.4 13.0 %collective-permute-start.8 = (bf16[2,2,64,1024]{3,2,1,0:T(8,128)(2,1)S(1)}, bf16[2,2,64,1024]{3,2,1,0:T(8,128)(2,1)S(1)}, u32[]{:S(2)}, u32[]{:S(2)}) collective-permute-start(bf16[2,2,64,1024]{3,2,1,0:T(8,128)(2,1)S(1)} %collective-permute-done.1.refs_1_.refs_2_), channel_id=1, source_target_pairs={{0,16},{1,17},{2,18},{3,19},{4,20},{5,21},{6,22},{7,23},{8,24},{9,... | collective-permute-start | bytes 1572872 | tf_op jit(solution)/shard_map/ppermute | solution.py:27
  28.6 12.6 %collective-permute-start.10 = (bf16[2,2,64,1024]{3,2,1,0:T(8,128)(2,1)S(1)}, bf16[2,2,64,1024]{3,2,1,0:T(8,128)(2,1)S(1)}, u32[]{:S(2)}, u32[]{:S(2)}) collective-permute-start(bf16[2,2,64,1024]{3,2,1,0:T(8,128)(2,1)S(1)} %collective-permute-done.6.refs_4_.refs_6_.refs_9_), channel_id=1, source_target_pairs={{0,2},{1,3},{2,4},{3,5},{4,6},{5,7},{6,8},{7,9},{8,10},{9,11},{10,... | collective-permute-start | bytes 1572872 | tf_op jit(solution)/shard_map/ppermute | solution.py:27
  31.7 7.7 %collective-permute-start.7 = (bf16[2,2,64,1024]{3,2,1,0:T(8,128)(2,1)S(1)}, bf16[2,2,64,1024]{3,2,1,0:T(8,128)(2,1)S(1)}, u32[]{:S(2)}, u32[]{:S(2)}) collective-permute-start(bf16[2,2,64,1024]{3,2,1,0:T(8,128)(2,1)S(1)} %collective-permute-done.6.refs_4_.refs_6_.refs_9_), channel_id=1, source_target_pairs={{0,16},{1,17},{2,18},{3,19},{4,20},{5,21},{6,22},{7,23},{8,24},{9,... | collective-permute-start | bytes 1572872 | tf_op jit(solution)/shard_map/ppermute | solution.py:27
  36.9 8.6 %collective-permute-start.5 = (bf16[2,2,64,1024]{3,2,1,0:T(8,128)(2,1)S(1)}, bf16[2,2,64,1024]{3,2,1,0:T(8,128)(2,1)S(1)}, u32[]{:S(2)}, u32[]{:S(2)}) collective-permute-start(bf16[2,2,64,1024]{3,2,1,0:T(8,128)(2,1)S(1)} %collective-permute-done.2.refs_4_.refs_0_.refs_3_), channel_id=1, source_target_pairs={{0,2},{1,3},{2,4},{3,5},{4,6},{5,7},{6,8},{7,9},{8,10},{9,11},{10,... | collective-permute-start | bytes 1572872 | tf_op jit(solution)/shard_map/ppermute | solution.py:27
  40.1 8.1 %collective-permute-start.9 = (bf16[3,2,128,128]{3,2,1,0:T(8,128)(2,1)S(1)}, bf16[3,2,128,128]{3,2,1,0:T(8,128)(2,1)S(1)}, u32[]{:S(2)}, u32[]{:S(2)}) collective-permute-start(bf16[3,2,128,128]{3,2,1,0:T(8,128)(2,1)S(1)} %shard_map.43), channel_id=1, source_target_pairs={{0,33},{1,0},{2,35},{3,2},{4,37},{5,4},{6,39},{7,6},{8,41},{9,8},{... | collective-permute-start | bytes 589832 | tf_op jit(solution)/shard_map/ppermute | solution.py:27
  40.2 10.4 %collective-permute-start.13 = (bf16[2,2,64,1024]{3,2,1,0:T(8,128)(2,1)S(1)}, bf16[2,2,64,1024]{3,2,1,0:T(8,128)(2,1)S(1)}, u32[]{:S(2)}, u32[]{:S(2)}) collective-permute-start(bf16[2,2,64,1024]{3,2,1,0:T(8,128)(2,1)S(1)} %collective-permute-done.2.refs_4_.refs_0_.refs_3_), channel_id=1, source_target_pairs={{0,16},{1,17},{2,18},{3,19},{4,20},{5,21},{6,22},{7,23},{8,24},{9,... | collective-permute-start | bytes 1572872 | tf_op jit(solution)/shard_map/ppermute | solution.py:27
  41.2 9.3 %collective-permute-start.12 = (bf16[2,2,64,1024]{3,2,1,0:T(8,128)(2,1)S(1)}, bf16[2,2,64,1024]{3,2,1,0:T(8,128)(2,1)S(1)}, u32[]{:S(2)}, u32[]{:S(2)}) collective-permute-start(bf16[2,2,64,1024]{3,2,1,0:T(8,128)(2,1)S(1)} %collective-permute-done.10.refs_8_.refs_2_.refs_11_), channel_id=1, source_target_pairs={{0,16},{1,17},{2,18},{3,19},{4,20},{5,21},{6,22},{7,23},{8,24},{9,... | collective-permute-start | bytes 1572872 | tf_op jit(solution)/shard_map/ppermute | solution.py:27
  41.7 11.1 %collective-permute-start.11 = (bf16[2,2,64,1024]{3,2,1,0:T(8,128)(2,1)S(1)}, bf16[2,2,64,1024]{3,2,1,0:T(8,128)(2,1)S(1)}, u32[]{:S(2)}, u32[]{:S(2)}) collective-permute-start(bf16[2,2,64,1024]{3,2,1,0:T(8,128)(2,1)S(1)} %collective-permute-done.10.refs_8_.refs_2_.refs_11_), channel_id=1, source_target_pairs={{0,2},{1,3},{2,4},{3,5},{4,6},{5,7},{6,8},{7,9},{8,10},{9,11},{10,... | collective-permute-start | bytes 1572872 | tf_op jit(solution)/shard_map/ppermute | solution.py:27
  48.2 13.7 %collective-permute-start.16 = (bf16[2,2,64,1024]{3,2,1,0:T(8,128)(2,1)S(1)}, bf16[2,2,64,1024]{3,2,1,0:T(8,128)(2,1)S(1)}, u32[]{:S(2)}, u32[]{:S(2)}) collective-permute-start(bf16[2,2,64,1024]{3,2,1,0:T(8,128)(2,1)S(1)} %collective-permute-done.5.refs_2_.own.refs_5_), channel_id=1, source_target_pairs={{0,2},{1,3},{2,4},{3,5},{4,6},{5,7},{6,8},{7,9},{8,10},{9,11},{10,... | collective-permute-start | bytes 1572872 | tf_op jit(solution)/shard_map/ppermute | solution.py:27
  51.2 10.7 %collective-permute-start.17 = (bf16[2,2,128,128]{3,2,1,0:T(8,128)(2,1)S(1)}, bf16[2,2,128,128]{3,2,1,0:T(8,128)(2,1)S(1)}, u32[]{:S(2)}, u32[]{:S(2)}) collective-permute-start(bf16[2,2,128,128]{3,2,1,0:T(8,128)(2,1)S(1)} %shard_map.46), channel_id=1, source_target_pairs={{0,33},{1,0},{2,35},{3,2},{4,37},{5,4},{6,39},{7,6},{8,41},{9,8},{... | collective-permute-start | bytes 393224 | tf_op jit(solution)/shard_map/ppermute | solution.py:27
  53.4 8.9 %collective-permute-start.19 = (bf16[2,128,128]{2,1,0:T(8,128)(2,1)S(1)}, bf16[2,128,128]{2,1,0:T(8,128)(2,1)S(1)}, u32[]{:S(2)}, u32[]{:S(2)}) collective-permute-start(bf16[2,128,128]{2,1,0:T(8,128)(2,1)S(1)} %get-tuple-element.35), channel_id=1, source_target_pairs={{0,33},{1,0},{2,35},{3,2},{4,37},{5,4},{6,39},{7,6},{8,41},{9,8},{... | collective-permute-start | bytes 196616 | tf_op jit(solution)/shard_map/ppermute | solution.py:27
  54.0 8.7 %collective-permute-start.20 = (bf16[2,128,128]{2,1,0:T(8,128)(2,1)S(1)}, bf16[2,128,128]{2,1,0:T(8,128)(2,1)S(1)}, u32[]{:S(2)}, u32[]{:S(2)}) collective-permute-start(bf16[2,128,128]{2,1,0:T(8,128)(2,1)S(1)} %get-tuple-element.36), channel_id=1, source_target_pairs={{0,48},{1,49},{2,50},{3,51},{4,52},{5,53},{6,54},{7,55},{8,56},{9,... | collective-permute-start | bytes 196616 | tf_op jit(solution)/shard_map/ppermute | solution.py:27
  58.3 7.6 %collective-permute-start.21 = (bf16[2,128,128]{2,1,0:T(8,128)(2,1)S(1)}, bf16[2,128,128]{2,1,0:T(8,128)(2,1)S(1)}, u32[]{:S(2)}, u32[]{:S(2)}) collective-permute-start(bf16[2,128,128]{2,1,0:T(8,128)(2,1)S(1)} %get-tuple-element.37), channel_id=1, source_target_pairs={{0,35},{1,2},{2,37},{3,4},{4,39},{5,6},{6,41},{7,8},{8,43},{9,10},... | collective-permute-start | bytes 196616 | tf_op jit(solution)/shard_map/ppermute | solution.py:27
  61.9 4.5 %collective-permute-start.15 = (bf16[2,2,64,1024]{3,2,1,0:T(8,128)(2,1)S(1)}, bf16[2,2,64,1024]{3,2,1,0:T(8,128)(2,1)S(1)}, u32[]{:S(2)}, u32[]{:S(2)}) collective-permute-start(bf16[2,2,64,1024]{3,2,1,0:T(8,128)(2,1)S(1)} %collective-permute-done.5.refs_2_.own.refs_5_), channel_id=1, source_target_pairs={{0,16},{1,17},{2,18},{3,19},{4,20},{5,21},{6,22},{7,23},{8,24},{9,... | collective-permute-start | bytes 1572872 | tf_op jit(solution)/shard_map/ppermute | solution.py:27
  61.9 4.5 %collective-permute-start.14 = (bf16[2,2,64,1024]{3,2,1,0:T(8,128)(2,1)S(1)}, bf16[2,2,64,1024]{3,2,1,0:T(8,128)(2,1)S(1)}, u32[]{:S(2)}, u32[]{:S(2)}) collective-permute-start(bf16[2,2,64,1024]{3,2,1,0:T(8,128)(2,1)S(1)} %collective-permute-done.11.refs_4_.other.refs_13_), channel_id=1, source_target_pairs={{0,16},{1,17},{2,18},{3,19},{4,20},{5,21},{6,22},{7,23},{8,24},{9,... | collective-permute-start | bytes 1572872 | tf_op jit(solution)/shard_map/ppermute | solution.py:27
  62.4 5.1 %collective-permute-start.18 = (bf16[2,2,64,1024]{3,2,1,0:T(8,128)(2,1)S(1)}, bf16[2,2,64,1024]{3,2,1,0:T(8,128)(2,1)S(1)}, u32[]{:S(2)}, u32[]{:S(2)}) collective-permute-start(bf16[2,2,64,1024]{3,2,1,0:T(8,128)(2,1)S(1)} %collective-permute-done.16.refs_7_), channel_id=1, source_target_pairs={{0,16},{1,17},{2,18},{3,19},{4,20},{5,21},{6,22},{7,23},{8,24},{9,... | collective-permute-start | bytes 1572872 | tf_op jit(solution)/shard_map/ppermute | solution.py:27
  69.8 9.3 %collective-permute-start.24 = (bf16[2,64,1024]{2,1,0:T(8,128)(2,1)S(1)}, bf16[2,64,1024]{2,1,0:T(8,128)(2,1)S(1)}, u32[]{:S(2)}, u32[]{:S(2)}) collective-permute-start(bf16[2,64,1024]{2,1,0:T(8,128)(2,1)S(1)} %get-tuple-element.42), channel_id=1, source_target_pairs={{0,128},{1,112},{2,130},{3,114},{4,132},{5,116},{6,134},{7,118},{8... | collective-permute-start | bytes 786440 | tf_op jit(solution)/shard_map/ppermute | solution.py:27
  71.8 4.0 %collective-permute-start.23 = (f32[1,128]{1,0:T(1,128)S(1)}, f32[1,128]{1,0:T(1,128)S(1)}, u32[]{:S(2)}, u32[]{:S(2)}) collective-permute-start(f32[1,128]{1,0:T(1,128)S(1)} %shard_map.50), channel_id=1, source_target_pairs={{0,2},{1,3},{2,4},{3,5},{4,6},{5,7},{6,8},{7,9},{8,10},{9,11},{10,... | collective-permute-start | bytes 1544 | tf_op jit(solution)/shard_map/ppermute | solution.py:27
  71.9 4.0 %collective-permute-start.22 = (f32[1,128]{1,0:T(1,128)S(1)}, f32[1,128]{1,0:T(1,128)S(1)}, u32[]{:S(2)}, u32[]{:S(2)}) collective-permute-start(f32[1,128]{1,0:T(1,128)S(1)} %shard_map.50), channel_id=1, source_target_pairs={{0,14},{1,15},{2,0},{3,1},{4,2},{5,3},{6,4},{7,5},{8,6},{9,7},{10,... | collective-permute-start | bytes 1544 | tf_op jit(solution)/shard_map/ppermute | solution.py:27
  74.7 14.5 %collective-permute-start.27 = (bf16[2,64,1024]{2,1,0:T(8,128)(2,1)S(1)}, bf16[2,64,1024]{2,1,0:T(8,128)(2,1)S(1)}, u32[]{:S(2)}, u32[]{:S(2)}) collective-permute-start(bf16[2,64,1024]{2,1,0:T(8,128)(2,1)S(1)} %get-tuple-element.46), channel_id=1, source_target_pairs={{0,129},{1,113},{2,131},{3,115},{4,133},{5,117},{6,135},{7,119},{8... | collective-permute-start | bytes 786440 | tf_op jit(solution)/shard_map/ppermute | solution.py:27
  79.1 6.6 %collective-permute-start.25 = (f32[1,128]{1,0:T(1,128)S(1)}, f32[1,128]{1,0:T(1,128)S(1)}, u32[]{:S(2)}, u32[]{:S(2)}) collective-permute-start(f32[1,128]{1,0:T(1,128)S(1)} %get-tuple-element.43), channel_id=1, source_target_pairs={{0,6},{1,7},{2,8},{3,9},{4,10},{5,11},{6,12},{7,13},{8,14},{9,15},... | collective-permute-start | bytes 1544 | tf_op jit(solution)/shard_map/ppermute | solution.py:27
  85.0 4.2 %collective-permute-start.26 = (f32[1,128]{1,0:T(1,128)S(1)}, f32[1,128]{1,0:T(1,128)S(1)}, u32[]{:S(2)}, u32[]{:S(2)}) collective-permute-start(f32[1,128]{1,0:T(1,128)S(1)} %get-tuple-element.44), channel_id=1, source_target_pairs={{0,10},{1,11},{2,12},{3,13},{4,14},{5,15},{6,0},{7,1},{8,2},{9,3},... | collective-permute-start | bytes 1544 | tf_op jit(solution)/shard_map/ppermute | solution.py:27
  89.2 4.5 %collective-permute-start.29 = (f32[1,128]{1,0:T(1,128)S(1)}, f32[1,128]{1,0:T(1,128)S(1)}, u32[]{:S(2)}, u32[]{:S(2)}) collective-permute-start(f32[1,128]{1,0:T(1,128)S(1)} %add_add_fusion), channel_id=1, source_target_pairs={{0,129},{1,113},{2,131},{3,115},{4,133},{5,117},{6,135},{7,119},{8... | collective-permute-start | bytes 1544 | tf_op jit(solution)/shard_map/ppermute | solution.py:27
  89.2 4.5 %collective-permute-start.28 = (f32[1,128]{1,0:T(1,128)S(1)}, f32[1,128]{1,0:T(1,128)S(1)}, u32[]{:S(2)}, u32[]{:S(2)}) collective-permute-start(f32[1,128]{1,0:T(1,128)S(1)} %add_add_fusion), channel_id=1, source_target_pairs={{0,128},{1,112},{2,130},{3,114},{4,132},{5,116},{6,134},{7,118},{8... | collective-permute-start | bytes 1544 | tf_op jit(solution)/shard_map/ppermute | solution.py:27

commit v12 on v9

--- a/solution.py
+++ b/solution.py
@@ -39,9 +39,13 @@
     return (m, 1 - c, z, h)
 
 
-def to_hub(m, c, z, h):
-    column, half = hub_of(2 * m + c)
-    return (column, h, z, half)
+def to_hub(step, turn=0):
+    def route(m, c, z, h):
+        column, half = hub_of(2 * m + c)
+        core = h ^ turn
+        return (column, core, z + (step if core == 0 else -step), half)
+
+    return route
 
 
 def hub_ahead(step):
@@ -61,6 +65,8 @@
 
 
 WEIGHT = 3_000_000_000
+WEIGHT0 = 1
+ROOM = 1_000_000_000
 
 VMEM = pl.BlockSpec(memory_space=pltpu.VMEM)
 SMEM = pl.BlockSpec(memory_space=pltpu.SMEM)
@@ -147,16 +153,22 @@
     block = jnp.concatenate([whole(info, own[7], other[7], info[3], part) for part in range(2)], axis=0)
     product = acc[...] + jnp.dot(left_side(info, a_ref, 4), block, preferred_element_type=F32)
     rounded = product.astype(BF16)
+    rounded_ref[0] = rounded
+    rounded_ref[1, 0:128], rounded_ref[1, 128:256] = -rounded[128:256], rounded[0:128]
     for part in range(2):
-        rounded_ref[part] = rounded[part * 128 : part * 128 + 128]
         low, high = rounded[part * 128 : part * 128 + 64], rounded[part * 128 + 64 : part * 128 + 128]
         keep[part], send[part] = halves(info, low, high)
-    total = None
-    for offset, one, two in zip(OFFSETS, own, other):
-        block = jnp.concatenate([whole(info, one, two, info[4], part) for part in range(2)], axis=0)
-        term = jnp.dot(left_side(info, rounded_ref, offset), block, preferred_element_type=F32)
-        total = term if total is None else total + term
-    out[...] = total
+    for tile in range(4):
+        columns = pl.ds(tile * 256, 256)
+        total = None
+        for offset, one, two in zip(OFFSETS, own, other):
+            parts = [halves(info, one[info[4], part, :, columns], two[info[4], part, :, columns]) for part in range(2)]
+            block = jnp.concatenate([parts[0][0], parts[0][1], parts[1][0], parts[1][1]], axis=0)
+            place = columns_of(info, offset)
+            left = jnp.concatenate([rounded_ref[0, :, place], rounded_ref[1, :, place]], axis=1)
+            term = jnp.dot(left, block, preferred_element_type=F32)
+            total = term if total is None else total + term
+        out[:, columns] = total
 
 
 def trace_kernel(info, product, near, middle, late, trace):
@@ -171,8 +183,25 @@
         im = more_im if im is None else im + more_im
     re = jnp.sum(jnp.sum(re, axis=0, keepdims=True), axis=1, keepdims=True)
     im = jnp.sum(jnp.sum(im, axis=0, keepdims=True), axis=1, keepdims=True)
+    re, im = re * (1.0 / 1024), im * (1.0 / 1024)
     lane = lax.broadcasted_iota(jnp.int32, (1, 128), 1)
     trace[...] = jnp.where(lane == 2 * info[0], re, jnp.where(lane == 2 * info[0] + 1, im, 0.0))
+
+
+def hold_kernel(info, block, out):
+    pass
+
+
+def hold(info, block, flops):
+    anywhere = pl.BlockSpec(memory_space=pl.ANY)
+    return pl.pallas_call(
+        hold_kernel,
+        out_shape=jax.ShapeDtypeStruct(block.shape, block.dtype),
+        in_specs=[SMEM, anywhere],
+        out_specs=anywhere,
+        input_output_aliases={1: 0},
+        cost_estimate=pl.CostEstimate(flops=flops, bytes_accessed=1 << 10, transcendentals=0),
+    )(info, block)
 
 
 def shards(fields, mom_table):
@@ -184,41 +213,33 @@
     wall = lax.optimization_barrier
     block_of_products = jax.ShapeDtypeStruct((256, 1024), F32)
 
-    own = moved(rows, to_hub)
-
-    ownx, p1 = moved(own, other_core), moved(own, onward)
-    q1 = moved(ownx, onward)
+    p1, q1, rows = wall((moved(rows, to_hub(1)), moved(rows, to_hub(1, 1)), rows))
+
+    p2, p1x = moved(p1, onward), moved(p1, other_core)
+    q2, q1x = moved(q1, onward), moved(q1, other_core)
+    own = moved(rows, to_hub(0))
+    ownx = moved(own, other_core)
     a = call(first_cut_kernel, info, [own, ownx], jax.ShapeDtypeStruct((2, 128, 1024), BF16), 1)
     a = moved(a, hub_ahead(0))
-
-    p2, p1x = moved(p1, onward), moved(p1, other_core)
-    q2, q1x = moved(q1, onward), moved(q1, other_core)
     three, three_x = [own, p1, q1x], [ownx, q1, p1x]
-    near = call(cut_kernel, info, three + three_x, slices_of(3), 1)
-    acc = call(lambda *refs: products_kernel(OFFSETS[:1], *refs), info, [a, own, ownx], block_of_products, WEIGHT)
-    p2, a, acc = wall((p2, a, acc))
-
-    near = moved(near, hub_ahead(0))
+    near = moved(call(cut_kernel, info, three + three_x, slices_of(3), 1), hub_ahead(0))
     p3, p2x = moved(p2, onward), moved(p2, other_core)
     q3, q2x = moved(q2, onward), moved(q2, other_core)
-    p3, near = wall((p3, near))
 
     p4, p3x = moved(p3, onward), moved(p3, other_core)
+    q3x = moved(q3, other_core)
     five, five_x = three + [p2, q2x], three_x + [q2, p2x]
+    two, two_x = [p3, q3x], [q3, p3x]
     middle = moved(call(cut_kernel, info, five[3:] + five_x[3:], slices_of(2), 1), hub_ahead(0))
     acc = call(
-        lambda *refs: products_kernel(OFFSETS[1:5], *refs), info, [a] + five[1:] + five_x[1:] + [acc], block_of_products, 1
-    )
-    q3, acc = wall((q3, acc))
-
-    q3x = moved(q3, other_core)
-    p4, middle = wall((p4, middle))
-
-    p4x = moved(p4, other_core)
-    two, two_x = [p3, q3x], [q3, p3x]
+        lambda *refs: products_kernel(OFFSETS[:5], *refs), info, [a] + five + five_x, block_of_products, WEIGHT0
+    )
     acc = call(
         lambda *refs: products_kernel(OFFSETS[5:7], *refs), info, [a] + two + two_x + [acc], block_of_products, 1
     )
+    p4, near, middle, acc = wall((hold(info, p4, ROOM), near, middle, acc))
+
+    p4x = moved(p4, other_core)
     late = moved(call(cut_kernel, info, two + [p4] + two_x + [p4x], slices_of(3), 1), hub_ahead(0))
     half_block = jax.ShapeDtypeStruct((2, 64, 1024), BF16)
     keep, send, product = call(
@@ -227,7 +248,7 @@
         [a, acc] + five + two + [p4] + five_x + two_x + [p4x],
         (half_block, half_block, block_of_products),
         WEIGHT,
-        [pltpu.VMEM((2, 128, 1024), BF16)],
+        [pltpu.VMEM((2, 256, 1024), BF16)],
     )
     share = jax.ShapeDtypeStruct((1, 128), F32)
     trace = call(trace_kernel, info, [product, near, middle, late], share, 1)
@@ -240,7 +261,7 @@
     first, second = moved(trace, from_hub(0)), moved(trace, from_hub(1))
     products = jnp.where(half == 0, jnp.stack([kept, sent]), jnp.stack([sent, kept]))[:, None, None]
     both = jnp.where(half == 0, jnp.concatenate([first, second]), jnp.concatenate([second, first]))
-    correlator = jnp.sum(both[:, :16].reshape(2, 8, 2), axis=1)[:, None, None, :] / F32(1024)
+    correlator = jnp.sum(both[:, :16].reshape(2, 8, 2), axis=1)[:, None, None, :]
     return products, correlator
 
 

time: 95 us -> 106 us (1.12); the launches traced: 94.9 us -> 104 us
  starting transfers between devices: 53.8 us -> 42.6 us
  waiting for transfers between devices: 29.9 us -> 37.7 us
  local copies, waits for them, and re-layouts: 0.09 us -> 6.84 us
  Pallas kernels: 8.83 us -> 13.9 us
    ppermute x28, starting transfers between devices: 53.8 us -> 42.6 us  [moved(): lax.ppermute(block, BOTH, [(index_of(*at), index_of(*route(*at))) for at...]
    ppermute x28, waiting for transfers between devices: 29.9 us -> 37.7 us  [moved(): lax.ppermute(block, BOTH, [(index_of(*at), index_of(*route(*at))) for at...]
    unnamed x2 -> x46, local copies, waits for them, and re-layouts: 0.01 us -> 6.76 us
    pallas_call x9 -> x8, Pallas kernels: 8.83 us -> 13.1 us  [call(): pl.pallas_call(kernel, out_shape=out_shape, in_specs=[SMEM] + [VMEM] * le...]
  transfers between devices with their start and end apart: 28 -> 28, of which waited for: 12 -> 13; matrix products, arithmetic and copies ran while one was open for 1% -> 1% of each run, Pallas kernels for 9% -> 12%
where the time goes in v12:
time: 106 us; the launch traced here: 104 us
  starting transfers between devices  42.6 us (40%)
  waiting for transfers between devices  37.7 us (36%)
  Pallas kernels  13.9 us (13%)
  local copies, waits for them, and re-layouts  6.84 us (6%)
  other arithmetic  1.55 us (1%)
    ppermute x28, starting transfers between devices, moved(): lax.ppermute(block, BOTH, [(index_of(*at), index_of(*route(*at))) for at...  42.6 us
    ppermute x28, waiting for transfers between devices, moved(): lax.ppermute(block, BOTH, [(index_of(*at), index_of(*route(*at))) for at...  37.7 us
    pallas_call x8, Pallas kernels, call(): pl.pallas_call(kernel, out_shape=out_shape, in_specs=[SMEM] + [VMEM] * le...  13.1 us
    unnamed x46, local copies, waits for them, and re-layouts  6.76 us
  transfers between devices with their start and end apart: 28, of which 13 were waited for; matrix products, arithmetic and copies ran while one was open for 1% of the time, Pallas kernels for 12%

profile of v12, /device:TPU:1, one launch (start us, length us, event | category | flops | bytes accessed | tf_op | source)
XLA Modules:
  0.0 103.6 jit_solution(5097090034897807534)
XLA Ops:
  0.6 0.0 copy-start
  0.6 8.9 %collective-permute-start.1 = (bf16[2,2,64,1024]{3,2,1,0:T(8,128)(2,1)}, bf16[2,2,64,1024]{3,2,1,0:T(8,128)(2,1)S(1)}, u32[]{:S(2)}, u32[]{:S(2)}) collective-permute-start(bf16[2,2,64,1024]{3,2,1,0:T(8,128)(2,1)} %bitcast.15), channel_id=1, source_target_pairs={{0,158},{1,130},{2,144},{3,132},{4,146},{5,134},{6,148},{7,136},{8... | collective-permute-start | bytes 1572872 | tf_op jit(solution)/shard_map/ppermute | solution.py:27
  9.6 11.2 %collective-permute-done.1.refs_4_.refs_8_.refs_9_ = bf16[2,2,64,1024]{3,2,1,0:T(8,128)(2,1)S(1)} collective-permute-done((bf16[2,2,64,1024]{3,2,1,0:T(8,128)(2,1)}, bf16[2,2,64,1024]{3,2,1,0:T(8,128)(2,1)S(1)}, u32[]{:S(2)}, u32[]{:S(2)}) %collective-permute-start.1) | collective-permute-done | bytes 524320 | tf_op jit(solution)/shard_map/ppermute | solution.py:27
  20.8 2.6 %collective-permute-done.refs_1_.refs_3_ = bf16[2,2,64,1024]{3,2,1,0:T(8,128)(2,1)S(1)} collective-permute-done((bf16[2,2,64,1024]{3,2,1,0:T(8,128)(2,1)}, bf16[2,2,64,1024]{3,2,1,0:T(8,128)(2,1)S(1)}, u32[]{:S(2)}, u32[]{:S(2)}) %collective-permute-start) | collective-permute-done | bytes 524320 | tf_op jit(solution)/shard_map/ppermute | solution.py:27
  23.4 3.6 %collective-permute-start.5 = (bf16[2,2,64,1024]{3,2,1,0:T(8,128)(2,1)S(1)}, bf16[2,2,64,1024]{3,2,1,0:T(8,128)(2,1)}, u32[]{:S(2)}, u32[]{:S(2)}) collective-permute-start(bf16[2,2,64,1024]{3,2,1,0:T(8,128)(2,1)S(1)} %collective-permute-done.refs_1_.refs_3_), channel_id=1, source_target_pairs={{0,2},{1,3},{2,4},{3,5},{4,6},{5,7},{6,8},{7,9},{8,10},{9,11},{10,... | collective-permute-start | bytes 1572872 | tf_op jit(solution)/shard_map/ppermute | solution.py:27
  27.0 1.3 %collective-permute-start.11 = (bf16[2,2,64,1024]{3,2,1,0:T(8,128)(2,1)S(1)}, bf16[2,2,64,1024]{3,2,1,0:T(8,128)(2,1)}, u32[]{:S(2)}, u32[]{:S(2)}) collective-permute-start(bf16[2,2,64,1024]{3,2,1,0:T(8,128)(2,1)S(1)} %collective-permute-done.1.refs_4_.refs_8_.refs_9_), channel_id=1, source_target_pairs={{0,2},{1,3},{2,4},{3,5},{4,6},{5,7},{6,8},{7,9},{8,10},{9,11},{10,... | collective-permute-start | bytes 1572872 | tf_op jit(solution)/shard_map/ppermute | solution.py:27
  28.3 0.8 copy-done.9
  29.1 4.2 %collective-permute-done.2.own.refs_0_.refs_2_ = bf16[2,2,64,1024]{3,2,1,0:T(8,128)(2,1)S(1)} collective-permute-done((bf16[2,2,64,1024]{3,2,1,0:T(8,128)(2,1)}, bf16[2,2,64,1024]{3,2,1,0:T(8,128)(2,1)S(1)}, u32[]{:S(2)}, u32[]{:S(2)}) %collective-permute-start.2) | collective-permute-done | bytes 524320 | tf_op jit(solution)/shard_map/ppermute | solution.py:27
  33.3 0.5 collective-permute-start.8
  33.8 0.0 collective-permute-done.5.refs_0_.refs_5_.refs_3_
  33.8 2.6 %collective-permute-start.6 = (bf16[2,2,64,1024]{3,2,1,0:T(8,128)(2,1)}, bf16[2,2,64,1024]{3,2,1,0:T(8,128)(2,1)S(1)}, u32[]{:S(2)}, u32[]{:S(2)}) collective-permute-start(bf16[2,2,64,1024]{3,2,1,0:T(8,128)(2,1)} %collective-permute-done.5.refs_0_.refs_5_.refs_3_), channel_id=1, source_target_pairs={{0,2},{1,3},{2,4},{3,5},{4,6},{5,7},{6,8},{7,9},{8,10},{9,11},{10,... | collective-permute-start | bytes 1572872 | tf_op jit(solution)/shard_map/ppermute | solution.py:27
  36.3 2.4 %collective-permute-done.11.refs_2_.refs_10_.refs_11_ = bf16[2,2,64,1024]{3,2,1,0:T(8,128)(2,1)} collective-permute-done((bf16[2,2,64,1024]{3,2,1,0:T(8,128)(2,1)S(1)}, bf16[2,2,64,1024]{3,2,1,0:T(8,128)(2,1)}, u32[]{:S(2)}, u32[]{:S(2)}) %collective-permute-start.11) | collective-permute-done | bytes 524320 | tf_op jit(solution)/shard_map/ppermute | solution.py:27
  38.7 3.2 %collective-permute-start.15 = (bf16[2,2,64,1024]{3,2,1,0:T(8,128)(2,1)}, bf16[2,2,64,1024]{3,2,1,0:T(8,128)(2,1)S(1)}, u32[]{:S(2)}, u32[]{:S(2)}) collective-permute-start(bf16[2,2,64,1024]{3,2,1,0:T(8,128)(2,1)} %collective-permute-done.11.refs_2_.refs_10_.refs_11_), channel_id=1, source_target_pairs={{0,2},{1,3},{2,4},{3,5},{4,6},{5,7},{6,8},{7,9},{8,10},{9,11},{10,... | collective-permute-start | bytes 1572872 | tf_op jit(solution)/shard_map/ppermute | solution.py:27
  42.0 0.0 collective-permute-done.9.refs_5_.refs_9_.refs_10_
  42.0 0.8 copy-done.12
  42.8 0.6 collective-permute-start.12
  43.4 0.1 pad_add_fusion.info.refs_0_
  43.4 0.6 shard_map.41
  44.0 0.0 collective-permute-done.8.refs_2_.refs_4_
  44.1 0.8 copy-done.15
  44.9 1.2 %collective-permute-start.4 = (bf16[2,128,1024]{2,1,0:T(8,128)(2,1)S(1)}, bf16[2,128,1024]{2,1,0:T(8,128)(2,1)S(1)}, u32[]{:S(2)}, u32[]{:S(2)}) collective-permute-start(bf16[2,128,1024]{2,1,0:T(8,128)(2,1)S(1)} %shard_map.41), channel_id=1, source_target_pairs={{0,33},{1,0},{2,35},{3,2},{4,37},{5,4},{6,39},{7,6},{8,41},{9,8},{... | collective-permute-start | bytes 1572872 | tf_op jit(solution)/shard_map/ppermute | solution.py:27
  46.1 0.8 collective-permute-start.17
  46.8 3.2 %collective-permute-done.15.refs_4_.refs_13_.refs_3_ = bf16[2,2,64,1024]{3,2,1,0:T(8,128)(2,1)S(1)} collective-permute-done((bf16[2,2,64,1024]{3,2,1,0:T(8,128)(2,1)}, bf16[2,2,64,1024]{3,2,1,0:T(8,128)(2,1)S(1)}, u32[]{:S(2)}, u32[]{:S(2)}) %collective-permute-start.15) | collective-permute-done | bytes 524320 | tf_op jit(solution)/shard_map/ppermute | solution.py:27
  50.1 2.1 %collective-permute-start.16 = (bf16[2,2,64,1024]{3,2,1,0:T(8,128)(2,1)S(1)}, bf16[2,2,64,1024]{3,2,1,0:T(8,128)(2,1)S(1)}, u32[]{:S(2)}, u32[]{:S(2)}) collective-permute-start(bf16[2,2,64,1024]{3,2,1,0:T(8,128)(2,1)S(1)} %collective-permute-done.15.refs_4_.refs_13_.refs_3_), channel_id=1, source_target_pairs={{0,16},{1,17},{2,18},{3,19},{4,20},{5,21},{6,22},{7,23},{8,24},{9,... | collective-permute-start | bytes 1572872 | tf_op jit(solution)/shard_map/ppermute | solution.py:27
  52.2 0.0 collective-permute-done.13.refs_3_.refs_11_.refs_12_
  52.2 1.2 %collective-permute-start.7 = (bf16[2,2,64,1024]{3,2,1,0:T(8,128)(2,1)S(1)}, bf16[2,2,64,1024]{3,2,1,0:T(8,128)(2,1)}, u32[]{:S(2)}, u32[]{:S(2)}) collective-permute-start(bf16[2,2,64,1024]{3,2,1,0:T(8,128)(2,1)S(1)} %collective-permute-done.6.refs_2_.refs_5_.refs_0_), channel_id=1, source_target_pairs={{0,2},{1,3},{2,4},{3,5},{4,6},{5,7},{6,8},{7,9},{8,10},{9,11},{10,... | collective-permute-start | bytes 1572872 | tf_op jit(solution)/shard_map/ppermute | solution.py:27
  53.4 1.0 %copy-done.6 = bf16[2,2,64,1024]{3,2,1,0:T(8,128)(2,1)S(1)} copy-done((bf16[2,2,64,1024]{3,2,1,0:T(8,128)(2,1)S(1)}, bf16[2,2,64,1024]{3,2,1,0:T(8,128)(2,1)}, u32[]{:S(2)}) %copy-start.6) | copy-done | bytes 524312
  54.4 1.0 %copy-done.16 = bf16[2,2,64,1024]{3,2,1,0:T(8,128)(2,1)S(1)} copy-done((bf16[2,2,64,1024]{3,2,1,0:T(8,128)(2,1)S(1)}, bf16[2,2,64,1024]{3,2,1,0:T(8,128)(2,1)}, u32[]{:S(2)}) %copy-start.16) | copy-done | bytes 524312
  55.5 0.7 shard_map.43
  56.2 0.0 collective-permute-done.12.refs_1_.refs_6_.refs_4_
  56.2 1.3 %collective-permute-start.10 = (bf16[3,2,128,128]{3,2,1,0:T(8,128)(2,1)S(1)}, bf16[3,2,128,128]{3,2,1,0:T(8,128)(2,1)S(1)}, u32[]{:S(2)}, u32[]{:S(2)}) collective-permute-start(bf16[3,2,128,128]{3,2,1,0:T(8,128)(2,1)S(1)} %shard_map.43), channel_id=1, source_target_pairs={{0,33},{1,0},{2,35},{3,2},{4,37},{5,4},{6,39},{7,6},{8,41},{9,8},{... | collective-permute-start | bytes 589832 | tf_op jit(solution)/shard_map/ppermute | solution.py:27
  57.5 2.1 %shard_map.44 = bf16[2,2,128,128]{3,2,1,0:T(8,128)(2,1)} custom-call(s32[6]{0:T(128)S(1)} %pad_add_fusion.info.refs_0_, bf16[2,2,64,1024]{3,2,1,0:T(8,128)(2,1)} %collective-permute-done.5.refs_0_.refs_5_.refs_3_, bf16[2,2,64,1024]{3,2,1,0:T(8,128)(2,1)S(1)} %collective-permute-done.12.refs_1_.refs_6_.refs_4_, ...), custom_call_target="tpu_custom_call" | custom-call | flops 1 | bytes 1048576 | tf_op jit(solution)/shard_map/pallas_call | solution.py:81
  59.6 3.0 %collective-permute-done.4.refs_1_.a_ref = bf16[2,128,1024]{2,1,0:T(8,128)(2,1)S(1)} collective-permute-done((bf16[2,128,1024]{2,1,0:T(8,128)(2,1)S(1)}, bf16[2,128,1024]{2,1,0:T(8,128)(2,1)S(1)}, u32[]{:S(2)}, u32[]{:S(2)}) %collective-permute-start.4) | collective-permute-done | bytes 524320 | tf_op jit(solution)/shard_map/ppermute | solution.py:27
  62.6 0.0 collective-permute-start.14
  62.6 2.4 %shard_map.45.refs_6_ = f32[256,1024]{1,0:T(8,128)S(1)} custom-call(s32[6]{0:T(128)S(1)} %pad_add_fusion.info.refs_0_, bf16[2,128,1024]{2,1,0:T(8,128)(2,1)S(1)} %collective-permute-done.4.refs_1_.a_ref, bf16[2,2,64,1024]{3,2,1,0:T(8,128)(2,1)S(1)} %collective-permute-done.2.own.refs_0_.refs_2_, bf16[2,2,64,1024]{3,2,1,0:T(8,128)(2,1)S(1)} %copy-done.10, ...), custom_call_target="tpu_custom_call" | custom-call | flops 1 | bytes 1048576 | tf_op jit(solution)/shard_map/pallas_call | solution.py:81
  65.1 0.0 collective-permute-done.17.refs_5_.refs_14_.refs_4_
  65.1 1.0 shard_map.46.acc
  66.1 1.0 copy-done.19
  67.1 0.8 shard_map.42.refs_7_.refs_2_
  67.9 0.0 copy-start.4
  68.0 2.1 %collective-permute-done.14.middle = bf16[2,2,128,128]{3,2,1,0:T(8,128)(2,1)} collective-permute-done((bf16[2,2,128,128]{3,2,1,0:T(8,128)(2,1)}, bf16[2,2,128,128]{3,2,1,0:T(8,128)(2,1)}, u32[]{:S(2)}, u32[]{:S(2)}) %collective-permute-start.14) | collective-permute-done | bytes 131104 | tf_op jit(solution)/shard_map/ppermute | solution.py:27
  70.1 0.0 collective-permute-start.18
  70.1 2.1 %collective-permute-done.18.refs_15_.refs_5_ = bf16[2,2,64,1024]{3,2,1,0:T(8,128)(2,1)S(1)} collective-permute-done((bf16[2,2,64,1024]{3,2,1,0:T(8,128)(2,1)}, bf16[2,2,64,1024]{3,2,1,0:T(8,128)(2,1)S(1)}, u32[]{:S(2)}, u32[]{:S(2)}) %collective-permute-start.18) | collective-permute-done | bytes 524320 | tf_op jit(solution)/shard_map/ppermute | solution.py:27
  72.2 1.2 %shard_map.48 = bf16[3,2,128,128]{3,2,1,0:T(8,128)(2,1)S(1)} custom-call(s32[6]{0:T(128)S(1)} %copy-done.22, bf16[2,2,64,1024]{3,2,1,0:T(8,128)(2,1)S(1)} %collective-permute-done.6.refs_2_.refs_5_.refs_0_, bf16[2,2,64,1024]{3,2,1,0:T(8,128)(2,1)S(1)} %collective-permute-done.16.refs_3_.refs_6_.refs_1_, bf16[2,2,64,1024]{3,2,1,0:T(8,128)(2,1)} %shard_map.42.refs_7_.refs_2_, ...), custom_call_target="tpu_custom_call" | custom-call | flops 1 | bytes 1048576 | tf_op jit(solution)/shard_map/pallas_call | solution.py:81
  73.4 0.1 collective-permute-start.19
  73.5 1.2 %copy-done.20 = f32[256,1024]{1,0:T(8,128)S(1)} copy-done((f32[256,1024]{1,0:T(8,128)S(1)}, f32[256,1024]{1,0:T(8,128)}, u32[]{:S(2)}) %copy-start.20) | copy-done | bytes 1048600
  74.8 3.8 %shard_map.47 = (bf16[2,64,1024]{2,1,0:T(8,128)(2,1)S(1)}, bf16[2,64,1024]{2,1,0:T(8,128)(2,1)}, f32[256,1024]{1,0:T(8,128)S(1)}) custom-call(s32[6]{0:T(128)S(1)} %copy-done.22, bf16[2,128,1024]{2,1,0:T(8,128)(2,1)S(1)} %copy-done.4, f32[256,1024]{1,0:T(8,128)S(1)} %copy-done.20, bf16[2,2,64,1024]{3,2,1,0:T(8,128)(2,1)S(1)} %collective-permute-done.2.own.refs_0_.refs_2_, ...), custom_call_target="tpu_custom_call" | custom-call | flops 3000000000 | bytes 1048576 | tf_op jit(solution)/shard_map/pallas_call | solution.py:81
  78.6 1.5 %collective-permute-start.22 = (bf16[2,64,1024]{2,1,0:T(8,128)(2,1)S(1)}, bf16[2,64,1024]{2,1,0:T(8,128)(2,1)S(1)}, u32[]{:S(2)}, u32[]{:S(2)}) collective-permute-start(bf16[2,64,1024]{2,1,0:T(8,128)(2,1)S(1)} %get-tuple-element.26), channel_id=1, source_target_pairs={{0,128},{1,112},{2,130},{3,114},{4,132},{5,116},{6,134},{7,118},{8... | collective-permute-start | bytes 786440 | tf_op jit(solution)/shard_map/ppermute | solution.py:27
  80.1 2.1 %collective-permute-done.19.late = bf16[3,2,128,128]{3,2,1,0:T(8,128)(2,1)S(1)} collective-permute-done((bf16[3,2,128,128]{3,2,1,0:T(8,128)(2,1)S(1)}, bf16[3,2,128,128]{3,2,1,0:T(8,128)(2,1)S(1)}, u32[]{:S(2)}, u32[]{:S(2)}) %collective-permute-start.19) | collective-permute-done | bytes 196640 | tf_op jit(solution)/shard_map/ppermute | solution.py:27
  82.2 1.3 %shard_map.49 = f32[1,128]{1,0:T(1,128)S(1)} custom-call(s32[6]{0:T(128)S(1)} %copy-done.22, f32[256,1024]{1,0:T(8,128)S(1)} %get-tuple-element.23.product, bf16[3,2,128,128]{3,2,1,0:T(8,128)(2,1)S(1)} %collective-permute-done.10.near, bf16[2,2,128,128]{3,2,1,0:T(8,128)(2,1)} %collective-permute-done.14.middle, ...), custom_call_target="tpu_custom_call" | custom-call | flops 1 | bytes 1048576 | tf_op jit(solution)/shard_map/pallas_call | solution.py:81
  83.5 0.0 collective-permute-start.21
  83.6 2.7 %collective-permute-start.20 = (f32[1,128]{1,0:T(1,128)S(1)}, f32[1,128]{1,0:T(1,128)S(1)}, u32[]{:S(2)}, u32[]{:S(2)}) collective-permute-start(f32[1,128]{1,0:T(1,128)S(1)} %shard_map.49), channel_id=1, source_target_pairs={{0,14},{1,15},{2,0},{3,1},{4,2},{5,3},{6,4},{7,5},{8,6},{9,7},{10,... | collective-permute-start | bytes 1544 | tf_op jit(solution)/shard_map/ppermute | solution.py:27
  86.2 0.4 collective-permute-start.25
  86.6 0.5 collective-permute-done.21
  87.2 0.1 collective-permute-done.22
  87.2 4.5 %collective-permute-start.23 = (f32[1,128]{1,0:T(1,128)S(1)}, f32[1,128]{1,0:T(1,128)S(1)}, u32[]{:S(2)}, u32[]{:S(2)}) collective-permute-start(f32[1,128]{1,0:T(1,128)S(1)} %get-tuple-element.27), channel_id=1, source_target_pairs={{0,6},{1,7},{2,8},{3,9},{4,10},{5,11},{6,12},{7,13},{8,14},{9,15},... | collective-permute-start | bytes 1544 | tf_op jit(solution)/shard_map/ppermute | solution.py:27
  91.7 0.0 collective-permute-start.24
  91.8 0.9 collective-permute-done.23
  92.7 3.3 %collective-permute-done.24 = f32[1,128]{1,0:T(1,128)S(1)} collective-permute-done((f32[1,128]{1,0:T(1,128)S(1)}, f32[1,128]{1,0:T(1,128)S(1)}, u32[]{:S(2)}, u32[]{:S(2)}) %collective-permute-start.24) | collective-permute-done | bytes 544 | tf_op jit(solution)/shard_map/ppermute | solution.py:27
  95.9 3.1 %collective-permute-start.27 = (f32[1,128]{1,0:T(1,128)S(1)}, f32[1,128]{1,0:T(1,128)S(1)}, u32[]{:S(2)}, u32[]{:S(2)}) collective-permute-start(f32[1,128]{1,0:T(1,128)S(1)} %add_add_fusion), channel_id=1, source_target_pairs={{0,129},{1,113},{2,131},{3,115},{4,133},{5,117},{6,135},{7,119},{8... | collective-permute-start | bytes 1544 | tf_op jit(solution)/shard_map/ppermute | solution.py:27
  99.0 3.0 %collective-permute-start.26 = (f32[1,128]{1,0:T(1,128)S(1)}, f32[1,128]{1,0:T(1,128)S(1)}, u32[]{:S(2)}, u32[]{:S(2)}) collective-permute-start(f32[1,128]{1,0:T(1,128)S(1)} %add_add_fusion), channel_id=1, source_target_pairs={{0,128},{1,112},{2,130},{3,114},{4,132},{5,116},{6,134},{7,118},{8... | collective-permute-start | bytes 1544 | tf_op jit(solution)/shard_map/ppermute | solution.py:27
  102.1 0.9 maximum_select_fusion
  102.9 0.1 reshape.67
  103.0 0.6 reduce_sum.9
  (55 shorter events, 0.1 us)
Async XLA Ops:
  0.6 42.1 %copy-start = (s32[2,1,4]{2,1,0:T(1,128)S(1)}, s32[2,1,4]{2,1,0:T(1,128)}, u32[]{:S(2)}) copy-start(s32[2,1,4]{2,1,0:T(1,128)} %param.3) | copy-start | bytes 100
  0.6 20.1 %collective-permute-start.1 = (bf16[2,2,64,1024]{3,2,1,0:T(8,128)(2,1)}, bf16[2,2,64,1024]{3,2,1,0:T(8,128)(2,1)S(1)}, u32[]{:S(2)}, u32[]{:S(2)}) collective-permute-start(bf16[2,2,64,1024]{3,2,1,0:T(8,128)(2,1)} %bitcast.15), channel_id=1, source_target_pairs={{0,158},{1,130},{2,144},{3,132},{4,146},{5,134},{6,148},{7,136},{8... | collective-permute-start | bytes 1572872 | tf_op jit(solution)/shard_map/ppermute | solution.py:27
  9.6 13.8 %collective-permute-start = (bf16[2,2,64,1024]{3,2,1,0:T(8,128)(2,1)}, bf16[2,2,64,1024]{3,2,1,0:T(8,128)(2,1)S(1)}, u32[]{:S(2)}, u32[]{:S(2)}) collective-permute-start(bf16[2,2,64,1024]{3,2,1,0:T(8,128)(2,1)} %bitcast.16), channel_id=1, source_target_pairs={{0,130},{1,158},{2,132},{3,144},{4,134},{5,146},{6,136},{7,148},{8... | collective-permute-start | bytes 1572872 | tf_op jit(solution)/shard_map/ppermute | solution.py:27
  20.8 23.3 %copy-start.5 = (bf16[2,2,64,1024]{3,2,1,0:T(8,128)(2,1)}, bf16[2,2,64,1024]{3,2,1,0:T(8,128)(2,1)S(1)}, u32[]{:S(2)}) copy-start(bf16[2,2,64,1024]{3,2,1,0:T(8,128)(2,1)S(1)} %collective-permute-done.1.refs_4_.refs_8_.refs_9_) | copy-start | bytes 1572868
  23.4 9.9 %collective-permute-start.2 = (bf16[2,2,64,1024]{3,2,1,0:T(8,128)(2,1)}, bf16[2,2,64,1024]{3,2,1,0:T(8,128)(2,1)S(1)}, u32[]{:S(2)}, u32[]{:S(2)}) collective-permute-start(bf16[2,2,64,1024]{3,2,1,0:T(8,128)(2,1)} %bitcast.17), channel_id=1, source_target_pairs={{0,128},{1,144},{2,130},{3,146},{4,132},{5,148},{6,134},{7,150},{8... | collective-permute-start | bytes 1572872 | tf_op jit(solution)/shard_map/ppermute | solution.py:27
  23.4 10.4 %collective-permute-start.5 = (bf16[2,2,64,1024]{3,2,1,0:T(8,128)(2,1)S(1)}, bf16[2,2,64,1024]{3,2,1,0:T(8,128)(2,1)}, u32[]{:S(2)}, u32[]{:S(2)}) collective-permute-start(bf16[2,2,64,1024]{3,2,1,0:T(8,128)(2,1)S(1)} %collective-permute-done.refs_1_.refs_3_), channel_id=1, source_target_pairs={{0,2},{1,3},{2,4},{3,5},{4,6},{5,7},{6,8},{7,9},{8,10},{9,11},{10,... | collective-permute-start | bytes 1572872 | tf_op jit(solution)/shard_map/ppermute | solution.py:27
  27.0 11.7 %collective-permute-start.11 = (bf16[2,2,64,1024]{3,2,1,0:T(8,128)(2,1)S(1)}, bf16[2,2,64,1024]{3,2,1,0:T(8,128)(2,1)}, u32[]{:S(2)}, u32[]{:S(2)}) collective-permute-start(bf16[2,2,64,1024]{3,2,1,0:T(8,128)(2,1)S(1)} %collective-permute-done.1.refs_4_.refs_8_.refs_9_), channel_id=1, source_target_pairs={{0,2},{1,3},{2,4},{3,5},{4,6},{5,7},{6,8},{7,9},{8,10},{9,11},{10,... | collective-permute-start | bytes 1572872 | tf_op jit(solution)/shard_map/ppermute | solution.py:27
  28.3 13.7 %collective-permute-start.9 = (bf16[2,2,64,1024]{3,2,1,0:T(8,128)(2,1)S(1)}, bf16[2,2,64,1024]{3,2,1,0:T(8,128)(2,1)S(1)}, u32[]{:S(2)}, u32[]{:S(2)}) collective-permute-start(bf16[2,2,64,1024]{3,2,1,0:T(8,128)(2,1)S(1)} %collective-permute-done.refs_1_.refs_3_), channel_id=1, source_target_pairs={{0,16},{1,17},{2,18},{3,19},{4,20},{5,21},{6,22},{7,23},{8,24},{9,... | collective-permute-start | bytes 1572872 | tf_op jit(solution)/shard_map/ppermute | solution.py:27
  28.3 0.8 copy-start.9
  33.3 9.5 %collective-permute-start.3 = (bf16[2,2,64,1024]{3,2,1,0:T(8,128)(2,1)S(1)}, bf16[2,2,64,1024]{3,2,1,0:T(8,128)(2,1)S(1)}, u32[]{:S(2)}, u32[]{:S(2)}) collective-permute-start(bf16[2,2,64,1024]{3,2,1,0:T(8,128)(2,1)S(1)} %collective-permute-done.2.own.refs_0_.refs_2_), channel_id=1, source_target_pairs={{0,16},{1,17},{2,18},{3,19},{4,20},{5,21},{6,22},{7,23},{8,24},{9,... | collective-permute-start | bytes 1572872 | tf_op jit(solution)/shard_map/ppermute | solution.py:27
  33.3 10.8 %collective-permute-start.8 = (bf16[2,2,64,1024]{3,2,1,0:T(8,128)(2,1)S(1)}, bf16[2,2,64,1024]{3,2,1,0:T(8,128)(2,1)S(1)}, u32[]{:S(2)}, u32[]{:S(2)}) collective-permute-start(bf16[2,2,64,1024]{3,2,1,0:T(8,128)(2,1)S(1)} %collective-permute-done.1.refs_4_.refs_8_.refs_9_), channel_id=1, source_target_pairs={{0,16},{1,17},{2,18},{3,19},{4,20},{5,21},{6,22},{7,23},{8,24},{9,... | collective-permute-start | bytes 1572872 | tf_op jit(solution)/shard_map/ppermute | solution.py:27
  33.8 12.3 %collective-permute-start.6 = (bf16[2,2,64,1024]{3,2,1,0:T(8,128)(2,1)}, bf16[2,2,64,1024]{3,2,1,0:T(8,128)(2,1)S(1)}, u32[]{:S(2)}, u32[]{:S(2)}) collective-permute-start(bf16[2,2,64,1024]{3,2,1,0:T(8,128)(2,1)} %collective-permute-done.5.refs_0_.refs_5_.refs_3_), channel_id=1, source_target_pairs={{0,2},{1,3},{2,4},{3,5},{4,6},{5,7},{6,8},{7,9},{8,10},{9,11},{10,... | collective-permute-start | bytes 1572872 | tf_op jit(solution)/shard_map/ppermute | solution.py:27
  38.7 11.3 %collective-permute-start.15 = (bf16[2,2,64,1024]{3,2,1,0:T(8,128)(2,1)}, bf16[2,2,64,1024]{3,2,1,0:T(8,128)(2,1)S(1)}, u32[]{:S(2)}, u32[]{:S(2)}) collective-permute-start(bf16[2,2,64,1024]{3,2,1,0:T(8,128)(2,1)} %collective-permute-done.11.refs_2_.refs_10_.refs_11_), channel_id=1, source_target_pairs={{0,2},{1,3},{2,4},{3,5},{4,6},{5,7},{6,8},{7,9},{8,10},{9,11},{10,... | collective-permute-start | bytes 1572872 | tf_op jit(solution)/shard_map/ppermute | solution.py:27
  42.0 0.8 copy-start.12
  42.8 9.4 %collective-permute-start.13 = (bf16[2,2,64,1024]{3,2,1,0:T(8,128)(2,1)}, bf16[2,2,64,1024]{3,2,1,0:T(8,128)(2,1)}, u32[]{:S(2)}, u32[]{:S(2)}) collective-permute-start(bf16[2,2,64,1024]{3,2,1,0:T(8,128)(2,1)} %collective-permute-done.5.refs_0_.refs_5_.refs_3_), channel_id=1, source_target_pairs={{0,16},{1,17},{2,18},{3,19},{4,20},{5,21},{6,22},{7,23},{8,24},{9,... | collective-permute-start | bytes 1572872 | tf_op jit(solution)/shard_map/ppermute | solution.py:27
  42.8 13.4 %collective-permute-start.12 = (bf16[2,2,64,1024]{3,2,1,0:T(8,128)(2,1)}, bf16[2,2,64,1024]{3,2,1,0:T(8,128)(2,1)S(1)}, u32[]{:S(2)}, u32[]{:S(2)}) collective-permute-start(bf16[2,2,64,1024]{3,2,1,0:T(8,128)(2,1)} %collective-permute-done.11.refs_2_.refs_10_.refs_11_), channel_id=1, source_target_pairs={{0,16},{1,17},{2,18},{3,19},{4,20},{5,21},{6,22},{7,23},{8,24},{9,... | collective-permute-start | bytes 1572872 | tf_op jit(solution)/shard_map/ppermute | solution.py:27
  43.4 21.6 %copy-start.21 = (s32[6]{0:T(128)}, s32[6]{0:T(128)S(1)}, u32[]{:S(2)}) copy-start(s32[6]{0:T(128)S(1)} %pad_add_fusion.info.refs_0_) | copy-start | bytes 76
  43.4 9.9 %copy-start.10 = (bf16[2,2,64,1024]{3,2,1,0:T(8,128)(2,1)S(1)}, bf16[2,2,64,1024]{3,2,1,0:T(8,128)(2,1)}, u32[]{:S(2)}) copy-start(bf16[2,2,64,1024]{3,2,1,0:T(8,128)(2,1)} %copy-done.9) | copy-start | bytes 1572868
  43.4 9.9 %copy-start.13 = (bf16[2,2,64,1024]{3,2,1,0:T(8,128)(2,1)S(1)}, bf16[2,2,64,1024]{3,2,1,0:T(8,128)(2,1)}, u32[]{:S(2)}) copy-start(bf16[2,2,64,1024]{3,2,1,0:T(8,128)(2,1)} %copy-done.12) | copy-start | bytes 1572868
  44.1 0.8 copy-start.15
  44.9 17.7 %collective-permute-start.4 = (bf16[2,128,1024]{2,1,0:T(8,128)(2,1)S(1)}, bf16[2,128,1024]{2,1,0:T(8,128)(2,1)S(1)}, u32[]{:S(2)}, u32[]{:S(2)}) collective-permute-start(bf16[2,128,1024]{2,1,0:T(8,128)(2,1)S(1)} %shard_map.41), channel_id=1, source_target_pairs={{0,33},{1,0},{2,35},{3,2},{4,37},{5,4},{6,39},{7,6},{8,41},{9,8},{... | collective-permute-start | bytes 1572872 | tf_op jit(solution)/shard_map/ppermute | solution.py:27
  46.1 19.0 %collective-permute-start.17 = (bf16[2,2,64,1024]{3,2,1,0:T(8,128)(2,1)S(1)}, bf16[2,2,64,1024]{3,2,1,0:T(8,128)(2,1)S(1)}, u32[]{:S(2)}, u32[]{:S(2)}) collective-permute-start(bf16[2,2,64,1024]{3,2,1,0:T(8,128)(2,1)S(1)} %collective-permute-done.6.refs_2_.refs_5_.refs_0_), channel_id=1, source_target_pairs={{0,16},{1,17},{2,18},{3,19},{4,20},{5,21},{6,22},{7,23},{8,24},{9,... | collective-permute-start | bytes 1572872 | tf_op jit(solution)/shard_map/ppermute | solution.py:27
  50.1 15.0 %collective-permute-start.16 = (bf16[2,2,64,1024]{3,2,1,0:T(8,128)(2,1)S(1)}, bf16[2,2,64,1024]{3,2,1,0:T(8,128)(2,1)S(1)}, u32[]{:S(2)}, u32[]{:S(2)}) collective-permute-start(bf16[2,2,64,1024]{3,2,1,0:T(8,128)(2,1)S(1)} %collective-permute-done.15.refs_4_.refs_13_.refs_3_), channel_id=1, source_target_pairs={{0,16},{1,17},{2,18},{3,19},{4,20},{5,21},{6,22},{7,23},{8,24},{9,... | collective-permute-start | bytes 1572872 | tf_op jit(solution)/shard_map/ppermute | solution.py:27
  52.2 14.9 %collective-permute-start.7 = (bf16[2,2,64,1024]{3,2,1,0:T(8,128)(2,1)S(1)}, bf16[2,2,64,1024]{3,2,1,0:T(8,128)(2,1)}, u32[]{:S(2)}, u32[]{:S(2)}) collective-permute-start(bf16[2,2,64,1024]{3,2,1,0:T(8,128)(2,1)S(1)} %collective-permute-done.6.refs_2_.refs_5_.refs_0_), channel_id=1, source_target_pairs={{0,2},{1,3},{2,4},{3,5},{4,6},{5,7},{6,8},{7,9},{8,10},{9,11},{10,... | collective-permute-start | bytes 1572872 | tf_op jit(solution)/shard_map/ppermute | solution.py:27
  53.4 1.0 %copy-start.6 = (bf16[2,2,64,1024]{3,2,1,0:T(8,128)(2,1)S(1)}, bf16[2,2,64,1024]{3,2,1,0:T(8,128)(2,1)}, u32[]{:S(2)}) copy-start(bf16[2,2,64,1024]{3,2,1,0:T(8,128)(2,1)} %copy-done.5) | copy-start | bytes 1572868
  54.4 1.0 %copy-start.16 = (bf16[2,2,64,1024]{3,2,1,0:T(8,128)(2,1)S(1)}, bf16[2,2,64,1024]{3,2,1,0:T(8,128)(2,1)}, u32[]{:S(2)}) copy-start(bf16[2,2,64,1024]{3,2,1,0:T(8,128)(2,1)} %copy-done.15) | copy-start | bytes 1572868
  56.2 6.5 %copy-start.7 = (bf16[2,2,64,1024]{3,2,1,0:T(8,128)(2,1)S(1)}, bf16[2,2,64,1024]{3,2,1,0:T(8,128)(2,1)}, u32[]{:S(2)}) copy-start(bf16[2,2,64,1024]{3,2,1,0:T(8,128)(2,1)} %copy-done.5) | copy-start | bytes 1572868
  56.2 6.5 %copy-start.17 = (bf16[2,2,64,1024]{3,2,1,0:T(8,128)(2,1)S(1)}, bf16[2,2,64,1024]{3,2,1,0:T(8,128)(2,1)}, u32[]{:S(2)}) copy-start(bf16[2,2,64,1024]{3,2,1,0:T(8,128)(2,1)} %copy-done.15) | copy-start | bytes 1572868
  56.2 6.4 %copy-start.1 = (bf16[2,2,64,1024]{3,2,1,0:T(8,128)(2,1)}, bf16[2,2,64,1024]{3,2,1,0:T(8,128)(2,1)S(1)}, u32[]{:S(2)}) copy-start(bf16[2,2,64,1024]{3,2,1,0:T(8,128)(2,1)S(1)} %collective-permute-done.12.refs_1_.refs_6_.refs_4_) | copy-start | bytes 1572868
  56.2 13.9 %collective-permute-start.10 = (bf16[3,2,128,128]{3,2,1,0:T(8,128)(2,1)S(1)}, bf16[3,2,128,128]{3,2,1,0:T(8,128)(2,1)S(1)}, u32[]{:S(2)}, u32[]{:S(2)}) collective-permute-start(bf16[3,2,128,128]{3,2,1,0:T(8,128)(2,1)S(1)} %shard_map.43), channel_id=1, source_target_pairs={{0,33},{1,0},{2,35},{3,2},{4,37},{5,4},{6,39},{7,6},{8,41},{9,8},{... | collective-permute-start | bytes 589832 | tf_op jit(solution)/shard_map/ppermute | solution.py:27
  62.6 2.5 %copy-start.3 = (bf16[2,128,1024]{2,1,0:T(8,128)(2,1)}, bf16[2,128,1024]{2,1,0:T(8,128)(2,1)S(1)}, u32[]{:S(2)}) copy-start(bf16[2,128,1024]{2,1,0:T(8,128)(2,1)S(1)} %collective-permute-done.4.refs_1_.a_ref) | copy-start | bytes 1572868
  62.6 7.5 %collective-permute-start.14 = (bf16[2,2,128,128]{3,2,1,0:T(8,128)(2,1)}, bf16[2,2,128,128]{3,2,1,0:T(8,128)(2,1)}, u32[]{:S(2)}, u32[]{:S(2)}) collective-permute-start(bf16[2,2,128,128]{3,2,1,0:T(8,128)(2,1)} %shard_map.44), channel_id=1, source_target_pairs={{0,33},{1,0},{2,35},{3,2},{4,37},{5,4},{6,39},{7,6},{8,41},{9,8},{... | collective-permute-start | bytes 393224 | tf_op jit(solution)/shard_map/ppermute | solution.py:27
  66.1 1.0 copy-start.19
  67.1 5.1 %copy-start.22 = (s32[6]{0:T(128)S(1)}, s32[6]{0:T(128)}, u32[]{:S(2)}) copy-start(s32[6]{0:T(128)} %copy-done.21) | copy-start | bytes 76
  67.9 5.6 %copy-start.2 = (bf16[2,2,64,1024]{3,2,1,0:T(8,128)(2,1)S(1)}, bf16[2,2,64,1024]{3,2,1,0:T(8,128)(2,1)}, u32[]{:S(2)}) copy-start(bf16[2,2,64,1024]{3,2,1,0:T(8,128)(2,1)} %copy-done.1) | copy-start | bytes 1572868
  67.9 5.6 %copy-start.4 = (bf16[2,128,1024]{2,1,0:T(8,128)(2,1)S(1)}, bf16[2,128,1024]{2,1,0:T(8,128)(2,1)}, u32[]{:S(2)}) copy-start(bf16[2,128,1024]{2,1,0:T(8,128)(2,1)} %copy-done.3) | copy-start | bytes 1572868
  67.9 5.6 %copy-start.8 = (bf16[2,2,64,1024]{3,2,1,0:T(8,128)(2,1)S(1)}, bf16[2,2,64,1024]{3,2,1,0:T(8,128)(2,1)}, u32[]{:S(2)}) copy-start(bf16[2,2,64,1024]{3,2,1,0:T(8,128)(2,1)} %copy-done.5) | copy-start | bytes 1572868
  67.9 5.6 %copy-start.11 = (bf16[2,2,64,1024]{3,2,1,0:T(8,128)(2,1)S(1)}, bf16[2,2,64,1024]{3,2,1,0:T(8,128)(2,1)}, u32[]{:S(2)}) copy-start(bf16[2,2,64,1024]{3,2,1,0:T(8,128)(2,1)} %copy-done.9) | copy-start | bytes 1572868
  68.0 5.6 %copy-start.14 = (bf16[2,2,64,1024]{3,2,1,0:T(8,128)(2,1)S(1)}, bf16[2,2,64,1024]{3,2,1,0:T(8,128)(2,1)}, u32[]{:S(2)}) copy-start(bf16[2,2,64,1024]{3,2,1,0:T(8,128)(2,1)} %copy-done.12) | copy-start | bytes 1572868
  68.0 5.6 %copy-start.18 = (bf16[2,2,64,1024]{3,2,1,0:T(8,128)(2,1)S(1)}, bf16[2,2,64,1024]{3,2,1,0:T(8,128)(2,1)}, u32[]{:S(2)}) copy-start(bf16[2,2,64,1024]{3,2,1,0:T(8,128)(2,1)} %copy-done.15) | copy-start | bytes 1572868
  70.1 2.1 %collective-permute-start.18 = (bf16[2,2,64,1024]{3,2,1,0:T(8,128)(2,1)}, bf16[2,2,64,1024]{3,2,1,0:T(8,128)(2,1)S(1)}, u32[]{:S(2)}, u32[]{:S(2)}) collective-permute-start(bf16[2,2,64,1024]{3,2,1,0:T(8,128)(2,1)} %shard_map.42.refs_7_.refs_2_), channel_id=1, source_target_pairs={{0,16},{1,17},{2,18},{3,19},{4,20},{5,21},{6,22},{7,23},{8,24},{9,... | collective-permute-start | bytes 1572872 | tf_op jit(solution)/shard_map/ppermute | solution.py:27
  73.4 8.8 %collective-permute-start.19 = (bf16[3,2,128,128]{3,2,1,0:T(8,128)(2,1)S(1)}, bf16[3,2,128,128]{3,2,1,0:T(8,128)(2,1)S(1)}, u32[]{:S(2)}, u32[]{:S(2)}) collective-permute-start(bf16[3,2,128,128]{3,2,1,0:T(8,128)(2,1)S(1)} %shard_map.48), channel_id=1, source_target_pairs={{0,33},{1,0},{2,35},{3,2},{4,37},{5,4},{6,39},{7,6},{8,41},{9,8},{... | collective-permute-start | bytes 589832 | tf_op jit(solution)/shard_map/ppermute | solution.py:27
  73.5 1.2 %copy-start.20 = (f32[256,1024]{1,0:T(8,128)S(1)}, f32[256,1024]{1,0:T(8,128)}, u32[]{:S(2)}) copy-start(f32[256,1024]{1,0:T(8,128)} %copy-done.19) | copy-start | bytes 3145732
  78.6 8.7 %collective-permute-start.22 = (bf16[2,64,1024]{2,1,0:T(8,128)(2,1)S(1)}, bf16[2,64,1024]{2,1,0:T(8,128)(2,1)S(1)}, u32[]{:S(2)}, u32[]{:S(2)}) collective-permute-start(bf16[2,64,1024]{2,1,0:T(8,128)(2,1)S(1)} %get-tuple-element.26), channel_id=1, source_target_pairs={{0,128},{1,112},{2,130},{3,114},{4,132},{5,116},{6,134},{7,118},{8... | collective-permute-start | bytes 786440 | tf_op jit(solution)/shard_map/ppermute | solution.py:27
  83.5 3.6 %collective-permute-start.21 = (f32[1,128]{1,0:T(1,128)S(1)}, f32[1,128]{1,0:T(1,128)S(1)}, u32[]{:S(2)}, u32[]{:S(2)}) collective-permute-start(f32[1,128]{1,0:T(1,128)S(1)} %shard_map.49), channel_id=1, source_target_pairs={{0,2},{1,3},{2,4},{3,5},{4,6},{5,7},{6,8},{7,9},{8,10},{9,11},{10,... | collective-permute-start | bytes 1544 | tf_op jit(solution)/shard_map/ppermute | solution.py:27
  83.6 3.6 %collective-permute-start.20 = (f32[1,128]{1,0:T(1,128)S(1)}, f32[1,128]{1,0:T(1,128)S(1)}, u32[]{:S(2)}, u32[]{:S(2)}) collective-permute-start(f32[1,128]{1,0:T(1,128)S(1)} %shard_map.49), channel_id=1, source_target_pairs={{0,14},{1,15},{2,0},{3,1},{4,2},{5,3},{6,4},{7,5},{8,6},{9,7},{10,... | collective-permute-start | bytes 1544 | tf_op jit(solution)/shard_map/ppermute | solution.py:27
  86.2 9.7 %collective-permute-start.25 = (bf16[2,64,1024]{2,1,0:T(8,128)(2,1)}, bf16[2,64,1024]{2,1,0:T(8,128)(2,1)S(1)}, u32[]{:S(2)}, u32[]{:S(2)}) collective-permute-start(bf16[2,64,1024]{2,1,0:T(8,128)(2,1)} %get-tuple-element.30), channel_id=1, source_target_pairs={{0,129},{1,113},{2,131},{3,115},{4,133},{5,117},{6,135},{7,119},{8... | collective-permute-start | bytes 786440 | tf_op jit(solution)/shard_map/ppermute | solution.py:27
  87.2 5.4 %collective-permute-start.23 = (f32[1,128]{1,0:T(1,128)S(1)}, f32[1,128]{1,0:T(1,128)S(1)}, u32[]{:S(2)}, u32[]{:S(2)}) collective-permute-start(f32[1,128]{1,0:T(1,128)S(1)} %get-tuple-element.27), channel_id=1, source_target_pairs={{0,6},{1,7},{2,8},{3,9},{4,10},{5,11},{6,12},{7,13},{8,14},{9,15},... | collective-permute-start | bytes 1544 | tf_op jit(solution)/shard_map/ppermute | solution.py:27
  91.7 4.2 %collective-permute-start.24 = (f32[1,128]{1,0:T(1,128)S(1)}, f32[1,128]{1,0:T(1,128)S(1)}, u32[]{:S(2)}, u32[]{:S(2)}) collective-permute-start(f32[1,128]{1,0:T(1,128)S(1)} %get-tuple-element.28), channel_id=1, source_target_pairs={{0,10},{1,11},{2,12},{3,13},{4,14},{5,15},{6,0},{7,1},{8,2},{9,3},... | collective-permute-start | bytes 1544 | tf_op jit(solution)/shard_map/ppermute | solution.py:27
  95.9 7.0 %collective-permute-start.27 = (f32[1,128]{1,0:T(1,128)S(1)}, f32[1,128]{1,0:T(1,128)S(1)}, u32[]{:S(2)}, u32[]{:S(2)}) collective-permute-start(f32[1,128]{1,0:T(1,128)S(1)} %add_add_fusion), channel_id=1, source_target_pairs={{0,129},{1,113},{2,131},{3,115},{4,133},{5,117},{6,135},{7,119},{8... | collective-permute-start | bytes 1544 | tf_op jit(solution)/shard_map/ppermute | solution.py:27
  99.0 3.9 %collective-permute-start.26 = (f32[1,128]{1,0:T(1,128)S(1)}, f32[1,128]{1,0:T(1,128)S(1)}, u32[]{:S(2)}, u32[]{:S(2)}) collective-permute-start(f32[1,128]{1,0:T(1,128)S(1)} %add_add_fusion), channel_id=1, source_target_pairs={{0,128},{1,112},{2,130},{3,114},{4,132},{5,116},{6,134},{7,118},{8... | collective-permute-start | bytes 1544 | tf_op jit(solution)/shard_map/ppermute | solution.py:27

commit v13 on v10

--- a/solution.py
+++ b/solution.py
@@ -27,12 +27,12 @@
     return lax.ppermute(block, BOTH, [(index_of(*at), index_of(*route(*at))) for at in places])
 
 
-def along(step):
-    return lambda m, c, z, h: (m, c, z + step, h)
-
-
 def onward(m, c, z, h):
     return (m, c, z + (1 if c == 0 else -1), h)
+
+
+def across(distance):
+    return lambda m, c, z, h: (m, c, z ^ distance, h)
 
 
 def other_core(m, c, z, h):
@@ -117,12 +117,6 @@
     count = len(refs) // 2
     for k in range(count):
         cut(info, refs[k], refs[count + k], 0, refs[-1].at[k])
-
-
-def late_kernel(info, own_u, own_d, other_u, other_d, out, across):
-    cut(info, own_u, other_u, 0, out.at[0])
-    cut(info, own_d, other_d, 0, out.at[1])
-    cut(info, own_u, other_u, -1, across)
 
 
 def left_side(info, a_ref, offset):
@@ -179,8 +173,8 @@
     return [jnp.sum(part, axis=0, keepdims=True) for part in (re, im)]
 
 
-def trace_kernel(info, product, early, late, across, trace):
-    re, im = trace_sum(info, product, [(3, late.at[0]), (-3, late.at[1]), (4, across)])
+def trace_kernel(info, product, early, late, trace):
+    re, im = trace_sum(info, product, [(3, late.at[0]), (-3, late.at[1]), (4, late.at[2])])
     re = jnp.sum(re + early[0:1, :], axis=1, keepdims=True)
     im = jnp.sum(im + early[1:2, :], axis=1, keepdims=True)
     lane = lax.broadcasted_iota(jnp.int32, (1, 128), 1)
@@ -224,31 +218,31 @@
     q3, acc = wall((q3, acc))
 
     q3x = moved(q3, other_core)
+    p4, middle = wall((p4, middle))
+
+    p4x = moved(p4, other_core)
     two, two_x = [p3, q3x], [q3, p3x]
-    late, across = call(late_kernel, info, two + two_x, (slices_of(2), jax.ShapeDtypeStruct((2, 128, 128), BF16)), 1)
-    p4, middle = wall((p4, middle))
-
-    p4x = moved(p4, other_core)
-    late, across = moved(late, hub_ahead(0)), moved(across, hub_ahead(1))
     acc = call(
         lambda *refs: products_kernel(OFFSETS[5:7], *refs), info, [a] + two + two_x + [acc], block_of_products, 1
     )
+    late = moved(call(cut_kernel, info, two + [p4] + two_x + [p4x], slices_of(3), 1), hub_ahead(0))
     half_block = jax.ShapeDtypeStruct((2, 64, 1024), BF16)
     keep, send, product, early = call(
         last_kernel,
         info,
         [a, acc, near, middle] + five + two + [p4] + five_x + two_x + [p4x],
         (half_block, half_block, block_of_products, jax.ShapeDtypeStruct((8, 128), F32)),
-        1,
+        WEIGHT,
         [pltpu.VMEM((2, 128, 1024), BF16)],
     )
-    trace = call(trace_kernel, info, [product, early, late, across], jax.ShapeDtypeStruct((1, 128), F32), 1)
-
-    below, above = moved(trace, along(1)), moved(trace, along(-1))
+    trace = call(trace_kernel, info, [product, early, late], jax.ShapeDtypeStruct((1, 128), F32), WEIGHT)
+
     kept, sent = moved(keep, from_hub(0)), moved(send, from_hub(1))
-    two, three, kept = wall((trace + above, below + trace + above, kept))
-    below, above = moved(two, along(3)), moved(three, along(-3))
-    trace, kept, sent = wall((below + three + above, kept, sent))
+    trace = trace + moved(trace, across(1))
+    trace = trace + moved(trace, across(2))
+    trace, kept = wall((trace, kept))
+    trace = trace + moved(trace, across(4))
+    trace, sent = wall((trace, sent))
     first, second = moved(trace, from_hub(0)), moved(trace, from_hub(1))
     products = jnp.where(half == 0, jnp.stack([kept, sent]), jnp.stack([sent, kept]))[:, None, None]
     both = jnp.where(half == 0, jnp.concatenate([first, second]), jnp.concatenate([second, first]))

time: 95 us -> 94.9 us (level)
  starting transfers between devices: 57.8 us -> 53.5 us
  waiting for transfers between devices: 25.9 us -> 30.1 us
    ppermute x29 -> x27, starting transfers between devices: 57.8 us -> 53.5 us  [moved(): lax.ppermute(block, BOTH, [(index_of(*at), index_of(*route(*at))) for at...]
    ppermute x29 -> x27, waiting for transfers between devices: 25.9 us -> 30.1 us  [moved(): lax.ppermute(block, BOTH, [(index_of(*at), index_of(*route(*at))) for at...]
  transfers between devices with their start and end apart: 29 -> 27, of which waited for: 11 -> 12; matrix products, arithmetic and copies ran while one was open for 1% -> 1% of each run, Pallas kernels for 9% -> 9%
where the time goes in v13:
time: 94.9 us; the launch traced here: 94.8 us
  starting transfers between devices  53.5 us (56%)
  waiting for transfers between devices  30.1 us (32%)
  Pallas kernels  8.83 us (9%)
  other arithmetic  1.56 us (2%)
    ppermute x27, starting transfers between devices, moved(): lax.ppermute(block, BOTH, [(index_of(*at), index_of(*route(*at))) for at...  53.5 us
    ppermute x27, waiting for transfers between devices, moved(): lax.ppermute(block, BOTH, [(index_of(*at), index_of(*route(*at))) for at...  30.1 us
    pallas_call x9, Pallas kernels, call(): pl.pallas_call(kernel, out_shape=out_shape, in_specs=[SMEM] + [VMEM] * le...  8.83 us
  transfers between devices with their start and end apart: 27, of which 12 were waited for; matrix products, arithmetic and copies ran while one was open for 1% of the time, Pallas kernels for 9%

profile of v13, /device:TPU:1, one launch (start us, length us, event | category | flops | bytes accessed | tf_op | source)
XLA Modules:
  0.0 94.8 jit_solution(16403444645347871887)
XLA Ops:
  0.6 0.0 copy-start
  0.6 4.2 %collective-permute-start = (bf16[2,2,64,1024]{3,2,1,0:T(8,128)(2,1)}, bf16[2,2,64,1024]{3,2,1,0:T(8,128)(2,1)S(1)}, u32[]{:S(2)}, u32[]{:S(2)}) collective-permute-start(bf16[2,2,64,1024]{3,2,1,0:T(8,128)(2,1)} %bitcast.15), channel_id=1, source_target_pairs={{0,128},{1,144},{2,130},{3,146},{4,132},{5,148},{6,134},{7,150},{8... | collective-permute-start | bytes 1572872 | tf_op jit(solution)/shard_map/ppermute | solution.py:27
  4.8 6.4 %collective-permute-done.own.refs_2_.refs_0_ = bf16[2,2,64,1024]{3,2,1,0:T(8,128)(2,1)S(1)} collective-permute-done((bf16[2,2,64,1024]{3,2,1,0:T(8,128)(2,1)}, bf16[2,2,64,1024]{3,2,1,0:T(8,128)(2,1)S(1)}, u32[]{:S(2)}, u32[]{:S(2)}) %collective-permute-start) | collective-permute-done | bytes 524320 | tf_op jit(solution)/shard_map/ppermute | solution.py:27
  11.3 1.5 %collective-permute-start.3 = (bf16[2,2,64,1024]{3,2,1,0:T(8,128)(2,1)S(1)}, bf16[2,2,64,1024]{3,2,1,0:T(8,128)(2,1)S(1)}, u32[]{:S(2)}, u32[]{:S(2)}) collective-permute-start(bf16[2,2,64,1024]{3,2,1,0:T(8,128)(2,1)S(1)} %collective-permute-done.own.refs_2_.refs_0_), channel_id=1, source_target_pairs={{0,16},{1,17},{2,18},{3,19},{4,20},{5,21},{6,22},{7,23},{8,24},{9,... | collective-permute-start | bytes 1572872 | tf_op jit(solution)/shard_map/ppermute | solution.py:27
  12.8 4.1 %collective-permute-start.1 = (bf16[2,2,64,1024]{3,2,1,0:T(8,128)(2,1)S(1)}, bf16[2,2,64,1024]{3,2,1,0:T(8,128)(2,1)S(1)}, u32[]{:S(2)}, u32[]{:S(2)}) collective-permute-start(bf16[2,2,64,1024]{3,2,1,0:T(8,128)(2,1)S(1)} %collective-permute-done.own.refs_2_.refs_0_), channel_id=1, source_target_pairs={{0,2},{1,3},{2,4},{3,5},{4,6},{5,7},{6,8},{7,9},{8,10},{9,11},{10,... | collective-permute-start | bytes 1572872 | tf_op jit(solution)/shard_map/ppermute | solution.py:27
  16.9 0.0 collective-permute-done.3.other.refs_3_.refs_8_
  16.9 1.9 %collective-permute-start.6 = (bf16[2,2,64,1024]{3,2,1,0:T(8,128)(2,1)S(1)}, bf16[2,2,64,1024]{3,2,1,0:T(8,128)(2,1)S(1)}, u32[]{:S(2)}, u32[]{:S(2)}) collective-permute-start(bf16[2,2,64,1024]{3,2,1,0:T(8,128)(2,1)S(1)} %collective-permute-done.3.other.refs_3_.refs_8_), channel_id=1, source_target_pairs={{0,2},{1,3},{2,4},{3,5},{4,6},{5,7},{6,8},{7,9},{8,10},{9,11},{10,... | collective-permute-start | bytes 1572872 | tf_op jit(solution)/shard_map/ppermute | solution.py:27
  18.8 0.1 pad_add_fusion.info.refs_0_
  18.9 0.6 shard_map.41
  19.4 1.3 %collective-permute-start.4 = (bf16[2,128,1024]{2,1,0:T(8,128)(2,1)S(1)}, bf16[2,128,1024]{2,1,0:T(8,128)(2,1)S(1)}, u32[]{:S(2)}, u32[]{:S(2)}) collective-permute-start(bf16[2,128,1024]{2,1,0:T(8,128)(2,1)S(1)} %shard_map.41), channel_id=1, source_target_pairs={{0,33},{1,0},{2,35},{3,2},{4,37},{5,4},{6,39},{7,6},{8,41},{9,8},{... | collective-permute-start | bytes 1572872 | tf_op jit(solution)/shard_map/ppermute | solution.py:27
  20.7 2.3 %collective-permute-done.1.refs_1_.refs_2_ = bf16[2,2,64,1024]{3,2,1,0:T(8,128)(2,1)S(1)} collective-permute-done((bf16[2,2,64,1024]{3,2,1,0:T(8,128)(2,1)S(1)}, bf16[2,2,64,1024]{3,2,1,0:T(8,128)(2,1)S(1)}, u32[]{:S(2)}, u32[]{:S(2)}) %collective-permute-start.1) | collective-permute-done | bytes 524320 | tf_op jit(solution)/shard_map/ppermute | solution.py:27
  23.0 3.4 %collective-permute-start.2 = (bf16[2,2,64,1024]{3,2,1,0:T(8,128)(2,1)S(1)}, bf16[2,2,64,1024]{3,2,1,0:T(8,128)(2,1)S(1)}, u32[]{:S(2)}, u32[]{:S(2)}) collective-permute-start(bf16[2,2,64,1024]{3,2,1,0:T(8,128)(2,1)S(1)} %collective-permute-done.1.refs_1_.refs_2_), channel_id=1, source_target_pairs={{0,2},{1,3},{2,4},{3,5},{4,6},{5,7},{6,8},{7,9},{8,10},{9,11},{10,... | collective-permute-start | bytes 1572872 | tf_op jit(solution)/shard_map/ppermute | solution.py:27
  26.4 0.0 collective-permute-start.8
  26.4 2.2 %collective-permute-done.6.refs_4_.refs_6_.refs_9_ = bf16[2,2,64,1024]{3,2,1,0:T(8,128)(2,1)S(1)} collective-permute-done((bf16[2,2,64,1024]{3,2,1,0:T(8,128)(2,1)S(1)}, bf16[2,2,64,1024]{3,2,1,0:T(8,128)(2,1)S(1)}, u32[]{:S(2)}, u32[]{:S(2)}) %collective-permute-start.6) | collective-permute-done | bytes 524320 | tf_op jit(solution)/shard_map/ppermute | solution.py:27
  28.6 3.1 %collective-permute-start.10 = (bf16[2,2,64,1024]{3,2,1,0:T(8,128)(2,1)S(1)}, bf16[2,2,64,1024]{3,2,1,0:T(8,128)(2,1)S(1)}, u32[]{:S(2)}, u32[]{:S(2)}) collective-permute-start(bf16[2,2,64,1024]{3,2,1,0:T(8,128)(2,1)S(1)} %collective-permute-done.6.refs_4_.refs_6_.refs_9_), channel_id=1, source_target_pairs={{0,2},{1,3},{2,4},{3,5},{4,6},{5,7},{6,8},{7,9},{8,10},{9,11},{10,... | collective-permute-start | bytes 1572872 | tf_op jit(solution)/shard_map/ppermute | solution.py:27
  31.7 0.0 collective-permute-start.7
  31.7 2.5 %collective-permute-done.4.refs_1_.a_ref = bf16[2,128,1024]{2,1,0:T(8,128)(2,1)S(1)} collective-permute-done((bf16[2,128,1024]{2,1,0:T(8,128)(2,1)S(1)}, bf16[2,128,1024]{2,1,0:T(8,128)(2,1)S(1)}, u32[]{:S(2)}, u32[]{:S(2)}) %collective-permute-start.4) | collective-permute-done | bytes 524320 | tf_op jit(solution)/shard_map/ppermute | solution.py:27
  34.2 0.8 shard_map.42.refs_10_
  35.1 0.0 collective-permute-done.2.refs_4_.refs_0_.refs_3_
  35.1 3.7 %collective-permute-start.5 = (bf16[2,2,64,1024]{3,2,1,0:T(8,128)(2,1)S(1)}, bf16[2,2,64,1024]{3,2,1,0:T(8,128)(2,1)S(1)}, u32[]{:S(2)}, u32[]{:S(2)}) collective-permute-start(bf16[2,2,64,1024]{3,2,1,0:T(8,128)(2,1)S(1)} %collective-permute-done.2.refs_4_.refs_0_.refs_3_), channel_id=1, source_target_pairs={{0,2},{1,3},{2,4},{3,5},{4,6},{5,7},{6,8},{7,9},{8,10},{9,11},{10,... | collective-permute-start | bytes 1572872 | tf_op jit(solution)/shard_map/ppermute | solution.py:27
  38.8 0.7 shard_map.43
  39.4 0.1 collective-permute-start.9
  39.5 1.2 %collective-permute-start.13 = (bf16[2,2,64,1024]{3,2,1,0:T(8,128)(2,1)S(1)}, bf16[2,2,64,1024]{3,2,1,0:T(8,128)(2,1)S(1)}, u32[]{:S(2)}, u32[]{:S(2)}) collective-permute-start(bf16[2,2,64,1024]{3,2,1,0:T(8,128)(2,1)S(1)} %collective-permute-done.2.refs_4_.refs_0_.refs_3_), channel_id=1, source_target_pairs={{0,16},{1,17},{2,18},{3,19},{4,20},{5,21},{6,22},{7,23},{8,24},{9,... | collective-permute-start | bytes 1572872 | tf_op jit(solution)/shard_map/ppermute | solution.py:27
  40.8 0.0 collective-permute-done.10.refs_8_.refs_2_.refs_11_
  40.8 0.9 collective-permute-start.12
  41.7 2.1 %collective-permute-start.11 = (bf16[2,2,64,1024]{3,2,1,0:T(8,128)(2,1)S(1)}, bf16[2,2,64,1024]{3,2,1,0:T(8,128)(2,1)S(1)}, u32[]{:S(2)}, u32[]{:S(2)}) collective-permute-start(bf16[2,2,64,1024]{3,2,1,0:T(8,128)(2,1)S(1)} %collective-permute-done.10.refs_8_.refs_2_.refs_11_), channel_id=1, source_target_pairs={{0,2},{1,3},{2,4},{3,5},{4,6},{5,7},{6,8},{7,9},{8,10},{9,11},{10,... | collective-permute-start | bytes 1572872 | tf_op jit(solution)/shard_map/ppermute | solution.py:27
  43.7 1.7 %collective-permute-done.5.refs_2_.refs_5_.refs_0_ = bf16[2,2,64,1024]{3,2,1,0:T(8,128)(2,1)S(1)} collective-permute-done((bf16[2,2,64,1024]{3,2,1,0:T(8,128)(2,1)S(1)}, bf16[2,2,64,1024]{3,2,1,0:T(8,128)(2,1)S(1)}, u32[]{:S(2)}, u32[]{:S(2)}) %collective-permute-start.5) | collective-permute-done | bytes 524320 | tf_op jit(solution)/shard_map/ppermute | solution.py:27
  45.5 2.1 %collective-permute-done.9.near = bf16[3,2,128,128]{3,2,1,0:T(8,128)(2,1)S(1)} collective-permute-done((bf16[3,2,128,128]{3,2,1,0:T(8,128)(2,1)S(1)}, bf16[3,2,128,128]{3,2,1,0:T(8,128)(2,1)S(1)}, u32[]{:S(2)}, u32[]{:S(2)}) %collective-permute-start.9) | collective-permute-done | bytes 196640 | tf_op jit(solution)/shard_map/ppermute | solution.py:27
  47.6 1.0 %collective-permute-start.16 = (bf16[2,2,64,1024]{3,2,1,0:T(8,128)(2,1)S(1)}, bf16[2,2,64,1024]{3,2,1,0:T(8,128)(2,1)S(1)}, u32[]{:S(2)}, u32[]{:S(2)}) collective-permute-start(bf16[2,2,64,1024]{3,2,1,0:T(8,128)(2,1)S(1)} %collective-permute-done.5.refs_2_.refs_5_.refs_0_), channel_id=1, source_target_pairs={{0,2},{1,3},{2,4},{3,5},{4,6},{5,7},{6,8},{7,9},{8,10},{9,11},{10,... | collective-permute-start | bytes 1572872 | tf_op jit(solution)/shard_map/ppermute | solution.py:27
  48.6 0.0 collective-permute-done.13.refs_9_.refs_3_.refs_12_
  48.6 0.0 collective-permute-done.12.refs_5_.refs_1_.refs_4_
  48.6 0.6 shard_map.46
  49.2 1.3 %collective-permute-start.17 = (bf16[2,2,128,128]{3,2,1,0:T(8,128)(2,1)S(1)}, bf16[2,2,128,128]{3,2,1,0:T(8,128)(2,1)S(1)}, u32[]{:S(2)}, u32[]{:S(2)}) collective-permute-start(bf16[2,2,128,128]{3,2,1,0:T(8,128)(2,1)S(1)} %shard_map.46), channel_id=1, source_target_pairs={{0,33},{1,0},{2,35},{3,2},{4,37},{5,4},{6,39},{7,6},{8,41},{9,8},{... | collective-permute-start | bytes 393224 | tf_op jit(solution)/shard_map/ppermute | solution.py:27
  50.5 1.4 %collective-permute-start.15 = (bf16[2,2,64,1024]{3,2,1,0:T(8,128)(2,1)S(1)}, bf16[2,2,64,1024]{3,2,1,0:T(8,128)(2,1)S(1)}, u32[]{:S(2)}, u32[]{:S(2)}) collective-permute-start(bf16[2,2,64,1024]{3,2,1,0:T(8,128)(2,1)S(1)} %collective-permute-done.5.refs_2_.refs_5_.refs_0_), channel_id=1, source_target_pairs={{0,16},{1,17},{2,18},{3,19},{4,20},{5,21},{6,22},{7,23},{8,24},{9,... | collective-permute-start | bytes 1572872 | tf_op jit(solution)/shard_map/ppermute | solution.py:27
  52.0 1.3 %shard_map.44.refs_6_ = f32[256,1024]{1,0:T(8,128)S(1)} custom-call(s32[6]{0:T(128)S(1)} %pad_add_fusion.info.refs_0_, bf16[2,128,1024]{2,1,0:T(8,128)(2,1)S(1)} %collective-permute-done.4.refs_1_.a_ref, bf16[2,2,64,1024]{3,2,1,0:T(8,128)(2,1)S(1)} %collective-permute-done.1.refs_1_.refs_2_, ...), custom_call_target="tpu_custom_call" | custom-call | flops 1 | bytes 1048576 | tf_op jit(solution)/shard_map/pallas_call | solution.py:75
  53.3 0.0 collective-permute-done.11.refs_4_.refs_13_.refs_3_
  53.3 0.1 collective-permute-start.14
  53.4 4.2 %collective-permute-done.17.middle = bf16[2,2,128,128]{3,2,1,0:T(8,128)(2,1)S(1)} collective-permute-done((bf16[2,2,128,128]{3,2,1,0:T(8,128)(2,1)S(1)}, bf16[2,2,128,128]{3,2,1,0:T(8,128)(2,1)S(1)}, u32[]{:S(2)}, u32[]{:S(2)}) %collective-permute-start.17) | collective-permute-done | bytes 131104 | tf_op jit(solution)/shard_map/ppermute | solution.py:27
  57.6 0.9 collective-permute-start.18
  58.5 0.0 collective-permute-done.14.refs_3_.refs_6_.refs_1_
  58.5 1.0 %shard_map.45.acc = f32[256,1024]{1,0:T(8,128)S(1)} custom-call(s32[6]{0:T(128)S(1)} %pad_add_fusion.info.refs_0_, bf16[2,128,1024]{2,1,0:T(8,128)(2,1)S(1)} %collective-permute-done.4.refs_1_.a_ref, bf16[2,2,64,1024]{3,2,1,0:T(8,128)(2,1)S(1)} %collective-permute-done.5.refs_2_.refs_5_.refs_0_, ...), custom_call_target="tpu_custom_call" | custom-call | flops 1 | bytes 1048576 | tf_op jit(solution)/shard_map/pallas_call | solution.py:75
  59.5 0.5 collective-permute-done.18.refs_15_.refs_5_
  60.1 0.7 shard_map.48
  60.7 1.3 %collective-permute-start.19 = (bf16[3,2,128,128]{3,2,1,0:T(8,128)(2,1)S(1)}, bf16[3,2,128,128]{3,2,1,0:T(8,128)(2,1)S(1)}, u32[]{:S(2)}, u32[]{:S(2)}) collective-permute-start(bf16[3,2,128,128]{3,2,1,0:T(8,128)(2,1)S(1)} %shard_map.48), channel_id=1, source_target_pairs={{0,33},{1,0},{2,35},{3,2},{4,37},{5,4},{6,39},{7,6},{8,41},{9,8},{... | collective-permute-start | bytes 589832 | tf_op jit(solution)/shard_map/ppermute | solution.py:27
  62.0 2.4 %shard_map.47 = (bf16[2,64,1024]{2,1,0:T(8,128)(2,1)S(1)}, bf16[2,64,1024]{2,1,0:T(8,128)(2,1)S(1)}, f32[256,1024]{1,0:T(8,128)S(1)}, f32[8,128]{1,0:T(8,128)S(1)}) custom-call(s32[6]{0:T(128)S(1)} %pad_add_fusion.info.refs_0_, bf16[2,128,1024]{2,1,0:T(8,128)(2,1)S(1)} %collective-permute-done.4.refs_1_.a_ref, f32[256,1024]{1,0:T(8,128)S(1)} %shard_map.45.acc, ...), custom_call_target="tpu_custom_call" | custom-call | flops 3000000000 | bytes 1048576 | tf_op jit(solution)/shard_map/pallas_call | solution.py:75
  64.4 3.9 %collective-permute-start.22 = (bf16[2,64,1024]{2,1,0:T(8,128)(2,1)S(1)}, bf16[2,64,1024]{2,1,0:T(8,128)(2,1)S(1)}, u32[]{:S(2)}, u32[]{:S(2)}) collective-permute-start(bf16[2,64,1024]{2,1,0:T(8,128)(2,1)S(1)} %get-tuple-element.30), channel_id=1, source_target_pairs={{0,128},{1,112},{2,130},{3,114},{4,132},{5,116},{6,134},{7,118},{8... | collective-permute-start | bytes 786440 | tf_op jit(solution)/shard_map/ppermute | solution.py:27
  68.3 1.8 %collective-permute-start.24 = (bf16[2,64,1024]{2,1,0:T(8,128)(2,1)S(1)}, bf16[2,64,1024]{2,1,0:T(8,128)(2,1)S(1)}, u32[]{:S(2)}, u32[]{:S(2)}) collective-permute-start(bf16[2,64,1024]{2,1,0:T(8,128)(2,1)S(1)} %get-tuple-element.33), channel_id=1, source_target_pairs={{0,129},{1,113},{2,131},{3,115},{4,133},{5,117},{6,135},{7,119},{8... | collective-permute-start | bytes 786440 | tf_op jit(solution)/shard_map/ppermute | solution.py:27
  70.1 0.7 collective-permute-done.19.late
  70.9 0.7 shard_map.49
  71.6 0.0 collective-permute-start.20
  71.6 2.7 %collective-permute-done.20 = f32[1,128]{1,0:T(1,128)S(1)} collective-permute-done((f32[1,128]{1,0:T(1,128)S(1)}, f32[1,128]{1,0:T(1,128)S(1)}, u32[]{:S(2)}, u32[]{:S(2)}) %collective-permute-start.20) | collective-permute-done | bytes 544 | tf_op jit(solution)/shard_map/ppermute | solution.py:27
  74.3 0.9 collective-permute-start.21
  75.2 2.7 %collective-permute-done.21 = f32[1,128]{1,0:T(1,128)S(1)} collective-permute-done((f32[1,128]{1,0:T(1,128)S(1)}, f32[1,128]{1,0:T(1,128)S(1)}, u32[]{:S(2)}, u32[]{:S(2)}) %collective-permute-start.21) | collective-permute-done | bytes 544 | tf_op jit(solution)/shard_map/ppermute | solution.py:27
  77.9 0.0 collective-permute-done.22
  77.9 4.3 %collective-permute-start.23 = (f32[1,128]{1,0:T(1,128)S(1)}, f32[1,128]{1,0:T(1,128)S(1)}, u32[]{:S(2)}, u32[]{:S(2)}) collective-permute-start(f32[1,128]{1,0:T(1,128)S(1)} %add.25), channel_id=1, source_target_pairs={{0,8},{1,9},{2,10},{3,11},{4,12},{5,13},{6,14},{7,15},{8,0},{9,1},... | collective-permute-start | bytes 1544 | tf_op jit(solution)/shard_map/ppermute | solution.py:27
  82.2 2.0 %collective-permute-done.23 = f32[1,128]{1,0:T(1,128)S(1)} collective-permute-done((f32[1,128]{1,0:T(1,128)S(1)}, f32[1,128]{1,0:T(1,128)S(1)}, u32[]{:S(2)}, u32[]{:S(2)}) %collective-permute-start.23) | collective-permute-done | bytes 544 | tf_op jit(solution)/shard_map/ppermute | solution.py:27
  84.2 0.0 collective-permute-done.24
  84.2 2.6 %collective-permute-start.26 = (f32[1,128]{1,0:T(1,128)S(1)}, f32[1,128]{1,0:T(1,128)S(1)}, u32[]{:S(2)}, u32[]{:S(2)}) collective-permute-start(f32[1,128]{1,0:T(1,128)S(1)} %add.26), channel_id=1, source_target_pairs={{0,129},{1,113},{2,131},{3,115},{4,133},{5,117},{6,135},{7,119},{8... | collective-permute-start | bytes 1544 | tf_op jit(solution)/shard_map/ppermute | solution.py:27
  86.8 6.4 %collective-permute-start.25 = (f32[1,128]{1,0:T(1,128)S(1)}, f32[1,128]{1,0:T(1,128)S(1)}, u32[]{:S(2)}, u32[]{:S(2)}) collective-permute-start(f32[1,128]{1,0:T(1,128)S(1)} %add.26), channel_id=1, source_target_pairs={{0,128},{1,112},{2,130},{3,114},{4,132},{5,116},{6,134},{7,118},{8... | collective-permute-start | bytes 1544 | tf_op jit(solution)/shard_map/ppermute | solution.py:27
  93.2 0.9 maximum_select_fusion
  94.1 0.0 collective-permute-done.26
  94.1 0.0 collective-permute-done.25
  94.1 0.1 reshape.77
  94.2 0.6 broadcast_multiply_fusion
  (11 shorter events, 0.1 us)
Async XLA Ops:
  0.6 16.2 %copy-start = (s32[2,1,4]{2,1,0:T(1,128)S(1)}, s32[2,1,4]{2,1,0:T(1,128)}, u32[]{:S(2)}) copy-start(s32[2,1,4]{2,1,0:T(1,128)} %param.3) | copy-start | bytes 100
  0.6 10.6 %collective-permute-start = (bf16[2,2,64,1024]{3,2,1,0:T(8,128)(2,1)}, bf16[2,2,64,1024]{3,2,1,0:T(8,128)(2,1)S(1)}, u32[]{:S(2)}, u32[]{:S(2)}) collective-permute-start(bf16[2,2,64,1024]{3,2,1,0:T(8,128)(2,1)} %bitcast.15), channel_id=1, source_target_pairs={{0,128},{1,144},{2,130},{3,146},{4,132},{5,148},{6,134},{7,150},{8... | collective-permute-start | bytes 1572872 | tf_op jit(solution)/shard_map/ppermute | solution.py:27
  11.3 5.6 %collective-permute-start.3 = (bf16[2,2,64,1024]{3,2,1,0:T(8,128)(2,1)S(1)}, bf16[2,2,64,1024]{3,2,1,0:T(8,128)(2,1)S(1)}, u32[]{:S(2)}, u32[]{:S(2)}) collective-permute-start(bf16[2,2,64,1024]{3,2,1,0:T(8,128)(2,1)S(1)} %collective-permute-done.own.refs_2_.refs_0_), channel_id=1, source_target_pairs={{0,16},{1,17},{2,18},{3,19},{4,20},{5,21},{6,22},{7,23},{8,24},{9,... | collective-permute-start | bytes 1572872 | tf_op jit(solution)/shard_map/ppermute | solution.py:27
  12.8 10.2 %collective-permute-start.1 = (bf16[2,2,64,1024]{3,2,1,0:T(8,128)(2,1)S(1)}, bf16[2,2,64,1024]{3,2,1,0:T(8,128)(2,1)S(1)}, u32[]{:S(2)}, u32[]{:S(2)}) collective-permute-start(bf16[2,2,64,1024]{3,2,1,0:T(8,128)(2,1)S(1)} %collective-permute-done.own.refs_2_.refs_0_), channel_id=1, source_target_pairs={{0,2},{1,3},{2,4},{3,5},{4,6},{5,7},{6,8},{7,9},{8,10},{9,11},{10,... | collective-permute-start | bytes 1572872 | tf_op jit(solution)/shard_map/ppermute | solution.py:27
  16.9 11.7 %collective-permute-start.6 = (bf16[2,2,64,1024]{3,2,1,0:T(8,128)(2,1)S(1)}, bf16[2,2,64,1024]{3,2,1,0:T(8,128)(2,1)S(1)}, u32[]{:S(2)}, u32[]{:S(2)}) collective-permute-start(bf16[2,2,64,1024]{3,2,1,0:T(8,128)(2,1)S(1)} %collective-permute-done.3.other.refs_3_.refs_8_), channel_id=1, source_target_pairs={{0,2},{1,3},{2,4},{3,5},{4,6},{5,7},{6,8},{7,9},{8,10},{9,11},{10,... | collective-permute-start | bytes 1572872 | tf_op jit(solution)/shard_map/ppermute | solution.py:27
  19.4 14.8 %collective-permute-start.4 = (bf16[2,128,1024]{2,1,0:T(8,128)(2,1)S(1)}, bf16[2,128,1024]{2,1,0:T(8,128)(2,1)S(1)}, u32[]{:S(2)}, u32[]{:S(2)}) collective-permute-start(bf16[2,128,1024]{2,1,0:T(8,128)(2,1)S(1)} %shard_map.41), channel_id=1, source_target_pairs={{0,33},{1,0},{2,35},{3,2},{4,37},{5,4},{6,39},{7,6},{8,41},{9,8},{... | collective-permute-start | bytes 1572872 | tf_op jit(solution)/shard_map/ppermute | solution.py:27
  23.0 12.1 %collective-permute-start.2 = (bf16[2,2,64,1024]{3,2,1,0:T(8,128)(2,1)S(1)}, bf16[2,2,64,1024]{3,2,1,0:T(8,128)(2,1)S(1)}, u32[]{:S(2)}, u32[]{:S(2)}) collective-permute-start(bf16[2,2,64,1024]{3,2,1,0:T(8,128)(2,1)S(1)} %collective-permute-done.1.refs_1_.refs_2_), channel_id=1, source_target_pairs={{0,2},{1,3},{2,4},{3,5},{4,6},{5,7},{6,8},{7,9},{8,10},{9,11},{10,... | collective-permute-start | bytes 1572872 | tf_op jit(solution)/shard_map/ppermute | solution.py:27
  26.4 12.3 %collective-permute-start.8 = (bf16[2,2,64,1024]{3,2,1,0:T(8,128)(2,1)S(1)}, bf16[2,2,64,1024]{3,2,1,0:T(8,128)(2,1)S(1)}, u32[]{:S(2)}, u32[]{:S(2)}) collective-permute-start(bf16[2,2,64,1024]{3,2,1,0:T(8,128)(2,1)S(1)} %collective-permute-done.1.refs_1_.refs_2_), channel_id=1, source_target_pairs={{0,16},{1,17},{2,18},{3,19},{4,20},{5,21},{6,22},{7,23},{8,24},{9,... | collective-permute-start | bytes 1572872 | tf_op jit(solution)/shard_map/ppermute | solution.py:27
  28.6 12.2 %collective-permute-start.10 = (bf16[2,2,64,1024]{3,2,1,0:T(8,128)(2,1)S(1)}, bf16[2,2,64,1024]{3,2,1,0:T(8,128)(2,1)S(1)}, u32[]{:S(2)}, u32[]{:S(2)}) collective-permute-start(bf16[2,2,64,1024]{3,2,1,0:T(8,128)(2,1)S(1)} %collective-permute-done.6.refs_4_.refs_6_.refs_9_), channel_id=1, source_target_pairs={{0,2},{1,3},{2,4},{3,5},{4,6},{5,7},{6,8},{7,9},{8,10},{9,11},{10,... | collective-permute-start | bytes 1572872 | tf_op jit(solution)/shard_map/ppermute | solution.py:27
  31.7 7.0 %collective-permute-start.7 = (bf16[2,2,64,1024]{3,2,1,0:T(8,128)(2,1)S(1)}, bf16[2,2,64,1024]{3,2,1,0:T(8,128)(2,1)S(1)}, u32[]{:S(2)}, u32[]{:S(2)}) collective-permute-start(bf16[2,2,64,1024]{3,2,1,0:T(8,128)(2,1)S(1)} %collective-permute-done.6.refs_4_.refs_6_.refs_9_), channel_id=1, source_target_pairs={{0,16},{1,17},{2,18},{3,19},{4,20},{5,21},{6,22},{7,23},{8,24},{9,... | collective-permute-start | bytes 1572872 | tf_op jit(solution)/shard_map/ppermute | solution.py:27
  35.1 10.4 %collective-permute-start.5 = (bf16[2,2,64,1024]{3,2,1,0:T(8,128)(2,1)S(1)}, bf16[2,2,64,1024]{3,2,1,0:T(8,128)(2,1)S(1)}, u32[]{:S(2)}, u32[]{:S(2)}) collective-permute-start(bf16[2,2,64,1024]{3,2,1,0:T(8,128)(2,1)S(1)} %collective-permute-done.2.refs_4_.refs_0_.refs_3_), channel_id=1, source_target_pairs={{0,2},{1,3},{2,4},{3,5},{4,6},{5,7},{6,8},{7,9},{8,10},{9,11},{10,... | collective-permute-start | bytes 1572872 | tf_op jit(solution)/shard_map/ppermute | solution.py:27
  39.4 8.1 %collective-permute-start.9 = (bf16[3,2,128,128]{3,2,1,0:T(8,128)(2,1)S(1)}, bf16[3,2,128,128]{3,2,1,0:T(8,128)(2,1)S(1)}, u32[]{:S(2)}, u32[]{:S(2)}) collective-permute-start(bf16[3,2,128,128]{3,2,1,0:T(8,128)(2,1)S(1)} %shard_map.43), channel_id=1, source_target_pairs={{0,33},{1,0},{2,35},{3,2},{4,37},{5,4},{6,39},{7,6},{8,41},{9,8},{... | collective-permute-start | bytes 589832 | tf_op jit(solution)/shard_map/ppermute | solution.py:27
  39.5 9.1 %collective-permute-start.13 = (bf16[2,2,64,1024]{3,2,1,0:T(8,128)(2,1)S(1)}, bf16[2,2,64,1024]{3,2,1,0:T(8,128)(2,1)S(1)}, u32[]{:S(2)}, u32[]{:S(2)}) collective-permute-start(bf16[2,2,64,1024]{3,2,1,0:T(8,128)(2,1)S(1)} %collective-permute-done.2.refs_4_.refs_0_.refs_3_), channel_id=1, source_target_pairs={{0,16},{1,17},{2,18},{3,19},{4,20},{5,21},{6,22},{7,23},{8,24},{9,... | collective-permute-start | bytes 1572872 | tf_op jit(solution)/shard_map/ppermute | solution.py:27
  40.8 7.8 %collective-permute-start.12 = (bf16[2,2,64,1024]{3,2,1,0:T(8,128)(2,1)S(1)}, bf16[2,2,64,1024]{3,2,1,0:T(8,128)(2,1)S(1)}, u32[]{:S(2)}, u32[]{:S(2)}) collective-permute-start(bf16[2,2,64,1024]{3,2,1,0:T(8,128)(2,1)S(1)} %collective-permute-done.10.refs_8_.refs_2_.refs_11_), channel_id=1, source_target_pairs={{0,16},{1,17},{2,18},{3,19},{4,20},{5,21},{6,22},{7,23},{8,24},{9,... | collective-permute-start | bytes 1572872 | tf_op jit(solution)/shard_map/ppermute | solution.py:27
  41.7 11.6 %collective-permute-start.11 = (bf16[2,2,64,1024]{3,2,1,0:T(8,128)(2,1)S(1)}, bf16[2,2,64,1024]{3,2,1,0:T(8,128)(2,1)S(1)}, u32[]{:S(2)}, u32[]{:S(2)}) collective-permute-start(bf16[2,2,64,1024]{3,2,1,0:T(8,128)(2,1)S(1)} %collective-permute-done.10.refs_8_.refs_2_.refs_11_), channel_id=1, source_target_pairs={{0,2},{1,3},{2,4},{3,5},{4,6},{5,7},{6,8},{7,9},{8,10},{9,11},{10,... | collective-permute-start | bytes 1572872 | tf_op jit(solution)/shard_map/ppermute | solution.py:27
  47.6 10.0 %collective-permute-start.16 = (bf16[2,2,64,1024]{3,2,1,0:T(8,128)(2,1)S(1)}, bf16[2,2,64,1024]{3,2,1,0:T(8,128)(2,1)S(1)}, u32[]{:S(2)}, u32[]{:S(2)}) collective-permute-start(bf16[2,2,64,1024]{3,2,1,0:T(8,128)(2,1)S(1)} %collective-permute-done.5.refs_2_.refs_5_.refs_0_), channel_id=1, source_target_pairs={{0,2},{1,3},{2,4},{3,5},{4,6},{5,7},{6,8},{7,9},{8,10},{9,11},{10,... | collective-permute-start | bytes 1572872 | tf_op jit(solution)/shard_map/ppermute | solution.py:27
  49.2 8.3 %collective-permute-start.17 = (bf16[2,2,128,128]{3,2,1,0:T(8,128)(2,1)S(1)}, bf16[2,2,128,128]{3,2,1,0:T(8,128)(2,1)S(1)}, u32[]{:S(2)}, u32[]{:S(2)}) collective-permute-start(bf16[2,2,128,128]{3,2,1,0:T(8,128)(2,1)S(1)} %shard_map.46), channel_id=1, source_target_pairs={{0,33},{1,0},{2,35},{3,2},{4,37},{5,4},{6,39},{7,6},{8,41},{9,8},{... | collective-permute-start | bytes 393224 | tf_op jit(solution)/shard_map/ppermute | solution.py:27
  50.5 8.0 %collective-permute-start.15 = (bf16[2,2,64,1024]{3,2,1,0:T(8,128)(2,1)S(1)}, bf16[2,2,64,1024]{3,2,1,0:T(8,128)(2,1)S(1)}, u32[]{:S(2)}, u32[]{:S(2)}) collective-permute-start(bf16[2,2,64,1024]{3,2,1,0:T(8,128)(2,1)S(1)} %collective-permute-done.5.refs_2_.refs_5_.refs_0_), channel_id=1, source_target_pairs={{0,16},{1,17},{2,18},{3,19},{4,20},{5,21},{6,22},{7,23},{8,24},{9,... | collective-permute-start | bytes 1572872 | tf_op jit(solution)/shard_map/ppermute | solution.py:27
  53.3 5.2 %collective-permute-start.14 = (bf16[2,2,64,1024]{3,2,1,0:T(8,128)(2,1)S(1)}, bf16[2,2,64,1024]{3,2,1,0:T(8,128)(2,1)S(1)}, u32[]{:S(2)}, u32[]{:S(2)}) collective-permute-start(bf16[2,2,64,1024]{3,2,1,0:T(8,128)(2,1)S(1)} %collective-permute-done.11.refs_4_.refs_13_.refs_3_), channel_id=1, source_target_pairs={{0,16},{1,17},{2,18},{3,19},{4,20},{5,21},{6,22},{7,23},{8,24},{9,... | collective-permute-start | bytes 1572872 | tf_op jit(solution)/shard_map/ppermute | solution.py:27
  57.6 2.5 %collective-permute-start.18 = (bf16[2,2,64,1024]{3,2,1,0:T(8,128)(2,1)S(1)}, bf16[2,2,64,1024]{3,2,1,0:T(8,128)(2,1)S(1)}, u32[]{:S(2)}, u32[]{:S(2)}) collective-permute-start(bf16[2,2,64,1024]{3,2,1,0:T(8,128)(2,1)S(1)} %collective-permute-done.16.refs_7_.refs_2_), channel_id=1, source_target_pairs={{0,16},{1,17},{2,18},{3,19},{4,20},{5,21},{6,22},{7,23},{8,24},{9,... | collective-permute-start | bytes 1572872 | tf_op jit(solution)/shard_map/ppermute | solution.py:27
  60.7 10.1 %collective-permute-start.19 = (bf16[3,2,128,128]{3,2,1,0:T(8,128)(2,1)S(1)}, bf16[3,2,128,128]{3,2,1,0:T(8,128)(2,1)S(1)}, u32[]{:S(2)}, u32[]{:S(2)}) collective-permute-start(bf16[3,2,128,128]{3,2,1,0:T(8,128)(2,1)S(1)} %shard_map.48), channel_id=1, source_target_pairs={{0,33},{1,0},{2,35},{3,2},{4,37},{5,4},{6,39},{7,6},{8,41},{9,8},{... | collective-permute-start | bytes 589832 | tf_op jit(solution)/shard_map/ppermute | solution.py:27
  64.4 13.5 %collective-permute-start.22 = (bf16[2,64,1024]{2,1,0:T(8,128)(2,1)S(1)}, bf16[2,64,1024]{2,1,0:T(8,128)(2,1)S(1)}, u32[]{:S(2)}, u32[]{:S(2)}) collective-permute-start(bf16[2,64,1024]{2,1,0:T(8,128)(2,1)S(1)} %get-tuple-element.30), channel_id=1, source_target_pairs={{0,128},{1,112},{2,130},{3,114},{4,132},{5,116},{6,134},{7,118},{8... | collective-permute-start | bytes 786440 | tf_op jit(solution)/shard_map/ppermute | solution.py:27
  68.3 15.9 %collective-permute-start.24 = (bf16[2,64,1024]{2,1,0:T(8,128)(2,1)S(1)}, bf16[2,64,1024]{2,1,0:T(8,128)(2,1)S(1)}, u32[]{:S(2)}, u32[]{:S(2)}) collective-permute-start(bf16[2,64,1024]{2,1,0:T(8,128)(2,1)S(1)} %get-tuple-element.33), channel_id=1, source_target_pairs={{0,129},{1,113},{2,131},{3,115},{4,133},{5,117},{6,135},{7,119},{8... | collective-permute-start | bytes 786440 | tf_op jit(solution)/shard_map/ppermute | solution.py:27
  71.6 2.7 %collective-permute-start.20 = (f32[1,128]{1,0:T(1,128)S(1)}, f32[1,128]{1,0:T(1,128)S(1)}, u32[]{:S(2)}, u32[]{:S(2)}) collective-permute-start(f32[1,128]{1,0:T(1,128)S(1)} %shard_map.49), channel_id=1, source_target_pairs={{0,2},{1,3},{2,0},{3,1},{4,6},{5,7},{6,4},{7,5},{8,10},{9,11},{10,... | collective-permute-start | bytes 1544 | tf_op jit(solution)/shard_map/ppermute | solution.py:27
  74.3 3.6 %collective-permute-start.21 = (f32[1,128]{1,0:T(1,128)S(1)}, f32[1,128]{1,0:T(1,128)S(1)}, u32[]{:S(2)}, u32[]{:S(2)}) collective-permute-start(f32[1,128]{1,0:T(1,128)S(1)} %add.24), channel_id=1, source_target_pairs={{0,4},{1,5},{2,6},{3,7},{4,0},{5,1},{6,2},{7,3},{8,12},{9,13},{10,... | collective-permute-start | bytes 1544 | tf_op jit(solution)/shard_map/ppermute | solution.py:27
  77.9 6.3 %collective-permute-start.23 = (f32[1,128]{1,0:T(1,128)S(1)}, f32[1,128]{1,0:T(1,128)S(1)}, u32[]{:S(2)}, u32[]{:S(2)}) collective-permute-start(f32[1,128]{1,0:T(1,128)S(1)} %add.25), channel_id=1, source_target_pairs={{0,8},{1,9},{2,10},{3,11},{4,12},{5,13},{6,14},{7,15},{8,0},{9,1},... | collective-permute-start | bytes 1544 | tf_op jit(solution)/shard_map/ppermute | solution.py:27
  84.2 9.9 %collective-permute-start.26 = (f32[1,128]{1,0:T(1,128)S(1)}, f32[1,128]{1,0:T(1,128)S(1)}, u32[]{:S(2)}, u32[]{:S(2)}) collective-permute-start(f32[1,128]{1,0:T(1,128)S(1)} %add.26), channel_id=1, source_target_pairs={{0,129},{1,113},{2,131},{3,115},{4,133},{5,117},{6,135},{7,119},{8... | collective-permute-start | bytes 1544 | tf_op jit(solution)/shard_map/ppermute | solution.py:27
  86.8 7.3 %collective-permute-start.25 = (f32[1,128]{1,0:T(1,128)S(1)}, f32[1,128]{1,0:T(1,128)S(1)}, u32[]{:S(2)}, u32[]{:S(2)}) collective-permute-start(f32[1,128]{1,0:T(1,128)S(1)} %add.26), channel_id=1, source_target_pairs={{0,128},{1,112},{2,130},{3,114},{4,132},{5,116},{6,134},{7,118},{8... | collective-permute-start | bytes 1544 | tf_op jit(solution)/shard_map/ppermute | solution.py:27

commit v14 on v13

--- a/solution.py
+++ b/solution.py
@@ -31,8 +31,8 @@
     return (m, c, z + (1 if c == 0 else -1), h)
 
 
-def across(distance):
-    return lambda m, c, z, h: (m, c, z ^ distance, h)
+def along(step):
+    return lambda m, c, z, h: (m, c, z + step, h)
 
 
 def other_core(m, c, z, h):
@@ -238,14 +238,13 @@
     trace = call(trace_kernel, info, [product, early, late], jax.ShapeDtypeStruct((1, 128), F32), WEIGHT)
 
     kept, sent = moved(keep, from_hub(0)), moved(send, from_hub(1))
-    trace = trace + moved(trace, across(1))
-    trace = trace + moved(trace, across(2))
-    trace, kept = wall((trace, kept))
-    trace = trace + moved(trace, across(4))
-    trace, sent = wall((trace, sent))
     first, second = moved(trace, from_hub(0)), moved(trace, from_hub(1))
+    both = jnp.where(half == 0, jnp.concatenate([first, second]), jnp.concatenate([second, first]))
+    below, above = moved(both, along(1)), moved(both, along(-1))
+    two, three, kept = wall((both + above, below + both + above, kept))
+    below, above = moved(two, along(3)), moved(three, along(-3))
+    both = below + three + above
     products = jnp.where(half == 0, jnp.stack([kept, sent]), jnp.stack([sent, kept]))[:, None, None]
-    both = jnp.where(half == 0, jnp.concatenate([first, second]), jnp.concatenate([second, first]))
     correlator = jnp.sum(both[:, :16].reshape(2, 8, 2), axis=1)[:, None, None, :] / F32(1024)
     return products, correlator
 

time: 94.9 us -> 94.5 us (level)
  the two profiles are of different devices: /device:TPU:1 before, /device:TPU:38 now
where the time goes in v14:
time: 94.5 us; the launch traced here: 94.4 us
  starting transfers between devices  45.5 us (48%)
  waiting for transfers between devices  37.7 us (40%)
  Pallas kernels  8.8 us (9%)
  other arithmetic  1.56 us (2%)
    ppermute x28, starting transfers between devices, moved(): lax.ppermute(block, BOTH, [(index_of(*at), index_of(*route(*at))) for at...  45.5 us
    ppermute x28, waiting for transfers between devices, moved(): lax.ppermute(block, BOTH, [(index_of(*at), index_of(*route(*at))) for at...  37.7 us
    pallas_call x9, Pallas kernels, call(): pl.pallas_call(kernel, out_shape=out_shape, in_specs=[SMEM] + [VMEM] * le...  8.8 us
  transfers between devices with their start and end apart: 28, of which 16 were waited for; matrix products, arithmetic and copies ran while one was open for 1% of the time, Pallas kernels for 8%

profile of v14, /device:TPU:38, one launch (start us, length us, event | category | flops | bytes accessed | tf_op | source)
XLA Modules:
  0.0 94.4 jit_solution(1608242031685786676)
XLA Ops:
  0.6 0.0 copy-start
  0.6 1.7 %collective-permute-start = (bf16[2,2,64,1024]{3,2,1,0:T(8,128)(2,1)}, bf16[2,2,64,1024]{3,2,1,0:T(8,128)(2,1)S(1)}, u32[]{:S(2)}, u32[]{:S(2)}) collective-permute-start(bf16[2,2,64,1024]{3,2,1,0:T(8,128)(2,1)} %bitcast.15), channel_id=1, source_target_pairs={{0,128},{1,144},{2,130},{3,146},{4,132},{5,148},{6,134},{7,150},{8... | collective-permute-start | bytes 1572872 | tf_op jit(solution)/shard_map/ppermute | solution.py:27
  2.3 7.2 %collective-permute-done.own.refs_2_.refs_0_ = bf16[2,2,64,1024]{3,2,1,0:T(8,128)(2,1)S(1)} collective-permute-done((bf16[2,2,64,1024]{3,2,1,0:T(8,128)(2,1)}, bf16[2,2,64,1024]{3,2,1,0:T(8,128)(2,1)S(1)}, u32[]{:S(2)}, u32[]{:S(2)}) %collective-permute-start) | collective-permute-done | bytes 524320 | tf_op jit(solution)/shard_map/ppermute | solution.py:27
  9.5 0.8 collective-permute-start.3
  10.3 1.9 %collective-permute-start.1 = (bf16[2,2,64,1024]{3,2,1,0:T(8,128)(2,1)S(1)}, bf16[2,2,64,1024]{3,2,1,0:T(8,128)(2,1)S(1)}, u32[]{:S(2)}, u32[]{:S(2)}) collective-permute-start(bf16[2,2,64,1024]{3,2,1,0:T(8,128)(2,1)S(1)} %collective-permute-done.own.refs_2_.refs_0_), channel_id=1, source_target_pairs={{0,2},{1,3},{2,4},{3,5},{4,6},{5,7},{6,8},{7,9},{8,10},{9,11},{10,... | collective-permute-start | bytes 1572872 | tf_op jit(solution)/shard_map/ppermute | solution.py:27
  12.2 0.0 collective-permute-done.3.other.refs_3_.refs_8_
  12.2 2.0 %collective-permute-start.6 = (bf16[2,2,64,1024]{3,2,1,0:T(8,128)(2,1)S(1)}, bf16[2,2,64,1024]{3,2,1,0:T(8,128)(2,1)S(1)}, u32[]{:S(2)}, u32[]{:S(2)}) collective-permute-start(bf16[2,2,64,1024]{3,2,1,0:T(8,128)(2,1)S(1)} %collective-permute-done.3.other.refs_3_.refs_8_), channel_id=1, source_target_pairs={{0,2},{1,3},{2,4},{3,5},{4,6},{5,7},{6,8},{7,9},{8,10},{9,11},{10,... | collective-permute-start | bytes 1572872 | tf_op jit(solution)/shard_map/ppermute | solution.py:27
  14.2 0.1 pad_add_fusion.info.refs_0_
  14.3 0.6 shard_map.41
  14.9 1.4 %collective-permute-start.4 = (bf16[2,128,1024]{2,1,0:T(8,128)(2,1)S(1)}, bf16[2,128,1024]{2,1,0:T(8,128)(2,1)S(1)}, u32[]{:S(2)}, u32[]{:S(2)}) collective-permute-start(bf16[2,128,1024]{2,1,0:T(8,128)(2,1)S(1)} %shard_map.41), channel_id=1, source_target_pairs={{0,33},{1,0},{2,35},{3,2},{4,37},{5,4},{6,39},{7,6},{8,41},{9,8},{... | collective-permute-start | bytes 1572872 | tf_op jit(solution)/shard_map/ppermute | solution.py:27
  16.3 3.2 %collective-permute-done.1.refs_1_.refs_2_ = bf16[2,2,64,1024]{3,2,1,0:T(8,128)(2,1)S(1)} collective-permute-done((bf16[2,2,64,1024]{3,2,1,0:T(8,128)(2,1)S(1)}, bf16[2,2,64,1024]{3,2,1,0:T(8,128)(2,1)S(1)}, u32[]{:S(2)}, u32[]{:S(2)}) %collective-permute-start.1) | collective-permute-done | bytes 524320 | tf_op jit(solution)/shard_map/ppermute | solution.py:27
  19.5 1.9 %collective-permute-start.2 = (bf16[2,2,64,1024]{3,2,1,0:T(8,128)(2,1)S(1)}, bf16[2,2,64,1024]{3,2,1,0:T(8,128)(2,1)S(1)}, u32[]{:S(2)}, u32[]{:S(2)}) collective-permute-start(bf16[2,2,64,1024]{3,2,1,0:T(8,128)(2,1)S(1)} %collective-permute-done.1.refs_1_.refs_2_), channel_id=1, source_target_pairs={{0,2},{1,3},{2,4},{3,5},{4,6},{5,7},{6,8},{7,9},{8,10},{9,11},{10,... | collective-permute-start | bytes 1572872 | tf_op jit(solution)/shard_map/ppermute | solution.py:27
  21.4 0.4 collective-permute-start.8
  21.8 3.3 %collective-permute-done.6.refs_4_.refs_6_.refs_9_ = bf16[2,2,64,1024]{3,2,1,0:T(8,128)(2,1)S(1)} collective-permute-done((bf16[2,2,64,1024]{3,2,1,0:T(8,128)(2,1)S(1)}, bf16[2,2,64,1024]{3,2,1,0:T(8,128)(2,1)S(1)}, u32[]{:S(2)}, u32[]{:S(2)}) %collective-permute-start.6) | collective-permute-done | bytes 524320 | tf_op jit(solution)/shard_map/ppermute | solution.py:27
  25.1 1.9 %collective-permute-start.10 = (bf16[2,2,64,1024]{3,2,1,0:T(8,128)(2,1)S(1)}, bf16[2,2,64,1024]{3,2,1,0:T(8,128)(2,1)S(1)}, u32[]{:S(2)}, u32[]{:S(2)}) collective-permute-start(bf16[2,2,64,1024]{3,2,1,0:T(8,128)(2,1)S(1)} %collective-permute-done.6.refs_4_.refs_6_.refs_9_), channel_id=1, source_target_pairs={{0,2},{1,3},{2,4},{3,5},{4,6},{5,7},{6,8},{7,9},{8,10},{9,11},{10,... | collective-permute-start | bytes 1572872 | tf_op jit(solution)/shard_map/ppermute | solution.py:27
  27.0 0.4 collective-permute-start.7
  27.4 0.0 collective-permute-done.4.refs_1_.a_ref
  27.4 0.8 shard_map.42.refs_10_
  28.3 2.4 %collective-permute-done.2.refs_4_.refs_0_.refs_3_ = bf16[2,2,64,1024]{3,2,1,0:T(8,128)(2,1)S(1)} collective-permute-done((bf16[2,2,64,1024]{3,2,1,0:T(8,128)(2,1)S(1)}, bf16[2,2,64,1024]{3,2,1,0:T(8,128)(2,1)S(1)}, u32[]{:S(2)}, u32[]{:S(2)}) %collective-permute-start.2) | collective-permute-done | bytes 524320 | tf_op jit(solution)/shard_map/ppermute | solution.py:27
  30.7 1.9 %collective-permute-start.5 = (bf16[2,2,64,1024]{3,2,1,0:T(8,128)(2,1)S(1)}, bf16[2,2,64,1024]{3,2,1,0:T(8,128)(2,1)S(1)}, u32[]{:S(2)}, u32[]{:S(2)}) collective-permute-start(bf16[2,2,64,1024]{3,2,1,0:T(8,128)(2,1)S(1)} %collective-permute-done.2.refs_4_.refs_0_.refs_3_), channel_id=1, source_target_pairs={{0,2},{1,3},{2,4},{3,5},{4,6},{5,7},{6,8},{7,9},{8,10},{9,11},{10,... | collective-permute-start | bytes 1572872 | tf_op jit(solution)/shard_map/ppermute | solution.py:27
  32.6 0.0 collective-permute-done.8.refs_5_.refs_7_.refs_10_
  32.6 0.0 collective-permute-done.7.refs_2_.refs_3_
  32.6 0.7 shard_map.43
  33.3 2.7 %collective-permute-start.9 = (bf16[3,2,128,128]{3,2,1,0:T(8,128)(2,1)S(1)}, bf16[3,2,128,128]{3,2,1,0:T(8,128)(2,1)S(1)}, u32[]{:S(2)}, u32[]{:S(2)}) collective-permute-start(bf16[3,2,128,128]{3,2,1,0:T(8,128)(2,1)S(1)} %shard_map.43), channel_id=1, source_target_pairs={{0,33},{1,0},{2,35},{3,2},{4,37},{5,4},{6,39},{7,6},{8,41},{9,8},{... | collective-permute-start | bytes 589832 | tf_op jit(solution)/shard_map/ppermute | solution.py:27
  36.0 1.4 %collective-permute-start.13 = (bf16[2,2,64,1024]{3,2,1,0:T(8,128)(2,1)S(1)}, bf16[2,2,64,1024]{3,2,1,0:T(8,128)(2,1)S(1)}, u32[]{:S(2)}, u32[]{:S(2)}) collective-permute-start(bf16[2,2,64,1024]{3,2,1,0:T(8,128)(2,1)S(1)} %collective-permute-done.2.refs_4_.refs_0_.refs_3_), channel_id=1, source_target_pairs={{0,16},{1,17},{2,18},{3,19},{4,20},{5,21},{6,22},{7,23},{8,24},{9,... | collective-permute-start | bytes 1572872 | tf_op jit(solution)/shard_map/ppermute | solution.py:27
  37.4 0.0 collective-permute-done.10.refs_8_.refs_2_.refs_11_
  37.4 0.0 collective-permute-start.12
  37.5 1.0 %collective-permute-start.11 = (bf16[2,2,64,1024]{3,2,1,0:T(8,128)(2,1)S(1)}, bf16[2,2,64,1024]{3,2,1,0:T(8,128)(2,1)S(1)}, u32[]{:S(2)}, u32[]{:S(2)}) collective-permute-start(bf16[2,2,64,1024]{3,2,1,0:T(8,128)(2,1)S(1)} %collective-permute-done.10.refs_8_.refs_2_.refs_11_), channel_id=1, source_target_pairs={{0,2},{1,3},{2,4},{3,5},{4,6},{5,7},{6,8},{7,9},{8,10},{9,11},{10,... | collective-permute-start | bytes 1572872 | tf_op jit(solution)/shard_map/ppermute | solution.py:27
  38.5 3.5 %collective-permute-done.5.refs_2_.refs_5_.refs_0_ = bf16[2,2,64,1024]{3,2,1,0:T(8,128)(2,1)S(1)} collective-permute-done((bf16[2,2,64,1024]{3,2,1,0:T(8,128)(2,1)S(1)}, bf16[2,2,64,1024]{3,2,1,0:T(8,128)(2,1)S(1)}, u32[]{:S(2)}, u32[]{:S(2)}) %collective-permute-start.5) | collective-permute-done | bytes 524320 | tf_op jit(solution)/shard_map/ppermute | solution.py:27
  41.9 0.0 collective-permute-done.9.near
  42.0 1.9 %collective-permute-start.16 = (bf16[2,2,64,1024]{3,2,1,0:T(8,128)(2,1)S(1)}, bf16[2,2,64,1024]{3,2,1,0:T(8,128)(2,1)S(1)}, u32[]{:S(2)}, u32[]{:S(2)}) collective-permute-start(bf16[2,2,64,1024]{3,2,1,0:T(8,128)(2,1)S(1)} %collective-permute-done.5.refs_2_.refs_5_.refs_0_), channel_id=1, source_target_pairs={{0,2},{1,3},{2,4},{3,5},{4,6},{5,7},{6,8},{7,9},{8,10},{9,11},{10,... | collective-permute-start | bytes 1572872 | tf_op jit(solution)/shard_map/ppermute | solution.py:27
  43.9 0.0 collective-permute-done.13.refs_9_.refs_3_.refs_12_
  43.9 0.0 collective-permute-done.12.refs_5_.refs_1_.refs_4_
  43.9 0.6 shard_map.46
  44.5 3.0 %collective-permute-start.17 = (bf16[2,2,128,128]{3,2,1,0:T(8,128)(2,1)S(1)}, bf16[2,2,128,128]{3,2,1,0:T(8,128)(2,1)S(1)}, u32[]{:S(2)}, u32[]{:S(2)}) collective-permute-start(bf16[2,2,128,128]{3,2,1,0:T(8,128)(2,1)S(1)} %shard_map.46), channel_id=1, source_target_pairs={{0,33},{1,0},{2,35},{3,2},{4,37},{5,4},{6,39},{7,6},{8,41},{9,8},{... | collective-permute-start | bytes 393224 | tf_op jit(solution)/shard_map/ppermute | solution.py:27
  47.6 1.6 %collective-permute-start.15 = (bf16[2,2,64,1024]{3,2,1,0:T(8,128)(2,1)S(1)}, bf16[2,2,64,1024]{3,2,1,0:T(8,128)(2,1)S(1)}, u32[]{:S(2)}, u32[]{:S(2)}) collective-permute-start(bf16[2,2,64,1024]{3,2,1,0:T(8,128)(2,1)S(1)} %collective-permute-done.5.refs_2_.refs_5_.refs_0_), channel_id=1, source_target_pairs={{0,16},{1,17},{2,18},{3,19},{4,20},{5,21},{6,22},{7,23},{8,24},{9,... | collective-permute-start | bytes 1572872 | tf_op jit(solution)/shard_map/ppermute | solution.py:27
  49.1 1.3 %shard_map.44.refs_6_ = f32[256,1024]{1,0:T(8,128)S(1)} custom-call(s32[6]{0:T(128)S(1)} %pad_add_fusion.info.refs_0_, bf16[2,128,1024]{2,1,0:T(8,128)(2,1)S(1)} %collective-permute-done.4.refs_1_.a_ref, bf16[2,2,64,1024]{3,2,1,0:T(8,128)(2,1)S(1)} %collective-permute-done.1.refs_1_.refs_2_, ...), custom_call_target="tpu_custom_call" | custom-call | flops 1 | bytes 1048576 | tf_op jit(solution)/shard_map/pallas_call | solution.py:75
  50.4 0.1 collective-permute-start.14
  50.5 0.5 collective-permute-done.17.middle
  51.1 2.5 %collective-permute-done.16.refs_7_.refs_2_ = bf16[2,2,64,1024]{3,2,1,0:T(8,128)(2,1)S(1)} collective-permute-done((bf16[2,2,64,1024]{3,2,1,0:T(8,128)(2,1)S(1)}, bf16[2,2,64,1024]{3,2,1,0:T(8,128)(2,1)S(1)}, u32[]{:S(2)}, u32[]{:S(2)}) %collective-permute-start.16) | collective-permute-done | bytes 524320 | tf_op jit(solution)/shard_map/ppermute | solution.py:27
  53.6 1.0 %shard_map.45.acc = f32[256,1024]{1,0:T(8,128)S(1)} custom-call(s32[6]{0:T(128)S(1)} %pad_add_fusion.info.refs_0_, bf16[2,128,1024]{2,1,0:T(8,128)(2,1)S(1)} %collective-permute-done.4.refs_1_.a_ref, bf16[2,2,64,1024]{3,2,1,0:T(8,128)(2,1)S(1)} %collective-permute-done.5.refs_2_.refs_5_.refs_0_, ...), custom_call_target="tpu_custom_call" | custom-call | flops 1 | bytes 1048576 | tf_op jit(solution)/shard_map/pallas_call | solution.py:75
  54.6 0.9 collective-permute-done.18.refs_15_.refs_5_
  55.5 0.7 shard_map.48
  56.2 1.7 %collective-permute-start.19 = (bf16[3,2,128,128]{3,2,1,0:T(8,128)(2,1)S(1)}, bf16[3,2,128,128]{3,2,1,0:T(8,128)(2,1)S(1)}, u32[]{:S(2)}, u32[]{:S(2)}) collective-permute-start(bf16[3,2,128,128]{3,2,1,0:T(8,128)(2,1)S(1)} %shard_map.48), channel_id=1, source_target_pairs={{0,33},{1,0},{2,35},{3,2},{4,37},{5,4},{6,39},{7,6},{8,41},{9,8},{... | collective-permute-start | bytes 589832 | tf_op jit(solution)/shard_map/ppermute | solution.py:27
  57.9 2.3 %shard_map.47 = (bf16[2,64,1024]{2,1,0:T(8,128)(2,1)S(1)}, bf16[2,64,1024]{2,1,0:T(8,128)(2,1)S(1)}, f32[256,1024]{1,0:T(8,128)S(1)}, f32[8,128]{1,0:T(8,128)S(1)}) custom-call(s32[6]{0:T(128)S(1)} %pad_add_fusion.info.refs_0_, bf16[2,128,1024]{2,1,0:T(8,128)(2,1)S(1)} %collective-permute-done.4.refs_1_.a_ref, f32[256,1024]{1,0:T(8,128)S(1)} %shard_map.45.acc, ...), custom_call_target="tpu_custom_call" | custom-call | flops 3000000000 | bytes 1048576 | tf_op jit(solution)/shard_map/pallas_call | solution.py:75
  60.2 3.2 %collective-permute-done.19.late = bf16[3,2,128,128]{3,2,1,0:T(8,128)(2,1)S(1)} collective-permute-done((bf16[3,2,128,128]{3,2,1,0:T(8,128)(2,1)S(1)}, bf16[3,2,128,128]{3,2,1,0:T(8,128)(2,1)S(1)}, u32[]{:S(2)}, u32[]{:S(2)}) %collective-permute-start.19) | collective-permute-done | bytes 196640 | tf_op jit(solution)/shard_map/ppermute | solution.py:27
  63.5 0.7 shard_map.49
  64.2 3.0 %collective-permute-start.21 = (f32[1,128]{1,0:T(1,128)S(1)}, f32[1,128]{1,0:T(1,128)S(1)}, u32[]{:S(2)}, u32[]{:S(2)}) collective-permute-start(f32[1,128]{1,0:T(1,128)S(1)} %shard_map.49), channel_id=1, source_target_pairs={{0,129},{1,113},{2,131},{3,115},{4,133},{5,117},{6,135},{7,119},{8... | collective-permute-start | bytes 1544 | tf_op jit(solution)/shard_map/ppermute | solution.py:27
  67.3 0.2 collective-permute-start.20
  67.4 0.1 collective-permute-start.24
  67.5 3.1 %collective-permute-start.25 = (bf16[2,64,1024]{2,1,0:T(8,128)(2,1)S(1)}, bf16[2,64,1024]{2,1,0:T(8,128)(2,1)S(1)}, u32[]{:S(2)}, u32[]{:S(2)}) collective-permute-start(bf16[2,64,1024]{2,1,0:T(8,128)(2,1)S(1)} %get-tuple-element.31), channel_id=1, source_target_pairs={{0,129},{1,113},{2,131},{3,115},{4,133},{5,117},{6,135},{7,119},{8... | collective-permute-start | bytes 786440 | tf_op jit(solution)/shard_map/ppermute | solution.py:27
  70.7 0.1 collective-permute-done.21
  70.8 1.2 %collective-permute-done.20 = f32[1,128]{1,0:T(1,128)S(1)} collective-permute-done((f32[1,128]{1,0:T(1,128)S(1)}, f32[1,128]{1,0:T(1,128)S(1)}, u32[]{:S(2)}, u32[]{:S(2)}) %collective-permute-start.20) | collective-permute-done | bytes 544 | tf_op jit(solution)/shard_map/ppermute | solution.py:27
  72.0 2.0 %collective-permute-start.23 = (f32[2,128]{1,0:T(2,128)S(1)}, f32[2,128]{1,0:T(2,128)S(1)}, u32[]{:S(2)}, u32[]{:S(2)}) collective-permute-start(f32[2,128]{1,0:T(2,128)S(1)} %maximum_select_fusion.1), channel_id=1, source_target_pairs={{0,2},{1,3},{2,4},{3,5},{4,6},{5,7},{6,8},{7,9},{8,10},{9,11},{10,... | collective-permute-start | bytes 3080 | tf_op jit(solution)/shard_map/ppermute | solution.py:27
  74.0 2.1 %collective-permute-start.22 = (f32[2,128]{1,0:T(2,128)S(1)}, f32[2,128]{1,0:T(2,128)S(1)}, u32[]{:S(2)}, u32[]{:S(2)}) collective-permute-start(f32[2,128]{1,0:T(2,128)S(1)} %maximum_select_fusion.1), channel_id=1, source_target_pairs={{0,14},{1,15},{2,0},{3,1},{4,2},{5,3},{6,4},{7,5},{8,6},{9,7},{10,... | collective-permute-start | bytes 3080 | tf_op jit(solution)/shard_map/ppermute | solution.py:27
  76.1 1.5 %collective-permute-done.23 = f32[2,128]{1,0:T(2,128)S(1)} collective-permute-done((f32[2,128]{1,0:T(2,128)S(1)}, f32[2,128]{1,0:T(2,128)S(1)}, u32[]{:S(2)}, u32[]{:S(2)}) %collective-permute-start.23) | collective-permute-done | bytes 1056 | tf_op jit(solution)/shard_map/ppermute | solution.py:27
  77.6 0.5 collective-permute-done.22
  78.1 1.8 %collective-permute-done.24 = bf16[2,64,1024]{2,1,0:T(8,128)(2,1)S(1)} collective-permute-done((bf16[2,64,1024]{2,1,0:T(8,128)(2,1)S(1)}, bf16[2,64,1024]{2,1,0:T(8,128)(2,1)S(1)}, u32[]{:S(2)}, u32[]{:S(2)}) %collective-permute-start.24) | collective-permute-done | bytes 262176 | tf_op jit(solution)/shard_map/ppermute | solution.py:27
  79.9 7.2 %collective-permute-start.26 = (f32[2,128]{1,0:T(2,128)S(1)}, f32[2,128]{1,0:T(2,128)S(1)}, u32[]{:S(2)}, u32[]{:S(2)}) collective-permute-start(f32[2,128]{1,0:T(2,128)S(1)} %get-tuple-element.32), channel_id=1, source_target_pairs={{0,6},{1,7},{2,8},{3,9},{4,10},{5,11},{6,12},{7,13},{8,14},{9,15},... | collective-permute-start | bytes 3080 | tf_op jit(solution)/shard_map/ppermute | solution.py:27
  87.2 0.9 maximum_select_fusion
  88.1 0.4 collective-permute-done.26
  88.5 5.3 %collective-permute-done.27 = f32[2,128]{1,0:T(2,128)S(1)} collective-permute-done((f32[2,128]{1,0:T(2,128)S(1)}, f32[2,128]{1,0:T(2,128)S(1)}, u32[]{:S(2)}, u32[]{:S(2)}) %collective-permute-start.27) | collective-permute-done | bytes 1056 | tf_op jit(solution)/shard_map/ppermute | solution.py:27
  93.8 0.1 reshape.77
  93.9 0.6 broadcast_multiply_fusion
  (12 shorter events, 0.1 us)
Async XLA Ops:
  0.6 11.6 %copy-start = (s32[2,1,4]{2,1,0:T(1,128)S(1)}, s32[2,1,4]{2,1,0:T(1,128)}, u32[]{:S(2)}) copy-start(s32[2,1,4]{2,1,0:T(1,128)} %param.3) | copy-start | bytes 100
  0.6 8.9 %collective-permute-start = (bf16[2,2,64,1024]{3,2,1,0:T(8,128)(2,1)}, bf16[2,2,64,1024]{3,2,1,0:T(8,128)(2,1)S(1)}, u32[]{:S(2)}, u32[]{:S(2)}) collective-permute-start(bf16[2,2,64,1024]{3,2,1,0:T(8,128)(2,1)} %bitcast.15), channel_id=1, source_target_pairs={{0,128},{1,144},{2,130},{3,146},{4,132},{5,148},{6,134},{7,150},{8... | collective-permute-start | bytes 1572872 | tf_op jit(solution)/shard_map/ppermute | solution.py:27
  9.5 2.7 %collective-permute-start.3 = (bf16[2,2,64,1024]{3,2,1,0:T(8,128)(2,1)S(1)}, bf16[2,2,64,1024]{3,2,1,0:T(8,128)(2,1)S(1)}, u32[]{:S(2)}, u32[]{:S(2)}) collective-permute-start(bf16[2,2,64,1024]{3,2,1,0:T(8,128)(2,1)S(1)} %collective-permute-done.own.refs_2_.refs_0_), channel_id=1, source_target_pairs={{0,16},{1,17},{2,18},{3,19},{4,20},{5,21},{6,22},{7,23},{8,24},{9,... | collective-permute-start | bytes 1572872 | tf_op jit(solution)/shard_map/ppermute | solution.py:27
  10.3 9.2 %collective-permute-start.1 = (bf16[2,2,64,1024]{3,2,1,0:T(8,128)(2,1)S(1)}, bf16[2,2,64,1024]{3,2,1,0:T(8,128)(2,1)S(1)}, u32[]{:S(2)}, u32[]{:S(2)}) collective-permute-start(bf16[2,2,64,1024]{3,2,1,0:T(8,128)(2,1)S(1)} %collective-permute-done.own.refs_2_.refs_0_), channel_id=1, source_target_pairs={{0,2},{1,3},{2,4},{3,5},{4,6},{5,7},{6,8},{7,9},{8,10},{9,11},{10,... | collective-permute-start | bytes 1572872 | tf_op jit(solution)/shard_map/ppermute | solution.py:27
  12.2 12.9 %collective-permute-start.6 = (bf16[2,2,64,1024]{3,2,1,0:T(8,128)(2,1)S(1)}, bf16[2,2,64,1024]{3,2,1,0:T(8,128)(2,1)S(1)}, u32[]{:S(2)}, u32[]{:S(2)}) collective-permute-start(bf16[2,2,64,1024]{3,2,1,0:T(8,128)(2,1)S(1)} %collective-permute-done.3.other.refs_3_.refs_8_), channel_id=1, source_target_pairs={{0,2},{1,3},{2,4},{3,5},{4,6},{5,7},{6,8},{7,9},{8,10},{9,11},{10,... | collective-permute-start | bytes 1572872 | tf_op jit(solution)/shard_map/ppermute | solution.py:27
  14.9 12.6 %collective-permute-start.4 = (bf16[2,128,1024]{2,1,0:T(8,128)(2,1)S(1)}, bf16[2,128,1024]{2,1,0:T(8,128)(2,1)S(1)}, u32[]{:S(2)}, u32[]{:S(2)}) collective-permute-start(bf16[2,128,1024]{2,1,0:T(8,128)(2,1)S(1)} %shard_map.41), channel_id=1, source_target_pairs={{0,33},{1,0},{2,35},{3,2},{4,37},{5,4},{6,39},{7,6},{8,41},{9,8},{... | collective-permute-start | bytes 1572872 | tf_op jit(solution)/shard_map/ppermute | solution.py:27
  19.5 11.2 %collective-permute-start.2 = (bf16[2,2,64,1024]{3,2,1,0:T(8,128)(2,1)S(1)}, bf16[2,2,64,1024]{3,2,1,0:T(8,128)(2,1)S(1)}, u32[]{:S(2)}, u32[]{:S(2)}) collective-permute-start(bf16[2,2,64,1024]{3,2,1,0:T(8,128)(2,1)S(1)} %collective-permute-done.1.refs_1_.refs_2_), channel_id=1, source_target_pairs={{0,2},{1,3},{2,4},{3,5},{4,6},{5,7},{6,8},{7,9},{8,10},{9,11},{10,... | collective-permute-start | bytes 1572872 | tf_op jit(solution)/shard_map/ppermute | solution.py:27
  21.4 11.2 %collective-permute-start.8 = (bf16[2,2,64,1024]{3,2,1,0:T(8,128)(2,1)S(1)}, bf16[2,2,64,1024]{3,2,1,0:T(8,128)(2,1)S(1)}, u32[]{:S(2)}, u32[]{:S(2)}) collective-permute-start(bf16[2,2,64,1024]{3,2,1,0:T(8,128)(2,1)S(1)} %collective-permute-done.1.refs_1_.refs_2_), channel_id=1, source_target_pairs={{0,16},{1,17},{2,18},{3,19},{4,20},{5,21},{6,22},{7,23},{8,24},{9,... | collective-permute-start | bytes 1572872 | tf_op jit(solution)/shard_map/ppermute | solution.py:27
  25.1 12.4 %collective-permute-start.10 = (bf16[2,2,64,1024]{3,2,1,0:T(8,128)(2,1)S(1)}, bf16[2,2,64,1024]{3,2,1,0:T(8,128)(2,1)S(1)}, u32[]{:S(2)}, u32[]{:S(2)}) collective-permute-start(bf16[2,2,64,1024]{3,2,1,0:T(8,128)(2,1)S(1)} %collective-permute-done.6.refs_4_.refs_6_.refs_9_), channel_id=1, source_target_pairs={{0,2},{1,3},{2,4},{3,5},{4,6},{5,7},{6,8},{7,9},{8,10},{9,11},{10,... | collective-permute-start | bytes 1572872 | tf_op jit(solution)/shard_map/ppermute | solution.py:27
  27.0 5.6 %collective-permute-start.7 = (bf16[2,2,64,1024]{3,2,1,0:T(8,128)(2,1)S(1)}, bf16[2,2,64,1024]{3,2,1,0:T(8,128)(2,1)S(1)}, u32[]{:S(2)}, u32[]{:S(2)}) collective-permute-start(bf16[2,2,64,1024]{3,2,1,0:T(8,128)(2,1)S(1)} %collective-permute-done.6.refs_4_.refs_6_.refs_9_), channel_id=1, source_target_pairs={{0,16},{1,17},{2,18},{3,19},{4,20},{5,21},{6,22},{7,23},{8,24},{9,... | collective-permute-start | bytes 1572872 | tf_op jit(solution)/shard_map/ppermute | solution.py:27
  30.7 11.2 %collective-permute-start.5 = (bf16[2,2,64,1024]{3,2,1,0:T(8,128)(2,1)S(1)}, bf16[2,2,64,1024]{3,2,1,0:T(8,128)(2,1)S(1)}, u32[]{:S(2)}, u32[]{:S(2)}) collective-permute-start(bf16[2,2,64,1024]{3,2,1,0:T(8,128)(2,1)S(1)} %collective-permute-done.2.refs_4_.refs_0_.refs_3_), channel_id=1, source_target_pairs={{0,2},{1,3},{2,4},{3,5},{4,6},{5,7},{6,8},{7,9},{8,10},{9,11},{10,... | collective-permute-start | bytes 1572872 | tf_op jit(solution)/shard_map/ppermute | solution.py:27
  33.3 8.6 %collective-permute-start.9 = (bf16[3,2,128,128]{3,2,1,0:T(8,128)(2,1)S(1)}, bf16[3,2,128,128]{3,2,1,0:T(8,128)(2,1)S(1)}, u32[]{:S(2)}, u32[]{:S(2)}) collective-permute-start(bf16[3,2,128,128]{3,2,1,0:T(8,128)(2,1)S(1)} %shard_map.43), channel_id=1, source_target_pairs={{0,33},{1,0},{2,35},{3,2},{4,37},{5,4},{6,39},{7,6},{8,41},{9,8},{... | collective-permute-start | bytes 589832 | tf_op jit(solution)/shard_map/ppermute | solution.py:27
  36.0 7.8 %collective-permute-start.13 = (bf16[2,2,64,1024]{3,2,1,0:T(8,128)(2,1)S(1)}, bf16[2,2,64,1024]{3,2,1,0:T(8,128)(2,1)S(1)}, u32[]{:S(2)}, u32[]{:S(2)}) collective-permute-start(bf16[2,2,64,1024]{3,2,1,0:T(8,128)(2,1)S(1)} %collective-permute-done.2.refs_4_.refs_0_.refs_3_), channel_id=1, source_target_pairs={{0,16},{1,17},{2,18},{3,19},{4,20},{5,21},{6,22},{7,23},{8,24},{9,... | collective-permute-start | bytes 1572872 | tf_op jit(solution)/shard_map/ppermute | solution.py:27
  37.4 6.4 %collective-permute-start.12 = (bf16[2,2,64,1024]{3,2,1,0:T(8,128)(2,1)S(1)}, bf16[2,2,64,1024]{3,2,1,0:T(8,128)(2,1)S(1)}, u32[]{:S(2)}, u32[]{:S(2)}) collective-permute-start(bf16[2,2,64,1024]{3,2,1,0:T(8,128)(2,1)S(1)} %collective-permute-done.10.refs_8_.refs_2_.refs_11_), channel_id=1, source_target_pairs={{0,16},{1,17},{2,18},{3,19},{4,20},{5,21},{6,22},{7,23},{8,24},{9,... | collective-permute-start | bytes 1572872 | tf_op jit(solution)/shard_map/ppermute | solution.py:27
  37.5 13.0 %collective-permute-start.11 = (bf16[2,2,64,1024]{3,2,1,0:T(8,128)(2,1)S(1)}, bf16[2,2,64,1024]{3,2,1,0:T(8,128)(2,1)S(1)}, u32[]{:S(2)}, u32[]{:S(2)}) collective-permute-start(bf16[2,2,64,1024]{3,2,1,0:T(8,128)(2,1)S(1)} %collective-permute-done.10.refs_8_.refs_2_.refs_11_), channel_id=1, source_target_pairs={{0,2},{1,3},{2,4},{3,5},{4,6},{5,7},{6,8},{7,9},{8,10},{9,11},{10,... | collective-permute-start | bytes 1572872 | tf_op jit(solution)/shard_map/ppermute | solution.py:27
  42.0 11.7 %collective-permute-start.16 = (bf16[2,2,64,1024]{3,2,1,0:T(8,128)(2,1)S(1)}, bf16[2,2,64,1024]{3,2,1,0:T(8,128)(2,1)S(1)}, u32[]{:S(2)}, u32[]{:S(2)}) collective-permute-start(bf16[2,2,64,1024]{3,2,1,0:T(8,128)(2,1)S(1)} %collective-permute-done.5.refs_2_.refs_5_.refs_0_), channel_id=1, source_target_pairs={{0,2},{1,3},{2,4},{3,5},{4,6},{5,7},{6,8},{7,9},{8,10},{9,11},{10,... | collective-permute-start | bytes 1572872 | tf_op jit(solution)/shard_map/ppermute | solution.py:27
  44.5 6.5 %collective-permute-start.17 = (bf16[2,2,128,128]{3,2,1,0:T(8,128)(2,1)S(1)}, bf16[2,2,128,128]{3,2,1,0:T(8,128)(2,1)S(1)}, u32[]{:S(2)}, u32[]{:S(2)}) collective-permute-start(bf16[2,2,128,128]{3,2,1,0:T(8,128)(2,1)S(1)} %shard_map.46), channel_id=1, source_target_pairs={{0,33},{1,0},{2,35},{3,2},{4,37},{5,4},{6,39},{7,6},{8,41},{9,8},{... | collective-permute-start | bytes 393224 | tf_op jit(solution)/shard_map/ppermute | solution.py:27
  47.6 6.1 %collective-permute-start.15 = (bf16[2,2,64,1024]{3,2,1,0:T(8,128)(2,1)S(1)}, bf16[2,2,64,1024]{3,2,1,0:T(8,128)(2,1)S(1)}, u32[]{:S(2)}, u32[]{:S(2)}) collective-permute-start(bf16[2,2,64,1024]{3,2,1,0:T(8,128)(2,1)S(1)} %collective-permute-done.5.refs_2_.refs_5_.refs_0_), channel_id=1, source_target_pairs={{0,16},{1,17},{2,18},{3,19},{4,20},{5,21},{6,22},{7,23},{8,24},{9,... | collective-permute-start | bytes 1572872 | tf_op jit(solution)/shard_map/ppermute | solution.py:27
  50.4 3.2 %collective-permute-start.14 = (bf16[2,2,64,1024]{3,2,1,0:T(8,128)(2,1)S(1)}, bf16[2,2,64,1024]{3,2,1,0:T(8,128)(2,1)S(1)}, u32[]{:S(2)}, u32[]{:S(2)}) collective-permute-start(bf16[2,2,64,1024]{3,2,1,0:T(8,128)(2,1)S(1)} %collective-permute-done.11.refs_4_.refs_13_.refs_3_), channel_id=1, source_target_pairs={{0,16},{1,17},{2,18},{3,19},{4,20},{5,21},{6,22},{7,23},{8,24},{9,... | collective-permute-start | bytes 1572872 | tf_op jit(solution)/shard_map/ppermute | solution.py:27
  53.6 1.9 %collective-permute-start.18 = (bf16[2,2,64,1024]{3,2,1,0:T(8,128)(2,1)S(1)}, bf16[2,2,64,1024]{3,2,1,0:T(8,128)(2,1)S(1)}, u32[]{:S(2)}, u32[]{:S(2)}) collective-permute-start(bf16[2,2,64,1024]{3,2,1,0:T(8,128)(2,1)S(1)} %collective-permute-done.16.refs_7_.refs_2_), channel_id=1, source_target_pairs={{0,16},{1,17},{2,18},{3,19},{4,20},{5,21},{6,22},{7,23},{8,24},{9,... | collective-permute-start | bytes 1572872 | tf_op jit(solution)/shard_map/ppermute | solution.py:27
  56.2 7.3 %collective-permute-start.19 = (bf16[3,2,128,128]{3,2,1,0:T(8,128)(2,1)S(1)}, bf16[3,2,128,128]{3,2,1,0:T(8,128)(2,1)S(1)}, u32[]{:S(2)}, u32[]{:S(2)}) collective-permute-start(bf16[3,2,128,128]{3,2,1,0:T(8,128)(2,1)S(1)} %shard_map.48), channel_id=1, source_target_pairs={{0,33},{1,0},{2,35},{3,2},{4,37},{5,4},{6,39},{7,6},{8,41},{9,8},{... | collective-permute-start | bytes 589832 | tf_op jit(solution)/shard_map/ppermute | solution.py:27
  64.2 6.6 %collective-permute-start.21 = (f32[1,128]{1,0:T(1,128)S(1)}, f32[1,128]{1,0:T(1,128)S(1)}, u32[]{:S(2)}, u32[]{:S(2)}) collective-permute-start(f32[1,128]{1,0:T(1,128)S(1)} %shard_map.49), channel_id=1, source_target_pairs={{0,129},{1,113},{2,131},{3,115},{4,133},{5,117},{6,135},{7,119},{8... | collective-permute-start | bytes 1544 | tf_op jit(solution)/shard_map/ppermute | solution.py:27
  67.3 4.8 %collective-permute-start.20 = (f32[1,128]{1,0:T(1,128)S(1)}, f32[1,128]{1,0:T(1,128)S(1)}, u32[]{:S(2)}, u32[]{:S(2)}) collective-permute-start(f32[1,128]{1,0:T(1,128)S(1)} %shard_map.49), channel_id=1, source_target_pairs={{0,128},{1,112},{2,130},{3,114},{4,132},{5,116},{6,134},{7,118},{8... | collective-permute-start | bytes 1544 | tf_op jit(solution)/shard_map/ppermute | solution.py:27
  67.4 12.5 %collective-permute-start.24 = (bf16[2,64,1024]{2,1,0:T(8,128)(2,1)S(1)}, bf16[2,64,1024]{2,1,0:T(8,128)(2,1)S(1)}, u32[]{:S(2)}, u32[]{:S(2)}) collective-permute-start(bf16[2,64,1024]{2,1,0:T(8,128)(2,1)S(1)} %get-tuple-element.29), channel_id=1, source_target_pairs={{0,128},{1,112},{2,130},{3,114},{4,132},{5,116},{6,134},{7,118},{8... | collective-permute-start | bytes 786440 | tf_op jit(solution)/shard_map/ppermute | solution.py:27
  67.5 19.7 %collective-permute-start.25 = (bf16[2,64,1024]{2,1,0:T(8,128)(2,1)S(1)}, bf16[2,64,1024]{2,1,0:T(8,128)(2,1)S(1)}, u32[]{:S(2)}, u32[]{:S(2)}) collective-permute-start(bf16[2,64,1024]{2,1,0:T(8,128)(2,1)S(1)} %get-tuple-element.31), channel_id=1, source_target_pairs={{0,129},{1,113},{2,131},{3,115},{4,133},{5,117},{6,135},{7,119},{8... | collective-permute-start | bytes 786440 | tf_op jit(solution)/shard_map/ppermute | solution.py:27
  72.0 5.6 %collective-permute-start.23 = (f32[2,128]{1,0:T(2,128)S(1)}, f32[2,128]{1,0:T(2,128)S(1)}, u32[]{:S(2)}, u32[]{:S(2)}) collective-permute-start(f32[2,128]{1,0:T(2,128)S(1)} %maximum_select_fusion.1), channel_id=1, source_target_pairs={{0,2},{1,3},{2,4},{3,5},{4,6},{5,7},{6,8},{7,9},{8,10},{9,11},{10,... | collective-permute-start | bytes 3080 | tf_op jit(solution)/shard_map/ppermute | solution.py:27
  74.0 4.1 %collective-permute-start.22 = (f32[2,128]{1,0:T(2,128)S(1)}, f32[2,128]{1,0:T(2,128)S(1)}, u32[]{:S(2)}, u32[]{:S(2)}) collective-permute-start(f32[2,128]{1,0:T(2,128)S(1)} %maximum_select_fusion.1), channel_id=1, source_target_pairs={{0,14},{1,15},{2,0},{3,1},{4,2},{5,3},{6,4},{7,5},{8,6},{9,7},{10,... | collective-permute-start | bytes 3080 | tf_op jit(solution)/shard_map/ppermute | solution.py:27
  79.9 8.5 %collective-permute-start.26 = (f32[2,128]{1,0:T(2,128)S(1)}, f32[2,128]{1,0:T(2,128)S(1)}, u32[]{:S(2)}, u32[]{:S(2)}) collective-permute-start(f32[2,128]{1,0:T(2,128)S(1)} %get-tuple-element.32), channel_id=1, source_target_pairs={{0,6},{1,7},{2,8},{3,9},{4,10},{5,11},{6,12},{7,13},{8,14},{9,15},... | collective-permute-start | bytes 3080 | tf_op jit(solution)/shard_map/ppermute | solution.py:27
  87.2 6.6 %collective-permute-start.27 = (f32[2,128]{1,0:T(2,128)S(1)}, f32[2,128]{1,0:T(2,128)S(1)}, u32[]{:S(2)}, u32[]{:S(2)}) collective-permute-start(f32[2,128]{1,0:T(2,128)S(1)} %get-tuple-element.33), channel_id=1, source_target_pairs={{0,10},{1,11},{2,12},{3,13},{4,14},{5,15},{6,0},{7,1},{8,2},{9,3},... | collective-permute-start | bytes 3080 | tf_op jit(solution)/shard_map/ppermute | solution.py:27

commit v15 on v14

--- a/solution.py
+++ b/solution.py
@@ -240,8 +240,9 @@
     kept, sent = moved(keep, from_hub(0)), moved(send, from_hub(1))
     first, second = moved(trace, from_hub(0)), moved(trace, from_hub(1))
     both = jnp.where(half == 0, jnp.concatenate([first, second]), jnp.concatenate([second, first]))
+    both, kept = wall((both, kept))
     below, above = moved(both, along(1)), moved(both, along(-1))
-    two, three, kept = wall((both + above, below + both + above, kept))
+    two, three = both + above, below + both + above
     below, above = moved(two, along(3)), moved(three, along(-3))
     both = below + three + above
     products = jnp.where(half == 0, jnp.stack([kept, sent]), jnp.stack([sent, kept]))[:, None, None]

time: 94.5 us -> 92.4 us (0.978)
  the two profiles are of different devices: /device:TPU:38 before, /device:TPU:1 now
where the time goes in v15:
time: 92.4 us; the launch traced here: 91.7 us
  starting transfers between devices  50.9 us (55%)
  waiting for transfers between devices  29.6 us (32%)
  Pallas kernels  8.83 us (10%)
  other arithmetic  1.55 us (2%)
    ppermute x28, starting transfers between devices, moved(): lax.ppermute(block, BOTH, [(index_of(*at), index_of(*route(*at))) for at...  50.9 us
    ppermute x28, waiting for transfers between devices, moved(): lax.ppermute(block, BOTH, [(index_of(*at), index_of(*route(*at))) for at...  29.6 us
    pallas_call x9, Pallas kernels, call(): pl.pallas_call(kernel, out_shape=out_shape, in_specs=[SMEM] + [VMEM] * le...  8.83 us
  transfers between devices with their start and end apart: 28, of which 13 were waited for; matrix products, arithmetic and copies ran while one was open for 1% of the time, Pallas kernels for 9%

profile of v15, /device:TPU:1, one launch (start us, length us, event | category | flops | bytes accessed | tf_op | source)
XLA Modules:
  0.0 91.7 jit_solution(3319127652652215125)
XLA Ops:
  0.6 0.0 copy-start
  0.6 4.2 %collective-permute-start = (bf16[2,2,64,1024]{3,2,1,0:T(8,128)(2,1)}, bf16[2,2,64,1024]{3,2,1,0:T(8,128)(2,1)S(1)}, u32[]{:S(2)}, u32[]{:S(2)}) collective-permute-start(bf16[2,2,64,1024]{3,2,1,0:T(8,128)(2,1)} %bitcast.15), channel_id=1, source_target_pairs={{0,128},{1,144},{2,130},{3,146},{4,132},{5,148},{6,134},{7,150},{8... | collective-permute-start | bytes 1572872 | tf_op jit(solution)/shard_map/ppermute | solution.py:27
  4.8 6.4 %collective-permute-done.own.refs_2_.refs_0_ = bf16[2,2,64,1024]{3,2,1,0:T(8,128)(2,1)S(1)} collective-permute-done((bf16[2,2,64,1024]{3,2,1,0:T(8,128)(2,1)}, bf16[2,2,64,1024]{3,2,1,0:T(8,128)(2,1)S(1)}, u32[]{:S(2)}, u32[]{:S(2)}) %collective-permute-start) | collective-permute-done | bytes 524320 | tf_op jit(solution)/shard_map/ppermute | solution.py:27
  11.3 1.5 %collective-permute-start.3 = (bf16[2,2,64,1024]{3,2,1,0:T(8,128)(2,1)S(1)}, bf16[2,2,64,1024]{3,2,1,0:T(8,128)(2,1)S(1)}, u32[]{:S(2)}, u32[]{:S(2)}) collective-permute-start(bf16[2,2,64,1024]{3,2,1,0:T(8,128)(2,1)S(1)} %collective-permute-done.own.refs_2_.refs_0_), channel_id=1, source_target_pairs={{0,16},{1,17},{2,18},{3,19},{4,20},{5,21},{6,22},{7,23},{8,24},{9,... | collective-permute-start | bytes 1572872 | tf_op jit(solution)/shard_map/ppermute | solution.py:27
  12.8 4.1 %collective-permute-start.1 = (bf16[2,2,64,1024]{3,2,1,0:T(8,128)(2,1)S(1)}, bf16[2,2,64,1024]{3,2,1,0:T(8,128)(2,1)S(1)}, u32[]{:S(2)}, u32[]{:S(2)}) collective-permute-start(bf16[2,2,64,1024]{3,2,1,0:T(8,128)(2,1)S(1)} %collective-permute-done.own.refs_2_.refs_0_), channel_id=1, source_target_pairs={{0,2},{1,3},{2,4},{3,5},{4,6},{5,7},{6,8},{7,9},{8,10},{9,11},{10,... | collective-permute-start | bytes 1572872 | tf_op jit(solution)/shard_map/ppermute | solution.py:27
  16.9 0.0 collective-permute-done.3.other.refs_3_.refs_8_
  16.9 1.9 %collective-permute-start.6 = (bf16[2,2,64,1024]{3,2,1,0:T(8,128)(2,1)S(1)}, bf16[2,2,64,1024]{3,2,1,0:T(8,128)(2,1)S(1)}, u32[]{:S(2)}, u32[]{:S(2)}) collective-permute-start(bf16[2,2,64,1024]{3,2,1,0:T(8,128)(2,1)S(1)} %collective-permute-done.3.other.refs_3_.refs_8_), channel_id=1, source_target_pairs={{0,2},{1,3},{2,4},{3,5},{4,6},{5,7},{6,8},{7,9},{8,10},{9,11},{10,... | collective-permute-start | bytes 1572872 | tf_op jit(solution)/shard_map/ppermute | solution.py:27
  18.8 0.1 pad_add_fusion.info.refs_0_
  18.9 0.6 shard_map.41
  19.4 1.3 %collective-permute-start.4 = (bf16[2,128,1024]{2,1,0:T(8,128)(2,1)S(1)}, bf16[2,128,1024]{2,1,0:T(8,128)(2,1)S(1)}, u32[]{:S(2)}, u32[]{:S(2)}) collective-permute-start(bf16[2,128,1024]{2,1,0:T(8,128)(2,1)S(1)} %shard_map.41), channel_id=1, source_target_pairs={{0,33},{1,0},{2,35},{3,2},{4,37},{5,4},{6,39},{7,6},{8,41},{9,8},{... | collective-permute-start | bytes 1572872 | tf_op jit(solution)/shard_map/ppermute | solution.py:27
  20.7 2.3 %collective-permute-done.1.refs_1_.refs_2_ = bf16[2,2,64,1024]{3,2,1,0:T(8,128)(2,1)S(1)} collective-permute-done((bf16[2,2,64,1024]{3,2,1,0:T(8,128)(2,1)S(1)}, bf16[2,2,64,1024]{3,2,1,0:T(8,128)(2,1)S(1)}, u32[]{:S(2)}, u32[]{:S(2)}) %collective-permute-start.1) | collective-permute-done | bytes 524320 | tf_op jit(solution)/shard_map/ppermute | solution.py:27
  23.0 3.4 %collective-permute-start.2 = (bf16[2,2,64,1024]{3,2,1,0:T(8,128)(2,1)S(1)}, bf16[2,2,64,1024]{3,2,1,0:T(8,128)(2,1)S(1)}, u32[]{:S(2)}, u32[]{:S(2)}) collective-permute-start(bf16[2,2,64,1024]{3,2,1,0:T(8,128)(2,1)S(1)} %collective-permute-done.1.refs_1_.refs_2_), channel_id=1, source_target_pairs={{0,2},{1,3},{2,4},{3,5},{4,6},{5,7},{6,8},{7,9},{8,10},{9,11},{10,... | collective-permute-start | bytes 1572872 | tf_op jit(solution)/shard_map/ppermute | solution.py:27
  26.4 0.0 collective-permute-start.8
  26.4 2.2 %collective-permute-done.6.refs_4_.refs_6_.refs_9_ = bf16[2,2,64,1024]{3,2,1,0:T(8,128)(2,1)S(1)} collective-permute-done((bf16[2,2,64,1024]{3,2,1,0:T(8,128)(2,1)S(1)}, bf16[2,2,64,1024]{3,2,1,0:T(8,128)(2,1)S(1)}, u32[]{:S(2)}, u32[]{:S(2)}) %collective-permute-start.6) | collective-permute-done | bytes 524320 | tf_op jit(solution)/shard_map/ppermute | solution.py:27
  28.6 3.1 %collective-permute-start.10 = (bf16[2,2,64,1024]{3,2,1,0:T(8,128)(2,1)S(1)}, bf16[2,2,64,1024]{3,2,1,0:T(8,128)(2,1)S(1)}, u32[]{:S(2)}, u32[]{:S(2)}) collective-permute-start(bf16[2,2,64,1024]{3,2,1,0:T(8,128)(2,1)S(1)} %collective-permute-done.6.refs_4_.refs_6_.refs_9_), channel_id=1, source_target_pairs={{0,2},{1,3},{2,4},{3,5},{4,6},{5,7},{6,8},{7,9},{8,10},{9,11},{10,... | collective-permute-start | bytes 1572872 | tf_op jit(solution)/shard_map/ppermute | solution.py:27
  31.7 0.0 collective-permute-start.7
  31.7 2.5 %collective-permute-done.4.refs_1_.a_ref = bf16[2,128,1024]{2,1,0:T(8,128)(2,1)S(1)} collective-permute-done((bf16[2,128,1024]{2,1,0:T(8,128)(2,1)S(1)}, bf16[2,128,1024]{2,1,0:T(8,128)(2,1)S(1)}, u32[]{:S(2)}, u32[]{:S(2)}) %collective-permute-start.4) | collective-permute-done | bytes 524320 | tf_op jit(solution)/shard_map/ppermute | solution.py:27
  34.2 0.8 shard_map.42.refs_10_
  35.1 0.0 collective-permute-done.2.refs_4_.refs_0_.refs_3_
  35.1 3.7 %collective-permute-start.5 = (bf16[2,2,64,1024]{3,2,1,0:T(8,128)(2,1)S(1)}, bf16[2,2,64,1024]{3,2,1,0:T(8,128)(2,1)S(1)}, u32[]{:S(2)}, u32[]{:S(2)}) collective-permute-start(bf16[2,2,64,1024]{3,2,1,0:T(8,128)(2,1)S(1)} %collective-permute-done.2.refs_4_.refs_0_.refs_3_), channel_id=1, source_target_pairs={{0,2},{1,3},{2,4},{3,5},{4,6},{5,7},{6,8},{7,9},{8,10},{9,11},{10,... | collective-permute-start | bytes 1572872 | tf_op jit(solution)/shard_map/ppermute | solution.py:27
  38.8 0.7 shard_map.43
  39.4 0.1 collective-permute-start.9
  39.5 1.2 %collective-permute-start.13 = (bf16[2,2,64,1024]{3,2,1,0:T(8,128)(2,1)S(1)}, bf16[2,2,64,1024]{3,2,1,0:T(8,128)(2,1)S(1)}, u32[]{:S(2)}, u32[]{:S(2)}) collective-permute-start(bf16[2,2,64,1024]{3,2,1,0:T(8,128)(2,1)S(1)} %collective-permute-done.2.refs_4_.refs_0_.refs_3_), channel_id=1, source_target_pairs={{0,16},{1,17},{2,18},{3,19},{4,20},{5,21},{6,22},{7,23},{8,24},{9,... | collective-permute-start | bytes 1572872 | tf_op jit(solution)/shard_map/ppermute | solution.py:27
  40.8 0.0 collective-permute-done.10.refs_8_.refs_2_.refs_11_
  40.8 0.9 collective-permute-start.12
  41.7 2.1 %collective-permute-start.11 = (bf16[2,2,64,1024]{3,2,1,0:T(8,128)(2,1)S(1)}, bf16[2,2,64,1024]{3,2,1,0:T(8,128)(2,1)S(1)}, u32[]{:S(2)}, u32[]{:S(2)}) collective-permute-start(bf16[2,2,64,1024]{3,2,1,0:T(8,128)(2,1)S(1)} %collective-permute-done.10.refs_8_.refs_2_.refs_11_), channel_id=1, source_target_pairs={{0,2},{1,3},{2,4},{3,5},{4,6},{5,7},{6,8},{7,9},{8,10},{9,11},{10,... | collective-permute-start | bytes 1572872 | tf_op jit(solution)/shard_map/ppermute | solution.py:27
  43.7 1.7 %collective-permute-done.5.refs_2_.refs_5_.refs_0_ = bf16[2,2,64,1024]{3,2,1,0:T(8,128)(2,1)S(1)} collective-permute-done((bf16[2,2,64,1024]{3,2,1,0:T(8,128)(2,1)S(1)}, bf16[2,2,64,1024]{3,2,1,0:T(8,128)(2,1)S(1)}, u32[]{:S(2)}, u32[]{:S(2)}) %collective-permute-start.5) | collective-permute-done | bytes 524320 | tf_op jit(solution)/shard_map/ppermute | solution.py:27
  45.5 2.1 %collective-permute-done.9.near = bf16[3,2,128,128]{3,2,1,0:T(8,128)(2,1)S(1)} collective-permute-done((bf16[3,2,128,128]{3,2,1,0:T(8,128)(2,1)S(1)}, bf16[3,2,128,128]{3,2,1,0:T(8,128)(2,1)S(1)}, u32[]{:S(2)}, u32[]{:S(2)}) %collective-permute-start.9) | collective-permute-done | bytes 196640 | tf_op jit(solution)/shard_map/ppermute | solution.py:27
  47.6 1.0 %collective-permute-start.16 = (bf16[2,2,64,1024]{3,2,1,0:T(8,128)(2,1)S(1)}, bf16[2,2,64,1024]{3,2,1,0:T(8,128)(2,1)S(1)}, u32[]{:S(2)}, u32[]{:S(2)}) collective-permute-start(bf16[2,2,64,1024]{3,2,1,0:T(8,128)(2,1)S(1)} %collective-permute-done.5.refs_2_.refs_5_.refs_0_), channel_id=1, source_target_pairs={{0,2},{1,3},{2,4},{3,5},{4,6},{5,7},{6,8},{7,9},{8,10},{9,11},{10,... | collective-permute-start | bytes 1572872 | tf_op jit(solution)/shard_map/ppermute | solution.py:27
  48.6 0.6 shard_map.46
  49.2 1.3 %collective-permute-start.17 = (bf16[2,2,128,128]{3,2,1,0:T(8,128)(2,1)S(1)}, bf16[2,2,128,128]{3,2,1,0:T(8,128)(2,1)S(1)}, u32[]{:S(2)}, u32[]{:S(2)}) collective-permute-start(bf16[2,2,128,128]{3,2,1,0:T(8,128)(2,1)S(1)} %shard_map.46), channel_id=1, source_target_pairs={{0,33},{1,0},{2,35},{3,2},{4,37},{5,4},{6,39},{7,6},{8,41},{9,8},{... | collective-permute-start | bytes 393224 | tf_op jit(solution)/shard_map/ppermute | solution.py:27
  50.5 1.4 %collective-permute-start.15 = (bf16[2,2,64,1024]{3,2,1,0:T(8,128)(2,1)S(1)}, bf16[2,2,64,1024]{3,2,1,0:T(8,128)(2,1)S(1)}, u32[]{:S(2)}, u32[]{:S(2)}) collective-permute-start(bf16[2,2,64,1024]{3,2,1,0:T(8,128)(2,1)S(1)} %collective-permute-done.5.refs_2_.refs_5_.refs_0_), channel_id=1, source_target_pairs={{0,16},{1,17},{2,18},{3,19},{4,20},{5,21},{6,22},{7,23},{8,24},{9,... | collective-permute-start | bytes 1572872 | tf_op jit(solution)/shard_map/ppermute | solution.py:27
  52.0 1.3 %shard_map.44.refs_6_ = f32[256,1024]{1,0:T(8,128)S(1)} custom-call(s32[6]{0:T(128)S(1)} %pad_add_fusion.info.refs_0_, bf16[2,128,1024]{2,1,0:T(8,128)(2,1)S(1)} %collective-permute-done.4.refs_1_.a_ref, bf16[2,2,64,1024]{3,2,1,0:T(8,128)(2,1)S(1)} %collective-permute-done.1.refs_1_.refs_2_, ...), custom_call_target="tpu_custom_call" | custom-call | flops 1 | bytes 1048576 | tf_op jit(solution)/shard_map/pallas_call | solution.py:75
  53.3 0.1 collective-permute-start.14
  53.4 4.2 %collective-permute-done.17.middle = bf16[2,2,128,128]{3,2,1,0:T(8,128)(2,1)S(1)} collective-permute-done((bf16[2,2,128,128]{3,2,1,0:T(8,128)(2,1)S(1)}, bf16[2,2,128,128]{3,2,1,0:T(8,128)(2,1)S(1)}, u32[]{:S(2)}, u32[]{:S(2)}) %collective-permute-start.17) | collective-permute-done | bytes 131104 | tf_op jit(solution)/shard_map/ppermute | solution.py:27
  57.6 0.9 %collective-permute-start.18 = (bf16[2,2,64,1024]{3,2,1,0:T(8,128)(2,1)S(1)}, bf16[2,2,64,1024]{3,2,1,0:T(8,128)(2,1)S(1)}, u32[]{:S(2)}, u32[]{:S(2)}) collective-permute-start(bf16[2,2,64,1024]{3,2,1,0:T(8,128)(2,1)S(1)} %collective-permute-done.16.refs_7_.refs_2_), channel_id=1, source_target_pairs={{0,16},{1,17},{2,18},{3,19},{4,20},{5,21},{6,22},{7,23},{8,24},{9,... | collective-permute-start | bytes 1572872 | tf_op jit(solution)/shard_map/ppermute | solution.py:27
  58.5 0.0 collective-permute-done.15.refs_5_.refs_14_.refs_4_
  58.5 0.0 collective-permute-done.14.refs_3_.refs_6_.refs_1_
  58.5 1.0 %shard_map.45.acc = f32[256,1024]{1,0:T(8,128)S(1)} custom-call(s32[6]{0:T(128)S(1)} %pad_add_fusion.info.refs_0_, bf16[2,128,1024]{2,1,0:T(8,128)(2,1)S(1)} %collective-permute-done.4.refs_1_.a_ref, bf16[2,2,64,1024]{3,2,1,0:T(8,128)(2,1)S(1)} %collective-permute-done.5.refs_2_.refs_5_.refs_0_, ...), custom_call_target="tpu_custom_call" | custom-call | flops 1 | bytes 1048576 | tf_op jit(solution)/shard_map/pallas_call | solution.py:75
  59.5 0.5 collective-permute-done.18.refs_15_.refs_5_
  60.1 0.7 shard_map.48
  60.7 1.3 %collective-permute-start.19 = (bf16[3,2,128,128]{3,2,1,0:T(8,128)(2,1)S(1)}, bf16[3,2,128,128]{3,2,1,0:T(8,128)(2,1)S(1)}, u32[]{:S(2)}, u32[]{:S(2)}) collective-permute-start(bf16[3,2,128,128]{3,2,1,0:T(8,128)(2,1)S(1)} %shard_map.48), channel_id=1, source_target_pairs={{0,33},{1,0},{2,35},{3,2},{4,37},{5,4},{6,39},{7,6},{8,41},{9,8},{... | collective-permute-start | bytes 589832 | tf_op jit(solution)/shard_map/ppermute | solution.py:27
  62.0 2.4 %shard_map.47 = (bf16[2,64,1024]{2,1,0:T(8,128)(2,1)S(1)}, bf16[2,64,1024]{2,1,0:T(8,128)(2,1)S(1)}, f32[256,1024]{1,0:T(8,128)S(1)}, f32[8,128]{1,0:T(8,128)S(1)}) custom-call(s32[6]{0:T(128)S(1)} %pad_add_fusion.info.refs_0_, bf16[2,128,1024]{2,1,0:T(8,128)(2,1)S(1)} %collective-permute-done.4.refs_1_.a_ref, f32[256,1024]{1,0:T(8,128)S(1)} %shard_map.45.acc, ...), custom_call_target="tpu_custom_call" | custom-call | flops 3000000000 | bytes 1048576 | tf_op jit(solution)/shard_map/pallas_call | solution.py:75
  64.4 3.9 %collective-permute-start.22 = (bf16[2,64,1024]{2,1,0:T(8,128)(2,1)S(1)}, bf16[2,64,1024]{2,1,0:T(8,128)(2,1)S(1)}, u32[]{:S(2)}, u32[]{:S(2)}) collective-permute-start(bf16[2,64,1024]{2,1,0:T(8,128)(2,1)S(1)} %get-tuple-element.28), channel_id=1, source_target_pairs={{0,128},{1,112},{2,130},{3,114},{4,132},{5,116},{6,134},{7,118},{8... | collective-permute-start | bytes 786440 | tf_op jit(solution)/shard_map/ppermute | solution.py:27
  68.3 2.6 %collective-permute-done.19.late = bf16[3,2,128,128]{3,2,1,0:T(8,128)(2,1)S(1)} collective-permute-done((bf16[3,2,128,128]{3,2,1,0:T(8,128)(2,1)S(1)}, bf16[3,2,128,128]{3,2,1,0:T(8,128)(2,1)S(1)}, u32[]{:S(2)}, u32[]{:S(2)}) %collective-permute-start.19) | collective-permute-done | bytes 196640 | tf_op jit(solution)/shard_map/ppermute | solution.py:27
  70.9 0.7 shard_map.49
  71.6 0.0 collective-permute-start.21
  71.6 6.2 %collective-permute-start.20 = (f32[1,128]{1,0:T(1,128)S(1)}, f32[1,128]{1,0:T(1,128)S(1)}, u32[]{:S(2)}, u32[]{:S(2)}) collective-permute-start(f32[1,128]{1,0:T(1,128)S(1)} %shard_map.49), channel_id=1, source_target_pairs={{0,128},{1,112},{2,130},{3,114},{4,132},{5,116},{6,134},{7,118},{8... | collective-permute-start | bytes 1544 | tf_op jit(solution)/shard_map/ppermute | solution.py:27
  77.8 0.0 collective-permute-start.23
  77.8 0.0 collective-permute-done.21
  77.8 0.7 collective-permute-done.20
  78.5 0.0 collective-permute-done.22
  78.5 0.1 collective-permute-start.26
  78.6 2.7 %collective-permute-start.24 = (f32[2,128]{1,0:T(2,128)S(1)}, f32[2,128]{1,0:T(2,128)S(1)}, u32[]{:S(2)}, u32[]{:S(2)}) collective-permute-start(f32[2,128]{1,0:T(2,128)S(1)} %maximum_select_fusion.1), channel_id=1, source_target_pairs={{0,14},{1,15},{2,0},{3,1},{4,2},{5,3},{6,4},{7,5},{8,6},{9,7},{10,... | collective-permute-start | bytes 3080 | tf_op jit(solution)/shard_map/ppermute | solution.py:27
  81.3 1.1 %collective-permute-done.26 = f32[2,128]{1,0:T(2,128)S(1)} collective-permute-done((f32[2,128]{1,0:T(2,128)S(1)}, f32[2,128]{1,0:T(2,128)S(1)}, u32[]{:S(2)}, u32[]{:S(2)}) %collective-permute-start.26) | collective-permute-done | bytes 1056 | tf_op jit(solution)/shard_map/ppermute | solution.py:27
  82.4 0.0 collective-permute-done.24
  82.4 4.4 %collective-permute-start.25 = (f32[2,128]{1,0:T(2,128)S(1)}, f32[2,128]{1,0:T(2,128)S(1)}, u32[]{:S(2)}, u32[]{:S(2)}) collective-permute-start(f32[2,128]{1,0:T(2,128)S(1)} %get-tuple-element.36), channel_id=1, source_target_pairs={{0,6},{1,7},{2,8},{3,9},{4,10},{5,11},{6,12},{7,13},{8,14},{9,15},... | collective-permute-start | bytes 3080 | tf_op jit(solution)/shard_map/ppermute | solution.py:27
  86.8 0.1 collective-permute-start.27
  86.9 0.0 collective-permute-done.23
  86.9 0.9 maximum_select_fusion
  87.8 0.1 collective-permute-done.25
  87.9 3.1 %collective-permute-done.27 = f32[2,128]{1,0:T(2,128)S(1)} collective-permute-done((f32[2,128]{1,0:T(2,128)S(1)}, f32[2,128]{1,0:T(2,128)S(1)}, u32[]{:S(2)}, u32[]{:S(2)}) %collective-permute-start.27) | collective-permute-done | bytes 1056 | tf_op jit(solution)/shard_map/ppermute | solution.py:27
  91.0 0.1 reshape.77
  91.1 0.6 broadcast_multiply_fusion
  (12 shorter events, 0.1 us)
Async XLA Ops:
  0.6 16.2 %copy-start = (s32[2,1,4]{2,1,0:T(1,128)S(1)}, s32[2,1,4]{2,1,0:T(1,128)}, u32[]{:S(2)}) copy-start(s32[2,1,4]{2,1,0:T(1,128)} %param.3) | copy-start | bytes 100
  0.6 10.6 %collective-permute-start = (bf16[2,2,64,1024]{3,2,1,0:T(8,128)(2,1)}, bf16[2,2,64,1024]{3,2,1,0:T(8,128)(2,1)S(1)}, u32[]{:S(2)}, u32[]{:S(2)}) collective-permute-start(bf16[2,2,64,1024]{3,2,1,0:T(8,128)(2,1)} %bitcast.15), channel_id=1, source_target_pairs={{0,128},{1,144},{2,130},{3,146},{4,132},{5,148},{6,134},{7,150},{8... | collective-permute-start | bytes 1572872 | tf_op jit(solution)/shard_map/ppermute | solution.py:27
  11.3 5.6 %collective-permute-start.3 = (bf16[2,2,64,1024]{3,2,1,0:T(8,128)(2,1)S(1)}, bf16[2,2,64,1024]{3,2,1,0:T(8,128)(2,1)S(1)}, u32[]{:S(2)}, u32[]{:S(2)}) collective-permute-start(bf16[2,2,64,1024]{3,2,1,0:T(8,128)(2,1)S(1)} %collective-permute-done.own.refs_2_.refs_0_), channel_id=1, source_target_pairs={{0,16},{1,17},{2,18},{3,19},{4,20},{5,21},{6,22},{7,23},{8,24},{9,... | collective-permute-start | bytes 1572872 | tf_op jit(solution)/shard_map/ppermute | solution.py:27
  12.8 10.2 %collective-permute-start.1 = (bf16[2,2,64,1024]{3,2,1,0:T(8,128)(2,1)S(1)}, bf16[2,2,64,1024]{3,2,1,0:T(8,128)(2,1)S(1)}, u32[]{:S(2)}, u32[]{:S(2)}) collective-permute-start(bf16[2,2,64,1024]{3,2,1,0:T(8,128)(2,1)S(1)} %collective-permute-done.own.refs_2_.refs_0_), channel_id=1, source_target_pairs={{0,2},{1,3},{2,4},{3,5},{4,6},{5,7},{6,8},{7,9},{8,10},{9,11},{10,... | collective-permute-start | bytes 1572872 | tf_op jit(solution)/shard_map/ppermute | solution.py:27
  16.9 11.7 %collective-permute-start.6 = (bf16[2,2,64,1024]{3,2,1,0:T(8,128)(2,1)S(1)}, bf16[2,2,64,1024]{3,2,1,0:T(8,128)(2,1)S(1)}, u32[]{:S(2)}, u32[]{:S(2)}) collective-permute-start(bf16[2,2,64,1024]{3,2,1,0:T(8,128)(2,1)S(1)} %collective-permute-done.3.other.refs_3_.refs_8_), channel_id=1, source_target_pairs={{0,2},{1,3},{2,4},{3,5},{4,6},{5,7},{6,8},{7,9},{8,10},{9,11},{10,... | collective-permute-start | bytes 1572872 | tf_op jit(solution)/shard_map/ppermute | solution.py:27
  19.4 14.8 %collective-permute-start.4 = (bf16[2,128,1024]{2,1,0:T(8,128)(2,1)S(1)}, bf16[2,128,1024]{2,1,0:T(8,128)(2,1)S(1)}, u32[]{:S(2)}, u32[]{:S(2)}) collective-permute-start(bf16[2,128,1024]{2,1,0:T(8,128)(2,1)S(1)} %shard_map.41), channel_id=1, source_target_pairs={{0,33},{1,0},{2,35},{3,2},{4,37},{5,4},{6,39},{7,6},{8,41},{9,8},{... | collective-permute-start | bytes 1572872 | tf_op jit(solution)/shard_map/ppermute | solution.py:27
  23.0 12.1 %collective-permute-start.2 = (bf16[2,2,64,1024]{3,2,1,0:T(8,128)(2,1)S(1)}, bf16[2,2,64,1024]{3,2,1,0:T(8,128)(2,1)S(1)}, u32[]{:S(2)}, u32[]{:S(2)}) collective-permute-start(bf16[2,2,64,1024]{3,2,1,0:T(8,128)(2,1)S(1)} %collective-permute-done.1.refs_1_.refs_2_), channel_id=1, source_target_pairs={{0,2},{1,3},{2,4},{3,5},{4,6},{5,7},{6,8},{7,9},{8,10},{9,11},{10,... | collective-permute-start | bytes 1572872 | tf_op jit(solution)/shard_map/ppermute | solution.py:27
  26.4 12.3 %collective-permute-start.8 = (bf16[2,2,64,1024]{3,2,1,0:T(8,128)(2,1)S(1)}, bf16[2,2,64,1024]{3,2,1,0:T(8,128)(2,1)S(1)}, u32[]{:S(2)}, u32[]{:S(2)}) collective-permute-start(bf16[2,2,64,1024]{3,2,1,0:T(8,128)(2,1)S(1)} %collective-permute-done.1.refs_1_.refs_2_), channel_id=1, source_target_pairs={{0,16},{1,17},{2,18},{3,19},{4,20},{5,21},{6,22},{7,23},{8,24},{9,... | collective-permute-start | bytes 1572872 | tf_op jit(solution)/shard_map/ppermute | solution.py:27
  28.6 12.2 %collective-permute-start.10 = (bf16[2,2,64,1024]{3,2,1,0:T(8,128)(2,1)S(1)}, bf16[2,2,64,1024]{3,2,1,0:T(8,128)(2,1)S(1)}, u32[]{:S(2)}, u32[]{:S(2)}) collective-permute-start(bf16[2,2,64,1024]{3,2,1,0:T(8,128)(2,1)S(1)} %collective-permute-done.6.refs_4_.refs_6_.refs_9_), channel_id=1, source_target_pairs={{0,2},{1,3},{2,4},{3,5},{4,6},{5,7},{6,8},{7,9},{8,10},{9,11},{10,... | collective-permute-start | bytes 1572872 | tf_op jit(solution)/shard_map/ppermute | solution.py:27
  31.7 7.0 %collective-permute-start.7 = (bf16[2,2,64,1024]{3,2,1,0:T(8,128)(2,1)S(1)}, bf16[2,2,64,1024]{3,2,1,0:T(8,128)(2,1)S(1)}, u32[]{:S(2)}, u32[]{:S(2)}) collective-permute-start(bf16[2,2,64,1024]{3,2,1,0:T(8,128)(2,1)S(1)} %collective-permute-done.6.refs_4_.refs_6_.refs_9_), channel_id=1, source_target_pairs={{0,16},{1,17},{2,18},{3,19},{4,20},{5,21},{6,22},{7,23},{8,24},{9,... | collective-permute-start | bytes 1572872 | tf_op jit(solution)/shard_map/ppermute | solution.py:27
  35.1 10.4 %collective-permute-start.5 = (bf16[2,2,64,1024]{3,2,1,0:T(8,128)(2,1)S(1)}, bf16[2,2,64,1024]{3,2,1,0:T(8,128)(2,1)S(1)}, u32[]{:S(2)}, u32[]{:S(2)}) collective-permute-start(bf16[2,2,64,1024]{3,2,1,0:T(8,128)(2,1)S(1)} %collective-permute-done.2.refs_4_.refs_0_.refs_3_), channel_id=1, source_target_pairs={{0,2},{1,3},{2,4},{3,5},{4,6},{5,7},{6,8},{7,9},{8,10},{9,11},{10,... | collective-permute-start | bytes 1572872 | tf_op jit(solution)/shard_map/ppermute | solution.py:27
  39.4 8.1 %collective-permute-start.9 = (bf16[3,2,128,128]{3,2,1,0:T(8,128)(2,1)S(1)}, bf16[3,2,128,128]{3,2,1,0:T(8,128)(2,1)S(1)}, u32[]{:S(2)}, u32[]{:S(2)}) collective-permute-start(bf16[3,2,128,128]{3,2,1,0:T(8,128)(2,1)S(1)} %shard_map.43), channel_id=1, source_target_pairs={{0,33},{1,0},{2,35},{3,2},{4,37},{5,4},{6,39},{7,6},{8,41},{9,8},{... | collective-permute-start | bytes 589832 | tf_op jit(solution)/shard_map/ppermute | solution.py:27
  39.5 9.1 %collective-permute-start.13 = (bf16[2,2,64,1024]{3,2,1,0:T(8,128)(2,1)S(1)}, bf16[2,2,64,1024]{3,2,1,0:T(8,128)(2,1)S(1)}, u32[]{:S(2)}, u32[]{:S(2)}) collective-permute-start(bf16[2,2,64,1024]{3,2,1,0:T(8,128)(2,1)S(1)} %collective-permute-done.2.refs_4_.refs_0_.refs_3_), channel_id=1, source_target_pairs={{0,16},{1,17},{2,18},{3,19},{4,20},{5,21},{6,22},{7,23},{8,24},{9,... | collective-permute-start | bytes 1572872 | tf_op jit(solution)/shard_map/ppermute | solution.py:27
  40.8 7.8 %collective-permute-start.12 = (bf16[2,2,64,1024]{3,2,1,0:T(8,128)(2,1)S(1)}, bf16[2,2,64,1024]{3,2,1,0:T(8,128)(2,1)S(1)}, u32[]{:S(2)}, u32[]{:S(2)}) collective-permute-start(bf16[2,2,64,1024]{3,2,1,0:T(8,128)(2,1)S(1)} %collective-permute-done.10.refs_8_.refs_2_.refs_11_), channel_id=1, source_target_pairs={{0,16},{1,17},{2,18},{3,19},{4,20},{5,21},{6,22},{7,23},{8,24},{9,... | collective-permute-start | bytes 1572872 | tf_op jit(solution)/shard_map/ppermute | solution.py:27
  41.7 11.6 %collective-permute-start.11 = (bf16[2,2,64,1024]{3,2,1,0:T(8,128)(2,1)S(1)}, bf16[2,2,64,1024]{3,2,1,0:T(8,128)(2,1)S(1)}, u32[]{:S(2)}, u32[]{:S(2)}) collective-permute-start(bf16[2,2,64,1024]{3,2,1,0:T(8,128)(2,1)S(1)} %collective-permute-done.10.refs_8_.refs_2_.refs_11_), channel_id=1, source_target_pairs={{0,2},{1,3},{2,4},{3,5},{4,6},{5,7},{6,8},{7,9},{8,10},{9,11},{10,... | collective-permute-start | bytes 1572872 | tf_op jit(solution)/shard_map/ppermute | solution.py:27
  47.6 10.0 %collective-permute-start.16 = (bf16[2,2,64,1024]{3,2,1,0:T(8,128)(2,1)S(1)}, bf16[2,2,64,1024]{3,2,1,0:T(8,128)(2,1)S(1)}, u32[]{:S(2)}, u32[]{:S(2)}) collective-permute-start(bf16[2,2,64,1024]{3,2,1,0:T(8,128)(2,1)S(1)} %collective-permute-done.5.refs_2_.refs_5_.refs_0_), channel_id=1, source_target_pairs={{0,2},{1,3},{2,4},{3,5},{4,6},{5,7},{6,8},{7,9},{8,10},{9,11},{10,... | collective-permute-start | bytes 1572872 | tf_op jit(solution)/shard_map/ppermute | solution.py:27
  49.2 8.3 %collective-permute-start.17 = (bf16[2,2,128,128]{3,2,1,0:T(8,128)(2,1)S(1)}, bf16[2,2,128,128]{3,2,1,0:T(8,128)(2,1)S(1)}, u32[]{:S(2)}, u32[]{:S(2)}) collective-permute-start(bf16[2,2,128,128]{3,2,1,0:T(8,128)(2,1)S(1)} %shard_map.46), channel_id=1, source_target_pairs={{0,33},{1,0},{2,35},{3,2},{4,37},{5,4},{6,39},{7,6},{8,41},{9,8},{... | collective-permute-start | bytes 393224 | tf_op jit(solution)/shard_map/ppermute | solution.py:27
  50.5 8.0 %collective-permute-start.15 = (bf16[2,2,64,1024]{3,2,1,0:T(8,128)(2,1)S(1)}, bf16[2,2,64,1024]{3,2,1,0:T(8,128)(2,1)S(1)}, u32[]{:S(2)}, u32[]{:S(2)}) collective-permute-start(bf16[2,2,64,1024]{3,2,1,0:T(8,128)(2,1)S(1)} %collective-permute-done.5.refs_2_.refs_5_.refs_0_), channel_id=1, source_target_pairs={{0,16},{1,17},{2,18},{3,19},{4,20},{5,21},{6,22},{7,23},{8,24},{9,... | collective-permute-start | bytes 1572872 | tf_op jit(solution)/shard_map/ppermute | solution.py:27
  53.3 5.2 %collective-permute-start.14 = (bf16[2,2,64,1024]{3,2,1,0:T(8,128)(2,1)S(1)}, bf16[2,2,64,1024]{3,2,1,0:T(8,128)(2,1)S(1)}, u32[]{:S(2)}, u32[]{:S(2)}) collective-permute-start(bf16[2,2,64,1024]{3,2,1,0:T(8,128)(2,1)S(1)} %collective-permute-done.11.refs_4_.refs_13_.refs_3_), channel_id=1, source_target_pairs={{0,16},{1,17},{2,18},{3,19},{4,20},{5,21},{6,22},{7,23},{8,24},{9,... | collective-permute-start | bytes 1572872 | tf_op jit(solution)/shard_map/ppermute | solution.py:27
  57.6 2.5 %collective-permute-start.18 = (bf16[2,2,64,1024]{3,2,1,0:T(8,128)(2,1)S(1)}, bf16[2,2,64,1024]{3,2,1,0:T(8,128)(2,1)S(1)}, u32[]{:S(2)}, u32[]{:S(2)}) collective-permute-start(bf16[2,2,64,1024]{3,2,1,0:T(8,128)(2,1)S(1)} %collective-permute-done.16.refs_7_.refs_2_), channel_id=1, source_target_pairs={{0,16},{1,17},{2,18},{3,19},{4,20},{5,21},{6,22},{7,23},{8,24},{9,... | collective-permute-start | bytes 1572872 | tf_op jit(solution)/shard_map/ppermute | solution.py:27
  60.7 10.1 %collective-permute-start.19 = (bf16[3,2,128,128]{3,2,1,0:T(8,128)(2,1)S(1)}, bf16[3,2,128,128]{3,2,1,0:T(8,128)(2,1)S(1)}, u32[]{:S(2)}, u32[]{:S(2)}) collective-permute-start(bf16[3,2,128,128]{3,2,1,0:T(8,128)(2,1)S(1)} %shard_map.48), channel_id=1, source_target_pairs={{0,33},{1,0},{2,35},{3,2},{4,37},{5,4},{6,39},{7,6},{8,41},{9,8},{... | collective-permute-start | bytes 589832 | tf_op jit(solution)/shard_map/ppermute | solution.py:27
  64.4 14.1 %collective-permute-start.22 = (bf16[2,64,1024]{2,1,0:T(8,128)(2,1)S(1)}, bf16[2,64,1024]{2,1,0:T(8,128)(2,1)S(1)}, u32[]{:S(2)}, u32[]{:S(2)}) collective-permute-start(bf16[2,64,1024]{2,1,0:T(8,128)(2,1)S(1)} %get-tuple-element.28), channel_id=1, source_target_pairs={{0,128},{1,112},{2,130},{3,114},{4,132},{5,116},{6,134},{7,118},{8... | collective-permute-start | bytes 786440 | tf_op jit(solution)/shard_map/ppermute | solution.py:27
  71.6 6.2 %collective-permute-start.21 = (f32[1,128]{1,0:T(1,128)S(1)}, f32[1,128]{1,0:T(1,128)S(1)}, u32[]{:S(2)}, u32[]{:S(2)}) collective-permute-start(f32[1,128]{1,0:T(1,128)S(1)} %shard_map.49), channel_id=1, source_target_pairs={{0,129},{1,113},{2,131},{3,115},{4,133},{5,117},{6,135},{7,119},{8... | collective-permute-start | bytes 1544 | tf_op jit(solution)/shard_map/ppermute | solution.py:27
  71.6 6.9 %collective-permute-start.20 = (f32[1,128]{1,0:T(1,128)S(1)}, f32[1,128]{1,0:T(1,128)S(1)}, u32[]{:S(2)}, u32[]{:S(2)}) collective-permute-start(f32[1,128]{1,0:T(1,128)S(1)} %shard_map.49), channel_id=1, source_target_pairs={{0,128},{1,112},{2,130},{3,114},{4,132},{5,116},{6,134},{7,118},{8... | collective-permute-start | bytes 1544 | tf_op jit(solution)/shard_map/ppermute | solution.py:27
  77.8 9.2 %collective-permute-start.23 = (bf16[2,64,1024]{2,1,0:T(8,128)(2,1)S(1)}, bf16[2,64,1024]{2,1,0:T(8,128)(2,1)S(1)}, u32[]{:S(2)}, u32[]{:S(2)}) collective-permute-start(bf16[2,64,1024]{2,1,0:T(8,128)(2,1)S(1)} %get-tuple-element.30), channel_id=1, source_target_pairs={{0,129},{1,113},{2,131},{3,115},{4,133},{5,117},{6,135},{7,119},{8... | collective-permute-start | bytes 786440 | tf_op jit(solution)/shard_map/ppermute | solution.py:27
  78.5 3.9 %collective-permute-start.26 = (f32[2,128]{1,0:T(2,128)S(1)}, f32[2,128]{1,0:T(2,128)S(1)}, u32[]{:S(2)}, u32[]{:S(2)}) collective-permute-start(f32[2,128]{1,0:T(2,128)S(1)} %maximum_select_fusion.1), channel_id=1, source_target_pairs={{0,2},{1,3},{2,4},{3,5},{4,6},{5,7},{6,8},{7,9},{8,10},{9,11},{10,... | collective-permute-start | bytes 3080 | tf_op jit(solution)/shard_map/ppermute | solution.py:27
  78.6 3.8 %collective-permute-start.24 = (f32[2,128]{1,0:T(2,128)S(1)}, f32[2,128]{1,0:T(2,128)S(1)}, u32[]{:S(2)}, u32[]{:S(2)}) collective-permute-start(f32[2,128]{1,0:T(2,128)S(1)} %maximum_select_fusion.1), channel_id=1, source_target_pairs={{0,14},{1,15},{2,0},{3,1},{4,2},{5,3},{6,4},{7,5},{8,6},{9,7},{10,... | collective-permute-start | bytes 3080 | tf_op jit(solution)/shard_map/ppermute | solution.py:27
  82.4 5.5 %collective-permute-start.25 = (f32[2,128]{1,0:T(2,128)S(1)}, f32[2,128]{1,0:T(2,128)S(1)}, u32[]{:S(2)}, u32[]{:S(2)}) collective-permute-start(f32[2,128]{1,0:T(2,128)S(1)} %get-tuple-element.36), channel_id=1, source_target_pairs={{0,6},{1,7},{2,8},{3,9},{4,10},{5,11},{6,12},{7,13},{8,14},{9,15},... | collective-permute-start | bytes 3080 | tf_op jit(solution)/shard_map/ppermute | solution.py:27
  86.8 4.2 %collective-permute-start.27 = (f32[2,128]{1,0:T(2,128)S(1)}, f32[2,128]{1,0:T(2,128)S(1)}, u32[]{:S(2)}, u32[]{:S(2)}) collective-permute-start(f32[2,128]{1,0:T(2,128)S(1)} %get-tuple-element.37), channel_id=1, source_target_pairs={{0,10},{1,11},{2,12},{3,13},{4,14},{5,15},{6,0},{7,1},{8,2},{9,3},... | collective-permute-start | bytes 3080 | tf_op jit(solution)/shard_map/ppermute | solution.py:27

commit v16 on v15

--- a/solution.py
+++ b/solution.py
@@ -31,8 +31,8 @@
     return (m, c, z + (1 if c == 0 else -1), h)
 
 
-def along(step):
-    return lambda m, c, z, h: (m, c, z + step, h)
+def across(distance):
+    return lambda m, c, z, h: (m, c, z ^ distance, h)
 
 
 def other_core(m, c, z, h):
@@ -241,10 +241,9 @@
     first, second = moved(trace, from_hub(0)), moved(trace, from_hub(1))
     both = jnp.where(half == 0, jnp.concatenate([first, second]), jnp.concatenate([second, first]))
     both, kept = wall((both, kept))
-    below, above = moved(both, along(1)), moved(both, along(-1))
-    two, three = both + above, below + both + above
-    below, above = moved(two, along(3)), moved(three, along(-3))
-    both = below + three + above
+    both, sent = wall((both + moved(both, across(1)), sent))
+    both = both + moved(both, across(2))
+    both = both + moved(both, across(4))
     products = jnp.where(half == 0, jnp.stack([kept, sent]), jnp.stack([sent, kept]))[:, None, None]
     correlator = jnp.sum(both[:, :16].reshape(2, 8, 2), axis=1)[:, None, None, :] / F32(1024)
     return products, correlator

time: 92.4 us -> 96 us (1.039)
  the two profiles are of different devices: /device:TPU:1 before, /device:TPU:30 now
where the time goes in v16:
time: 96 us; the launch traced here: 95.9 us
  waiting for transfers between devices  60.3 us (63%)
  starting transfers between devices  24.3 us (25%)
  Pallas kernels  8.82 us (9%)
  other arithmetic  1.55 us (2%)
    ppermute x27, waiting for transfers between devices, moved(): lax.ppermute(block, BOTH, [(index_of(*at), index_of(*route(*at))) for at...  60.3 us
    ppermute x27, starting transfers between devices, moved(): lax.ppermute(block, BOTH, [(index_of(*at), index_of(*route(*at))) for at...  24.3 us
    pallas_call x9, Pallas kernels, call(): pl.pallas_call(kernel, out_shape=out_shape, in_specs=[SMEM] + [VMEM] * le...  8.82 us
  transfers between devices with their start and end apart: 27, of which 16 were waited for; matrix products, arithmetic and copies ran while one was open for 1% of the time, Pallas kernels for 8%

profile of v16, /device:TPU:30, one launch (start us, length us, event | category | flops | bytes accessed | tf_op | source)
XLA Modules:
  0.0 95.9 jit_solution(84598000183443448)
XLA Ops:
  0.6 0.0 copy-start
  0.6 0.3 collective-permute-start
  0.9 9.8 %collective-permute-done.own.refs_2_.refs_0_ = bf16[2,2,64,1024]{3,2,1,0:T(8,128)(2,1)S(1)} collective-permute-done((bf16[2,2,64,1024]{3,2,1,0:T(8,128)(2,1)}, bf16[2,2,64,1024]{3,2,1,0:T(8,128)(2,1)S(1)}, u32[]{:S(2)}, u32[]{:S(2)}) %collective-permute-start) | collective-permute-done | bytes 524320 | tf_op jit(solution)/shard_map/ppermute | solution.py:27
  10.8 0.0 collective-permute-start.3
  10.8 1.9 %collective-permute-start.1 = (bf16[2,2,64,1024]{3,2,1,0:T(8,128)(2,1)S(1)}, bf16[2,2,64,1024]{3,2,1,0:T(8,128)(2,1)S(1)}, u32[]{:S(2)}, u32[]{:S(2)}) collective-permute-start(bf16[2,2,64,1024]{3,2,1,0:T(8,128)(2,1)S(1)} %collective-permute-done.own.refs_2_.refs_0_), channel_id=1, source_target_pairs={{0,2},{1,3},{2,4},{3,5},{4,6},{5,7},{6,8},{7,9},{8,10},{9,11},{10,... | collective-permute-start | bytes 1572872 | tf_op jit(solution)/shard_map/ppermute | solution.py:27
  12.7 0.0 collective-permute-done.3.other.refs_3_.refs_8_
  12.7 2.0 %collective-permute-start.6 = (bf16[2,2,64,1024]{3,2,1,0:T(8,128)(2,1)S(1)}, bf16[2,2,64,1024]{3,2,1,0:T(8,128)(2,1)S(1)}, u32[]{:S(2)}, u32[]{:S(2)}) collective-permute-start(bf16[2,2,64,1024]{3,2,1,0:T(8,128)(2,1)S(1)} %collective-permute-done.3.other.refs_3_.refs_8_), channel_id=1, source_target_pairs={{0,2},{1,3},{2,4},{3,5},{4,6},{5,7},{6,8},{7,9},{8,10},{9,11},{10,... | collective-permute-start | bytes 1572872 | tf_op jit(solution)/shard_map/ppermute | solution.py:27
  14.7 0.1 pad_add_fusion.info.refs_0_
  14.7 0.6 shard_map.41
  15.3 0.1 collective-permute-start.4
  15.4 8.3 %collective-permute-done.1.refs_1_.refs_2_ = bf16[2,2,64,1024]{3,2,1,0:T(8,128)(2,1)S(1)} collective-permute-done((bf16[2,2,64,1024]{3,2,1,0:T(8,128)(2,1)S(1)}, bf16[2,2,64,1024]{3,2,1,0:T(8,128)(2,1)S(1)}, u32[]{:S(2)}, u32[]{:S(2)}) %collective-permute-start.1) | collective-permute-done | bytes 524320 | tf_op jit(solution)/shard_map/ppermute | solution.py:27
  23.8 0.0 collective-permute-start.2
  23.8 2.6 %collective-permute-start.8 = (bf16[2,2,64,1024]{3,2,1,0:T(8,128)(2,1)S(1)}, bf16[2,2,64,1024]{3,2,1,0:T(8,128)(2,1)S(1)}, u32[]{:S(2)}, u32[]{:S(2)}) collective-permute-start(bf16[2,2,64,1024]{3,2,1,0:T(8,128)(2,1)S(1)} %collective-permute-done.1.refs_1_.refs_2_), channel_id=1, source_target_pairs={{0,16},{1,17},{2,18},{3,19},{4,20},{5,21},{6,22},{7,23},{8,24},{9,... | collective-permute-start | bytes 1572872 | tf_op jit(solution)/shard_map/ppermute | solution.py:27
  26.4 3.0 %collective-permute-done.6.refs_4_.refs_6_.refs_9_ = bf16[2,2,64,1024]{3,2,1,0:T(8,128)(2,1)S(1)} collective-permute-done((bf16[2,2,64,1024]{3,2,1,0:T(8,128)(2,1)S(1)}, bf16[2,2,64,1024]{3,2,1,0:T(8,128)(2,1)S(1)}, u32[]{:S(2)}, u32[]{:S(2)}) %collective-permute-start.6) | collective-permute-done | bytes 524320 | tf_op jit(solution)/shard_map/ppermute | solution.py:27
  29.4 0.0 collective-permute-start.10
  29.4 2.3 %collective-permute-start.7 = (bf16[2,2,64,1024]{3,2,1,0:T(8,128)(2,1)S(1)}, bf16[2,2,64,1024]{3,2,1,0:T(8,128)(2,1)S(1)}, u32[]{:S(2)}, u32[]{:S(2)}) collective-permute-start(bf16[2,2,64,1024]{3,2,1,0:T(8,128)(2,1)S(1)} %collective-permute-done.6.refs_4_.refs_6_.refs_9_), channel_id=1, source_target_pairs={{0,16},{1,17},{2,18},{3,19},{4,20},{5,21},{6,22},{7,23},{8,24},{9,... | collective-permute-start | bytes 1572872 | tf_op jit(solution)/shard_map/ppermute | solution.py:27
  31.7 0.0 collective-permute-done.4.refs_1_.a_ref
  31.7 0.8 shard_map.42.refs_10_
  32.6 2.4 %collective-permute-done.2.refs_4_.refs_0_.refs_3_ = bf16[2,2,64,1024]{3,2,1,0:T(8,128)(2,1)S(1)} collective-permute-done((bf16[2,2,64,1024]{3,2,1,0:T(8,128)(2,1)S(1)}, bf16[2,2,64,1024]{3,2,1,0:T(8,128)(2,1)S(1)}, u32[]{:S(2)}, u32[]{:S(2)}) %collective-permute-start.2) | collective-permute-done | bytes 524320 | tf_op jit(solution)/shard_map/ppermute | solution.py:27
  35.0 0.0 collective-permute-start.5
  35.0 0.0 collective-permute-done.8.refs_5_.refs_7_.refs_10_
  35.0 0.0 collective-permute-done.7.refs_2_.refs_3_
  35.0 0.7 shard_map.43
  35.7 0.1 collective-permute-start.9
  35.8 2.6 %collective-permute-start.13 = (bf16[2,2,64,1024]{3,2,1,0:T(8,128)(2,1)S(1)}, bf16[2,2,64,1024]{3,2,1,0:T(8,128)(2,1)S(1)}, u32[]{:S(2)}, u32[]{:S(2)}) collective-permute-start(bf16[2,2,64,1024]{3,2,1,0:T(8,128)(2,1)S(1)} %collective-permute-done.2.refs_4_.refs_0_.refs_3_), channel_id=1, source_target_pairs={{0,16},{1,17},{2,18},{3,19},{4,20},{5,21},{6,22},{7,23},{8,24},{9,... | collective-permute-start | bytes 1572872 | tf_op jit(solution)/shard_map/ppermute | solution.py:27
  38.4 2.2 %collective-permute-done.10.refs_8_.refs_2_.refs_11_ = bf16[2,2,64,1024]{3,2,1,0:T(8,128)(2,1)S(1)} collective-permute-done((bf16[2,2,64,1024]{3,2,1,0:T(8,128)(2,1)S(1)}, bf16[2,2,64,1024]{3,2,1,0:T(8,128)(2,1)S(1)}, u32[]{:S(2)}, u32[]{:S(2)}) %collective-permute-start.10) | collective-permute-done | bytes 524320 | tf_op jit(solution)/shard_map/ppermute | solution.py:27
  40.6 0.0 collective-permute-start.12
  40.6 0.0 collective-permute-start.11
  40.6 5.6 %collective-permute-done.5.refs_2_.refs_5_.refs_0_ = bf16[2,2,64,1024]{3,2,1,0:T(8,128)(2,1)S(1)} collective-permute-done((bf16[2,2,64,1024]{3,2,1,0:T(8,128)(2,1)S(1)}, bf16[2,2,64,1024]{3,2,1,0:T(8,128)(2,1)S(1)}, u32[]{:S(2)}, u32[]{:S(2)}) %collective-permute-start.5) | collective-permute-done | bytes 524320 | tf_op jit(solution)/shard_map/ppermute | solution.py:27
  46.2 0.0 collective-permute-done.9.near
  46.2 0.0 collective-permute-start.16
  46.2 0.0 collective-permute-done.13.refs_9_.refs_3_.refs_12_
  46.3 0.0 collective-permute-done.12.refs_5_.refs_1_.refs_4_
  46.3 0.6 shard_map.46
  46.9 0.1 collective-permute-start.17
  47.0 2.6 %collective-permute-start.15 = (bf16[2,2,64,1024]{3,2,1,0:T(8,128)(2,1)S(1)}, bf16[2,2,64,1024]{3,2,1,0:T(8,128)(2,1)S(1)}, u32[]{:S(2)}, u32[]{:S(2)}) collective-permute-start(bf16[2,2,64,1024]{3,2,1,0:T(8,128)(2,1)S(1)} %collective-permute-done.5.refs_2_.refs_5_.refs_0_), channel_id=1, source_target_pairs={{0,16},{1,17},{2,18},{3,19},{4,20},{5,21},{6,22},{7,23},{8,24},{9,... | collective-permute-start | bytes 1572872 | tf_op jit(solution)/shard_map/ppermute | solution.py:27
  49.6 1.3 %shard_map.44.refs_6_ = f32[256,1024]{1,0:T(8,128)S(1)} custom-call(s32[6]{0:T(128)S(1)} %pad_add_fusion.info.refs_0_, bf16[2,128,1024]{2,1,0:T(8,128)(2,1)S(1)} %collective-permute-done.4.refs_1_.a_ref, bf16[2,2,64,1024]{3,2,1,0:T(8,128)(2,1)S(1)} %collective-permute-done.1.refs_1_.refs_2_, ...), custom_call_target="tpu_custom_call" | custom-call | flops 1 | bytes 1048576 | tf_op jit(solution)/shard_map/pallas_call | solution.py:75
  50.9 1.0 %collective-permute-done.11.refs_4_.refs_13_.refs_3_ = bf16[2,2,64,1024]{3,2,1,0:T(8,128)(2,1)S(1)} collective-permute-done((bf16[2,2,64,1024]{3,2,1,0:T(8,128)(2,1)S(1)}, bf16[2,2,64,1024]{3,2,1,0:T(8,128)(2,1)S(1)}, u32[]{:S(2)}, u32[]{:S(2)}) %collective-permute-start.11) | collective-permute-done | bytes 524320 | tf_op jit(solution)/shard_map/ppermute | solution.py:27
  51.9 0.0 collective-permute-start.14
  51.9 1.6 %collective-permute-done.17.middle = bf16[2,2,128,128]{3,2,1,0:T(8,128)(2,1)S(1)} collective-permute-done((bf16[2,2,128,128]{3,2,1,0:T(8,128)(2,1)S(1)}, bf16[2,2,128,128]{3,2,1,0:T(8,128)(2,1)S(1)}, u32[]{:S(2)}, u32[]{:S(2)}) %collective-permute-start.17) | collective-permute-done | bytes 131104 | tf_op jit(solution)/shard_map/ppermute | solution.py:27
  53.5 4.0 %collective-permute-done.16.refs_7_.refs_2_ = bf16[2,2,64,1024]{3,2,1,0:T(8,128)(2,1)S(1)} collective-permute-done((bf16[2,2,64,1024]{3,2,1,0:T(8,128)(2,1)S(1)}, bf16[2,2,64,1024]{3,2,1,0:T(8,128)(2,1)S(1)}, u32[]{:S(2)}, u32[]{:S(2)}) %collective-permute-start.16) | collective-permute-done | bytes 524320 | tf_op jit(solution)/shard_map/ppermute | solution.py:27
  57.5 1.0 %shard_map.45.acc = f32[256,1024]{1,0:T(8,128)S(1)} custom-call(s32[6]{0:T(128)S(1)} %pad_add_fusion.info.refs_0_, bf16[2,128,1024]{2,1,0:T(8,128)(2,1)S(1)} %collective-permute-done.4.refs_1_.a_ref, bf16[2,2,64,1024]{3,2,1,0:T(8,128)(2,1)S(1)} %collective-permute-done.5.refs_2_.refs_5_.refs_0_, ...), custom_call_target="tpu_custom_call" | custom-call | flops 1 | bytes 1048576 | tf_op jit(solution)/shard_map/pallas_call | solution.py:75
  58.5 0.9 collective-permute-done.18.refs_15_.refs_5_
  59.4 0.7 shard_map.48
  60.1 0.1 collective-permute-start.19
  60.2 2.4 %shard_map.47 = (bf16[2,64,1024]{2,1,0:T(8,128)(2,1)S(1)}, bf16[2,64,1024]{2,1,0:T(8,128)(2,1)S(1)}, f32[256,1024]{1,0:T(8,128)S(1)}, f32[8,128]{1,0:T(8,128)S(1)}) custom-call(s32[6]{0:T(128)S(1)} %pad_add_fusion.info.refs_0_, bf16[2,128,1024]{2,1,0:T(8,128)(2,1)S(1)} %collective-permute-done.4.refs_1_.a_ref, f32[256,1024]{1,0:T(8,128)S(1)} %shard_map.45.acc, ...), custom_call_target="tpu_custom_call" | custom-call | flops 3000000000 | bytes 1048576 | tf_op jit(solution)/shard_map/pallas_call | solution.py:75
  62.5 1.1 %collective-permute-start.22 = (bf16[2,64,1024]{2,1,0:T(8,128)(2,1)S(1)}, bf16[2,64,1024]{2,1,0:T(8,128)(2,1)S(1)}, u32[]{:S(2)}, u32[]{:S(2)}) collective-permute-start(bf16[2,64,1024]{2,1,0:T(8,128)(2,1)S(1)} %get-tuple-element.30), channel_id=1, source_target_pairs={{0,128},{1,112},{2,130},{3,114},{4,132},{5,116},{6,134},{7,118},{8... | collective-permute-start | bytes 786440 | tf_op jit(solution)/shard_map/ppermute | solution.py:27
  63.7 0.4 collective-permute-start.24
  64.1 3.2 %collective-permute-done.19.late = bf16[3,2,128,128]{3,2,1,0:T(8,128)(2,1)S(1)} collective-permute-done((bf16[3,2,128,128]{3,2,1,0:T(8,128)(2,1)S(1)}, bf16[3,2,128,128]{3,2,1,0:T(8,128)(2,1)S(1)}, u32[]{:S(2)}, u32[]{:S(2)}) %collective-permute-start.19) | collective-permute-done | bytes 196640 | tf_op jit(solution)/shard_map/ppermute | solution.py:27
  67.3 0.7 shard_map.49
  68.1 1.0 %collective-permute-start.21 = (f32[1,128]{1,0:T(1,128)S(1)}, f32[1,128]{1,0:T(1,128)S(1)}, u32[]{:S(2)}, u32[]{:S(2)}) collective-permute-start(f32[1,128]{1,0:T(1,128)S(1)} %shard_map.49), channel_id=1, source_target_pairs={{0,129},{1,113},{2,131},{3,115},{4,133},{5,117},{6,135},{7,119},{8... | collective-permute-start | bytes 1544 | tf_op jit(solution)/shard_map/ppermute | solution.py:27
  69.1 2.2 %collective-permute-start.20 = (f32[1,128]{1,0:T(1,128)S(1)}, f32[1,128]{1,0:T(1,128)S(1)}, u32[]{:S(2)}, u32[]{:S(2)}) collective-permute-start(f32[1,128]{1,0:T(1,128)S(1)} %shard_map.49), channel_id=1, source_target_pairs={{0,128},{1,112},{2,130},{3,114},{4,132},{5,116},{6,134},{7,118},{8... | collective-permute-start | bytes 1544 | tf_op jit(solution)/shard_map/ppermute | solution.py:27
  71.3 3.7 %collective-permute-done.21 = f32[1,128]{1,0:T(1,128)S(1)} collective-permute-done((f32[1,128]{1,0:T(1,128)S(1)}, f32[1,128]{1,0:T(1,128)S(1)}, u32[]{:S(2)}, u32[]{:S(2)}) %collective-permute-start.21) | collective-permute-done | bytes 544 | tf_op jit(solution)/shard_map/ppermute | solution.py:27
  75.0 4.5 %collective-permute-done.20 = f32[1,128]{1,0:T(1,128)S(1)} collective-permute-done((f32[1,128]{1,0:T(1,128)S(1)}, f32[1,128]{1,0:T(1,128)S(1)}, u32[]{:S(2)}, u32[]{:S(2)}) %collective-permute-start.20) | collective-permute-done | bytes 544 | tf_op jit(solution)/shard_map/ppermute | solution.py:27
  79.6 0.1 collective-permute-start.23
  79.7 3.6 %collective-permute-done.23 = f32[2,128]{1,0:T(2,128)S(1)} collective-permute-done((f32[2,128]{1,0:T(2,128)S(1)}, f32[2,128]{1,0:T(2,128)S(1)}, u32[]{:S(2)}, u32[]{:S(2)}) %collective-permute-start.23) | collective-permute-done | bytes 1056 | tf_op jit(solution)/shard_map/ppermute | solution.py:27
  83.3 0.0 collective-permute-done.24
  83.3 0.3 collective-permute-start.25
  83.5 4.2 %collective-permute-done.25 = f32[2,128]{1,0:T(2,128)S(1)} collective-permute-done((f32[2,128]{1,0:T(2,128)S(1)}, f32[2,128]{1,0:T(2,128)S(1)}, u32[]{:S(2)}, u32[]{:S(2)}) %collective-permute-start.25) | collective-permute-done | bytes 1056 | tf_op jit(solution)/shard_map/ppermute | solution.py:27
  87.7 4.6 %collective-permute-start.26 = (f32[2,128]{1,0:T(2,128)S(1)}, f32[2,128]{1,0:T(2,128)S(1)}, u32[]{:S(2)}, u32[]{:S(2)}) collective-permute-start(f32[2,128]{1,0:T(2,128)S(1)} %add.25), channel_id=1, source_target_pairs={{0,8},{1,9},{2,10},{3,11},{4,12},{5,13},{6,14},{7,15},{8,0},{9,1},... | collective-permute-start | bytes 3080 | tf_op jit(solution)/shard_map/ppermute | solution.py:27
  92.3 0.9 maximum_select_fusion
  93.2 2.1 %collective-permute-done.26 = f32[2,128]{1,0:T(2,128)S(1)} collective-permute-done((f32[2,128]{1,0:T(2,128)S(1)}, f32[2,128]{1,0:T(2,128)S(1)}, u32[]{:S(2)}, u32[]{:S(2)}) %collective-permute-start.26) | collective-permute-done | bytes 1056 | tf_op jit(solution)/shard_map/ppermute | solution.py:27
  95.2 0.1 reshape.77
  95.3 0.6 broadcast_multiply_fusion
  (11 shorter events, 0.1 us)
Async XLA Ops:
  0.6 12.0 %copy-start = (s32[2,1,4]{2,1,0:T(1,128)S(1)}, s32[2,1,4]{2,1,0:T(1,128)}, u32[]{:S(2)}) copy-start(s32[2,1,4]{2,1,0:T(1,128)} %param.3) | copy-start | bytes 100
  0.6 10.1 %collective-permute-start = (bf16[2,2,64,1024]{3,2,1,0:T(8,128)(2,1)}, bf16[2,2,64,1024]{3,2,1,0:T(8,128)(2,1)S(1)}, u32[]{:S(2)}, u32[]{:S(2)}) collective-permute-start(bf16[2,2,64,1024]{3,2,1,0:T(8,128)(2,1)} %bitcast.15), channel_id=1, source_target_pairs={{0,128},{1,144},{2,130},{3,146},{4,132},{5,148},{6,134},{7,150},{8... | collective-permute-start | bytes 1572872 | tf_op jit(solution)/shard_map/ppermute | solution.py:27
  10.8 1.9 %collective-permute-start.3 = (bf16[2,2,64,1024]{3,2,1,0:T(8,128)(2,1)S(1)}, bf16[2,2,64,1024]{3,2,1,0:T(8,128)(2,1)S(1)}, u32[]{:S(2)}, u32[]{:S(2)}) collective-permute-start(bf16[2,2,64,1024]{3,2,1,0:T(8,128)(2,1)S(1)} %collective-permute-done.own.refs_2_.refs_0_), channel_id=1, source_target_pairs={{0,16},{1,17},{2,18},{3,19},{4,20},{5,21},{6,22},{7,23},{8,24},{9,... | collective-permute-start | bytes 1572872 | tf_op jit(solution)/shard_map/ppermute | solution.py:27
  10.8 13.0 %collective-permute-start.1 = (bf16[2,2,64,1024]{3,2,1,0:T(8,128)(2,1)S(1)}, bf16[2,2,64,1024]{3,2,1,0:T(8,128)(2,1)S(1)}, u32[]{:S(2)}, u32[]{:S(2)}) collective-permute-start(bf16[2,2,64,1024]{3,2,1,0:T(8,128)(2,1)S(1)} %collective-permute-done.own.refs_2_.refs_0_), channel_id=1, source_target_pairs={{0,2},{1,3},{2,4},{3,5},{4,6},{5,7},{6,8},{7,9},{8,10},{9,11},{10,... | collective-permute-start | bytes 1572872 | tf_op jit(solution)/shard_map/ppermute | solution.py:27
  12.7 16.7 %collective-permute-start.6 = (bf16[2,2,64,1024]{3,2,1,0:T(8,128)(2,1)S(1)}, bf16[2,2,64,1024]{3,2,1,0:T(8,128)(2,1)S(1)}, u32[]{:S(2)}, u32[]{:S(2)}) collective-permute-start(bf16[2,2,64,1024]{3,2,1,0:T(8,128)(2,1)S(1)} %collective-permute-done.3.other.refs_3_.refs_8_), channel_id=1, source_target_pairs={{0,2},{1,3},{2,4},{3,5},{4,6},{5,7},{6,8},{7,9},{8,10},{9,11},{10,... | collective-permute-start | bytes 1572872 | tf_op jit(solution)/shard_map/ppermute | solution.py:27
  15.3 16.4 %collective-permute-start.4 = (bf16[2,128,1024]{2,1,0:T(8,128)(2,1)S(1)}, bf16[2,128,1024]{2,1,0:T(8,128)(2,1)S(1)}, u32[]{:S(2)}, u32[]{:S(2)}) collective-permute-start(bf16[2,128,1024]{2,1,0:T(8,128)(2,1)S(1)} %shard_map.41), channel_id=1, source_target_pairs={{0,33},{1,0},{2,35},{3,2},{4,37},{5,4},{6,39},{7,6},{8,41},{9,8},{... | collective-permute-start | bytes 1572872 | tf_op jit(solution)/shard_map/ppermute | solution.py:27
  23.8 11.2 %collective-permute-start.2 = (bf16[2,2,64,1024]{3,2,1,0:T(8,128)(2,1)S(1)}, bf16[2,2,64,1024]{3,2,1,0:T(8,128)(2,1)S(1)}, u32[]{:S(2)}, u32[]{:S(2)}) collective-permute-start(bf16[2,2,64,1024]{3,2,1,0:T(8,128)(2,1)S(1)} %collective-permute-done.1.refs_1_.refs_2_), channel_id=1, source_target_pairs={{0,2},{1,3},{2,4},{3,5},{4,6},{5,7},{6,8},{7,9},{8,10},{9,11},{10,... | collective-permute-start | bytes 1572872 | tf_op jit(solution)/shard_map/ppermute | solution.py:27
  23.8 11.2 %collective-permute-start.8 = (bf16[2,2,64,1024]{3,2,1,0:T(8,128)(2,1)S(1)}, bf16[2,2,64,1024]{3,2,1,0:T(8,128)(2,1)S(1)}, u32[]{:S(2)}, u32[]{:S(2)}) collective-permute-start(bf16[2,2,64,1024]{3,2,1,0:T(8,128)(2,1)S(1)} %collective-permute-done.1.refs_1_.refs_2_), channel_id=1, source_target_pairs={{0,16},{1,17},{2,18},{3,19},{4,20},{5,21},{6,22},{7,23},{8,24},{9,... | collective-permute-start | bytes 1572872 | tf_op jit(solution)/shard_map/ppermute | solution.py:27
  29.4 11.2 %collective-permute-start.10 = (bf16[2,2,64,1024]{3,2,1,0:T(8,128)(2,1)S(1)}, bf16[2,2,64,1024]{3,2,1,0:T(8,128)(2,1)S(1)}, u32[]{:S(2)}, u32[]{:S(2)}) collective-permute-start(bf16[2,2,64,1024]{3,2,1,0:T(8,128)(2,1)S(1)} %collective-permute-done.6.refs_4_.refs_6_.refs_9_), channel_id=1, source_target_pairs={{0,2},{1,3},{2,4},{3,5},{4,6},{5,7},{6,8},{7,9},{8,10},{9,11},{10,... | collective-permute-start | bytes 1572872 | tf_op jit(solution)/shard_map/ppermute | solution.py:27
  29.4 5.6 %collective-permute-start.7 = (bf16[2,2,64,1024]{3,2,1,0:T(8,128)(2,1)S(1)}, bf16[2,2,64,1024]{3,2,1,0:T(8,128)(2,1)S(1)}, u32[]{:S(2)}, u32[]{:S(2)}) collective-permute-start(bf16[2,2,64,1024]{3,2,1,0:T(8,128)(2,1)S(1)} %collective-permute-done.6.refs_4_.refs_6_.refs_9_), channel_id=1, source_target_pairs={{0,16},{1,17},{2,18},{3,19},{4,20},{5,21},{6,22},{7,23},{8,24},{9,... | collective-permute-start | bytes 1572872 | tf_op jit(solution)/shard_map/ppermute | solution.py:27
  35.0 11.2 %collective-permute-start.5 = (bf16[2,2,64,1024]{3,2,1,0:T(8,128)(2,1)S(1)}, bf16[2,2,64,1024]{3,2,1,0:T(8,128)(2,1)S(1)}, u32[]{:S(2)}, u32[]{:S(2)}) collective-permute-start(bf16[2,2,64,1024]{3,2,1,0:T(8,128)(2,1)S(1)} %collective-permute-done.2.refs_4_.refs_0_.refs_3_), channel_id=1, source_target_pairs={{0,2},{1,3},{2,4},{3,5},{4,6},{5,7},{6,8},{7,9},{8,10},{9,11},{10,... | collective-permute-start | bytes 1572872 | tf_op jit(solution)/shard_map/ppermute | solution.py:27
  35.7 10.5 %collective-permute-start.9 = (bf16[3,2,128,128]{3,2,1,0:T(8,128)(2,1)S(1)}, bf16[3,2,128,128]{3,2,1,0:T(8,128)(2,1)S(1)}, u32[]{:S(2)}, u32[]{:S(2)}) collective-permute-start(bf16[3,2,128,128]{3,2,1,0:T(8,128)(2,1)S(1)} %shard_map.43), channel_id=1, source_target_pairs={{0,33},{1,0},{2,35},{3,2},{4,37},{5,4},{6,39},{7,6},{8,41},{9,8},{... | collective-permute-start | bytes 589832 | tf_op jit(solution)/shard_map/ppermute | solution.py:27
  35.8 10.4 %collective-permute-start.13 = (bf16[2,2,64,1024]{3,2,1,0:T(8,128)(2,1)S(1)}, bf16[2,2,64,1024]{3,2,1,0:T(8,128)(2,1)S(1)}, u32[]{:S(2)}, u32[]{:S(2)}) collective-permute-start(bf16[2,2,64,1024]{3,2,1,0:T(8,128)(2,1)S(1)} %collective-permute-done.2.refs_4_.refs_0_.refs_3_), channel_id=1, source_target_pairs={{0,16},{1,17},{2,18},{3,19},{4,20},{5,21},{6,22},{7,23},{8,24},{9,... | collective-permute-start | bytes 1572872 | tf_op jit(solution)/shard_map/ppermute | solution.py:27
  40.6 5.6 %collective-permute-start.12 = (bf16[2,2,64,1024]{3,2,1,0:T(8,128)(2,1)S(1)}, bf16[2,2,64,1024]{3,2,1,0:T(8,128)(2,1)S(1)}, u32[]{:S(2)}, u32[]{:S(2)}) collective-permute-start(bf16[2,2,64,1024]{3,2,1,0:T(8,128)(2,1)S(1)} %collective-permute-done.10.refs_8_.refs_2_.refs_11_), channel_id=1, source_target_pairs={{0,16},{1,17},{2,18},{3,19},{4,20},{5,21},{6,22},{7,23},{8,24},{9,... | collective-permute-start | bytes 1572872 | tf_op jit(solution)/shard_map/ppermute | solution.py:27
  40.6 11.2 %collective-permute-start.11 = (bf16[2,2,64,1024]{3,2,1,0:T(8,128)(2,1)S(1)}, bf16[2,2,64,1024]{3,2,1,0:T(8,128)(2,1)S(1)}, u32[]{:S(2)}, u32[]{:S(2)}) collective-permute-start(bf16[2,2,64,1024]{3,2,1,0:T(8,128)(2,1)S(1)} %collective-permute-done.10.refs_8_.refs_2_.refs_11_), channel_id=1, source_target_pairs={{0,2},{1,3},{2,4},{3,5},{4,6},{5,7},{6,8},{7,9},{8,10},{9,11},{10,... | collective-permute-start | bytes 1572872 | tf_op jit(solution)/shard_map/ppermute | solution.py:27
  46.2 11.2 %collective-permute-start.16 = (bf16[2,2,64,1024]{3,2,1,0:T(8,128)(2,1)S(1)}, bf16[2,2,64,1024]{3,2,1,0:T(8,128)(2,1)S(1)}, u32[]{:S(2)}, u32[]{:S(2)}) collective-permute-start(bf16[2,2,64,1024]{3,2,1,0:T(8,128)(2,1)S(1)} %collective-permute-done.5.refs_2_.refs_5_.refs_0_), channel_id=1, source_target_pairs={{0,2},{1,3},{2,4},{3,5},{4,6},{5,7},{6,8},{7,9},{8,10},{9,11},{10,... | collective-permute-start | bytes 1572872 | tf_op jit(solution)/shard_map/ppermute | solution.py:27
  46.9 6.5 %collective-permute-start.17 = (bf16[2,2,128,128]{3,2,1,0:T(8,128)(2,1)S(1)}, bf16[2,2,128,128]{3,2,1,0:T(8,128)(2,1)S(1)}, u32[]{:S(2)}, u32[]{:S(2)}) collective-permute-start(bf16[2,2,128,128]{3,2,1,0:T(8,128)(2,1)S(1)} %shard_map.46), channel_id=1, source_target_pairs={{0,33},{1,0},{2,35},{3,2},{4,37},{5,4},{6,39},{7,6},{8,41},{9,8},{... | collective-permute-start | bytes 393224 | tf_op jit(solution)/shard_map/ppermute | solution.py:27
  47.0 10.5 %collective-permute-start.15 = (bf16[2,2,64,1024]{3,2,1,0:T(8,128)(2,1)S(1)}, bf16[2,2,64,1024]{3,2,1,0:T(8,128)(2,1)S(1)}, u32[]{:S(2)}, u32[]{:S(2)}) collective-permute-start(bf16[2,2,64,1024]{3,2,1,0:T(8,128)(2,1)S(1)} %collective-permute-done.5.refs_2_.refs_5_.refs_0_), channel_id=1, source_target_pairs={{0,16},{1,17},{2,18},{3,19},{4,20},{5,21},{6,22},{7,23},{8,24},{9,... | collective-permute-start | bytes 1572872 | tf_op jit(solution)/shard_map/ppermute | solution.py:27
  51.9 5.6 %collective-permute-start.14 = (bf16[2,2,64,1024]{3,2,1,0:T(8,128)(2,1)S(1)}, bf16[2,2,64,1024]{3,2,1,0:T(8,128)(2,1)S(1)}, u32[]{:S(2)}, u32[]{:S(2)}) collective-permute-start(bf16[2,2,64,1024]{3,2,1,0:T(8,128)(2,1)S(1)} %collective-permute-done.11.refs_4_.refs_13_.refs_3_), channel_id=1, source_target_pairs={{0,16},{1,17},{2,18},{3,19},{4,20},{5,21},{6,22},{7,23},{8,24},{9,... | collective-permute-start | bytes 1572872 | tf_op jit(solution)/shard_map/ppermute | solution.py:27
  57.5 1.9 %collective-permute-start.18 = (bf16[2,2,64,1024]{3,2,1,0:T(8,128)(2,1)S(1)}, bf16[2,2,64,1024]{3,2,1,0:T(8,128)(2,1)S(1)}, u32[]{:S(2)}, u32[]{:S(2)}) collective-permute-start(bf16[2,2,64,1024]{3,2,1,0:T(8,128)(2,1)S(1)} %collective-permute-done.16.refs_7_.refs_2_), channel_id=1, source_target_pairs={{0,16},{1,17},{2,18},{3,19},{4,20},{5,21},{6,22},{7,23},{8,24},{9,... | collective-permute-start | bytes 1572872 | tf_op jit(solution)/shard_map/ppermute | solution.py:27
  60.1 7.3 %collective-permute-start.19 = (bf16[3,2,128,128]{3,2,1,0:T(8,128)(2,1)S(1)}, bf16[3,2,128,128]{3,2,1,0:T(8,128)(2,1)S(1)}, u32[]{:S(2)}, u32[]{:S(2)}) collective-permute-start(bf16[3,2,128,128]{3,2,1,0:T(8,128)(2,1)S(1)} %shard_map.48), channel_id=1, source_target_pairs={{0,33},{1,0},{2,35},{3,2},{4,37},{5,4},{6,39},{7,6},{8,41},{9,8},{... | collective-permute-start | bytes 589832 | tf_op jit(solution)/shard_map/ppermute | solution.py:27
  62.5 17.1 %collective-permute-start.22 = (bf16[2,64,1024]{2,1,0:T(8,128)(2,1)S(1)}, bf16[2,64,1024]{2,1,0:T(8,128)(2,1)S(1)}, u32[]{:S(2)}, u32[]{:S(2)}) collective-permute-start(bf16[2,64,1024]{2,1,0:T(8,128)(2,1)S(1)} %get-tuple-element.30), channel_id=1, source_target_pairs={{0,128},{1,112},{2,130},{3,114},{4,132},{5,116},{6,134},{7,118},{8... | collective-permute-start | bytes 786440 | tf_op jit(solution)/shard_map/ppermute | solution.py:27
  63.7 19.6 %collective-permute-start.24 = (bf16[2,64,1024]{2,1,0:T(8,128)(2,1)S(1)}, bf16[2,64,1024]{2,1,0:T(8,128)(2,1)S(1)}, u32[]{:S(2)}, u32[]{:S(2)}) collective-permute-start(bf16[2,64,1024]{2,1,0:T(8,128)(2,1)S(1)} %get-tuple-element.33), channel_id=1, source_target_pairs={{0,129},{1,113},{2,131},{3,115},{4,133},{5,117},{6,135},{7,119},{8... | collective-permute-start | bytes 786440 | tf_op jit(solution)/shard_map/ppermute | solution.py:27
  68.1 7.0 %collective-permute-start.21 = (f32[1,128]{1,0:T(1,128)S(1)}, f32[1,128]{1,0:T(1,128)S(1)}, u32[]{:S(2)}, u32[]{:S(2)}) collective-permute-start(f32[1,128]{1,0:T(1,128)S(1)} %shard_map.49), channel_id=1, source_target_pairs={{0,129},{1,113},{2,131},{3,115},{4,133},{5,117},{6,135},{7,119},{8... | collective-permute-start | bytes 1544 | tf_op jit(solution)/shard_map/ppermute | solution.py:27
  69.1 10.5 %collective-permute-start.20 = (f32[1,128]{1,0:T(1,128)S(1)}, f32[1,128]{1,0:T(1,128)S(1)}, u32[]{:S(2)}, u32[]{:S(2)}) collective-permute-start(f32[1,128]{1,0:T(1,128)S(1)} %shard_map.49), channel_id=1, source_target_pairs={{0,128},{1,112},{2,130},{3,114},{4,132},{5,116},{6,134},{7,118},{8... | collective-permute-start | bytes 1544 | tf_op jit(solution)/shard_map/ppermute | solution.py:27
  79.6 3.7 %collective-permute-start.23 = (f32[2,128]{1,0:T(2,128)S(1)}, f32[2,128]{1,0:T(2,128)S(1)}, u32[]{:S(2)}, u32[]{:S(2)}) collective-permute-start(f32[2,128]{1,0:T(2,128)S(1)} %maximum_select_fusion.1), channel_id=1, source_target_pairs={{0,2},{1,3},{2,0},{3,1},{4,6},{5,7},{6,4},{7,5},{8,10},{9,11},{10,... | collective-permute-start | bytes 3080 | tf_op jit(solution)/shard_map/ppermute | solution.py:27
  83.3 4.5 %collective-permute-start.25 = (f32[2,128]{1,0:T(2,128)S(1)}, f32[2,128]{1,0:T(2,128)S(1)}, u32[]{:S(2)}, u32[]{:S(2)}) collective-permute-start(f32[2,128]{1,0:T(2,128)S(1)} %add.24), channel_id=1, source_target_pairs={{0,4},{1,5},{2,6},{3,7},{4,0},{5,1},{6,2},{7,3},{8,12},{9,13},{10,... | collective-permute-start | bytes 3080 | tf_op jit(solution)/shard_map/ppermute | solution.py:27
  87.7 7.5 %collective-permute-start.26 = (f32[2,128]{1,0:T(2,128)S(1)}, f32[2,128]{1,0:T(2,128)S(1)}, u32[]{:S(2)}, u32[]{:S(2)}) collective-permute-start(f32[2,128]{1,0:T(2,128)S(1)} %add.25), channel_id=1, source_target_pairs={{0,8},{1,9},{2,10},{3,11},{4,12},{5,13},{6,14},{7,15},{8,0},{9,1},... | collective-permute-start | bytes 3080 | tf_op jit(solution)/shard_map/ppermute | solution.py:27

commit v17 on v15

--- a/solution.py
+++ b/solution.py
@@ -181,6 +181,11 @@
     trace[...] = jnp.where(lane == 2 * info[0], re, jnp.where(lane == 2 * info[0] + 1, im, 0.0))
 
 
+def add_kernel(info, below, own, above, two, three):
+    two[...] = own[...] + above[...]
+    three[...] = below[...] + own[...] + above[...]
+
+
 def shards(fields, mom_table):
     rows = fields[:, 0]
     tm, row = lax.axis_index("tm"), lax.axis_index("row")
@@ -242,7 +247,8 @@
     both = jnp.where(half == 0, jnp.concatenate([first, second]), jnp.concatenate([second, first]))
     both, kept = wall((both, kept))
     below, above = moved(both, along(1)), moved(both, along(-1))
-    two, three = both + above, below + both + above
+    pair = jax.ShapeDtypeStruct((2, 128), F32)
+    two, three = call(add_kernel, info, [below, both, above], (pair, pair), WEIGHT)
     below, above = moved(two, along(3)), moved(three, along(-3))
     both = below + three + above
     products = jnp.where(half == 0, jnp.stack([kept, sent]), jnp.stack([sent, kept]))[:, None, None]

time: 92.4 us -> 92.8 us (level); the launches traced: 91.7 us -> 91.2 us
    pallas_call x9 -> x10, Pallas kernels: 8.83 us -> 9.37 us  [call(): pl.pallas_call(kernel, out_shape=out_shape, in_specs=[SMEM] + [VMEM] * le...]
  transfers between devices with their start and end apart: 28 -> 28, of which waited for: 13 -> 13; matrix products, arithmetic and copies ran while one was open for 1% -> 1% of each run, Pallas kernels for 9% -> 10%
where the time goes in v17:
time: 92.8 us; the launch traced here: 91.2 us
  starting transfers between devices  50.3 us (54%)
  waiting for transfers between devices  29.1 us (31%)
  Pallas kernels  9.37 us (10%)
  other arithmetic  1.55 us (2%)
    ppermute x28, starting transfers between devices, moved(): lax.ppermute(block, BOTH, [(index_of(*at), index_of(*route(*at))) for at...  50.3 us
    ppermute x28, waiting for transfers between devices, moved(): lax.ppermute(block, BOTH, [(index_of(*at), index_of(*route(*at))) for at...  29.1 us
    pallas_call x10, Pallas kernels, call(): pl.pallas_call(kernel, out_shape=out_shape, in_specs=[SMEM] + [VMEM] * le...  9.37 us
  transfers between devices with their start and end apart: 28, of which 13 were waited for; matrix products, arithmetic and copies ran while one was open for 1% of the time, Pallas kernels for 10%

profile of v17, /device:TPU:1, one launch (start us, length us, event | category | flops | bytes accessed | tf_op | source)
XLA Modules:
  0.0 91.2 jit_solution(8763749978730501138)
XLA Ops:
  0.6 0.0 copy-start
  0.6 4.2 %collective-permute-start = (bf16[2,2,64,1024]{3,2,1,0:T(8,128)(2,1)}, bf16[2,2,64,1024]{3,2,1,0:T(8,128)(2,1)S(1)}, u32[]{:S(2)}, u32[]{:S(2)}) collective-permute-start(bf16[2,2,64,1024]{3,2,1,0:T(8,128)(2,1)} %bitcast.15), channel_id=1, source_target_pairs={{0,128},{1,144},{2,130},{3,146},{4,132},{5,148},{6,134},{7,150},{8... | collective-permute-start | bytes 1572872 | tf_op jit(solution)/shard_map/ppermute | solution.py:27
  4.8 6.4 %collective-permute-done.own.refs_2_.refs_0_ = bf16[2,2,64,1024]{3,2,1,0:T(8,128)(2,1)S(1)} collective-permute-done((bf16[2,2,64,1024]{3,2,1,0:T(8,128)(2,1)}, bf16[2,2,64,1024]{3,2,1,0:T(8,128)(2,1)S(1)}, u32[]{:S(2)}, u32[]{:S(2)}) %collective-permute-start) | collective-permute-done | bytes 524320 | tf_op jit(solution)/shard_map/ppermute | solution.py:27
  11.3 1.5 %collective-permute-start.3 = (bf16[2,2,64,1024]{3,2,1,0:T(8,128)(2,1)S(1)}, bf16[2,2,64,1024]{3,2,1,0:T(8,128)(2,1)S(1)}, u32[]{:S(2)}, u32[]{:S(2)}) collective-permute-start(bf16[2,2,64,1024]{3,2,1,0:T(8,128)(2,1)S(1)} %collective-permute-done.own.refs_2_.refs_0_), channel_id=1, source_target_pairs={{0,16},{1,17},{2,18},{3,19},{4,20},{5,21},{6,22},{7,23},{8,24},{9,... | collective-permute-start | bytes 1572872 | tf_op jit(solution)/shard_map/ppermute | solution.py:27
  12.8 4.1 %collective-permute-start.1 = (bf16[2,2,64,1024]{3,2,1,0:T(8,128)(2,1)S(1)}, bf16[2,2,64,1024]{3,2,1,0:T(8,128)(2,1)S(1)}, u32[]{:S(2)}, u32[]{:S(2)}) collective-permute-start(bf16[2,2,64,1024]{3,2,1,0:T(8,128)(2,1)S(1)} %collective-permute-done.own.refs_2_.refs_0_), channel_id=1, source_target_pairs={{0,2},{1,3},{2,4},{3,5},{4,6},{5,7},{6,8},{7,9},{8,10},{9,11},{10,... | collective-permute-start | bytes 1572872 | tf_op jit(solution)/shard_map/ppermute | solution.py:27
  16.9 1.9 %collective-permute-start.6 = (bf16[2,2,64,1024]{3,2,1,0:T(8,128)(2,1)S(1)}, bf16[2,2,64,1024]{3,2,1,0:T(8,128)(2,1)S(1)}, u32[]{:S(2)}, u32[]{:S(2)}) collective-permute-start(bf16[2,2,64,1024]{3,2,1,0:T(8,128)(2,1)S(1)} %collective-permute-done.3.other.refs_3_.refs_8_), channel_id=1, source_target_pairs={{0,2},{1,3},{2,4},{3,5},{4,6},{5,7},{6,8},{7,9},{8,10},{9,11},{10,... | collective-permute-start | bytes 1572872 | tf_op jit(solution)/shard_map/ppermute | solution.py:27
  18.8 0.1 pad_add_fusion.info.refs_0_
  18.9 0.6 shard_map.41
  19.4 1.3 %collective-permute-start.4 = (bf16[2,128,1024]{2,1,0:T(8,128)(2,1)S(1)}, bf16[2,128,1024]{2,1,0:T(8,128)(2,1)S(1)}, u32[]{:S(2)}, u32[]{:S(2)}) collective-permute-start(bf16[2,128,1024]{2,1,0:T(8,128)(2,1)S(1)} %shard_map.41), channel_id=1, source_target_pairs={{0,33},{1,0},{2,35},{3,2},{4,37},{5,4},{6,39},{7,6},{8,41},{9,8},{... | collective-permute-start | bytes 1572872 | tf_op jit(solution)/shard_map/ppermute | solution.py:27
  20.7 2.3 %collective-permute-done.1.refs_1_.refs_2_ = bf16[2,2,64,1024]{3,2,1,0:T(8,128)(2,1)S(1)} collective-permute-done((bf16[2,2,64,1024]{3,2,1,0:T(8,128)(2,1)S(1)}, bf16[2,2,64,1024]{3,2,1,0:T(8,128)(2,1)S(1)}, u32[]{:S(2)}, u32[]{:S(2)}) %collective-permute-start.1) | collective-permute-done | bytes 524320 | tf_op jit(solution)/shard_map/ppermute | solution.py:27
  23.0 3.4 %collective-permute-start.2 = (bf16[2,2,64,1024]{3,2,1,0:T(8,128)(2,1)S(1)}, bf16[2,2,64,1024]{3,2,1,0:T(8,128)(2,1)S(1)}, u32[]{:S(2)}, u32[]{:S(2)}) collective-permute-start(bf16[2,2,64,1024]{3,2,1,0:T(8,128)(2,1)S(1)} %collective-permute-done.1.refs_1_.refs_2_), channel_id=1, source_target_pairs={{0,2},{1,3},{2,4},{3,5},{4,6},{5,7},{6,8},{7,9},{8,10},{9,11},{10,... | collective-permute-start | bytes 1572872 | tf_op jit(solution)/shard_map/ppermute | solution.py:27
  26.4 0.0 collective-permute-start.8
  26.4 2.2 %collective-permute-done.6.refs_4_.refs_6_.refs_9_ = bf16[2,2,64,1024]{3,2,1,0:T(8,128)(2,1)S(1)} collective-permute-done((bf16[2,2,64,1024]{3,2,1,0:T(8,128)(2,1)S(1)}, bf16[2,2,64,1024]{3,2,1,0:T(8,128)(2,1)S(1)}, u32[]{:S(2)}, u32[]{:S(2)}) %collective-permute-start.6) | collective-permute-done | bytes 524320 | tf_op jit(solution)/shard_map/ppermute | solution.py:27
  28.6 3.1 %collective-permute-start.10 = (bf16[2,2,64,1024]{3,2,1,0:T(8,128)(2,1)S(1)}, bf16[2,2,64,1024]{3,2,1,0:T(8,128)(2,1)S(1)}, u32[]{:S(2)}, u32[]{:S(2)}) collective-permute-start(bf16[2,2,64,1024]{3,2,1,0:T(8,128)(2,1)S(1)} %collective-permute-done.6.refs_4_.refs_6_.refs_9_), channel_id=1, source_target_pairs={{0,2},{1,3},{2,4},{3,5},{4,6},{5,7},{6,8},{7,9},{8,10},{9,11},{10,... | collective-permute-start | bytes 1572872 | tf_op jit(solution)/shard_map/ppermute | solution.py:27
  31.7 0.0 collective-permute-start.7
  31.7 2.5 %collective-permute-done.4.refs_1_.a_ref = bf16[2,128,1024]{2,1,0:T(8,128)(2,1)S(1)} collective-permute-done((bf16[2,128,1024]{2,1,0:T(8,128)(2,1)S(1)}, bf16[2,128,1024]{2,1,0:T(8,128)(2,1)S(1)}, u32[]{:S(2)}, u32[]{:S(2)}) %collective-permute-start.4) | collective-permute-done | bytes 524320 | tf_op jit(solution)/shard_map/ppermute | solution.py:27
  34.2 0.8 shard_map.42.refs_10_
  35.1 0.0 collective-permute-done.2.refs_4_.refs_0_.refs_3_
  35.1 3.7 %collective-permute-start.5 = (bf16[2,2,64,1024]{3,2,1,0:T(8,128)(2,1)S(1)}, bf16[2,2,64,1024]{3,2,1,0:T(8,128)(2,1)S(1)}, u32[]{:S(2)}, u32[]{:S(2)}) collective-permute-start(bf16[2,2,64,1024]{3,2,1,0:T(8,128)(2,1)S(1)} %collective-permute-done.2.refs_4_.refs_0_.refs_3_), channel_id=1, source_target_pairs={{0,2},{1,3},{2,4},{3,5},{4,6},{5,7},{6,8},{7,9},{8,10},{9,11},{10,... | collective-permute-start | bytes 1572872 | tf_op jit(solution)/shard_map/ppermute | solution.py:27
  38.8 0.0 collective-permute-done.8.refs_5_.refs_7_.refs_10_
  38.8 0.0 collective-permute-done.7.refs_2_.refs_3_
  38.8 0.7 shard_map.43
  39.4 0.1 collective-permute-start.9
  39.5 1.2 %collective-permute-start.13 = (bf16[2,2,64,1024]{3,2,1,0:T(8,128)(2,1)S(1)}, bf16[2,2,64,1024]{3,2,1,0:T(8,128)(2,1)S(1)}, u32[]{:S(2)}, u32[]{:S(2)}) collective-permute-start(bf16[2,2,64,1024]{3,2,1,0:T(8,128)(2,1)S(1)} %collective-permute-done.2.refs_4_.refs_0_.refs_3_), channel_id=1, source_target_pairs={{0,16},{1,17},{2,18},{3,19},{4,20},{5,21},{6,22},{7,23},{8,24},{9,... | collective-permute-start | bytes 1572872 | tf_op jit(solution)/shard_map/ppermute | solution.py:27
  40.8 0.9 collective-permute-start.12
  41.7 2.1 %collective-permute-start.11 = (bf16[2,2,64,1024]{3,2,1,0:T(8,128)(2,1)S(1)}, bf16[2,2,64,1024]{3,2,1,0:T(8,128)(2,1)S(1)}, u32[]{:S(2)}, u32[]{:S(2)}) collective-permute-start(bf16[2,2,64,1024]{3,2,1,0:T(8,128)(2,1)S(1)} %collective-permute-done.10.refs_8_.refs_2_.refs_11_), channel_id=1, source_target_pairs={{0,2},{1,3},{2,4},{3,5},{4,6},{5,7},{6,8},{7,9},{8,10},{9,11},{10,... | collective-permute-start | bytes 1572872 | tf_op jit(solution)/shard_map/ppermute | solution.py:27
  43.7 1.7 %collective-permute-done.5.refs_2_.refs_5_.refs_0_ = bf16[2,2,64,1024]{3,2,1,0:T(8,128)(2,1)S(1)} collective-permute-done((bf16[2,2,64,1024]{3,2,1,0:T(8,128)(2,1)S(1)}, bf16[2,2,64,1024]{3,2,1,0:T(8,128)(2,1)S(1)}, u32[]{:S(2)}, u32[]{:S(2)}) %collective-permute-start.5) | collective-permute-done | bytes 524320 | tf_op jit(solution)/shard_map/ppermute | solution.py:27
  45.5 2.1 %collective-permute-done.9.near = bf16[3,2,128,128]{3,2,1,0:T(8,128)(2,1)S(1)} collective-permute-done((bf16[3,2,128,128]{3,2,1,0:T(8,128)(2,1)S(1)}, bf16[3,2,128,128]{3,2,1,0:T(8,128)(2,1)S(1)}, u32[]{:S(2)}, u32[]{:S(2)}) %collective-permute-start.9) | collective-permute-done | bytes 196640 | tf_op jit(solution)/shard_map/ppermute | solution.py:27
  47.6 1.0 %collective-permute-start.16 = (bf16[2,2,64,1024]{3,2,1,0:T(8,128)(2,1)S(1)}, bf16[2,2,64,1024]{3,2,1,0:T(8,128)(2,1)S(1)}, u32[]{:S(2)}, u32[]{:S(2)}) collective-permute-start(bf16[2,2,64,1024]{3,2,1,0:T(8,128)(2,1)S(1)} %collective-permute-done.5.refs_2_.refs_5_.refs_0_), channel_id=1, source_target_pairs={{0,2},{1,3},{2,4},{3,5},{4,6},{5,7},{6,8},{7,9},{8,10},{9,11},{10,... | collective-permute-start | bytes 1572872 | tf_op jit(solution)/shard_map/ppermute | solution.py:27
  48.6 0.0 collective-permute-done.13.refs_9_.refs_3_.refs_12_
  48.6 0.0 collective-permute-done.12.refs_5_.refs_1_.refs_4_
  48.6 0.6 shard_map.46
  49.2 1.3 %collective-permute-start.17 = (bf16[2,2,128,128]{3,2,1,0:T(8,128)(2,1)S(1)}, bf16[2,2,128,128]{3,2,1,0:T(8,128)(2,1)S(1)}, u32[]{:S(2)}, u32[]{:S(2)}) collective-permute-start(bf16[2,2,128,128]{3,2,1,0:T(8,128)(2,1)S(1)} %shard_map.46), channel_id=1, source_target_pairs={{0,33},{1,0},{2,35},{3,2},{4,37},{5,4},{6,39},{7,6},{8,41},{9,8},{... | collective-permute-start | bytes 393224 | tf_op jit(solution)/shard_map/ppermute | solution.py:27
  50.5 1.4 %collective-permute-start.15 = (bf16[2,2,64,1024]{3,2,1,0:T(8,128)(2,1)S(1)}, bf16[2,2,64,1024]{3,2,1,0:T(8,128)(2,1)S(1)}, u32[]{:S(2)}, u32[]{:S(2)}) collective-permute-start(bf16[2,2,64,1024]{3,2,1,0:T(8,128)(2,1)S(1)} %collective-permute-done.5.refs_2_.refs_5_.refs_0_), channel_id=1, source_target_pairs={{0,16},{1,17},{2,18},{3,19},{4,20},{5,21},{6,22},{7,23},{8,24},{9,... | collective-permute-start | bytes 1572872 | tf_op jit(solution)/shard_map/ppermute | solution.py:27
  52.0 1.3 %shard_map.44.refs_6_ = f32[256,1024]{1,0:T(8,128)S(1)} custom-call(s32[6]{0:T(128)S(1)} %pad_add_fusion.info.refs_0_, bf16[2,128,1024]{2,1,0:T(8,128)(2,1)S(1)} %collective-permute-done.4.refs_1_.a_ref, bf16[2,2,64,1024]{3,2,1,0:T(8,128)(2,1)S(1)} %collective-permute-done.1.refs_1_.refs_2_, ...), custom_call_target="tpu_custom_call" | custom-call | flops 1 | bytes 1048576 | tf_op jit(solution)/shard_map/pallas_call | solution.py:75
  53.3 0.0 collective-permute-done.11.refs_4_.refs_13_.refs_3_
  53.3 0.1 collective-permute-start.14
  53.4 4.2 %collective-permute-done.17.middle = bf16[2,2,128,128]{3,2,1,0:T(8,128)(2,1)S(1)} collective-permute-done((bf16[2,2,128,128]{3,2,1,0:T(8,128)(2,1)S(1)}, bf16[2,2,128,128]{3,2,1,0:T(8,128)(2,1)S(1)}, u32[]{:S(2)}, u32[]{:S(2)}) %collective-permute-start.17) | collective-permute-done | bytes 131104 | tf_op jit(solution)/shard_map/ppermute | solution.py:27
  57.6 0.0 collective-permute-done.16.refs_7_.refs_2_
  57.6 0.9 %collective-permute-start.18 = (bf16[2,2,64,1024]{3,2,1,0:T(8,128)(2,1)S(1)}, bf16[2,2,64,1024]{3,2,1,0:T(8,128)(2,1)S(1)}, u32[]{:S(2)}, u32[]{:S(2)}) collective-permute-start(bf16[2,2,64,1024]{3,2,1,0:T(8,128)(2,1)S(1)} %collective-permute-done.16.refs_7_.refs_2_), channel_id=1, source_target_pairs={{0,16},{1,17},{2,18},{3,19},{4,20},{5,21},{6,22},{7,23},{8,24},{9,... | collective-permute-start | bytes 1572872 | tf_op jit(solution)/shard_map/ppermute | solution.py:27
  58.5 0.0 collective-permute-done.15.refs_5_.refs_14_.refs_4_
  58.5 1.0 %shard_map.45.acc = f32[256,1024]{1,0:T(8,128)S(1)} custom-call(s32[6]{0:T(128)S(1)} %pad_add_fusion.info.refs_0_, bf16[2,128,1024]{2,1,0:T(8,128)(2,1)S(1)} %collective-permute-done.4.refs_1_.a_ref, bf16[2,2,64,1024]{3,2,1,0:T(8,128)(2,1)S(1)} %collective-permute-done.5.refs_2_.refs_5_.refs_0_, ...), custom_call_target="tpu_custom_call" | custom-call | flops 1 | bytes 1048576 | tf_op jit(solution)/shard_map/pallas_call | solution.py:75
  59.5 0.5 collective-permute-done.18.refs_15_.refs_5_
  60.1 0.7 shard_map.48
  60.7 1.3 %collective-permute-start.19 = (bf16[3,2,128,128]{3,2,1,0:T(8,128)(2,1)S(1)}, bf16[3,2,128,128]{3,2,1,0:T(8,128)(2,1)S(1)}, u32[]{:S(2)}, u32[]{:S(2)}) collective-permute-start(bf16[3,2,128,128]{3,2,1,0:T(8,128)(2,1)S(1)} %shard_map.48), channel_id=1, source_target_pairs={{0,33},{1,0},{2,35},{3,2},{4,37},{5,4},{6,39},{7,6},{8,41},{9,8},{... | collective-permute-start | bytes 589832 | tf_op jit(solution)/shard_map/ppermute | solution.py:27
  62.0 2.4 %shard_map.47 = (bf16[2,64,1024]{2,1,0:T(8,128)(2,1)S(1)}, bf16[2,64,1024]{2,1,0:T(8,128)(2,1)S(1)}, f32[256,1024]{1,0:T(8,128)S(1)}, f32[8,128]{1,0:T(8,128)S(1)}) custom-call(s32[6]{0:T(128)S(1)} %pad_add_fusion.info.refs_0_, bf16[2,128,1024]{2,1,0:T(8,128)(2,1)S(1)} %collective-permute-done.4.refs_1_.a_ref, f32[256,1024]{1,0:T(8,128)S(1)} %shard_map.45.acc, ...), custom_call_target="tpu_custom_call" | custom-call | flops 3000000000 | bytes 1048576 | tf_op jit(solution)/shard_map/pallas_call | solution.py:75
  64.4 3.9 %collective-permute-start.22 = (bf16[2,64,1024]{2,1,0:T(8,128)(2,1)S(1)}, bf16[2,64,1024]{2,1,0:T(8,128)(2,1)S(1)}, u32[]{:S(2)}, u32[]{:S(2)}) collective-permute-start(bf16[2,64,1024]{2,1,0:T(8,128)(2,1)S(1)} %get-tuple-element.30), channel_id=1, source_target_pairs={{0,128},{1,112},{2,130},{3,114},{4,132},{5,116},{6,134},{7,118},{8... | collective-permute-start | bytes 786440 | tf_op jit(solution)/shard_map/ppermute | solution.py:27
  68.3 2.6 %collective-permute-done.19.late = bf16[3,2,128,128]{3,2,1,0:T(8,128)(2,1)S(1)} collective-permute-done((bf16[3,2,128,128]{3,2,1,0:T(8,128)(2,1)S(1)}, bf16[3,2,128,128]{3,2,1,0:T(8,128)(2,1)S(1)}, u32[]{:S(2)}, u32[]{:S(2)}) %collective-permute-start.19) | collective-permute-done | bytes 196640 | tf_op jit(solution)/shard_map/ppermute | solution.py:27
  70.9 0.7 shard_map.49
  71.6 0.0 collective-permute-start.21
  71.6 6.2 %collective-permute-start.20 = (f32[1,128]{1,0:T(1,128)S(1)}, f32[1,128]{1,0:T(1,128)S(1)}, u32[]{:S(2)}, u32[]{:S(2)}) collective-permute-start(f32[1,128]{1,0:T(1,128)S(1)} %shard_map.49), channel_id=1, source_target_pairs={{0,128},{1,112},{2,130},{3,114},{4,132},{5,116},{6,134},{7,118},{8... | collective-permute-start | bytes 1544 | tf_op jit(solution)/shard_map/ppermute | solution.py:27
  77.8 0.0 collective-permute-done.21
  77.8 0.7 collective-permute-done.20
  78.5 2.0 %collective-permute-start.25 = (f32[2,128]{1,0:T(2,128)S(1)}, f32[2,128]{1,0:T(2,128)S(1)}, u32[]{:S(2)}, u32[]{:S(2)}) collective-permute-start(f32[2,128]{1,0:T(2,128)S(1)} %maximum_select_fusion.1.own), channel_id=1, source_target_pairs={{0,14},{1,15},{2,0},{3,1},{4,2},{5,3},{6,4},{7,5},{8,6},{9,7},{10,... | collective-permute-start | bytes 3080 | tf_op jit(solution)/shard_map/ppermute | solution.py:27
  80.6 0.1 collective-permute-start.23
  80.7 0.6 collective-permute-done.25.above
  81.3 3.1 %collective-permute-done.24.below = f32[2,128]{1,0:T(2,128)S(1)} collective-permute-done((f32[2,128]{1,0:T(2,128)S(1)}, f32[2,128]{1,0:T(2,128)S(1)}, u32[]{:S(2)}, u32[]{:S(2)}) %collective-permute-start.24) | collective-permute-done | bytes 1056 | tf_op jit(solution)/shard_map/ppermute | solution.py:27
  84.4 0.5 shard_map.50
  85.0 0.1 collective-permute-start.26
  85.1 4.5 %collective-permute-start.27 = (f32[2,128]{1,0:T(2,128)S(1)}, f32[2,128]{1,0:T(2,128)S(1)}, u32[]{:S(2)}, u32[]{:S(2)}) collective-permute-start(f32[2,128]{1,0:T(2,128)S(1)} %get-tuple-element.35), channel_id=1, source_target_pairs={{0,10},{1,11},{2,12},{3,13},{4,14},{5,15},{6,0},{7,1},{8,2},{9,3},... | collective-permute-start | bytes 3080 | tf_op jit(solution)/shard_map/ppermute | solution.py:27
  89.5 0.9 maximum_select_fusion
  90.4 0.1 collective-permute-done.26
  90.5 0.1 reshape.77
  90.6 0.6 broadcast_multiply_fusion
  (12 shorter events, 0.1 us)
Async XLA Ops:
  0.6 16.2 %copy-start = (s32[2,1,4]{2,1,0:T(1,128)S(1)}, s32[2,1,4]{2,1,0:T(1,128)}, u32[]{:S(2)}) copy-start(s32[2,1,4]{2,1,0:T(1,128)} %param.3) | copy-start | bytes 100
  0.6 10.6 %collective-permute-start = (bf16[2,2,64,1024]{3,2,1,0:T(8,128)(2,1)}, bf16[2,2,64,1024]{3,2,1,0:T(8,128)(2,1)S(1)}, u32[]{:S(2)}, u32[]{:S(2)}) collective-permute-start(bf16[2,2,64,1024]{3,2,1,0:T(8,128)(2,1)} %bitcast.15), channel_id=1, source_target_pairs={{0,128},{1,144},{2,130},{3,146},{4,132},{5,148},{6,134},{7,150},{8... | collective-permute-start | bytes 1572872 | tf_op jit(solution)/shard_map/ppermute | solution.py:27
  11.3 5.6 %collective-permute-start.3 = (bf16[2,2,64,1024]{3,2,1,0:T(8,128)(2,1)S(1)}, bf16[2,2,64,1024]{3,2,1,0:T(8,128)(2,1)S(1)}, u32[]{:S(2)}, u32[]{:S(2)}) collective-permute-start(bf16[2,2,64,1024]{3,2,1,0:T(8,128)(2,1)S(1)} %collective-permute-done.own.refs_2_.refs_0_), channel_id=1, source_target_pairs={{0,16},{1,17},{2,18},{3,19},{4,20},{5,21},{6,22},{7,23},{8,24},{9,... | collective-permute-start | bytes 1572872 | tf_op jit(solution)/shard_map/ppermute | solution.py:27
  12.8 10.2 %collective-permute-start.1 = (bf16[2,2,64,1024]{3,2,1,0:T(8,128)(2,1)S(1)}, bf16[2,2,64,1024]{3,2,1,0:T(8,128)(2,1)S(1)}, u32[]{:S(2)}, u32[]{:S(2)}) collective-permute-start(bf16[2,2,64,1024]{3,2,1,0:T(8,128)(2,1)S(1)} %collective-permute-done.own.refs_2_.refs_0_), channel_id=1, source_target_pairs={{0,2},{1,3},{2,4},{3,5},{4,6},{5,7},{6,8},{7,9},{8,10},{9,11},{10,... | collective-permute-start | bytes 1572872 | tf_op jit(solution)/shard_map/ppermute | solution.py:27
  16.9 11.7 %collective-permute-start.6 = (bf16[2,2,64,1024]{3,2,1,0:T(8,128)(2,1)S(1)}, bf16[2,2,64,1024]{3,2,1,0:T(8,128)(2,1)S(1)}, u32[]{:S(2)}, u32[]{:S(2)}) collective-permute-start(bf16[2,2,64,1024]{3,2,1,0:T(8,128)(2,1)S(1)} %collective-permute-done.3.other.refs_3_.refs_8_), channel_id=1, source_target_pairs={{0,2},{1,3},{2,4},{3,5},{4,6},{5,7},{6,8},{7,9},{8,10},{9,11},{10,... | collective-permute-start | bytes 1572872 | tf_op jit(solution)/shard_map/ppermute | solution.py:27
  19.4 14.8 %collective-permute-start.4 = (bf16[2,128,1024]{2,1,0:T(8,128)(2,1)S(1)}, bf16[2,128,1024]{2,1,0:T(8,128)(2,1)S(1)}, u32[]{:S(2)}, u32[]{:S(2)}) collective-permute-start(bf16[2,128,1024]{2,1,0:T(8,128)(2,1)S(1)} %shard_map.41), channel_id=1, source_target_pairs={{0,33},{1,0},{2,35},{3,2},{4,37},{5,4},{6,39},{7,6},{8,41},{9,8},{... | collective-permute-start | bytes 1572872 | tf_op jit(solution)/shard_map/ppermute | solution.py:27
  23.0 12.1 %collective-permute-start.2 = (bf16[2,2,64,1024]{3,2,1,0:T(8,128)(2,1)S(1)}, bf16[2,2,64,1024]{3,2,1,0:T(8,128)(2,1)S(1)}, u32[]{:S(2)}, u32[]{:S(2)}) collective-permute-start(bf16[2,2,64,1024]{3,2,1,0:T(8,128)(2,1)S(1)} %collective-permute-done.1.refs_1_.refs_2_), channel_id=1, source_target_pairs={{0,2},{1,3},{2,4},{3,5},{4,6},{5,7},{6,8},{7,9},{8,10},{9,11},{10,... | collective-permute-start | bytes 1572872 | tf_op jit(solution)/shard_map/ppermute | solution.py:27
  26.4 12.3 %collective-permute-start.8 = (bf16[2,2,64,1024]{3,2,1,0:T(8,128)(2,1)S(1)}, bf16[2,2,64,1024]{3,2,1,0:T(8,128)(2,1)S(1)}, u32[]{:S(2)}, u32[]{:S(2)}) collective-permute-start(bf16[2,2,64,1024]{3,2,1,0:T(8,128)(2,1)S(1)} %collective-permute-done.1.refs_1_.refs_2_), channel_id=1, source_target_pairs={{0,16},{1,17},{2,18},{3,19},{4,20},{5,21},{6,22},{7,23},{8,24},{9,... | collective-permute-start | bytes 1572872 | tf_op jit(solution)/shard_map/ppermute | solution.py:27
  28.6 12.2 %collective-permute-start.10 = (bf16[2,2,64,1024]{3,2,1,0:T(8,128)(2,1)S(1)}, bf16[2,2,64,1024]{3,2,1,0:T(8,128)(2,1)S(1)}, u32[]{:S(2)}, u32[]{:S(2)}) collective-permute-start(bf16[2,2,64,1024]{3,2,1,0:T(8,128)(2,1)S(1)} %collective-permute-done.6.refs_4_.refs_6_.refs_9_), channel_id=1, source_target_pairs={{0,2},{1,3},{2,4},{3,5},{4,6},{5,7},{6,8},{7,9},{8,10},{9,11},{10,... | collective-permute-start | bytes 1572872 | tf_op jit(solution)/shard_map/ppermute | solution.py:27
  31.7 7.0 %collective-permute-start.7 = (bf16[2,2,64,1024]{3,2,1,0:T(8,128)(2,1)S(1)}, bf16[2,2,64,1024]{3,2,1,0:T(8,128)(2,1)S(1)}, u32[]{:S(2)}, u32[]{:S(2)}) collective-permute-start(bf16[2,2,64,1024]{3,2,1,0:T(8,128)(2,1)S(1)} %collective-permute-done.6.refs_4_.refs_6_.refs_9_), channel_id=1, source_target_pairs={{0,16},{1,17},{2,18},{3,19},{4,20},{5,21},{6,22},{7,23},{8,24},{9,... | collective-permute-start | bytes 1572872 | tf_op jit(solution)/shard_map/ppermute | solution.py:27
  35.1 10.4 %collective-permute-start.5 = (bf16[2,2,64,1024]{3,2,1,0:T(8,128)(2,1)S(1)}, bf16[2,2,64,1024]{3,2,1,0:T(8,128)(2,1)S(1)}, u32[]{:S(2)}, u32[]{:S(2)}) collective-permute-start(bf16[2,2,64,1024]{3,2,1,0:T(8,128)(2,1)S(1)} %collective-permute-done.2.refs_4_.refs_0_.refs_3_), channel_id=1, source_target_pairs={{0,2},{1,3},{2,4},{3,5},{4,6},{5,7},{6,8},{7,9},{8,10},{9,11},{10,... | collective-permute-start | bytes 1572872 | tf_op jit(solution)/shard_map/ppermute | solution.py:27
  39.4 8.1 %collective-permute-start.9 = (bf16[3,2,128,128]{3,2,1,0:T(8,128)(2,1)S(1)}, bf16[3,2,128,128]{3,2,1,0:T(8,128)(2,1)S(1)}, u32[]{:S(2)}, u32[]{:S(2)}) collective-permute-start(bf16[3,2,128,128]{3,2,1,0:T(8,128)(2,1)S(1)} %shard_map.43), channel_id=1, source_target_pairs={{0,33},{1,0},{2,35},{3,2},{4,37},{5,4},{6,39},{7,6},{8,41},{9,8},{... | collective-permute-start | bytes 589832 | tf_op jit(solution)/shard_map/ppermute | solution.py:27
  39.5 9.1 %collective-permute-start.13 = (bf16[2,2,64,1024]{3,2,1,0:T(8,128)(2,1)S(1)}, bf16[2,2,64,1024]{3,2,1,0:T(8,128)(2,1)S(1)}, u32[]{:S(2)}, u32[]{:S(2)}) collective-permute-start(bf16[2,2,64,1024]{3,2,1,0:T(8,128)(2,1)S(1)} %collective-permute-done.2.refs_4_.refs_0_.refs_3_), channel_id=1, source_target_pairs={{0,16},{1,17},{2,18},{3,19},{4,20},{5,21},{6,22},{7,23},{8,24},{9,... | collective-permute-start | bytes 1572872 | tf_op jit(solution)/shard_map/ppermute | solution.py:27
  40.8 7.8 %collective-permute-start.12 = (bf16[2,2,64,1024]{3,2,1,0:T(8,128)(2,1)S(1)}, bf16[2,2,64,1024]{3,2,1,0:T(8,128)(2,1)S(1)}, u32[]{:S(2)}, u32[]{:S(2)}) collective-permute-start(bf16[2,2,64,1024]{3,2,1,0:T(8,128)(2,1)S(1)} %collective-permute-done.10.refs_8_.refs_2_.refs_11_), channel_id=1, source_target_pairs={{0,16},{1,17},{2,18},{3,19},{4,20},{5,21},{6,22},{7,23},{8,24},{9,... | collective-permute-start | bytes 1572872 | tf_op jit(solution)/shard_map/ppermute | solution.py:27
  41.7 11.6 %collective-permute-start.11 = (bf16[2,2,64,1024]{3,2,1,0:T(8,128)(2,1)S(1)}, bf16[2,2,64,1024]{3,2,1,0:T(8,128)(2,1)S(1)}, u32[]{:S(2)}, u32[]{:S(2)}) collective-permute-start(bf16[2,2,64,1024]{3,2,1,0:T(8,128)(2,1)S(1)} %collective-permute-done.10.refs_8_.refs_2_.refs_11_), channel_id=1, source_target_pairs={{0,2},{1,3},{2,4},{3,5},{4,6},{5,7},{6,8},{7,9},{8,10},{9,11},{10,... | collective-permute-start | bytes 1572872 | tf_op jit(solution)/shard_map/ppermute | solution.py:27
  47.6 10.0 %collective-permute-start.16 = (bf16[2,2,64,1024]{3,2,1,0:T(8,128)(2,1)S(1)}, bf16[2,2,64,1024]{3,2,1,0:T(8,128)(2,1)S(1)}, u32[]{:S(2)}, u32[]{:S(2)}) collective-permute-start(bf16[2,2,64,1024]{3,2,1,0:T(8,128)(2,1)S(1)} %collective-permute-done.5.refs_2_.refs_5_.refs_0_), channel_id=1, source_target_pairs={{0,2},{1,3},{2,4},{3,5},{4,6},{5,7},{6,8},{7,9},{8,10},{9,11},{10,... | collective-permute-start | bytes 1572872 | tf_op jit(solution)/shard_map/ppermute | solution.py:27
  49.2 8.3 %collective-permute-start.17 = (bf16[2,2,128,128]{3,2,1,0:T(8,128)(2,1)S(1)}, bf16[2,2,128,128]{3,2,1,0:T(8,128)(2,1)S(1)}, u32[]{:S(2)}, u32[]{:S(2)}) collective-permute-start(bf16[2,2,128,128]{3,2,1,0:T(8,128)(2,1)S(1)} %shard_map.46), channel_id=1, source_target_pairs={{0,33},{1,0},{2,35},{3,2},{4,37},{5,4},{6,39},{7,6},{8,41},{9,8},{... | collective-permute-start | bytes 393224 | tf_op jit(solution)/shard_map/ppermute | solution.py:27
  50.5 8.0 %collective-permute-start.15 = (bf16[2,2,64,1024]{3,2,1,0:T(8,128)(2,1)S(1)}, bf16[2,2,64,1024]{3,2,1,0:T(8,128)(2,1)S(1)}, u32[]{:S(2)}, u32[]{:S(2)}) collective-permute-start(bf16[2,2,64,1024]{3,2,1,0:T(8,128)(2,1)S(1)} %collective-permute-done.5.refs_2_.refs_5_.refs_0_), channel_id=1, source_target_pairs={{0,16},{1,17},{2,18},{3,19},{4,20},{5,21},{6,22},{7,23},{8,24},{9,... | collective-permute-start | bytes 1572872 | tf_op jit(solution)/shard_map/ppermute | solution.py:27
  53.3 5.2 %collective-permute-start.14 = (bf16[2,2,64,1024]{3,2,1,0:T(8,128)(2,1)S(1)}, bf16[2,2,64,1024]{3,2,1,0:T(8,128)(2,1)S(1)}, u32[]{:S(2)}, u32[]{:S(2)}) collective-permute-start(bf16[2,2,64,1024]{3,2,1,0:T(8,128)(2,1)S(1)} %collective-permute-done.11.refs_4_.refs_13_.refs_3_), channel_id=1, source_target_pairs={{0,16},{1,17},{2,18},{3,19},{4,20},{5,21},{6,22},{7,23},{8,24},{9,... | collective-permute-start | bytes 1572872 | tf_op jit(solution)/shard_map/ppermute | solution.py:27
  57.6 2.5 %collective-permute-start.18 = (bf16[2,2,64,1024]{3,2,1,0:T(8,128)(2,1)S(1)}, bf16[2,2,64,1024]{3,2,1,0:T(8,128)(2,1)S(1)}, u32[]{:S(2)}, u32[]{:S(2)}) collective-permute-start(bf16[2,2,64,1024]{3,2,1,0:T(8,128)(2,1)S(1)} %collective-permute-done.16.refs_7_.refs_2_), channel_id=1, source_target_pairs={{0,16},{1,17},{2,18},{3,19},{4,20},{5,21},{6,22},{7,23},{8,24},{9,... | collective-permute-start | bytes 1572872 | tf_op jit(solution)/shard_map/ppermute | solution.py:27
  60.7 10.1 %collective-permute-start.19 = (bf16[3,2,128,128]{3,2,1,0:T(8,128)(2,1)S(1)}, bf16[3,2,128,128]{3,2,1,0:T(8,128)(2,1)S(1)}, u32[]{:S(2)}, u32[]{:S(2)}) collective-permute-start(bf16[3,2,128,128]{3,2,1,0:T(8,128)(2,1)S(1)} %shard_map.48), channel_id=1, source_target_pairs={{0,33},{1,0},{2,35},{3,2},{4,37},{5,4},{6,39},{7,6},{8,41},{9,8},{... | collective-permute-start | bytes 589832 | tf_op jit(solution)/shard_map/ppermute | solution.py:27
  64.4 14.1 %collective-permute-start.22 = (bf16[2,64,1024]{2,1,0:T(8,128)(2,1)S(1)}, bf16[2,64,1024]{2,1,0:T(8,128)(2,1)S(1)}, u32[]{:S(2)}, u32[]{:S(2)}) collective-permute-start(bf16[2,64,1024]{2,1,0:T(8,128)(2,1)S(1)} %get-tuple-element.30), channel_id=1, source_target_pairs={{0,128},{1,112},{2,130},{3,114},{4,132},{5,116},{6,134},{7,118},{8... | collective-permute-start | bytes 786440 | tf_op jit(solution)/shard_map/ppermute | solution.py:27
  71.6 6.2 %collective-permute-start.21 = (f32[1,128]{1,0:T(1,128)S(1)}, f32[1,128]{1,0:T(1,128)S(1)}, u32[]{:S(2)}, u32[]{:S(2)}) collective-permute-start(f32[1,128]{1,0:T(1,128)S(1)} %shard_map.49), channel_id=1, source_target_pairs={{0,129},{1,113},{2,131},{3,115},{4,133},{5,117},{6,135},{7,119},{8... | collective-permute-start | bytes 1544 | tf_op jit(solution)/shard_map/ppermute | solution.py:27
  71.6 6.9 %collective-permute-start.20 = (f32[1,128]{1,0:T(1,128)S(1)}, f32[1,128]{1,0:T(1,128)S(1)}, u32[]{:S(2)}, u32[]{:S(2)}) collective-permute-start(f32[1,128]{1,0:T(1,128)S(1)} %shard_map.49), channel_id=1, source_target_pairs={{0,128},{1,112},{2,130},{3,114},{4,132},{5,116},{6,134},{7,118},{8... | collective-permute-start | bytes 1544 | tf_op jit(solution)/shard_map/ppermute | solution.py:27
  78.5 2.8 %collective-permute-start.25 = (f32[2,128]{1,0:T(2,128)S(1)}, f32[2,128]{1,0:T(2,128)S(1)}, u32[]{:S(2)}, u32[]{:S(2)}) collective-permute-start(f32[2,128]{1,0:T(2,128)S(1)} %maximum_select_fusion.1.own), channel_id=1, source_target_pairs={{0,14},{1,15},{2,0},{3,1},{4,2},{5,3},{6,4},{7,5},{8,6},{9,7},{10,... | collective-permute-start | bytes 3080 | tf_op jit(solution)/shard_map/ppermute | solution.py:27
  80.6 3.9 %collective-permute-start.24 = (f32[2,128]{1,0:T(2,128)S(1)}, f32[2,128]{1,0:T(2,128)S(1)}, u32[]{:S(2)}, u32[]{:S(2)}) collective-permute-start(f32[2,128]{1,0:T(2,128)S(1)} %maximum_select_fusion.1.own), channel_id=1, source_target_pairs={{0,2},{1,3},{2,4},{3,5},{4,6},{5,7},{6,8},{7,9},{8,10},{9,11},{10,... | collective-permute-start | bytes 3080 | tf_op jit(solution)/shard_map/ppermute | solution.py:27
  80.6 9.0 %collective-permute-start.23 = (bf16[2,64,1024]{2,1,0:T(8,128)(2,1)S(1)}, bf16[2,64,1024]{2,1,0:T(8,128)(2,1)S(1)}, u32[]{:S(2)}, u32[]{:S(2)}) collective-permute-start(bf16[2,64,1024]{2,1,0:T(8,128)(2,1)S(1)} %get-tuple-element.32), channel_id=1, source_target_pairs={{0,129},{1,113},{2,131},{3,115},{4,133},{5,117},{6,135},{7,119},{8... | collective-permute-start | bytes 786440 | tf_op jit(solution)/shard_map/ppermute | solution.py:27
  85.0 5.5 %collective-permute-start.26 = (f32[2,128]{1,0:T(2,128)S(1)}, f32[2,128]{1,0:T(2,128)S(1)}, u32[]{:S(2)}, u32[]{:S(2)}) collective-permute-start(f32[2,128]{1,0:T(2,128)S(1)} %get-tuple-element.34), channel_id=1, source_target_pairs={{0,6},{1,7},{2,8},{3,9},{4,10},{5,11},{6,12},{7,13},{8,14},{9,15},... | collective-permute-start | bytes 3080 | tf_op jit(solution)/shard_map/ppermute | solution.py:27
  85.1 5.4 %collective-permute-start.27 = (f32[2,128]{1,0:T(2,128)S(1)}, f32[2,128]{1,0:T(2,128)S(1)}, u32[]{:S(2)}, u32[]{:S(2)}) collective-permute-start(f32[2,128]{1,0:T(2,128)S(1)} %get-tuple-element.35), channel_id=1, source_target_pairs={{0,10},{1,11},{2,12},{3,13},{4,14},{5,15},{6,0},{7,1},{8,2},{9,3},... | collective-permute-start | bytes 3080 | tf_op jit(solution)/shard_map/ppermute | solution.py:27

commit v18 on v17

--- a/solution.py
+++ b/solution.py
@@ -182,7 +182,7 @@
 
 
 def add_kernel(info, below, own, above, two, three):
-    two[...] = own[...] + above[...]
+    two[...] = below[...] + own[...]
     three[...] = below[...] + own[...] + above[...]
 
 
@@ -246,10 +246,10 @@
     first, second = moved(trace, from_hub(0)), moved(trace, from_hub(1))
     both = jnp.where(half == 0, jnp.concatenate([first, second]), jnp.concatenate([second, first]))
     both, kept = wall((both, kept))
-    below, above = moved(both, along(1)), moved(both, along(-1))
+    below, above = moved(both, along(3)), moved(both, along(-3))
     pair = jax.ShapeDtypeStruct((2, 128), F32)
     two, three = call(add_kernel, info, [below, both, above], (pair, pair), WEIGHT)
-    below, above = moved(two, along(3)), moved(three, along(-3))
+    below, above = moved(three, along(1)), moved(two, along(-1))
     both = below + three + above
     products = jnp.where(half == 0, jnp.stack([kept, sent]), jnp.stack([sent, kept]))[:, None, None]
     correlator = jnp.sum(both[:, :16].reshape(2, 8, 2), axis=1)[:, None, None, :] / F32(1024)

time: 92.8 us -> 93 us (level); the launches traced: 91.2 us -> 92.3 us
  waiting for transfers between devices: 29.1 us -> 32.1 us
  starting transfers between devices: 50.3 us -> 48.5 us
    ppermute x28, waiting for transfers between devices: 29.1 us -> 32.1 us  [moved(): lax.ppermute(block, BOTH, [(index_of(*at), index_of(*route(*at))) for at...]
    ppermute x28, starting transfers between devices: 50.3 us -> 48.5 us  [moved(): lax.ppermute(block, BOTH, [(index_of(*at), index_of(*route(*at))) for at...]
  transfers between devices with their start and end apart: 28 -> 28, of which waited for: 13 -> 14; matrix products, arithmetic and copies ran while one was open for 1% -> 1% of each run, Pallas kernels for 10% -> 9%
where the time goes in v18:
time: 93 us; the launch traced here: 92.3 us
  starting transfers between devices  48.5 us (52%)
  waiting for transfers between devices  32.1 us (35%)
  Pallas kernels  9.37 us (10%)
  other arithmetic  1.55 us (2%)
    ppermute x28, starting transfers between devices, moved(): lax.ppermute(block, BOTH, [(index_of(*at), index_of(*route(*at))) for at...  48.5 us
    ppermute x28, waiting for transfers between devices, moved(): lax.ppermute(block, BOTH, [(index_of(*at), index_of(*route(*at))) for at...  32.1 us
    pallas_call x10, Pallas kernels, call(): pl.pallas_call(kernel, out_shape=out_shape, in_specs=[SMEM] + [VMEM] * le...  9.37 us
  transfers between devices with their start and end apart: 28, of which 14 were waited for; matrix products, arithmetic and copies ran while one was open for 1% of the time, Pallas kernels for 9%

profile of v18, /device:TPU:1, one launch (start us, length us, event | category | flops | bytes accessed | tf_op | source)
XLA Modules:
  0.0 92.3 jit_solution(9610834476490671943)
XLA Ops:
  0.6 0.0 copy-start
  0.6 4.2 %collective-permute-start = (bf16[2,2,64,1024]{3,2,1,0:T(8,128)(2,1)}, bf16[2,2,64,1024]{3,2,1,0:T(8,128)(2,1)S(1)}, u32[]{:S(2)}, u32[]{:S(2)}) collective-permute-start(bf16[2,2,64,1024]{3,2,1,0:T(8,128)(2,1)} %bitcast.15), channel_id=1, source_target_pairs={{0,128},{1,144},{2,130},{3,146},{4,132},{5,148},{6,134},{7,150},{8... | collective-permute-start | bytes 1572872 | tf_op jit(solution)/shard_map/ppermute | solution.py:27
  4.8 6.4 %collective-permute-done.own.refs_2_.refs_0_ = bf16[2,2,64,1024]{3,2,1,0:T(8,128)(2,1)S(1)} collective-permute-done((bf16[2,2,64,1024]{3,2,1,0:T(8,128)(2,1)}, bf16[2,2,64,1024]{3,2,1,0:T(8,128)(2,1)S(1)}, u32[]{:S(2)}, u32[]{:S(2)}) %collective-permute-start) | collective-permute-done | bytes 524320 | tf_op jit(solution)/shard_map/ppermute | solution.py:27
  11.3 1.5 %collective-permute-start.3 = (bf16[2,2,64,1024]{3,2,1,0:T(8,128)(2,1)S(1)}, bf16[2,2,64,1024]{3,2,1,0:T(8,128)(2,1)S(1)}, u32[]{:S(2)}, u32[]{:S(2)}) collective-permute-start(bf16[2,2,64,1024]{3,2,1,0:T(8,128)(2,1)S(1)} %collective-permute-done.own.refs_2_.refs_0_), channel_id=1, source_target_pairs={{0,16},{1,17},{2,18},{3,19},{4,20},{5,21},{6,22},{7,23},{8,24},{9,... | collective-permute-start | bytes 1572872 | tf_op jit(solution)/shard_map/ppermute | solution.py:27
  12.8 4.1 %collective-permute-start.1 = (bf16[2,2,64,1024]{3,2,1,0:T(8,128)(2,1)S(1)}, bf16[2,2,64,1024]{3,2,1,0:T(8,128)(2,1)S(1)}, u32[]{:S(2)}, u32[]{:S(2)}) collective-permute-start(bf16[2,2,64,1024]{3,2,1,0:T(8,128)(2,1)S(1)} %collective-permute-done.own.refs_2_.refs_0_), channel_id=1, source_target_pairs={{0,2},{1,3},{2,4},{3,5},{4,6},{5,7},{6,8},{7,9},{8,10},{9,11},{10,... | collective-permute-start | bytes 1572872 | tf_op jit(solution)/shard_map/ppermute | solution.py:27
  16.9 0.0 collective-permute-done.3.other.refs_3_.refs_8_
  16.9 1.9 %collective-permute-start.6 = (bf16[2,2,64,1024]{3,2,1,0:T(8,128)(2,1)S(1)}, bf16[2,2,64,1024]{3,2,1,0:T(8,128)(2,1)S(1)}, u32[]{:S(2)}, u32[]{:S(2)}) collective-permute-start(bf16[2,2,64,1024]{3,2,1,0:T(8,128)(2,1)S(1)} %collective-permute-done.3.other.refs_3_.refs_8_), channel_id=1, source_target_pairs={{0,2},{1,3},{2,4},{3,5},{4,6},{5,7},{6,8},{7,9},{8,10},{9,11},{10,... | collective-permute-start | bytes 1572872 | tf_op jit(solution)/shard_map/ppermute | solution.py:27
  18.8 0.1 pad_add_fusion.info.refs_0_
  18.9 0.6 shard_map.41
  19.4 1.3 %collective-permute-start.4 = (bf16[2,128,1024]{2,1,0:T(8,128)(2,1)S(1)}, bf16[2,128,1024]{2,1,0:T(8,128)(2,1)S(1)}, u32[]{:S(2)}, u32[]{:S(2)}) collective-permute-start(bf16[2,128,1024]{2,1,0:T(8,128)(2,1)S(1)} %shard_map.41), channel_id=1, source_target_pairs={{0,33},{1,0},{2,35},{3,2},{4,37},{5,4},{6,39},{7,6},{8,41},{9,8},{... | collective-permute-start | bytes 1572872 | tf_op jit(solution)/shard_map/ppermute | solution.py:27
  20.7 2.3 %collective-permute-done.1.refs_1_.refs_2_ = bf16[2,2,64,1024]{3,2,1,0:T(8,128)(2,1)S(1)} collective-permute-done((bf16[2,2,64,1024]{3,2,1,0:T(8,128)(2,1)S(1)}, bf16[2,2,64,1024]{3,2,1,0:T(8,128)(2,1)S(1)}, u32[]{:S(2)}, u32[]{:S(2)}) %collective-permute-start.1) | collective-permute-done | bytes 524320 | tf_op jit(solution)/shard_map/ppermute | solution.py:27
  23.0 3.4 %collective-permute-start.2 = (bf16[2,2,64,1024]{3,2,1,0:T(8,128)(2,1)S(1)}, bf16[2,2,64,1024]{3,2,1,0:T(8,128)(2,1)S(1)}, u32[]{:S(2)}, u32[]{:S(2)}) collective-permute-start(bf16[2,2,64,1024]{3,2,1,0:T(8,128)(2,1)S(1)} %collective-permute-done.1.refs_1_.refs_2_), channel_id=1, source_target_pairs={{0,2},{1,3},{2,4},{3,5},{4,6},{5,7},{6,8},{7,9},{8,10},{9,11},{10,... | collective-permute-start | bytes 1572872 | tf_op jit(solution)/shard_map/ppermute | solution.py:27
  26.4 0.0 collective-permute-start.8
  26.4 2.2 %collective-permute-done.6.refs_4_.refs_6_.refs_9_ = bf16[2,2,64,1024]{3,2,1,0:T(8,128)(2,1)S(1)} collective-permute-done((bf16[2,2,64,1024]{3,2,1,0:T(8,128)(2,1)S(1)}, bf16[2,2,64,1024]{3,2,1,0:T(8,128)(2,1)S(1)}, u32[]{:S(2)}, u32[]{:S(2)}) %collective-permute-start.6) | collective-permute-done | bytes 524320 | tf_op jit(solution)/shard_map/ppermute | solution.py:27
  28.6 3.1 %collective-permute-start.10 = (bf16[2,2,64,1024]{3,2,1,0:T(8,128)(2,1)S(1)}, bf16[2,2,64,1024]{3,2,1,0:T(8,128)(2,1)S(1)}, u32[]{:S(2)}, u32[]{:S(2)}) collective-permute-start(bf16[2,2,64,1024]{3,2,1,0:T(8,128)(2,1)S(1)} %collective-permute-done.6.refs_4_.refs_6_.refs_9_), channel_id=1, source_target_pairs={{0,2},{1,3},{2,4},{3,5},{4,6},{5,7},{6,8},{7,9},{8,10},{9,11},{10,... | collective-permute-start | bytes 1572872 | tf_op jit(solution)/shard_map/ppermute | solution.py:27
  31.7 2.5 %collective-permute-done.4.refs_1_.a_ref = bf16[2,128,1024]{2,1,0:T(8,128)(2,1)S(1)} collective-permute-done((bf16[2,128,1024]{2,1,0:T(8,128)(2,1)S(1)}, bf16[2,128,1024]{2,1,0:T(8,128)(2,1)S(1)}, u32[]{:S(2)}, u32[]{:S(2)}) %collective-permute-start.4) | collective-permute-done | bytes 524320 | tf_op jit(solution)/shard_map/ppermute | solution.py:27
  34.2 0.8 shard_map.42.refs_10_
  35.1 3.7 %collective-permute-start.5 = (bf16[2,2,64,1024]{3,2,1,0:T(8,128)(2,1)S(1)}, bf16[2,2,64,1024]{3,2,1,0:T(8,128)(2,1)S(1)}, u32[]{:S(2)}, u32[]{:S(2)}) collective-permute-start(bf16[2,2,64,1024]{3,2,1,0:T(8,128)(2,1)S(1)} %collective-permute-done.2.refs_4_.refs_0_.refs_3_), channel_id=1, source_target_pairs={{0,2},{1,3},{2,4},{3,5},{4,6},{5,7},{6,8},{7,9},{8,10},{9,11},{10,... | collective-permute-start | bytes 1572872 | tf_op jit(solution)/shard_map/ppermute | solution.py:27
  38.8 0.7 shard_map.43
  39.4 0.1 collective-permute-start.9
  39.5 1.2 %collective-permute-start.13 = (bf16[2,2,64,1024]{3,2,1,0:T(8,128)(2,1)S(1)}, bf16[2,2,64,1024]{3,2,1,0:T(8,128)(2,1)S(1)}, u32[]{:S(2)}, u32[]{:S(2)}) collective-permute-start(bf16[2,2,64,1024]{3,2,1,0:T(8,128)(2,1)S(1)} %collective-permute-done.2.refs_4_.refs_0_.refs_3_), channel_id=1, source_target_pairs={{0,16},{1,17},{2,18},{3,19},{4,20},{5,21},{6,22},{7,23},{8,24},{9,... | collective-permute-start | bytes 1572872 | tf_op jit(solution)/shard_map/ppermute | solution.py:27
  40.8 0.0 collective-permute-done.10.refs_8_.refs_2_.refs_11_
  40.8 0.9 collective-permute-start.12
  41.7 2.1 %collective-permute-start.11 = (bf16[2,2,64,1024]{3,2,1,0:T(8,128)(2,1)S(1)}, bf16[2,2,64,1024]{3,2,1,0:T(8,128)(2,1)S(1)}, u32[]{:S(2)}, u32[]{:S(2)}) collective-permute-start(bf16[2,2,64,1024]{3,2,1,0:T(8,128)(2,1)S(1)} %collective-permute-done.10.refs_8_.refs_2_.refs_11_), channel_id=1, source_target_pairs={{0,2},{1,3},{2,4},{3,5},{4,6},{5,7},{6,8},{7,9},{8,10},{9,11},{10,... | collective-permute-start | bytes 1572872 | tf_op jit(solution)/shard_map/ppermute | solution.py:27
  43.7 1.7 %collective-permute-done.5.refs_2_.refs_5_.refs_0_ = bf16[2,2,64,1024]{3,2,1,0:T(8,128)(2,1)S(1)} collective-permute-done((bf16[2,2,64,1024]{3,2,1,0:T(8,128)(2,1)S(1)}, bf16[2,2,64,1024]{3,2,1,0:T(8,128)(2,1)S(1)}, u32[]{:S(2)}, u32[]{:S(2)}) %collective-permute-start.5) | collective-permute-done | bytes 524320 | tf_op jit(solution)/shard_map/ppermute | solution.py:27
  45.5 2.1 %collective-permute-done.9.near = bf16[3,2,128,128]{3,2,1,0:T(8,128)(2,1)S(1)} collective-permute-done((bf16[3,2,128,128]{3,2,1,0:T(8,128)(2,1)S(1)}, bf16[3,2,128,128]{3,2,1,0:T(8,128)(2,1)S(1)}, u32[]{:S(2)}, u32[]{:S(2)}) %collective-permute-start.9) | collective-permute-done | bytes 196640 | tf_op jit(solution)/shard_map/ppermute | solution.py:27
  47.6 1.0 %collective-permute-start.16 = (bf16[2,2,64,1024]{3,2,1,0:T(8,128)(2,1)S(1)}, bf16[2,2,64,1024]{3,2,1,0:T(8,128)(2,1)S(1)}, u32[]{:S(2)}, u32[]{:S(2)}) collective-permute-start(bf16[2,2,64,1024]{3,2,1,0:T(8,128)(2,1)S(1)} %collective-permute-done.5.refs_2_.refs_5_.refs_0_), channel_id=1, source_target_pairs={{0,2},{1,3},{2,4},{3,5},{4,6},{5,7},{6,8},{7,9},{8,10},{9,11},{10,... | collective-permute-start | bytes 1572872 | tf_op jit(solution)/shard_map/ppermute | solution.py:27
  48.6 0.0 collective-permute-done.13.refs_9_.refs_3_.refs_12_
  48.6 0.0 collective-permute-done.12.refs_5_.refs_1_.refs_4_
  48.6 0.6 shard_map.46
  49.2 1.3 %collective-permute-start.17 = (bf16[2,2,128,128]{3,2,1,0:T(8,128)(2,1)S(1)}, bf16[2,2,128,128]{3,2,1,0:T(8,128)(2,1)S(1)}, u32[]{:S(2)}, u32[]{:S(2)}) collective-permute-start(bf16[2,2,128,128]{3,2,1,0:T(8,128)(2,1)S(1)} %shard_map.46), channel_id=1, source_target_pairs={{0,33},{1,0},{2,35},{3,2},{4,37},{5,4},{6,39},{7,6},{8,41},{9,8},{... | collective-permute-start | bytes 393224 | tf_op jit(solution)/shard_map/ppermute | solution.py:27
  50.5 1.4 %collective-permute-start.15 = (bf16[2,2,64,1024]{3,2,1,0:T(8,128)(2,1)S(1)}, bf16[2,2,64,1024]{3,2,1,0:T(8,128)(2,1)S(1)}, u32[]{:S(2)}, u32[]{:S(2)}) collective-permute-start(bf16[2,2,64,1024]{3,2,1,0:T(8,128)(2,1)S(1)} %collective-permute-done.5.refs_2_.refs_5_.refs_0_), channel_id=1, source_target_pairs={{0,16},{1,17},{2,18},{3,19},{4,20},{5,21},{6,22},{7,23},{8,24},{9,... | collective-permute-start | bytes 1572872 | tf_op jit(solution)/shard_map/ppermute | solution.py:27
  52.0 1.3 %shard_map.44.refs_6_ = f32[256,1024]{1,0:T(8,128)S(1)} custom-call(s32[6]{0:T(128)S(1)} %pad_add_fusion.info.refs_0_, bf16[2,128,1024]{2,1,0:T(8,128)(2,1)S(1)} %collective-permute-done.4.refs_1_.a_ref, bf16[2,2,64,1024]{3,2,1,0:T(8,128)(2,1)S(1)} %collective-permute-done.1.refs_1_.refs_2_, ...), custom_call_target="tpu_custom_call" | custom-call | flops 1 | bytes 1048576 | tf_op jit(solution)/shard_map/pallas_call | solution.py:75
  53.3 0.0 collective-permute-done.11.refs_4_.refs_13_.refs_3_
  53.3 0.1 collective-permute-start.14
  53.4 4.2 %collective-permute-done.17.middle = bf16[2,2,128,128]{3,2,1,0:T(8,128)(2,1)S(1)} collective-permute-done((bf16[2,2,128,128]{3,2,1,0:T(8,128)(2,1)S(1)}, bf16[2,2,128,128]{3,2,1,0:T(8,128)(2,1)S(1)}, u32[]{:S(2)}, u32[]{:S(2)}) %collective-permute-start.17) | collective-permute-done | bytes 131104 | tf_op jit(solution)/shard_map/ppermute | solution.py:27
  57.6 0.9 %collective-permute-start.18 = (bf16[2,2,64,1024]{3,2,1,0:T(8,128)(2,1)S(1)}, bf16[2,2,64,1024]{3,2,1,0:T(8,128)(2,1)S(1)}, u32[]{:S(2)}, u32[]{:S(2)}) collective-permute-start(bf16[2,2,64,1024]{3,2,1,0:T(8,128)(2,1)S(1)} %collective-permute-done.16.refs_7_.refs_2_), channel_id=1, source_target_pairs={{0,16},{1,17},{2,18},{3,19},{4,20},{5,21},{6,22},{7,23},{8,24},{9,... | collective-permute-start | bytes 1572872 | tf_op jit(solution)/shard_map/ppermute | solution.py:27
  58.5 0.0 collective-permute-done.14.refs_3_.refs_6_.refs_1_
  58.5 1.0 %shard_map.45.acc = f32[256,1024]{1,0:T(8,128)S(1)} custom-call(s32[6]{0:T(128)S(1)} %pad_add_fusion.info.refs_0_, bf16[2,128,1024]{2,1,0:T(8,128)(2,1)S(1)} %collective-permute-done.4.refs_1_.a_ref, bf16[2,2,64,1024]{3,2,1,0:T(8,128)(2,1)S(1)} %collective-permute-done.5.refs_2_.refs_5_.refs_0_, ...), custom_call_target="tpu_custom_call" | custom-call | flops 1 | bytes 1048576 | tf_op jit(solution)/shard_map/pallas_call | solution.py:75
  59.5 0.5 collective-permute-done.18.refs_15_.refs_5_
  60.1 0.7 shard_map.48
  60.7 1.3 %collective-permute-start.19 = (bf16[3,2,128,128]{3,2,1,0:T(8,128)(2,1)S(1)}, bf16[3,2,128,128]{3,2,1,0:T(8,128)(2,1)S(1)}, u32[]{:S(2)}, u32[]{:S(2)}) collective-permute-start(bf16[3,2,128,128]{3,2,1,0:T(8,128)(2,1)S(1)} %shard_map.48), channel_id=1, source_target_pairs={{0,33},{1,0},{2,35},{3,2},{4,37},{5,4},{6,39},{7,6},{8,41},{9,8},{... | collective-permute-start | bytes 589832 | tf_op jit(solution)/shard_map/ppermute | solution.py:27
  62.0 2.4 %shard_map.47 = (bf16[2,64,1024]{2,1,0:T(8,128)(2,1)S(1)}, bf16[2,64,1024]{2,1,0:T(8,128)(2,1)S(1)}, f32[256,1024]{1,0:T(8,128)S(1)}, f32[8,128]{1,0:T(8,128)S(1)}) custom-call(s32[6]{0:T(128)S(1)} %pad_add_fusion.info.refs_0_, bf16[2,128,1024]{2,1,0:T(8,128)(2,1)S(1)} %collective-permute-done.4.refs_1_.a_ref, f32[256,1024]{1,0:T(8,128)S(1)} %shard_map.45.acc, ...), custom_call_target="tpu_custom_call" | custom-call | flops 3000000000 | bytes 1048576 | tf_op jit(solution)/shard_map/pallas_call | solution.py:75
  64.4 3.9 %collective-permute-start.22 = (bf16[2,64,1024]{2,1,0:T(8,128)(2,1)S(1)}, bf16[2,64,1024]{2,1,0:T(8,128)(2,1)S(1)}, u32[]{:S(2)}, u32[]{:S(2)}) collective-permute-start(bf16[2,64,1024]{2,1,0:T(8,128)(2,1)S(1)} %get-tuple-element.30), channel_id=1, source_target_pairs={{0,128},{1,112},{2,130},{3,114},{4,132},{5,116},{6,134},{7,118},{8... | collective-permute-start | bytes 786440 | tf_op jit(solution)/shard_map/ppermute | solution.py:27
  68.3 2.6 %collective-permute-done.19.late = bf16[3,2,128,128]{3,2,1,0:T(8,128)(2,1)S(1)} collective-permute-done((bf16[3,2,128,128]{3,2,1,0:T(8,128)(2,1)S(1)}, bf16[3,2,128,128]{3,2,1,0:T(8,128)(2,1)S(1)}, u32[]{:S(2)}, u32[]{:S(2)}) %collective-permute-start.19) | collective-permute-done | bytes 196640 | tf_op jit(solution)/shard_map/ppermute | solution.py:27
  70.9 0.7 shard_map.49
  71.6 0.0 collective-permute-start.21
  71.6 6.2 %collective-permute-start.20 = (f32[1,128]{1,0:T(1,128)S(1)}, f32[1,128]{1,0:T(1,128)S(1)}, u32[]{:S(2)}, u32[]{:S(2)}) collective-permute-start(f32[1,128]{1,0:T(1,128)S(1)} %shard_map.49), channel_id=1, source_target_pairs={{0,128},{1,112},{2,130},{3,114},{4,132},{5,116},{6,134},{7,118},{8... | collective-permute-start | bytes 1544 | tf_op jit(solution)/shard_map/ppermute | solution.py:27
  77.8 0.7 collective-permute-done.20
  78.5 0.0 collective-permute-done.22
  78.5 2.7 %collective-permute-start.25 = (f32[2,128]{1,0:T(2,128)S(1)}, f32[2,128]{1,0:T(2,128)S(1)}, u32[]{:S(2)}, u32[]{:S(2)}) collective-permute-start(f32[2,128]{1,0:T(2,128)S(1)} %maximum_select_fusion.1.own), channel_id=1, source_target_pairs={{0,10},{1,11},{2,12},{3,13},{4,14},{5,15},{6,0},{7,1},{8,2},{9,3},... | collective-permute-start | bytes 3080 | tf_op jit(solution)/shard_map/ppermute | solution.py:27
  81.2 0.6 collective-permute-start.24
  81.9 0.0 collective-permute-start.23
  81.9 1.1 %collective-permute-done.25.above = f32[2,128]{1,0:T(2,128)S(1)} collective-permute-done((f32[2,128]{1,0:T(2,128)S(1)}, f32[2,128]{1,0:T(2,128)S(1)}, u32[]{:S(2)}, u32[]{:S(2)}) %collective-permute-start.25) | collective-permute-done | bytes 1056 | tf_op jit(solution)/shard_map/ppermute | solution.py:27
  83.0 3.7 %collective-permute-done.24.below = f32[2,128]{1,0:T(2,128)S(1)} collective-permute-done((f32[2,128]{1,0:T(2,128)S(1)}, f32[2,128]{1,0:T(2,128)S(1)}, u32[]{:S(2)}, u32[]{:S(2)}) %collective-permute-start.24) | collective-permute-done | bytes 1056 | tf_op jit(solution)/shard_map/ppermute | solution.py:27
  86.7 0.5 shard_map.50
  87.2 0.8 collective-permute-start.27
  88.0 0.7 collective-permute-start.26
  88.8 0.4 collective-permute-done.23
  89.2 0.9 maximum_select_fusion
  90.1 0.0 collective-permute-done.27
  90.1 1.6 %collective-permute-done.26 = f32[2,128]{1,0:T(2,128)S(1)} collective-permute-done((f32[2,128]{1,0:T(2,128)S(1)}, f32[2,128]{1,0:T(2,128)S(1)}, u32[]{:S(2)}, u32[]{:S(2)}) %collective-permute-start.26) | collective-permute-done | bytes 1056 | tf_op jit(solution)/shard_map/ppermute | solution.py:27
  91.7 0.1 reshape.77
  91.8 0.6 broadcast_multiply_fusion
  (12 shorter events, 0.1 us)
Async XLA Ops:
  0.6 16.2 %copy-start = (s32[2,1,4]{2,1,0:T(1,128)S(1)}, s32[2,1,4]{2,1,0:T(1,128)}, u32[]{:S(2)}) copy-start(s32[2,1,4]{2,1,0:T(1,128)} %param.3) | copy-start | bytes 100
  0.6 10.6 %collective-permute-start = (bf16[2,2,64,1024]{3,2,1,0:T(8,128)(2,1)}, bf16[2,2,64,1024]{3,2,1,0:T(8,128)(2,1)S(1)}, u32[]{:S(2)}, u32[]{:S(2)}) collective-permute-start(bf16[2,2,64,1024]{3,2,1,0:T(8,128)(2,1)} %bitcast.15), channel_id=1, source_target_pairs={{0,128},{1,144},{2,130},{3,146},{4,132},{5,148},{6,134},{7,150},{8... | collective-permute-start | bytes 1572872 | tf_op jit(solution)/shard_map/ppermute | solution.py:27
  11.3 5.6 %collective-permute-start.3 = (bf16[2,2,64,1024]{3,2,1,0:T(8,128)(2,1)S(1)}, bf16[2,2,64,1024]{3,2,1,0:T(8,128)(2,1)S(1)}, u32[]{:S(2)}, u32[]{:S(2)}) collective-permute-start(bf16[2,2,64,1024]{3,2,1,0:T(8,128)(2,1)S(1)} %collective-permute-done.own.refs_2_.refs_0_), channel_id=1, source_target_pairs={{0,16},{1,17},{2,18},{3,19},{4,20},{5,21},{6,22},{7,23},{8,24},{9,... | collective-permute-start | bytes 1572872 | tf_op jit(solution)/shard_map/ppermute | solution.py:27
  12.8 10.2 %collective-permute-start.1 = (bf16[2,2,64,1024]{3,2,1,0:T(8,128)(2,1)S(1)}, bf16[2,2,64,1024]{3,2,1,0:T(8,128)(2,1)S(1)}, u32[]{:S(2)}, u32[]{:S(2)}) collective-permute-start(bf16[2,2,64,1024]{3,2,1,0:T(8,128)(2,1)S(1)} %collective-permute-done.own.refs_2_.refs_0_), channel_id=1, source_target_pairs={{0,2},{1,3},{2,4},{3,5},{4,6},{5,7},{6,8},{7,9},{8,10},{9,11},{10,... | collective-permute-start | bytes 1572872 | tf_op jit(solution)/shard_map/ppermute | solution.py:27
  16.9 11.7 %collective-permute-start.6 = (bf16[2,2,64,1024]{3,2,1,0:T(8,128)(2,1)S(1)}, bf16[2,2,64,1024]{3,2,1,0:T(8,128)(2,1)S(1)}, u32[]{:S(2)}, u32[]{:S(2)}) collective-permute-start(bf16[2,2,64,1024]{3,2,1,0:T(8,128)(2,1)S(1)} %collective-permute-done.3.other.refs_3_.refs_8_), channel_id=1, source_target_pairs={{0,2},{1,3},{2,4},{3,5},{4,6},{5,7},{6,8},{7,9},{8,10},{9,11},{10,... | collective-permute-start | bytes 1572872 | tf_op jit(solution)/shard_map/ppermute | solution.py:27
  19.4 14.8 %collective-permute-start.4 = (bf16[2,128,1024]{2,1,0:T(8,128)(2,1)S(1)}, bf16[2,128,1024]{2,1,0:T(8,128)(2,1)S(1)}, u32[]{:S(2)}, u32[]{:S(2)}) collective-permute-start(bf16[2,128,1024]{2,1,0:T(8,128)(2,1)S(1)} %shard_map.41), channel_id=1, source_target_pairs={{0,33},{1,0},{2,35},{3,2},{4,37},{5,4},{6,39},{7,6},{8,41},{9,8},{... | collective-permute-start | bytes 1572872 | tf_op jit(solution)/shard_map/ppermute | solution.py:27
  23.0 12.1 %collective-permute-start.2 = (bf16[2,2,64,1024]{3,2,1,0:T(8,128)(2,1)S(1)}, bf16[2,2,64,1024]{3,2,1,0:T(8,128)(2,1)S(1)}, u32[]{:S(2)}, u32[]{:S(2)}) collective-permute-start(bf16[2,2,64,1024]{3,2,1,0:T(8,128)(2,1)S(1)} %collective-permute-done.1.refs_1_.refs_2_), channel_id=1, source_target_pairs={{0,2},{1,3},{2,4},{3,5},{4,6},{5,7},{6,8},{7,9},{8,10},{9,11},{10,... | collective-permute-start | bytes 1572872 | tf_op jit(solution)/shard_map/ppermute | solution.py:27
  26.4 12.3 %collective-permute-start.8 = (bf16[2,2,64,1024]{3,2,1,0:T(8,128)(2,1)S(1)}, bf16[2,2,64,1024]{3,2,1,0:T(8,128)(2,1)S(1)}, u32[]{:S(2)}, u32[]{:S(2)}) collective-permute-start(bf16[2,2,64,1024]{3,2,1,0:T(8,128)(2,1)S(1)} %collective-permute-done.1.refs_1_.refs_2_), channel_id=1, source_target_pairs={{0,16},{1,17},{2,18},{3,19},{4,20},{5,21},{6,22},{7,23},{8,24},{9,... | collective-permute-start | bytes 1572872 | tf_op jit(solution)/shard_map/ppermute | solution.py:27
  28.6 12.2 %collective-permute-start.10 = (bf16[2,2,64,1024]{3,2,1,0:T(8,128)(2,1)S(1)}, bf16[2,2,64,1024]{3,2,1,0:T(8,128)(2,1)S(1)}, u32[]{:S(2)}, u32[]{:S(2)}) collective-permute-start(bf16[2,2,64,1024]{3,2,1,0:T(8,128)(2,1)S(1)} %collective-permute-done.6.refs_4_.refs_6_.refs_9_), channel_id=1, source_target_pairs={{0,2},{1,3},{2,4},{3,5},{4,6},{5,7},{6,8},{7,9},{8,10},{9,11},{10,... | collective-permute-start | bytes 1572872 | tf_op jit(solution)/shard_map/ppermute | solution.py:27
  31.7 7.0 %collective-permute-start.7 = (bf16[2,2,64,1024]{3,2,1,0:T(8,128)(2,1)S(1)}, bf16[2,2,64,1024]{3,2,1,0:T(8,128)(2,1)S(1)}, u32[]{:S(2)}, u32[]{:S(2)}) collective-permute-start(bf16[2,2,64,1024]{3,2,1,0:T(8,128)(2,1)S(1)} %collective-permute-done.6.refs_4_.refs_6_.refs_9_), channel_id=1, source_target_pairs={{0,16},{1,17},{2,18},{3,19},{4,20},{5,21},{6,22},{7,23},{8,24},{9,... | collective-permute-start | bytes 1572872 | tf_op jit(solution)/shard_map/ppermute | solution.py:27
  35.1 10.4 %collective-permute-start.5 = (bf16[2,2,64,1024]{3,2,1,0:T(8,128)(2,1)S(1)}, bf16[2,2,64,1024]{3,2,1,0:T(8,128)(2,1)S(1)}, u32[]{:S(2)}, u32[]{:S(2)}) collective-permute-start(bf16[2,2,64,1024]{3,2,1,0:T(8,128)(2,1)S(1)} %collective-permute-done.2.refs_4_.refs_0_.refs_3_), channel_id=1, source_target_pairs={{0,2},{1,3},{2,4},{3,5},{4,6},{5,7},{6,8},{7,9},{8,10},{9,11},{10,... | collective-permute-start | bytes 1572872 | tf_op jit(solution)/shard_map/ppermute | solution.py:27
  39.4 8.1 %collective-permute-start.9 = (bf16[3,2,128,128]{3,2,1,0:T(8,128)(2,1)S(1)}, bf16[3,2,128,128]{3,2,1,0:T(8,128)(2,1)S(1)}, u32[]{:S(2)}, u32[]{:S(2)}) collective-permute-start(bf16[3,2,128,128]{3,2,1,0:T(8,128)(2,1)S(1)} %shard_map.43), channel_id=1, source_target_pairs={{0,33},{1,0},{2,35},{3,2},{4,37},{5,4},{6,39},{7,6},{8,41},{9,8},{... | collective-permute-start | bytes 589832 | tf_op jit(solution)/shard_map/ppermute | solution.py:27
  39.5 9.1 %collective-permute-start.13 = (bf16[2,2,64,1024]{3,2,1,0:T(8,128)(2,1)S(1)}, bf16[2,2,64,1024]{3,2,1,0:T(8,128)(2,1)S(1)}, u32[]{:S(2)}, u32[]{:S(2)}) collective-permute-start(bf16[2,2,64,1024]{3,2,1,0:T(8,128)(2,1)S(1)} %collective-permute-done.2.refs_4_.refs_0_.refs_3_), channel_id=1, source_target_pairs={{0,16},{1,17},{2,18},{3,19},{4,20},{5,21},{6,22},{7,23},{8,24},{9,... | collective-permute-start | bytes 1572872 | tf_op jit(solution)/shard_map/ppermute | solution.py:27
  40.8 7.8 %collective-permute-start.12 = (bf16[2,2,64,1024]{3,2,1,0:T(8,128)(2,1)S(1)}, bf16[2,2,64,1024]{3,2,1,0:T(8,128)(2,1)S(1)}, u32[]{:S(2)}, u32[]{:S(2)}) collective-permute-start(bf16[2,2,64,1024]{3,2,1,0:T(8,128)(2,1)S(1)} %collective-permute-done.10.refs_8_.refs_2_.refs_11_), channel_id=1, source_target_pairs={{0,16},{1,17},{2,18},{3,19},{4,20},{5,21},{6,22},{7,23},{8,24},{9,... | collective-permute-start | bytes 1572872 | tf_op jit(solution)/shard_map/ppermute | solution.py:27
  41.7 11.6 %collective-permute-start.11 = (bf16[2,2,64,1024]{3,2,1,0:T(8,128)(2,1)S(1)}, bf16[2,2,64,1024]{3,2,1,0:T(8,128)(2,1)S(1)}, u32[]{:S(2)}, u32[]{:S(2)}) collective-permute-start(bf16[2,2,64,1024]{3,2,1,0:T(8,128)(2,1)S(1)} %collective-permute-done.10.refs_8_.refs_2_.refs_11_), channel_id=1, source_target_pairs={{0,2},{1,3},{2,4},{3,5},{4,6},{5,7},{6,8},{7,9},{8,10},{9,11},{10,... | collective-permute-start | bytes 1572872 | tf_op jit(solution)/shard_map/ppermute | solution.py:27
  47.6 10.0 %collective-permute-start.16 = (bf16[2,2,64,1024]{3,2,1,0:T(8,128)(2,1)S(1)}, bf16[2,2,64,1024]{3,2,1,0:T(8,128)(2,1)S(1)}, u32[]{:S(2)}, u32[]{:S(2)}) collective-permute-start(bf16[2,2,64,1024]{3,2,1,0:T(8,128)(2,1)S(1)} %collective-permute-done.5.refs_2_.refs_5_.refs_0_), channel_id=1, source_target_pairs={{0,2},{1,3},{2,4},{3,5},{4,6},{5,7},{6,8},{7,9},{8,10},{9,11},{10,... | collective-permute-start | bytes 1572872 | tf_op jit(solution)/shard_map/ppermute | solution.py:27
  49.2 8.3 %collective-permute-start.17 = (bf16[2,2,128,128]{3,2,1,0:T(8,128)(2,1)S(1)}, bf16[2,2,128,128]{3,2,1,0:T(8,128)(2,1)S(1)}, u32[]{:S(2)}, u32[]{:S(2)}) collective-permute-start(bf16[2,2,128,128]{3,2,1,0:T(8,128)(2,1)S(1)} %shard_map.46), channel_id=1, source_target_pairs={{0,33},{1,0},{2,35},{3,2},{4,37},{5,4},{6,39},{7,6},{8,41},{9,8},{... | collective-permute-start | bytes 393224 | tf_op jit(solution)/shard_map/ppermute | solution.py:27
  50.5 8.0 %collective-permute-start.15 = (bf16[2,2,64,1024]{3,2,1,0:T(8,128)(2,1)S(1)}, bf16[2,2,64,1024]{3,2,1,0:T(8,128)(2,1)S(1)}, u32[]{:S(2)}, u32[]{:S(2)}) collective-permute-start(bf16[2,2,64,1024]{3,2,1,0:T(8,128)(2,1)S(1)} %collective-permute-done.5.refs_2_.refs_5_.refs_0_), channel_id=1, source_target_pairs={{0,16},{1,17},{2,18},{3,19},{4,20},{5,21},{6,22},{7,23},{8,24},{9,... | collective-permute-start | bytes 1572872 | tf_op jit(solution)/shard_map/ppermute | solution.py:27
  53.3 5.2 %collective-permute-start.14 = (bf16[2,2,64,1024]{3,2,1,0:T(8,128)(2,1)S(1)}, bf16[2,2,64,1024]{3,2,1,0:T(8,128)(2,1)S(1)}, u32[]{:S(2)}, u32[]{:S(2)}) collective-permute-start(bf16[2,2,64,1024]{3,2,1,0:T(8,128)(2,1)S(1)} %collective-permute-done.11.refs_4_.refs_13_.refs_3_), channel_id=1, source_target_pairs={{0,16},{1,17},{2,18},{3,19},{4,20},{5,21},{6,22},{7,23},{8,24},{9,... | collective-permute-start | bytes 1572872 | tf_op jit(solution)/shard_map/ppermute | solution.py:27
  57.6 2.5 %collective-permute-start.18 = (bf16[2,2,64,1024]{3,2,1,0:T(8,128)(2,1)S(1)}, bf16[2,2,64,1024]{3,2,1,0:T(8,128)(2,1)S(1)}, u32[]{:S(2)}, u32[]{:S(2)}) collective-permute-start(bf16[2,2,64,1024]{3,2,1,0:T(8,128)(2,1)S(1)} %collective-permute-done.16.refs_7_.refs_2_), channel_id=1, source_target_pairs={{0,16},{1,17},{2,18},{3,19},{4,20},{5,21},{6,22},{7,23},{8,24},{9,... | collective-permute-start | bytes 1572872 | tf_op jit(solution)/shard_map/ppermute | solution.py:27
  60.7 10.1 %collective-permute-start.19 = (bf16[3,2,128,128]{3,2,1,0:T(8,128)(2,1)S(1)}, bf16[3,2,128,128]{3,2,1,0:T(8,128)(2,1)S(1)}, u32[]{:S(2)}, u32[]{:S(2)}) collective-permute-start(bf16[3,2,128,128]{3,2,1,0:T(8,128)(2,1)S(1)} %shard_map.48), channel_id=1, source_target_pairs={{0,33},{1,0},{2,35},{3,2},{4,37},{5,4},{6,39},{7,6},{8,41},{9,8},{... | collective-permute-start | bytes 589832 | tf_op jit(solution)/shard_map/ppermute | solution.py:27
  64.4 14.1 %collective-permute-start.22 = (bf16[2,64,1024]{2,1,0:T(8,128)(2,1)S(1)}, bf16[2,64,1024]{2,1,0:T(8,128)(2,1)S(1)}, u32[]{:S(2)}, u32[]{:S(2)}) collective-permute-start(bf16[2,64,1024]{2,1,0:T(8,128)(2,1)S(1)} %get-tuple-element.30), channel_id=1, source_target_pairs={{0,128},{1,112},{2,130},{3,114},{4,132},{5,116},{6,134},{7,118},{8... | collective-permute-start | bytes 786440 | tf_op jit(solution)/shard_map/ppermute | solution.py:27
  71.6 6.2 %collective-permute-start.21 = (f32[1,128]{1,0:T(1,128)S(1)}, f32[1,128]{1,0:T(1,128)S(1)}, u32[]{:S(2)}, u32[]{:S(2)}) collective-permute-start(f32[1,128]{1,0:T(1,128)S(1)} %shard_map.49), channel_id=1, source_target_pairs={{0,129},{1,113},{2,131},{3,115},{4,133},{5,117},{6,135},{7,119},{8... | collective-permute-start | bytes 1544 | tf_op jit(solution)/shard_map/ppermute | solution.py:27
  71.6 6.9 %collective-permute-start.20 = (f32[1,128]{1,0:T(1,128)S(1)}, f32[1,128]{1,0:T(1,128)S(1)}, u32[]{:S(2)}, u32[]{:S(2)}) collective-permute-start(f32[1,128]{1,0:T(1,128)S(1)} %shard_map.49), channel_id=1, source_target_pairs={{0,128},{1,112},{2,130},{3,114},{4,132},{5,116},{6,134},{7,118},{8... | collective-permute-start | bytes 1544 | tf_op jit(solution)/shard_map/ppermute | solution.py:27
  78.5 4.4 %collective-permute-start.25 = (f32[2,128]{1,0:T(2,128)S(1)}, f32[2,128]{1,0:T(2,128)S(1)}, u32[]{:S(2)}, u32[]{:S(2)}) collective-permute-start(f32[2,128]{1,0:T(2,128)S(1)} %maximum_select_fusion.1.own), channel_id=1, source_target_pairs={{0,10},{1,11},{2,12},{3,13},{4,14},{5,15},{6,0},{7,1},{8,2},{9,3},... | collective-permute-start | bytes 3080 | tf_op jit(solution)/shard_map/ppermute | solution.py:27
  81.2 5.4 %collective-permute-start.24 = (f32[2,128]{1,0:T(2,128)S(1)}, f32[2,128]{1,0:T(2,128)S(1)}, u32[]{:S(2)}, u32[]{:S(2)}) collective-permute-start(f32[2,128]{1,0:T(2,128)S(1)} %maximum_select_fusion.1.own), channel_id=1, source_target_pairs={{0,6},{1,7},{2,8},{3,9},{4,10},{5,11},{6,12},{7,13},{8,14},{9,15},... | collective-permute-start | bytes 3080 | tf_op jit(solution)/shard_map/ppermute | solution.py:27
  81.9 7.3 %collective-permute-start.23 = (bf16[2,64,1024]{2,1,0:T(8,128)(2,1)S(1)}, bf16[2,64,1024]{2,1,0:T(8,128)(2,1)S(1)}, u32[]{:S(2)}, u32[]{:S(2)}) collective-permute-start(bf16[2,64,1024]{2,1,0:T(8,128)(2,1)S(1)} %get-tuple-element.32), channel_id=1, source_target_pairs={{0,129},{1,113},{2,131},{3,115},{4,133},{5,117},{6,135},{7,119},{8... | collective-permute-start | bytes 786440 | tf_op jit(solution)/shard_map/ppermute | solution.py:27
  87.2 2.9 %collective-permute-start.27 = (f32[2,128]{1,0:T(2,128)S(1)}, f32[2,128]{1,0:T(2,128)S(1)}, u32[]{:S(2)}, u32[]{:S(2)}) collective-permute-start(f32[2,128]{1,0:T(2,128)S(1)} %get-tuple-element.35), channel_id=1, source_target_pairs={{0,14},{1,15},{2,0},{3,1},{4,2},{5,3},{6,4},{7,5},{8,6},{9,7},{10,... | collective-permute-start | bytes 3080 | tf_op jit(solution)/shard_map/ppermute | solution.py:27
  88.0 3.6 %collective-permute-start.26 = (f32[2,128]{1,0:T(2,128)S(1)}, f32[2,128]{1,0:T(2,128)S(1)}, u32[]{:S(2)}, u32[]{:S(2)}) collective-permute-start(f32[2,128]{1,0:T(2,128)S(1)} %get-tuple-element.34), channel_id=1, source_target_pairs={{0,2},{1,3},{2,4},{3,5},{4,6},{5,7},{6,8},{7,9},{8,10},{9,11},{10,... | collective-permute-start | bytes 3080 | tf_op jit(solution)/shard_map/ppermute | solution.py:27

commit v19 on v18

--- a/solution.py
+++ b/solution.py
@@ -181,11 +181,6 @@
     trace[...] = jnp.where(lane == 2 * info[0], re, jnp.where(lane == 2 * info[0] + 1, im, 0.0))
 
 
-def add_kernel(info, below, own, above, two, three):
-    two[...] = below[...] + own[...]
-    three[...] = below[...] + own[...] + above[...]
-
-
 def shards(fields, mom_table):
     rows = fields[:, 0]
     tm, row = lax.axis_index("tm"), lax.axis_index("row")
@@ -247,8 +242,7 @@
     both = jnp.where(half == 0, jnp.concatenate([first, second]), jnp.concatenate([second, first]))
     both, kept = wall((both, kept))
     below, above = moved(both, along(3)), moved(both, along(-3))
-    pair = jax.ShapeDtypeStruct((2, 128), F32)
-    two, three = call(add_kernel, info, [below, both, above], (pair, pair), WEIGHT)
+    two, three = below + both, below + both + above
     below, above = moved(three, along(1)), moved(two, along(-1))
     both = below + three + above
     products = jnp.where(half == 0, jnp.stack([kept, sent]), jnp.stack([sent, kept]))[:, None, None]

time: 93 us -> 92.4 us (level)
    pallas_call x10 -> x9, Pallas kernels: 9.37 us -> 8.83 us  [call(): pl.pallas_call(kernel, out_shape=out_shape, in_specs=[SMEM] + [VMEM] * le...]
where the time goes in v19:
time: 92.4 us; the launch traced here: 91.7 us
  starting transfers between devices  48.4 us (52%)
  waiting for transfers between devices  32.1 us (35%)
  Pallas kernels  8.83 us (10%)
  other arithmetic  1.55 us (2%)
    ppermute x28, starting transfers between devices, moved(): lax.ppermute(block, BOTH, [(index_of(*at), index_of(*route(*at))) for at...  48.4 us
    ppermute x28, waiting for transfers between devices, moved(): lax.ppermute(block, BOTH, [(index_of(*at), index_of(*route(*at))) for at...  32.1 us
    pallas_call x9, Pallas kernels, call(): pl.pallas_call(kernel, out_shape=out_shape, in_specs=[SMEM] + [VMEM] * le...  8.83 us
  transfers between devices with their start and end apart: 28, of which 14 were waited for; matrix products, arithmetic and copies ran while one was open for 1% of the time, Pallas kernels for 9%

profile of v19, /device:TPU:1, one launch (start us, length us, event | category | flops | bytes accessed | tf_op | source)
XLA Modules:
  0.0 91.7 jit_solution(14164853672757465564)
XLA Ops:
  0.6 0.0 copy-start
  0.6 4.2 %collective-permute-start = (bf16[2,2,64,1024]{3,2,1,0:T(8,128)(2,1)}, bf16[2,2,64,1024]{3,2,1,0:T(8,128)(2,1)S(1)}, u32[]{:S(2)}, u32[]{:S(2)}) collective-permute-start(bf16[2,2,64,1024]{3,2,1,0:T(8,128)(2,1)} %bitcast.15), channel_id=1, source_target_pairs={{0,128},{1,144},{2,130},{3,146},{4,132},{5,148},{6,134},{7,150},{8... | collective-permute-start | bytes 1572872 | tf_op jit(solution)/shard_map/ppermute | solution.py:27
  4.8 6.4 %collective-permute-done.own.refs_2_.refs_0_ = bf16[2,2,64,1024]{3,2,1,0:T(8,128)(2,1)S(1)} collective-permute-done((bf16[2,2,64,1024]{3,2,1,0:T(8,128)(2,1)}, bf16[2,2,64,1024]{3,2,1,0:T(8,128)(2,1)S(1)}, u32[]{:S(2)}, u32[]{:S(2)}) %collective-permute-start) | collective-permute-done | bytes 524320 | tf_op jit(solution)/shard_map/ppermute | solution.py:27
  11.3 1.5 %collective-permute-start.3 = (bf16[2,2,64,1024]{3,2,1,0:T(8,128)(2,1)S(1)}, bf16[2,2,64,1024]{3,2,1,0:T(8,128)(2,1)S(1)}, u32[]{:S(2)}, u32[]{:S(2)}) collective-permute-start(bf16[2,2,64,1024]{3,2,1,0:T(8,128)(2,1)S(1)} %collective-permute-done.own.refs_2_.refs_0_), channel_id=1, source_target_pairs={{0,16},{1,17},{2,18},{3,19},{4,20},{5,21},{6,22},{7,23},{8,24},{9,... | collective-permute-start | bytes 1572872 | tf_op jit(solution)/shard_map/ppermute | solution.py:27
  12.8 4.1 %collective-permute-start.1 = (bf16[2,2,64,1024]{3,2,1,0:T(8,128)(2,1)S(1)}, bf16[2,2,64,1024]{3,2,1,0:T(8,128)(2,1)S(1)}, u32[]{:S(2)}, u32[]{:S(2)}) collective-permute-start(bf16[2,2,64,1024]{3,2,1,0:T(8,128)(2,1)S(1)} %collective-permute-done.own.refs_2_.refs_0_), channel_id=1, source_target_pairs={{0,2},{1,3},{2,4},{3,5},{4,6},{5,7},{6,8},{7,9},{8,10},{9,11},{10,... | collective-permute-start | bytes 1572872 | tf_op jit(solution)/shard_map/ppermute | solution.py:27
  16.9 0.0 collective-permute-done.3.other.refs_3_.refs_8_
  16.9 1.9 %collective-permute-start.6 = (bf16[2,2,64,1024]{3,2,1,0:T(8,128)(2,1)S(1)}, bf16[2,2,64,1024]{3,2,1,0:T(8,128)(2,1)S(1)}, u32[]{:S(2)}, u32[]{:S(2)}) collective-permute-start(bf16[2,2,64,1024]{3,2,1,0:T(8,128)(2,1)S(1)} %collective-permute-done.3.other.refs_3_.refs_8_), channel_id=1, source_target_pairs={{0,2},{1,3},{2,4},{3,5},{4,6},{5,7},{6,8},{7,9},{8,10},{9,11},{10,... | collective-permute-start | bytes 1572872 | tf_op jit(solution)/shard_map/ppermute | solution.py:27
  18.8 0.1 pad_add_fusion.info.refs_0_
  18.9 0.6 shard_map.41
  19.4 1.3 %collective-permute-start.4 = (bf16[2,128,1024]{2,1,0:T(8,128)(2,1)S(1)}, bf16[2,128,1024]{2,1,0:T(8,128)(2,1)S(1)}, u32[]{:S(2)}, u32[]{:S(2)}) collective-permute-start(bf16[2,128,1024]{2,1,0:T(8,128)(2,1)S(1)} %shard_map.41), channel_id=1, source_target_pairs={{0,33},{1,0},{2,35},{3,2},{4,37},{5,4},{6,39},{7,6},{8,41},{9,8},{... | collective-permute-start | bytes 1572872 | tf_op jit(solution)/shard_map/ppermute | solution.py:27
  20.7 2.3 %collective-permute-done.1.refs_1_.refs_2_ = bf16[2,2,64,1024]{3,2,1,0:T(8,128)(2,1)S(1)} collective-permute-done((bf16[2,2,64,1024]{3,2,1,0:T(8,128)(2,1)S(1)}, bf16[2,2,64,1024]{3,2,1,0:T(8,128)(2,1)S(1)}, u32[]{:S(2)}, u32[]{:S(2)}) %collective-permute-start.1) | collective-permute-done | bytes 524320 | tf_op jit(solution)/shard_map/ppermute | solution.py:27
  23.0 3.4 %collective-permute-start.2 = (bf16[2,2,64,1024]{3,2,1,0:T(8,128)(2,1)S(1)}, bf16[2,2,64,1024]{3,2,1,0:T(8,128)(2,1)S(1)}, u32[]{:S(2)}, u32[]{:S(2)}) collective-permute-start(bf16[2,2,64,1024]{3,2,1,0:T(8,128)(2,1)S(1)} %collective-permute-done.1.refs_1_.refs_2_), channel_id=1, source_target_pairs={{0,2},{1,3},{2,4},{3,5},{4,6},{5,7},{6,8},{7,9},{8,10},{9,11},{10,... | collective-permute-start | bytes 1572872 | tf_op jit(solution)/shard_map/ppermute | solution.py:27
  26.4 0.0 collective-permute-start.8
  26.4 2.2 %collective-permute-done.6.refs_4_.refs_6_.refs_9_ = bf16[2,2,64,1024]{3,2,1,0:T(8,128)(2,1)S(1)} collective-permute-done((bf16[2,2,64,1024]{3,2,1,0:T(8,128)(2,1)S(1)}, bf16[2,2,64,1024]{3,2,1,0:T(8,128)(2,1)S(1)}, u32[]{:S(2)}, u32[]{:S(2)}) %collective-permute-start.6) | collective-permute-done | bytes 524320 | tf_op jit(solution)/shard_map/ppermute | solution.py:27
  28.6 3.1 %collective-permute-start.10 = (bf16[2,2,64,1024]{3,2,1,0:T(8,128)(2,1)S(1)}, bf16[2,2,64,1024]{3,2,1,0:T(8,128)(2,1)S(1)}, u32[]{:S(2)}, u32[]{:S(2)}) collective-permute-start(bf16[2,2,64,1024]{3,2,1,0:T(8,128)(2,1)S(1)} %collective-permute-done.6.refs_4_.refs_6_.refs_9_), channel_id=1, source_target_pairs={{0,2},{1,3},{2,4},{3,5},{4,6},{5,7},{6,8},{7,9},{8,10},{9,11},{10,... | collective-permute-start | bytes 1572872 | tf_op jit(solution)/shard_map/ppermute | solution.py:27
  31.7 0.0 collective-permute-start.7
  31.7 2.5 %collective-permute-done.4.refs_1_.a_ref = bf16[2,128,1024]{2,1,0:T(8,128)(2,1)S(1)} collective-permute-done((bf16[2,128,1024]{2,1,0:T(8,128)(2,1)S(1)}, bf16[2,128,1024]{2,1,0:T(8,128)(2,1)S(1)}, u32[]{:S(2)}, u32[]{:S(2)}) %collective-permute-start.4) | collective-permute-done | bytes 524320 | tf_op jit(solution)/shard_map/ppermute | solution.py:27
  34.2 0.8 shard_map.42.refs_10_
  35.1 0.0 collective-permute-done.2.refs_4_.refs_0_.refs_3_
  35.1 3.7 %collective-permute-start.5 = (bf16[2,2,64,1024]{3,2,1,0:T(8,128)(2,1)S(1)}, bf16[2,2,64,1024]{3,2,1,0:T(8,128)(2,1)S(1)}, u32[]{:S(2)}, u32[]{:S(2)}) collective-permute-start(bf16[2,2,64,1024]{3,2,1,0:T(8,128)(2,1)S(1)} %collective-permute-done.2.refs_4_.refs_0_.refs_3_), channel_id=1, source_target_pairs={{0,2},{1,3},{2,4},{3,5},{4,6},{5,7},{6,8},{7,9},{8,10},{9,11},{10,... | collective-permute-start | bytes 1572872 | tf_op jit(solution)/shard_map/ppermute | solution.py:27
  38.8 0.0 collective-permute-done.8.refs_5_.refs_7_.refs_10_
  38.8 0.0 collective-permute-done.7.refs_2_.refs_3_
  38.8 0.7 shard_map.43
  39.4 0.1 collective-permute-start.9
  39.5 1.2 %collective-permute-start.13 = (bf16[2,2,64,1024]{3,2,1,0:T(8,128)(2,1)S(1)}, bf16[2,2,64,1024]{3,2,1,0:T(8,128)(2,1)S(1)}, u32[]{:S(2)}, u32[]{:S(2)}) collective-permute-start(bf16[2,2,64,1024]{3,2,1,0:T(8,128)(2,1)S(1)} %collective-permute-done.2.refs_4_.refs_0_.refs_3_), channel_id=1, source_target_pairs={{0,16},{1,17},{2,18},{3,19},{4,20},{5,21},{6,22},{7,23},{8,24},{9,... | collective-permute-start | bytes 1572872 | tf_op jit(solution)/shard_map/ppermute | solution.py:27
  40.8 0.0 collective-permute-done.10.refs_8_.refs_2_.refs_11_
  40.8 0.9 collective-permute-start.12
  41.7 2.1 %collective-permute-start.11 = (bf16[2,2,64,1024]{3,2,1,0:T(8,128)(2,1)S(1)}, bf16[2,2,64,1024]{3,2,1,0:T(8,128)(2,1)S(1)}, u32[]{:S(2)}, u32[]{:S(2)}) collective-permute-start(bf16[2,2,64,1024]{3,2,1,0:T(8,128)(2,1)S(1)} %collective-permute-done.10.refs_8_.refs_2_.refs_11_), channel_id=1, source_target_pairs={{0,2},{1,3},{2,4},{3,5},{4,6},{5,7},{6,8},{7,9},{8,10},{9,11},{10,... | collective-permute-start | bytes 1572872 | tf_op jit(solution)/shard_map/ppermute | solution.py:27
  43.7 1.7 %collective-permute-done.5.refs_2_.refs_5_.refs_0_ = bf16[2,2,64,1024]{3,2,1,0:T(8,128)(2,1)S(1)} collective-permute-done((bf16[2,2,64,1024]{3,2,1,0:T(8,128)(2,1)S(1)}, bf16[2,2,64,1024]{3,2,1,0:T(8,128)(2,1)S(1)}, u32[]{:S(2)}, u32[]{:S(2)}) %collective-permute-start.5) | collective-permute-done | bytes 524320 | tf_op jit(solution)/shard_map/ppermute | solution.py:27
  45.5 2.1 %collective-permute-done.9.near = bf16[3,2,128,128]{3,2,1,0:T(8,128)(2,1)S(1)} collective-permute-done((bf16[3,2,128,128]{3,2,1,0:T(8,128)(2,1)S(1)}, bf16[3,2,128,128]{3,2,1,0:T(8,128)(2,1)S(1)}, u32[]{:S(2)}, u32[]{:S(2)}) %collective-permute-start.9) | collective-permute-done | bytes 196640 | tf_op jit(solution)/shard_map/ppermute | solution.py:27
  47.6 1.0 %collective-permute-start.16 = (bf16[2,2,64,1024]{3,2,1,0:T(8,128)(2,1)S(1)}, bf16[2,2,64,1024]{3,2,1,0:T(8,128)(2,1)S(1)}, u32[]{:S(2)}, u32[]{:S(2)}) collective-permute-start(bf16[2,2,64,1024]{3,2,1,0:T(8,128)(2,1)S(1)} %collective-permute-done.5.refs_2_.refs_5_.refs_0_), channel_id=1, source_target_pairs={{0,2},{1,3},{2,4},{3,5},{4,6},{5,7},{6,8},{7,9},{8,10},{9,11},{10,... | collective-permute-start | bytes 1572872 | tf_op jit(solution)/shard_map/ppermute | solution.py:27
  48.6 0.6 shard_map.46
  49.2 1.3 %collective-permute-start.17 = (bf16[2,2,128,128]{3,2,1,0:T(8,128)(2,1)S(1)}, bf16[2,2,128,128]{3,2,1,0:T(8,128)(2,1)S(1)}, u32[]{:S(2)}, u32[]{:S(2)}) collective-permute-start(bf16[2,2,128,128]{3,2,1,0:T(8,128)(2,1)S(1)} %shard_map.46), channel_id=1, source_target_pairs={{0,33},{1,0},{2,35},{3,2},{4,37},{5,4},{6,39},{7,6},{8,41},{9,8},{... | collective-permute-start | bytes 393224 | tf_op jit(solution)/shard_map/ppermute | solution.py:27
  50.5 1.4 %collective-permute-start.15 = (bf16[2,2,64,1024]{3,2,1,0:T(8,128)(2,1)S(1)}, bf16[2,2,64,1024]{3,2,1,0:T(8,128)(2,1)S(1)}, u32[]{:S(2)}, u32[]{:S(2)}) collective-permute-start(bf16[2,2,64,1024]{3,2,1,0:T(8,128)(2,1)S(1)} %collective-permute-done.5.refs_2_.refs_5_.refs_0_), channel_id=1, source_target_pairs={{0,16},{1,17},{2,18},{3,19},{4,20},{5,21},{6,22},{7,23},{8,24},{9,... | collective-permute-start | bytes 1572872 | tf_op jit(solution)/shard_map/ppermute | solution.py:27
  52.0 1.3 %shard_map.44.refs_6_ = f32[256,1024]{1,0:T(8,128)S(1)} custom-call(s32[6]{0:T(128)S(1)} %pad_add_fusion.info.refs_0_, bf16[2,128,1024]{2,1,0:T(8,128)(2,1)S(1)} %collective-permute-done.4.refs_1_.a_ref, bf16[2,2,64,1024]{3,2,1,0:T(8,128)(2,1)S(1)} %collective-permute-done.1.refs_1_.refs_2_, ...), custom_call_target="tpu_custom_call" | custom-call | flops 1 | bytes 1048576 | tf_op jit(solution)/shard_map/pallas_call | solution.py:75
  53.3 0.1 collective-permute-start.14
  53.4 4.2 %collective-permute-done.17.middle = bf16[2,2,128,128]{3,2,1,0:T(8,128)(2,1)S(1)} collective-permute-done((bf16[2,2,128,128]{3,2,1,0:T(8,128)(2,1)S(1)}, bf16[2,2,128,128]{3,2,1,0:T(8,128)(2,1)S(1)}, u32[]{:S(2)}, u32[]{:S(2)}) %collective-permute-start.17) | collective-permute-done | bytes 131104 | tf_op jit(solution)/shard_map/ppermute | solution.py:27
  57.6 0.9 %collective-permute-start.18 = (bf16[2,2,64,1024]{3,2,1,0:T(8,128)(2,1)S(1)}, bf16[2,2,64,1024]{3,2,1,0:T(8,128)(2,1)S(1)}, u32[]{:S(2)}, u32[]{:S(2)}) collective-permute-start(bf16[2,2,64,1024]{3,2,1,0:T(8,128)(2,1)S(1)} %collective-permute-done.16.refs_7_.refs_2_), channel_id=1, source_target_pairs={{0,16},{1,17},{2,18},{3,19},{4,20},{5,21},{6,22},{7,23},{8,24},{9,... | collective-permute-start | bytes 1572872 | tf_op jit(solution)/shard_map/ppermute | solution.py:27
  58.5 0.0 collective-permute-done.15.refs_5_.refs_14_.refs_4_
  58.5 0.0 collective-permute-done.14.refs_3_.refs_6_.refs_1_
  58.5 1.0 %shard_map.45.acc = f32[256,1024]{1,0:T(8,128)S(1)} custom-call(s32[6]{0:T(128)S(1)} %pad_add_fusion.info.refs_0_, bf16[2,128,1024]{2,1,0:T(8,128)(2,1)S(1)} %collective-permute-done.4.refs_1_.a_ref, bf16[2,2,64,1024]{3,2,1,0:T(8,128)(2,1)S(1)} %collective-permute-done.5.refs_2_.refs_5_.refs_0_, ...), custom_call_target="tpu_custom_call" | custom-call | flops 1 | bytes 1048576 | tf_op jit(solution)/shard_map/pallas_call | solution.py:75
  59.5 0.5 collective-permute-done.18.refs_15_.refs_5_
  60.1 0.7 shard_map.48
  60.7 1.3 %collective-permute-start.19 = (bf16[3,2,128,128]{3,2,1,0:T(8,128)(2,1)S(1)}, bf16[3,2,128,128]{3,2,1,0:T(8,128)(2,1)S(1)}, u32[]{:S(2)}, u32[]{:S(2)}) collective-permute-start(bf16[3,2,128,128]{3,2,1,0:T(8,128)(2,1)S(1)} %shard_map.48), channel_id=1, source_target_pairs={{0,33},{1,0},{2,35},{3,2},{4,37},{5,4},{6,39},{7,6},{8,41},{9,8},{... | collective-permute-start | bytes 589832 | tf_op jit(solution)/shard_map/ppermute | solution.py:27
  62.0 2.4 %shard_map.47 = (bf16[2,64,1024]{2,1,0:T(8,128)(2,1)S(1)}, bf16[2,64,1024]{2,1,0:T(8,128)(2,1)S(1)}, f32[256,1024]{1,0:T(8,128)S(1)}, f32[8,128]{1,0:T(8,128)S(1)}) custom-call(s32[6]{0:T(128)S(1)} %pad_add_fusion.info.refs_0_, bf16[2,128,1024]{2,1,0:T(8,128)(2,1)S(1)} %collective-permute-done.4.refs_1_.a_ref, f32[256,1024]{1,0:T(8,128)S(1)} %shard_map.45.acc, ...), custom_call_target="tpu_custom_call" | custom-call | flops 3000000000 | bytes 1048576 | tf_op jit(solution)/shard_map/pallas_call | solution.py:75
  64.4 3.9 %collective-permute-start.22 = (bf16[2,64,1024]{2,1,0:T(8,128)(2,1)S(1)}, bf16[2,64,1024]{2,1,0:T(8,128)(2,1)S(1)}, u32[]{:S(2)}, u32[]{:S(2)}) collective-permute-start(bf16[2,64,1024]{2,1,0:T(8,128)(2,1)S(1)} %get-tuple-element.28), channel_id=1, source_target_pairs={{0,128},{1,112},{2,130},{3,114},{4,132},{5,116},{6,134},{7,118},{8... | collective-permute-start | bytes 786440 | tf_op jit(solution)/shard_map/ppermute | solution.py:27
  68.3 2.6 %collective-permute-done.19.late = bf16[3,2,128,128]{3,2,1,0:T(8,128)(2,1)S(1)} collective-permute-done((bf16[3,2,128,128]{3,2,1,0:T(8,128)(2,1)S(1)}, bf16[3,2,128,128]{3,2,1,0:T(8,128)(2,1)S(1)}, u32[]{:S(2)}, u32[]{:S(2)}) %collective-permute-start.19) | collective-permute-done | bytes 196640 | tf_op jit(solution)/shard_map/ppermute | solution.py:27
  70.9 0.7 shard_map.49
  71.6 0.0 collective-permute-start.21
  71.6 6.2 %collective-permute-start.20 = (f32[1,128]{1,0:T(1,128)S(1)}, f32[1,128]{1,0:T(1,128)S(1)}, u32[]{:S(2)}, u32[]{:S(2)}) collective-permute-start(f32[1,128]{1,0:T(1,128)S(1)} %shard_map.49), channel_id=1, source_target_pairs={{0,128},{1,112},{2,130},{3,114},{4,132},{5,116},{6,134},{7,118},{8... | collective-permute-start | bytes 1544 | tf_op jit(solution)/shard_map/ppermute | solution.py:27
  77.8 0.0 collective-permute-start.23
  77.8 0.0 collective-permute-done.21
  77.8 0.7 collective-permute-done.20
  78.5 2.7 %collective-permute-start.25 = (f32[2,128]{1,0:T(2,128)S(1)}, f32[2,128]{1,0:T(2,128)S(1)}, u32[]{:S(2)}, u32[]{:S(2)}) collective-permute-start(f32[2,128]{1,0:T(2,128)S(1)} %maximum_select_fusion.1), channel_id=1, source_target_pairs={{0,10},{1,11},{2,12},{3,13},{4,14},{5,15},{6,0},{7,1},{8,2},{9,3},... | collective-permute-start | bytes 3080 | tf_op jit(solution)/shard_map/ppermute | solution.py:27
  81.2 0.6 collective-permute-start.24
  81.9 1.1 %collective-permute-done.25 = f32[2,128]{1,0:T(2,128)S(1)} collective-permute-done((f32[2,128]{1,0:T(2,128)S(1)}, f32[2,128]{1,0:T(2,128)S(1)}, u32[]{:S(2)}, u32[]{:S(2)}) %collective-permute-start.25) | collective-permute-done | bytes 1056 | tf_op jit(solution)/shard_map/ppermute | solution.py:27
  83.0 3.7 %collective-permute-done.24 = f32[2,128]{1,0:T(2,128)S(1)} collective-permute-done((f32[2,128]{1,0:T(2,128)S(1)}, f32[2,128]{1,0:T(2,128)S(1)}, u32[]{:S(2)}, u32[]{:S(2)}) %collective-permute-start.24) | collective-permute-done | bytes 1056 | tf_op jit(solution)/shard_map/ppermute | solution.py:27
  86.7 0.7 collective-permute-start.27
  87.4 0.7 collective-permute-start.26
  88.1 0.9 maximum_select_fusion
  89.0 0.1 collective-permute-done.27
  89.1 1.9 %collective-permute-done.26 = f32[2,128]{1,0:T(2,128)S(1)} collective-permute-done((f32[2,128]{1,0:T(2,128)S(1)}, f32[2,128]{1,0:T(2,128)S(1)}, u32[]{:S(2)}, u32[]{:S(2)}) %collective-permute-start.26) | collective-permute-done | bytes 1056 | tf_op jit(solution)/shard_map/ppermute | solution.py:27
  91.0 0.1 reshape.77
  91.1 0.6 broadcast_multiply_fusion
  (12 shorter events, 0.1 us)
Async XLA Ops:
  0.6 16.2 %copy-start = (s32[2,1,4]{2,1,0:T(1,128)S(1)}, s32[2,1,4]{2,1,0:T(1,128)}, u32[]{:S(2)}) copy-start(s32[2,1,4]{2,1,0:T(1,128)} %param.3) | copy-start | bytes 100
  0.6 10.6 %collective-permute-start = (bf16[2,2,64,1024]{3,2,1,0:T(8,128)(2,1)}, bf16[2,2,64,1024]{3,2,1,0:T(8,128)(2,1)S(1)}, u32[]{:S(2)}, u32[]{:S(2)}) collective-permute-start(bf16[2,2,64,1024]{3,2,1,0:T(8,128)(2,1)} %bitcast.15), channel_id=1, source_target_pairs={{0,128},{1,144},{2,130},{3,146},{4,132},{5,148},{6,134},{7,150},{8... | collective-permute-start | bytes 1572872 | tf_op jit(solution)/shard_map/ppermute | solution.py:27
  11.3 5.6 %collective-permute-start.3 = (bf16[2,2,64,1024]{3,2,1,0:T(8,128)(2,1)S(1)}, bf16[2,2,64,1024]{3,2,1,0:T(8,128)(2,1)S(1)}, u32[]{:S(2)}, u32[]{:S(2)}) collective-permute-start(bf16[2,2,64,1024]{3,2,1,0:T(8,128)(2,1)S(1)} %collective-permute-done.own.refs_2_.refs_0_), channel_id=1, source_target_pairs={{0,16},{1,17},{2,18},{3,19},{4,20},{5,21},{6,22},{7,23},{8,24},{9,... | collective-permute-start | bytes 1572872 | tf_op jit(solution)/shard_map/ppermute | solution.py:27
  12.8 10.2 %collective-permute-start.1 = (bf16[2,2,64,1024]{3,2,1,0:T(8,128)(2,1)S(1)}, bf16[2,2,64,1024]{3,2,1,0:T(8,128)(2,1)S(1)}, u32[]{:S(2)}, u32[]{:S(2)}) collective-permute-start(bf16[2,2,64,1024]{3,2,1,0:T(8,128)(2,1)S(1)} %collective-permute-done.own.refs_2_.refs_0_), channel_id=1, source_target_pairs={{0,2},{1,3},{2,4},{3,5},{4,6},{5,7},{6,8},{7,9},{8,10},{9,11},{10,... | collective-permute-start | bytes 1572872 | tf_op jit(solution)/shard_map/ppermute | solution.py:27
  16.9 11.7 %collective-permute-start.6 = (bf16[2,2,64,1024]{3,2,1,0:T(8,128)(2,1)S(1)}, bf16[2,2,64,1024]{3,2,1,0:T(8,128)(2,1)S(1)}, u32[]{:S(2)}, u32[]{:S(2)}) collective-permute-start(bf16[2,2,64,1024]{3,2,1,0:T(8,128)(2,1)S(1)} %collective-permute-done.3.other.refs_3_.refs_8_), channel_id=1, source_target_pairs={{0,2},{1,3},{2,4},{3,5},{4,6},{5,7},{6,8},{7,9},{8,10},{9,11},{10,... | collective-permute-start | bytes 1572872 | tf_op jit(solution)/shard_map/ppermute | solution.py:27
  19.4 14.8 %collective-permute-start.4 = (bf16[2,128,1024]{2,1,0:T(8,128)(2,1)S(1)}, bf16[2,128,1024]{2,1,0:T(8,128)(2,1)S(1)}, u32[]{:S(2)}, u32[]{:S(2)}) collective-permute-start(bf16[2,128,1024]{2,1,0:T(8,128)(2,1)S(1)} %shard_map.41), channel_id=1, source_target_pairs={{0,33},{1,0},{2,35},{3,2},{4,37},{5,4},{6,39},{7,6},{8,41},{9,8},{... | collective-permute-start | bytes 1572872 | tf_op jit(solution)/shard_map/ppermute | solution.py:27
  23.0 12.1 %collective-permute-start.2 = (bf16[2,2,64,1024]{3,2,1,0:T(8,128)(2,1)S(1)}, bf16[2,2,64,1024]{3,2,1,0:T(8,128)(2,1)S(1)}, u32[]{:S(2)}, u32[]{:S(2)}) collective-permute-start(bf16[2,2,64,1024]{3,2,1,0:T(8,128)(2,1)S(1)} %collective-permute-done.1.refs_1_.refs_2_), channel_id=1, source_target_pairs={{0,2},{1,3},{2,4},{3,5},{4,6},{5,7},{6,8},{7,9},{8,10},{9,11},{10,... | collective-permute-start | bytes 1572872 | tf_op jit(solution)/shard_map/ppermute | solution.py:27
  26.4 12.3 %collective-permute-start.8 = (bf16[2,2,64,1024]{3,2,1,0:T(8,128)(2,1)S(1)}, bf16[2,2,64,1024]{3,2,1,0:T(8,128)(2,1)S(1)}, u32[]{:S(2)}, u32[]{:S(2)}) collective-permute-start(bf16[2,2,64,1024]{3,2,1,0:T(8,128)(2,1)S(1)} %collective-permute-done.1.refs_1_.refs_2_), channel_id=1, source_target_pairs={{0,16},{1,17},{2,18},{3,19},{4,20},{5,21},{6,22},{7,23},{8,24},{9,... | collective-permute-start | bytes 1572872 | tf_op jit(solution)/shard_map/ppermute | solution.py:27
  28.6 12.2 %collective-permute-start.10 = (bf16[2,2,64,1024]{3,2,1,0:T(8,128)(2,1)S(1)}, bf16[2,2,64,1024]{3,2,1,0:T(8,128)(2,1)S(1)}, u32[]{:S(2)}, u32[]{:S(2)}) collective-permute-start(bf16[2,2,64,1024]{3,2,1,0:T(8,128)(2,1)S(1)} %collective-permute-done.6.refs_4_.refs_6_.refs_9_), channel_id=1, source_target_pairs={{0,2},{1,3},{2,4},{3,5},{4,6},{5,7},{6,8},{7,9},{8,10},{9,11},{10,... | collective-permute-start | bytes 1572872 | tf_op jit(solution)/shard_map/ppermute | solution.py:27
  31.7 7.0 %collective-permute-start.7 = (bf16[2,2,64,1024]{3,2,1,0:T(8,128)(2,1)S(1)}, bf16[2,2,64,1024]{3,2,1,0:T(8,128)(2,1)S(1)}, u32[]{:S(2)}, u32[]{:S(2)}) collective-permute-start(bf16[2,2,64,1024]{3,2,1,0:T(8,128)(2,1)S(1)} %collective-permute-done.6.refs_4_.refs_6_.refs_9_), channel_id=1, source_target_pairs={{0,16},{1,17},{2,18},{3,19},{4,20},{5,21},{6,22},{7,23},{8,24},{9,... | collective-permute-start | bytes 1572872 | tf_op jit(solution)/shard_map/ppermute | solution.py:27
  35.1 10.4 %collective-permute-start.5 = (bf16[2,2,64,1024]{3,2,1,0:T(8,128)(2,1)S(1)}, bf16[2,2,64,1024]{3,2,1,0:T(8,128)(2,1)S(1)}, u32[]{:S(2)}, u32[]{:S(2)}) collective-permute-start(bf16[2,2,64,1024]{3,2,1,0:T(8,128)(2,1)S(1)} %collective-permute-done.2.refs_4_.refs_0_.refs_3_), channel_id=1, source_target_pairs={{0,2},{1,3},{2,4},{3,5},{4,6},{5,7},{6,8},{7,9},{8,10},{9,11},{10,... | collective-permute-start | bytes 1572872 | tf_op jit(solution)/shard_map/ppermute | solution.py:27
  39.4 8.1 %collective-permute-start.9 = (bf16[3,2,128,128]{3,2,1,0:T(8,128)(2,1)S(1)}, bf16[3,2,128,128]{3,2,1,0:T(8,128)(2,1)S(1)}, u32[]{:S(2)}, u32[]{:S(2)}) collective-permute-start(bf16[3,2,128,128]{3,2,1,0:T(8,128)(2,1)S(1)} %shard_map.43), channel_id=1, source_target_pairs={{0,33},{1,0},{2,35},{3,2},{4,37},{5,4},{6,39},{7,6},{8,41},{9,8},{... | collective-permute-start | bytes 589832 | tf_op jit(solution)/shard_map/ppermute | solution.py:27
  39.5 9.1 %collective-permute-start.13 = (bf16[2,2,64,1024]{3,2,1,0:T(8,128)(2,1)S(1)}, bf16[2,2,64,1024]{3,2,1,0:T(8,128)(2,1)S(1)}, u32[]{:S(2)}, u32[]{:S(2)}) collective-permute-start(bf16[2,2,64,1024]{3,2,1,0:T(8,128)(2,1)S(1)} %collective-permute-done.2.refs_4_.refs_0_.refs_3_), channel_id=1, source_target_pairs={{0,16},{1,17},{2,18},{3,19},{4,20},{5,21},{6,22},{7,23},{8,24},{9,... | collective-permute-start | bytes 1572872 | tf_op jit(solution)/shard_map/ppermute | solution.py:27
  40.8 7.8 %collective-permute-start.12 = (bf16[2,2,64,1024]{3,2,1,0:T(8,128)(2,1)S(1)}, bf16[2,2,64,1024]{3,2,1,0:T(8,128)(2,1)S(1)}, u32[]{:S(2)}, u32[]{:S(2)}) collective-permute-start(bf16[2,2,64,1024]{3,2,1,0:T(8,128)(2,1)S(1)} %collective-permute-done.10.refs_8_.refs_2_.refs_11_), channel_id=1, source_target_pairs={{0,16},{1,17},{2,18},{3,19},{4,20},{5,21},{6,22},{7,23},{8,24},{9,... | collective-permute-start | bytes 1572872 | tf_op jit(solution)/shard_map/ppermute | solution.py:27
  41.7 11.6 %collective-permute-start.11 = (bf16[2,2,64,1024]{3,2,1,0:T(8,128)(2,1)S(1)}, bf16[2,2,64,1024]{3,2,1,0:T(8,128)(2,1)S(1)}, u32[]{:S(2)}, u32[]{:S(2)}) collective-permute-start(bf16[2,2,64,1024]{3,2,1,0:T(8,128)(2,1)S(1)} %collective-permute-done.10.refs_8_.refs_2_.refs_11_), channel_id=1, source_target_pairs={{0,2},{1,3},{2,4},{3,5},{4,6},{5,7},{6,8},{7,9},{8,10},{9,11},{10,... | collective-permute-start | bytes 1572872 | tf_op jit(solution)/shard_map/ppermute | solution.py:27
  47.6 10.0 %collective-permute-start.16 = (bf16[2,2,64,1024]{3,2,1,0:T(8,128)(2,1)S(1)}, bf16[2,2,64,1024]{3,2,1,0:T(8,128)(2,1)S(1)}, u32[]{:S(2)}, u32[]{:S(2)}) collective-permute-start(bf16[2,2,64,1024]{3,2,1,0:T(8,128)(2,1)S(1)} %collective-permute-done.5.refs_2_.refs_5_.refs_0_), channel_id=1, source_target_pairs={{0,2},{1,3},{2,4},{3,5},{4,6},{5,7},{6,8},{7,9},{8,10},{9,11},{10,... | collective-permute-start | bytes 1572872 | tf_op jit(solution)/shard_map/ppermute | solution.py:27
  49.2 8.3 %collective-permute-start.17 = (bf16[2,2,128,128]{3,2,1,0:T(8,128)(2,1)S(1)}, bf16[2,2,128,128]{3,2,1,0:T(8,128)(2,1)S(1)}, u32[]{:S(2)}, u32[]{:S(2)}) collective-permute-start(bf16[2,2,128,128]{3,2,1,0:T(8,128)(2,1)S(1)} %shard_map.46), channel_id=1, source_target_pairs={{0,33},{1,0},{2,35},{3,2},{4,37},{5,4},{6,39},{7,6},{8,41},{9,8},{... | collective-permute-start | bytes 393224 | tf_op jit(solution)/shard_map/ppermute | solution.py:27
  50.5 8.0 %collective-permute-start.15 = (bf16[2,2,64,1024]{3,2,1,0:T(8,128)(2,1)S(1)}, bf16[2,2,64,1024]{3,2,1,0:T(8,128)(2,1)S(1)}, u32[]{:S(2)}, u32[]{:S(2)}) collective-permute-start(bf16[2,2,64,1024]{3,2,1,0:T(8,128)(2,1)S(1)} %collective-permute-done.5.refs_2_.refs_5_.refs_0_), channel_id=1, source_target_pairs={{0,16},{1,17},{2,18},{3,19},{4,20},{5,21},{6,22},{7,23},{8,24},{9,... | collective-permute-start | bytes 1572872 | tf_op jit(solution)/shard_map/ppermute | solution.py:27
  53.3 5.2 %collective-permute-start.14 = (bf16[2,2,64,1024]{3,2,1,0:T(8,128)(2,1)S(1)}, bf16[2,2,64,1024]{3,2,1,0:T(8,128)(2,1)S(1)}, u32[]{:S(2)}, u32[]{:S(2)}) collective-permute-start(bf16[2,2,64,1024]{3,2,1,0:T(8,128)(2,1)S(1)} %collective-permute-done.11.refs_4_.refs_13_.refs_3_), channel_id=1, source_target_pairs={{0,16},{1,17},{2,18},{3,19},{4,20},{5,21},{6,22},{7,23},{8,24},{9,... | collective-permute-start | bytes 1572872 | tf_op jit(solution)/shard_map/ppermute | solution.py:27
  57.6 2.5 %collective-permute-start.18 = (bf16[2,2,64,1024]{3,2,1,0:T(8,128)(2,1)S(1)}, bf16[2,2,64,1024]{3,2,1,0:T(8,128)(2,1)S(1)}, u32[]{:S(2)}, u32[]{:S(2)}) collective-permute-start(bf16[2,2,64,1024]{3,2,1,0:T(8,128)(2,1)S(1)} %collective-permute-done.16.refs_7_.refs_2_), channel_id=1, source_target_pairs={{0,16},{1,17},{2,18},{3,19},{4,20},{5,21},{6,22},{7,23},{8,24},{9,... | collective-permute-start | bytes 1572872 | tf_op jit(solution)/shard_map/ppermute | solution.py:27
  60.7 10.1 %collective-permute-start.19 = (bf16[3,2,128,128]{3,2,1,0:T(8,128)(2,1)S(1)}, bf16[3,2,128,128]{3,2,1,0:T(8,128)(2,1)S(1)}, u32[]{:S(2)}, u32[]{:S(2)}) collective-permute-start(bf16[3,2,128,128]{3,2,1,0:T(8,128)(2,1)S(1)} %shard_map.48), channel_id=1, source_target_pairs={{0,33},{1,0},{2,35},{3,2},{4,37},{5,4},{6,39},{7,6},{8,41},{9,8},{... | collective-permute-start | bytes 589832 | tf_op jit(solution)/shard_map/ppermute | solution.py:27
  64.4 14.1 %collective-permute-start.22 = (bf16[2,64,1024]{2,1,0:T(8,128)(2,1)S(1)}, bf16[2,64,1024]{2,1,0:T(8,128)(2,1)S(1)}, u32[]{:S(2)}, u32[]{:S(2)}) collective-permute-start(bf16[2,64,1024]{2,1,0:T(8,128)(2,1)S(1)} %get-tuple-element.28), channel_id=1, source_target_pairs={{0,128},{1,112},{2,130},{3,114},{4,132},{5,116},{6,134},{7,118},{8... | collective-permute-start | bytes 786440 | tf_op jit(solution)/shard_map/ppermute | solution.py:27
  71.6 6.2 %collective-permute-start.21 = (f32[1,128]{1,0:T(1,128)S(1)}, f32[1,128]{1,0:T(1,128)S(1)}, u32[]{:S(2)}, u32[]{:S(2)}) collective-permute-start(f32[1,128]{1,0:T(1,128)S(1)} %shard_map.49), channel_id=1, source_target_pairs={{0,129},{1,113},{2,131},{3,115},{4,133},{5,117},{6,135},{7,119},{8... | collective-permute-start | bytes 1544 | tf_op jit(solution)/shard_map/ppermute | solution.py:27
  71.6 6.9 %collective-permute-start.20 = (f32[1,128]{1,0:T(1,128)S(1)}, f32[1,128]{1,0:T(1,128)S(1)}, u32[]{:S(2)}, u32[]{:S(2)}) collective-permute-start(f32[1,128]{1,0:T(1,128)S(1)} %shard_map.49), channel_id=1, source_target_pairs={{0,128},{1,112},{2,130},{3,114},{4,132},{5,116},{6,134},{7,118},{8... | collective-permute-start | bytes 1544 | tf_op jit(solution)/shard_map/ppermute | solution.py:27
  77.8 10.4 %collective-permute-start.23 = (bf16[2,64,1024]{2,1,0:T(8,128)(2,1)S(1)}, bf16[2,64,1024]{2,1,0:T(8,128)(2,1)S(1)}, u32[]{:S(2)}, u32[]{:S(2)}) collective-permute-start(bf16[2,64,1024]{2,1,0:T(8,128)(2,1)S(1)} %get-tuple-element.30), channel_id=1, source_target_pairs={{0,129},{1,113},{2,131},{3,115},{4,133},{5,117},{6,135},{7,119},{8... | collective-permute-start | bytes 786440 | tf_op jit(solution)/shard_map/ppermute | solution.py:27
  78.5 4.4 %collective-permute-start.25 = (f32[2,128]{1,0:T(2,128)S(1)}, f32[2,128]{1,0:T(2,128)S(1)}, u32[]{:S(2)}, u32[]{:S(2)}) collective-permute-start(f32[2,128]{1,0:T(2,128)S(1)} %maximum_select_fusion.1), channel_id=1, source_target_pairs={{0,10},{1,11},{2,12},{3,13},{4,14},{5,15},{6,0},{7,1},{8,2},{9,3},... | collective-permute-start | bytes 3080 | tf_op jit(solution)/shard_map/ppermute | solution.py:27
  81.2 5.4 %collective-permute-start.24 = (f32[2,128]{1,0:T(2,128)S(1)}, f32[2,128]{1,0:T(2,128)S(1)}, u32[]{:S(2)}, u32[]{:S(2)}) collective-permute-start(f32[2,128]{1,0:T(2,128)S(1)} %maximum_select_fusion.1), channel_id=1, source_target_pairs={{0,6},{1,7},{2,8},{3,9},{4,10},{5,11},{6,12},{7,13},{8,14},{9,15},... | collective-permute-start | bytes 3080 | tf_op jit(solution)/shard_map/ppermute | solution.py:27
  86.7 2.4 %collective-permute-start.27 = (f32[2,128]{1,0:T(2,128)S(1)}, f32[2,128]{1,0:T(2,128)S(1)}, u32[]{:S(2)}, u32[]{:S(2)}) collective-permute-start(f32[2,128]{1,0:T(2,128)S(1)} %get-tuple-element.37), channel_id=1, source_target_pairs={{0,14},{1,15},{2,0},{3,1},{4,2},{5,3},{6,4},{7,5},{8,6},{9,7},{10,... | collective-permute-start | bytes 3080 | tf_op jit(solution)/shard_map/ppermute | solution.py:27
  87.4 3.6 %collective-permute-start.26 = (f32[2,128]{1,0:T(2,128)S(1)}, f32[2,128]{1,0:T(2,128)S(1)}, u32[]{:S(2)}, u32[]{:S(2)}) collective-permute-start(f32[2,128]{1,0:T(2,128)S(1)} %get-tuple-element.36), channel_id=1, source_target_pairs={{0,2},{1,3},{2,4},{3,5},{4,6},{5,7},{6,8},{7,9},{8,10},{9,11},{10,... | collective-permute-start | bytes 3080 | tf_op jit(solution)/shard_map/ppermute | solution.py:27
